TPU v7x, 32 devices: a whole 2x2x4 slice. The times are simulated.
32 devices in a mesh: page: 8 (over z, core), query: 2 (over y), head: 2 (over x).
Axes of the slice: x: 2, y: 2, z: 4, core: 2. Of those that a mesh axis runs over, the one named last changes fastest.
Arguments:
- queries: float32 [8, 512, 128], P('head', 'query'), may hold values from -40 to 40
- compact_keys: float32 [8, 2048, 128], P('head', 'page'), may hold values from -4 to 4
- compact_values: float32 [8, 2048, 128], P('head', 'page'), may hold values from -6 to 6
- slot_bias: float32 [8, 2048], P('head', 'page'), may hold values from -0.25 to 0.25
- targets: float32 [8, 512, 128], P('head', 'query'), may hold values from -4 to 4
- positions: int32 [8, 512], P('head', 'query'), may hold values from 0 to 262143
- assignment: int32 [8], replicated, may hold values from 0 to 7, as said below
Outputs:
- new_keys: float32 [8, 2048, 128], P('head', 'page')
- new_values: float32 [8, 2048, 128], P('head', 'page')
- new_bias: float32 [8, 2048], P('head', 'page')
Inputs may be any that keep to these rules, and one draw needn't show every extreme that they name: `assignment`: a permutation: every page 0 to 7 is held by exactly one page-axis block.
All inputs are finite; a program needn't handle non-finite values.
Results may differ from a plain program's by a relative error of at most 0.0003.
Values sent between devices are 32-bit elements; how exact they have to be, the bound alone decides.
No kernel may reach another device: no remote copies, remote signals or barrier semaphores. Data moves between devices by JAX's collectives and lax.ppermute only.
A program may use at most 64 MiB of HBM per device.

v0:
```python
import math

import jax
import jax.numpy as jnp
from jax import lax
from jax.sharding import PartitionSpec as P

STEPS = 2
PAGE_LEN = 32768


MASKED = -1e30
EPSILON = 1e-06
RATE_KEYS = 0.05
RATE_VALUES = 0.05
RATE_BIAS = 0.2
HIGHEST = lax.Precision.HIGHEST


def from_partner(value, axis, stride):
    mask = 2**stride
    pairs = [(source, source ^ mask) for source in range(lax.axis_size(axis))]
    return lax.ppermute(value, axis, pairs)


def squared_sums(grad_keys, grad_values, grad_bias):
    return jnp.stack(
        [
            jnp.sum(grad_keys * grad_keys),
            jnp.sum(grad_values * grad_values),
            jnp.sum(grad_bias * grad_bias),
        ]
    )


def apply_update(states, grads, totals, entry_count, slot_total):
    key_state, value_state, bias_state = states
    grad_keys, grad_values, grad_bias = grads
    rms_keys = jnp.sqrt(totals[0] / entry_count + EPSILON)
    rms_values = jnp.sqrt(totals[1] / entry_count + EPSILON)
    rms_bias = jnp.sqrt(totals[2] / slot_total + EPSILON)
    return (
        key_state - RATE_KEYS * grad_keys / rms_keys,
        value_state - RATE_VALUES * grad_values / rms_values,
        bias_state - RATE_BIAS * grad_bias / rms_bias,
    )


def local_gradients(queries, targets, visible, compact_keys, compact_values, slot_bias):
    score_scale = 1.0 / math.sqrt(queries.shape[2])
    scores = jnp.einsum("hqd,hsd->hqs", queries, compact_keys, precision=HIGHEST) * score_scale
    scores = jnp.where(visible, scores + slot_bias[:, None, :], MASKED)
    local_max = jnp.max(scores, axis=2)
    row_max = lax.pmax(local_max, "page")
    weights = jnp.where(visible, jnp.exp(scores - row_max[:, :, None]), 0.0)
    local_sum = jnp.einsum("hqs,hsd->hqd", weights, compact_values, precision=HIGHEST)
    row_total, row_sum = lax.psum((jnp.sum(weights, axis=2), local_sum), "page")
    attention = weights / row_total[:, :, None]
    output = row_sum / row_total[:, :, None]
    residual = output - targets
    grad_values = jnp.einsum("hqs,hqd->hsd", attention, residual, precision=HIGHEST)
    row_delta = jnp.sum(residual * output, axis=2)
    grad_probs = jnp.einsum("hqd,hsd->hqs", residual, compact_values, precision=HIGHEST)
    grad_scores = attention * (grad_probs - row_delta[:, :, None])
    grad_bias = jnp.sum(grad_scores, axis=1)
    grad_keys = jnp.einsum("hqs,hqd->hsd", grad_scores, queries, precision=HIGHEST) * score_scale
    return (grad_keys, grad_values, grad_bias)


def per_device(queries, compact_keys, compact_values, slot_bias, targets, positions, assignment):
    page_number = assignment[lax.axis_index("page")]
    local_heads = compact_keys.shape[0]
    slot_total = local_heads * lax.axis_size("head") * compact_keys.shape[1] * lax.axis_size("page")
    entry_count = slot_total * compact_keys.shape[2]
    query_count = lax.axis_size("query")
    heads_kept = max(local_heads // query_count, 1)
    query_parts = max(query_count // local_heads, 1)
    part_rows = queries.shape[1] // query_parts

    def split_items(array):
        width = array.shape[2]
        array = array.reshape(local_heads // heads_kept, heads_kept, query_parts, part_rows, width)
        array = jnp.transpose(array, (0, 2, 1, 3, 4))
        return array.reshape(query_count, heads_kept, part_rows, width)

    def join_items(array):
        width = array.shape[3]
        array = jnp.transpose(array, (1, 0, 2, 3))
        return array.reshape(heads_kept, query_count * part_rows, width)

    position_column = positions.astype(jnp.float32)[:, :, None]
    got_queries, got_targets, got_positions = (
        lax.all_to_all(split_items(queries), "query", split_axis=0, concat_axis=0, tiled=True),
        lax.all_to_all(split_items(targets), "query", split_axis=0, concat_axis=0, tiled=True),
        lax.all_to_all(
            split_items(position_column), "query", split_axis=0, concat_axis=0, tiled=True
        ),
    )
    group_queries = join_items(got_queries)
    group_targets = join_items(got_targets)
    group_positions = join_items(got_positions)[:, :, 0]
    visible = (page_number.astype(jnp.float32) <= jnp.floor(group_positions / PAGE_LEN))[:, :, None]
    query_index = lax.axis_index("query")
    first_head = query_index // query_parts * heads_kept
    key_state = lax.dynamic_slice_in_dim(compact_keys, first_head, heads_kept, 0)
    value_state = lax.dynamic_slice_in_dim(compact_values, first_head, heads_kept, 0)
    bias_state = lax.dynamic_slice_in_dim(slot_bias, first_head, heads_kept, 0)
    counted = (query_index % query_parts == 0).astype(jnp.float32)
    for repeat in range(STEPS):
        grads = local_gradients(
            group_queries, group_targets, visible, key_state, value_state, bias_state
        )
        for bit in range(query_parts.bit_length() - 1):
            partner = from_partner((grads[0], grads[1], grads[2]), "query", bit)
            grads = (grads[0] + partner[0], grads[1] + partner[1], grads[2] + partner[2])
        totals = lax.psum(
            squared_sums(grads[0], grads[1], grads[2]) * counted, ("page", "query", "head")
        )
        key_state, value_state, bias_state = apply_update(
            (key_state, value_state, bias_state), grads, totals, entry_count, slot_total
        )
    all_keys, all_values, all_bias = (
        lax.all_gather(key_state, "query", axis=0, tiled=True),
        lax.all_gather(value_state, "query", axis=0, tiled=True),
        lax.all_gather(bias_state, "query", axis=0, tiled=True),
    )
    slot_rows = compact_keys.shape[1]
    head_width = compact_keys.shape[2]
    all_keys = all_keys.reshape(
        local_heads // heads_kept, query_parts, heads_kept, slot_rows, head_width
    )[:, 0]
    all_values = all_values.reshape(
        local_heads // heads_kept, query_parts, heads_kept, slot_rows, head_width
    )[:, 0]
    all_bias = all_bias.reshape(local_heads // heads_kept, query_parts, heads_kept, slot_rows)[:, 0]
    return (
        all_keys.reshape(local_heads, slot_rows, head_width),
        all_values.reshape(local_heads, slot_rows, head_width),
        all_bias.reshape(local_heads, slot_rows),
    )


def solution(mesh):
    placed = (
        P("head", "query", None),
        P("head", "page", None),
        P("head", "page", None),
        P("head", "page"),
        P("head", "query", None),
        P("head", "query"),
        P(),
    )
    return jax.shard_map(
        per_device,
        mesh=mesh,
        in_specs=placed,
        out_specs=(P("head", "page", None), P("head", "page", None), P("head", "page")),
        check_vma=False,
    )
```

profile of v0, /device:TPU:0, one launch (start us, length us, event | category | flops | bytes accessed | tf_op | source)
XLA Modules:
  0.0 309.2 jit_solution(7510844970410608544)
XLA Ops:
  7.2 0.7 convert_element_type.12
  7.9 0.6 reshape_transpose_reshape_broadcast_in_dim.3
  8.5 4.2 %all-to-all-start = ((f32[2,2,256,1]{2,1,3,0:T(2,128)}), f32[2,2,256,1]{2,1,3,0:T(2,128)S(1)}, u32[]{:S(2)}, u32[]{:S(2)}) async-start(f32[2,2,256,1]{2,1,3,0:T(2,128)} %reshape_transpose_reshape_broadcast_in_dim.3), calls=%async_computation | async-start | bytes 8192 | tf_op jit(solution)/shard_map/all_to_all | solution.py:95
  12.7 3.8 %all-to-all-done = f32[2,2,256,1]{2,1,3,0:T(2,128)S(1)} async-done(((f32[2,2,256,1]{2,1,3,0:T(2,128)}), f32[2,2,256,1]{2,1,3,0:T(2,128)S(1)}, u32[]{:S(2)}, u32[]{:S(2)}) %all-to-all-start) | async-done | bytes 4128 | tf_op jit(solution)/shard_map/all_to_all | solution.py:95
  16.5 3.6 %all-to-all-start.1 = ((f32[2,2,256,128]{3,2,1,0:T(8,128)}), f32[2,2,256,128]{3,2,1,0:T(8,128)S(1)}, u32[]{:S(2)}, u32[]{:S(2)}) async-start(f32[2,2,256,128]{3,2,1,0:T(8,128)} %bitcast.52), calls=%async_computation.1 | async-start | bytes 1048576 | tf_op jit(solution)/shard_map/all_to_all | solution.py:93
  20.2 0.6 copy-done.4
  20.8 0.6 dynamic_slice.13
  22.1 5.4 %all-to-all-done.1 = f32[2,2,256,128]{3,2,1,0:T(8,128)S(1)} async-done(((f32[2,2,256,128]{3,2,1,0:T(8,128)}), f32[2,2,256,128]{3,2,1,0:T(8,128)S(1)}, u32[]{:S(2)}, u32[]{:S(2)}) %all-to-all-start.1) | async-done | bytes 524320 | tf_op jit(solution)/shard_map/all_to_all | solution.py:93
  27.4 3.5 %all-to-all-start.2 = ((f32[2,2,256,128]{3,2,1,0:T(8,128)}), f32[2,2,256,128]{3,2,1,0:T(8,128)S(1)}, u32[]{:S(2)}, u32[]{:S(2)}) async-start(f32[2,2,256,128]{3,2,1,0:T(8,128)} %bitcast.8), calls=%async_computation.2 | async-start | bytes 1048576 | tf_op jit(solution)/shard_map/all_to_all | solution.py:94
  30.9 0.0 all-reduce.3.cloned.1.call-start
  31.0 1.0 copy-done.1
  32.0 1.1 fusion.37
  33.1 14.8 %pmax.14 = f32[2,512]{1,0:T(2,128)S(1)} all-reduce(f32[2,512]{1,0:T(2,128)S(1)} %get-tuple-element.13), channel_id=1, replica_groups=mesh['page'=8,'query'=2,'head'=2] {'page'}, use_global_device_ids=true, to_apply=%region_1.2 | all-reduce | flops 1024 | bytes 8192 | tf_op jit(solution)/shard_map/pmax | solution.py:54
  47.9 2.7 fusion.8
  50.6 0.0 all-reduce.3.cloned.1.call-update
  50.6 0.0 all-reduce.5.cloned.1.call-start
  50.7 0.2 fusion.10
  50.9 13.7 %psum.42 = f32[2,512]{1,0:T(2,128)S(1)} all-reduce(f32[2,512]{1,0:T(2,128)S(1)} %fusion.10), channel_id=1, replica_groups=mesh['page'=8,'query'=2,'head'=2] {'page'}, use_global_device_ids=true, to_apply=%region_3.4 | all-reduce | flops 1024 | bytes 8192 | tf_op jit(solution)/shard_map/psum | solution.py:57
  64.6 40.6 %all-reduce.3.cloned.1.call-done = f32[2,512,128]{2,1,0:T(8,128)} async-done(((f32[2,512,128]{2,1,0:T(8,128)}), f32[2,512,128]{2,1,0:T(8,128)}) %all-reduce.3.cloned.1.call-update) | async-done | bytes 524304 | tf_op jit(solution)/shard_map/psum | solution.py:57
  105.2 1.4 multiply_reduce_fusion.1
  106.6 1.9 multiply_reduce_fusion.4
  108.5 1.2 fusion.38
  109.7 0.6 multiply_reduce_fusion.7
  110.3 1.7 multiply_reduce_fusion.5
  112.0 2.0 pad_maximum_fusion
  114.0 39.2 %psum.44 = f32[3]{0:T(128)S(1)} all-reduce(f32[3]{0:T(128)S(1)} %pad_maximum_fusion), channel_id=1, replica_groups=mesh['page'=8,'query'=2,'head'=2] {'page','query','head'}, use_global_device_ids=true, to_apply=%region_10.11 | all-reduce | flops 3 | bytes 24 | tf_op jit(solution)/shard_map/psum | solution.py:116
  153.2 0.6 fusion.36
  155.9 2.0 fusion.39
  158.0 14.7 %pmax.15 = f32[2,512]{1,0:T(2,128)S(1)} all-reduce(f32[2,512]{1,0:T(2,128)S(1)} %get-tuple-element.21), channel_id=1, replica_groups=mesh['page'=8,'query'=2,'head'=2] {'page'}, use_global_device_ids=true, to_apply=%region_12.13 | all-reduce | flops 1024 | bytes 8192 | tf_op jit(solution)/shard_map/pmax | solution.py:54
  172.7 2.7 fusion.11
  175.4 0.2 fusion.13
  175.6 13.6 %psum.45 = f32[2,512]{1,0:T(2,128)S(1)} all-reduce(f32[2,512]{1,0:T(2,128)S(1)} %fusion.13), channel_id=1, replica_groups=mesh['page'=8,'query'=2,'head'=2] {'page'}, use_global_device_ids=true, to_apply=%region_14.15 | all-reduce | flops 1024 | bytes 8192 | tf_op jit(solution)/shard_map/psum | solution.py:57
  189.2 40.6 %all-reduce.5.cloned.1.call-done = f32[2,512,128]{2,1,0:T(8,128)} async-done(((f32[2,512,128]{2,1,0:T(8,128)}), f32[2,512,128]{2,1,0:T(8,128)}) %all-reduce.5.cloned.1.call-update) | async-done | bytes 524304 | tf_op jit(solution)/shard_map/psum | solution.py:57
  229.8 1.4 multiply_reduce_fusion
  231.2 2.0 multiply_reduce_fusion.2
  233.2 1.2 fusion.40
  234.4 1.7 multiply_reduce_fusion.3
  236.1 0.6 multiply_reduce_fusion.6
  236.7 2.1 pad_maximum_fusion.1
  238.8 39.2 %psum.47 = f32[3]{0:T(128)S(1)} all-reduce(f32[3]{0:T(128)S(1)} %pad_maximum_fusion.1), channel_id=1, replica_groups=mesh['page'=8,'query'=2,'head'=2] {'page','query','head'}, use_global_device_ids=true, to_apply=%region_21.22 | all-reduce | flops 3 | bytes 24 | tf_op jit(solution)/shard_map/psum | solution.py:116
  277.9 0.7 fusion.35
  279.4 0.1 divide_subtract_fusion.1
  279.4 7.9 %all_gather.9 = f32[4,256,128]{2,1,0:T(8,128)S(1)} all-gather(f32[2,256,128]{2,1,0:T(8,128)S(1)} %divide_subtract_fusion.1), channel_id=1, replica_groups=mesh['page'=8,'query'=2,'head'=2] {'query'}, dimensions={0}, use_global_device_ids=true | all-gather | bytes 786432 | tf_op jit(solution)/shard_map/all_gather | solution.py:123
  288.1 7.0 %all_gather.10 = f32[4,256,128]{2,1,0:T(8,128)S(1)} all-gather(f32[2,256,128]{2,1,0:T(8,128)S(1)} %divide_subtract_fusion), channel_id=1, replica_groups=mesh['page'=8,'query'=2,'head'=2] {'query'}, dimensions={0}, use_global_device_ids=true | all-gather | bytes 786432 | tf_op jit(solution)/shard_map/all_gather | solution.py:124
  295.8 4.3 %all-gather = f32[2,2,256]{2,1,0:T(2,128)S(1)} all-gather(f32[1,2,256]{2,1,0:T(2,128)S(1)} %fusion.27), channel_id=1, replica_groups=mesh['page'=8,'query'=2,'head'=2] {'query'}, dimensions={0}, use_global_device_ids=true | all-gather | bytes 6144 | tf_op jit(solution)/shard_map/all_gather | solution.py:125
  300.2 0.6 reshape.66
  300.8 0.8 copy.30
  301.6 0.8 copy.31
  (18 shorter events, 0.2 us)
Async XLA Ops:
  8.5 8.0 %all-to-all-start = ((f32[2,2,256,1]{2,1,3,0:T(2,128)}), f32[2,2,256,1]{2,1,3,0:T(2,128)S(1)}, u32[]{:S(2)}, u32[]{:S(2)}) async-start(f32[2,2,256,1]{2,1,3,0:T(2,128)} %reshape_transpose_reshape_broadcast_in_dim.3), calls=%async_computation | async-start | bytes 8192 | tf_op jit(solution)/shard_map/all_to_all | solution.py:95
  16.5 3.6 %copy-start.3 = (f32[4,256]{1,0:T(4,128)S(1)}, f32[4,256]{1,0:T(4,128)}, u32[]{:S(2)}) copy-start(f32[4,256]{1,0:T(4,128)} %param.10) | copy-start | bytes 12292
  16.5 10.9 %all-to-all-start.1 = ((f32[2,2,256,128]{3,2,1,0:T(8,128)}), f32[2,2,256,128]{3,2,1,0:T(8,128)S(1)}, u32[]{:S(2)}, u32[]{:S(2)}) async-start(f32[2,2,256,128]{3,2,1,0:T(8,128)} %bitcast.52), calls=%async_computation.1 | async-start | bytes 1048576 | tf_op jit(solution)/shard_map/all_to_all | solution.py:93
  20.2 0.7 copy-start.4
  27.4 23.2 %all-to-all-start.2 = ((f32[2,2,256,128]{3,2,1,0:T(8,128)}), f32[2,2,256,128]{3,2,1,0:T(8,128)S(1)}, u32[]{:S(2)}, u32[]{:S(2)}) async-start(f32[2,2,256,128]{3,2,1,0:T(8,128)} %bitcast.8), calls=%async_computation.2 | async-start | bytes 1048576 | tf_op jit(solution)/shard_map/all_to_all | solution.py:94
  30.9 74.3 %all-reduce.3.cloned.1.call-start = ((), (), s32[]{:S(2)}) async-start(), calls=%async_computation.3 | async-start | bytes 1048576 | tf_op jit(solution)/shard_map/psum | solution.py:57
  31.0 1.0 copy-start.1
  32.0 15.9 %copy-start = (f32[4,256,128]{2,1,0:T(8,128)S(1)}, f32[4,256,128]{2,1,0:T(8,128)}, u32[]{:S(2)}) copy-start(f32[4,256,128]{2,1,0:T(8,128)} %param.9) | copy-start | bytes 1572868
  50.6 179.2 %all-reduce.5.cloned.1.call-start = ((), (), s32[]{:S(2)}) async-start(), calls=%async_computation.4 | async-start | bytes 1048576 | tf_op jit(solution)/shard_map/psum | solution.py:57
  234.4 44.9 %copy-start.2 = (f32[4,256,128]{2,1,0:T(8,128)S(1)}, f32[4,256,128]{2,1,0:T(8,128)}, u32[]{:S(2)}) copy-start(f32[4,256,128]{2,1,0:T(8,128)} %param.8) | copy-start | bytes 1572868
Sparse Core Ops, SparseCore 0:
  50.7 54.4 all-reduce.2
  175.5 54.2 all-reduce.4
where the time goes:
time: 310 us; the launch traced here: 309 us
  blocking collectives  154 us (50%)
  waiting for transfers between devices  90.4 us (29%)
  between operations  19.1 us (6%)
  matrix products  18.2 us (6%)
  starting transfers between devices  11.4 us (4%)
  other arithmetic  9.33 us (3%)
  local copies, waits for them, and re-layouts  6.37 us (2%)
    psum x2, waiting for transfers between devices, local_gradients(): row_total, row_sum = lax.psum((jnp.sum(weights, axis=2), local_sum), 'page')  81.2 us
    psum x2, blocking collectives, per_device(): lax.psum(squared_sums(grads[0], grads[1], grads[2]) * counted, ('page', '...  78.4 us
    pmax x2, blocking collectives, local_gradients(): row_max = lax.pmax(local_max, 'page')  29.5 us
    psum x2, blocking collectives, local_gradients(): row_total, row_sum = lax.psum((jnp.sum(weights, axis=2), local_sum), 'page')  27.3 us
    all_gather x1, blocking collectives, per_device(): lax.all_gather(key_state, 'query', axis=0, tiled=True)  7.91 us
    all_gather x1, blocking collectives, per_device(): lax.all_gather(value_state, 'query', axis=0, tiled=True)  7.05 us
  transfers between devices with their start and end apart: 5, of which 4 were waited for; matrix products, arithmetic and copies ran while one was open for 2% of the time, Pallas kernels for 0%

commit v1 on v0

--- a/solution.py
+++ b/solution.py
@@ -1,8 +1,11 @@
+import itertools
 import math
 
 import jax
 import jax.numpy as jnp
 from jax import lax
+from jax.experimental import pallas as pl
+from jax.experimental.pallas import tpu as pltpu
 from jax.sharding import PartitionSpec as P
 
 STEPS = 2
@@ -15,6 +18,456 @@
 RATE_VALUES = 0.05
 RATE_BIAS = 0.2
 HIGHEST = lax.Precision.HIGHEST
+TAIL = 8
+CORES = 2
+
+
+def send(value, axes, move):
+    sizes = [lax.axis_size(axis) for axis in axes]
+
+    def flat(place):
+        index = 0
+        for size, at in zip(sizes, place):
+            index = index * size + at % size
+        return index
+
+    pairs = [
+        (flat(place), flat(move(*place))) for place in itertools.product(*map(range, sizes))
+    ]
+    return lax.ppermute(value, axes, pairs)
+
+
+def dot(left, right, left_dim, right_dim):
+    return lax.dot_general(
+        left,
+        right,
+        (((left_dim,), (right_dim,)), ((), ())),
+        precision=HIGHEST,
+        preferred_element_type=jnp.float32,
+    )
+
+
+def call(body, out_shapes, name, cost, scalars, blocks, scratch=()):
+    def whole(shape):
+        return pl.BlockSpec(shape, lambda step, numbers: (0,) * len(shape))
+
+    arrays, specs = [], []
+    for block in blocks:
+        if isinstance(block, tuple):
+            array, shape, index = block
+            arrays.append(array)
+            specs.append(pl.BlockSpec(shape, index))
+        else:
+            arrays.append(block)
+            specs.append(whole(block.shape))
+    return pl.pallas_call(
+        body,
+        out_shape=[jax.ShapeDtypeStruct(shape, jnp.float32) for shape in out_shapes],
+        grid_spec=pltpu.PrefetchScalarGridSpec(
+            num_scalar_prefetch=1,
+            grid=(1,),
+            in_specs=specs,
+            out_specs=[whole(shape) for shape in out_shapes],
+            scratch_shapes=scratch,
+        ),
+        compiler_params=pltpu.CompilerParams(vmem_limit_bytes=48 * 2**20),
+        cost_estimate=pl.CostEstimate(flops=cost, bytes_accessed=2**20, transcendentals=0),
+        name=name,
+    )(scalars, *arrays)
+
+
+def row_as_tail(row, width):
+    rows = [row[:, at : at + width] for at in range(0, row.shape[1], width)]
+    rows.append(jnp.zeros((TAIL - len(rows), width), row.dtype))
+    return jnp.concatenate(rows, axis=0)
+
+
+def tail_as_row(ref, start, count):
+    return jnp.concatenate([ref[start + at : start + at + 1, :] for at in range(count)], axis=1)
+
+
+def row_as_column(row, width):
+    parts = []
+    for at in range(0, row.shape[1], width):
+        parts.append(jnp.broadcast_to(row[:, at : at + width], (width, width)).T)
+    return jnp.concatenate(parts, axis=0)
+
+
+def direct_plan_fits(mesh, queries, compact_keys):
+    pages, query_devices, head_devices = (mesh.shape[axis] for axis in ("page", "query", "head"))
+    local_heads = queries.shape[0] // head_devices
+    part_rows = queries.shape[1] // query_devices
+    slot_rows = compact_keys.shape[1] // pages
+    width = queries.shape[2]
+    if pages % CORES or local_heads != CORES * query_devices or width % 128:
+        return False
+    ranks = pages // CORES
+    chunk = part_rows * query_devices // ranks
+    return (
+        part_rows * query_devices % ranks == 0
+        and chunk % 128 == 0
+        and part_rows % chunk == 0
+        and slot_rows % width == 0
+        and part_rows % width == 0
+        and max(slot_rows, part_rows) <= TAIL * width
+    )
+
+
+def direct_per_device(
+    queries, compact_keys, compact_values, slot_bias, targets, positions, assignment
+):
+    local_heads, part_rows, width = queries.shape
+    slot_rows = compact_keys.shape[1]
+    query_devices = lax.axis_size("query")
+    head_devices = lax.axis_size("head")
+    ranks = lax.axis_size("page") // CORES
+    query_rows = part_rows * query_devices
+    chunk = query_rows // ranks
+    slot_total = local_heads * head_devices * slot_rows * lax.axis_size("page")
+    entry_total = slot_total * width
+    score_scale = 1.0 / math.sqrt(width)
+    slots = CORES * slot_rows
+    pos_rows = part_rows // width
+    bias_rows = slot_rows // width
+    packed_rows = 2 * slot_rows + TAIL
+    matmul_cost = 2 * slots * query_rows * width
+
+    page = lax.axis_index("page")
+    rank, core = page // CORES, page % CORES
+    me = lax.axis_index("query")
+    own_head = CORES * me + core
+
+    def part_of(z):
+        return z * chunk // part_rows
+
+    chunk_part = rank * chunk // part_rows
+    target_head = CORES * lax.rem(me - chunk_part + query_devices, query_devices) + core
+    target_block = lax.rem(rank, part_rows // chunk)
+    send_heads = [
+        CORES * lax.rem(me - turn + query_devices, query_devices) + core
+        for turn in range(1, query_devices)
+    ]
+    mate_head = CORES * me + (CORES - 1 - core)
+    mate_page = CORES * rank + (CORES - 1 - core)
+
+    prep_numbers = jnp.stack(
+        [own_head, mate_head, target_head, target_block, *send_heads]
+    ).astype(jnp.int32)
+
+    def prep_body(numbers, *refs):
+        positions_ref, bias_ref, targets_ref, *refs = refs
+        key_refs, refs = refs[:2], refs[2:]
+        value_refs, refs = refs[:2], refs[2:]
+        query_refs, refs = refs[:query_devices], refs[query_devices:]
+        state_outs, refs = refs[:2], refs[2:]
+        query_outs, (targets_out,) = refs[:query_devices], refs[query_devices:]
+        for turn in range(query_devices):
+            head = numbers[0] if turn == 0 else numbers[3 + turn]
+            query_outs[turn][:part_rows, :] = query_refs[turn][0]
+            row = positions_ref[pl.ds(head, 1), :].astype(jnp.float32)
+            query_outs[turn][part_rows:, :] = row_as_tail(row, width)
+        for at in range(2):
+            state_outs[at][:slot_rows, :] = key_refs[at][0]
+            state_outs[at][slot_rows : 2 * slot_rows, :] = value_refs[at][0]
+            row = bias_ref[pl.ds(numbers[at], 1), :]
+            state_outs[at][2 * slot_rows :, :] = row_as_tail(row, width)
+        targets_out[...] = targets_ref[0]
+
+    def head_block(array, number):
+        shape = (1,) + array.shape[1:]
+        return (array, shape, lambda step, numbers: (numbers[number], 0, 0))
+
+    targets_block = (
+        targets,
+        (1, chunk, width),
+        lambda step, numbers: (numbers[2], numbers[3], 0),
+    )
+    packed = call(
+        prep_body,
+        [(packed_rows, width)] * 2 + [(part_rows + TAIL, width)] * query_devices + [(chunk, width)],
+        "pack",
+        2**20,
+        prep_numbers,
+        [positions, slot_bias, targets_block]
+        + [head_block(compact_keys, at) for at in range(2)]
+        + [head_block(compact_values, at) for at in range(2)]
+        + [head_block(queries, 0)]
+        + [head_block(queries, 3 + turn) for turn in range(1, query_devices)],
+    )
+    own_state, mate_state = packed[0], packed[1]
+    query_parts = [packed[2]] + [
+        send(packed[2 + turn], ("query",), lambda y, turn=turn: (y - turn,))
+        for turn in range(1, query_devices)
+    ]
+    states = [own_state, send(mate_state, ("page",), lambda p: (p + 1 - 2 * (p % CORES),))]
+    chunk_targets = send(
+        packed[2 + query_devices],
+        ("page", "query"),
+        lambda p, y: (p, y - part_of(p // CORES)),
+    )
+
+    to_chunks = [lax.rem(rank + turn, ranks) for turn in range(ranks)]
+    from_chunks = [lax.rem(rank - turn + ranks, ranks) for turn in range(ranks)]
+    numbers = jnp.stack(
+        [assignment[page] * PAGE_LEN, assignment[mate_page] * PAGE_LEN, *to_chunks, *from_chunks]
+    ).astype(jnp.int32)
+
+    def along_rank(value, turn):
+        return send(value, ("page",), lambda p: (p + CORES * turn,))
+
+    def step_sizes(tile_refs):
+        tile = tile_refs[0][...]
+        for ref in tile_refs[1:]:
+            tile = tile + ref[...]
+        sums = jnp.sum(tile, axis=1, keepdims=True)
+        return (
+            RATE_KEYS / jnp.sqrt(sums[0:1] / entry_total + EPSILON),
+            RATE_VALUES / jnp.sqrt(sums[1:2] / entry_total + EPSILON),
+            RATE_BIAS / jnp.sqrt(sums[2:3] / slot_total + EPSILON),
+        )
+
+    def updated(state_ref, grad_ref, sizes):
+        key_end, value_end = slot_rows, 2 * slot_rows
+        return (
+            state_ref[:key_end, :] - sizes[0] * grad_ref[:key_end, :],
+            state_ref[key_end:value_end, :] - sizes[1] * grad_ref[key_end:value_end, :],
+            state_ref[value_end:, :] - sizes[2] * grad_ref[value_end:, :],
+        )
+
+    def forward(state_refs, query_refs, number_ref, chunk_outs, weights_out, max_out, chunks):
+        all_queries = jnp.concatenate([ref[:part_rows, :] for ref in query_refs], axis=0)
+        position_row = jnp.concatenate(
+            [tail_as_row(ref, part_rows, pos_rows) for ref in query_refs], axis=1
+        )
+        all_scores, all_visible = [], []
+        for at, ref in enumerate(state_refs):
+            scores = dot(ref[:slot_rows, :], all_queries, 1, 1) * score_scale
+            bias = row_as_column(tail_as_row(ref, 2 * slot_rows, bias_rows), width)
+            scores = scores + jnp.concatenate([bias] * (query_rows // width), axis=1)
+            page_start = number_ref[at].astype(jnp.float32)
+            visible = jnp.broadcast_to(position_row, scores.shape) >= page_start
+            all_scores.append(jnp.where(visible, scores, MASKED))
+            all_visible.append(visible)
+        row_max = jnp.max(all_scores[0], axis=0, keepdims=True)
+        for scores in all_scores[1:]:
+            row_max = jnp.maximum(row_max, jnp.max(scores, axis=0, keepdims=True))
+        row_total = jnp.zeros_like(row_max)
+        row_sum = jnp.zeros((width, query_rows), jnp.float32)
+        for at, ref in enumerate(state_refs):
+            weights = jnp.where(all_visible[at], jnp.exp(all_scores[at] - row_max), 0.0)
+            weights_out[at * slot_rows : (at + 1) * slot_rows, :] = weights
+            row_total = row_total + jnp.sum(weights, axis=0, keepdims=True)
+            row_sum = row_sum + dot(ref[slot_rows : 2 * slot_rows, :], weights, 0, 0)
+        max_out[...] = jnp.broadcast_to(row_max, (TAIL, query_rows))
+        tail = jnp.concatenate(
+            [row_max, row_total, jnp.zeros((TAIL - 2, query_rows), jnp.float32)], axis=0
+        )
+        for at in range(ranks):
+            columns = slice(at * chunk, (at + 1) * chunk)
+            chunks[at, :width, :] = row_sum[:, columns]
+            chunks[at, width:, :] = tail[:, columns]
+        for turn in range(ranks):
+            chunk_outs[turn][...] = chunks[number_ref[2 + turn]]
+
+    forward_shapes = (
+        [(width + TAIL, chunk)] * ranks + [(slots, query_rows), (TAIL, query_rows)]
+    )
+    chunk_scratch = [pltpu.VMEM((ranks, width + TAIL, chunk), jnp.float32)]
+
+    def first_body(number_ref, *refs):
+        state_refs, refs = refs[:2], refs[2:]
+        query_refs, refs = refs[:query_devices], refs[query_devices:]
+        chunk_outs, (weights_out, max_out, chunks) = refs[:ranks], refs[ranks:]
+        forward(state_refs, query_refs, number_ref, chunk_outs, weights_out, max_out, chunks)
+
+    def next_body(number_ref, *refs):
+        state_refs, refs = refs[:2], refs[2:]
+        query_refs, refs = refs[:query_devices], refs[query_devices:]
+        grad_refs, refs = refs[:2], refs[2:]
+        tile_refs, refs = refs[:ranks], refs[ranks:]
+        state_outs, refs = refs[:2], refs[2:]
+        chunk_outs, (weights_out, max_out, chunks) = refs[:ranks], refs[ranks:]
+        sizes = step_sizes(tile_refs)
+        for at in range(2):
+            keys, values, bias = updated(state_refs[at], grad_refs[at], sizes)
+            state_outs[at][:slot_rows, :] = keys
+            state_outs[at][slot_rows : 2 * slot_rows, :] = values
+            state_outs[at][2 * slot_rows :, :] = bias
+        forward(state_outs, query_refs, number_ref, chunk_outs, weights_out, max_out, chunks)
+
+    def merge_body(number_ref, targets_ref, *refs):
+        chunk_refs, (merged_out,) = refs[:ranks], refs[ranks:]
+        row_max = chunk_refs[0][width : width + 1, :]
+        for ref in chunk_refs[1:]:
+            row_max = jnp.maximum(row_max, ref[width : width + 1, :])
+        row_total = jnp.zeros_like(row_max)
+        row_sum = jnp.zeros((width, chunk), jnp.float32)
+        for ref in chunk_refs:
+            factor = jnp.exp(ref[width : width + 1, :] - row_max)
+            row_total = row_total + ref[width + 1 : width + 2, :] * factor
+            row_sum = row_sum + ref[:width, :] * factor
+        output = row_sum / row_total
+        residual = output - targets_ref[...].T
+        row_delta = jnp.sum(residual * output, axis=0, keepdims=True)
+        merged_out[:width, :] = residual
+        merged_out[width:, :] = jnp.concatenate(
+            [row_max, row_total, row_delta, jnp.zeros((TAIL - 3, chunk), jnp.float32)], axis=0
+        )
+
+    def backward_body(number_ref, *refs):
+        weights_ref, max_ref, *refs = refs
+        state_refs, refs = refs[:2], refs[2:]
+        query_refs, refs = refs[:query_devices], refs[query_devices:]
+        merged_refs, refs = refs[:ranks], refs[ranks:]
+        grad_outs, (squares_out, chunks) = refs[:2], refs[2:]
+        for turn in range(ranks):
+            chunks[number_ref[2 + ranks + turn]] = merged_refs[turn][...]
+        joined = jnp.concatenate([chunks[at] for at in range(ranks)], axis=1)
+        residual = joined[:width, :]
+        row_max, row_total, row_delta = (
+            joined[width + at : width + at + 1, :] for at in range(3)
+        )
+        all_queries = jnp.concatenate([ref[:part_rows, :] for ref in query_refs], axis=0)
+        factor = jnp.exp(max_ref[0:1, :] - row_max) / row_total
+        ones = jnp.ones((TAIL, query_rows), jnp.float32)
+        squares = [jnp.zeros((1, width), jnp.float32)] * 3
+        for at, ref in enumerate(state_refs):
+            attention = weights_ref[at * slot_rows : (at + 1) * slot_rows, :] * factor
+            grad_values = dot(attention, residual, 1, 1)
+            grad_probs = dot(ref[slot_rows : 2 * slot_rows, :], residual, 1, 0)
+            grad_scores = attention * (grad_probs - row_delta)
+            grad_keys = dot(grad_scores, all_queries, 1, 0) * score_scale
+            grad_bias = row_as_tail(dot(ones, grad_scores, 1, 1)[0:1, :], width)
+            grad_outs[at][:slot_rows, :] = grad_keys
+            grad_outs[at][slot_rows : 2 * slot_rows, :] = grad_values
+            grad_outs[at][2 * slot_rows :, :] = grad_bias
+            for which, grad in enumerate((grad_keys, grad_values, grad_bias)):
+                squares[which] = squares[which] + jnp.sum(grad * grad, axis=0, keepdims=True)
+        squares_out[...] = jnp.concatenate(
+            squares + [jnp.zeros((TAIL - 3, width), jnp.float32)], axis=0
+        )
+
+    def to_outputs(packs):
+        received = []
+        for turn in range(query_devices):
+            for flip in range(CORES):
+                if turn == 0 and flip == 0:
+                    received.append(packs[0])
+                else:
+                    received.append(
+                        send(
+                            packs[flip],
+                            ("page", "query"),
+                            lambda p, y, turn=turn, flip=flip: (
+                                p + flip * (1 - 2 * (p % CORES)),
+                                y + turn,
+                            ),
+                        )
+                    )
+        return received
+
+    def over_block(tile):
+        total = tile
+        for dc, dy, dx in itertools.product(
+            range(CORES), range(query_devices), range(head_devices)
+        ):
+            if dc or dy or dx:
+                total = total + send(
+                    tile,
+                    ("page", "query", "head"),
+                    lambda p, y, x, dc=dc, dy=dy, dx=dx: (
+                        p + dc * (1 - 2 * (p % CORES)),
+                        y + dy,
+                        x + dx,
+                    ),
+                )
+        return total
+
+    state_copies, grads, tiles = None, None, None
+    for repeat in range(STEPS):
+        if repeat == 0:
+            *chunk_parts, weights, maxima = call(
+                first_body,
+                forward_shapes,
+                "forward",
+                6 * 2 * matmul_cost,
+                numbers,
+                states + query_parts,
+                chunk_scratch,
+            )
+        else:
+            own_new, mate_new, *chunk_parts, weights, maxima = call(
+                next_body,
+                [(packed_rows, width)] * 2 + forward_shapes,
+                "update_forward",
+                6 * 2 * matmul_cost,
+                numbers,
+                states + query_parts + grads + tiles,
+                chunk_scratch,
+            )
+            states = [own_new, mate_new]
+            state_copies = states
+        arrived = [chunk_parts[0]] + [
+            along_rank(chunk_parts[turn], turn) for turn in range(1, ranks)
+        ]
+        (merged,) = call(
+            merge_body,
+            [(width + TAIL, chunk)],
+            "merge",
+            2**20,
+            numbers,
+            [chunk_targets] + arrived,
+        )
+        all_merged = [merged] + [along_rank(merged, turn) for turn in range(1, ranks)]
+        own_grad, mate_grad, squares = call(
+            backward_body,
+            [(packed_rows, width)] * 2 + [(TAIL, width)],
+            "backward",
+            6 * 3 * matmul_cost,
+            numbers,
+            [weights, maxima] + states + query_parts + all_merged,
+            chunk_scratch,
+        )
+        grads = [own_grad, mate_grad]
+        block_squares = over_block(squares)
+        tiles = [block_squares] + [
+            along_rank(block_squares, turn) for turn in range(1, ranks)
+        ]
+
+    all_states = to_outputs(state_copies)
+    all_grads = to_outputs(grads)
+    out_heads = jnp.stack(
+        [
+            CORES * lax.rem(me - turn + query_devices, query_devices)
+            + (core if flip == 0 else CORES - 1 - core)
+            for turn in range(query_devices)
+            for flip in range(CORES)
+        ]
+    ).astype(jnp.int32)
+
+    def last_body(number_ref, *refs):
+        state_refs, refs = refs[:local_heads], refs[local_heads:]
+        grad_refs, refs = refs[:local_heads], refs[local_heads:]
+        tile_refs, (keys_out, values_out, bias_out) = refs[:ranks], refs[ranks:]
+        sizes = step_sizes(tile_refs)
+        for at in range(local_heads):
+            keys, values, bias = updated(state_refs[at], grad_refs[at], sizes)
+            head = number_ref[at]
+            keys_out[head] = keys
+            values_out[head] = values
+            bias_row = jnp.concatenate([bias[row : row + 1] for row in range(bias_rows)], axis=1)
+            bias_out[pl.ds(head, 1), :] = bias_row
+
+    return tuple(
+        call(
+            last_body,
+            [compact_keys.shape, compact_values.shape, slot_bias.shape],
+            "last_update",
+            2**20,
+            out_heads,
+            all_states + all_grads + tiles,
+        )
+    )
 
 
 def from_partner(value, axis, stride):
@@ -150,10 +603,15 @@
         P("head", "query"),
         P(),
     )
-    return jax.shard_map(
-        per_device,
-        mesh=mesh,
-        in_specs=placed,
-        out_specs=(P("head", "page", None), P("head", "page", None), P("head", "page")),
-        check_vma=False,
-    )
+
+    def program(*args):
+        plan = direct_per_device if direct_plan_fits(mesh, args[0], args[1]) else per_device
+        return jax.shard_map(
+            plan,
+            mesh=mesh,
+            in_specs=placed,
+            out_specs=(P("head", "page", None), P("head", "page", None), P("head", "page")),
+            check_vma=False,
+        )(*args)
+
+    return program

time: 310 us -> 115 us (0.37)
  blocking collectives: 154 us -> 0 us
  waiting for transfers between devices: 90.4 us -> 42.8 us
  starting transfers between devices: 11.4 us -> 46.7 us
  matrix products: 18.2 us -> 0 us
  between operations: 19.1 us -> 2.14 us
  Pallas kernels: 0 us -> 16.4 us
  other arithmetic: 9.33 us -> 0.1 us
    psum x4 -> x0, blocking collectives: 106 us -> none  [the longest x2 78.4 us: per_device(): lax.psum(squared_sums(grads[0], grads[1], grads[2]) * counted, ('page', '...]
    psum x2 -> x0, waiting for transfers between devices: 81.2 us -> none  [local_gradients(): row_total, row_sum = lax.psum((jnp.sum(weights, axis=2), local_sum), 'page')]
    ppermute x0 -> x41, starting transfers between devices: none -> 46.7 us  [send(): return lax.ppermute(value, axes, pairs)]
    ppermute x0 -> x41, waiting for transfers between devices: none -> 42.8 us  [send(): return lax.ppermute(value, axes, pairs)]
    pmax x2 -> x0, blocking collectives: 29.5 us -> none  [local_gradients(): row_max = lax.pmax(local_max, 'page')]
    all_gather x3 -> x0, blocking collectives: 19.3 us -> none  [the longest x1 7.91 us: per_device(): lax.all_gather(key_state, 'query', axis=0, tiled=True)]
    dot_general x10 -> x0, matrix products: 18.2 us -> none  [the longest x2 5.32 us: local_gradients(): jnp.einsum('hqs,hsd->hqd', weights, compact_values, precision=HIGHEST)]
    pallas_call x0 -> x8, Pallas kernels: none -> 16.4 us  [call(): pl.pallas_call(body, out_shape=[jax.ShapeDtypeStruct(shape, jnp.float32)...]
  transfers between devices with their start and end apart: 5 -> 41, of which waited for: 4 -> 25; matrix products, arithmetic and copies ran while one was open for 2% -> 1% of each run, Pallas kernels for 0% -> 3%
where the time goes in v1:
time: 115 us; the launch traced here: 114 us
  starting transfers between devices  46.7 us (41%)
  waiting for transfers between devices  42.8 us (37%)
  Pallas kernels  16.4 us (14%)
  local copies, waits for them, and re-layouts  6.18 us (5%)
  between operations  2.14 us (2%)
    ppermute x41, starting transfers between devices, send(): return lax.ppermute(value, axes, pairs)  46.7 us
    ppermute x41, waiting for transfers between devices, send(): return lax.ppermute(value, axes, pairs)  42.8 us
    pallas_call x8, Pallas kernels, call(): pl.pallas_call(body, out_shape=[jax.ShapeDtypeStruct(shape, jnp.float32)...  16.4 us
    unnamed x14, local copies, waits for them, and re-layouts  5.42 us
  transfers between devices with their start and end apart: 41, of which 25 were waited for; matrix products, arithmetic and copies ran while one was open for 1% of the time, Pallas kernels for 3%

profile of v1, /device:TPU:0, one launch (start us, length us, event | category | flops | bytes accessed | tf_op | source)
XLA Modules:
  0.0 114.4 jit_solution(690951900609767725)
XLA Ops:
  1.4 1.0 copy-done
  2.5 1.0 copy-done.1
  3.5 1.0 copy-done.2
  4.5 1.0 copy-done.3
  6.7 2.6 %collective-permute-start.1 = (f32[264,128]{1,0:T(8,128)S(1)}, f32[264,128]{1,0:T(8,128)S(1)}, u32[]{:S(2)}, u32[]{:S(2)}) collective-permute-start(f32[264,128]{1,0:T(8,128)S(1)} %get-tuple-element.31), channel_id=1, source_target_pairs={{0,2},{2,0},{1,3},{3,1},{4,6},{6,4},{5,7},{7,5},{8,10},{10,8},{9,1... | collective-permute-start | bytes 405512 | tf_op jit(solution)/shard_map/ppermute | solution.py:37
  11.9 1.5 %collective-permute-done.1.refs_3_.refs_5_ = f32[264,128]{1,0:T(8,128)S(1)} collective-permute-done((f32[264,128]{1,0:T(8,128)S(1)}, f32[264,128]{1,0:T(8,128)S(1)}, u32[]{:S(2)}, u32[]{:S(2)}) %collective-permute-start.1) | collective-permute-done | bytes 135200 | tf_op jit(solution)/shard_map/ppermute | solution.py:37
  13.5 2.5 %forward.1 = (f32[136,128]{1,0:T(8,128)S(1)}, f32[136,128]{1,0:T(8,128)S(1)}, f32[136,128]{1,0:T(8,128)S(1)}, f32[136,128]{1,0:T(8,128)S(1)}, f32[512,512]{1,0:T(8,128)S(1)}, /*index=5*/f32[8,512]{1,0:T(8,128)S(1)}) custom-call(s32[10]{0:T(128)S(1)} %stack.64.number_ref, f32[520,128]{1,0:T(8,128)S(1)} %get-tuple-element.28.refs_0_.refs_2_, ...), custom_call_target="tpu_custom_call" | custom-call | flops 805306368 | bytes 1048576 | tf_op jit(solution)/shard_map/forward/pallas_call | solution.py:63
  16.0 1.9 %collective-permute-start.3 = (f32[136,128]{1,0:T(8,128)S(1)}, f32[136,128]{1,0:T(8,128)S(1)}, u32[]{:S(2)}, u32[]{:S(2)}) collective-permute-start(f32[136,128]{1,0:T(8,128)S(1)} %get-tuple-element.36), channel_id=1, source_target_pairs={{0,8},{4,12},{8,16},{12,20},{16,24},{20,28},{24,0},{28,4},{1,9},{5... | collective-permute-start | bytes 208904 | tf_op jit(solution)/shard_map/ppermute | solution.py:37
  17.8 2.6 %collective-permute-start.4 = (f32[136,128]{1,0:T(8,128)S(1)}, f32[136,128]{1,0:T(8,128)S(1)}, u32[]{:S(2)}, u32[]{:S(2)}) collective-permute-start(f32[136,128]{1,0:T(8,128)S(1)} %get-tuple-element.37), channel_id=1, source_target_pairs={{0,16},{4,20},{8,24},{12,28},{16,0},{20,4},{24,8},{28,12},{1,17},{... | collective-permute-start | bytes 208904 | tf_op jit(solution)/shard_map/ppermute | solution.py:37
  20.4 1.3 %collective-permute-start.5 = (f32[136,128]{1,0:T(8,128)S(1)}, f32[136,128]{1,0:T(8,128)S(1)}, u32[]{:S(2)}, u32[]{:S(2)}) collective-permute-start(f32[136,128]{1,0:T(8,128)S(1)} %get-tuple-element.38), channel_id=1, source_target_pairs={{0,24},{4,28},{8,0},{12,4},{16,8},{20,12},{24,16},{28,20},{1,25},{... | collective-permute-start | bytes 208904 | tf_op jit(solution)/shard_map/ppermute | solution.py:37
  22.6 2.6 %collective-permute-done.4.refs_2_ = f32[136,128]{1,0:T(8,128)S(1)} collective-permute-done((f32[136,128]{1,0:T(8,128)S(1)}, f32[136,128]{1,0:T(8,128)S(1)}, u32[]{:S(2)}, u32[]{:S(2)}) %collective-permute-start.4) | collective-permute-done | bytes 69664 | tf_op jit(solution)/shard_map/ppermute | solution.py:37
  25.8 3.3 %collective-permute-start.8 = (f32[136,128]{1,0:T(8,128)S(1)}, f32[136,128]{1,0:T(8,128)S(1)}, u32[]{:S(2)}, u32[]{:S(2)}) collective-permute-start(f32[136,128]{1,0:T(8,128)S(1)} %merge.2.refs_6_), channel_id=1, source_target_pairs={{0,24},{4,28},{8,0},{12,4},{16,8},{20,12},{24,16},{28,20},{1,25},{... | collective-permute-start | bytes 208904 | tf_op jit(solution)/shard_map/ppermute | solution.py:37
  29.1 1.8 %collective-permute-start.6 = (f32[136,128]{1,0:T(8,128)S(1)}, f32[136,128]{1,0:T(8,128)S(1)}, u32[]{:S(2)}, u32[]{:S(2)}) collective-permute-start(f32[136,128]{1,0:T(8,128)S(1)} %merge.2.refs_6_), channel_id=1, source_target_pairs={{0,8},{4,12},{8,16},{12,20},{16,24},{20,28},{24,0},{28,4},{1,9},{5... | collective-permute-start | bytes 208904 | tf_op jit(solution)/shard_map/ppermute | solution.py:37
  31.0 4.5 %collective-permute-done.7.refs_8_ = f32[136,128]{1,0:T(8,128)S(1)} collective-permute-done((f32[136,128]{1,0:T(8,128)S(1)}, f32[136,128]{1,0:T(8,128)S(1)}, u32[]{:S(2)}, u32[]{:S(2)}) %collective-permute-start.7) | collective-permute-done | bytes 69664 | tf_op jit(solution)/shard_map/ppermute | solution.py:37
  35.6 3.9 %backward.2 = (f32[520,128]{1,0:T(8,128)S(1)}, f32[520,128]{1,0:T(8,128)S(1)}, f32[8,128]{1,0:T(8,128)S(1)}) custom-call(s32[10]{0:T(128)S(1)} %stack.64.number_ref, f32[512,512]{1,0:T(8,128)S(1)} %get-tuple-element.32.refs_0_, f32[8,512]{1,0:T(8,128)S(1)} %get-tuple-element.33.refs_1_, f32[520,128]{1,0:T(8,128)S(1)} %get-tuple-element.28.refs_0_.refs_2_, ...), custom_call_target="tpu_custom_call" | custom-call | flops 1207959552 | bytes 1048576 | tf_op jit(solution)/shard_map/backward/pallas_call | solution.py:63
  39.6 2.7 %collective-permute-start.14 = (f32[8,128]{1,0:T(8,128)S(1)}, f32[8,128]{1,0:T(8,128)S(1)}, u32[]{:S(2)}, u32[]{:S(2)}) collective-permute-start(f32[8,128]{1,0:T(8,128)S(1)} %get-tuple-element.41), channel_id=1, source_target_pairs={{0,6},{1,7},{2,4},{3,5},{4,2},{5,3},{6,0},{7,1},{8,14},{9,15},{10,... | collective-permute-start | bytes 12296 | tf_op jit(solution)/shard_map/ppermute | solution.py:37
  42.9 2.6 %collective-permute-start.11 = (f32[8,128]{1,0:T(8,128)S(1)}, f32[8,128]{1,0:T(8,128)S(1)}, u32[]{:S(2)}, u32[]{:S(2)}) collective-permute-start(f32[8,128]{1,0:T(8,128)S(1)} %get-tuple-element.41), channel_id=1, source_target_pairs={{0,3},{1,2},{2,1},{3,0},{4,7},{5,6},{6,5},{7,4},{8,11},{9,10},{10,... | collective-permute-start | bytes 12296 | tf_op jit(solution)/shard_map/ppermute | solution.py:37
  46.7 0.7 collective-permute-done.11
  47.4 1.7 %collective-permute-done.10 = f32[8,128]{1,0:T(8,128)S(1)} collective-permute-done((f32[8,128]{1,0:T(8,128)S(1)}, f32[8,128]{1,0:T(8,128)S(1)}, u32[]{:S(2)}, u32[]{:S(2)}) %collective-permute-start.10) | collective-permute-done | bytes 4128 | tf_op jit(solution)/shard_map/ppermute | solution.py:37
  49.6 1.0 collective-permute-start.18
  50.7 1.8 %collective-permute-start.16 = (f32[8,128]{1,0:T(8,128)S(1)}, f32[8,128]{1,0:T(8,128)S(1)}, u32[]{:S(2)}, u32[]{:S(2)}) collective-permute-start(f32[8,128]{1,0:T(8,128)S(1)} %add_add_fusion.1.refs_6_), channel_id=1, source_target_pairs={{0,8},{4,12},{8,16},{12,20},{16,24},{20,28},{24,0},{28,4},{1,9},{5... | collective-permute-start | bytes 12296 | tf_op jit(solution)/shard_map/ppermute | solution.py:37
  52.5 0.8 collective-permute-done.18.refs_9_
  53.3 1.9 %collective-permute-done.17.refs_8_ = f32[8,128]{1,0:T(8,128)S(1)} collective-permute-done((f32[8,128]{1,0:T(8,128)S(1)}, f32[8,128]{1,0:T(8,128)S(1)}, u32[]{:S(2)}, u32[]{:S(2)}) %collective-permute-start.17) | collective-permute-done | bytes 4128 | tf_op jit(solution)/shard_map/ppermute | solution.py:37
  55.2 1.0 collective-permute-done.16.refs_7_
  56.1 2.5 %update_forward.1 = (f32[520,128]{1,0:T(8,128)S(1)}, f32[520,128]{1,0:T(8,128)S(1)}, f32[136,128]{1,0:T(8,128)S(1)}, f32[136,128]{1,0:T(8,128)S(1)}, f32[136,128...) custom-call(s32[10]{0:T(128)S(1)} %stack.64.number_ref, ...), custom_call_target="tpu_custom_call" | custom-call | flops 805306368 | bytes 1048576 | tf_op jit(solution)/shard_map/update_forward/pallas_call | solution.py:63
  58.8 2.0 %collective-permute-start.23 = (f32[136,128]{1,0:T(8,128)S(1)}, f32[136,128]{1,0:T(8,128)S(1)}, u32[]{:S(2)}, u32[]{:S(2)}) collective-permute-start(f32[136,128]{1,0:T(8,128)S(1)} %get-tuple-element.48), channel_id=1, source_target_pairs={{0,16},{4,20},{8,24},{12,28},{16,0},{20,4},{24,8},{28,12},{1,17},{... | collective-permute-start | bytes 208904 | tf_op jit(solution)/shard_map/ppermute | solution.py:37
  60.8 1.9 %collective-permute-start.24 = (f32[136,128]{1,0:T(8,128)S(1)}, f32[136,128]{1,0:T(8,128)S(1)}, u32[]{:S(2)}, u32[]{:S(2)}) collective-permute-start(f32[136,128]{1,0:T(8,128)S(1)} %get-tuple-element.49), channel_id=1, source_target_pairs={{0,24},{4,28},{8,0},{12,4},{16,8},{20,12},{24,16},{28,20},{1,25},{... | collective-permute-start | bytes 208904 | tf_op jit(solution)/shard_map/ppermute | solution.py:37
  62.7 2.2 %collective-permute-done.22.refs_1_ = f32[136,128]{1,0:T(8,128)S(1)} collective-permute-done((f32[136,128]{1,0:T(8,128)S(1)}, f32[136,128]{1,0:T(8,128)S(1)}, u32[]{:S(2)}, u32[]{:S(2)}) %collective-permute-start.22) | collective-permute-done | bytes 69664 | tf_op jit(solution)/shard_map/ppermute | solution.py:37
  64.9 1.5 %collective-permute-done.24.refs_3_ = f32[136,128]{1,0:T(8,128)S(1)} collective-permute-done((f32[136,128]{1,0:T(8,128)S(1)}, f32[136,128]{1,0:T(8,128)S(1)}, u32[]{:S(2)}, u32[]{:S(2)}) %collective-permute-start.24) | collective-permute-done | bytes 69664 | tf_op jit(solution)/shard_map/ppermute | solution.py:37
  67.0 2.6 %collective-permute-start.27 = (f32[136,128]{1,0:T(8,128)S(1)}, f32[136,128]{1,0:T(8,128)S(1)}, u32[]{:S(2)}, u32[]{:S(2)}) collective-permute-start(f32[136,128]{1,0:T(8,128)S(1)} %merge.3.refs_6_), channel_id=1, source_target_pairs={{0,24},{4,28},{8,0},{12,4},{16,8},{20,12},{24,16},{28,20},{1,25},{... | collective-permute-start | bytes 208904 | tf_op jit(solution)/shard_map/ppermute | solution.py:37
  70.2 2.2 %collective-permute-start.20 = (f32[520,128]{1,0:T(8,128)S(1)}, f32[520,128]{1,0:T(8,128)S(1)}, u32[]{:S(2)}, u32[]{:S(2)}) collective-permute-start(f32[520,128]{1,0:T(8,128)S(1)} %get-tuple-element.42.refs_2_.refs_0_), channel_id=1, source_target_pairs={{0,2},{2,0},{4,6},{6,4},{8,10},{10,8},{12,14},{14,12},{16,18},{18,... | collective-permute-start | bytes 798728 | tf_op jit(solution)/shard_map/ppermute | solution.py:37
  72.3 2.4 %collective-permute-done.26.refs_8_ = f32[136,128]{1,0:T(8,128)S(1)} collective-permute-done((f32[136,128]{1,0:T(8,128)S(1)}, f32[136,128]{1,0:T(8,128)S(1)}, u32[]{:S(2)}, u32[]{:S(2)}) %collective-permute-start.26) | collective-permute-done | bytes 69664 | tf_op jit(solution)/shard_map/ppermute | solution.py:37
  74.7 1.2 %collective-permute-done.25.refs_7_ = f32[136,128]{1,0:T(8,128)S(1)} collective-permute-done((f32[136,128]{1,0:T(8,128)S(1)}, f32[136,128]{1,0:T(8,128)S(1)}, u32[]{:S(2)}, u32[]{:S(2)}) %collective-permute-start.25) | collective-permute-done | bytes 69664 | tf_op jit(solution)/shard_map/ppermute | solution.py:37
  76.0 3.9 %backward.3 = (f32[520,128]{1,0:T(8,128)S(1)}, f32[520,128]{1,0:T(8,128)S(1)}, f32[8,128]{1,0:T(8,128)S(1)}) custom-call(s32[10]{0:T(128)S(1)} %stack.64.number_ref, f32[512,512]{1,0:T(8,128)S(1)} %get-tuple-element.44.refs_0_, f32[8,512]{1,0:T(8,128)S(1)} %get-tuple-element.45.refs_1_, f32[520,128]{1,0:T(8,128)S(1)} %get-tuple-element.42.refs_2_.refs_0_, ...), custom_call_target="tpu_custom_call" | custom-call | flops 1207959552 | bytes 1048576 | tf_op jit(solution)/shard_map/backward/pallas_call | solution.py:63
  80.0 2.8 %collective-permute-start.36 = (f32[8,128]{1,0:T(8,128)S(1)}, f32[8,128]{1,0:T(8,128)S(1)}, u32[]{:S(2)}, u32[]{:S(2)}) collective-permute-start(f32[8,128]{1,0:T(8,128)S(1)} %get-tuple-element.52), channel_id=1, source_target_pairs={{0,6},{1,7},{2,4},{3,5},{4,2},{5,3},{6,0},{7,1},{8,14},{9,15},{10,... | collective-permute-start | bytes 12296 | tf_op jit(solution)/shard_map/ppermute | solution.py:37
  82.8 0.8 collective-permute-start.35
  83.9 2.4 %collective-permute-start.33 = (f32[8,128]{1,0:T(8,128)S(1)}, f32[8,128]{1,0:T(8,128)S(1)}, u32[]{:S(2)}, u32[]{:S(2)}) collective-permute-start(f32[8,128]{1,0:T(8,128)S(1)} %get-tuple-element.52), channel_id=1, source_target_pairs={{0,3},{1,2},{2,1},{3,0},{4,7},{5,6},{6,5},{7,4},{8,11},{9,10},{10,... | collective-permute-start | bytes 12296 | tf_op jit(solution)/shard_map/ppermute | solution.py:37
  87.0 0.9 collective-permute-start.31
  88.4 1.5 %collective-permute-done.32 = f32[8,128]{1,0:T(8,128)S(1)} collective-permute-done((f32[8,128]{1,0:T(8,128)S(1)}, f32[8,128]{1,0:T(8,128)S(1)}, u32[]{:S(2)}, u32[]{:S(2)}) %collective-permute-start.32) | collective-permute-done | bytes 4128 | tf_op jit(solution)/shard_map/ppermute | solution.py:37
  91.1 1.6 %collective-permute-start.38 = (f32[8,128]{1,0:T(8,128)S(1)}, f32[8,128]{1,0:T(8,128)S(1)}, u32[]{:S(2)}, u32[]{:S(2)}) collective-permute-start(f32[8,128]{1,0:T(8,128)S(1)} %add_add_fusion.refs_8_), channel_id=1, source_target_pairs={{0,8},{4,12},{8,16},{12,20},{16,24},{20,28},{24,0},{28,4},{1,9},{5... | collective-permute-start | bytes 12296 | tf_op jit(solution)/shard_map/ppermute | solution.py:37
  92.7 1.6 %collective-permute-done.40.refs_11_ = f32[8,128]{1,0:T(8,128)S(1)} collective-permute-done((f32[8,128]{1,0:T(8,128)S(1)}, f32[8,128]{1,0:T(8,128)S(1)}, u32[]{:S(2)}, u32[]{:S(2)}) %collective-permute-start.40) | collective-permute-done | bytes 4128 | tf_op jit(solution)/shard_map/ppermute | solution.py:37
  94.3 1.0 collective-permute-done.39.refs_10_
  95.3 1.4 %collective-permute-start.29 = (f32[520,128]{1,0:T(8,128)S(1)}, f32[520,128]{1,0:T(8,128)S(1)}, u32[]{:S(2)}, u32[]{:S(2)}) collective-permute-start(f32[520,128]{1,0:T(8,128)S(1)} %get-tuple-element.50.refs_4_), channel_id=1, source_target_pairs={{0,2},{2,0},{4,6},{6,4},{8,10},{10,8},{12,14},{14,12},{16,18},{18,... | collective-permute-start | bytes 798728 | tf_op jit(solution)/shard_map/ppermute | solution.py:37
  96.7 1.5 %collective-permute-start.28 = (f32[520,128]{1,0:T(8,128)S(1)}, f32[520,128]{1,0:T(8,128)S(1)}, u32[]{:S(2)}, u32[]{:S(2)}) collective-permute-start(f32[520,128]{1,0:T(8,128)S(1)} %get-tuple-element.51), channel_id=1, source_target_pairs={{0,4},{2,6},{4,0},{6,2},{8,12},{10,14},{12,8},{14,10},{16,20},{18,... | collective-permute-start | bytes 798728 | tf_op jit(solution)/shard_map/ppermute | solution.py:37
  98.3 3.1 %collective-permute-done.21.refs_3_ = f32[520,128]{1,0:T(8,128)S(1)} collective-permute-done((f32[520,128]{1,0:T(8,128)S(1)}, f32[520,128]{1,0:T(8,128)S(1)}, u32[]{:S(2)}, u32[]{:S(2)}) %collective-permute-start.21) | collective-permute-done | bytes 266272 | tf_op jit(solution)/shard_map/ppermute | solution.py:37
  101.4 5.6 %collective-permute-done.29.refs_6_ = f32[520,128]{1,0:T(8,128)S(1)} collective-permute-done((f32[520,128]{1,0:T(8,128)S(1)}, f32[520,128]{1,0:T(8,128)S(1)}, u32[]{:S(2)}, u32[]{:S(2)}) %collective-permute-start.29) | collective-permute-done | bytes 266272 | tf_op jit(solution)/shard_map/ppermute | solution.py:37
  107.0 5.8 %collective-permute-done.30.refs_7_ = f32[520,128]{1,0:T(8,128)S(1)} collective-permute-done((f32[520,128]{1,0:T(8,128)S(1)}, f32[520,128]{1,0:T(8,128)S(1)}, u32[]{:S(2)}, u32[]{:S(2)}) %collective-permute-start.30) | collective-permute-done | bytes 266272 | tf_op jit(solution)/shard_map/ppermute | solution.py:37
  112.7 1.7 %last_update.1 = (f32[4,256,128]{2,1,0:T(8,128)}, f32[4,256,128]{2,1,0:T(8,128)}, f32[4,256]{1,0:T(4,128)}) custom-call(s32[4]{0:T(128)S(1)} %pad_add_fusion.number_ref, f32[520,128]{1,0:T(8,128)S(1)} %get-tuple-element.42.refs_2_.refs_0_, f32[520,128]{1,0:T(8,128)S(1)} %collective-permute-done.19.refs_1_, f32[520,128]{1,0:T(8,128)S(1)} %collective-permute-done.20.refs_2_, ...), custom_call_target="tpu_custom_call" | custom-call | flops 1048576 | bytes 1048576 | tf_op jit(solution)/shard_map/last_update/pallas_call | solution.py:63
  (62 shorter events, 11.4 us)
Async XLA Ops:
  0.7 0.7 copy-start.4
  0.7 0.7 copy-start.5
  1.4 1.0 copy-start
  2.5 1.0 copy-start.1
  3.5 1.0 copy-start.2
  4.5 1.0 copy-start.3
  6.2 7.3 %collective-permute-start = (f32[520,128]{1,0:T(8,128)S(1)}, f32[520,128]{1,0:T(8,128)S(1)}, u32[]{:S(2)}, u32[]{:S(2)}) collective-permute-start(f32[520,128]{1,0:T(8,128)S(1)} %get-tuple-element.29), channel_id=1, source_target_pairs={{0,4},{4,0},{8,12},{12,8},{16,20},{20,16},{24,28},{28,24},{1,5},{5... | collective-permute-start | bytes 798728 | tf_op jit(solution)/shard_map/ppermute | solution.py:37
  6.7 6.8 %collective-permute-start.1 = (f32[264,128]{1,0:T(8,128)S(1)}, f32[264,128]{1,0:T(8,128)S(1)}, u32[]{:S(2)}, u32[]{:S(2)}) collective-permute-start(f32[264,128]{1,0:T(8,128)S(1)} %get-tuple-element.31), channel_id=1, source_target_pairs={{0,2},{2,0},{1,3},{3,1},{4,6},{6,4},{5,7},{7,5},{8,10},{10,8},{9,1... | collective-permute-start | bytes 405512 | tf_op jit(solution)/shard_map/ppermute | solution.py:37
  9.3 0.7 copy-start.6
  16.0 6.6 %collective-permute-start.3 = (f32[136,128]{1,0:T(8,128)S(1)}, f32[136,128]{1,0:T(8,128)S(1)}, u32[]{:S(2)}, u32[]{:S(2)}) collective-permute-start(f32[136,128]{1,0:T(8,128)S(1)} %get-tuple-element.36), channel_id=1, source_target_pairs={{0,8},{4,12},{8,16},{12,20},{16,24},{20,28},{24,0},{28,4},{1,9},{5... | collective-permute-start | bytes 208904 | tf_op jit(solution)/shard_map/ppermute | solution.py:37
  17.8 7.3 %collective-permute-start.4 = (f32[136,128]{1,0:T(8,128)S(1)}, f32[136,128]{1,0:T(8,128)S(1)}, u32[]{:S(2)}, u32[]{:S(2)}) collective-permute-start(f32[136,128]{1,0:T(8,128)S(1)} %get-tuple-element.37), channel_id=1, source_target_pairs={{0,16},{4,20},{8,24},{12,28},{16,0},{20,4},{24,8},{28,12},{1,17},{... | collective-permute-start | bytes 208904 | tf_op jit(solution)/shard_map/ppermute | solution.py:37
  20.4 4.7 %collective-permute-start.5 = (f32[136,128]{1,0:T(8,128)S(1)}, f32[136,128]{1,0:T(8,128)S(1)}, u32[]{:S(2)}, u32[]{:S(2)}) collective-permute-start(f32[136,128]{1,0:T(8,128)S(1)} %get-tuple-element.38), channel_id=1, source_target_pairs={{0,24},{4,28},{8,0},{12,4},{16,8},{20,12},{24,16},{28,20},{1,25},{... | collective-permute-start | bytes 208904 | tf_op jit(solution)/shard_map/ppermute | solution.py:37
  21.8 0.7 collective-permute-start.2
  25.8 5.2 %collective-permute-start.8 = (f32[136,128]{1,0:T(8,128)S(1)}, f32[136,128]{1,0:T(8,128)S(1)}, u32[]{:S(2)}, u32[]{:S(2)}) collective-permute-start(f32[136,128]{1,0:T(8,128)S(1)} %merge.2.refs_6_), channel_id=1, source_target_pairs={{0,24},{4,28},{8,0},{12,4},{16,8},{20,12},{24,16},{28,20},{1,25},{... | collective-permute-start | bytes 208904 | tf_op jit(solution)/shard_map/ppermute | solution.py:37
  29.1 6.5 %collective-permute-start.7 = (f32[136,128]{1,0:T(8,128)S(1)}, f32[136,128]{1,0:T(8,128)S(1)}, u32[]{:S(2)}, u32[]{:S(2)}) collective-permute-start(f32[136,128]{1,0:T(8,128)S(1)} %merge.2.refs_6_), channel_id=1, source_target_pairs={{0,16},{4,20},{8,24},{12,28},{16,0},{20,4},{24,8},{28,12},{1,17},{... | collective-permute-start | bytes 208904 | tf_op jit(solution)/shard_map/ppermute | solution.py:37
  29.1 6.5 %collective-permute-start.6 = (f32[136,128]{1,0:T(8,128)S(1)}, f32[136,128]{1,0:T(8,128)S(1)}, u32[]{:S(2)}, u32[]{:S(2)}) collective-permute-start(f32[136,128]{1,0:T(8,128)S(1)} %merge.2.refs_6_), channel_id=1, source_target_pairs={{0,8},{4,12},{8,16},{12,20},{16,24},{20,28},{24,0},{28,4},{1,9},{5... | collective-permute-start | bytes 208904 | tf_op jit(solution)/shard_map/ppermute | solution.py:37
  39.5 6.0 %collective-permute-start.15 = (f32[8,128]{1,0:T(8,128)S(1)}, f32[8,128]{1,0:T(8,128)S(1)}, u32[]{:S(2)}, u32[]{:S(2)}) collective-permute-start(f32[8,128]{1,0:T(8,128)S(1)} %get-tuple-element.41), channel_id=1, source_target_pairs={{0,7},{1,6},{2,5},{3,4},{4,3},{5,2},{6,1},{7,0},{8,15},{9,14},{10,... | collective-permute-start | bytes 12296 | tf_op jit(solution)/shard_map/ppermute | solution.py:37
  39.6 6.3 %collective-permute-start.14 = (f32[8,128]{1,0:T(8,128)S(1)}, f32[8,128]{1,0:T(8,128)S(1)}, u32[]{:S(2)}, u32[]{:S(2)}) collective-permute-start(f32[8,128]{1,0:T(8,128)S(1)} %get-tuple-element.41), channel_id=1, source_target_pairs={{0,6},{1,7},{2,4},{3,5},{4,2},{5,3},{6,0},{7,1},{8,14},{9,15},{10,... | collective-permute-start | bytes 12296 | tf_op jit(solution)/shard_map/ppermute | solution.py:37
  42.4 4.3 %collective-permute-start.13 = (f32[8,128]{1,0:T(8,128)S(1)}, f32[8,128]{1,0:T(8,128)S(1)}, u32[]{:S(2)}, u32[]{:S(2)}) collective-permute-start(f32[8,128]{1,0:T(8,128)S(1)} %get-tuple-element.41), channel_id=1, source_target_pairs={{0,5},{1,4},{2,7},{3,6},{4,1},{5,0},{6,3},{7,2},{8,13},{9,12},{10,... | collective-permute-start | bytes 12296 | tf_op jit(solution)/shard_map/ppermute | solution.py:37
  42.5 4.1 %collective-permute-start.12 = (f32[8,128]{1,0:T(8,128)S(1)}, f32[8,128]{1,0:T(8,128)S(1)}, u32[]{:S(2)}, u32[]{:S(2)}) collective-permute-start(f32[8,128]{1,0:T(8,128)S(1)} %get-tuple-element.41), channel_id=1, source_target_pairs={{0,4},{1,5},{2,6},{3,7},{4,0},{5,1},{6,2},{7,3},{8,12},{9,13},{10,... | collective-permute-start | bytes 12296 | tf_op jit(solution)/shard_map/ppermute | solution.py:37
  42.9 4.5 %collective-permute-start.11 = (f32[8,128]{1,0:T(8,128)S(1)}, f32[8,128]{1,0:T(8,128)S(1)}, u32[]{:S(2)}, u32[]{:S(2)}) collective-permute-start(f32[8,128]{1,0:T(8,128)S(1)} %get-tuple-element.41), channel_id=1, source_target_pairs={{0,3},{1,2},{2,1},{3,0},{4,7},{5,6},{6,5},{7,4},{8,11},{9,10},{10,... | collective-permute-start | bytes 12296 | tf_op jit(solution)/shard_map/ppermute | solution.py:37
  45.5 3.6 %collective-permute-start.10 = (f32[8,128]{1,0:T(8,128)S(1)}, f32[8,128]{1,0:T(8,128)S(1)}, u32[]{:S(2)}, u32[]{:S(2)}) collective-permute-start(f32[8,128]{1,0:T(8,128)S(1)} %get-tuple-element.41), channel_id=1, source_target_pairs={{0,2},{1,3},{2,0},{3,1},{4,6},{5,7},{6,4},{7,5},{8,10},{9,11},{10,... | collective-permute-start | bytes 12296 | tf_op jit(solution)/shard_map/ppermute | solution.py:37
  46.0 3.6 %collective-permute-start.9 = (f32[8,128]{1,0:T(8,128)S(1)}, f32[8,128]{1,0:T(8,128)S(1)}, u32[]{:S(2)}, u32[]{:S(2)}) collective-permute-start(f32[8,128]{1,0:T(8,128)S(1)} %get-tuple-element.41), channel_id=1, source_target_pairs={{0,1},{1,0},{2,3},{3,2},{4,5},{5,4},{6,7},{7,6},{8,9},{9,8},{10,11... | collective-permute-start | bytes 12296 | tf_op jit(solution)/shard_map/ppermute | solution.py:37
  49.6 3.7 %collective-permute-start.18 = (f32[8,128]{1,0:T(8,128)S(1)}, f32[8,128]{1,0:T(8,128)S(1)}, u32[]{:S(2)}, u32[]{:S(2)}) collective-permute-start(f32[8,128]{1,0:T(8,128)S(1)} %add_add_fusion.1.refs_6_), channel_id=1, source_target_pairs={{0,24},{4,28},{8,0},{12,4},{16,8},{20,12},{24,16},{28,20},{1,25},{... | collective-permute-start | bytes 12296 | tf_op jit(solution)/shard_map/ppermute | solution.py:37
  50.6 4.5 %collective-permute-start.17 = (f32[8,128]{1,0:T(8,128)S(1)}, f32[8,128]{1,0:T(8,128)S(1)}, u32[]{:S(2)}, u32[]{:S(2)}) collective-permute-start(f32[8,128]{1,0:T(8,128)S(1)} %add_add_fusion.1.refs_6_), channel_id=1, source_target_pairs={{0,16},{4,20},{8,24},{12,28},{16,0},{20,4},{24,8},{28,12},{1,17},{... | collective-permute-start | bytes 12296 | tf_op jit(solution)/shard_map/ppermute | solution.py:37
  50.7 5.4 %collective-permute-start.16 = (f32[8,128]{1,0:T(8,128)S(1)}, f32[8,128]{1,0:T(8,128)S(1)}, u32[]{:S(2)}, u32[]{:S(2)}) collective-permute-start(f32[8,128]{1,0:T(8,128)S(1)} %add_add_fusion.1.refs_6_), channel_id=1, source_target_pairs={{0,8},{4,12},{8,16},{12,20},{16,24},{20,28},{24,0},{28,4},{1,9},{5... | collective-permute-start | bytes 12296 | tf_op jit(solution)/shard_map/ppermute | solution.py:37
  58.7 6.2 %collective-permute-start.22 = (f32[136,128]{1,0:T(8,128)S(1)}, f32[136,128]{1,0:T(8,128)S(1)}, u32[]{:S(2)}, u32[]{:S(2)}) collective-permute-start(f32[136,128]{1,0:T(8,128)S(1)} %get-tuple-element.47), channel_id=1, source_target_pairs={{0,8},{4,12},{8,16},{12,20},{16,24},{20,28},{24,0},{28,4},{1,9},{5... | collective-permute-start | bytes 208904 | tf_op jit(solution)/shard_map/ppermute | solution.py:37
  58.8 6.1 %collective-permute-start.23 = (f32[136,128]{1,0:T(8,128)S(1)}, f32[136,128]{1,0:T(8,128)S(1)}, u32[]{:S(2)}, u32[]{:S(2)}) collective-permute-start(f32[136,128]{1,0:T(8,128)S(1)} %get-tuple-element.48), channel_id=1, source_target_pairs={{0,16},{4,20},{8,24},{12,28},{16,0},{20,4},{24,8},{28,12},{1,17},{... | collective-permute-start | bytes 208904 | tf_op jit(solution)/shard_map/ppermute | solution.py:37
  60.8 5.5 %collective-permute-start.24 = (f32[136,128]{1,0:T(8,128)S(1)}, f32[136,128]{1,0:T(8,128)S(1)}, u32[]{:S(2)}, u32[]{:S(2)}) collective-permute-start(f32[136,128]{1,0:T(8,128)S(1)} %get-tuple-element.49), channel_id=1, source_target_pairs={{0,24},{4,28},{8,0},{12,4},{16,8},{20,12},{24,16},{28,20},{1,25},{... | collective-permute-start | bytes 208904 | tf_op jit(solution)/shard_map/ppermute | solution.py:37
  67.0 5.4 %collective-permute-start.27 = (f32[136,128]{1,0:T(8,128)S(1)}, f32[136,128]{1,0:T(8,128)S(1)}, u32[]{:S(2)}, u32[]{:S(2)}) collective-permute-start(f32[136,128]{1,0:T(8,128)S(1)} %merge.3.refs_6_), channel_id=1, source_target_pairs={{0,24},{4,28},{8,0},{12,4},{16,8},{20,12},{24,16},{28,20},{1,25},{... | collective-permute-start | bytes 208904 | tf_op jit(solution)/shard_map/ppermute | solution.py:37
  69.5 5.2 %collective-permute-start.26 = (f32[136,128]{1,0:T(8,128)S(1)}, f32[136,128]{1,0:T(8,128)S(1)}, u32[]{:S(2)}, u32[]{:S(2)}) collective-permute-start(f32[136,128]{1,0:T(8,128)S(1)} %merge.3.refs_6_), channel_id=1, source_target_pairs={{0,16},{4,20},{8,24},{12,28},{16,0},{20,4},{24,8},{28,12},{1,17},{... | collective-permute-start | bytes 208904 | tf_op jit(solution)/shard_map/ppermute | solution.py:37
  69.9 6.1 %collective-permute-start.25 = (f32[136,128]{1,0:T(8,128)S(1)}, f32[136,128]{1,0:T(8,128)S(1)}, u32[]{:S(2)}, u32[]{:S(2)}) collective-permute-start(f32[136,128]{1,0:T(8,128)S(1)} %merge.3.refs_6_), channel_id=1, source_target_pairs={{0,8},{4,12},{8,16},{12,20},{16,24},{20,28},{24,0},{28,4},{1,9},{5... | collective-permute-start | bytes 208904 | tf_op jit(solution)/shard_map/ppermute | solution.py:37
  70.2 26.5 %collective-permute-start.20 = (f32[520,128]{1,0:T(8,128)S(1)}, f32[520,128]{1,0:T(8,128)S(1)}, u32[]{:S(2)}, u32[]{:S(2)}) collective-permute-start(f32[520,128]{1,0:T(8,128)S(1)} %get-tuple-element.42.refs_2_.refs_0_), channel_id=1, source_target_pairs={{0,2},{2,0},{4,6},{6,4},{8,10},{10,8},{12,14},{14,12},{16,18},{18,... | collective-permute-start | bytes 798728 | tf_op jit(solution)/shard_map/ppermute | solution.py:37
  79.9 4.0 %collective-permute-start.37 = (f32[8,128]{1,0:T(8,128)S(1)}, f32[8,128]{1,0:T(8,128)S(1)}, u32[]{:S(2)}, u32[]{:S(2)}) collective-permute-start(f32[8,128]{1,0:T(8,128)S(1)} %get-tuple-element.52), channel_id=1, source_target_pairs={{0,7},{1,6},{2,5},{3,4},{4,3},{5,2},{6,1},{7,0},{8,15},{9,14},{10,... | collective-permute-start | bytes 12296 | tf_op jit(solution)/shard_map/ppermute | solution.py:37
  80.0 6.4 %collective-permute-start.36 = (f32[8,128]{1,0:T(8,128)S(1)}, f32[8,128]{1,0:T(8,128)S(1)}, u32[]{:S(2)}, u32[]{:S(2)}) collective-permute-start(f32[8,128]{1,0:T(8,128)S(1)} %get-tuple-element.52), channel_id=1, source_target_pairs={{0,6},{1,7},{2,4},{3,5},{4,2},{5,3},{6,0},{7,1},{8,14},{9,15},{10,... | collective-permute-start | bytes 12296 | tf_op jit(solution)/shard_map/ppermute | solution.py:37
  82.8 4.2 %collective-permute-start.35 = (f32[8,128]{1,0:T(8,128)S(1)}, f32[8,128]{1,0:T(8,128)S(1)}, u32[]{:S(2)}, u32[]{:S(2)}) collective-permute-start(f32[8,128]{1,0:T(8,128)S(1)} %get-tuple-element.52), channel_id=1, source_target_pairs={{0,5},{1,4},{2,7},{3,6},{4,1},{5,0},{6,3},{7,2},{8,13},{9,12},{10,... | collective-permute-start | bytes 12296 | tf_op jit(solution)/shard_map/ppermute | solution.py:37
  83.6 4.3 %collective-permute-start.34 = (f32[8,128]{1,0:T(8,128)S(1)}, f32[8,128]{1,0:T(8,128)S(1)}, u32[]{:S(2)}, u32[]{:S(2)}) collective-permute-start(f32[8,128]{1,0:T(8,128)S(1)} %get-tuple-element.52), channel_id=1, source_target_pairs={{0,4},{1,5},{2,6},{3,7},{4,0},{5,1},{6,2},{7,3},{8,12},{9,13},{10,... | collective-permute-start | bytes 12296 | tf_op jit(solution)/shard_map/ppermute | solution.py:37
  83.9 4.5 %collective-permute-start.33 = (f32[8,128]{1,0:T(8,128)S(1)}, f32[8,128]{1,0:T(8,128)S(1)}, u32[]{:S(2)}, u32[]{:S(2)}) collective-permute-start(f32[8,128]{1,0:T(8,128)S(1)} %get-tuple-element.52), channel_id=1, source_target_pairs={{0,3},{1,2},{2,1},{3,0},{4,7},{5,6},{6,5},{7,4},{8,11},{9,10},{10,... | collective-permute-start | bytes 12296 | tf_op jit(solution)/shard_map/ppermute | solution.py:37
  86.3 3.6 %collective-permute-start.32 = (f32[8,128]{1,0:T(8,128)S(1)}, f32[8,128]{1,0:T(8,128)S(1)}, u32[]{:S(2)}, u32[]{:S(2)}) collective-permute-start(f32[8,128]{1,0:T(8,128)S(1)} %get-tuple-element.52), channel_id=1, source_target_pairs={{0,2},{1,3},{2,0},{3,1},{4,6},{5,7},{6,4},{7,5},{8,10},{9,11},{10,... | collective-permute-start | bytes 12296 | tf_op jit(solution)/shard_map/ppermute | solution.py:37
  87.0 3.6 %collective-permute-start.31 = (f32[8,128]{1,0:T(8,128)S(1)}, f32[8,128]{1,0:T(8,128)S(1)}, u32[]{:S(2)}, u32[]{:S(2)}) collective-permute-start(f32[8,128]{1,0:T(8,128)S(1)} %get-tuple-element.52), channel_id=1, source_target_pairs={{0,1},{1,0},{2,3},{3,2},{4,5},{5,4},{6,7},{7,6},{8,9},{9,8},{10,11... | collective-permute-start | bytes 12296 | tf_op jit(solution)/shard_map/ppermute | solution.py:37
  90.6 3.7 %collective-permute-start.40 = (f32[8,128]{1,0:T(8,128)S(1)}, f32[8,128]{1,0:T(8,128)S(1)}, u32[]{:S(2)}, u32[]{:S(2)}) collective-permute-start(f32[8,128]{1,0:T(8,128)S(1)} %add_add_fusion.refs_8_), channel_id=1, source_target_pairs={{0,24},{4,28},{8,0},{12,4},{16,8},{20,12},{24,16},{28,20},{1,25},{... | collective-permute-start | bytes 12296 | tf_op jit(solution)/shard_map/ppermute | solution.py:37
  90.7 4.6 %collective-permute-start.39 = (f32[8,128]{1,0:T(8,128)S(1)}, f32[8,128]{1,0:T(8,128)S(1)}, u32[]{:S(2)}, u32[]{:S(2)}) collective-permute-start(f32[8,128]{1,0:T(8,128)S(1)} %add_add_fusion.refs_8_), channel_id=1, source_target_pairs={{0,16},{4,20},{8,24},{12,28},{16,0},{20,4},{24,8},{28,12},{1,17},{... | collective-permute-start | bytes 12296 | tf_op jit(solution)/shard_map/ppermute | solution.py:37
  91.1 5.6 %collective-permute-start.38 = (f32[8,128]{1,0:T(8,128)S(1)}, f32[8,128]{1,0:T(8,128)S(1)}, u32[]{:S(2)}, u32[]{:S(2)}) collective-permute-start(f32[8,128]{1,0:T(8,128)S(1)} %add_add_fusion.refs_8_), channel_id=1, source_target_pairs={{0,8},{4,12},{8,16},{12,20},{16,24},{20,28},{24,0},{28,4},{1,9},{5... | collective-permute-start | bytes 12296 | tf_op jit(solution)/shard_map/ppermute | solution.py:37
  92.7 8.7 %collective-permute-start.21 = (f32[520,128]{1,0:T(8,128)S(1)}, f32[520,128]{1,0:T(8,128)S(1)}, u32[]{:S(2)}, u32[]{:S(2)}) collective-permute-start(f32[520,128]{1,0:T(8,128)S(1)} %get-tuple-element.43.refs_3_), channel_id=1, source_target_pairs={{0,6},{2,4},{4,2},{6,0},{8,14},{10,12},{12,10},{14,8},{16,22},{18,... | collective-permute-start | bytes 798728 | tf_op jit(solution)/shard_map/ppermute | solution.py:37
  94.3 7.1 %collective-permute-start.19 = (f32[520,128]{1,0:T(8,128)S(1)}, f32[520,128]{1,0:T(8,128)S(1)}, u32[]{:S(2)}, u32[]{:S(2)}) collective-permute-start(f32[520,128]{1,0:T(8,128)S(1)} %get-tuple-element.43.refs_3_), channel_id=1, source_target_pairs={{0,4},{2,6},{4,0},{6,2},{8,12},{10,14},{12,8},{14,10},{16,20},{18,... | collective-permute-start | bytes 798728 | tf_op jit(solution)/shard_map/ppermute | solution.py:37
  95.3 11.7 %collective-permute-start.29 = (f32[520,128]{1,0:T(8,128)S(1)}, f32[520,128]{1,0:T(8,128)S(1)}, u32[]{:S(2)}, u32[]{:S(2)}) collective-permute-start(f32[520,128]{1,0:T(8,128)S(1)} %get-tuple-element.50.refs_4_), channel_id=1, source_target_pairs={{0,2},{2,0},{4,6},{6,4},{8,10},{10,8},{12,14},{14,12},{16,18},{18,... | collective-permute-start | bytes 798728 | tf_op jit(solution)/shard_map/ppermute | solution.py:37
  96.7 16.0 %collective-permute-start.30 = (f32[520,128]{1,0:T(8,128)S(1)}, f32[520,128]{1,0:T(8,128)S(1)}, u32[]{:S(2)}, u32[]{:S(2)}) collective-permute-start(f32[520,128]{1,0:T(8,128)S(1)} %get-tuple-element.51), channel_id=1, source_target_pairs={{0,6},{2,4},{4,2},{6,0},{8,14},{10,12},{12,10},{14,8},{16,22},{18,... | collective-permute-start | bytes 798728 | tf_op jit(solution)/shard_map/ppermute | solution.py:37
  96.7 16.0 %collective-permute-start.28 = (f32[520,128]{1,0:T(8,128)S(1)}, f32[520,128]{1,0:T(8,128)S(1)}, u32[]{:S(2)}, u32[]{:S(2)}) collective-permute-start(f32[520,128]{1,0:T(8,128)S(1)} %get-tuple-element.51), channel_id=1, source_target_pairs={{0,4},{2,6},{4,0},{6,2},{8,12},{10,14},{12,8},{14,10},{16,20},{18,... | collective-permute-start | bytes 798728 | tf_op jit(solution)/shard_map/ppermute | solution.py:37

commit v2 on v1

--- a/solution.py
+++ b/solution.py
@@ -22,17 +22,19 @@
 CORES = 2
 
 
-def send(value, axes, move):
+def exchange(value, **masks):
+    axes = tuple(masks)
     sizes = [lax.axis_size(axis) for axis in axes]
 
     def flat(place):
         index = 0
         for size, at in zip(sizes, place):
-            index = index * size + at % size
+            index = index * size + at
         return index
 
     pairs = [
-        (flat(place), flat(move(*place))) for place in itertools.product(*map(range, sizes))
+        (flat(place), flat([at ^ mask for at, mask in zip(place, masks.values())]))
+        for place in itertools.product(*map(range, sizes))
     ]
     return lax.ppermute(value, axes, pairs)
 
@@ -47,33 +49,23 @@
     )
 
 
-def call(body, out_shapes, name, cost, scalars, blocks, scratch=()):
-    def whole(shape):
-        return pl.BlockSpec(shape, lambda step, numbers: (0,) * len(shape))
-
-    arrays, specs = [], []
-    for block in blocks:
-        if isinstance(block, tuple):
-            array, shape, index = block
-            arrays.append(array)
-            specs.append(pl.BlockSpec(shape, index))
-        else:
-            arrays.append(block)
-            specs.append(whole(block.shape))
+def call(body, out_shapes, name, cost, operands, spaces=(), scratch=(), after=()):
+    spaces = list(spaces) + [pltpu.VMEM] * (len(operands) - len(spaces)) + [pl.ANY] * len(after)
+    count = len(operands)
+
+    def without_after(*refs):
+        body(*refs[:count], *refs[count + len(after) :])
+
     return pl.pallas_call(
-        body,
+        without_after,
         out_shape=[jax.ShapeDtypeStruct(shape, jnp.float32) for shape in out_shapes],
-        grid_spec=pltpu.PrefetchScalarGridSpec(
-            num_scalar_prefetch=1,
-            grid=(1,),
-            in_specs=specs,
-            out_specs=[whole(shape) for shape in out_shapes],
-            scratch_shapes=scratch,
-        ),
-        compiler_params=pltpu.CompilerParams(vmem_limit_bytes=48 * 2**20),
+        in_specs=[pl.BlockSpec(memory_space=space) for space in spaces],
+        out_specs=[pl.BlockSpec(memory_space=pltpu.VMEM) for _ in out_shapes],
+        scratch_shapes=scratch,
+        compiler_params=pltpu.CompilerParams(vmem_limit_bytes=32 * 2**20),
         cost_estimate=pl.CostEstimate(flops=cost, bytes_accessed=2**20, transcendentals=0),
         name=name,
-    )(scalars, *arrays)
+    )(*operands, *after)
 
 
 def row_as_tail(row, width):
@@ -94,12 +86,15 @@
 
 
 def direct_plan_fits(mesh, queries, compact_keys):
-    pages, query_devices, head_devices = (mesh.shape[axis] for axis in ("page", "query", "head"))
+    sizes = [mesh.shape[axis] for axis in ("page", "query", "head")]
+    pages, query_devices, head_devices = sizes
     local_heads = queries.shape[0] // head_devices
     part_rows = queries.shape[1] // query_devices
     slot_rows = compact_keys.shape[1] // pages
     width = queries.shape[2]
-    if pages % CORES or local_heads != CORES * query_devices or width % 128:
+    if any(size & (size - 1) for size in sizes) or pages < CORES or width % 128:
+        return False
+    if local_heads != CORES * query_devices:
         return False
     ranks = pages // CORES
     chunk = part_rows * query_devices // ranks
@@ -130,90 +125,66 @@
     pos_rows = part_rows // width
     bias_rows = slot_rows // width
     packed_rows = 2 * slot_rows + TAIL
-    matmul_cost = 2 * slots * query_rows * width
-
-    page = lax.axis_index("page")
-    rank, core = page // CORES, page % CORES
-    me = lax.axis_index("query")
-    own_head = CORES * me + core
-
-    def part_of(z):
-        return z * chunk // part_rows
-
-    chunk_part = rank * chunk // part_rows
-    target_head = CORES * lax.rem(me - chunk_part + query_devices, query_devices) + core
-    target_block = lax.rem(rank, part_rows // chunk)
-    send_heads = [
-        CORES * lax.rem(me - turn + query_devices, query_devices) + core
-        for turn in range(1, query_devices)
-    ]
-    mate_head = CORES * me + (CORES - 1 - core)
-    mate_page = CORES * rank + (CORES - 1 - core)
-
-    prep_numbers = jnp.stack(
-        [own_head, mate_head, target_head, target_block, *send_heads]
-    ).astype(jnp.int32)
-
-    def prep_body(numbers, *refs):
-        positions_ref, bias_ref, targets_ref, *refs = refs
-        key_refs, refs = refs[:2], refs[2:]
-        value_refs, refs = refs[:2], refs[2:]
-        query_refs, refs = refs[:query_devices], refs[query_devices:]
+    packed_shapes = [(packed_rows, width)] * 2
+    matmul_cost = 6 * 2 * slots * query_rows * width
+
+    def places():
+        page = lax.axis_index("page")
+        return page // CORES, page % CORES, lax.axis_index("query")
+
+    def prep_body(queries, keys, values, bias_ref, targets, positions_ref, *refs):
         state_outs, refs = refs[:2], refs[2:]
-        query_outs, (targets_out,) = refs[:query_devices], refs[query_devices:]
+        query_outs, (targets_out, sems) = refs[:query_devices], refs[query_devices:]
+        rank, core, me = places()
+        copies = []
         for turn in range(query_devices):
-            head = numbers[0] if turn == 0 else numbers[3 + turn]
-            query_outs[turn][:part_rows, :] = query_refs[turn][0]
-            row = positions_ref[pl.ds(head, 1), :].astype(jnp.float32)
+            head = CORES * (me ^ turn) + core
+            copies.append((queries.at[head], query_outs[turn].at[pl.ds(0, part_rows)]))
+        for at in range(2):
+            head = CORES * me + (core ^ at)
+            copies.append((keys.at[head], state_outs[at].at[pl.ds(0, slot_rows)]))
+            copies.append((values.at[head], state_outs[at].at[pl.ds(slot_rows, slot_rows)]))
+        first = rank * chunk
+        head = CORES * (me ^ (first // part_rows)) + core
+        rows = pl.ds(pl.multiple_of(first % part_rows, chunk), chunk)
+        copies.append((targets.at[head, rows], targets_out))
+        copies = [
+            pltpu.make_async_copy(source, target, sems.at[at])
+            for at, (source, target) in enumerate(copies)
+        ]
+        for copy in copies:
+            copy.start()
+        for turn in range(query_devices):
+            row = positions_ref[pl.ds(CORES * (me ^ turn) + core, 1), :].astype(jnp.float32)
             query_outs[turn][part_rows:, :] = row_as_tail(row, width)
         for at in range(2):
-            state_outs[at][:slot_rows, :] = key_refs[at][0]
-            state_outs[at][slot_rows : 2 * slot_rows, :] = value_refs[at][0]
-            row = bias_ref[pl.ds(numbers[at], 1), :]
+            row = bias_ref[pl.ds(CORES * me + (core ^ at), 1), :]
             state_outs[at][2 * slot_rows :, :] = row_as_tail(row, width)
-        targets_out[...] = targets_ref[0]
-
-    def head_block(array, number):
-        shape = (1,) + array.shape[1:]
-        return (array, shape, lambda step, numbers: (numbers[number], 0, 0))
-
-    targets_block = (
-        targets,
-        (1, chunk, width),
-        lambda step, numbers: (numbers[2], numbers[3], 0),
-    )
-    packed = call(
+        for copy in copies:
+            copy.wait()
+
+    own_state, mate_state, *packed_queries, packed_targets = call(
         prep_body,
-        [(packed_rows, width)] * 2 + [(part_rows + TAIL, width)] * query_devices + [(chunk, width)],
+        packed_shapes + [(part_rows + TAIL, width)] * query_devices + [(chunk, width)],
         "pack",
         2**20,
-        prep_numbers,
-        [positions, slot_bias, targets_block]
-        + [head_block(compact_keys, at) for at in range(2)]
-        + [head_block(compact_values, at) for at in range(2)]
-        + [head_block(queries, 0)]
-        + [head_block(queries, 3 + turn) for turn in range(1, query_devices)],
-    )
-    own_state, mate_state = packed[0], packed[1]
-    query_parts = [packed[2]] + [
-        send(packed[2 + turn], ("query",), lambda y, turn=turn: (y - turn,))
-        for turn in range(1, query_devices)
+        [queries, compact_keys, compact_values, slot_bias, targets, positions],
+        [pltpu.HBM] * 3 + [pltpu.VMEM, pltpu.HBM],
+        [pltpu.SemaphoreType.DMA((query_devices + 5,))],
+    )
+    query_parts = packed_queries[:1] + [
+        exchange(packed_queries[turn], query=turn) for turn in range(1, query_devices)
     ]
-    states = [own_state, send(mate_state, ("page",), lambda p: (p + 1 - 2 * (p % CORES),))]
-    chunk_targets = send(
-        packed[2 + query_devices],
+    states = [own_state, exchange(mate_state, page=1)]
+    chunk_targets = lax.ppermute(
+        packed_targets,
         ("page", "query"),
-        lambda p, y: (p, y - part_of(p // CORES)),
-    )
-
-    to_chunks = [lax.rem(rank + turn, ranks) for turn in range(ranks)]
-    from_chunks = [lax.rem(rank - turn + ranks, ranks) for turn in range(ranks)]
-    numbers = jnp.stack(
-        [assignment[page] * PAGE_LEN, assignment[mate_page] * PAGE_LEN, *to_chunks, *from_chunks]
-    ).astype(jnp.int32)
-
-    def along_rank(value, turn):
-        return send(value, ("page",), lambda p: (p + CORES * turn,))
+        [
+            (p * query_devices + y, p * query_devices + (y ^ (p // CORES * chunk // part_rows)))
+            for p in range(ranks * CORES)
+            for y in range(query_devices)
+        ],
+    )
 
     def step_sizes(tile_refs):
         tile = tile_refs[0][...]
@@ -234,7 +205,8 @@
             state_ref[value_end:, :] - sizes[2] * grad_ref[value_end:, :],
         )
 
-    def forward(state_refs, query_refs, number_ref, chunk_outs, weights_out, max_out, chunks):
+    def forward(assignment_ref, state_refs, query_refs, chunk_outs, weights_out, max_out, chunks):
+        rank, core, _ = places()
         all_queries = jnp.concatenate([ref[:part_rows, :] for ref in query_refs], axis=0)
         position_row = jnp.concatenate(
             [tail_as_row(ref, part_rows, pos_rows) for ref in query_refs], axis=1
@@ -244,8 +216,8 @@
             scores = dot(ref[:slot_rows, :], all_queries, 1, 1) * score_scale
             bias = row_as_column(tail_as_row(ref, 2 * slot_rows, bias_rows), width)
             scores = scores + jnp.concatenate([bias] * (query_rows // width), axis=1)
-            page_start = number_ref[at].astype(jnp.float32)
-            visible = jnp.broadcast_to(position_row, scores.shape) >= page_start
+            page_start = assignment_ref[CORES * rank + (core ^ at)] * PAGE_LEN
+            visible = jnp.broadcast_to(position_row, scores.shape) >= page_start.astype(jnp.float32)
             all_scores.append(jnp.where(visible, scores, MASKED))
             all_visible.append(visible)
         row_max = jnp.max(all_scores[0], axis=0, keepdims=True)
@@ -267,35 +239,33 @@
             chunks[at, :width, :] = row_sum[:, columns]
             chunks[at, width:, :] = tail[:, columns]
         for turn in range(ranks):
-            chunk_outs[turn][...] = chunks[number_ref[2 + turn]]
-
-    forward_shapes = (
-        [(width + TAIL, chunk)] * ranks + [(slots, query_rows), (TAIL, query_rows)]
-    )
-    chunk_scratch = [pltpu.VMEM((ranks, width + TAIL, chunk), jnp.float32)]
-
-    def first_body(number_ref, *refs):
+            chunk_outs[turn][...] = chunks[rank ^ turn]
+
+    chunk_shape = (width + TAIL, chunk)
+    forward_shapes = [chunk_shape] * ranks + [(slots, query_rows), (TAIL, query_rows)]
+    chunk_scratch = [pltpu.VMEM((ranks,) + chunk_shape, jnp.float32)]
+
+    def first_body(assignment_ref, *refs):
         state_refs, refs = refs[:2], refs[2:]
         query_refs, refs = refs[:query_devices], refs[query_devices:]
-        chunk_outs, (weights_out, max_out, chunks) = refs[:ranks], refs[ranks:]
-        forward(state_refs, query_refs, number_ref, chunk_outs, weights_out, max_out, chunks)
-
-    def next_body(number_ref, *refs):
+        chunk_outs, refs = refs[:ranks], refs[ranks:]
+        forward(assignment_ref, state_refs, query_refs, chunk_outs, *refs)
+
+    def next_body(assignment_ref, *refs):
         state_refs, refs = refs[:2], refs[2:]
         query_refs, refs = refs[:query_devices], refs[query_devices:]
-        grad_refs, refs = refs[:2], refs[2:]
-        tile_refs, refs = refs[:ranks], refs[ranks:]
+        grad_refs, tile_refs, refs = refs[:2], refs[2:4], refs[4:]
         state_outs, refs = refs[:2], refs[2:]
-        chunk_outs, (weights_out, max_out, chunks) = refs[:ranks], refs[ranks:]
+        chunk_outs, refs = refs[:ranks], refs[ranks:]
         sizes = step_sizes(tile_refs)
         for at in range(2):
             keys, values, bias = updated(state_refs[at], grad_refs[at], sizes)
             state_outs[at][:slot_rows, :] = keys
             state_outs[at][slot_rows : 2 * slot_rows, :] = values
             state_outs[at][2 * slot_rows :, :] = bias
-        forward(state_outs, query_refs, number_ref, chunk_outs, weights_out, max_out, chunks)
-
-    def merge_body(number_ref, targets_ref, *refs):
+        forward(assignment_ref, state_outs, query_refs, chunk_outs, *refs)
+
+    def merge_body(targets_ref, *refs):
         chunk_refs, (merged_out,) = refs[:ranks], refs[ranks:]
         row_max = chunk_refs[0][width : width + 1, :]
         for ref in chunk_refs[1:]:
@@ -314,14 +284,14 @@
             [row_max, row_total, row_delta, jnp.zeros((TAIL - 3, chunk), jnp.float32)], axis=0
         )
 
-    def backward_body(number_ref, *refs):
-        weights_ref, max_ref, *refs = refs
+    def backward_body(weights_ref, max_ref, *refs):
         state_refs, refs = refs[:2], refs[2:]
         query_refs, refs = refs[:query_devices], refs[query_devices:]
         merged_refs, refs = refs[:ranks], refs[ranks:]
         grad_outs, (squares_out, chunks) = refs[:2], refs[2:]
+        rank, _, _ = places()
         for turn in range(ranks):
-            chunks[number_ref[2 + ranks + turn]] = merged_refs[turn][...]
+            chunks[rank ^ turn] = merged_refs[turn][...]
         joined = jnp.concatenate([chunks[at] for at in range(ranks)], axis=1)
         residual = joined[:width, :]
         row_max, row_total, row_delta = (
@@ -347,112 +317,99 @@
             squares + [jnp.zeros((TAIL - 3, width), jnp.float32)], axis=0
         )
 
-    def to_outputs(packs):
-        received = []
-        for turn in range(query_devices):
-            for flip in range(CORES):
-                if turn == 0 and flip == 0:
-                    received.append(packs[0])
-                else:
-                    received.append(
-                        send(
-                            packs[flip],
-                            ("page", "query"),
-                            lambda p, y, turn=turn, flip=flip: (
-                                p + flip * (1 - 2 * (p % CORES)),
-                                y + turn,
-                            ),
-                        )
-                    )
-        return received
-
-    def over_block(tile):
-        total = tile
-        for dc, dy, dx in itertools.product(
-            range(CORES), range(query_devices), range(head_devices)
-        ):
-            if dc or dy or dx:
-                total = total + send(
-                    tile,
-                    ("page", "query", "head"),
-                    lambda p, y, x, dc=dc, dy=dy, dx=dx: (
-                        p + dc * (1 - 2 * (p % CORES)),
-                        y + dy,
-                        x + dx,
-                    ),
-                )
-        return total
-
-    state_copies, grads, tiles = None, None, None
+    def join_body(left_ref, right_ref, out_ref):
+        out_ref[...] = left_ref[...] + right_ref[...]
+
+    def axis_rounds(axis, size, least=1):
+        return [{axis: 1 << bit} for bit in range(size.bit_length() - 1) if 1 << bit >= least]
+
+    rounds = (
+        axis_rounds("query", query_devices)
+        + [{"page": 1}]
+        + axis_rounds("head", head_devices)
+        + axis_rounds("page", ranks * CORES, CORES)
+    )
+
+    out_masks = list(itertools.product(range(query_devices), range(CORES)))
+
+    def to_output(packs, mask):
+        if mask == (0, 0):
+            return packs[0]
+        return exchange(packs[mask[1]], page=mask[1], query=mask[0])
+
     for repeat in range(STEPS):
+        last = repeat == STEPS - 1
+        before_merge, before_backward = [], []
         if repeat == 0:
             *chunk_parts, weights, maxima = call(
                 first_body,
                 forward_shapes,
                 "forward",
-                6 * 2 * matmul_cost,
-                numbers,
-                states + query_parts,
+                2 * matmul_cost,
+                [assignment] + states + query_parts,
+                [pltpu.SMEM],
                 chunk_scratch,
             )
         else:
             own_new, mate_new, *chunk_parts, weights, maxima = call(
                 next_body,
-                [(packed_rows, width)] * 2 + forward_shapes,
+                packed_shapes + forward_shapes,
                 "update_forward",
-                6 * 2 * matmul_cost,
-                numbers,
-                states + query_parts + grads + tiles,
+                2 * matmul_cost,
+                [assignment] + states + query_parts + grads + tiles,
+                [pltpu.SMEM],
                 chunk_scratch,
             )
             states = [own_new, mate_new]
-            state_copies = states
-        arrived = [chunk_parts[0]] + [
-            along_rank(chunk_parts[turn], turn) for turn in range(1, ranks)
+        if last:
+            all_states = [to_output(states, mask) for mask in out_masks]
+            if repeat:
+                before_merge, before_backward = all_states[2:3], all_states[1:2] + all_states[3:]
+        arrived = chunk_parts[:1] + [
+            exchange(chunk_parts[turn], page=CORES * turn) for turn in range(1, ranks)
         ]
         (merged,) = call(
             merge_body,
-            [(width + TAIL, chunk)],
+            [chunk_shape],
             "merge",
             2**20,
-            numbers,
             [chunk_targets] + arrived,
-        )
-        all_merged = [merged] + [along_rank(merged, turn) for turn in range(1, ranks)]
+            after=before_merge,
+        )
+        all_merged = [merged] + [
+            exchange(merged, page=CORES * turn) for turn in range(1, ranks)
+        ]
         own_grad, mate_grad, squares = call(
             backward_body,
-            [(packed_rows, width)] * 2 + [(TAIL, width)],
+            packed_shapes + [(TAIL, width)],
             "backward",
-            6 * 3 * matmul_cost,
-            numbers,
+            3 * matmul_cost,
             [weights, maxima] + states + query_parts + all_merged,
-            chunk_scratch,
+            scratch=chunk_scratch,
+            after=before_backward,
         )
         grads = [own_grad, mate_grad]
-        block_squares = over_block(squares)
-        tiles = [block_squares] + [
-            along_rank(block_squares, turn) for turn in range(1, ranks)
-        ]
-
-    all_states = to_outputs(state_copies)
-    all_grads = to_outputs(grads)
-    out_heads = jnp.stack(
-        [
-            CORES * lax.rem(me - turn + query_devices, query_devices)
-            + (core if flip == 0 else CORES - 1 - core)
-            for turn in range(query_devices)
-            for flip in range(CORES)
-        ]
-    ).astype(jnp.int32)
-
-    def last_body(number_ref, *refs):
+        if last:
+            all_grads = [to_output(grads, mask) for mask in out_masks]
+        tiles = [squares, exchange(squares, **rounds[0])]
+        for at, masks in enumerate(rounds[1:], 1):
+            if last and at == len(rounds) - 1:
+                (joined,) = call(
+                    join_body, [squares.shape], "join", 2**10, tiles, after=all_grads[2:3]
+                )
+            else:
+                joined = tiles[0] + tiles[1]
+            tiles = [joined, exchange(joined, **masks)]
+
+    def last_body(*refs):
         state_refs, refs = refs[:local_heads], refs[local_heads:]
         grad_refs, refs = refs[:local_heads], refs[local_heads:]
-        tile_refs, (keys_out, values_out, bias_out) = refs[:ranks], refs[ranks:]
+        tile_refs, (keys_out, values_out, bias_out) = refs[:2], refs[2:]
+        _, core, me = places()
         sizes = step_sizes(tile_refs)
-        for at in range(local_heads):
+        for at, (turn, flip) in enumerate(out_masks):
             keys, values, bias = updated(state_refs[at], grad_refs[at], sizes)
-            head = number_ref[at]
+            head = CORES * (me ^ turn) + (core ^ flip)
             keys_out[head] = keys
             values_out[head] = values
             bias_row = jnp.concatenate([bias[row : row + 1] for row in range(bias_rows)], axis=1)
@@ -464,7 +421,6 @@
             [compact_keys.shape, compact_values.shape, slot_bias.shape],
             "last_update",
             2**20,
-            out_heads,
             all_states + all_grads + tiles,
         )
     )

time: 115 us -> 111 us (0.965)
  waiting for transfers between devices: 42.8 us -> 54.5 us
  starting transfers between devices: 46.7 us -> 35.3 us
  Pallas kernels: 16.4 us -> 14.3 us
  between operations: 2.14 us -> 0.74 us
    ppermute x41 -> x31, waiting for transfers between devices: 42.8 us -> 54.5 us  [the longest x30 54.5 us: exchange(): return lax.ppermute(value, axes, pairs)]
    ppermute x41 -> x31, starting transfers between devices: 46.7 us -> 35.3 us  [the longest x30 34.4 us: exchange(): return lax.ppermute(value, axes, pairs)]
    pallas_call x8 -> x9, Pallas kernels: 16.4 us -> 14.3 us  [call(): pl.pallas_call(without_after, out_shape=[jax.ShapeDtypeStruct(shape, jnp....]
  transfers between devices with their start and end apart: 41 -> 31, of which waited for: 25 -> 20; matrix products, arithmetic and copies ran while one was open for 1% -> 0% of each run, Pallas kernels for 3% -> 0%
where the time goes in v2:
time: 111 us
  waiting for transfers between devices  54.5 us (49%)
  starting transfers between devices  35.3 us (32%)
  Pallas kernels  14.3 us (13%)
  local copies, waits for them, and re-layouts  6.19 us (6%)
    ppermute x30, waiting for transfers between devices, exchange(): return lax.ppermute(value, axes, pairs)  54.5 us
    ppermute x30, starting transfers between devices, exchange(): return lax.ppermute(value, axes, pairs)  34.4 us
    pallas_call x9, Pallas kernels, call(): pl.pallas_call(without_after, out_shape=[jax.ShapeDtypeStruct(shape, jnp....  14.3 us
    unnamed x14, local copies, waits for them, and re-layouts  6.19 us
  transfers between devices with their start and end apart: 31, of which 20 were waited for; matrix products, arithmetic and copies ran while one was open for 0% of the time, Pallas kernels for 0%

profile of v2, /device:TPU:0, one launch (start us, length us, event | category | flops | bytes accessed | tf_op | source)
XLA Modules:
  0.0 111.0 jit_solution(6156060319547519508)
XLA Ops:
  0.6 1.0 copy-done
  1.7 1.0 copy-done.1
  2.7 1.0 copy-done.2
  3.8 1.0 copy-done.3
  4.8 0.7 copy-done.4
  5.5 0.7 copy-done.5
  6.2 1.1 %pack.1 = (f32[520,128]{1,0:T(8,128)S(1)}, f32[520,128]{1,0:T(8,128)S(1)}, f32[264,128]{1,0:T(8,128)S(1)}, f32[264,128]{1,0:T(8,128)S(1)}, f32[128,128]{1,0:T(8,128)S(1)}) custom-call(f32[4,256,128]{2,1,0:T(8,128)S(1)} %copy-done, f32[4,256,128]{2,1,0:T(8,128)S(1)} %copy-done.1, f32[4,256,128]{2,1,0:T(8,128)S(1)} %copy-done.2, f32[4,256]{1,0:T(4,128)S(1)} %copy-done.4, ...), custom_call_target="tpu_custom_call" | custom-call | flops 1048576 | bytes 1048576 | tf_op jit(solution)/shard_map/pack/pallas_call | solution.py:59
  7.8 2.6 %collective-permute-start.1 = (f32[264,128]{1,0:T(8,128)S(1)}, f32[264,128]{1,0:T(8,128)S(1)}, u32[]{:S(2)}, u32[]{:S(2)}) collective-permute-start(f32[264,128]{1,0:T(8,128)S(1)} %get-tuple-element.31), channel_id=1, source_target_pairs={{0,2},{2,0},{1,3},{3,1},{4,6},{6,4},{5,7},{7,5},{8,10},{10,8},{9,1... | collective-permute-start | bytes 405512 | tf_op jit(solution)/shard_map/ppermute | solution.py:39
  10.4 4.2 %collective-permute-done.1.refs_4_.refs_5_ = f32[264,128]{1,0:T(8,128)S(1)} collective-permute-done((f32[264,128]{1,0:T(8,128)S(1)}, f32[264,128]{1,0:T(8,128)S(1)}, u32[]{:S(2)}, u32[]{:S(2)}) %collective-permute-start.1) | collective-permute-done | bytes 135200 | tf_op jit(solution)/shard_map/ppermute | solution.py:39
  15.3 2.5 %forward.1 = (f32[136,128]{1,0:T(8,128)S(1)}, f32[136,128]{1,0:T(8,128)S(1)}, f32[136,128]{1,0:T(8,128)S(1)}, f32[136,128]{1,0:T(8,128)S(1)}, f32[512,512]{1,0:T(8,128)S(1)}, /*index=5*/f32[8,512]{1,0:T(8,128)S(1)}) custom-call(s32[8]{0:T(128)S(1)} %copy-done.6, f32[520,128]{1,0:T(8,128)S(1)} %get-tuple-element.28.refs_1_.refs_2_, ...), custom_call_target="tpu_custom_call" | custom-call | flops 805306368 | bytes 1048576 | tf_op jit(solution)/shard_map/forward/pallas_call | solution.py:59
  17.8 1.9 %collective-permute-start.3 = (f32[136,128]{1,0:T(8,128)S(1)}, f32[136,128]{1,0:T(8,128)S(1)}, u32[]{:S(2)}, u32[]{:S(2)}) collective-permute-start(f32[136,128]{1,0:T(8,128)S(1)} %get-tuple-element.36), channel_id=1, source_target_pairs={{0,8},{4,12},{8,0},{12,4},{16,24},{20,28},{24,16},{28,20},{1,9},{5... | collective-permute-start | bytes 208904 | tf_op jit(solution)/shard_map/ppermute | solution.py:39
  19.6 2.6 %collective-permute-start.4 = (f32[136,128]{1,0:T(8,128)S(1)}, f32[136,128]{1,0:T(8,128)S(1)}, u32[]{:S(2)}, u32[]{:S(2)}) collective-permute-start(f32[136,128]{1,0:T(8,128)S(1)} %get-tuple-element.37), channel_id=1, source_target_pairs={{0,16},{4,20},{8,24},{12,28},{16,0},{20,4},{24,8},{28,12},{1,17},{... | collective-permute-start | bytes 208904 | tf_op jit(solution)/shard_map/ppermute | solution.py:39
  22.2 0.8 collective-permute-start.2
  23.1 3.9 %collective-permute-done.4.refs_3_ = f32[136,128]{1,0:T(8,128)S(1)} collective-permute-done((f32[136,128]{1,0:T(8,128)S(1)}, f32[136,128]{1,0:T(8,128)S(1)}, u32[]{:S(2)}, u32[]{:S(2)}) %collective-permute-start.4) | collective-permute-done | bytes 69664 | tf_op jit(solution)/shard_map/ppermute | solution.py:39
  27.0 1.5 %collective-permute-done.5.refs_4_ = f32[136,128]{1,0:T(8,128)S(1)} collective-permute-done((f32[136,128]{1,0:T(8,128)S(1)}, f32[136,128]{1,0:T(8,128)S(1)}, u32[]{:S(2)}, u32[]{:S(2)}) %collective-permute-start.5) | collective-permute-done | bytes 69664 | tf_op jit(solution)/shard_map/ppermute | solution.py:39
  28.6 3.8 %collective-permute-start.8 = (f32[136,128]{1,0:T(8,128)S(1)}, f32[136,128]{1,0:T(8,128)S(1)}, u32[]{:S(2)}, u32[]{:S(2)}) collective-permute-start(f32[136,128]{1,0:T(8,128)S(1)} %merge.2.refs_6_), channel_id=1, source_target_pairs={{0,24},{4,28},{8,16},{12,20},{16,8},{20,12},{24,0},{28,4},{1,25},{... | collective-permute-start | bytes 208904 | tf_op jit(solution)/shard_map/ppermute | solution.py:39
  33.0 1.8 %collective-permute-done.8.refs_9_ = f32[136,128]{1,0:T(8,128)S(1)} collective-permute-done((f32[136,128]{1,0:T(8,128)S(1)}, f32[136,128]{1,0:T(8,128)S(1)}, u32[]{:S(2)}, u32[]{:S(2)}) %collective-permute-start.8) | collective-permute-done | bytes 69664 | tf_op jit(solution)/shard_map/ppermute | solution.py:39
  34.8 2.8 %collective-permute-done.7.refs_8_ = f32[136,128]{1,0:T(8,128)S(1)} collective-permute-done((f32[136,128]{1,0:T(8,128)S(1)}, f32[136,128]{1,0:T(8,128)S(1)}, u32[]{:S(2)}, u32[]{:S(2)}) %collective-permute-start.7) | collective-permute-done | bytes 69664 | tf_op jit(solution)/shard_map/ppermute | solution.py:39
  37.6 3.4 %backward.2 = (f32[520,128]{1,0:T(8,128)S(1)}, f32[520,128]{1,0:T(8,128)S(1)}, f32[8,128]{1,0:T(8,128)S(1)}) custom-call(f32[512,512]{1,0:T(8,128)S(1)} %get-tuple-element.32.refs_0_, f32[8,512]{1,0:T(8,128)S(1)} %get-tuple-element.33.refs_1_, f32[520,128]{1,0:T(8,128)S(1)} %get-tuple-element.28.refs_1_.refs_2_, ...), custom_call_target="tpu_custom_call" | custom-call | flops 1207959552 | bytes 1048576 | tf_op jit(solution)/shard_map/backward/pallas_call | solution.py:59
  41.0 1.6 %collective-permute-start.9 = (f32[8,128]{1,0:T(8,128)S(1)}, f32[8,128]{1,0:T(8,128)S(1)}, u32[]{:S(2)}, u32[]{:S(2)}) collective-permute-start(f32[8,128]{1,0:T(8,128)S(1)} %get-tuple-element.41), channel_id=1, source_target_pairs={{0,2},{2,0},{1,3},{3,1},{4,6},{6,4},{5,7},{7,5},{8,10},{10,8},{9,1... | collective-permute-start | bytes 12296 | tf_op jit(solution)/shard_map/ppermute | solution.py:39
  42.6 2.1 %collective-permute-done.9 = f32[8,128]{1,0:T(8,128)S(1)} collective-permute-done((f32[8,128]{1,0:T(8,128)S(1)}, f32[8,128]{1,0:T(8,128)S(1)}, u32[]{:S(2)}, u32[]{:S(2)}) %collective-permute-start.9) | collective-permute-done | bytes 4128 | tf_op jit(solution)/shard_map/ppermute | solution.py:39
  44.7 1.2 %collective-permute-done.10 = f32[8,128]{1,0:T(8,128)S(1)} collective-permute-done((f32[8,128]{1,0:T(8,128)S(1)}, f32[8,128]{1,0:T(8,128)S(1)}, u32[]{:S(2)}, u32[]{:S(2)}) %collective-permute-start.10) | collective-permute-done | bytes 4128 | tf_op jit(solution)/shard_map/ppermute | solution.py:39
  45.9 1.5 %collective-permute-start.11 = (f32[8,128]{1,0:T(8,128)S(1)}, f32[8,128]{1,0:T(8,128)S(1)}, u32[]{:S(2)}, u32[]{:S(2)}) collective-permute-start(f32[8,128]{1,0:T(8,128)S(1)} %add.22), channel_id=1, source_target_pairs={{0,1},{1,0},{2,3},{3,2},{4,5},{5,4},{6,7},{7,6},{8,9},{9,8},{10,11... | collective-permute-start | bytes 12296 | tf_op jit(solution)/shard_map/ppermute | solution.py:39
  47.3 2.1 %collective-permute-done.11 = f32[8,128]{1,0:T(8,128)S(1)} collective-permute-done((f32[8,128]{1,0:T(8,128)S(1)}, f32[8,128]{1,0:T(8,128)S(1)}, u32[]{:S(2)}, u32[]{:S(2)}) %collective-permute-start.11) | collective-permute-done | bytes 4128 | tf_op jit(solution)/shard_map/ppermute | solution.py:39
  50.1 3.0 %collective-permute-done.12 = f32[8,128]{1,0:T(8,128)S(1)} collective-permute-done((f32[8,128]{1,0:T(8,128)S(1)}, f32[8,128]{1,0:T(8,128)S(1)}, u32[]{:S(2)}, u32[]{:S(2)}) %collective-permute-start.12) | collective-permute-done | bytes 4128 | tf_op jit(solution)/shard_map/ppermute | solution.py:39
  53.1 2.0 %collective-permute-start.13 = (f32[8,128]{1,0:T(8,128)S(1)}, f32[8,128]{1,0:T(8,128)S(1)}, u32[]{:S(2)}, u32[]{:S(2)}) collective-permute-start(f32[8,128]{1,0:T(8,128)S(1)} %add.24.refs_7_), channel_id=1, source_target_pairs={{0,16},{4,20},{8,24},{12,28},{16,0},{20,4},{24,8},{28,12},{1,17},{... | collective-permute-start | bytes 12296 | tf_op jit(solution)/shard_map/ppermute | solution.py:39
  55.1 2.5 %collective-permute-done.13.refs_8_ = f32[8,128]{1,0:T(8,128)S(1)} collective-permute-done((f32[8,128]{1,0:T(8,128)S(1)}, f32[8,128]{1,0:T(8,128)S(1)}, u32[]{:S(2)}, u32[]{:S(2)}) %collective-permute-start.13) | collective-permute-done | bytes 4128 | tf_op jit(solution)/shard_map/ppermute | solution.py:39
  57.6 2.5 %update_forward.1 = (f32[520,128]{1,0:T(8,128)S(1)}, f32[520,128]{1,0:T(8,128)S(1)}, f32[136,128]{1,0:T(8,128)S(1)}, f32[136,128]{1,0:T(8,128)S(1)}, f32[136,128...) custom-call(s32[8]{0:T(128)S(1)} %copy-done.6, ...), custom_call_target="tpu_custom_call" | custom-call | flops 805306368 | bytes 1048576 | tf_op jit(solution)/shard_map/update_forward/pallas_call | solution.py:59
  60.1 1.6 %collective-permute-start.15 = (f32[520,128]{1,0:T(8,128)S(1)}, f32[520,128]{1,0:T(8,128)S(1)}, u32[]{:S(2)}, u32[]{:S(2)}) collective-permute-start(f32[520,128]{1,0:T(8,128)S(1)} %get-tuple-element.42.refs_2_.refs_0_), channel_id=1, source_target_pairs={{0,2},{2,0},{4,6},{6,4},{8,10},{10,8},{12,14},{14,12},{16,18},{18,... | collective-permute-start | bytes 798728 | tf_op jit(solution)/shard_map/ppermute | solution.py:39
  62.9 1.6 %collective-permute-start.18 = (f32[136,128]{1,0:T(8,128)S(1)}, f32[136,128]{1,0:T(8,128)S(1)}, u32[]{:S(2)}, u32[]{:S(2)}) collective-permute-start(f32[136,128]{1,0:T(8,128)S(1)} %get-tuple-element.48), channel_id=1, source_target_pairs={{0,16},{4,20},{8,24},{12,28},{16,0},{20,4},{24,8},{28,12},{1,17},{... | collective-permute-start | bytes 208904 | tf_op jit(solution)/shard_map/ppermute | solution.py:39
  64.5 2.9 %collective-permute-done.17.refs_2_ = f32[136,128]{1,0:T(8,128)S(1)} collective-permute-done((f32[136,128]{1,0:T(8,128)S(1)}, f32[136,128]{1,0:T(8,128)S(1)}, u32[]{:S(2)}, u32[]{:S(2)}) %collective-permute-start.17) | collective-permute-done | bytes 69664 | tf_op jit(solution)/shard_map/ppermute | solution.py:39
  67.4 0.9 collective-permute-start.19
  68.7 4.8 %collective-permute-done.19.refs_4_ = f32[136,128]{1,0:T(8,128)S(1)} collective-permute-done((f32[136,128]{1,0:T(8,128)S(1)}, f32[136,128]{1,0:T(8,128)S(1)}, u32[]{:S(2)}, u32[]{:S(2)}) %collective-permute-start.19) | collective-permute-done | bytes 69664 | tf_op jit(solution)/shard_map/ppermute | solution.py:39
  73.6 1.0 collective-permute-start.22
  74.7 3.4 %collective-permute-start.20 = (f32[136,128]{1,0:T(8,128)S(1)}, f32[136,128]{1,0:T(8,128)S(1)}, u32[]{:S(2)}, u32[]{:S(2)}) collective-permute-start(f32[136,128]{1,0:T(8,128)S(1)} %merge.3.refs_6_), channel_id=1, source_target_pairs={{0,8},{4,12},{8,0},{12,4},{16,24},{20,28},{24,16},{28,20},{1,9},{5... | collective-permute-start | bytes 208904 | tf_op jit(solution)/shard_map/ppermute | solution.py:39
  78.1 1.8 %collective-permute-done.22.refs_9_ = f32[136,128]{1,0:T(8,128)S(1)} collective-permute-done((f32[136,128]{1,0:T(8,128)S(1)}, f32[136,128]{1,0:T(8,128)S(1)}, u32[]{:S(2)}, u32[]{:S(2)}) %collective-permute-start.22) | collective-permute-done | bytes 69664 | tf_op jit(solution)/shard_map/ppermute | solution.py:39
  79.9 1.4 %collective-permute-done.21.refs_8_ = f32[136,128]{1,0:T(8,128)S(1)} collective-permute-done((f32[136,128]{1,0:T(8,128)S(1)}, f32[136,128]{1,0:T(8,128)S(1)}, u32[]{:S(2)}, u32[]{:S(2)}) %collective-permute-start.21) | collective-permute-done | bytes 69664 | tf_op jit(solution)/shard_map/ppermute | solution.py:39
  81.3 3.4 %backward.3 = (f32[520,128]{1,0:T(8,128)S(1)}, f32[520,128]{1,0:T(8,128)S(1)}, f32[8,128]{1,0:T(8,128)S(1)}) custom-call(f32[512,512]{1,0:T(8,128)S(1)} %get-tuple-element.44.refs_0_, f32[8,512]{1,0:T(8,128)S(1)} %get-tuple-element.45.refs_1_, f32[520,128]{1,0:T(8,128)S(1)} %get-tuple-element.42.refs_2_.refs_0_, f32[520,128]{1,0:T(8,128)S(1)} %get-tuple-element.43.refs_3_, ...), custom_call_target="tpu_custom_call" | custom-call | flops 1207959552 | bytes 1048576 | tf_op jit(solution)/shard_map/backward/pallas_call | solution.py:59
  84.7 1.6 %collective-permute-start.24 = (f32[520,128]{1,0:T(8,128)S(1)}, f32[520,128]{1,0:T(8,128)S(1)}, u32[]{:S(2)}, u32[]{:S(2)}) collective-permute-start(f32[520,128]{1,0:T(8,128)S(1)} %get-tuple-element.50.refs_4_), channel_id=1, source_target_pairs={{0,2},{2,0},{4,6},{6,4},{8,10},{10,8},{12,14},{14,12},{16,18},{18,... | collective-permute-start | bytes 798728 | tf_op jit(solution)/shard_map/ppermute | solution.py:39
  86.9 1.5 %collective-permute-start.26 = (f32[8,128]{1,0:T(8,128)S(1)}, f32[8,128]{1,0:T(8,128)S(1)}, u32[]{:S(2)}, u32[]{:S(2)}) collective-permute-start(f32[8,128]{1,0:T(8,128)S(1)} %get-tuple-element.52), channel_id=1, source_target_pairs={{0,2},{2,0},{1,3},{3,1},{4,6},{6,4},{5,7},{7,5},{8,10},{10,8},{9,1... | collective-permute-start | bytes 12296 | tf_op jit(solution)/shard_map/ppermute | solution.py:39
  88.4 8.5 %collective-permute-done.26 = f32[8,128]{1,0:T(8,128)S(1)} collective-permute-done((f32[8,128]{1,0:T(8,128)S(1)}, f32[8,128]{1,0:T(8,128)S(1)}, u32[]{:S(2)}, u32[]{:S(2)}) %collective-permute-start.26) | collective-permute-done | bytes 4128 | tf_op jit(solution)/shard_map/ppermute | solution.py:39
  97.0 1.2 %collective-permute-done.27 = f32[8,128]{1,0:T(8,128)S(1)} collective-permute-done((f32[8,128]{1,0:T(8,128)S(1)}, f32[8,128]{1,0:T(8,128)S(1)}, u32[]{:S(2)}, u32[]{:S(2)}) %collective-permute-start.27) | collective-permute-done | bytes 4128 | tf_op jit(solution)/shard_map/ppermute | solution.py:39
  98.2 1.5 %collective-permute-start.28 = (f32[8,128]{1,0:T(8,128)S(1)}, f32[8,128]{1,0:T(8,128)S(1)}, u32[]{:S(2)}, u32[]{:S(2)}) collective-permute-start(f32[8,128]{1,0:T(8,128)S(1)} %add.26), channel_id=1, source_target_pairs={{0,1},{1,0},{2,3},{3,2},{4,5},{5,4},{6,7},{7,6},{8,9},{9,8},{10,11... | collective-permute-start | bytes 12296 | tf_op jit(solution)/shard_map/ppermute | solution.py:39
  99.6 2.1 %collective-permute-done.28 = f32[8,128]{1,0:T(8,128)S(1)} collective-permute-done((f32[8,128]{1,0:T(8,128)S(1)}, f32[8,128]{1,0:T(8,128)S(1)}, u32[]{:S(2)}, u32[]{:S(2)}) %collective-permute-start.28) | collective-permute-done | bytes 4128 | tf_op jit(solution)/shard_map/ppermute | solution.py:39
  101.8 1.1 collective-permute-start.29
  102.9 2.5 %collective-permute-done.29.refs_1_ = f32[8,128]{1,0:T(8,128)S(1)} collective-permute-done((f32[8,128]{1,0:T(8,128)S(1)}, f32[8,128]{1,0:T(8,128)S(1)}, u32[]{:S(2)}, u32[]{:S(2)}) %collective-permute-start.29) | collective-permute-done | bytes 4128 | tf_op jit(solution)/shard_map/ppermute | solution.py:39
  106.0 3.9 %collective-permute-done.30.refs_9_ = f32[8,128]{1,0:T(8,128)S(1)} collective-permute-done((f32[8,128]{1,0:T(8,128)S(1)}, f32[8,128]{1,0:T(8,128)S(1)}, u32[]{:S(2)}, u32[]{:S(2)}) %collective-permute-start.30) | collective-permute-done | bytes 4128 | tf_op jit(solution)/shard_map/ppermute | solution.py:39
  109.9 1.1 %last_update.1 = (f32[4,256,128]{2,1,0:T(8,128)}, f32[4,256,128]{2,1,0:T(8,128)}, f32[4,256]{1,0:T(4,128)}) custom-call(f32[520,128]{1,0:T(8,128)S(1)} %get-tuple-element.42.refs_2_.refs_0_, f32[520,128]{1,0:T(8,128)S(1)} %collective-permute-done.14.refs_10_.refs_1_, f32[520,128]{1,0:T(8,128)S(1)} %collective-permute-done.15.refs_5_.refs_2_, ...), custom_call_target="tpu_custom_call" | custom-call | flops 1048576 | bytes 1048576 | tf_op jit(solution)/shard_map/last_update/pallas_call | solution.py:59
  (44 shorter events, 5.5 us)
Async XLA Ops:
  0.6 1.0 copy-start
  1.7 1.0 copy-start.1
  2.7 1.0 copy-start.2
  3.8 1.0 copy-start.3
  4.8 0.7 copy-start.4
  5.5 0.7 copy-start.5
  7.3 7.3 %collective-permute-start = (f32[520,128]{1,0:T(8,128)S(1)}, f32[520,128]{1,0:T(8,128)S(1)}, u32[]{:S(2)}, u32[]{:S(2)}) collective-permute-start(f32[520,128]{1,0:T(8,128)S(1)} %get-tuple-element.29), channel_id=1, source_target_pairs={{0,4},{4,0},{8,12},{12,8},{16,20},{20,16},{24,28},{28,24},{1,5},{5... | collective-permute-start | bytes 798728 | tf_op jit(solution)/shard_map/ppermute | solution.py:39
  7.8 6.8 %collective-permute-start.1 = (f32[264,128]{1,0:T(8,128)S(1)}, f32[264,128]{1,0:T(8,128)S(1)}, u32[]{:S(2)}, u32[]{:S(2)}) collective-permute-start(f32[264,128]{1,0:T(8,128)S(1)} %get-tuple-element.31), channel_id=1, source_target_pairs={{0,2},{2,0},{1,3},{3,1},{4,6},{6,4},{5,7},{7,5},{8,10},{10,8},{9,1... | collective-permute-start | bytes 405512 | tf_op jit(solution)/shard_map/ppermute | solution.py:39
  14.6 0.7 copy-start.6
  17.8 5.3 %collective-permute-start.3 = (f32[136,128]{1,0:T(8,128)S(1)}, f32[136,128]{1,0:T(8,128)S(1)}, u32[]{:S(2)}, u32[]{:S(2)}) collective-permute-start(f32[136,128]{1,0:T(8,128)S(1)} %get-tuple-element.36), channel_id=1, source_target_pairs={{0,8},{4,12},{8,0},{12,4},{16,24},{20,28},{24,16},{28,20},{1,9},{5... | collective-permute-start | bytes 208904 | tf_op jit(solution)/shard_map/ppermute | solution.py:39
  19.6 7.3 %collective-permute-start.4 = (f32[136,128]{1,0:T(8,128)S(1)}, f32[136,128]{1,0:T(8,128)S(1)}, u32[]{:S(2)}, u32[]{:S(2)}) collective-permute-start(f32[136,128]{1,0:T(8,128)S(1)} %get-tuple-element.37), channel_id=1, source_target_pairs={{0,16},{4,20},{8,24},{12,28},{16,0},{20,4},{24,8},{28,12},{1,17},{... | collective-permute-start | bytes 208904 | tf_op jit(solution)/shard_map/ppermute | solution.py:39
  22.2 6.2 %collective-permute-start.5 = (f32[136,128]{1,0:T(8,128)S(1)}, f32[136,128]{1,0:T(8,128)S(1)}, u32[]{:S(2)}, u32[]{:S(2)}) collective-permute-start(f32[136,128]{1,0:T(8,128)S(1)} %get-tuple-element.38), channel_id=1, source_target_pairs={{0,24},{4,28},{8,16},{12,20},{16,8},{20,12},{24,0},{28,4},{1,25},{... | collective-permute-start | bytes 208904 | tf_op jit(solution)/shard_map/ppermute | solution.py:39
  22.2 0.8 collective-permute-start.2
  28.6 6.3 %collective-permute-start.8 = (f32[136,128]{1,0:T(8,128)S(1)}, f32[136,128]{1,0:T(8,128)S(1)}, u32[]{:S(2)}, u32[]{:S(2)}) collective-permute-start(f32[136,128]{1,0:T(8,128)S(1)} %merge.2.refs_6_), channel_id=1, source_target_pairs={{0,24},{4,28},{8,16},{12,20},{16,8},{20,12},{24,0},{28,4},{1,25},{... | collective-permute-start | bytes 208904 | tf_op jit(solution)/shard_map/ppermute | solution.py:39
  32.4 5.2 %collective-permute-start.7 = (f32[136,128]{1,0:T(8,128)S(1)}, f32[136,128]{1,0:T(8,128)S(1)}, u32[]{:S(2)}, u32[]{:S(2)}) collective-permute-start(f32[136,128]{1,0:T(8,128)S(1)} %merge.2.refs_6_), channel_id=1, source_target_pairs={{0,16},{4,20},{8,24},{12,28},{16,0},{20,4},{24,8},{28,12},{1,17},{... | collective-permute-start | bytes 208904 | tf_op jit(solution)/shard_map/ppermute | solution.py:39
  32.4 5.2 %collective-permute-start.6 = (f32[136,128]{1,0:T(8,128)S(1)}, f32[136,128]{1,0:T(8,128)S(1)}, u32[]{:S(2)}, u32[]{:S(2)}) collective-permute-start(f32[136,128]{1,0:T(8,128)S(1)} %merge.2.refs_6_), channel_id=1, source_target_pairs={{0,8},{4,12},{8,0},{12,4},{16,24},{20,28},{24,16},{28,20},{1,9},{5... | collective-permute-start | bytes 208904 | tf_op jit(solution)/shard_map/ppermute | solution.py:39
  41.0 3.7 %collective-permute-start.9 = (f32[8,128]{1,0:T(8,128)S(1)}, f32[8,128]{1,0:T(8,128)S(1)}, u32[]{:S(2)}, u32[]{:S(2)}) collective-permute-start(f32[8,128]{1,0:T(8,128)S(1)} %get-tuple-element.41), channel_id=1, source_target_pairs={{0,2},{2,0},{1,3},{3,1},{4,6},{6,4},{5,7},{7,5},{8,10},{10,8},{9,1... | collective-permute-start | bytes 12296 | tf_op jit(solution)/shard_map/ppermute | solution.py:39
  44.7 1.2 %collective-permute-start.10 = (f32[8,128]{1,0:T(8,128)S(1)}, f32[8,128]{1,0:T(8,128)S(1)}, u32[]{:S(2)}, u32[]{:S(2)}) collective-permute-start(f32[8,128]{1,0:T(8,128)S(1)} %add.21), channel_id=1, source_target_pairs={{0,4},{4,0},{8,12},{12,8},{16,20},{20,16},{24,28},{28,24},{1,5},{5... | collective-permute-start | bytes 12296 | tf_op jit(solution)/shard_map/ppermute | solution.py:39
  45.9 3.6 %collective-permute-start.11 = (f32[8,128]{1,0:T(8,128)S(1)}, f32[8,128]{1,0:T(8,128)S(1)}, u32[]{:S(2)}, u32[]{:S(2)}) collective-permute-start(f32[8,128]{1,0:T(8,128)S(1)} %add.22), channel_id=1, source_target_pairs={{0,1},{1,0},{2,3},{3,2},{4,5},{5,4},{6,7},{7,6},{8,9},{9,8},{10,11... | collective-permute-start | bytes 12296 | tf_op jit(solution)/shard_map/ppermute | solution.py:39
  49.5 3.6 %collective-permute-start.12 = (f32[8,128]{1,0:T(8,128)S(1)}, f32[8,128]{1,0:T(8,128)S(1)}, u32[]{:S(2)}, u32[]{:S(2)}) collective-permute-start(f32[8,128]{1,0:T(8,128)S(1)} %add.23), channel_id=1, source_target_pairs={{0,8},{4,12},{8,0},{12,4},{16,24},{20,28},{24,16},{28,20},{1,9},{5... | collective-permute-start | bytes 12296 | tf_op jit(solution)/shard_map/ppermute | solution.py:39
  53.1 4.5 %collective-permute-start.13 = (f32[8,128]{1,0:T(8,128)S(1)}, f32[8,128]{1,0:T(8,128)S(1)}, u32[]{:S(2)}, u32[]{:S(2)}) collective-permute-start(f32[8,128]{1,0:T(8,128)S(1)} %add.24.refs_7_), channel_id=1, source_target_pairs={{0,16},{4,20},{8,24},{12,28},{16,0},{20,4},{24,8},{28,12},{1,17},{... | collective-permute-start | bytes 12296 | tf_op jit(solution)/shard_map/ppermute | solution.py:39
  60.1 13.4 %collective-permute-start.15 = (f32[520,128]{1,0:T(8,128)S(1)}, f32[520,128]{1,0:T(8,128)S(1)}, u32[]{:S(2)}, u32[]{:S(2)}) collective-permute-start(f32[520,128]{1,0:T(8,128)S(1)} %get-tuple-element.42.refs_2_.refs_0_), channel_id=1, source_target_pairs={{0,2},{2,0},{4,6},{6,4},{8,10},{10,8},{12,14},{14,12},{16,18},{18,... | collective-permute-start | bytes 798728 | tf_op jit(solution)/shard_map/ppermute | solution.py:39
  61.7 16.4 %collective-permute-start.16 = (f32[520,128]{1,0:T(8,128)S(1)}, f32[520,128]{1,0:T(8,128)S(1)}, u32[]{:S(2)}, u32[]{:S(2)}) collective-permute-start(f32[520,128]{1,0:T(8,128)S(1)} %get-tuple-element.43.refs_3_), channel_id=1, source_target_pairs={{0,6},{2,4},{4,2},{6,0},{8,14},{10,12},{12,10},{14,8},{16,22},{18,... | collective-permute-start | bytes 798728 | tf_op jit(solution)/shard_map/ppermute | solution.py:39
  61.7 16.4 %collective-permute-start.14 = (f32[520,128]{1,0:T(8,128)S(1)}, f32[520,128]{1,0:T(8,128)S(1)}, u32[]{:S(2)}, u32[]{:S(2)}) collective-permute-start(f32[520,128]{1,0:T(8,128)S(1)} %get-tuple-element.43.refs_3_), channel_id=1, source_target_pairs={{0,4},{2,6},{4,0},{6,2},{8,12},{10,14},{12,8},{14,10},{16,20},{18,... | collective-permute-start | bytes 798728 | tf_op jit(solution)/shard_map/ppermute | solution.py:39
  62.3 5.1 %collective-permute-start.17 = (f32[136,128]{1,0:T(8,128)S(1)}, f32[136,128]{1,0:T(8,128)S(1)}, u32[]{:S(2)}, u32[]{:S(2)}) collective-permute-start(f32[136,128]{1,0:T(8,128)S(1)} %get-tuple-element.47), channel_id=1, source_target_pairs={{0,8},{4,12},{8,0},{12,4},{16,24},{20,28},{24,16},{28,20},{1,9},{5... | collective-permute-start | bytes 208904 | tf_op jit(solution)/shard_map/ppermute | solution.py:39
  62.9 5.7 %collective-permute-start.18 = (f32[136,128]{1,0:T(8,128)S(1)}, f32[136,128]{1,0:T(8,128)S(1)}, u32[]{:S(2)}, u32[]{:S(2)}) collective-permute-start(f32[136,128]{1,0:T(8,128)S(1)} %get-tuple-element.48), channel_id=1, source_target_pairs={{0,16},{4,20},{8,24},{12,28},{16,0},{20,4},{24,8},{28,12},{1,17},{... | collective-permute-start | bytes 208904 | tf_op jit(solution)/shard_map/ppermute | solution.py:39
  67.4 6.1 %collective-permute-start.19 = (f32[136,128]{1,0:T(8,128)S(1)}, f32[136,128]{1,0:T(8,128)S(1)}, u32[]{:S(2)}, u32[]{:S(2)}) collective-permute-start(f32[136,128]{1,0:T(8,128)S(1)} %get-tuple-element.49), channel_id=1, source_target_pairs={{0,24},{4,28},{8,16},{12,20},{16,8},{20,12},{24,0},{28,4},{1,25},{... | collective-permute-start | bytes 208904 | tf_op jit(solution)/shard_map/ppermute | solution.py:39
  73.6 6.3 %collective-permute-start.22 = (f32[136,128]{1,0:T(8,128)S(1)}, f32[136,128]{1,0:T(8,128)S(1)}, u32[]{:S(2)}, u32[]{:S(2)}) collective-permute-start(f32[136,128]{1,0:T(8,128)S(1)} %merge.3.refs_6_), channel_id=1, source_target_pairs={{0,24},{4,28},{8,16},{12,20},{16,8},{20,12},{24,0},{28,4},{1,25},{... | collective-permute-start | bytes 208904 | tf_op jit(solution)/shard_map/ppermute | solution.py:39
  74.7 6.6 %collective-permute-start.21 = (f32[136,128]{1,0:T(8,128)S(1)}, f32[136,128]{1,0:T(8,128)S(1)}, u32[]{:S(2)}, u32[]{:S(2)}) collective-permute-start(f32[136,128]{1,0:T(8,128)S(1)} %merge.3.refs_6_), channel_id=1, source_target_pairs={{0,16},{4,20},{8,24},{12,28},{16,0},{20,4},{24,8},{28,12},{1,17},{... | collective-permute-start | bytes 208904 | tf_op jit(solution)/shard_map/ppermute | solution.py:39
  74.7 6.6 %collective-permute-start.20 = (f32[136,128]{1,0:T(8,128)S(1)}, f32[136,128]{1,0:T(8,128)S(1)}, u32[]{:S(2)}, u32[]{:S(2)}) collective-permute-start(f32[136,128]{1,0:T(8,128)S(1)} %merge.3.refs_6_), channel_id=1, source_target_pairs={{0,8},{4,12},{8,0},{12,4},{16,24},{20,28},{24,16},{28,20},{1,9},{5... | collective-permute-start | bytes 208904 | tf_op jit(solution)/shard_map/ppermute | solution.py:39
  84.7 20.7 %collective-permute-start.24 = (f32[520,128]{1,0:T(8,128)S(1)}, f32[520,128]{1,0:T(8,128)S(1)}, u32[]{:S(2)}, u32[]{:S(2)}) collective-permute-start(f32[520,128]{1,0:T(8,128)S(1)} %get-tuple-element.50.refs_4_), channel_id=1, source_target_pairs={{0,2},{2,0},{4,6},{6,4},{8,10},{10,8},{12,14},{14,12},{16,18},{18,... | collective-permute-start | bytes 798728 | tf_op jit(solution)/shard_map/ppermute | solution.py:39
  86.3 19.7 %collective-permute-start.25 = (f32[520,128]{1,0:T(8,128)S(1)}, f32[520,128]{1,0:T(8,128)S(1)}, u32[]{:S(2)}, u32[]{:S(2)}) collective-permute-start(f32[520,128]{1,0:T(8,128)S(1)} %get-tuple-element.51), channel_id=1, source_target_pairs={{0,6},{2,4},{4,2},{6,0},{8,14},{10,12},{12,10},{14,8},{16,22},{18,... | collective-permute-start | bytes 798728 | tf_op jit(solution)/shard_map/ppermute | solution.py:39
  86.3 19.7 %collective-permute-start.23 = (f32[520,128]{1,0:T(8,128)S(1)}, f32[520,128]{1,0:T(8,128)S(1)}, u32[]{:S(2)}, u32[]{:S(2)}) collective-permute-start(f32[520,128]{1,0:T(8,128)S(1)} %get-tuple-element.51), channel_id=1, source_target_pairs={{0,4},{2,6},{4,0},{6,2},{8,12},{10,14},{12,8},{14,10},{16,20},{18,... | collective-permute-start | bytes 798728 | tf_op jit(solution)/shard_map/ppermute | solution.py:39
  86.9 10.1 %collective-permute-start.26 = (f32[8,128]{1,0:T(8,128)S(1)}, f32[8,128]{1,0:T(8,128)S(1)}, u32[]{:S(2)}, u32[]{:S(2)}) collective-permute-start(f32[8,128]{1,0:T(8,128)S(1)} %get-tuple-element.52), channel_id=1, source_target_pairs={{0,2},{2,0},{1,3},{3,1},{4,6},{6,4},{5,7},{7,5},{8,10},{10,8},{9,1... | collective-permute-start | bytes 12296 | tf_op jit(solution)/shard_map/ppermute | solution.py:39
  97.0 1.2 %collective-permute-start.27 = (f32[8,128]{1,0:T(8,128)S(1)}, f32[8,128]{1,0:T(8,128)S(1)}, u32[]{:S(2)}, u32[]{:S(2)}) collective-permute-start(f32[8,128]{1,0:T(8,128)S(1)} %add.25), channel_id=1, source_target_pairs={{0,4},{4,0},{8,12},{12,8},{16,20},{20,16},{24,28},{28,24},{1,5},{5... | collective-permute-start | bytes 12296 | tf_op jit(solution)/shard_map/ppermute | solution.py:39
  98.2 3.6 %collective-permute-start.28 = (f32[8,128]{1,0:T(8,128)S(1)}, f32[8,128]{1,0:T(8,128)S(1)}, u32[]{:S(2)}, u32[]{:S(2)}) collective-permute-start(f32[8,128]{1,0:T(8,128)S(1)} %add.26), channel_id=1, source_target_pairs={{0,1},{1,0},{2,3},{3,2},{4,5},{5,4},{6,7},{7,6},{8,9},{9,8},{10,11... | collective-permute-start | bytes 12296 | tf_op jit(solution)/shard_map/ppermute | solution.py:39
  101.8 3.6 %collective-permute-start.29 = (f32[8,128]{1,0:T(8,128)S(1)}, f32[8,128]{1,0:T(8,128)S(1)}, u32[]{:S(2)}, u32[]{:S(2)}) collective-permute-start(f32[8,128]{1,0:T(8,128)S(1)} %add.27.refs_0_), channel_id=1, source_target_pairs={{0,8},{4,12},{8,0},{12,4},{16,24},{20,28},{24,16},{28,20},{1,9},{5... | collective-permute-start | bytes 12296 | tf_op jit(solution)/shard_map/ppermute | solution.py:39
  105.4 4.5 %collective-permute-start.30 = (f32[8,128]{1,0:T(8,128)S(1)}, f32[8,128]{1,0:T(8,128)S(1)}, u32[]{:S(2)}, u32[]{:S(2)}) collective-permute-start(f32[8,128]{1,0:T(8,128)S(1)} %join.1.refs_8_), channel_id=1, source_target_pairs={{0,16},{4,20},{8,24},{12,28},{16,0},{20,4},{24,8},{28,12},{1,17},{... | collective-permute-start | bytes 12296 | tf_op jit(solution)/shard_map/ppermute | solution.py:39

commit v3 on v2

--- a/solution.py
+++ b/solution.py
@@ -39,18 +39,26 @@
     return lax.ppermute(value, axes, pairs)
 
 
+def halves(value):
+    high = value.astype(jnp.bfloat16)
+    return high, (value - high.astype(jnp.float32)).astype(jnp.bfloat16)
+
+
 def dot(left, right, left_dim, right_dim):
-    return lax.dot_general(
-        left,
-        right,
-        (((left_dim,), (right_dim,)), ((), ())),
-        precision=HIGHEST,
-        preferred_element_type=jnp.float32,
-    )
-
-
-def call(body, out_shapes, name, cost, operands, spaces=(), scratch=(), after=()):
-    spaces = list(spaces) + [pltpu.VMEM] * (len(operands) - len(spaces)) + [pl.ANY] * len(after)
+    def one_pass(left_half, right_half):
+        return lax.dot_general(
+            left_half,
+            right_half,
+            (((left_dim,), (right_dim,)), ((), ())),
+            preferred_element_type=jnp.float32,
+        )
+
+    cross = one_pass(left[0], right[1]) + one_pass(left[1], right[0])
+    return one_pass(left[0], right[0]) + cross
+
+
+def call(body, out_shapes, name, cost, operands, scratch=(), after=(), space=pltpu.VMEM, vmem=32):
+    spaces = [space] * len(operands) + [pl.ANY] * len(after)
     count = len(operands)
 
     def without_after(*refs):
@@ -62,7 +70,7 @@
         in_specs=[pl.BlockSpec(memory_space=space) for space in spaces],
         out_specs=[pl.BlockSpec(memory_space=pltpu.VMEM) for _ in out_shapes],
         scratch_shapes=scratch,
-        compiler_params=pltpu.CompilerParams(vmem_limit_bytes=32 * 2**20),
+        compiler_params=pltpu.CompilerParams(vmem_limit_bytes=vmem * 2**20),
         cost_estimate=pl.CostEstimate(flops=cost, bytes_accessed=2**20, transcendentals=0),
         name=name,
     )(*operands, *after)
@@ -104,7 +112,7 @@
         and part_rows % chunk == 0
         and slot_rows % width == 0
         and part_rows % width == 0
-        and max(slot_rows, part_rows) <= TAIL * width
+        and max(slot_rows, part_rows) < TAIL * width
     )
 
 
@@ -126,17 +134,24 @@
     bias_rows = slot_rows // width
     packed_rows = 2 * slot_rows + TAIL
     packed_shapes = [(packed_rows, width)] * 2
-    matmul_cost = 6 * 2 * slots * query_rows * width
+    matmul_cost = 3 * 2 * slots * query_rows * width
 
     def places():
         page = lax.axis_index("page")
         return page // CORES, page % CORES, lax.axis_index("query")
 
-    def prep_body(queries, keys, values, bias_ref, targets, positions_ref, *refs):
+    def prep_body(
+        queries, keys, values, biases, targets, positions, assignment, *refs
+    ):
         state_outs, refs = refs[:2], refs[2:]
-        query_outs, (targets_out, sems) = refs[:query_devices], refs[query_devices:]
+        query_outs, (targets_out, *refs) = refs[:query_devices], refs[query_devices:]
+        bias_ref, positions_ref, assignment_ref, sems = refs
         rank, core, me = places()
-        copies = []
+        copies = [
+            (assignment, assignment_ref),
+            (positions, positions_ref),
+            (biases, bias_ref),
+        ]
         for turn in range(query_devices):
             head = CORES * (me ^ turn) + core
             copies.append((queries.at[head], query_outs[turn].at[pl.ds(0, part_rows)]))
@@ -154,13 +169,19 @@
         ]
         for copy in copies:
             copy.start()
+        for copy in copies[:3]:
+            copy.wait()
         for turn in range(query_devices):
             row = positions_ref[pl.ds(CORES * (me ^ turn) + core, 1), :].astype(jnp.float32)
             query_outs[turn][part_rows:, :] = row_as_tail(row, width)
+        page_start = assignment_ref[CORES * rank + core] * PAGE_LEN
         for at in range(2):
             row = bias_ref[pl.ds(CORES * me + (core ^ at), 1), :]
             state_outs[at][2 * slot_rows :, :] = row_as_tail(row, width)
-        for copy in copies:
+            state_outs[at][packed_rows - 1 :, :] = jnp.full(
+                (1, width), page_start.astype(jnp.float32)
+            )
+        for copy in copies[3:]:
             copy.wait()
 
     own_state, mate_state, *packed_queries, packed_targets = call(
@@ -168,9 +189,15 @@
         packed_shapes + [(part_rows + TAIL, width)] * query_devices + [(chunk, width)],
         "pack",
         2**20,
-        [queries, compact_keys, compact_values, slot_bias, targets, positions],
-        [pltpu.HBM] * 3 + [pltpu.VMEM, pltpu.HBM],
-        [pltpu.SemaphoreType.DMA((query_devices + 5,))],
+        [queries, compact_keys, compact_values, slot_bias, targets, positions, assignment],
+        [
+            pltpu.VMEM(slot_bias.shape, jnp.float32),
+            pltpu.VMEM(positions.shape, jnp.int32),
+            pltpu.SMEM(assignment.shape, jnp.int32),
+            pltpu.SemaphoreType.DMA((query_devices + 8,)),
+        ],
+        space=pl.ANY,
+        vmem=60,
     )
     query_parts = packed_queries[:1] + [
         exchange(packed_queries[turn], query=turn) for turn in range(1, query_devices)
@@ -205,19 +232,19 @@
             state_ref[value_end:, :] - sizes[2] * grad_ref[value_end:, :],
         )
 
-    def forward(assignment_ref, state_refs, query_refs, chunk_outs, weights_out, max_out, chunks):
-        rank, core, _ = places()
-        all_queries = jnp.concatenate([ref[:part_rows, :] for ref in query_refs], axis=0)
+    def forward(state_refs, query_refs, chunk_outs, weights_out, max_out, chunks):
+        rank, _, _ = places()
+        all_queries = halves(jnp.concatenate([ref[:part_rows, :] for ref in query_refs], axis=0))
         position_row = jnp.concatenate(
             [tail_as_row(ref, part_rows, pos_rows) for ref in query_refs], axis=1
         )
         all_scores, all_visible = [], []
         for at, ref in enumerate(state_refs):
-            scores = dot(ref[:slot_rows, :], all_queries, 1, 1) * score_scale
+            scores = dot(halves(ref[:slot_rows, :]), all_queries, 1, 1) * score_scale
             bias = row_as_column(tail_as_row(ref, 2 * slot_rows, bias_rows), width)
             scores = scores + jnp.concatenate([bias] * (query_rows // width), axis=1)
-            page_start = assignment_ref[CORES * rank + (core ^ at)] * PAGE_LEN
-            visible = jnp.broadcast_to(position_row, scores.shape) >= page_start.astype(jnp.float32)
+            page_start = ref[packed_rows - 1 : packed_rows, 0:1]
+            visible = jnp.broadcast_to(position_row >= page_start, scores.shape)
             all_scores.append(jnp.where(visible, scores, MASKED))
             all_visible.append(visible)
         row_max = jnp.max(all_scores[0], axis=0, keepdims=True)
@@ -229,7 +256,8 @@
             weights = jnp.where(all_visible[at], jnp.exp(all_scores[at] - row_max), 0.0)
             weights_out[at * slot_rows : (at + 1) * slot_rows, :] = weights
             row_total = row_total + jnp.sum(weights, axis=0, keepdims=True)
-            row_sum = row_sum + dot(ref[slot_rows : 2 * slot_rows, :], weights, 0, 0)
+            values = halves(ref[slot_rows : 2 * slot_rows, :])
+            row_sum = row_sum + dot(values, halves(weights), 0, 0)
         max_out[...] = jnp.broadcast_to(row_max, (TAIL, query_rows))
         tail = jnp.concatenate(
             [row_max, row_total, jnp.zeros((TAIL - 2, query_rows), jnp.float32)], axis=0
@@ -245,16 +273,17 @@
     forward_shapes = [chunk_shape] * ranks + [(slots, query_rows), (TAIL, query_rows)]
     chunk_scratch = [pltpu.VMEM((ranks,) + chunk_shape, jnp.float32)]
 
-    def first_body(assignment_ref, *refs):
+    def first_body(*refs):
         state_refs, refs = refs[:2], refs[2:]
         query_refs, refs = refs[:query_devices], refs[query_devices:]
         chunk_outs, refs = refs[:ranks], refs[ranks:]
-        forward(assignment_ref, state_refs, query_refs, chunk_outs, *refs)
-
-    def next_body(assignment_ref, *refs):
+        forward(state_refs, query_refs, chunk_outs, *refs)
+
+    def next_body(*refs):
         state_refs, refs = refs[:2], refs[2:]
         query_refs, refs = refs[:query_devices], refs[query_devices:]
-        grad_refs, tile_refs, refs = refs[:2], refs[2:4], refs[4:]
+        grad_refs, refs = refs[:2], refs[2:]
+        tile_refs, refs = refs[: len(tiles)], refs[len(tiles) :]
         state_outs, refs = refs[:2], refs[2:]
         chunk_outs, refs = refs[:ranks], refs[ranks:]
         sizes = step_sizes(tile_refs)
@@ -263,7 +292,7 @@
             state_outs[at][:slot_rows, :] = keys
             state_outs[at][slot_rows : 2 * slot_rows, :] = values
             state_outs[at][2 * slot_rows :, :] = bias
-        forward(assignment_ref, state_outs, query_refs, chunk_outs, *refs)
+        forward(state_outs, query_refs, chunk_outs, *refs)
 
     def merge_body(targets_ref, *refs):
         chunk_refs, (merged_out,) = refs[:ranks], refs[ranks:]
@@ -297,15 +326,17 @@
         row_max, row_total, row_delta = (
             joined[width + at : width + at + 1, :] for at in range(3)
         )
-        all_queries = jnp.concatenate([ref[:part_rows, :] for ref in query_refs], axis=0)
+        all_queries = halves(jnp.concatenate([ref[:part_rows, :] for ref in query_refs], axis=0))
+        residual = halves(residual)
         factor = jnp.exp(max_ref[0:1, :] - row_max) / row_total
-        ones = jnp.ones((TAIL, query_rows), jnp.float32)
+        ones = jnp.ones((TAIL, query_rows), jnp.bfloat16)
+        ones = (ones, jnp.zeros_like(ones))
         squares = [jnp.zeros((1, width), jnp.float32)] * 3
         for at, ref in enumerate(state_refs):
             attention = weights_ref[at * slot_rows : (at + 1) * slot_rows, :] * factor
-            grad_values = dot(attention, residual, 1, 1)
-            grad_probs = dot(ref[slot_rows : 2 * slot_rows, :], residual, 1, 0)
-            grad_scores = attention * (grad_probs - row_delta)
+            grad_values = dot(halves(attention), residual, 1, 1)
+            grad_probs = dot(halves(ref[slot_rows : 2 * slot_rows, :]), residual, 1, 0)
+            grad_scores = halves(attention * (grad_probs - row_delta))
             grad_keys = dot(grad_scores, all_queries, 1, 0) * score_scale
             grad_bias = row_as_tail(dot(ones, grad_scores, 1, 1)[0:1, :], width)
             grad_outs[at][:slot_rows, :] = grad_keys
@@ -317,18 +348,29 @@
             squares + [jnp.zeros((TAIL - 3, width), jnp.float32)], axis=0
         )
 
-    def join_body(left_ref, right_ref, out_ref):
-        out_ref[...] = left_ref[...] + right_ref[...]
-
-    def axis_rounds(axis, size, least=1):
-        return [{axis: 1 << bit} for bit in range(size.bit_length() - 1) if 1 << bit >= least]
-
-    rounds = (
-        axis_rounds("query", query_devices)
-        + [{"page": 1}]
-        + axis_rounds("head", head_devices)
-        + axis_rounds("page", ranks * CORES, CORES)
-    )
+    def join_body(*refs):
+        total = refs[0][...]
+        for ref in refs[1:-1]:
+            total = total + ref[...]
+        refs[-1][...] = total
+
+    def group(**sizes):
+        masks = itertools.product(*(range(0, size, step) for size, step in sizes.values()))
+        return [dict(zip(sizes, mask)) for mask in masks if any(mask)]
+
+    core_round = group(page=(CORES, 1))
+    rank_round = group(page=(ranks * CORES, CORES))
+    first_rounds = [
+        core_round,
+        group(query=(query_devices, 1), head=(head_devices, 1)),
+        rank_round,
+    ]
+    last_rounds = [
+        core_round,
+        group(head=(head_devices, 1)),
+        rank_round,
+        group(query=(query_devices, 1)),
+    ]
 
     out_masks = list(itertools.product(range(query_devices), range(CORES)))
 
@@ -346,8 +388,7 @@
                 forward_shapes,
                 "forward",
                 2 * matmul_cost,
-                [assignment] + states + query_parts,
-                [pltpu.SMEM],
+                states + query_parts,
                 chunk_scratch,
             )
         else:
@@ -356,8 +397,7 @@
                 packed_shapes + forward_shapes,
                 "update_forward",
                 2 * matmul_cost,
-                [assignment] + states + query_parts + grads + tiles,
-                [pltpu.SMEM],
+                states + query_parts + grads + tiles,
                 chunk_scratch,
             )
             states = [own_new, mate_new]
@@ -391,20 +431,23 @@
         grads = [own_grad, mate_grad]
         if last:
             all_grads = [to_output(grads, mask) for mask in out_masks]
-        tiles = [squares, exchange(squares, **rounds[0])]
-        for at, masks in enumerate(rounds[1:], 1):
+        rounds = last_rounds if last else first_rounds
+        tiles = [squares]
+        for at, masks in enumerate(rounds):
+            joined = tiles[0]
             if last and at == len(rounds) - 1:
                 (joined,) = call(
                     join_body, [squares.shape], "join", 2**10, tiles, after=all_grads[2:3]
                 )
             else:
-                joined = tiles[0] + tiles[1]
-            tiles = [joined, exchange(joined, **masks)]
+                for tile in tiles[1:]:
+                    joined = joined + tile
+            tiles = [joined] + [exchange(joined, **mask) for mask in masks]
 
     def last_body(*refs):
         state_refs, refs = refs[:local_heads], refs[local_heads:]
         grad_refs, refs = refs[:local_heads], refs[local_heads:]
-        tile_refs, (keys_out, values_out, bias_out) = refs[:2], refs[2:]
+        tile_refs, (keys_out, values_out, bias_out) = refs[: len(tiles)], refs[len(tiles) :]
         _, core, me = places()
         sizes = step_sizes(tile_refs)
         for at, (turn, flip) in enumerate(out_masks):

time: 111 us -> 94.5 us (0.85)
  waiting for transfers between devices: 54.5 us -> 42 us
  local copies, waits for them, and re-layouts: 6.19 us -> 1.87 us
  starting transfers between devices: 35.3 us -> 39.4 us
  Pallas kernels: 14.3 us -> 10.3 us
    ppermute x30 -> x33, waiting for transfers between devices: 54.5 us -> 42 us  [exchange(): return lax.ppermute(value, axes, pairs)]
    unnamed x14 -> x10, local copies, waits for them, and re-layouts: 6.19 us -> 1.87 us
    ppermute x30 -> x33, starting transfers between devices: 34.4 us -> 38.7 us  [exchange(): return lax.ppermute(value, axes, pairs)]
    pallas_call x9, Pallas kernels: 14.3 us -> 10.3 us  [call(): pl.pallas_call(without_after, out_shape=[jax.ShapeDtypeStruct(shape, jnp....]
  transfers between devices with their start and end apart: 31 -> 34, of which waited for: 20 -> 22; matrix products, arithmetic and copies ran while one was open for 0% -> 0% of each run, Pallas kernels for 0% -> 0%
where the time goes in v3:
time: 94.5 us; the launch traced here: 94.3 us
  waiting for transfers between devices  42 us (44%)
  starting transfers between devices  39.4 us (42%)
  Pallas kernels  10.3 us (11%)
  local copies, waits for them, and re-layouts  1.87 us (2%)
    ppermute x33, waiting for transfers between devices, exchange(): return lax.ppermute(value, axes, pairs)  42 us
    ppermute x33, starting transfers between devices, exchange(): return lax.ppermute(value, axes, pairs)  38.7 us
    pallas_call x9, Pallas kernels, call(): pl.pallas_call(without_after, out_shape=[jax.ShapeDtypeStruct(shape, jnp....  10.3 us
  transfers between devices with their start and end apart: 34, of which 22 were waited for; matrix products, arithmetic and copies ran while one was open for 0% of the time, Pallas kernels for 0%

profile of v3, /device:TPU:0, one launch (start us, length us, event | category | flops | bytes accessed | tf_op | source)
XLA Modules:
  0.0 94.3 jit_solution(17669874115343591708)
XLA Ops:
  0.6 2.2 %pack.1 = (f32[520,128]{1,0:T(8,128)}, f32[520,128]{1,0:T(8,128)}, f32[264,128]{1,0:T(8,128)}, f32[264,128]{1,0:T(8,128)}, f32[128,128]{1,0:T(8,128)}) custom-call(f32[4,256,128]{2,1,0:T(8,128)} %refs_0_.1, f32[4,256,128]{2,1,0:T(8,128)} %refs_1_.1, f32[4,256,128]{2,1,0:T(8,128)} %refs_2_.1, f32[4,256]{1,0:T(4,128)} %refs_3_.1, f32[4,256,128]{2,1,0:T(8,128)} %refs_4_.1, ...), custom_call_target="tpu_custom_call" | custom-call | flops 1048576 | bytes 1048576 | tf_op jit(solution)/shard_map/pack/pallas_call | solution.py:67
  3.4 2.6 %collective-permute-start.1 = (f32[264,128]{1,0:T(8,128)}, f32[264,128]{1,0:T(8,128)S(1)}, u32[]{:S(2)}, u32[]{:S(2)}) collective-permute-start(f32[264,128]{1,0:T(8,128)} %get-tuple-element.31), channel_id=1, source_target_pairs={{0,2},{2,0},{1,3},{3,1},{4,6},{6,4},{5,7},{7,5},{8,10},{10,8},{9,1... | collective-permute-start | bytes 405512 | tf_op jit(solution)/shard_map/ppermute | solution.py:39
  6.0 4.4 %collective-permute-done.1.refs_3_.refs_5_ = f32[264,128]{1,0:T(8,128)S(1)} collective-permute-done((f32[264,128]{1,0:T(8,128)}, f32[264,128]{1,0:T(8,128)S(1)}, u32[]{:S(2)}, u32[]{:S(2)}) %collective-permute-start.1) | collective-permute-done | bytes 135200 | tf_op jit(solution)/shard_map/ppermute | solution.py:39
  10.3 0.9 copy-done
  11.3 0.9 %copy-done.2 = f32[520,128]{1,0:T(8,128)S(1)} copy-done((f32[520,128]{1,0:T(8,128)S(1)}, f32[520,128]{1,0:T(8,128)}, u32[]{:S(2)}) %copy-start.2) | copy-done | bytes 266264
  12.2 1.2 %forward.1 = (f32[136,128]{1,0:T(8,128)S(1)}, f32[136,128]{1,0:T(8,128)S(1)}, f32[136,128]{1,0:T(8,128)S(1)}, f32[136,128]{1,0:T(8,128)S(1)}, f32[512,512]{1,0:T(8,128)S(1)}, /*index=5*/f32[8,512]{1,0:T(8,128)S(1)}) custom-call(f32[520,128]{1,0:T(8,128)S(1)} %copy-done.2, f32[520,128]{1,0:T(8,128)S(1)} %collective-permute-done.refs_1_.refs_3_, ...), custom_call_target="tpu_custom_call" | custom-call | flops 402653184 | bytes 1048576 | tf_op jit(solution)/shard_map/forward/pallas_call | solution.py:67
  13.5 1.9 %collective-permute-start.3 = (f32[136,128]{1,0:T(8,128)S(1)}, f32[136,128]{1,0:T(8,128)S(1)}, u32[]{:S(2)}, u32[]{:S(2)}) collective-permute-start(f32[136,128]{1,0:T(8,128)S(1)} %get-tuple-element.36), channel_id=1, source_target_pairs={{0,8},{4,12},{8,0},{12,4},{16,24},{20,28},{24,16},{28,20},{1,9},{5... | collective-permute-start | bytes 208904 | tf_op jit(solution)/shard_map/ppermute | solution.py:39
  15.4 2.6 %collective-permute-start.4 = (f32[136,128]{1,0:T(8,128)S(1)}, f32[136,128]{1,0:T(8,128)S(1)}, u32[]{:S(2)}, u32[]{:S(2)}) collective-permute-start(f32[136,128]{1,0:T(8,128)S(1)} %get-tuple-element.37), channel_id=1, source_target_pairs={{0,16},{4,20},{8,24},{12,28},{16,0},{20,4},{24,8},{28,12},{1,17},{... | collective-permute-start | bytes 208904 | tf_op jit(solution)/shard_map/ppermute | solution.py:39
  18.0 0.7 collective-permute-start.2
  18.6 4.1 %collective-permute-done.4.refs_3_ = f32[136,128]{1,0:T(8,128)S(1)} collective-permute-done((f32[136,128]{1,0:T(8,128)S(1)}, f32[136,128]{1,0:T(8,128)S(1)}, u32[]{:S(2)}, u32[]{:S(2)}) %collective-permute-start.4) | collective-permute-done | bytes 69664 | tf_op jit(solution)/shard_map/ppermute | solution.py:39
  22.7 1.5 %collective-permute-done.5.refs_4_ = f32[136,128]{1,0:T(8,128)S(1)} collective-permute-done((f32[136,128]{1,0:T(8,128)S(1)}, f32[136,128]{1,0:T(8,128)S(1)}, u32[]{:S(2)}, u32[]{:S(2)}) %collective-permute-start.5) | collective-permute-done | bytes 69664 | tf_op jit(solution)/shard_map/ppermute | solution.py:39
  24.3 3.8 %collective-permute-start.8 = (f32[136,128]{1,0:T(8,128)S(1)}, f32[136,128]{1,0:T(8,128)S(1)}, u32[]{:S(2)}, u32[]{:S(2)}) collective-permute-start(f32[136,128]{1,0:T(8,128)S(1)} %merge.2.refs_6_), channel_id=1, source_target_pairs={{0,24},{4,28},{8,16},{12,20},{16,8},{20,12},{24,0},{28,4},{1,25},{... | collective-permute-start | bytes 208904 | tf_op jit(solution)/shard_map/ppermute | solution.py:39
  28.1 0.6 collective-permute-start.6
  28.8 1.8 %collective-permute-done.8.refs_9_ = f32[136,128]{1,0:T(8,128)S(1)} collective-permute-done((f32[136,128]{1,0:T(8,128)S(1)}, f32[136,128]{1,0:T(8,128)S(1)}, u32[]{:S(2)}, u32[]{:S(2)}) %collective-permute-start.8) | collective-permute-done | bytes 69664 | tf_op jit(solution)/shard_map/ppermute | solution.py:39
  30.6 2.8 %collective-permute-done.7.refs_8_ = f32[136,128]{1,0:T(8,128)S(1)} collective-permute-done((f32[136,128]{1,0:T(8,128)S(1)}, f32[136,128]{1,0:T(8,128)S(1)}, u32[]{:S(2)}, u32[]{:S(2)}) %collective-permute-start.7) | collective-permute-done | bytes 69664 | tf_op jit(solution)/shard_map/ppermute | solution.py:39
  33.3 2.1 %backward.2 = (f32[520,128]{1,0:T(8,128)S(1)}, f32[520,128]{1,0:T(8,128)S(1)}, f32[8,128]{1,0:T(8,128)S(1)}) custom-call(f32[512,512]{1,0:T(8,128)S(1)} %get-tuple-element.32.refs_0_, f32[8,512]{1,0:T(8,128)S(1)} %get-tuple-element.33.refs_1_, f32[520,128]{1,0:T(8,128)S(1)} %copy-done.3, f32[520,128]{1,0:T(8,128)S(1)} %collective-permute-done.refs_1_.refs_3_, ...), custom_call_target="tpu_custom_call" | custom-call | flops 603979776 | bytes 1048576 | tf_op jit(solution)/shard_map/backward/pallas_call | solution.py:67
  35.5 1.2 %collective-permute-done.9 = f32[8,128]{1,0:T(8,128)S(1)} collective-permute-done((f32[8,128]{1,0:T(8,128)S(1)}, f32[8,128]{1,0:T(8,128)S(1)}, u32[]{:S(2)}, u32[]{:S(2)}) %collective-permute-start.9) | collective-permute-done | bytes 4128 | tf_op jit(solution)/shard_map/ppermute | solution.py:39
  36.7 2.4 %collective-permute-start.12 = (f32[8,128]{1,0:T(8,128)S(1)}, f32[8,128]{1,0:T(8,128)S(1)}, u32[]{:S(2)}, u32[]{:S(2)}) collective-permute-start(f32[8,128]{1,0:T(8,128)S(1)} %add.18), channel_id=1, source_target_pairs={{0,3},{1,2},{2,1},{3,0},{4,7},{5,6},{6,5},{7,4},{8,11},{9,10},{10,... | collective-permute-start | bytes 12296 | tf_op jit(solution)/shard_map/ppermute | solution.py:39
  40.2 1.0 %collective-permute-done.12 = f32[8,128]{1,0:T(8,128)S(1)} collective-permute-done((f32[8,128]{1,0:T(8,128)S(1)}, f32[8,128]{1,0:T(8,128)S(1)}, u32[]{:S(2)}, u32[]{:S(2)}) %collective-permute-start.12) | collective-permute-done | bytes 4128 | tf_op jit(solution)/shard_map/ppermute | solution.py:39
  41.2 1.5 %collective-permute-done.11 = f32[8,128]{1,0:T(8,128)S(1)} collective-permute-done((f32[8,128]{1,0:T(8,128)S(1)}, f32[8,128]{1,0:T(8,128)S(1)}, u32[]{:S(2)}, u32[]{:S(2)}) %collective-permute-start.11) | collective-permute-done | bytes 4128 | tf_op jit(solution)/shard_map/ppermute | solution.py:39
  43.2 1.6 %collective-permute-start.15 = (f32[8,128]{1,0:T(8,128)S(1)}, f32[8,128]{1,0:T(8,128)S(1)}, u32[]{:S(2)}, u32[]{:S(2)}) collective-permute-start(f32[8,128]{1,0:T(8,128)S(1)} %add_add_fusion.refs_6_), channel_id=1, source_target_pairs={{0,24},{4,28},{8,16},{12,20},{16,8},{20,12},{24,0},{28,4},{1,25},{... | collective-permute-start | bytes 12296 | tf_op jit(solution)/shard_map/ppermute | solution.py:39
  45.3 2.3 %collective-permute-start.13 = (f32[8,128]{1,0:T(8,128)S(1)}, f32[8,128]{1,0:T(8,128)S(1)}, u32[]{:S(2)}, u32[]{:S(2)}) collective-permute-start(f32[8,128]{1,0:T(8,128)S(1)} %add_add_fusion.refs_6_), channel_id=1, source_target_pairs={{0,8},{4,12},{8,0},{12,4},{16,24},{20,28},{24,16},{28,20},{1,9},{5... | collective-permute-start | bytes 12296 | tf_op jit(solution)/shard_map/ppermute | solution.py:39
  47.6 1.0 %collective-permute-done.15.refs_9_ = f32[8,128]{1,0:T(8,128)S(1)} collective-permute-done((f32[8,128]{1,0:T(8,128)S(1)}, f32[8,128]{1,0:T(8,128)S(1)}, u32[]{:S(2)}, u32[]{:S(2)}) %collective-permute-start.15) | collective-permute-done | bytes 4128 | tf_op jit(solution)/shard_map/ppermute | solution.py:39
  48.6 0.7 collective-permute-done.14.refs_8_
  49.4 1.3 %update_forward.1 = (f32[520,128]{1,0:T(8,128)S(1)}, f32[520,128]{1,0:T(8,128)S(1)}, f32[136,128]{1,0:T(8,128)S(1)}, f32[136,128]{1,0:T(8,128)S(1)}, f32[136,128...) custom-call(f32[520,128]{1,0:T(8,128)S(1)} %copy-done.3, ...), custom_call_target="tpu_custom_call" | custom-call | flops 402653184 | bytes 1048576 | tf_op jit(solution)/shard_map/update_forward/pallas_call | solution.py:67
  50.7 1.6 %collective-permute-start.17 = (f32[520,128]{1,0:T(8,128)S(1)}, f32[520,128]{1,0:T(8,128)S(1)}, u32[]{:S(2)}, u32[]{:S(2)}) collective-permute-start(f32[520,128]{1,0:T(8,128)S(1)} %get-tuple-element.42.refs_2_.refs_0_), channel_id=1, source_target_pairs={{0,2},{2,0},{4,6},{6,4},{8,10},{10,8},{12,14},{14,12},{16,18},{18,... | collective-permute-start | bytes 798728 | tf_op jit(solution)/shard_map/ppermute | solution.py:39
  52.3 0.6 collective-permute-start.16
  52.9 1.8 %collective-permute-start.19 = (f32[136,128]{1,0:T(8,128)S(1)}, f32[136,128]{1,0:T(8,128)S(1)}, u32[]{:S(2)}, u32[]{:S(2)}) collective-permute-start(f32[136,128]{1,0:T(8,128)S(1)} %get-tuple-element.47), channel_id=1, source_target_pairs={{0,8},{4,12},{8,0},{12,4},{16,24},{20,28},{24,16},{28,20},{1,9},{5... | collective-permute-start | bytes 208904 | tf_op jit(solution)/shard_map/ppermute | solution.py:39
  54.8 1.1 %collective-permute-start.20 = (f32[136,128]{1,0:T(8,128)S(1)}, f32[136,128]{1,0:T(8,128)S(1)}, u32[]{:S(2)}, u32[]{:S(2)}) collective-permute-start(f32[136,128]{1,0:T(8,128)S(1)} %get-tuple-element.48), channel_id=1, source_target_pairs={{0,16},{4,20},{8,24},{12,28},{16,0},{20,4},{24,8},{28,12},{1,17},{... | collective-permute-start | bytes 208904 | tf_op jit(solution)/shard_map/ppermute | solution.py:39
  55.9 1.3 %collective-permute-done.19.refs_2_ = f32[136,128]{1,0:T(8,128)S(1)} collective-permute-done((f32[136,128]{1,0:T(8,128)S(1)}, f32[136,128]{1,0:T(8,128)S(1)}, u32[]{:S(2)}, u32[]{:S(2)}) %collective-permute-start.19) | collective-permute-done | bytes 69664 | tf_op jit(solution)/shard_map/ppermute | solution.py:39
  57.2 2.4 %collective-permute-start.21 = (f32[136,128]{1,0:T(8,128)S(1)}, f32[136,128]{1,0:T(8,128)S(1)}, u32[]{:S(2)}, u32[]{:S(2)}) collective-permute-start(f32[136,128]{1,0:T(8,128)S(1)} %get-tuple-element.49), channel_id=1, source_target_pairs={{0,24},{4,28},{8,16},{12,20},{16,8},{20,12},{24,0},{28,4},{1,25},{... | collective-permute-start | bytes 208904 | tf_op jit(solution)/shard_map/ppermute | solution.py:39
  59.6 2.3 %collective-permute-done.20.refs_3_ = f32[136,128]{1,0:T(8,128)S(1)} collective-permute-done((f32[136,128]{1,0:T(8,128)S(1)}, f32[136,128]{1,0:T(8,128)S(1)}, u32[]{:S(2)}, u32[]{:S(2)}) %collective-permute-start.20) | collective-permute-done | bytes 69664 | tf_op jit(solution)/shard_map/ppermute | solution.py:39
  61.9 1.5 %collective-permute-done.21.refs_4_ = f32[136,128]{1,0:T(8,128)S(1)} collective-permute-done((f32[136,128]{1,0:T(8,128)S(1)}, f32[136,128]{1,0:T(8,128)S(1)}, u32[]{:S(2)}, u32[]{:S(2)}) %collective-permute-start.21) | collective-permute-done | bytes 69664 | tf_op jit(solution)/shard_map/ppermute | solution.py:39
  63.5 2.4 %collective-permute-start.24 = (f32[136,128]{1,0:T(8,128)S(1)}, f32[136,128]{1,0:T(8,128)S(1)}, u32[]{:S(2)}, u32[]{:S(2)}) collective-permute-start(f32[136,128]{1,0:T(8,128)S(1)} %merge.3.refs_6_), channel_id=1, source_target_pairs={{0,24},{4,28},{8,16},{12,20},{16,8},{20,12},{24,0},{28,4},{1,25},{... | collective-permute-start | bytes 208904 | tf_op jit(solution)/shard_map/ppermute | solution.py:39
  66.3 1.7 %collective-permute-start.22 = (f32[136,128]{1,0:T(8,128)S(1)}, f32[136,128]{1,0:T(8,128)S(1)}, u32[]{:S(2)}, u32[]{:S(2)}) collective-permute-start(f32[136,128]{1,0:T(8,128)S(1)} %merge.3.refs_6_), channel_id=1, source_target_pairs={{0,8},{4,12},{8,0},{12,4},{16,24},{20,28},{24,16},{28,20},{1,9},{5... | collective-permute-start | bytes 208904 | tf_op jit(solution)/shard_map/ppermute | solution.py:39
  68.0 1.9 %collective-permute-done.24.refs_9_ = f32[136,128]{1,0:T(8,128)S(1)} collective-permute-done((f32[136,128]{1,0:T(8,128)S(1)}, f32[136,128]{1,0:T(8,128)S(1)}, u32[]{:S(2)}, u32[]{:S(2)}) %collective-permute-start.24) | collective-permute-done | bytes 69664 | tf_op jit(solution)/shard_map/ppermute | solution.py:39
  69.9 1.5 %collective-permute-done.23.refs_8_ = f32[136,128]{1,0:T(8,128)S(1)} collective-permute-done((f32[136,128]{1,0:T(8,128)S(1)}, f32[136,128]{1,0:T(8,128)S(1)}, u32[]{:S(2)}, u32[]{:S(2)}) %collective-permute-start.23) | collective-permute-done | bytes 69664 | tf_op jit(solution)/shard_map/ppermute | solution.py:39
  71.4 2.1 %backward.3 = (f32[520,128]{1,0:T(8,128)S(1)}, f32[520,128]{1,0:T(8,128)S(1)}, f32[8,128]{1,0:T(8,128)S(1)}) custom-call(f32[512,512]{1,0:T(8,128)S(1)} %get-tuple-element.44.refs_0_, f32[8,512]{1,0:T(8,128)S(1)} %get-tuple-element.45.refs_1_, f32[520,128]{1,0:T(8,128)S(1)} %get-tuple-element.42.refs_2_.refs_0_, f32[520,128]{1,0:T(8,128)S(1)} %get-tuple-element.43.refs_3_, ...), custom_call_target="tpu_custom_call" | custom-call | flops 603979776 | bytes 1048576 | tf_op jit(solution)/shard_map/backward/pallas_call | solution.py:67
  73.5 1.6 %collective-permute-start.26 = (f32[520,128]{1,0:T(8,128)S(1)}, f32[520,128]{1,0:T(8,128)S(1)}, u32[]{:S(2)}, u32[]{:S(2)}) collective-permute-start(f32[520,128]{1,0:T(8,128)S(1)} %get-tuple-element.50.refs_4_), channel_id=1, source_target_pairs={{0,2},{2,0},{4,6},{6,4},{8,10},{10,8},{12,14},{14,12},{16,18},{18,... | collective-permute-start | bytes 798728 | tf_op jit(solution)/shard_map/ppermute | solution.py:39
  75.7 1.2 %collective-permute-done.28 = f32[8,128]{1,0:T(8,128)S(1)} collective-permute-done((f32[8,128]{1,0:T(8,128)S(1)}, f32[8,128]{1,0:T(8,128)S(1)}, u32[]{:S(2)}, u32[]{:S(2)}) %collective-permute-start.28) | collective-permute-done | bytes 4128 | tf_op jit(solution)/shard_map/ppermute | solution.py:39
  77.4 3.1 %collective-permute-done.29 = f32[8,128]{1,0:T(8,128)S(1)} collective-permute-done((f32[8,128]{1,0:T(8,128)S(1)}, f32[8,128]{1,0:T(8,128)S(1)}, u32[]{:S(2)}, u32[]{:S(2)}) %collective-permute-start.29) | collective-permute-done | bytes 4128 | tf_op jit(solution)/shard_map/ppermute | solution.py:39
  80.5 2.2 %collective-permute-start.32 = (f32[8,128]{1,0:T(8,128)S(1)}, f32[8,128]{1,0:T(8,128)S(1)}, u32[]{:S(2)}, u32[]{:S(2)}) collective-permute-start(f32[8,128]{1,0:T(8,128)S(1)} %add.23.refs_0_), channel_id=1, source_target_pairs={{0,24},{4,28},{8,16},{12,20},{16,8},{20,12},{24,0},{28,4},{1,25},{... | collective-permute-start | bytes 12296 | tf_op jit(solution)/shard_map/ppermute | solution.py:39
  82.8 3.1 %collective-permute-done.32.refs_3_ = f32[8,128]{1,0:T(8,128)S(1)} collective-permute-done((f32[8,128]{1,0:T(8,128)S(1)}, f32[8,128]{1,0:T(8,128)S(1)}, u32[]{:S(2)}, u32[]{:S(2)}) %collective-permute-start.32) | collective-permute-done | bytes 4128 | tf_op jit(solution)/shard_map/ppermute | solution.py:39
  85.9 1.3 %collective-permute-done.31.refs_2_ = f32[8,128]{1,0:T(8,128)S(1)} collective-permute-done((f32[8,128]{1,0:T(8,128)S(1)}, f32[8,128]{1,0:T(8,128)S(1)}, u32[]{:S(2)}, u32[]{:S(2)}) %collective-permute-start.31) | collective-permute-done | bytes 4128 | tf_op jit(solution)/shard_map/ppermute | solution.py:39
  87.2 2.3 %collective-permute-done.30.refs_1_ = f32[8,128]{1,0:T(8,128)S(1)} collective-permute-done((f32[8,128]{1,0:T(8,128)S(1)}, f32[8,128]{1,0:T(8,128)S(1)}, u32[]{:S(2)}, u32[]{:S(2)}) %collective-permute-start.30) | collective-permute-done | bytes 4128 | tf_op jit(solution)/shard_map/ppermute | solution.py:39
  89.5 1.6 %collective-permute-start.33 = (f32[8,128]{1,0:T(8,128)S(1)}, f32[8,128]{1,0:T(8,128)S(1)}, u32[]{:S(2)}, u32[]{:S(2)}) collective-permute-start(f32[8,128]{1,0:T(8,128)S(1)} %join.1.refs_8_), channel_id=1, source_target_pairs={{0,2},{2,0},{1,3},{3,1},{4,6},{6,4},{5,7},{7,5},{8,10},{10,8},{9,1... | collective-permute-start | bytes 12296 | tf_op jit(solution)/shard_map/ppermute | solution.py:39
  91.1 2.1 %collective-permute-done.33.refs_9_ = f32[8,128]{1,0:T(8,128)S(1)} collective-permute-done((f32[8,128]{1,0:T(8,128)S(1)}, f32[8,128]{1,0:T(8,128)S(1)}, u32[]{:S(2)}, u32[]{:S(2)}) %collective-permute-start.33) | collective-permute-done | bytes 4128 | tf_op jit(solution)/shard_map/ppermute | solution.py:39
  93.2 1.1 %last_update.1 = (f32[4,256,128]{2,1,0:T(8,128)}, f32[4,256,128]{2,1,0:T(8,128)}, f32[4,256]{1,0:T(4,128)}) custom-call(f32[520,128]{1,0:T(8,128)S(1)} %get-tuple-element.42.refs_2_.refs_0_, f32[520,128]{1,0:T(8,128)S(1)} %collective-permute-done.16.refs_10_.refs_1_, f32[520,128]{1,0:T(8,128)S(1)} %collective-permute-done.17.refs_5_.refs_2_, ...), custom_call_target="tpu_custom_call" | custom-call | flops 1048576 | bytes 1048576 | tf_op jit(solution)/shard_map/last_update/pallas_call | solution.py:67
  (43 shorter events, 4.5 us)
Async XLA Ops:
  2.8 7.5 %collective-permute-start = (f32[520,128]{1,0:T(8,128)}, f32[520,128]{1,0:T(8,128)S(1)}, u32[]{:S(2)}, u32[]{:S(2)}) collective-permute-start(f32[520,128]{1,0:T(8,128)} %get-tuple-element.29), channel_id=1, source_target_pairs={{0,4},{4,0},{8,12},{12,8},{16,20},{20,16},{24,28},{28,24},{1,5},{5... | collective-permute-start | bytes 798728 | tf_op jit(solution)/shard_map/ppermute | solution.py:39
  3.4 7.0 %collective-permute-start.1 = (f32[264,128]{1,0:T(8,128)}, f32[264,128]{1,0:T(8,128)S(1)}, u32[]{:S(2)}, u32[]{:S(2)}) collective-permute-start(f32[264,128]{1,0:T(8,128)} %get-tuple-element.31), channel_id=1, source_target_pairs={{0,2},{2,0},{1,3},{3,1},{4,6},{6,4},{5,7},{7,5},{8,10},{10,8},{9,1... | collective-permute-start | bytes 405512 | tf_op jit(solution)/shard_map/ppermute | solution.py:39
  10.3 0.9 copy-start
  11.3 1.0 %copy-start.2 = (f32[520,128]{1,0:T(8,128)S(1)}, f32[520,128]{1,0:T(8,128)}, u32[]{:S(2)}) copy-start(f32[520,128]{1,0:T(8,128)} %get-tuple-element.28.refs_0_.refs_2_) | copy-start | bytes 798724
  12.2 5.7 %copy-start.4 = (f32[128,128]{1,0:T(8,128)S(1)}, f32[128,128]{1,0:T(8,128)}, u32[]{:S(2)}) copy-start(f32[128,128]{1,0:T(8,128)} %get-tuple-element.34) | copy-start | bytes 196612
  13.5 19.9 %copy-start.3 = (f32[520,128]{1,0:T(8,128)S(1)}, f32[520,128]{1,0:T(8,128)}, u32[]{:S(2)}) copy-start(f32[520,128]{1,0:T(8,128)} %get-tuple-element.28.refs_0_.refs_2_) | copy-start | bytes 798724
  13.5 5.2 %collective-permute-start.3 = (f32[136,128]{1,0:T(8,128)S(1)}, f32[136,128]{1,0:T(8,128)S(1)}, u32[]{:S(2)}, u32[]{:S(2)}) collective-permute-start(f32[136,128]{1,0:T(8,128)S(1)} %get-tuple-element.36), channel_id=1, source_target_pairs={{0,8},{4,12},{8,0},{12,4},{16,24},{20,28},{24,16},{28,20},{1,9},{5... | collective-permute-start | bytes 208904 | tf_op jit(solution)/shard_map/ppermute | solution.py:39
  15.4 7.3 %collective-permute-start.4 = (f32[136,128]{1,0:T(8,128)S(1)}, f32[136,128]{1,0:T(8,128)S(1)}, u32[]{:S(2)}, u32[]{:S(2)}) collective-permute-start(f32[136,128]{1,0:T(8,128)S(1)} %get-tuple-element.37), channel_id=1, source_target_pairs={{0,16},{4,20},{8,24},{12,28},{16,0},{20,4},{24,8},{28,12},{1,17},{... | collective-permute-start | bytes 208904 | tf_op jit(solution)/shard_map/ppermute | solution.py:39
  17.9 6.2 %collective-permute-start.5 = (f32[136,128]{1,0:T(8,128)S(1)}, f32[136,128]{1,0:T(8,128)S(1)}, u32[]{:S(2)}, u32[]{:S(2)}) collective-permute-start(f32[136,128]{1,0:T(8,128)S(1)} %get-tuple-element.38), channel_id=1, source_target_pairs={{0,24},{4,28},{8,16},{12,20},{16,8},{20,12},{24,0},{28,4},{1,25},{... | collective-permute-start | bytes 208904 | tf_op jit(solution)/shard_map/ppermute | solution.py:39
  18.0 0.7 collective-permute-start.2
  24.2 9.2 %copy-start.1 = (f32[264,128]{1,0:T(8,128)S(1)}, f32[264,128]{1,0:T(8,128)}, u32[]{:S(2)}) copy-start(f32[264,128]{1,0:T(8,128)} %get-tuple-element.30.refs_2_.refs_4_) | copy-start | bytes 405508
  24.3 6.3 %collective-permute-start.8 = (f32[136,128]{1,0:T(8,128)S(1)}, f32[136,128]{1,0:T(8,128)S(1)}, u32[]{:S(2)}, u32[]{:S(2)}) collective-permute-start(f32[136,128]{1,0:T(8,128)S(1)} %merge.2.refs_6_), channel_id=1, source_target_pairs={{0,24},{4,28},{8,16},{12,20},{16,8},{20,12},{24,0},{28,4},{1,25},{... | collective-permute-start | bytes 208904 | tf_op jit(solution)/shard_map/ppermute | solution.py:39
  28.1 5.2 %collective-permute-start.7 = (f32[136,128]{1,0:T(8,128)S(1)}, f32[136,128]{1,0:T(8,128)S(1)}, u32[]{:S(2)}, u32[]{:S(2)}) collective-permute-start(f32[136,128]{1,0:T(8,128)S(1)} %merge.2.refs_6_), channel_id=1, source_target_pairs={{0,16},{4,20},{8,24},{12,28},{16,0},{20,4},{24,8},{28,12},{1,17},{... | collective-permute-start | bytes 208904 | tf_op jit(solution)/shard_map/ppermute | solution.py:39
  28.1 5.2 %collective-permute-start.6 = (f32[136,128]{1,0:T(8,128)S(1)}, f32[136,128]{1,0:T(8,128)S(1)}, u32[]{:S(2)}, u32[]{:S(2)}) collective-permute-start(f32[136,128]{1,0:T(8,128)S(1)} %merge.2.refs_6_), channel_id=1, source_target_pairs={{0,8},{4,12},{8,0},{12,4},{16,24},{20,28},{24,16},{28,20},{1,9},{5... | collective-permute-start | bytes 208904 | tf_op jit(solution)/shard_map/ppermute | solution.py:39
  35.4 1.2 %collective-permute-start.9 = (f32[8,128]{1,0:T(8,128)S(1)}, f32[8,128]{1,0:T(8,128)S(1)}, u32[]{:S(2)}, u32[]{:S(2)}) collective-permute-start(f32[8,128]{1,0:T(8,128)S(1)} %get-tuple-element.41), channel_id=1, source_target_pairs={{0,4},{4,0},{8,12},{12,8},{16,20},{20,16},{24,28},{28,24},{1,5},{5... | collective-permute-start | bytes 12296 | tf_op jit(solution)/shard_map/ppermute | solution.py:39
  36.7 4.5 %collective-permute-start.12 = (f32[8,128]{1,0:T(8,128)S(1)}, f32[8,128]{1,0:T(8,128)S(1)}, u32[]{:S(2)}, u32[]{:S(2)}) collective-permute-start(f32[8,128]{1,0:T(8,128)S(1)} %add.18), channel_id=1, source_target_pairs={{0,3},{1,2},{2,1},{3,0},{4,7},{5,6},{6,5},{7,4},{8,11},{9,10},{10,... | collective-permute-start | bytes 12296 | tf_op jit(solution)/shard_map/ppermute | solution.py:39
  39.1 3.6 %collective-permute-start.11 = (f32[8,128]{1,0:T(8,128)S(1)}, f32[8,128]{1,0:T(8,128)S(1)}, u32[]{:S(2)}, u32[]{:S(2)}) collective-permute-start(f32[8,128]{1,0:T(8,128)S(1)} %add.18), channel_id=1, source_target_pairs={{0,2},{1,3},{2,0},{3,1},{4,6},{5,7},{6,4},{7,5},{8,10},{9,11},{10,... | collective-permute-start | bytes 12296 | tf_op jit(solution)/shard_map/ppermute | solution.py:39
  39.6 3.6 %collective-permute-start.10 = (f32[8,128]{1,0:T(8,128)S(1)}, f32[8,128]{1,0:T(8,128)S(1)}, u32[]{:S(2)}, u32[]{:S(2)}) collective-permute-start(f32[8,128]{1,0:T(8,128)S(1)} %add.18), channel_id=1, source_target_pairs={{0,1},{1,0},{2,3},{3,2},{4,5},{5,4},{6,7},{7,6},{8,9},{9,8},{10,11... | collective-permute-start | bytes 12296 | tf_op jit(solution)/shard_map/ppermute | solution.py:39
  43.2 5.4 %collective-permute-start.15 = (f32[8,128]{1,0:T(8,128)S(1)}, f32[8,128]{1,0:T(8,128)S(1)}, u32[]{:S(2)}, u32[]{:S(2)}) collective-permute-start(f32[8,128]{1,0:T(8,128)S(1)} %add_add_fusion.refs_6_), channel_id=1, source_target_pairs={{0,24},{4,28},{8,16},{12,20},{16,8},{20,12},{24,0},{28,4},{1,25},{... | collective-permute-start | bytes 12296 | tf_op jit(solution)/shard_map/ppermute | solution.py:39
  44.9 4.5 %collective-permute-start.14 = (f32[8,128]{1,0:T(8,128)S(1)}, f32[8,128]{1,0:T(8,128)S(1)}, u32[]{:S(2)}, u32[]{:S(2)}) collective-permute-start(f32[8,128]{1,0:T(8,128)S(1)} %add_add_fusion.refs_6_), channel_id=1, source_target_pairs={{0,16},{4,20},{8,24},{12,28},{16,0},{20,4},{24,8},{28,12},{1,17},{... | collective-permute-start | bytes 12296 | tf_op jit(solution)/shard_map/ppermute | solution.py:39
  45.3 4.1 %collective-permute-start.13 = (f32[8,128]{1,0:T(8,128)S(1)}, f32[8,128]{1,0:T(8,128)S(1)}, u32[]{:S(2)}, u32[]{:S(2)}) collective-permute-start(f32[8,128]{1,0:T(8,128)S(1)} %add_add_fusion.refs_6_), channel_id=1, source_target_pairs={{0,8},{4,12},{8,0},{12,4},{16,24},{20,28},{24,16},{28,20},{1,9},{5... | collective-permute-start | bytes 12296 | tf_op jit(solution)/shard_map/ppermute | solution.py:39
  50.7 12.7 %collective-permute-start.17 = (f32[520,128]{1,0:T(8,128)S(1)}, f32[520,128]{1,0:T(8,128)S(1)}, u32[]{:S(2)}, u32[]{:S(2)}) collective-permute-start(f32[520,128]{1,0:T(8,128)S(1)} %get-tuple-element.42.refs_2_.refs_0_), channel_id=1, source_target_pairs={{0,2},{2,0},{4,6},{6,4},{8,10},{10,8},{12,14},{14,12},{16,18},{18,... | collective-permute-start | bytes 798728 | tf_op jit(solution)/shard_map/ppermute | solution.py:39
  52.3 15.7 %collective-permute-start.18 = (f32[520,128]{1,0:T(8,128)S(1)}, f32[520,128]{1,0:T(8,128)S(1)}, u32[]{:S(2)}, u32[]{:S(2)}) collective-permute-start(f32[520,128]{1,0:T(8,128)S(1)} %get-tuple-element.43.refs_3_), channel_id=1, source_target_pairs={{0,6},{2,4},{4,2},{6,0},{8,14},{10,12},{12,10},{14,8},{16,22},{18,... | collective-permute-start | bytes 798728 | tf_op jit(solution)/shard_map/ppermute | solution.py:39
  52.3 15.7 %collective-permute-start.16 = (f32[520,128]{1,0:T(8,128)S(1)}, f32[520,128]{1,0:T(8,128)S(1)}, u32[]{:S(2)}, u32[]{:S(2)}) collective-permute-start(f32[520,128]{1,0:T(8,128)S(1)} %get-tuple-element.43.refs_3_), channel_id=1, source_target_pairs={{0,4},{2,6},{4,0},{6,2},{8,12},{10,14},{12,8},{14,10},{16,20},{18,... | collective-permute-start | bytes 798728 | tf_op jit(solution)/shard_map/ppermute | solution.py:39
  52.9 4.3 %collective-permute-start.19 = (f32[136,128]{1,0:T(8,128)S(1)}, f32[136,128]{1,0:T(8,128)S(1)}, u32[]{:S(2)}, u32[]{:S(2)}) collective-permute-start(f32[136,128]{1,0:T(8,128)S(1)} %get-tuple-element.47), channel_id=1, source_target_pairs={{0,8},{4,12},{8,0},{12,4},{16,24},{20,28},{24,16},{28,20},{1,9},{5... | collective-permute-start | bytes 208904 | tf_op jit(solution)/shard_map/ppermute | solution.py:39
  54.8 7.2 %collective-permute-start.20 = (f32[136,128]{1,0:T(8,128)S(1)}, f32[136,128]{1,0:T(8,128)S(1)}, u32[]{:S(2)}, u32[]{:S(2)}) collective-permute-start(f32[136,128]{1,0:T(8,128)S(1)} %get-tuple-element.48), channel_id=1, source_target_pairs={{0,16},{4,20},{8,24},{12,28},{16,0},{20,4},{24,8},{28,12},{1,17},{... | collective-permute-start | bytes 208904 | tf_op jit(solution)/shard_map/ppermute | solution.py:39
  57.2 6.2 %collective-permute-start.21 = (f32[136,128]{1,0:T(8,128)S(1)}, f32[136,128]{1,0:T(8,128)S(1)}, u32[]{:S(2)}, u32[]{:S(2)}) collective-permute-start(f32[136,128]{1,0:T(8,128)S(1)} %get-tuple-element.49), channel_id=1, source_target_pairs={{0,24},{4,28},{8,16},{12,20},{16,8},{20,12},{24,0},{28,4},{1,25},{... | collective-permute-start | bytes 208904 | tf_op jit(solution)/shard_map/ppermute | solution.py:39
  63.5 6.4 %collective-permute-start.24 = (f32[136,128]{1,0:T(8,128)S(1)}, f32[136,128]{1,0:T(8,128)S(1)}, u32[]{:S(2)}, u32[]{:S(2)}) collective-permute-start(f32[136,128]{1,0:T(8,128)S(1)} %merge.3.refs_6_), channel_id=1, source_target_pairs={{0,24},{4,28},{8,16},{12,20},{16,8},{20,12},{24,0},{28,4},{1,25},{... | collective-permute-start | bytes 208904 | tf_op jit(solution)/shard_map/ppermute | solution.py:39
  65.9 5.5 %collective-permute-start.23 = (f32[136,128]{1,0:T(8,128)S(1)}, f32[136,128]{1,0:T(8,128)S(1)}, u32[]{:S(2)}, u32[]{:S(2)}) collective-permute-start(f32[136,128]{1,0:T(8,128)S(1)} %merge.3.refs_6_), channel_id=1, source_target_pairs={{0,16},{4,20},{8,24},{12,28},{16,0},{20,4},{24,8},{28,12},{1,17},{... | collective-permute-start | bytes 208904 | tf_op jit(solution)/shard_map/ppermute | solution.py:39
  66.3 5.1 %collective-permute-start.22 = (f32[136,128]{1,0:T(8,128)S(1)}, f32[136,128]{1,0:T(8,128)S(1)}, u32[]{:S(2)}, u32[]{:S(2)}) collective-permute-start(f32[136,128]{1,0:T(8,128)S(1)} %merge.3.refs_6_), channel_id=1, source_target_pairs={{0,8},{4,12},{8,0},{12,4},{16,24},{20,28},{24,16},{28,20},{1,9},{5... | collective-permute-start | bytes 208904 | tf_op jit(solution)/shard_map/ppermute | solution.py:39
  73.5 16.0 %collective-permute-start.26 = (f32[520,128]{1,0:T(8,128)S(1)}, f32[520,128]{1,0:T(8,128)S(1)}, u32[]{:S(2)}, u32[]{:S(2)}) collective-permute-start(f32[520,128]{1,0:T(8,128)S(1)} %get-tuple-element.50.refs_4_), channel_id=1, source_target_pairs={{0,2},{2,0},{4,6},{6,4},{8,10},{10,8},{12,14},{14,12},{16,18},{18,... | collective-permute-start | bytes 798728 | tf_op jit(solution)/shard_map/ppermute | solution.py:39
  75.1 16.0 %collective-permute-start.27 = (f32[520,128]{1,0:T(8,128)S(1)}, f32[520,128]{1,0:T(8,128)S(1)}, u32[]{:S(2)}, u32[]{:S(2)}) collective-permute-start(f32[520,128]{1,0:T(8,128)S(1)} %get-tuple-element.51), channel_id=1, source_target_pairs={{0,6},{2,4},{4,2},{6,0},{8,14},{10,12},{12,10},{14,8},{16,22},{18,... | collective-permute-start | bytes 798728 | tf_op jit(solution)/shard_map/ppermute | solution.py:39
  75.1 16.0 %collective-permute-start.25 = (f32[520,128]{1,0:T(8,128)S(1)}, f32[520,128]{1,0:T(8,128)S(1)}, u32[]{:S(2)}, u32[]{:S(2)}) collective-permute-start(f32[520,128]{1,0:T(8,128)S(1)} %get-tuple-element.51), channel_id=1, source_target_pairs={{0,4},{2,6},{4,0},{6,2},{8,12},{10,14},{12,8},{14,10},{16,20},{18,... | collective-permute-start | bytes 798728 | tf_op jit(solution)/shard_map/ppermute | solution.py:39
  75.7 1.2 %collective-permute-start.28 = (f32[8,128]{1,0:T(8,128)S(1)}, f32[8,128]{1,0:T(8,128)S(1)}, u32[]{:S(2)}, u32[]{:S(2)}) collective-permute-start(f32[8,128]{1,0:T(8,128)S(1)} %get-tuple-element.52), channel_id=1, source_target_pairs={{0,4},{4,0},{8,12},{12,8},{16,20},{20,16},{24,28},{28,24},{1,5},{5... | collective-permute-start | bytes 12296 | tf_op jit(solution)/shard_map/ppermute | solution.py:39
  76.9 3.6 %collective-permute-start.29 = (f32[8,128]{1,0:T(8,128)S(1)}, f32[8,128]{1,0:T(8,128)S(1)}, u32[]{:S(2)}, u32[]{:S(2)}) collective-permute-start(f32[8,128]{1,0:T(8,128)S(1)} %add.22), channel_id=1, source_target_pairs={{0,1},{1,0},{2,3},{3,2},{4,5},{5,4},{6,7},{7,6},{8,9},{9,8},{10,11... | collective-permute-start | bytes 12296 | tf_op jit(solution)/shard_map/ppermute | solution.py:39
  80.5 5.4 %collective-permute-start.32 = (f32[8,128]{1,0:T(8,128)S(1)}, f32[8,128]{1,0:T(8,128)S(1)}, u32[]{:S(2)}, u32[]{:S(2)}) collective-permute-start(f32[8,128]{1,0:T(8,128)S(1)} %add.23.refs_0_), channel_id=1, source_target_pairs={{0,24},{4,28},{8,16},{12,20},{16,8},{20,12},{24,0},{28,4},{1,25},{... | collective-permute-start | bytes 12296 | tf_op jit(solution)/shard_map/ppermute | solution.py:39
  82.7 4.5 %collective-permute-start.31 = (f32[8,128]{1,0:T(8,128)S(1)}, f32[8,128]{1,0:T(8,128)S(1)}, u32[]{:S(2)}, u32[]{:S(2)}) collective-permute-start(f32[8,128]{1,0:T(8,128)S(1)} %add.23.refs_0_), channel_id=1, source_target_pairs={{0,16},{4,20},{8,24},{12,28},{16,0},{20,4},{24,8},{28,12},{1,17},{... | collective-permute-start | bytes 12296 | tf_op jit(solution)/shard_map/ppermute | solution.py:39
  85.9 3.6 %collective-permute-start.30 = (f32[8,128]{1,0:T(8,128)S(1)}, f32[8,128]{1,0:T(8,128)S(1)}, u32[]{:S(2)}, u32[]{:S(2)}) collective-permute-start(f32[8,128]{1,0:T(8,128)S(1)} %add.23.refs_0_), channel_id=1, source_target_pairs={{0,8},{4,12},{8,0},{12,4},{16,24},{20,28},{24,16},{28,20},{1,9},{5... | collective-permute-start | bytes 12296 | tf_op jit(solution)/shard_map/ppermute | solution.py:39
  89.5 3.7 %collective-permute-start.33 = (f32[8,128]{1,0:T(8,128)S(1)}, f32[8,128]{1,0:T(8,128)S(1)}, u32[]{:S(2)}, u32[]{:S(2)}) collective-permute-start(f32[8,128]{1,0:T(8,128)S(1)} %join.1.refs_8_), channel_id=1, source_target_pairs={{0,2},{2,0},{1,3},{3,1},{4,6},{6,4},{5,7},{7,5},{8,10},{10,8},{9,1... | collective-permute-start | bytes 12296 | tf_op jit(solution)/shard_map/ppermute | solution.py:39

commit v4 on v3

--- a/solution.py
+++ b/solution.py
@@ -130,6 +130,7 @@
     entry_total = slot_total * width
     score_scale = 1.0 / math.sqrt(width)
     slots = CORES * slot_rows
+    devices = ranks * CORES * query_devices * head_devices
     pos_rows = part_rows // width
     bias_rows = slot_rows // width
     packed_rows = 2 * slot_rows + TAIL
@@ -214,9 +215,7 @@
     )
 
     def step_sizes(tile_refs):
-        tile = tile_refs[0][...]
-        for ref in tile_refs[1:]:
-            tile = tile + ref[...]
+        tile = jnp.sum(tile_refs[0][...], axis=0)
         sums = jnp.sum(tile, axis=1, keepdims=True)
         return (
             RATE_KEYS / jnp.sqrt(sums[0:1] / entry_total + EPSILON),
@@ -344,33 +343,9 @@
             grad_outs[at][2 * slot_rows :, :] = grad_bias
             for which, grad in enumerate((grad_keys, grad_values, grad_bias)):
                 squares[which] = squares[which] + jnp.sum(grad * grad, axis=0, keepdims=True)
-        squares_out[...] = jnp.concatenate(
-            squares + [jnp.zeros((TAIL - 3, width), jnp.float32)], axis=0
-        )
-
-    def join_body(*refs):
-        total = refs[0][...]
-        for ref in refs[1:-1]:
-            total = total + ref[...]
-        refs[-1][...] = total
-
-    def group(**sizes):
-        masks = itertools.product(*(range(0, size, step) for size, step in sizes.values()))
-        return [dict(zip(sizes, mask)) for mask in masks if any(mask)]
-
-    core_round = group(page=(CORES, 1))
-    rank_round = group(page=(ranks * CORES, CORES))
-    first_rounds = [
-        core_round,
-        group(query=(query_devices, 1), head=(head_devices, 1)),
-        rank_round,
-    ]
-    last_rounds = [
-        core_round,
-        group(head=(head_devices, 1)),
-        rank_round,
-        group(query=(query_devices, 1)),
-    ]
+        tile = jnp.concatenate(squares + [jnp.zeros((TAIL - 3, width), jnp.float32)], axis=0)
+        for at in range(devices):
+            squares_out[at] = tile
 
     out_masks = list(itertools.product(range(query_devices), range(CORES)))
 
@@ -421,7 +396,7 @@
         ]
         own_grad, mate_grad, squares = call(
             backward_body,
-            packed_shapes + [(TAIL, width)],
+            packed_shapes + [(devices, TAIL, width)],
             "backward",
             3 * matmul_cost,
             [weights, maxima] + states + query_parts + all_merged,
@@ -431,18 +406,11 @@
         grads = [own_grad, mate_grad]
         if last:
             all_grads = [to_output(grads, mask) for mask in out_masks]
-        rounds = last_rounds if last else first_rounds
-        tiles = [squares]
-        for at, masks in enumerate(rounds):
-            joined = tiles[0]
-            if last and at == len(rounds) - 1:
-                (joined,) = call(
-                    join_body, [squares.shape], "join", 2**10, tiles, after=all_grads[2:3]
-                )
-            else:
-                for tile in tiles[1:]:
-                    joined = joined + tile
-            tiles = [joined] + [exchange(joined, **mask) for mask in masks]
+        tiles = [
+            lax.all_to_all(
+                squares, ("page", "query", "head"), split_axis=0, concat_axis=0, tiled=True
+            )
+        ]
 
     def last_body(*refs):
         state_refs, refs = refs[:local_heads], refs[local_heads:]

time: 94.5 us -> 87.1 us (0.922)
  blocking collectives: 0 us -> 23.3 us
  waiting for transfers between devices: 42 us -> 25.7 us
  starting transfers between devices: 39.4 us -> 24.8 us
    all_to_all x0 -> x2, blocking collectives: none -> 23.3 us  [direct_per_device(): lax.all_to_all(squares, ('page', 'query', 'head'), split_axis=0, concat_a...]
    ppermute x33 -> x20, waiting for transfers between devices: 42 us -> 25.7 us  [exchange(): return lax.ppermute(value, axes, pairs)]
    ppermute x33 -> x20, starting transfers between devices: 38.7 us -> 24.2 us  [exchange(): return lax.ppermute(value, axes, pairs)]
    pallas_call x9 -> x8, Pallas kernels: 10.3 us -> 10.4 us  [call(): pl.pallas_call(without_after, out_shape=[jax.ShapeDtypeStruct(shape, jnp....]
  transfers between devices with their start and end apart: 34 -> 21, of which waited for: 22 -> 10; matrix products, arithmetic and copies ran while one was open for 0% -> 0% of each run, Pallas kernels for 0% -> 0%
where the time goes in v4:
time: 87.1 us; the launch traced here: 86.9 us
  waiting for transfers between devices  25.7 us (30%)
  starting transfers between devices  24.8 us (28%)
  blocking collectives  23.3 us (27%)
  Pallas kernels  10.4 us (12%)
  local copies, waits for them, and re-layouts  1.87 us (2%)
    ppermute x20, waiting for transfers between devices, exchange(): return lax.ppermute(value, axes, pairs)  25.7 us
    ppermute x20, starting transfers between devices, exchange(): return lax.ppermute(value, axes, pairs)  24.2 us
    all_to_all x2, blocking collectives, direct_per_device(): lax.all_to_all(squares, ('page', 'query', 'head'), split_axis=0, concat_a...  23.3 us
    pallas_call x8, Pallas kernels, call(): pl.pallas_call(without_after, out_shape=[jax.ShapeDtypeStruct(shape, jnp....  10.4 us
    unnamed x10, local copies, waits for them, and re-layouts  1.87 us
  transfers between devices with their start and end apart: 21, of which 10 were waited for; matrix products, arithmetic and copies ran while one was open for 0% of the time, Pallas kernels for 0%

profile of v4, /device:TPU:0, one launch (start us, length us, event | category | flops | bytes accessed | tf_op | source)
XLA Modules:
  0.0 86.9 jit_solution(8532158211723207336)
XLA Ops:
  0.6 2.2 %pack.1 = (f32[520,128]{1,0:T(8,128)}, f32[520,128]{1,0:T(8,128)}, f32[264,128]{1,0:T(8,128)}, f32[264,128]{1,0:T(8,128)}, f32[128,128]{1,0:T(8,128)}) custom-call(f32[4,256,128]{2,1,0:T(8,128)} %refs_0_.1, f32[4,256,128]{2,1,0:T(8,128)} %refs_1_.1, f32[4,256,128]{2,1,0:T(8,128)} %refs_2_.1, f32[4,256]{1,0:T(4,128)} %refs_3_.1, f32[4,256,128]{2,1,0:T(8,128)} %refs_4_.1, ...), custom_call_target="tpu_custom_call" | custom-call | flops 1048576 | bytes 1048576 | tf_op jit(solution)/shard_map/pack/pallas_call | solution.py:67
  2.9 0.5 collective-permute-start
  3.4 2.6 %collective-permute-start.1 = (f32[264,128]{1,0:T(8,128)}, f32[264,128]{1,0:T(8,128)S(1)}, u32[]{:S(2)}, u32[]{:S(2)}) collective-permute-start(f32[264,128]{1,0:T(8,128)} %get-tuple-element.31), channel_id=1, source_target_pairs={{0,2},{2,0},{1,3},{3,1},{4,6},{6,4},{5,7},{7,5},{8,10},{10,8},{9,1... | collective-permute-start | bytes 405512 | tf_op jit(solution)/shard_map/ppermute | solution.py:39
  6.0 4.4 %collective-permute-done.1.refs_3_.refs_5_ = f32[264,128]{1,0:T(8,128)S(1)} collective-permute-done((f32[264,128]{1,0:T(8,128)}, f32[264,128]{1,0:T(8,128)S(1)}, u32[]{:S(2)}, u32[]{:S(2)}) %collective-permute-start.1) | collective-permute-done | bytes 135200 | tf_op jit(solution)/shard_map/ppermute | solution.py:39
  10.4 0.0 collective-permute-done.refs_1_.refs_3_
  10.4 0.9 %copy-done = f32[264,128]{1,0:T(8,128)S(1)} copy-done((f32[264,128]{1,0:T(8,128)S(1)}, f32[264,128]{1,0:T(8,128)}, u32[]{:S(2)}) %copy-start) | copy-done | bytes 135192
  11.3 0.9 %copy-done.2 = f32[520,128]{1,0:T(8,128)S(1)} copy-done((f32[520,128]{1,0:T(8,128)S(1)}, f32[520,128]{1,0:T(8,128)}, u32[]{:S(2)}) %copy-start.2) | copy-done | bytes 266264
  12.2 1.2 %forward.1 = (f32[136,128]{1,0:T(8,128)S(1)}, f32[136,128]{1,0:T(8,128)S(1)}, f32[136,128]{1,0:T(8,128)S(1)}, f32[136,128]{1,0:T(8,128)S(1)}, f32[512,512]{1,0:T(8,128)S(1)}, /*index=5*/f32[8,512]{1,0:T(8,128)S(1)}) custom-call(f32[520,128]{1,0:T(8,128)S(1)} %copy-done.2, f32[520,128]{1,0:T(8,128)S(1)} %collective-permute-done.refs_1_.refs_3_, ...), custom_call_target="tpu_custom_call" | custom-call | flops 402653184 | bytes 1048576 | tf_op jit(solution)/shard_map/forward/pallas_call | solution.py:67
  13.5 0.0 copy-start.3
  13.5 1.9 %collective-permute-start.3 = (f32[136,128]{1,0:T(8,128)S(1)}, f32[136,128]{1,0:T(8,128)S(1)}, u32[]{:S(2)}, u32[]{:S(2)}) collective-permute-start(f32[136,128]{1,0:T(8,128)S(1)} %get-tuple-element.36), channel_id=1, source_target_pairs={{0,8},{4,12},{8,0},{12,4},{16,24},{20,28},{24,16},{28,20},{1,9},{5... | collective-permute-start | bytes 208904 | tf_op jit(solution)/shard_map/ppermute | solution.py:39
  15.4 2.6 %collective-permute-start.4 = (f32[136,128]{1,0:T(8,128)S(1)}, f32[136,128]{1,0:T(8,128)S(1)}, u32[]{:S(2)}, u32[]{:S(2)}) collective-permute-start(f32[136,128]{1,0:T(8,128)S(1)} %get-tuple-element.37), channel_id=1, source_target_pairs={{0,16},{4,20},{8,24},{12,28},{16,0},{20,4},{24,8},{28,12},{1,17},{... | collective-permute-start | bytes 208904 | tf_op jit(solution)/shard_map/ppermute | solution.py:39
  18.0 0.7 collective-permute-start.2
  18.6 0.0 collective-permute-done.2.refs_0_
  18.6 0.0 collective-permute-done.3.refs_2_
  18.6 4.1 %collective-permute-done.4.refs_3_ = f32[136,128]{1,0:T(8,128)S(1)} collective-permute-done((f32[136,128]{1,0:T(8,128)S(1)}, f32[136,128]{1,0:T(8,128)S(1)}, u32[]{:S(2)}, u32[]{:S(2)}) %collective-permute-start.4) | collective-permute-done | bytes 69664 | tf_op jit(solution)/shard_map/ppermute | solution.py:39
  22.7 1.5 %collective-permute-done.5.refs_4_ = f32[136,128]{1,0:T(8,128)S(1)} collective-permute-done((f32[136,128]{1,0:T(8,128)S(1)}, f32[136,128]{1,0:T(8,128)S(1)}, u32[]{:S(2)}, u32[]{:S(2)}) %collective-permute-start.5) | collective-permute-done | bytes 69664 | tf_op jit(solution)/shard_map/ppermute | solution.py:39
  24.2 0.1 merge.2.refs_6_
  24.3 3.8 %collective-permute-start.8 = (f32[136,128]{1,0:T(8,128)S(1)}, f32[136,128]{1,0:T(8,128)S(1)}, u32[]{:S(2)}, u32[]{:S(2)}) collective-permute-start(f32[136,128]{1,0:T(8,128)S(1)} %merge.2.refs_6_), channel_id=1, source_target_pairs={{0,24},{4,28},{8,16},{12,20},{16,8},{20,12},{24,0},{28,4},{1,25},{... | collective-permute-start | bytes 208904 | tf_op jit(solution)/shard_map/ppermute | solution.py:39
  28.1 0.0 collective-permute-start.7
  28.1 0.6 collective-permute-start.6
  28.8 1.8 %collective-permute-done.8.refs_9_ = f32[136,128]{1,0:T(8,128)S(1)} collective-permute-done((f32[136,128]{1,0:T(8,128)S(1)}, f32[136,128]{1,0:T(8,128)S(1)}, u32[]{:S(2)}, u32[]{:S(2)}) %collective-permute-start.8) | collective-permute-done | bytes 69664 | tf_op jit(solution)/shard_map/ppermute | solution.py:39
  30.6 2.8 %collective-permute-done.7.refs_8_ = f32[136,128]{1,0:T(8,128)S(1)} collective-permute-done((f32[136,128]{1,0:T(8,128)S(1)}, f32[136,128]{1,0:T(8,128)S(1)}, u32[]{:S(2)}, u32[]{:S(2)}) %collective-permute-start.7) | collective-permute-done | bytes 69664 | tf_op jit(solution)/shard_map/ppermute | solution.py:39
  33.4 2.1 %backward.2 = (f32[520,128]{1,0:T(8,128)S(1)}, f32[520,128]{1,0:T(8,128)S(1)}, f32[32,8,128]{2,1,0:T(8,128)S(1)}) custom-call(f32[512,512]{1,0:T(8,128)S(1)} %get-tuple-element.32.refs_0_, f32[8,512]{1,0:T(8,128)S(1)} %get-tuple-element.33.refs_1_, f32[520,128]{1,0:T(8,128)S(1)} %copy-done.3, f32[520,128]{1,0:T(8,128)S(1)} %collective-permute-done.refs_1_.refs_3_, ...), custom_call_target="tpu_custom_call" | custom-call | flops 603979776 | bytes 1048576 | tf_op jit(solution)/shard_map/backward/pallas_call | solution.py:67
  35.5 12.5 %all_to_all.10.refs_6_ = f32[32,8,128]{2,1,0:T(8,128)S(1)} all-to-all(f32[32,8,128]{2,1,0:T(8,128)S(1)} %get-tuple-element.41), channel_id=1, replica_groups=mesh['page'=8,'query'=2,'head'=2] {'page','query','head'}, dimensions={0} | all-to-all | bytes 262144 | tf_op jit(solution)/shard_map/all_to_all | solution.py:410
  48.0 1.3 %update_forward.1 = (f32[520,128]{1,0:T(8,128)S(1)}, f32[520,128]{1,0:T(8,128)S(1)}, f32[136,128]{1,0:T(8,128)S(1)}, f32[136,128]{1,0:T(8,128)S(1)}, f32[136,128...) custom-call(f32[520,128]{1,0:T(8,128)S(1)} %copy-done.3, ...), custom_call_target="tpu_custom_call" | custom-call | flops 402653184 | bytes 1048576 | tf_op jit(solution)/shard_map/update_forward/pallas_call | solution.py:67
  49.3 0.3 collective-permute-start.10
  49.6 0.2 collective-permute-start.11
  49.9 1.6 %collective-permute-start.9 = (f32[520,128]{1,0:T(8,128)S(1)}, f32[520,128]{1,0:T(8,128)S(1)}, u32[]{:S(2)}, u32[]{:S(2)}) collective-permute-start(f32[520,128]{1,0:T(8,128)S(1)} %get-tuple-element.43.refs_3_), channel_id=1, source_target_pairs={{0,4},{2,6},{4,0},{6,2},{8,12},{10,14},{12,8},{14,10},{16,20},{18,... | collective-permute-start | bytes 798728 | tf_op jit(solution)/shard_map/ppermute | solution.py:39
  51.5 0.7 collective-permute-start.12
  52.2 1.3 %collective-permute-start.13 = (f32[136,128]{1,0:T(8,128)S(1)}, f32[136,128]{1,0:T(8,128)S(1)}, u32[]{:S(2)}, u32[]{:S(2)}) collective-permute-start(f32[136,128]{1,0:T(8,128)S(1)} %get-tuple-element.48), channel_id=1, source_target_pairs={{0,16},{4,20},{8,24},{12,28},{16,0},{20,4},{24,8},{28,12},{1,17},{... | collective-permute-start | bytes 208904 | tf_op jit(solution)/shard_map/ppermute | solution.py:39
  53.4 3.1 %collective-permute-done.12.refs_2_ = f32[136,128]{1,0:T(8,128)S(1)} collective-permute-done((f32[136,128]{1,0:T(8,128)S(1)}, f32[136,128]{1,0:T(8,128)S(1)}, u32[]{:S(2)}, u32[]{:S(2)}) %collective-permute-start.12) | collective-permute-done | bytes 69664 | tf_op jit(solution)/shard_map/ppermute | solution.py:39
  56.6 1.3 %collective-permute-start.14 = (f32[136,128]{1,0:T(8,128)S(1)}, f32[136,128]{1,0:T(8,128)S(1)}, u32[]{:S(2)}, u32[]{:S(2)}) collective-permute-start(f32[136,128]{1,0:T(8,128)S(1)} %get-tuple-element.49), channel_id=1, source_target_pairs={{0,24},{4,28},{8,16},{12,20},{16,8},{20,12},{24,0},{28,4},{1,25},{... | collective-permute-start | bytes 208904 | tf_op jit(solution)/shard_map/ppermute | solution.py:39
  57.9 0.7 collective-permute-done.13.refs_3_
  58.6 4.2 %collective-permute-done.14.refs_4_ = f32[136,128]{1,0:T(8,128)S(1)} collective-permute-done((f32[136,128]{1,0:T(8,128)S(1)}, f32[136,128]{1,0:T(8,128)S(1)}, u32[]{:S(2)}, u32[]{:S(2)}) %collective-permute-start.14) | collective-permute-done | bytes 69664 | tf_op jit(solution)/shard_map/ppermute | solution.py:39
  62.8 0.1 merge.3.refs_6_
  62.9 1.3 %collective-permute-start.17 = (f32[136,128]{1,0:T(8,128)S(1)}, f32[136,128]{1,0:T(8,128)S(1)}, u32[]{:S(2)}, u32[]{:S(2)}) collective-permute-start(f32[136,128]{1,0:T(8,128)S(1)} %merge.3.refs_6_), channel_id=1, source_target_pairs={{0,24},{4,28},{8,16},{12,20},{16,8},{20,12},{24,0},{28,4},{1,25},{... | collective-permute-start | bytes 208904 | tf_op jit(solution)/shard_map/ppermute | solution.py:39
  64.2 3.1 %collective-permute-start.15 = (f32[136,128]{1,0:T(8,128)S(1)}, f32[136,128]{1,0:T(8,128)S(1)}, u32[]{:S(2)}, u32[]{:S(2)}) collective-permute-start(f32[136,128]{1,0:T(8,128)S(1)} %merge.3.refs_6_), channel_id=1, source_target_pairs={{0,8},{4,12},{8,0},{12,4},{16,24},{20,28},{24,16},{28,20},{1,9},{5... | collective-permute-start | bytes 208904 | tf_op jit(solution)/shard_map/ppermute | solution.py:39
  67.3 0.0 collective-permute-done.11.refs_11_.refs_3_
  67.3 0.0 collective-permute-done.9.refs_10_.refs_1_
  67.3 1.8 %collective-permute-done.17.refs_9_ = f32[136,128]{1,0:T(8,128)S(1)} collective-permute-done((f32[136,128]{1,0:T(8,128)S(1)}, f32[136,128]{1,0:T(8,128)S(1)}, u32[]{:S(2)}, u32[]{:S(2)}) %collective-permute-start.17) | collective-permute-done | bytes 69664 | tf_op jit(solution)/shard_map/ppermute | solution.py:39
  69.1 1.4 %collective-permute-done.16.refs_8_ = f32[136,128]{1,0:T(8,128)S(1)} collective-permute-done((f32[136,128]{1,0:T(8,128)S(1)}, f32[136,128]{1,0:T(8,128)S(1)}, u32[]{:S(2)}, u32[]{:S(2)}) %collective-permute-start.16) | collective-permute-done | bytes 69664 | tf_op jit(solution)/shard_map/ppermute | solution.py:39
  70.5 2.1 %backward.3 = (f32[520,128]{1,0:T(8,128)S(1)}, f32[520,128]{1,0:T(8,128)S(1)}, f32[32,8,128]{2,1,0:T(8,128)S(1)}) custom-call(f32[512,512]{1,0:T(8,128)S(1)} %get-tuple-element.44.refs_0_, f32[8,512]{1,0:T(8,128)S(1)} %get-tuple-element.45.refs_1_, f32[520,128]{1,0:T(8,128)S(1)} %get-tuple-element.42.refs_2_.refs_0_, ...), custom_call_target="tpu_custom_call" | custom-call | flops 603979776 | bytes 1048576 | tf_op jit(solution)/shard_map/backward/pallas_call | solution.py:67
  72.7 0.1 collective-permute-start.19
  72.8 0.1 collective-permute-start.20
  72.8 2.0 %collective-permute-start.18 = (f32[520,128]{1,0:T(8,128)S(1)}, f32[520,128]{1,0:T(8,128)S(1)}, u32[]{:S(2)}, u32[]{:S(2)}) collective-permute-start(f32[520,128]{1,0:T(8,128)S(1)} %get-tuple-element.51), channel_id=1, source_target_pairs={{0,4},{2,6},{4,0},{6,2},{8,12},{10,14},{12,8},{14,10},{16,20},{18,... | collective-permute-start | bytes 798728 | tf_op jit(solution)/shard_map/ppermute | solution.py:39
  74.9 10.8 %all_to_all.11.refs_8_ = f32[32,8,128]{2,1,0:T(8,128)S(1)} all-to-all(f32[32,8,128]{2,1,0:T(8,128)S(1)} %get-tuple-element.52), channel_id=1, replica_groups=mesh['page'=8,'query'=2,'head'=2] {'page','query','head'}, dimensions={0} | all-to-all | bytes 262144 | tf_op jit(solution)/shard_map/all_to_all | solution.py:410
  85.7 0.0 collective-permute-done.19.refs_6_
  85.7 1.1 %last_update.1 = (f32[4,256,128]{2,1,0:T(8,128)}, f32[4,256,128]{2,1,0:T(8,128)}, f32[4,256]{1,0:T(4,128)}) custom-call(f32[520,128]{1,0:T(8,128)S(1)} %get-tuple-element.42.refs_2_.refs_0_, f32[520,128]{1,0:T(8,128)S(1)} %collective-permute-done.9.refs_10_.refs_1_, f32[520,128]{1,0:T(8,128)S(1)} %collective-permute-done.10.refs_5_.refs_2_, ...), custom_call_target="tpu_custom_call" | custom-call | flops 1048576 | bytes 1048576 | tf_op jit(solution)/shard_map/last_update/pallas_call | solution.py:67
  (14 shorter events, 0.0 us)
Async XLA Ops:
  2.9 7.5 %collective-permute-start = (f32[520,128]{1,0:T(8,128)}, f32[520,128]{1,0:T(8,128)S(1)}, u32[]{:S(2)}, u32[]{:S(2)}) collective-permute-start(f32[520,128]{1,0:T(8,128)} %get-tuple-element.29), channel_id=1, source_target_pairs={{0,4},{4,0},{8,12},{12,8},{16,20},{20,16},{24,28},{28,24},{1,5},{5... | collective-permute-start | bytes 798728 | tf_op jit(solution)/shard_map/ppermute | solution.py:39
  3.4 7.0 %collective-permute-start.1 = (f32[264,128]{1,0:T(8,128)}, f32[264,128]{1,0:T(8,128)S(1)}, u32[]{:S(2)}, u32[]{:S(2)}) collective-permute-start(f32[264,128]{1,0:T(8,128)} %get-tuple-element.31), channel_id=1, source_target_pairs={{0,2},{2,0},{1,3},{3,1},{4,6},{6,4},{5,7},{7,5},{8,10},{10,8},{9,1... | collective-permute-start | bytes 405512 | tf_op jit(solution)/shard_map/ppermute | solution.py:39
  10.4 0.9 %copy-start = (f32[264,128]{1,0:T(8,128)S(1)}, f32[264,128]{1,0:T(8,128)}, u32[]{:S(2)}) copy-start(f32[264,128]{1,0:T(8,128)} %get-tuple-element.30.refs_2_.refs_4_) | copy-start | bytes 405508
  11.3 1.0 %copy-start.2 = (f32[520,128]{1,0:T(8,128)S(1)}, f32[520,128]{1,0:T(8,128)}, u32[]{:S(2)}) copy-start(f32[520,128]{1,0:T(8,128)} %get-tuple-element.28.refs_0_.refs_2_) | copy-start | bytes 798724
  12.2 5.7 %copy-start.4 = (f32[128,128]{1,0:T(8,128)S(1)}, f32[128,128]{1,0:T(8,128)}, u32[]{:S(2)}) copy-start(f32[128,128]{1,0:T(8,128)} %get-tuple-element.34) | copy-start | bytes 196612
  13.5 19.9 %copy-start.3 = (f32[520,128]{1,0:T(8,128)S(1)}, f32[520,128]{1,0:T(8,128)}, u32[]{:S(2)}) copy-start(f32[520,128]{1,0:T(8,128)} %get-tuple-element.28.refs_0_.refs_2_) | copy-start | bytes 798724
  13.5 5.2 %collective-permute-start.3 = (f32[136,128]{1,0:T(8,128)S(1)}, f32[136,128]{1,0:T(8,128)S(1)}, u32[]{:S(2)}, u32[]{:S(2)}) collective-permute-start(f32[136,128]{1,0:T(8,128)S(1)} %get-tuple-element.36), channel_id=1, source_target_pairs={{0,8},{4,12},{8,0},{12,4},{16,24},{20,28},{24,16},{28,20},{1,9},{5... | collective-permute-start | bytes 208904 | tf_op jit(solution)/shard_map/ppermute | solution.py:39
  15.4 7.3 %collective-permute-start.4 = (f32[136,128]{1,0:T(8,128)S(1)}, f32[136,128]{1,0:T(8,128)S(1)}, u32[]{:S(2)}, u32[]{:S(2)}) collective-permute-start(f32[136,128]{1,0:T(8,128)S(1)} %get-tuple-element.37), channel_id=1, source_target_pairs={{0,16},{4,20},{8,24},{12,28},{16,0},{20,4},{24,8},{28,12},{1,17},{... | collective-permute-start | bytes 208904 | tf_op jit(solution)/shard_map/ppermute | solution.py:39
  18.0 6.2 %collective-permute-start.5 = (f32[136,128]{1,0:T(8,128)S(1)}, f32[136,128]{1,0:T(8,128)S(1)}, u32[]{:S(2)}, u32[]{:S(2)}) collective-permute-start(f32[136,128]{1,0:T(8,128)S(1)} %get-tuple-element.38), channel_id=1, source_target_pairs={{0,24},{4,28},{8,16},{12,20},{16,8},{20,12},{24,0},{28,4},{1,25},{... | collective-permute-start | bytes 208904 | tf_op jit(solution)/shard_map/ppermute | solution.py:39
  18.0 0.7 collective-permute-start.2
  24.2 9.2 %copy-start.1 = (f32[264,128]{1,0:T(8,128)S(1)}, f32[264,128]{1,0:T(8,128)}, u32[]{:S(2)}) copy-start(f32[264,128]{1,0:T(8,128)} %get-tuple-element.30.refs_2_.refs_4_) | copy-start | bytes 405508
  24.3 6.3 %collective-permute-start.8 = (f32[136,128]{1,0:T(8,128)S(1)}, f32[136,128]{1,0:T(8,128)S(1)}, u32[]{:S(2)}, u32[]{:S(2)}) collective-permute-start(f32[136,128]{1,0:T(8,128)S(1)} %merge.2.refs_6_), channel_id=1, source_target_pairs={{0,24},{4,28},{8,16},{12,20},{16,8},{20,12},{24,0},{28,4},{1,25},{... | collective-permute-start | bytes 208904 | tf_op jit(solution)/shard_map/ppermute | solution.py:39
  28.1 5.2 %collective-permute-start.7 = (f32[136,128]{1,0:T(8,128)S(1)}, f32[136,128]{1,0:T(8,128)S(1)}, u32[]{:S(2)}, u32[]{:S(2)}) collective-permute-start(f32[136,128]{1,0:T(8,128)S(1)} %merge.2.refs_6_), channel_id=1, source_target_pairs={{0,16},{4,20},{8,24},{12,28},{16,0},{20,4},{24,8},{28,12},{1,17},{... | collective-permute-start | bytes 208904 | tf_op jit(solution)/shard_map/ppermute | solution.py:39
  28.1 5.2 %collective-permute-start.6 = (f32[136,128]{1,0:T(8,128)S(1)}, f32[136,128]{1,0:T(8,128)S(1)}, u32[]{:S(2)}, u32[]{:S(2)}) collective-permute-start(f32[136,128]{1,0:T(8,128)S(1)} %merge.2.refs_6_), channel_id=1, source_target_pairs={{0,8},{4,12},{8,0},{12,4},{16,24},{20,28},{24,16},{28,20},{1,9},{5... | collective-permute-start | bytes 208904 | tf_op jit(solution)/shard_map/ppermute | solution.py:39
  49.3 13.4 %collective-permute-start.10 = (f32[520,128]{1,0:T(8,128)S(1)}, f32[520,128]{1,0:T(8,128)S(1)}, u32[]{:S(2)}, u32[]{:S(2)}) collective-permute-start(f32[520,128]{1,0:T(8,128)S(1)} %get-tuple-element.42.refs_2_.refs_0_), channel_id=1, source_target_pairs={{0,2},{2,0},{4,6},{6,4},{8,10},{10,8},{12,14},{14,12},{16,18},{18,... | collective-permute-start | bytes 798728 | tf_op jit(solution)/shard_map/ppermute | solution.py:39
  49.6 17.7 %collective-permute-start.11 = (f32[520,128]{1,0:T(8,128)S(1)}, f32[520,128]{1,0:T(8,128)S(1)}, u32[]{:S(2)}, u32[]{:S(2)}) collective-permute-start(f32[520,128]{1,0:T(8,128)S(1)} %get-tuple-element.43.refs_3_), channel_id=1, source_target_pairs={{0,6},{2,4},{4,2},{6,0},{8,14},{10,12},{12,10},{14,8},{16,22},{18,... | collective-permute-start | bytes 798728 | tf_op jit(solution)/shard_map/ppermute | solution.py:39
  49.9 17.4 %collective-permute-start.9 = (f32[520,128]{1,0:T(8,128)S(1)}, f32[520,128]{1,0:T(8,128)S(1)}, u32[]{:S(2)}, u32[]{:S(2)}) collective-permute-start(f32[520,128]{1,0:T(8,128)S(1)} %get-tuple-element.43.refs_3_), channel_id=1, source_target_pairs={{0,4},{2,6},{4,0},{6,2},{8,12},{10,14},{12,8},{14,10},{16,20},{18,... | collective-permute-start | bytes 798728 | tf_op jit(solution)/shard_map/ppermute | solution.py:39
  51.5 5.1 %collective-permute-start.12 = (f32[136,128]{1,0:T(8,128)S(1)}, f32[136,128]{1,0:T(8,128)S(1)}, u32[]{:S(2)}, u32[]{:S(2)}) collective-permute-start(f32[136,128]{1,0:T(8,128)S(1)} %get-tuple-element.47), channel_id=1, source_target_pairs={{0,8},{4,12},{8,0},{12,4},{16,24},{20,28},{24,16},{28,20},{1,9},{5... | collective-permute-start | bytes 208904 | tf_op jit(solution)/shard_map/ppermute | solution.py:39
  52.2 6.4 %collective-permute-start.13 = (f32[136,128]{1,0:T(8,128)S(1)}, f32[136,128]{1,0:T(8,128)S(1)}, u32[]{:S(2)}, u32[]{:S(2)}) collective-permute-start(f32[136,128]{1,0:T(8,128)S(1)} %get-tuple-element.48), channel_id=1, source_target_pairs={{0,16},{4,20},{8,24},{12,28},{16,0},{20,4},{24,8},{28,12},{1,17},{... | collective-permute-start | bytes 208904 | tf_op jit(solution)/shard_map/ppermute | solution.py:39
  56.6 6.2 %collective-permute-start.14 = (f32[136,128]{1,0:T(8,128)S(1)}, f32[136,128]{1,0:T(8,128)S(1)}, u32[]{:S(2)}, u32[]{:S(2)}) collective-permute-start(f32[136,128]{1,0:T(8,128)S(1)} %get-tuple-element.49), channel_id=1, source_target_pairs={{0,24},{4,28},{8,16},{12,20},{16,8},{20,12},{24,0},{28,4},{1,25},{... | collective-permute-start | bytes 208904 | tf_op jit(solution)/shard_map/ppermute | solution.py:39
  62.9 6.2 %collective-permute-start.17 = (f32[136,128]{1,0:T(8,128)S(1)}, f32[136,128]{1,0:T(8,128)S(1)}, u32[]{:S(2)}, u32[]{:S(2)}) collective-permute-start(f32[136,128]{1,0:T(8,128)S(1)} %merge.3.refs_6_), channel_id=1, source_target_pairs={{0,24},{4,28},{8,16},{12,20},{16,8},{20,12},{24,0},{28,4},{1,25},{... | collective-permute-start | bytes 208904 | tf_op jit(solution)/shard_map/ppermute | solution.py:39
  64.2 6.3 %collective-permute-start.16 = (f32[136,128]{1,0:T(8,128)S(1)}, f32[136,128]{1,0:T(8,128)S(1)}, u32[]{:S(2)}, u32[]{:S(2)}) collective-permute-start(f32[136,128]{1,0:T(8,128)S(1)} %merge.3.refs_6_), channel_id=1, source_target_pairs={{0,16},{4,20},{8,24},{12,28},{16,0},{20,4},{24,8},{28,12},{1,17},{... | collective-permute-start | bytes 208904 | tf_op jit(solution)/shard_map/ppermute | solution.py:39
  64.2 6.3 %collective-permute-start.15 = (f32[136,128]{1,0:T(8,128)S(1)}, f32[136,128]{1,0:T(8,128)S(1)}, u32[]{:S(2)}, u32[]{:S(2)}) collective-permute-start(f32[136,128]{1,0:T(8,128)S(1)} %merge.3.refs_6_), channel_id=1, source_target_pairs={{0,8},{4,12},{8,0},{12,4},{16,24},{20,28},{24,16},{28,20},{1,9},{5... | collective-permute-start | bytes 208904 | tf_op jit(solution)/shard_map/ppermute | solution.py:39
  72.7 13.1 %collective-permute-start.19 = (f32[520,128]{1,0:T(8,128)S(1)}, f32[520,128]{1,0:T(8,128)S(1)}, u32[]{:S(2)}, u32[]{:S(2)}) collective-permute-start(f32[520,128]{1,0:T(8,128)S(1)} %get-tuple-element.50.refs_4_), channel_id=1, source_target_pairs={{0,2},{2,0},{4,6},{6,4},{8,10},{10,8},{12,14},{14,12},{16,18},{18,... | collective-permute-start | bytes 798728 | tf_op jit(solution)/shard_map/ppermute | solution.py:39
  72.8 13.0 %collective-permute-start.20 = (f32[520,128]{1,0:T(8,128)S(1)}, f32[520,128]{1,0:T(8,128)S(1)}, u32[]{:S(2)}, u32[]{:S(2)}) collective-permute-start(f32[520,128]{1,0:T(8,128)S(1)} %get-tuple-element.51), channel_id=1, source_target_pairs={{0,6},{2,4},{4,2},{6,0},{8,14},{10,12},{12,10},{14,8},{16,22},{18,... | collective-permute-start | bytes 798728 | tf_op jit(solution)/shard_map/ppermute | solution.py:39
  72.8 12.9 %collective-permute-start.18 = (f32[520,128]{1,0:T(8,128)S(1)}, f32[520,128]{1,0:T(8,128)S(1)}, u32[]{:S(2)}, u32[]{:S(2)}) collective-permute-start(f32[520,128]{1,0:T(8,128)S(1)} %get-tuple-element.51), channel_id=1, source_target_pairs={{0,4},{2,6},{4,0},{6,2},{8,12},{10,14},{12,8},{14,10},{16,20},{18,... | collective-permute-start | bytes 798728 | tf_op jit(solution)/shard_map/ppermute | solution.py:39

commit v5 on v4

--- a/solution.py
+++ b/solution.py
@@ -57,7 +57,8 @@
     return one_pass(left[0], right[0]) + cross
 
 
-def call(body, out_shapes, name, cost, operands, scratch=(), after=(), space=pltpu.VMEM, vmem=32):
+def call(body, out_shapes, name, cost, operands, scratch=(), after=(), space=pltpu.VMEM,
+         out_space=pltpu.VMEM, vmem=32):
     spaces = [space] * len(operands) + [pl.ANY] * len(after)
     count = len(operands)
 
@@ -68,7 +69,7 @@
         without_after,
         out_shape=[jax.ShapeDtypeStruct(shape, jnp.float32) for shape in out_shapes],
         in_specs=[pl.BlockSpec(memory_space=space) for space in spaces],
-        out_specs=[pl.BlockSpec(memory_space=pltpu.VMEM) for _ in out_shapes],
+        out_specs=[pl.BlockSpec(memory_space=out_space) for _ in out_shapes],
         scratch_shapes=scratch,
         compiler_params=pltpu.CompilerParams(vmem_limit_bytes=vmem * 2**20),
         cost_estimate=pl.CostEstimate(flops=cost, bytes_accessed=2**20, transcendentals=0),
@@ -109,7 +110,7 @@
     return (
         part_rows * query_devices % ranks == 0
         and chunk % 128 == 0
-        and part_rows % chunk == 0
+        and part_rows % (8 * ranks) == 0
         and slot_rows % width == 0
         and part_rows % width == 0
         and max(slot_rows, part_rows) < TAIL * width
@@ -125,7 +126,7 @@
     head_devices = lax.axis_size("head")
     ranks = lax.axis_size("page") // CORES
     query_rows = part_rows * query_devices
-    chunk = query_rows // ranks
+    chunk, piece = query_rows // ranks, part_rows // ranks
     slot_total = local_heads * head_devices * slot_rows * lax.axis_size("page")
     entry_total = slot_total * width
     score_scale = 1.0 / math.sqrt(width)
@@ -141,78 +142,142 @@
         page = lax.axis_index("page")
         return page // CORES, page % CORES, lax.axis_index("query")
 
-    def prep_body(
-        queries, keys, values, biases, targets, positions, assignment, *refs
-    ):
-        state_outs, refs = refs[:2], refs[2:]
-        query_outs, (targets_out, *refs) = refs[:query_devices], refs[query_devices:]
-        bias_ref, positions_ref, assignment_ref, sems = refs
-        rank, core, me = places()
+    def pack_queries(head, rank, queries, targets, out):
+        rows = pl.ds(pl.multiple_of(rank * piece, piece), piece)
+        return [
+            (queries.at[head], out.at[pl.ds(0, part_rows)]),
+            (targets.at[head, rows], out.at[pl.ds(part_rows, piece)]),
+        ]
+
+    def pack_state(head, keys, values, out):
+        return [
+            (keys.at[head], out.at[pl.ds(0, slot_rows)]),
+            (values.at[head], out.at[pl.ds(slot_rows, slot_rows)]),
+        ]
+
+    def start_all(copies, sems, first=0):
         copies = [
-            (assignment, assignment_ref),
-            (positions, positions_ref),
-            (biases, bias_ref),
-        ]
-        for turn in range(query_devices):
-            head = CORES * (me ^ turn) + core
-            copies.append((queries.at[head], query_outs[turn].at[pl.ds(0, part_rows)]))
-        for at in range(2):
-            head = CORES * me + (core ^ at)
-            copies.append((keys.at[head], state_outs[at].at[pl.ds(0, slot_rows)]))
-            copies.append((values.at[head], state_outs[at].at[pl.ds(slot_rows, slot_rows)]))
-        first = rank * chunk
-        head = CORES * (me ^ (first // part_rows)) + core
-        rows = pl.ds(pl.multiple_of(first % part_rows, chunk), chunk)
-        copies.append((targets.at[head, rows], targets_out))
-        copies = [
-            pltpu.make_async_copy(source, target, sems.at[at])
+            pltpu.make_async_copy(source, target, sems.at[first + at])
             for at, (source, target) in enumerate(copies)
         ]
         for copy in copies:
             copy.start()
-        for copy in copies[:3]:
+        return copies
+
+    def position_tail(head, positions_ref):
+        return row_as_tail(positions_ref[pl.ds(head, 1), :].astype(jnp.float32), width)
+
+    def state_tail(head, page, bias_ref, assignment_ref):
+        page_start = (assignment_ref[page] * PAGE_LEN).astype(jnp.float32)
+        tail = row_as_tail(bias_ref[pl.ds(head, 1), :], width)
+        return jnp.concatenate(
+            [tail[: TAIL - 1], jnp.full((1, width), page_start, jnp.float32)], axis=0
+        )
+
+    def send_body(
+        queries, keys, values, biases, targets, positions, assignment, state_out, *refs
+    ):
+        query_outs = refs[: query_devices - 1]
+        bias_ref, positions_ref, assignment_ref, tails, sems = refs[query_devices - 1 :]
+        rank, core, me = places()
+        heads = [CORES * (me ^ turn) + core for turn in range(1, query_devices)]
+        mate_head = CORES * me + (core ^ 1)
+        small = start_all(
+            [(assignment, assignment_ref), (positions, positions_ref), (biases, bias_ref)], sems
+        )
+        copies = pack_state(mate_head, keys, values, state_out)
+        for head, out in zip(heads, query_outs):
+            copies += pack_queries(head, rank, queries, targets, out)
+        copies = start_all(copies, sems, 3)
+        for copy in small:
             copy.wait()
-        for turn in range(query_devices):
-            row = positions_ref[pl.ds(CORES * (me ^ turn) + core, 1), :].astype(jnp.float32)
-            query_outs[turn][part_rows:, :] = row_as_tail(row, width)
-        page_start = assignment_ref[CORES * rank + core] * PAGE_LEN
-        for at in range(2):
-            row = bias_ref[pl.ds(CORES * me + (core ^ at), 1), :]
-            state_outs[at][2 * slot_rows :, :] = row_as_tail(row, width)
-            state_outs[at][packed_rows - 1 :, :] = jnp.full(
-                (1, width), page_start.astype(jnp.float32)
-            )
-        for copy in copies[3:]:
+        tails[0] = state_tail(mate_head, CORES * rank + core, bias_ref, assignment_ref)
+        for at, head in enumerate(heads):
+            tails[1 + at] = position_tail(head, positions_ref)
+        ends = [(tails.at[0], state_out.at[pl.ds(2 * slot_rows, TAIL)])]
+        for at, out in enumerate(query_outs):
+            ends.append((tails.at[1 + at], out.at[pl.ds(part_rows + piece, TAIL)]))
+        copies += start_all(ends, sems, 3 + len(copies))
+        for copy in copies:
             copy.wait()
 
-    own_state, mate_state, *packed_queries, packed_targets = call(
-        prep_body,
-        packed_shapes + [(part_rows + TAIL, width)] * query_devices + [(chunk, width)],
+    def own_body(
+        queries, keys, values, biases, targets, positions, assignment, state_out, query_out, *refs
+    ):
+        bias_ref, positions_ref, assignment_ref, sems = refs
+        rank, core, me = places()
+        head = CORES * me + core
+        small = start_all(
+            [(assignment, assignment_ref), (positions, positions_ref), (biases, bias_ref)], sems
+        )
+        copies = pack_state(head, keys, values, state_out)
+        copies += pack_queries(head, rank, queries, targets, query_out)
+        copies = start_all(copies, sems, 3)
+        for copy in small:
+            copy.wait()
+        state_out[2 * slot_rows :, :] = state_tail(
+            head, CORES * rank + core, bias_ref, assignment_ref
+        )
+        query_out[part_rows + piece :, :] = position_tail(head, positions_ref)
+        for copy in copies:
+            copy.wait()
+
+    state_shape, query_shape = (packed_rows, width), (part_rows + piece + TAIL, width)
+    small_scratch = [
+        pltpu.VMEM(slot_bias.shape, jnp.float32),
+        pltpu.VMEM(positions.shape, jnp.int32),
+        pltpu.SMEM(assignment.shape, jnp.int32),
+    ]
+    arguments = [
+        queries, compact_keys, compact_values, slot_bias, targets, positions, assignment
+    ]
+    mate_state, *sent_queries = call(
+        send_body,
+        [state_shape] + [query_shape] * (query_devices - 1),
         "pack",
         2**20,
-        [queries, compact_keys, compact_values, slot_bias, targets, positions, assignment],
-        [
-            pltpu.VMEM(slot_bias.shape, jnp.float32),
-            pltpu.VMEM(positions.shape, jnp.int32),
-            pltpu.SMEM(assignment.shape, jnp.int32),
-            pltpu.SemaphoreType.DMA((query_devices + 8,)),
+        arguments,
+        small_scratch
+        + [
+            pltpu.VMEM((query_devices, TAIL, width), jnp.float32),
+            pltpu.SemaphoreType.DMA((5 + 3 * query_devices,)),
         ],
         space=pl.ANY,
+        out_space=pl.ANY,
         vmem=60,
     )
-    query_parts = packed_queries[:1] + [
-        exchange(packed_queries[turn], query=turn) for turn in range(1, query_devices)
+    own_state, own_queries = call(
+        own_body,
+        [state_shape, query_shape],
+        "own",
+        2**24,
+        arguments,
+        small_scratch + [pltpu.SemaphoreType.DMA((7,))],
+        space=pl.ANY,
+    )
+    query_parts = [own_queries] + [
+        exchange(sent_queries[turn - 1], query=turn) for turn in range(1, query_devices)
     ]
     states = [own_state, exchange(mate_state, page=1)]
-    chunk_targets = lax.ppermute(
-        packed_targets,
-        ("page", "query"),
-        [
-            (p * query_devices + y, p * query_devices + (y ^ (p // CORES * chunk // part_rows)))
-            for p in range(ranks * CORES)
-            for y in range(query_devices)
-        ],
-    )
+
+    def in_columns(parts, axis):
+        return jnp.concatenate(
+            [
+                lax.slice_in_dim(part, at * piece, (at + 1) * piece, axis=axis)
+                for at in range(ranks)
+                for part in parts
+            ],
+            axis=axis,
+        )
+
+    def read_queries(query_refs):
+        return halves(in_columns([ref[:part_rows, :] for ref in query_refs], 0))
+
+    def part_of(ref, at):
+        return ref.at[pl.ds(at * packed_rows, packed_rows)]
+
+    def parts_of(refs):
+        return refs if len(refs) == CORES else [part_of(refs[0], at) for at in range(CORES)]
 
     def step_sizes(tile_refs):
         tile = jnp.sum(tile_refs[0][...], axis=0)
@@ -233,9 +298,9 @@
 
     def forward(state_refs, query_refs, chunk_outs, weights_out, max_out, chunks):
         rank, _, _ = places()
-        all_queries = halves(jnp.concatenate([ref[:part_rows, :] for ref in query_refs], axis=0))
-        position_row = jnp.concatenate(
-            [tail_as_row(ref, part_rows, pos_rows) for ref in query_refs], axis=1
+        all_queries = read_queries(query_refs)
+        position_row = in_columns(
+            [tail_as_row(ref, part_rows + piece, pos_rows) for ref in query_refs], 1
         )
         all_scores, all_visible = [], []
         for at, ref in enumerate(state_refs):
@@ -283,7 +348,7 @@
         query_refs, refs = refs[:query_devices], refs[query_devices:]
         grad_refs, refs = refs[:2], refs[2:]
         tile_refs, refs = refs[: len(tiles)], refs[len(tiles) :]
-        state_outs, refs = refs[:2], refs[2:]
+        state_outs, refs = parts_of(refs[:1]), refs[1:]
         chunk_outs, refs = refs[:ranks], refs[ranks:]
         sizes = step_sizes(tile_refs)
         for at in range(2):
@@ -293,8 +358,12 @@
             state_outs[at][2 * slot_rows :, :] = bias
         forward(state_outs, query_refs, chunk_outs, *refs)
 
-    def merge_body(targets_ref, *refs):
+    def merge_body(*refs):
+        query_refs, refs = refs[:query_devices], refs[query_devices:]
         chunk_refs, (merged_out,) = refs[:ranks], refs[ranks:]
+        targets = jnp.concatenate(
+            [ref[part_rows : part_rows + piece, :] for ref in query_refs], axis=0
+        )
         row_max = chunk_refs[0][width : width + 1, :]
         for ref in chunk_refs[1:]:
             row_max = jnp.maximum(row_max, ref[width : width + 1, :])
@@ -305,7 +374,7 @@
             row_total = row_total + ref[width + 1 : width + 2, :] * factor
             row_sum = row_sum + ref[:width, :] * factor
         output = row_sum / row_total
-        residual = output - targets_ref[...].T
+        residual = output - targets.T
         row_delta = jnp.sum(residual * output, axis=0, keepdims=True)
         merged_out[:width, :] = residual
         merged_out[width:, :] = jnp.concatenate(
@@ -313,7 +382,7 @@
         )
 
     def backward_body(weights_ref, max_ref, *refs):
-        state_refs, refs = refs[:2], refs[2:]
+        state_refs, refs = parts_of(refs[: len(states)]), refs[len(states) :]
         query_refs, refs = refs[:query_devices], refs[query_devices:]
         merged_refs, refs = refs[:ranks], refs[ranks:]
         grad_outs, (squares_out, chunks) = refs[:2], refs[2:]
@@ -325,7 +394,7 @@
         row_max, row_total, row_delta = (
             joined[width + at : width + at + 1, :] for at in range(3)
         )
-        all_queries = halves(jnp.concatenate([ref[:part_rows, :] for ref in query_refs], axis=0))
+        all_queries = read_queries(query_refs)
         residual = halves(residual)
         factor = jnp.exp(max_ref[0:1, :] - row_max) / row_total
         ones = jnp.ones((TAIL, query_rows), jnp.bfloat16)
@@ -347,6 +416,11 @@
         for at in range(devices):
             squares_out[at] = tile
 
+    def mate_body(*refs):
+        *state_refs, out_ref = refs
+        for at, ref in enumerate(state_refs):
+            out_ref[pl.ds(at * packed_rows, packed_rows), :] = part_of(ref, 1)[...]
+
     out_masks = list(itertools.product(range(query_devices), range(CORES)))
 
     def to_output(packs, mask):
@@ -356,7 +430,6 @@
 
     for repeat in range(STEPS):
         last = repeat == STEPS - 1
-        before_merge, before_backward = [], []
         if repeat == 0:
             *chunk_parts, weights, maxima = call(
                 first_body,
@@ -367,33 +440,43 @@
                 chunk_scratch,
             )
         else:
-            own_new, mate_new, *chunk_parts, weights, maxima = call(
+            new_state, *chunk_parts, weights, maxima = call(
                 next_body,
-                packed_shapes + forward_shapes,
+                [(CORES * packed_rows, width)] + forward_shapes,
                 "update_forward",
                 2 * matmul_cost,
                 states + query_parts + grads + tiles,
                 chunk_scratch,
             )
-            states = [own_new, mate_new]
-        if last:
-            all_states = [to_output(states, mask) for mask in out_masks]
-            if repeat:
-                before_merge, before_backward = all_states[2:3], all_states[1:2] + all_states[3:]
-        arrived = chunk_parts[:1] + [
-            exchange(chunk_parts[turn], page=CORES * turn) for turn in range(1, ranks)
-        ]
+            states = [new_state]
+        arrived = {
+            turn: exchange(chunk_parts[turn], page=CORES * turn)
+            for turn in reversed(range(1, ranks))
+        }
+        if repeat:
+            new_states = states + [
+                exchange(states[0], query=turn) for turn in range(1, query_devices)
+            ]
         (merged,) = call(
             merge_body,
             [chunk_shape],
             "merge",
             2**20,
-            [chunk_targets] + arrived,
-            after=before_merge,
+            query_parts + chunk_parts[:1] + list(arrived.values()),
         )
         all_merged = [merged] + [
             exchange(merged, page=CORES * turn) for turn in range(1, ranks)
         ]
+        if repeat:
+            (for_mate,) = call(
+                mate_body,
+                [(query_devices * packed_rows, width)],
+                "mate_parts",
+                2**20,
+                new_states,
+                after=all_merged[1:],
+            )
+            from_mate = exchange(for_mate, page=1)
         own_grad, mate_grad, squares = call(
             backward_body,
             packed_shapes + [(devices, TAIL, width)],
@@ -401,7 +484,6 @@
             3 * matmul_cost,
             [weights, maxima] + states + query_parts + all_merged,
             scratch=chunk_scratch,
-            after=before_backward,
         )
         grads = [own_grad, mate_grad]
         if last:
@@ -413,7 +495,11 @@
         ]
 
     def last_body(*refs):
-        state_refs, refs = refs[:local_heads], refs[local_heads:]
+        state_refs, (mate_ref, *refs) = refs[:query_devices], refs[query_devices:]
+        state_refs = [
+            part_of(mate_ref, turn) if flip else part_of(state_refs[turn], 0)
+            for turn, flip in out_masks
+        ]
         grad_refs, refs = refs[:local_heads], refs[local_heads:]
         tile_refs, (keys_out, values_out, bias_out) = refs[: len(tiles)], refs[len(tiles) :]
         _, core, me = places()
@@ -432,7 +518,7 @@
             [compact_keys.shape, compact_values.shape, slot_bias.shape],
             "last_update",
             2**20,
-            all_states + all_grads + tiles,
+            new_states + [from_mate] + all_grads + tiles,
         )
     )
 

time: 87.1 us -> 96.5 us (1.11)
  Pallas kernels: 10.4 us -> 23.1 us
  waiting for transfers between devices: 25.7 us -> 23.4 us
  blocking collectives: 23.3 us -> 25.5 us
  local copies, waits for them, and re-layouts: 1.87 us -> 0.03 us
  starting transfers between devices: 24.8 us -> 23.6 us
    pallas_call x8 -> x10, Pallas kernels: 10.4 us -> 23.1 us  [call(): pl.pallas_call(without_after, out_shape=[jax.ShapeDtypeStruct(shape, jnp....]
    ppermute x20 -> x19, waiting for transfers between devices: 25.7 us -> 23.4 us  [exchange(): return lax.ppermute(value, axes, pairs)]
    all_to_all x2, blocking collectives: 23.3 us -> 25.5 us  [direct_per_device(): lax.all_to_all(squares, ('page', 'query', 'head'), split_axis=0, concat_a...]
    unnamed x10 -> x14, local copies, waits for them, and re-layouts: 1.87 us -> 0.03 us
    ppermute x20 -> x19, starting transfers between devices: 24.2 us -> 23.6 us  [exchange(): return lax.ppermute(value, axes, pairs)]
  transfers between devices with their start and end apart: 21 -> 19, of which waited for: 10 -> 9; matrix products, arithmetic and copies ran while one was open for 0% -> 0% of each run, Pallas kernels for 0% -> 3%
where the time goes in v5:
time: 96.5 us; the launch traced here: 96.3 us
  blocking collectives  25.5 us (26%)
  starting transfers between devices  23.6 us (24%)
  waiting for transfers between devices  23.4 us (24%)
  Pallas kernels  23.1 us (24%)
    all_to_all x2, blocking collectives, direct_per_device(): lax.all_to_all(squares, ('page', 'query', 'head'), split_axis=0, concat_a...  25.5 us
    ppermute x19, starting transfers between devices, exchange(): return lax.ppermute(value, axes, pairs)  23.6 us
    ppermute x19, waiting for transfers between devices, exchange(): return lax.ppermute(value, axes, pairs)  23.4 us
    pallas_call x10, Pallas kernels, call(): pl.pallas_call(without_after, out_shape=[jax.ShapeDtypeStruct(shape, jnp....  23.1 us
  transfers between devices with their start and end apart: 19, of which 9 were waited for; matrix products, arithmetic and copies ran while one was open for 0% of the time, Pallas kernels for 3%

profile of v5, /device:TPU:0, one launch (start us, length us, event | category | flops | bytes accessed | tf_op | source)
XLA Modules:
  0.0 96.3 jit_solution(1902792931156059063)
XLA Ops:
  0.7 14.1 %pack.1 = (f32[520,128]{1,0:T(8,128)}, f32[328,128]{1,0:T(8,128)}) custom-call(f32[4,256,128]{2,1,0:T(8,128)} %refs_0_.3, f32[4,256,128]{2,1,0:T(8,128)} %refs_1_.3, f32[4,256,128]{2,1,0:T(8,128)} %refs_2_.3, f32[4,256]{1,0:T(4,128)} %refs_3_.3, f32[4,256,128]{2,1,0:T(8,128)} %refs_4_.3, s32[4,256]{1,0:T(4,128)} %refs_5_.3, s32[8]{0:T(128)} %refs_6_.3), custom_call_target="tpu_custom_call" | custom-call | flops 1048576 | bytes 1048576 | tf_op jit(solution)/shard_map/pack/pallas_call | solution.py:68
  14.8 0.0 copy-start.6
  14.8 0.5 collective-permute-start
  15.4 2.6 %collective-permute-start.1 = (f32[328,128]{1,0:T(8,128)}, f32[328,128]{1,0:T(8,128)S(1)}, u32[]{:S(2)}, u32[]{:S(2)}) collective-permute-start(f32[328,128]{1,0:T(8,128)} %get-tuple-element.29), channel_id=1, source_target_pairs={{0,2},{2,0},{1,3},{3,1},{4,6},{6,4},{5,7},{7,5},{8,10},{10,8},{9,1... | collective-permute-start | bytes 503816 | tf_op jit(solution)/shard_map/ppermute | solution.py:39
  18.0 0.7 own.1
  18.7 4.4 %collective-permute-done.1.refs_3_.refs_1_.refs_5_.refs_4_ = f32[328,128]{1,0:T(8,128)S(1)} collective-permute-done((f32[328,128]{1,0:T(8,128)}, f32[328,128]{1,0:T(8,128)S(1)}, u32[]{:S(2)}, u32[]{:S(2)}) %collective-permute-start.1) | collective-permute-done | bytes 167968 | tf_op jit(solution)/shard_map/ppermute | solution.py:39
  23.0 0.0 collective-permute-done.refs_1_.refs_3_
  23.0 1.2 %forward.1 = (f32[136,128]{1,0:T(8,128)S(1)}, f32[136,128]{1,0:T(8,128)S(1)}, f32[136,128]{1,0:T(8,128)S(1)}, f32[136,128]{1,0:T(8,128)S(1)}, f32[512,512]{1,0:T(8,128)S(1)}, /*index=5*/f32[8,512]{1,0:T(8,128)S(1)}) custom-call(f32[520,128]{1,0:T(8,128)S(1)} %get-tuple-element.26.refs_0_.refs_2_, f32[520,128]{1,0:T(8,128)S(1)} %collective-permute-done.refs_1_.refs_3_, ...), custom_call_target="tpu_custom_call" | custom-call | flops 402653184 | bytes 1048576 | tf_op jit(solution)/shard_map/forward/pallas_call | solution.py:68
  24.3 3.9 %collective-permute-start.2 = (f32[136,128]{1,0:T(8,128)S(1)}, f32[136,128]{1,0:T(8,128)S(1)}, u32[]{:S(2)}, u32[]{:S(2)}) collective-permute-start(f32[136,128]{1,0:T(8,128)S(1)} %get-tuple-element.33), channel_id=1, source_target_pairs={{0,24},{4,28},{8,16},{12,20},{16,8},{20,12},{24,0},{28,4},{1,25},{... | collective-permute-start | bytes 208904 | tf_op jit(solution)/shard_map/ppermute | solution.py:39
  28.2 0.0 collective-permute-start.3
  28.2 0.6 collective-permute-start.4
  28.8 2.1 %collective-permute-done.2.refs_3_ = f32[136,128]{1,0:T(8,128)S(1)} collective-permute-done((f32[136,128]{1,0:T(8,128)S(1)}, f32[136,128]{1,0:T(8,128)S(1)}, u32[]{:S(2)}, u32[]{:S(2)}) %collective-permute-start.2) | collective-permute-done | bytes 69664 | tf_op jit(solution)/shard_map/ppermute | solution.py:39
  31.0 3.0 %collective-permute-done.3.refs_4_ = f32[136,128]{1,0:T(8,128)S(1)} collective-permute-done((f32[136,128]{1,0:T(8,128)S(1)}, f32[136,128]{1,0:T(8,128)S(1)}, u32[]{:S(2)}, u32[]{:S(2)}) %collective-permute-start.3) | collective-permute-done | bytes 69664 | tf_op jit(solution)/shard_map/ppermute | solution.py:39
  33.9 0.0 collective-permute-done.4.refs_5_
  33.9 0.1 merge.2.refs_6_
  34.1 2.8 %collective-permute-start.7 = (f32[136,128]{1,0:T(8,128)S(1)}, f32[136,128]{1,0:T(8,128)S(1)}, u32[]{:S(2)}, u32[]{:S(2)}) collective-permute-start(f32[136,128]{1,0:T(8,128)S(1)} %merge.2.refs_6_), channel_id=1, source_target_pairs={{0,24},{4,28},{8,16},{12,20},{16,8},{20,12},{24,0},{28,4},{1,25},{... | collective-permute-start | bytes 208904 | tf_op jit(solution)/shard_map/ppermute | solution.py:39
  36.8 0.0 collective-permute-start.6
  36.9 1.7 %collective-permute-start.5 = (f32[136,128]{1,0:T(8,128)S(1)}, f32[136,128]{1,0:T(8,128)S(1)}, u32[]{:S(2)}, u32[]{:S(2)}) collective-permute-start(f32[136,128]{1,0:T(8,128)S(1)} %merge.2.refs_6_), channel_id=1, source_target_pairs={{0,8},{4,12},{8,0},{12,4},{16,24},{20,28},{24,16},{28,20},{1,9},{5... | collective-permute-start | bytes 208904 | tf_op jit(solution)/shard_map/ppermute | solution.py:39
  38.5 2.5 %collective-permute-done.7.refs_9_ = f32[136,128]{1,0:T(8,128)S(1)} collective-permute-done((f32[136,128]{1,0:T(8,128)S(1)}, f32[136,128]{1,0:T(8,128)S(1)}, u32[]{:S(2)}, u32[]{:S(2)}) %collective-permute-start.7) | collective-permute-done | bytes 69664 | tf_op jit(solution)/shard_map/ppermute | solution.py:39
  41.0 2.4 %collective-permute-done.6.refs_8_ = f32[136,128]{1,0:T(8,128)S(1)} collective-permute-done((f32[136,128]{1,0:T(8,128)S(1)}, f32[136,128]{1,0:T(8,128)S(1)}, u32[]{:S(2)}, u32[]{:S(2)}) %collective-permute-start.6) | collective-permute-done | bytes 69664 | tf_op jit(solution)/shard_map/ppermute | solution.py:39
  43.4 0.0 collective-permute-done.5.refs_7_
  43.4 2.1 %backward.2 = (f32[520,128]{1,0:T(8,128)S(1)}, f32[520,128]{1,0:T(8,128)S(1)}, f32[32,8,128]{2,1,0:T(8,128)S(1)}) custom-call(f32[512,512]{1,0:T(8,128)S(1)} %get-tuple-element.30.refs_0_, f32[8,512]{1,0:T(8,128)S(1)} %get-tuple-element.31.refs_1_, f32[520,128]{1,0:T(8,128)S(1)} %get-tuple-element.26.refs_0_.refs_2_, ...), custom_call_target="tpu_custom_call" | custom-call | flops 603979776 | bytes 1048576 | tf_op jit(solution)/shard_map/backward/pallas_call | solution.py:68
  45.5 11.8 %all_to_all.10.refs_6_ = f32[32,8,128]{2,1,0:T(8,128)S(1)} all-to-all(f32[32,8,128]{2,1,0:T(8,128)S(1)} %get-tuple-element.38), channel_id=1, replica_groups=mesh['page'=8,'query'=2,'head'=2] {'page','query','head'}, dimensions={0} | all-to-all | bytes 262144 | tf_op jit(solution)/shard_map/all_to_all | solution.py:492
  57.3 1.3 %update_forward.1 = (f32[1040,128]{1,0:T(8,128)S(1)}, f32[136,128]{1,0:T(8,128)S(1)}, f32[136,128]{1,0:T(8,128)S(1)}, f32[136,128]{1,0:T(8,128)S(1)}, f32[136,12...) custom-call(f32[520,128]{1,0:T(8,128)S(1)} %get-tuple-element.26.refs_0_.refs_2_, ...), custom_call_target="tpu_custom_call" | custom-call | flops 402653184 | bytes 1048576 | tf_op jit(solution)/shard_map/update_forward/pallas_call | solution.py:68
  58.6 0.3 collective-permute-start.8
  59.0 1.4 %collective-permute-start.9 = (f32[136,128]{1,0:T(8,128)S(1)}, f32[136,128]{1,0:T(8,128)S(1)}, u32[]{:S(2)}, u32[]{:S(2)}) collective-permute-start(f32[136,128]{1,0:T(8,128)S(1)} %get-tuple-element.41), channel_id=1, source_target_pairs={{0,24},{4,28},{8,16},{12,20},{16,8},{20,12},{24,0},{28,4},{1,25},{... | collective-permute-start | bytes 208904 | tf_op jit(solution)/shard_map/ppermute | solution.py:39
  60.3 0.8 collective-permute-start.10
  61.1 2.2 %collective-permute-start.11 = (f32[136,128]{1,0:T(8,128)S(1)}, f32[136,128]{1,0:T(8,128)S(1)}, u32[]{:S(2)}, u32[]{:S(2)}) collective-permute-start(f32[136,128]{1,0:T(8,128)S(1)} %get-tuple-element.43), channel_id=1, source_target_pairs={{0,8},{4,12},{8,0},{12,4},{16,24},{20,28},{24,16},{28,20},{1,9},{5... | collective-permute-start | bytes 208904 | tf_op jit(solution)/shard_map/ppermute | solution.py:39
  63.3 2.5 %collective-permute-done.9.refs_3_ = f32[136,128]{1,0:T(8,128)S(1)} collective-permute-done((f32[136,128]{1,0:T(8,128)S(1)}, f32[136,128]{1,0:T(8,128)S(1)}, u32[]{:S(2)}, u32[]{:S(2)}) %collective-permute-start.9) | collective-permute-done | bytes 69664 | tf_op jit(solution)/shard_map/ppermute | solution.py:39
  65.8 2.0 %collective-permute-done.10.refs_4_ = f32[136,128]{1,0:T(8,128)S(1)} collective-permute-done((f32[136,128]{1,0:T(8,128)S(1)}, f32[136,128]{1,0:T(8,128)S(1)}, u32[]{:S(2)}, u32[]{:S(2)}) %collective-permute-start.10) | collective-permute-done | bytes 69664 | tf_op jit(solution)/shard_map/ppermute | solution.py:39
  67.9 0.0 collective-permute-done.11.refs_5_
  67.9 0.1 merge.3.refs_5_
  68.0 1.7 %collective-permute-start.14 = (f32[136,128]{1,0:T(8,128)S(1)}, f32[136,128]{1,0:T(8,128)S(1)}, u32[]{:S(2)}, u32[]{:S(2)}) collective-permute-start(f32[136,128]{1,0:T(8,128)S(1)} %merge.3.refs_5_), channel_id=1, source_target_pairs={{0,24},{4,28},{8,16},{12,20},{16,8},{20,12},{24,0},{28,4},{1,25},{... | collective-permute-start | bytes 208904 | tf_op jit(solution)/shard_map/ppermute | solution.py:39
  69.7 0.0 collective-permute-start.13
  69.7 2.8 %collective-permute-start.12 = (f32[136,128]{1,0:T(8,128)S(1)}, f32[136,128]{1,0:T(8,128)S(1)}, u32[]{:S(2)}, u32[]{:S(2)}) collective-permute-start(f32[136,128]{1,0:T(8,128)S(1)} %merge.3.refs_5_), channel_id=1, source_target_pairs={{0,8},{4,12},{8,0},{12,4},{16,24},{20,28},{24,16},{28,20},{1,9},{5... | collective-permute-start | bytes 208904 | tf_op jit(solution)/shard_map/ppermute | solution.py:39
  72.4 2.5 %collective-permute-done.14.refs_4_.refs_8_ = f32[136,128]{1,0:T(8,128)S(1)} collective-permute-done((f32[136,128]{1,0:T(8,128)S(1)}, f32[136,128]{1,0:T(8,128)S(1)}, u32[]{:S(2)}, u32[]{:S(2)}) %collective-permute-start.14) | collective-permute-done | bytes 69664 | tf_op jit(solution)/shard_map/ppermute | solution.py:39
  75.0 2.0 %collective-permute-done.13.refs_3_.refs_7_ = f32[136,128]{1,0:T(8,128)S(1)} collective-permute-done((f32[136,128]{1,0:T(8,128)S(1)}, f32[136,128]{1,0:T(8,128)S(1)}, u32[]{:S(2)}, u32[]{:S(2)}) %collective-permute-start.13) | collective-permute-done | bytes 69664 | tf_op jit(solution)/shard_map/ppermute | solution.py:39
  76.9 0.0 collective-permute-done.12.refs_2_.refs_6_
  77.0 0.0 collective-permute-done.8.refs_1_
  77.0 0.1 collective-permute-start.15
  77.1 2.2 %backward.3 = (f32[520,128]{1,0:T(8,128)S(1)}, f32[520,128]{1,0:T(8,128)S(1)}, f32[32,8,128]{2,1,0:T(8,128)S(1)}) custom-call(f32[512,512]{1,0:T(8,128)S(1)} %get-tuple-element.44.refs_0_, f32[8,512]{1,0:T(8,128)S(1)} %get-tuple-element.45.refs_1_, f32[1040,128]{1,0:T(8,128)S(1)} %get-tuple-element.39.refs_0_.refs_2_, ...), custom_call_target="tpu_custom_call" | custom-call | flops 603979776 | bytes 1048576 | tf_op jit(solution)/shard_map/backward/pallas_call | solution.py:68
  79.2 0.9 collective-permute-start.17
  80.2 1.0 %collective-permute-start.18 = (f32[520,128]{1,0:T(8,128)S(1)}, f32[520,128]{1,0:T(8,128)S(1)}, u32[]{:S(2)}, u32[]{:S(2)}) collective-permute-start(f32[520,128]{1,0:T(8,128)S(1)} %get-tuple-element.47), channel_id=1, source_target_pairs={{0,6},{2,4},{4,2},{6,0},{8,14},{10,12},{12,10},{14,8},{16,22},{18,... | collective-permute-start | bytes 798728 | tf_op jit(solution)/shard_map/ppermute | solution.py:39
  81.2 0.3 collective-permute-start.16
  81.5 13.7 %all_to_all.11.refs_7_ = f32[32,8,128]{2,1,0:T(8,128)S(1)} all-to-all(f32[32,8,128]{2,1,0:T(8,128)S(1)} %get-tuple-element.48), channel_id=1, replica_groups=mesh['page'=8,'query'=2,'head'=2] {'page','query','head'}, dimensions={0} | all-to-all | bytes 262144 | tf_op jit(solution)/shard_map/all_to_all | solution.py:492
  95.2 0.0 collective-permute-done.17.refs_5_
  95.2 0.0 collective-permute-done.18.refs_6_
  95.2 1.1 %last_update.1 = (f32[4,256,128]{2,1,0:T(8,128)}, f32[4,256,128]{2,1,0:T(8,128)}, f32[4,256]{1,0:T(4,128)}) custom-call(f32[1040,128]{1,0:T(8,128)S(1)} %get-tuple-element.39.refs_0_.refs_2_, f32[1040,128]{1,0:T(8,128)S(1)} %collective-permute-done.8.refs_1_, f32[1040,128]{1,0:T(8,128)S(1)} %collective-permute-done.15.refs_2_, ...), custom_call_target="tpu_custom_call" | custom-call | flops 1048576 | bytes 1048576 | tf_op jit(solution)/shard_map/last_update/pallas_call | solution.py:68
  (16 shorter events, 0.1 us)
Async XLA Ops:
  0.6 17.3 %copy-start.3 = (f32[4,256,128]{2,1,0:T(8,128)S(1)}, f32[4,256,128]{2,1,0:T(8,128)}, u32[]{:S(2)}) copy-start(f32[4,256,128]{2,1,0:T(8,128)} %refs_4_.3) | copy-start | bytes 1572868
  0.6 17.3 %copy-start.2 = (f32[4,256,128]{2,1,0:T(8,128)S(1)}, f32[4,256,128]{2,1,0:T(8,128)}, u32[]{:S(2)}) copy-start(f32[4,256,128]{2,1,0:T(8,128)} %refs_2_.3) | copy-start | bytes 1572868
  0.7 17.3 %copy-start.1 = (f32[4,256,128]{2,1,0:T(8,128)S(1)}, f32[4,256,128]{2,1,0:T(8,128)}, u32[]{:S(2)}) copy-start(f32[4,256,128]{2,1,0:T(8,128)} %refs_1_.3) | copy-start | bytes 1572868
  0.7 17.3 %copy-start = (f32[4,256,128]{2,1,0:T(8,128)S(1)}, f32[4,256,128]{2,1,0:T(8,128)}, u32[]{:S(2)}) copy-start(f32[4,256,128]{2,1,0:T(8,128)} %refs_0_.3) | copy-start | bytes 1572868
  0.7 17.3 %copy-start.4 = (f32[4,256]{1,0:T(4,128)S(1)}, f32[4,256]{1,0:T(4,128)}, u32[]{:S(2)}) copy-start(f32[4,256]{1,0:T(4,128)} %refs_3_.3) | copy-start | bytes 12292
  0.7 17.3 %copy-start.5 = (s32[4,256]{1,0:T(4,128)S(1)}, s32[4,256]{1,0:T(4,128)}, u32[]{:S(2)}) copy-start(s32[4,256]{1,0:T(4,128)} %refs_5_.3) | copy-start | bytes 12292
  14.8 3.2 %copy-start.6 = (s32[8]{0:T(128)S(1)}, s32[8]{0:T(128)}, u32[]{:S(2)}) copy-start(s32[8]{0:T(128)} %refs_6_.3) | copy-start | bytes 100
  14.8 8.2 %collective-permute-start = (f32[520,128]{1,0:T(8,128)}, f32[520,128]{1,0:T(8,128)S(1)}, u32[]{:S(2)}, u32[]{:S(2)}) collective-permute-start(f32[520,128]{1,0:T(8,128)} %get-tuple-element.27), channel_id=1, source_target_pairs={{0,4},{4,0},{8,12},{12,8},{16,20},{20,16},{24,28},{28,24},{1,5},{5... | collective-permute-start | bytes 798728 | tf_op jit(solution)/shard_map/ppermute | solution.py:39
  15.4 7.7 %collective-permute-start.1 = (f32[328,128]{1,0:T(8,128)}, f32[328,128]{1,0:T(8,128)S(1)}, u32[]{:S(2)}, u32[]{:S(2)}) collective-permute-start(f32[328,128]{1,0:T(8,128)} %get-tuple-element.29), channel_id=1, source_target_pairs={{0,2},{2,0},{1,3},{3,1},{4,6},{6,4},{5,7},{7,5},{8,10},{10,8},{9,1... | collective-permute-start | bytes 503816 | tf_op jit(solution)/shard_map/ppermute | solution.py:39
  24.3 6.7 %collective-permute-start.2 = (f32[136,128]{1,0:T(8,128)S(1)}, f32[136,128]{1,0:T(8,128)S(1)}, u32[]{:S(2)}, u32[]{:S(2)}) collective-permute-start(f32[136,128]{1,0:T(8,128)S(1)} %get-tuple-element.33), channel_id=1, source_target_pairs={{0,24},{4,28},{8,16},{12,20},{16,8},{20,12},{24,0},{28,4},{1,25},{... | collective-permute-start | bytes 208904 | tf_op jit(solution)/shard_map/ppermute | solution.py:39
  28.2 5.7 %collective-permute-start.3 = (f32[136,128]{1,0:T(8,128)S(1)}, f32[136,128]{1,0:T(8,128)S(1)}, u32[]{:S(2)}, u32[]{:S(2)}) collective-permute-start(f32[136,128]{1,0:T(8,128)S(1)} %get-tuple-element.34), channel_id=1, source_target_pairs={{0,16},{4,20},{8,24},{12,28},{16,0},{20,4},{24,8},{28,12},{1,17},{... | collective-permute-start | bytes 208904 | tf_op jit(solution)/shard_map/ppermute | solution.py:39
  28.2 5.7 %collective-permute-start.4 = (f32[136,128]{1,0:T(8,128)S(1)}, f32[136,128]{1,0:T(8,128)S(1)}, u32[]{:S(2)}, u32[]{:S(2)}) collective-permute-start(f32[136,128]{1,0:T(8,128)S(1)} %get-tuple-element.35), channel_id=1, source_target_pairs={{0,8},{4,12},{8,0},{12,4},{16,24},{20,28},{24,16},{28,20},{1,9},{5... | collective-permute-start | bytes 208904 | tf_op jit(solution)/shard_map/ppermute | solution.py:39
  34.1 7.0 %collective-permute-start.7 = (f32[136,128]{1,0:T(8,128)S(1)}, f32[136,128]{1,0:T(8,128)S(1)}, u32[]{:S(2)}, u32[]{:S(2)}) collective-permute-start(f32[136,128]{1,0:T(8,128)S(1)} %merge.2.refs_6_), channel_id=1, source_target_pairs={{0,24},{4,28},{8,16},{12,20},{16,8},{20,12},{24,0},{28,4},{1,25},{... | collective-permute-start | bytes 208904 | tf_op jit(solution)/shard_map/ppermute | solution.py:39
  36.8 6.5 %collective-permute-start.6 = (f32[136,128]{1,0:T(8,128)S(1)}, f32[136,128]{1,0:T(8,128)S(1)}, u32[]{:S(2)}, u32[]{:S(2)}) collective-permute-start(f32[136,128]{1,0:T(8,128)S(1)} %merge.2.refs_6_), channel_id=1, source_target_pairs={{0,16},{4,20},{8,24},{12,28},{16,0},{20,4},{24,8},{28,12},{1,17},{... | collective-permute-start | bytes 208904 | tf_op jit(solution)/shard_map/ppermute | solution.py:39
  36.9 6.5 %collective-permute-start.5 = (f32[136,128]{1,0:T(8,128)S(1)}, f32[136,128]{1,0:T(8,128)S(1)}, u32[]{:S(2)}, u32[]{:S(2)}) collective-permute-start(f32[136,128]{1,0:T(8,128)S(1)} %merge.2.refs_6_), channel_id=1, source_target_pairs={{0,8},{4,12},{8,0},{12,4},{16,24},{20,28},{24,16},{28,20},{1,9},{5... | collective-permute-start | bytes 208904 | tf_op jit(solution)/shard_map/ppermute | solution.py:39
  58.6 18.3 %collective-permute-start.8 = (f32[1040,128]{1,0:T(8,128)S(1)}, f32[1040,128]{1,0:T(8,128)S(1)}, u32[]{:S(2)}, u32[]{:S(2)}) collective-permute-start(f32[1040,128]{1,0:T(8,128)S(1)} %get-tuple-element.39.refs_0_.refs_2_), channel_id=1, source_target_pairs={{0,2},{2,0},{1,3},{3,1},{4,6},{6,4},{5,7},{7,5},{8,10},{10,8},{9,1... | collective-permute-start | bytes 1597448 | tf_op jit(solution)/shard_map/ppermute | solution.py:39
  59.0 6.9 %collective-permute-start.9 = (f32[136,128]{1,0:T(8,128)S(1)}, f32[136,128]{1,0:T(8,128)S(1)}, u32[]{:S(2)}, u32[]{:S(2)}) collective-permute-start(f32[136,128]{1,0:T(8,128)S(1)} %get-tuple-element.41), channel_id=1, source_target_pairs={{0,24},{4,28},{8,16},{12,20},{16,8},{20,12},{24,0},{28,4},{1,25},{... | collective-permute-start | bytes 208904 | tf_op jit(solution)/shard_map/ppermute | solution.py:39
  60.3 7.5 %collective-permute-start.10 = (f32[136,128]{1,0:T(8,128)S(1)}, f32[136,128]{1,0:T(8,128)S(1)}, u32[]{:S(2)}, u32[]{:S(2)}) collective-permute-start(f32[136,128]{1,0:T(8,128)S(1)} %get-tuple-element.42), channel_id=1, source_target_pairs={{0,16},{4,20},{8,24},{12,28},{16,0},{20,4},{24,8},{28,12},{1,17},{... | collective-permute-start | bytes 208904 | tf_op jit(solution)/shard_map/ppermute | solution.py:39
  61.1 6.8 %collective-permute-start.11 = (f32[136,128]{1,0:T(8,128)S(1)}, f32[136,128]{1,0:T(8,128)S(1)}, u32[]{:S(2)}, u32[]{:S(2)}) collective-permute-start(f32[136,128]{1,0:T(8,128)S(1)} %get-tuple-element.43), channel_id=1, source_target_pairs={{0,8},{4,12},{8,0},{12,4},{16,24},{20,28},{24,16},{28,20},{1,9},{5... | collective-permute-start | bytes 208904 | tf_op jit(solution)/shard_map/ppermute | solution.py:39
  68.0 7.0 %collective-permute-start.14 = (f32[136,128]{1,0:T(8,128)S(1)}, f32[136,128]{1,0:T(8,128)S(1)}, u32[]{:S(2)}, u32[]{:S(2)}) collective-permute-start(f32[136,128]{1,0:T(8,128)S(1)} %merge.3.refs_5_), channel_id=1, source_target_pairs={{0,24},{4,28},{8,16},{12,20},{16,8},{20,12},{24,0},{28,4},{1,25},{... | collective-permute-start | bytes 208904 | tf_op jit(solution)/shard_map/ppermute | solution.py:39
  69.7 7.3 %collective-permute-start.13 = (f32[136,128]{1,0:T(8,128)S(1)}, f32[136,128]{1,0:T(8,128)S(1)}, u32[]{:S(2)}, u32[]{:S(2)}) collective-permute-start(f32[136,128]{1,0:T(8,128)S(1)} %merge.3.refs_5_), channel_id=1, source_target_pairs={{0,16},{4,20},{8,24},{12,28},{16,0},{20,4},{24,8},{28,12},{1,17},{... | collective-permute-start | bytes 208904 | tf_op jit(solution)/shard_map/ppermute | solution.py:39
  69.7 7.3 %collective-permute-start.12 = (f32[136,128]{1,0:T(8,128)S(1)}, f32[136,128]{1,0:T(8,128)S(1)}, u32[]{:S(2)}, u32[]{:S(2)}) collective-permute-start(f32[136,128]{1,0:T(8,128)S(1)} %merge.3.refs_5_), channel_id=1, source_target_pairs={{0,8},{4,12},{8,0},{12,4},{16,24},{20,28},{24,16},{28,20},{1,9},{5... | collective-permute-start | bytes 208904 | tf_op jit(solution)/shard_map/ppermute | solution.py:39
  77.0 18.2 %collective-permute-start.15 = (f32[1040,128]{1,0:T(8,128)S(1)}, f32[1040,128]{1,0:T(8,128)S(1)}, u32[]{:S(2)}, u32[]{:S(2)}) collective-permute-start(f32[1040,128]{1,0:T(8,128)S(1)} %mate_parts.1), channel_id=1, source_target_pairs={{0,4},{4,0},{8,12},{12,8},{16,20},{20,16},{24,28},{28,24},{1,5},{5... | collective-permute-start | bytes 1597448 | tf_op jit(solution)/shard_map/ppermute | solution.py:39
  79.2 15.9 %collective-permute-start.17 = (f32[520,128]{1,0:T(8,128)S(1)}, f32[520,128]{1,0:T(8,128)S(1)}, u32[]{:S(2)}, u32[]{:S(2)}) collective-permute-start(f32[520,128]{1,0:T(8,128)S(1)} %get-tuple-element.46.refs_3_), channel_id=1, source_target_pairs={{0,2},{2,0},{4,6},{6,4},{8,10},{10,8},{12,14},{14,12},{16,18},{18,... | collective-permute-start | bytes 798728 | tf_op jit(solution)/shard_map/ppermute | solution.py:39
  80.2 15.0 %collective-permute-start.18 = (f32[520,128]{1,0:T(8,128)S(1)}, f32[520,128]{1,0:T(8,128)S(1)}, u32[]{:S(2)}, u32[]{:S(2)}) collective-permute-start(f32[520,128]{1,0:T(8,128)S(1)} %get-tuple-element.47), channel_id=1, source_target_pairs={{0,6},{2,4},{4,2},{6,0},{8,14},{10,12},{12,10},{14,8},{16,22},{18,... | collective-permute-start | bytes 798728 | tf_op jit(solution)/shard_map/ppermute | solution.py:39
  81.2 14.0 %collective-permute-start.16 = (f32[520,128]{1,0:T(8,128)S(1)}, f32[520,128]{1,0:T(8,128)S(1)}, u32[]{:S(2)}, u32[]{:S(2)}) collective-permute-start(f32[520,128]{1,0:T(8,128)S(1)} %get-tuple-element.47), channel_id=1, source_target_pairs={{0,4},{2,6},{4,0},{6,2},{8,12},{10,14},{12,8},{14,10},{16,20},{18,... | collective-permute-start | bytes 798728 | tf_op jit(solution)/shard_map/ppermute | solution.py:39

commit v6 on v5

--- a/solution.py
+++ b/solution.py
@@ -57,8 +57,7 @@
     return one_pass(left[0], right[0]) + cross
 
 
-def call(body, out_shapes, name, cost, operands, scratch=(), after=(), space=pltpu.VMEM,
-         out_space=pltpu.VMEM, vmem=32):
+def call(body, out_shapes, name, cost, operands, scratch=(), after=(), space=pltpu.VMEM, vmem=32):
     spaces = [space] * len(operands) + [pl.ANY] * len(after)
     count = len(operands)
 
@@ -69,7 +68,7 @@
         without_after,
         out_shape=[jax.ShapeDtypeStruct(shape, jnp.float32) for shape in out_shapes],
         in_specs=[pl.BlockSpec(memory_space=space) for space in spaces],
-        out_specs=[pl.BlockSpec(memory_space=out_space) for _ in out_shapes],
+        out_specs=[pl.BlockSpec(memory_space=pltpu.VMEM) for _ in out_shapes],
         scratch_shapes=scratch,
         compiler_params=pltpu.CompilerParams(vmem_limit_bytes=vmem * 2**20),
         cost_estimate=pl.CostEstimate(flops=cost, bytes_accessed=2**20, transcendentals=0),
@@ -178,7 +177,7 @@
         queries, keys, values, biases, targets, positions, assignment, state_out, *refs
     ):
         query_outs = refs[: query_devices - 1]
-        bias_ref, positions_ref, assignment_ref, tails, sems = refs[query_devices - 1 :]
+        bias_ref, positions_ref, assignment_ref, sems = refs[query_devices - 1 :]
         rank, core, me = places()
         heads = [CORES * (me ^ turn) + core for turn in range(1, query_devices)]
         mate_head = CORES * me + (core ^ 1)
@@ -191,13 +190,11 @@
         copies = start_all(copies, sems, 3)
         for copy in small:
             copy.wait()
-        tails[0] = state_tail(mate_head, CORES * rank + core, bias_ref, assignment_ref)
-        for at, head in enumerate(heads):
-            tails[1 + at] = position_tail(head, positions_ref)
-        ends = [(tails.at[0], state_out.at[pl.ds(2 * slot_rows, TAIL)])]
-        for at, out in enumerate(query_outs):
-            ends.append((tails.at[1 + at], out.at[pl.ds(part_rows + piece, TAIL)]))
-        copies += start_all(ends, sems, 3 + len(copies))
+        state_out[2 * slot_rows :, :] = state_tail(
+            mate_head, CORES * rank + core, bias_ref, assignment_ref
+        )
+        for head, out in zip(heads, query_outs):
+            out[part_rows + piece :, :] = position_tail(head, positions_ref)
         for copy in copies:
             copy.wait()
 
@@ -237,13 +234,8 @@
         "pack",
         2**20,
         arguments,
-        small_scratch
-        + [
-            pltpu.VMEM((query_devices, TAIL, width), jnp.float32),
-            pltpu.SemaphoreType.DMA((5 + 3 * query_devices,)),
-        ],
+        small_scratch + [pltpu.SemaphoreType.DMA((3 + 2 * query_devices,))],
         space=pl.ANY,
-        out_space=pl.ANY,
         vmem=60,
     )
     own_state, own_queries = call(

time: 96.5 us -> 84.4 us (0.87)
  Pallas kernels: 23.1 us -> 10.9 us
    pallas_call x10, Pallas kernels: 23.1 us -> 10.9 us  [call(): pl.pallas_call(without_after, out_shape=[jax.ShapeDtypeStruct(shape, jnp....]
where the time goes in v6:
time: 84.4 us; the launch traced here: 84.2 us
  blocking collectives  25.5 us (30%)
  starting transfers between devices  23.6 us (28%)
  waiting for transfers between devices  23.4 us (28%)
  Pallas kernels  10.9 us (13%)
    all_to_all x2, blocking collectives, direct_per_device(): lax.all_to_all(squares, ('page', 'query', 'head'), split_axis=0, concat_a...  25.5 us
    ppermute x19, starting transfers between devices, exchange(): return lax.ppermute(value, axes, pairs)  23.6 us
    ppermute x19, waiting for transfers between devices, exchange(): return lax.ppermute(value, axes, pairs)  23.4 us
    pallas_call x10, Pallas kernels, call(): pl.pallas_call(without_after, out_shape=[jax.ShapeDtypeStruct(shape, jnp....  10.9 us
  transfers between devices with their start and end apart: 19, of which 9 were waited for; matrix products, arithmetic and copies ran while one was open for 0% of the time, Pallas kernels for 3%

profile of v6, /device:TPU:0, one launch (start us, length us, event | category | flops | bytes accessed | tf_op | source)
XLA Modules:
  0.0 84.2 jit_solution(2562000116437776472)
XLA Ops:
  0.7 2.0 %pack.1 = (f32[520,128]{1,0:T(8,128)}, f32[328,128]{1,0:T(8,128)}) custom-call(f32[4,256,128]{2,1,0:T(8,128)} %refs_0_.3, f32[4,256,128]{2,1,0:T(8,128)} %refs_1_.3, f32[4,256,128]{2,1,0:T(8,128)} %refs_2_.3, f32[4,256]{1,0:T(4,128)} %refs_3_.3, f32[4,256,128]{2,1,0:T(8,128)} %refs_4_.3, s32[4,256]{1,0:T(4,128)} %refs_5_.3, s32[8]{0:T(128)} %refs_6_.3), custom_call_target="tpu_custom_call" | custom-call | flops 1048576 | bytes 1048576 | tf_op jit(solution)/shard_map/pack/pallas_call | solution.py:67
  2.7 0.0 copy-start.6
  2.7 0.5 collective-permute-start
  3.3 2.6 %collective-permute-start.1 = (f32[328,128]{1,0:T(8,128)}, f32[328,128]{1,0:T(8,128)S(1)}, u32[]{:S(2)}, u32[]{:S(2)}) collective-permute-start(f32[328,128]{1,0:T(8,128)} %get-tuple-element.29), channel_id=1, source_target_pairs={{0,2},{2,0},{1,3},{3,1},{4,6},{6,4},{5,7},{7,5},{8,10},{10,8},{9,1... | collective-permute-start | bytes 503816 | tf_op jit(solution)/shard_map/ppermute | solution.py:39
  5.9 0.7 own.1
  6.6 4.4 %collective-permute-done.1.refs_3_.refs_1_.refs_5_.refs_4_ = f32[328,128]{1,0:T(8,128)S(1)} collective-permute-done((f32[328,128]{1,0:T(8,128)}, f32[328,128]{1,0:T(8,128)S(1)}, u32[]{:S(2)}, u32[]{:S(2)}) %collective-permute-start.1) | collective-permute-done | bytes 167968 | tf_op jit(solution)/shard_map/ppermute | solution.py:39
  10.9 0.0 collective-permute-done.refs_1_.refs_3_
  10.9 1.2 %forward.1 = (f32[136,128]{1,0:T(8,128)S(1)}, f32[136,128]{1,0:T(8,128)S(1)}, f32[136,128]{1,0:T(8,128)S(1)}, f32[136,128]{1,0:T(8,128)S(1)}, f32[512,512]{1,0:T(8,128)S(1)}, /*index=5*/f32[8,512]{1,0:T(8,128)S(1)}) custom-call(f32[520,128]{1,0:T(8,128)S(1)} %get-tuple-element.26.refs_0_.refs_2_, f32[520,128]{1,0:T(8,128)S(1)} %collective-permute-done.refs_1_.refs_3_, ...), custom_call_target="tpu_custom_call" | custom-call | flops 402653184 | bytes 1048576 | tf_op jit(solution)/shard_map/forward/pallas_call | solution.py:67
  12.2 3.9 %collective-permute-start.2 = (f32[136,128]{1,0:T(8,128)S(1)}, f32[136,128]{1,0:T(8,128)S(1)}, u32[]{:S(2)}, u32[]{:S(2)}) collective-permute-start(f32[136,128]{1,0:T(8,128)S(1)} %get-tuple-element.33), channel_id=1, source_target_pairs={{0,24},{4,28},{8,16},{12,20},{16,8},{20,12},{24,0},{28,4},{1,25},{... | collective-permute-start | bytes 208904 | tf_op jit(solution)/shard_map/ppermute | solution.py:39
  16.1 0.0 collective-permute-start.3
  16.1 0.6 collective-permute-start.4
  16.7 2.1 %collective-permute-done.2.refs_3_ = f32[136,128]{1,0:T(8,128)S(1)} collective-permute-done((f32[136,128]{1,0:T(8,128)S(1)}, f32[136,128]{1,0:T(8,128)S(1)}, u32[]{:S(2)}, u32[]{:S(2)}) %collective-permute-start.2) | collective-permute-done | bytes 69664 | tf_op jit(solution)/shard_map/ppermute | solution.py:39
  18.9 3.0 %collective-permute-done.3.refs_4_ = f32[136,128]{1,0:T(8,128)S(1)} collective-permute-done((f32[136,128]{1,0:T(8,128)S(1)}, f32[136,128]{1,0:T(8,128)S(1)}, u32[]{:S(2)}, u32[]{:S(2)}) %collective-permute-start.3) | collective-permute-done | bytes 69664 | tf_op jit(solution)/shard_map/ppermute | solution.py:39
  21.8 0.0 collective-permute-done.4.refs_5_
  21.8 0.1 merge.2.refs_6_
  22.0 2.8 %collective-permute-start.7 = (f32[136,128]{1,0:T(8,128)S(1)}, f32[136,128]{1,0:T(8,128)S(1)}, u32[]{:S(2)}, u32[]{:S(2)}) collective-permute-start(f32[136,128]{1,0:T(8,128)S(1)} %merge.2.refs_6_), channel_id=1, source_target_pairs={{0,24},{4,28},{8,16},{12,20},{16,8},{20,12},{24,0},{28,4},{1,25},{... | collective-permute-start | bytes 208904 | tf_op jit(solution)/shard_map/ppermute | solution.py:39
  24.7 0.0 collective-permute-start.6
  24.7 1.7 %collective-permute-start.5 = (f32[136,128]{1,0:T(8,128)S(1)}, f32[136,128]{1,0:T(8,128)S(1)}, u32[]{:S(2)}, u32[]{:S(2)}) collective-permute-start(f32[136,128]{1,0:T(8,128)S(1)} %merge.2.refs_6_), channel_id=1, source_target_pairs={{0,8},{4,12},{8,0},{12,4},{16,24},{20,28},{24,16},{28,20},{1,9},{5... | collective-permute-start | bytes 208904 | tf_op jit(solution)/shard_map/ppermute | solution.py:39
  26.4 2.5 %collective-permute-done.7.refs_9_ = f32[136,128]{1,0:T(8,128)S(1)} collective-permute-done((f32[136,128]{1,0:T(8,128)S(1)}, f32[136,128]{1,0:T(8,128)S(1)}, u32[]{:S(2)}, u32[]{:S(2)}) %collective-permute-start.7) | collective-permute-done | bytes 69664 | tf_op jit(solution)/shard_map/ppermute | solution.py:39
  28.9 2.4 %collective-permute-done.6.refs_8_ = f32[136,128]{1,0:T(8,128)S(1)} collective-permute-done((f32[136,128]{1,0:T(8,128)S(1)}, f32[136,128]{1,0:T(8,128)S(1)}, u32[]{:S(2)}, u32[]{:S(2)}) %collective-permute-start.6) | collective-permute-done | bytes 69664 | tf_op jit(solution)/shard_map/ppermute | solution.py:39
  31.3 2.1 %backward.2 = (f32[520,128]{1,0:T(8,128)S(1)}, f32[520,128]{1,0:T(8,128)S(1)}, f32[32,8,128]{2,1,0:T(8,128)S(1)}) custom-call(f32[512,512]{1,0:T(8,128)S(1)} %get-tuple-element.30.refs_0_, f32[8,512]{1,0:T(8,128)S(1)} %get-tuple-element.31.refs_1_, f32[520,128]{1,0:T(8,128)S(1)} %get-tuple-element.26.refs_0_.refs_2_, ...), custom_call_target="tpu_custom_call" | custom-call | flops 603979776 | bytes 1048576 | tf_op jit(solution)/shard_map/backward/pallas_call | solution.py:67
  33.4 11.8 %all_to_all.10.refs_6_ = f32[32,8,128]{2,1,0:T(8,128)S(1)} all-to-all(f32[32,8,128]{2,1,0:T(8,128)S(1)} %get-tuple-element.38), channel_id=1, replica_groups=mesh['page'=8,'query'=2,'head'=2] {'page','query','head'}, dimensions={0} | all-to-all | bytes 262144 | tf_op jit(solution)/shard_map/all_to_all | solution.py:484
  45.2 1.3 %update_forward.1 = (f32[1040,128]{1,0:T(8,128)S(1)}, f32[136,128]{1,0:T(8,128)S(1)}, f32[136,128]{1,0:T(8,128)S(1)}, f32[136,128]{1,0:T(8,128)S(1)}, f32[136,12...) custom-call(f32[520,128]{1,0:T(8,128)S(1)} %get-tuple-element.26.refs_0_.refs_2_, ...), custom_call_target="tpu_custom_call" | custom-call | flops 402653184 | bytes 1048576 | tf_op jit(solution)/shard_map/update_forward/pallas_call | solution.py:67
  46.5 0.3 collective-permute-start.8
  46.9 1.4 %collective-permute-start.9 = (f32[136,128]{1,0:T(8,128)S(1)}, f32[136,128]{1,0:T(8,128)S(1)}, u32[]{:S(2)}, u32[]{:S(2)}) collective-permute-start(f32[136,128]{1,0:T(8,128)S(1)} %get-tuple-element.41), channel_id=1, source_target_pairs={{0,24},{4,28},{8,16},{12,20},{16,8},{20,12},{24,0},{28,4},{1,25},{... | collective-permute-start | bytes 208904 | tf_op jit(solution)/shard_map/ppermute | solution.py:39
  48.2 0.8 collective-permute-start.10
  49.0 2.2 %collective-permute-start.11 = (f32[136,128]{1,0:T(8,128)S(1)}, f32[136,128]{1,0:T(8,128)S(1)}, u32[]{:S(2)}, u32[]{:S(2)}) collective-permute-start(f32[136,128]{1,0:T(8,128)S(1)} %get-tuple-element.43), channel_id=1, source_target_pairs={{0,8},{4,12},{8,0},{12,4},{16,24},{20,28},{24,16},{28,20},{1,9},{5... | collective-permute-start | bytes 208904 | tf_op jit(solution)/shard_map/ppermute | solution.py:39
  51.2 2.5 %collective-permute-done.9.refs_3_ = f32[136,128]{1,0:T(8,128)S(1)} collective-permute-done((f32[136,128]{1,0:T(8,128)S(1)}, f32[136,128]{1,0:T(8,128)S(1)}, u32[]{:S(2)}, u32[]{:S(2)}) %collective-permute-start.9) | collective-permute-done | bytes 69664 | tf_op jit(solution)/shard_map/ppermute | solution.py:39
  53.7 2.0 %collective-permute-done.10.refs_4_ = f32[136,128]{1,0:T(8,128)S(1)} collective-permute-done((f32[136,128]{1,0:T(8,128)S(1)}, f32[136,128]{1,0:T(8,128)S(1)}, u32[]{:S(2)}, u32[]{:S(2)}) %collective-permute-start.10) | collective-permute-done | bytes 69664 | tf_op jit(solution)/shard_map/ppermute | solution.py:39
  55.8 0.0 collective-permute-done.11.refs_5_
  55.8 0.1 merge.3.refs_5_
  55.9 1.7 %collective-permute-start.14 = (f32[136,128]{1,0:T(8,128)S(1)}, f32[136,128]{1,0:T(8,128)S(1)}, u32[]{:S(2)}, u32[]{:S(2)}) collective-permute-start(f32[136,128]{1,0:T(8,128)S(1)} %merge.3.refs_5_), channel_id=1, source_target_pairs={{0,24},{4,28},{8,16},{12,20},{16,8},{20,12},{24,0},{28,4},{1,25},{... | collective-permute-start | bytes 208904 | tf_op jit(solution)/shard_map/ppermute | solution.py:39
  57.6 0.0 collective-permute-start.13
  57.6 2.8 %collective-permute-start.12 = (f32[136,128]{1,0:T(8,128)S(1)}, f32[136,128]{1,0:T(8,128)S(1)}, u32[]{:S(2)}, u32[]{:S(2)}) collective-permute-start(f32[136,128]{1,0:T(8,128)S(1)} %merge.3.refs_5_), channel_id=1, source_target_pairs={{0,8},{4,12},{8,0},{12,4},{16,24},{20,28},{24,16},{28,20},{1,9},{5... | collective-permute-start | bytes 208904 | tf_op jit(solution)/shard_map/ppermute | solution.py:39
  60.3 2.5 %collective-permute-done.14.refs_4_.refs_8_ = f32[136,128]{1,0:T(8,128)S(1)} collective-permute-done((f32[136,128]{1,0:T(8,128)S(1)}, f32[136,128]{1,0:T(8,128)S(1)}, u32[]{:S(2)}, u32[]{:S(2)}) %collective-permute-start.14) | collective-permute-done | bytes 69664 | tf_op jit(solution)/shard_map/ppermute | solution.py:39
  62.9 2.0 %collective-permute-done.13.refs_3_.refs_7_ = f32[136,128]{1,0:T(8,128)S(1)} collective-permute-done((f32[136,128]{1,0:T(8,128)S(1)}, f32[136,128]{1,0:T(8,128)S(1)}, u32[]{:S(2)}, u32[]{:S(2)}) %collective-permute-start.13) | collective-permute-done | bytes 69664 | tf_op jit(solution)/shard_map/ppermute | solution.py:39
  64.9 0.0 collective-permute-done.12.refs_2_.refs_6_
  64.9 0.0 collective-permute-done.8.refs_1_
  64.9 0.1 collective-permute-start.15
  65.0 2.2 %backward.3 = (f32[520,128]{1,0:T(8,128)S(1)}, f32[520,128]{1,0:T(8,128)S(1)}, f32[32,8,128]{2,1,0:T(8,128)S(1)}) custom-call(f32[512,512]{1,0:T(8,128)S(1)} %get-tuple-element.44.refs_0_, f32[8,512]{1,0:T(8,128)S(1)} %get-tuple-element.45.refs_1_, f32[1040,128]{1,0:T(8,128)S(1)} %get-tuple-element.39.refs_0_.refs_2_, ...), custom_call_target="tpu_custom_call" | custom-call | flops 603979776 | bytes 1048576 | tf_op jit(solution)/shard_map/backward/pallas_call | solution.py:67
  67.2 0.9 %collective-permute-start.17 = (f32[520,128]{1,0:T(8,128)S(1)}, f32[520,128]{1,0:T(8,128)S(1)}, u32[]{:S(2)}, u32[]{:S(2)}) collective-permute-start(f32[520,128]{1,0:T(8,128)S(1)} %get-tuple-element.46.refs_3_), channel_id=1, source_target_pairs={{0,2},{2,0},{4,6},{6,4},{8,10},{10,8},{12,14},{14,12},{16,18},{18,... | collective-permute-start | bytes 798728 | tf_op jit(solution)/shard_map/ppermute | solution.py:39
  68.1 1.0 %collective-permute-start.18 = (f32[520,128]{1,0:T(8,128)S(1)}, f32[520,128]{1,0:T(8,128)S(1)}, u32[]{:S(2)}, u32[]{:S(2)}) collective-permute-start(f32[520,128]{1,0:T(8,128)S(1)} %get-tuple-element.47), channel_id=1, source_target_pairs={{0,6},{2,4},{4,2},{6,0},{8,14},{10,12},{12,10},{14,8},{16,22},{18,... | collective-permute-start | bytes 798728 | tf_op jit(solution)/shard_map/ppermute | solution.py:39
  69.1 0.3 collective-permute-start.16
  69.4 13.7 %all_to_all.11.refs_7_ = f32[32,8,128]{2,1,0:T(8,128)S(1)} all-to-all(f32[32,8,128]{2,1,0:T(8,128)S(1)} %get-tuple-element.48), channel_id=1, replica_groups=mesh['page'=8,'query'=2,'head'=2] {'page','query','head'}, dimensions={0} | all-to-all | bytes 262144 | tf_op jit(solution)/shard_map/all_to_all | solution.py:484
  83.1 0.0 collective-permute-done.17.refs_5_
  83.1 0.0 collective-permute-done.18.refs_6_
  83.1 0.0 collective-permute-done.16.refs_4_
  83.1 1.1 %last_update.1 = (f32[4,256,128]{2,1,0:T(8,128)}, f32[4,256,128]{2,1,0:T(8,128)}, f32[4,256]{1,0:T(4,128)}) custom-call(f32[1040,128]{1,0:T(8,128)S(1)} %get-tuple-element.39.refs_0_.refs_2_, f32[1040,128]{1,0:T(8,128)S(1)} %collective-permute-done.8.refs_1_, f32[1040,128]{1,0:T(8,128)S(1)} %collective-permute-done.15.refs_2_, ...), custom_call_target="tpu_custom_call" | custom-call | flops 1048576 | bytes 1048576 | tf_op jit(solution)/shard_map/last_update/pallas_call | solution.py:67
  (16 shorter events, 0.1 us)
Async XLA Ops:
  0.6 5.2 %copy-start.3 = (f32[4,256,128]{2,1,0:T(8,128)S(1)}, f32[4,256,128]{2,1,0:T(8,128)}, u32[]{:S(2)}) copy-start(f32[4,256,128]{2,1,0:T(8,128)} %refs_4_.3) | copy-start | bytes 1572868
  0.6 5.2 %copy-start.2 = (f32[4,256,128]{2,1,0:T(8,128)S(1)}, f32[4,256,128]{2,1,0:T(8,128)}, u32[]{:S(2)}) copy-start(f32[4,256,128]{2,1,0:T(8,128)} %refs_2_.3) | copy-start | bytes 1572868
  0.7 5.2 %copy-start.1 = (f32[4,256,128]{2,1,0:T(8,128)S(1)}, f32[4,256,128]{2,1,0:T(8,128)}, u32[]{:S(2)}) copy-start(f32[4,256,128]{2,1,0:T(8,128)} %refs_1_.3) | copy-start | bytes 1572868
  0.7 5.2 %copy-start = (f32[4,256,128]{2,1,0:T(8,128)S(1)}, f32[4,256,128]{2,1,0:T(8,128)}, u32[]{:S(2)}) copy-start(f32[4,256,128]{2,1,0:T(8,128)} %refs_0_.3) | copy-start | bytes 1572868
  0.7 5.2 %copy-start.4 = (f32[4,256]{1,0:T(4,128)S(1)}, f32[4,256]{1,0:T(4,128)}, u32[]{:S(2)}) copy-start(f32[4,256]{1,0:T(4,128)} %refs_3_.3) | copy-start | bytes 12292
  0.7 5.2 %copy-start.5 = (s32[4,256]{1,0:T(4,128)S(1)}, s32[4,256]{1,0:T(4,128)}, u32[]{:S(2)}) copy-start(s32[4,256]{1,0:T(4,128)} %refs_5_.3) | copy-start | bytes 12292
  2.7 3.2 %copy-start.6 = (s32[8]{0:T(128)S(1)}, s32[8]{0:T(128)}, u32[]{:S(2)}) copy-start(s32[8]{0:T(128)} %refs_6_.3) | copy-start | bytes 100
  2.7 8.2 %collective-permute-start = (f32[520,128]{1,0:T(8,128)}, f32[520,128]{1,0:T(8,128)S(1)}, u32[]{:S(2)}, u32[]{:S(2)}) collective-permute-start(f32[520,128]{1,0:T(8,128)} %get-tuple-element.27), channel_id=1, source_target_pairs={{0,4},{4,0},{8,12},{12,8},{16,20},{20,16},{24,28},{28,24},{1,5},{5... | collective-permute-start | bytes 798728 | tf_op jit(solution)/shard_map/ppermute | solution.py:39
  3.3 7.7 %collective-permute-start.1 = (f32[328,128]{1,0:T(8,128)}, f32[328,128]{1,0:T(8,128)S(1)}, u32[]{:S(2)}, u32[]{:S(2)}) collective-permute-start(f32[328,128]{1,0:T(8,128)} %get-tuple-element.29), channel_id=1, source_target_pairs={{0,2},{2,0},{1,3},{3,1},{4,6},{6,4},{5,7},{7,5},{8,10},{10,8},{9,1... | collective-permute-start | bytes 503816 | tf_op jit(solution)/shard_map/ppermute | solution.py:39
  12.2 6.7 %collective-permute-start.2 = (f32[136,128]{1,0:T(8,128)S(1)}, f32[136,128]{1,0:T(8,128)S(1)}, u32[]{:S(2)}, u32[]{:S(2)}) collective-permute-start(f32[136,128]{1,0:T(8,128)S(1)} %get-tuple-element.33), channel_id=1, source_target_pairs={{0,24},{4,28},{8,16},{12,20},{16,8},{20,12},{24,0},{28,4},{1,25},{... | collective-permute-start | bytes 208904 | tf_op jit(solution)/shard_map/ppermute | solution.py:39
  16.1 5.7 %collective-permute-start.3 = (f32[136,128]{1,0:T(8,128)S(1)}, f32[136,128]{1,0:T(8,128)S(1)}, u32[]{:S(2)}, u32[]{:S(2)}) collective-permute-start(f32[136,128]{1,0:T(8,128)S(1)} %get-tuple-element.34), channel_id=1, source_target_pairs={{0,16},{4,20},{8,24},{12,28},{16,0},{20,4},{24,8},{28,12},{1,17},{... | collective-permute-start | bytes 208904 | tf_op jit(solution)/shard_map/ppermute | solution.py:39
  16.1 5.7 %collective-permute-start.4 = (f32[136,128]{1,0:T(8,128)S(1)}, f32[136,128]{1,0:T(8,128)S(1)}, u32[]{:S(2)}, u32[]{:S(2)}) collective-permute-start(f32[136,128]{1,0:T(8,128)S(1)} %get-tuple-element.35), channel_id=1, source_target_pairs={{0,8},{4,12},{8,0},{12,4},{16,24},{20,28},{24,16},{28,20},{1,9},{5... | collective-permute-start | bytes 208904 | tf_op jit(solution)/shard_map/ppermute | solution.py:39
  22.0 7.0 %collective-permute-start.7 = (f32[136,128]{1,0:T(8,128)S(1)}, f32[136,128]{1,0:T(8,128)S(1)}, u32[]{:S(2)}, u32[]{:S(2)}) collective-permute-start(f32[136,128]{1,0:T(8,128)S(1)} %merge.2.refs_6_), channel_id=1, source_target_pairs={{0,24},{4,28},{8,16},{12,20},{16,8},{20,12},{24,0},{28,4},{1,25},{... | collective-permute-start | bytes 208904 | tf_op jit(solution)/shard_map/ppermute | solution.py:39
  24.7 6.5 %collective-permute-start.6 = (f32[136,128]{1,0:T(8,128)S(1)}, f32[136,128]{1,0:T(8,128)S(1)}, u32[]{:S(2)}, u32[]{:S(2)}) collective-permute-start(f32[136,128]{1,0:T(8,128)S(1)} %merge.2.refs_6_), channel_id=1, source_target_pairs={{0,16},{4,20},{8,24},{12,28},{16,0},{20,4},{24,8},{28,12},{1,17},{... | collective-permute-start | bytes 208904 | tf_op jit(solution)/shard_map/ppermute | solution.py:39
  24.7 6.5 %collective-permute-start.5 = (f32[136,128]{1,0:T(8,128)S(1)}, f32[136,128]{1,0:T(8,128)S(1)}, u32[]{:S(2)}, u32[]{:S(2)}) collective-permute-start(f32[136,128]{1,0:T(8,128)S(1)} %merge.2.refs_6_), channel_id=1, source_target_pairs={{0,8},{4,12},{8,0},{12,4},{16,24},{20,28},{24,16},{28,20},{1,9},{5... | collective-permute-start | bytes 208904 | tf_op jit(solution)/shard_map/ppermute | solution.py:39
  46.5 18.3 %collective-permute-start.8 = (f32[1040,128]{1,0:T(8,128)S(1)}, f32[1040,128]{1,0:T(8,128)S(1)}, u32[]{:S(2)}, u32[]{:S(2)}) collective-permute-start(f32[1040,128]{1,0:T(8,128)S(1)} %get-tuple-element.39.refs_0_.refs_2_), channel_id=1, source_target_pairs={{0,2},{2,0},{1,3},{3,1},{4,6},{6,4},{5,7},{7,5},{8,10},{10,8},{9,1... | collective-permute-start | bytes 1597448 | tf_op jit(solution)/shard_map/ppermute | solution.py:39
  46.9 6.9 %collective-permute-start.9 = (f32[136,128]{1,0:T(8,128)S(1)}, f32[136,128]{1,0:T(8,128)S(1)}, u32[]{:S(2)}, u32[]{:S(2)}) collective-permute-start(f32[136,128]{1,0:T(8,128)S(1)} %get-tuple-element.41), channel_id=1, source_target_pairs={{0,24},{4,28},{8,16},{12,20},{16,8},{20,12},{24,0},{28,4},{1,25},{... | collective-permute-start | bytes 208904 | tf_op jit(solution)/shard_map/ppermute | solution.py:39
  48.2 7.5 %collective-permute-start.10 = (f32[136,128]{1,0:T(8,128)S(1)}, f32[136,128]{1,0:T(8,128)S(1)}, u32[]{:S(2)}, u32[]{:S(2)}) collective-permute-start(f32[136,128]{1,0:T(8,128)S(1)} %get-tuple-element.42), channel_id=1, source_target_pairs={{0,16},{4,20},{8,24},{12,28},{16,0},{20,4},{24,8},{28,12},{1,17},{... | collective-permute-start | bytes 208904 | tf_op jit(solution)/shard_map/ppermute | solution.py:39
  49.0 6.8 %collective-permute-start.11 = (f32[136,128]{1,0:T(8,128)S(1)}, f32[136,128]{1,0:T(8,128)S(1)}, u32[]{:S(2)}, u32[]{:S(2)}) collective-permute-start(f32[136,128]{1,0:T(8,128)S(1)} %get-tuple-element.43), channel_id=1, source_target_pairs={{0,8},{4,12},{8,0},{12,4},{16,24},{20,28},{24,16},{28,20},{1,9},{5... | collective-permute-start | bytes 208904 | tf_op jit(solution)/shard_map/ppermute | solution.py:39
  55.9 7.0 %collective-permute-start.14 = (f32[136,128]{1,0:T(8,128)S(1)}, f32[136,128]{1,0:T(8,128)S(1)}, u32[]{:S(2)}, u32[]{:S(2)}) collective-permute-start(f32[136,128]{1,0:T(8,128)S(1)} %merge.3.refs_5_), channel_id=1, source_target_pairs={{0,24},{4,28},{8,16},{12,20},{16,8},{20,12},{24,0},{28,4},{1,25},{... | collective-permute-start | bytes 208904 | tf_op jit(solution)/shard_map/ppermute | solution.py:39
  57.6 7.3 %collective-permute-start.13 = (f32[136,128]{1,0:T(8,128)S(1)}, f32[136,128]{1,0:T(8,128)S(1)}, u32[]{:S(2)}, u32[]{:S(2)}) collective-permute-start(f32[136,128]{1,0:T(8,128)S(1)} %merge.3.refs_5_), channel_id=1, source_target_pairs={{0,16},{4,20},{8,24},{12,28},{16,0},{20,4},{24,8},{28,12},{1,17},{... | collective-permute-start | bytes 208904 | tf_op jit(solution)/shard_map/ppermute | solution.py:39
  57.6 7.3 %collective-permute-start.12 = (f32[136,128]{1,0:T(8,128)S(1)}, f32[136,128]{1,0:T(8,128)S(1)}, u32[]{:S(2)}, u32[]{:S(2)}) collective-permute-start(f32[136,128]{1,0:T(8,128)S(1)} %merge.3.refs_5_), channel_id=1, source_target_pairs={{0,8},{4,12},{8,0},{12,4},{16,24},{20,28},{24,16},{28,20},{1,9},{5... | collective-permute-start | bytes 208904 | tf_op jit(solution)/shard_map/ppermute | solution.py:39
  64.9 18.2 %collective-permute-start.15 = (f32[1040,128]{1,0:T(8,128)S(1)}, f32[1040,128]{1,0:T(8,128)S(1)}, u32[]{:S(2)}, u32[]{:S(2)}) collective-permute-start(f32[1040,128]{1,0:T(8,128)S(1)} %mate_parts.1), channel_id=1, source_target_pairs={{0,4},{4,0},{8,12},{12,8},{16,20},{20,16},{24,28},{28,24},{1,5},{5... | collective-permute-start | bytes 1597448 | tf_op jit(solution)/shard_map/ppermute | solution.py:39
  67.2 15.9 %collective-permute-start.17 = (f32[520,128]{1,0:T(8,128)S(1)}, f32[520,128]{1,0:T(8,128)S(1)}, u32[]{:S(2)}, u32[]{:S(2)}) collective-permute-start(f32[520,128]{1,0:T(8,128)S(1)} %get-tuple-element.46.refs_3_), channel_id=1, source_target_pairs={{0,2},{2,0},{4,6},{6,4},{8,10},{10,8},{12,14},{14,12},{16,18},{18,... | collective-permute-start | bytes 798728 | tf_op jit(solution)/shard_map/ppermute | solution.py:39
  68.1 15.0 %collective-permute-start.18 = (f32[520,128]{1,0:T(8,128)S(1)}, f32[520,128]{1,0:T(8,128)S(1)}, u32[]{:S(2)}, u32[]{:S(2)}) collective-permute-start(f32[520,128]{1,0:T(8,128)S(1)} %get-tuple-element.47), channel_id=1, source_target_pairs={{0,6},{2,4},{4,2},{6,0},{8,14},{10,12},{12,10},{14,8},{16,22},{18,... | collective-permute-start | bytes 798728 | tf_op jit(solution)/shard_map/ppermute | solution.py:39
  69.1 14.0 %collective-permute-start.16 = (f32[520,128]{1,0:T(8,128)S(1)}, f32[520,128]{1,0:T(8,128)S(1)}, u32[]{:S(2)}, u32[]{:S(2)}) collective-permute-start(f32[520,128]{1,0:T(8,128)S(1)} %get-tuple-element.47), channel_id=1, source_target_pairs={{0,4},{2,6},{4,0},{6,2},{8,12},{10,14},{12,8},{14,10},{16,20},{18,... | collective-permute-start | bytes 798728 | tf_op jit(solution)/shard_map/ppermute | solution.py:39

commit v7 on v6

--- a/solution.py
+++ b/solution.py
@@ -110,6 +110,7 @@
         part_rows * query_devices % ranks == 0
         and chunk % 128 == 0
         and part_rows % (8 * ranks) == 0
+        and (part_rows // ranks % 128 == 0 or 1024 % (part_rows // ranks * 8) == 0)
         and slot_rows % width == 0
         and part_rows % width == 0
         and max(slot_rows, part_rows) < TAIL * width
@@ -134,7 +135,7 @@
     pos_rows = part_rows // width
     bias_rows = slot_rows // width
     packed_rows = 2 * slot_rows + TAIL
-    packed_shapes = [(packed_rows, width)] * 2
+    packed_shapes = [(packed_rows, width)] * CORES
     matmul_cost = 3 * 2 * slots * query_rows * width
 
     def places():
@@ -173,84 +174,84 @@
             [tail[: TAIL - 1], jnp.full((1, width), page_start, jnp.float32)], axis=0
         )
 
-    def send_body(
-        queries, keys, values, biases, targets, positions, assignment, state_out, *refs
+    def pack_tails(refs, heads, page, bias_ref, assignment_ref):
+        for ref, head in zip(refs, heads):
+            ref[2 * slot_rows :, :] = state_tail(head, page, bias_ref, assignment_ref)
+
+    def part_of(ref, at):
+        return ref.at[pl.ds(at * packed_rows, packed_rows)]
+
+    def send_body(keys, values, biases, assignment, states_out, bias_ref, assignment_ref, sems):
+        rank, core, me = places()
+        heads = [CORES * (me ^ turn) + (core ^ 1) for turn in range(query_devices)]
+        outs = [part_of(states_out, turn) for turn in range(query_devices)]
+        small = start_all([(assignment, assignment_ref), (biases, bias_ref)], sems)
+        copies = [pair for head, out in zip(heads, outs) for pair in pack_state(head, keys, values, out)]
+        copies = start_all(copies, sems, 2)
+        for copy in small:
+            copy.wait()
+        pack_tails(outs, heads, CORES * rank + core, bias_ref, assignment_ref)
+        for copy in copies:
+            copy.wait()
+
+    def own_body(
+        queries, keys, values, biases, targets, positions, assignment, states_out, *refs
     ):
-        query_outs = refs[: query_devices - 1]
-        bias_ref, positions_ref, assignment_ref, sems = refs[query_devices - 1 :]
+        query_outs, refs = refs[:query_devices], refs[query_devices:]
+        bias_ref, assignment_ref, positions_ref, sems = refs
         rank, core, me = places()
-        heads = [CORES * (me ^ turn) + core for turn in range(1, query_devices)]
-        mate_head = CORES * me + (core ^ 1)
+        heads = [CORES * (me ^ turn) + core for turn in range(query_devices)]
+        outs = [part_of(states_out, turn) for turn in range(query_devices)]
         small = start_all(
-            [(assignment, assignment_ref), (positions, positions_ref), (biases, bias_ref)], sems
-        )
-        copies = pack_state(mate_head, keys, values, state_out)
-        for head, out in zip(heads, query_outs):
-            copies += pack_queries(head, rank, queries, targets, out)
+            [(assignment, assignment_ref), (biases, bias_ref), (positions, positions_ref)], sems
+        )
+        copies = []
+        for head, out, query_out in zip(heads, outs, query_outs):
+            copies += pack_state(head, keys, values, out)
+            copies += pack_queries(head, rank, queries, targets, query_out)
         copies = start_all(copies, sems, 3)
         for copy in small:
             copy.wait()
-        state_out[2 * slot_rows :, :] = state_tail(
-            mate_head, CORES * rank + core, bias_ref, assignment_ref
-        )
-        for head, out in zip(heads, query_outs):
-            out[part_rows + piece :, :] = position_tail(head, positions_ref)
+        pack_tails(outs, heads, CORES * rank + core, bias_ref, assignment_ref)
+        for head, query_out in zip(heads, query_outs):
+            query_out[part_rows + piece :, :] = position_tail(head, positions_ref)
         for copy in copies:
             copy.wait()
 
-    def own_body(
-        queries, keys, values, biases, targets, positions, assignment, state_out, query_out, *refs
-    ):
-        bias_ref, positions_ref, assignment_ref, sems = refs
-        rank, core, me = places()
-        head = CORES * me + core
-        small = start_all(
-            [(assignment, assignment_ref), (positions, positions_ref), (biases, bias_ref)], sems
-        )
-        copies = pack_state(head, keys, values, state_out)
-        copies += pack_queries(head, rank, queries, targets, query_out)
-        copies = start_all(copies, sems, 3)
-        for copy in small:
-            copy.wait()
-        state_out[2 * slot_rows :, :] = state_tail(
-            head, CORES * rank + core, bias_ref, assignment_ref
-        )
-        query_out[part_rows + piece :, :] = position_tail(head, positions_ref)
-        for copy in copies:
-            copy.wait()
-
-    state_shape, query_shape = (packed_rows, width), (part_rows + piece + TAIL, width)
+    states_shape = (query_devices * packed_rows, width)
+    query_shape = (part_rows + piece + TAIL, width)
     small_scratch = [
         pltpu.VMEM(slot_bias.shape, jnp.float32),
-        pltpu.VMEM(positions.shape, jnp.int32),
         pltpu.SMEM(assignment.shape, jnp.int32),
     ]
-    arguments = [
-        queries, compact_keys, compact_values, slot_bias, targets, positions, assignment
-    ]
-    mate_state, *sent_queries = call(
+    (sent_states,) = call(
         send_body,
-        [state_shape] + [query_shape] * (query_devices - 1),
+        [states_shape],
         "pack",
         2**20,
-        arguments,
-        small_scratch + [pltpu.SemaphoreType.DMA((3 + 2 * query_devices,))],
+        [compact_keys, compact_values, slot_bias, assignment],
+        small_scratch + [pltpu.SemaphoreType.DMA((2 + 2 * query_devices,))],
         space=pl.ANY,
         vmem=60,
     )
-    own_state, own_queries = call(
+    mate_states = exchange(sent_states, page=1)
+    own_states, *own_queries = call(
         own_body,
-        [state_shape, query_shape],
+        [states_shape] + [query_shape] * query_devices,
         "own",
         2**24,
-        arguments,
-        small_scratch + [pltpu.SemaphoreType.DMA((7,))],
+        [queries, compact_keys, compact_values, slot_bias, targets, positions, assignment],
+        small_scratch
+        + [
+            pltpu.VMEM(positions.shape, jnp.int32),
+            pltpu.SemaphoreType.DMA((3 + 4 * query_devices,)),
+        ],
         space=pl.ANY,
     )
-    query_parts = [own_queries] + [
-        exchange(sent_queries[turn - 1], query=turn) for turn in range(1, query_devices)
+    query_parts = own_queries[:1] + [
+        exchange(own_queries[turn], query=turn) for turn in range(1, query_devices)
     ]
-    states = [own_state, exchange(mate_state, page=1)]
+    states = [own_states, mate_states]
 
     def in_columns(parts, axis):
         return jnp.concatenate(
@@ -265,11 +266,10 @@
     def read_queries(query_refs):
         return halves(in_columns([ref[:part_rows, :] for ref in query_refs], 0))
 
-    def part_of(ref, at):
-        return ref.at[pl.ds(at * packed_rows, packed_rows)]
-
-    def parts_of(refs):
-        return refs if len(refs) == CORES else [part_of(refs[0], at) for at in range(CORES)]
+    def pages_of(refs):
+        if len(refs) == CORES:
+            return [part_of(ref, 0) for ref in refs]
+        return [part_of(refs[0], at) for at in range(CORES)]
 
     def step_sizes(tile_refs):
         tile = jnp.sum(tile_refs[0][...], axis=0)
@@ -288,71 +288,94 @@
             state_ref[value_end:, :] - sizes[2] * grad_ref[value_end:, :],
         )
 
-    def forward(state_refs, query_refs, chunk_outs, weights_out, max_out, chunks):
-        rank, _, _ = places()
-        all_queries = read_queries(query_refs)
-        position_row = in_columns(
-            [tail_as_row(ref, part_rows + piece, pos_rows) for ref in query_refs], 1
-        )
+    def position_row(ref):
+        return tail_as_row(ref, part_rows + piece, pos_rows)
+
+    def local_weights(state_refs, queries, positions):
+        columns = positions.shape[1]
         all_scores, all_visible = [], []
-        for at, ref in enumerate(state_refs):
-            scores = dot(halves(ref[:slot_rows, :]), all_queries, 1, 1) * score_scale
+        for ref in state_refs:
+            scores = dot(halves(ref[:slot_rows, :]), queries, 1, 1) * score_scale
             bias = row_as_column(tail_as_row(ref, 2 * slot_rows, bias_rows), width)
-            scores = scores + jnp.concatenate([bias] * (query_rows // width), axis=1)
+            scores = scores + jnp.concatenate([bias] * (columns // width), axis=1)
             page_start = ref[packed_rows - 1 : packed_rows, 0:1]
-            visible = jnp.broadcast_to(position_row >= page_start, scores.shape)
+            visible = jnp.broadcast_to(positions >= page_start, scores.shape)
             all_scores.append(jnp.where(visible, scores, MASKED))
             all_visible.append(visible)
         row_max = jnp.max(all_scores[0], axis=0, keepdims=True)
         for scores in all_scores[1:]:
             row_max = jnp.maximum(row_max, jnp.max(scores, axis=0, keepdims=True))
+        weights = [
+            jnp.where(visible, jnp.exp(scores - row_max), 0.0)
+            for scores, visible in zip(all_scores, all_visible)
+        ]
+        return weights, row_max
+
+    def local_sums(state_refs, weights, row_max):
         row_total = jnp.zeros_like(row_max)
-        row_sum = jnp.zeros((width, query_rows), jnp.float32)
-        for at, ref in enumerate(state_refs):
-            weights = jnp.where(all_visible[at], jnp.exp(all_scores[at] - row_max), 0.0)
-            weights_out[at * slot_rows : (at + 1) * slot_rows, :] = weights
-            row_total = row_total + jnp.sum(weights, axis=0, keepdims=True)
+        row_sum = jnp.zeros((width, row_max.shape[1]), jnp.float32)
+        for ref, part in zip(state_refs, weights):
+            row_total = row_total + jnp.sum(part, axis=0, keepdims=True)
             values = halves(ref[slot_rows : 2 * slot_rows, :])
-            row_sum = row_sum + dot(values, halves(weights), 0, 0)
-        max_out[...] = jnp.broadcast_to(row_max, (TAIL, query_rows))
-        tail = jnp.concatenate(
-            [row_max, row_total, jnp.zeros((TAIL - 2, query_rows), jnp.float32)], axis=0
-        )
+            row_sum = row_sum + dot(values, halves(part), 0, 0)
+        empty = jnp.zeros((TAIL - 2, row_max.shape[1]), jnp.float32)
+        return jnp.concatenate([row_sum, row_max, row_total, empty], axis=0)
+
+    def store_chunks(sums, chunk_outs, chunks):
+        rank, _, _ = places()
         for at in range(ranks):
-            columns = slice(at * chunk, (at + 1) * chunk)
-            chunks[at, :width, :] = row_sum[:, columns]
-            chunks[at, width:, :] = tail[:, columns]
+            chunks[at] = sums[:, at * chunk : (at + 1) * chunk]
         for turn in range(ranks):
             chunk_outs[turn][...] = chunks[rank ^ turn]
 
+    def store_weights(weights, row_max, weights_out, max_out):
+        for at, part in enumerate(weights):
+            weights_out[at * slot_rows : (at + 1) * slot_rows, :] = part
+        max_out[...] = jnp.broadcast_to(row_max, (TAIL, query_rows))
+
     chunk_shape = (width + TAIL, chunk)
-    forward_shapes = [chunk_shape] * ranks + [(slots, query_rows), (TAIL, query_rows)]
+    weight_shapes = [(slots, query_rows), (TAIL, query_rows)]
     chunk_scratch = [pltpu.VMEM((ranks,) + chunk_shape, jnp.float32)]
 
-    def first_body(*refs):
-        state_refs, refs = refs[:2], refs[2:]
+    def first_body(own_ref, mate_ref, *refs):
         query_refs, refs = refs[:query_devices], refs[query_devices:]
-        chunk_outs, refs = refs[:ranks], refs[ranks:]
-        forward(state_refs, query_refs, chunk_outs, *refs)
+        chunk_outs, (chunks,) = refs[:ranks], refs[ranks:]
+        sums = []
+        for turn, ref in enumerate(query_refs):
+            state_refs = [part_of(own_ref, turn), part_of(mate_ref, turn)]
+            weights, row_max = local_weights(
+                state_refs, halves(ref[:part_rows, :]), position_row(ref)
+            )
+            sums.append(local_sums(state_refs, weights, row_max))
+        store_chunks(in_columns(sums, 1), chunk_outs, chunks)
+
+    def all_weights(state_refs, query_refs):
+        positions = in_columns([position_row(ref) for ref in query_refs], 1)
+        return local_weights(state_refs, read_queries(query_refs), positions)
+
+    def weights_body(*refs):
+        state_refs, refs = pages_of(refs[:2]), refs[2:]
+        query_refs, outs = refs[:query_devices], refs[query_devices:]
+        store_weights(*all_weights(state_refs, query_refs), *outs)
 
     def next_body(*refs):
-        state_refs, refs = refs[:2], refs[2:]
+        state_refs, refs = pages_of(refs[:2]), refs[2:]
         query_refs, refs = refs[:query_devices], refs[query_devices:]
         grad_refs, refs = refs[:2], refs[2:]
         tile_refs, refs = refs[: len(tiles)], refs[len(tiles) :]
-        state_outs, refs = parts_of(refs[:1]), refs[1:]
-        chunk_outs, refs = refs[:ranks], refs[ranks:]
+        state_outs, refs = pages_of(refs[:1]), refs[1:]
+        chunk_outs, (weights_out, max_out, chunks) = refs[:ranks], refs[ranks:]
         sizes = step_sizes(tile_refs)
         for at in range(2):
             keys, values, bias = updated(state_refs[at], grad_refs[at], sizes)
             state_outs[at][:slot_rows, :] = keys
             state_outs[at][slot_rows : 2 * slot_rows, :] = values
             state_outs[at][2 * slot_rows :, :] = bias
-        forward(state_outs, query_refs, chunk_outs, *refs)
-
-    def merge_body(*refs):
-        query_refs, refs = refs[:query_devices], refs[query_devices:]
-        chunk_refs, (merged_out,) = refs[:ranks], refs[ranks:]
+        weights, row_max = all_weights(state_outs, query_refs)
+        store_weights(weights, row_max, weights_out, max_out)
+        store_chunks(local_sums(state_outs, weights, row_max), chunk_outs, chunks)
+
+    def merged_chunk(query_refs, chunk_refs):
         targets = jnp.concatenate(
             [ref[part_rows : part_rows + piece, :] for ref in query_refs], axis=0
         )
@@ -368,20 +391,62 @@
         output = row_sum / row_total
         residual = output - targets.T
         row_delta = jnp.sum(residual * output, axis=0, keepdims=True)
+        empty = jnp.zeros((TAIL - 3, chunk), jnp.float32)
+        return residual, jnp.concatenate([row_max, row_total, row_delta, empty], axis=0)
+
+    fold = max(1, 128 // piece)
+    folded = width // fold
+    piece_shape = (folded + TAIL, fold * piece)
+
+    def first_merge_body(*refs):
+        query_refs, refs = refs[:query_devices], refs[query_devices:]
+        chunk_refs, piece_outs = refs[:ranks], refs[ranks:]
+        residual, tail = merged_chunk(query_refs, chunk_refs)
+        for turn, out in enumerate(piece_outs):
+            columns = slice(turn * piece, (turn + 1) * piece)
+            out[:folded, :] = jnp.concatenate(
+                [residual[at * folded : (at + 1) * folded, columns] for at in range(fold)], axis=1
+            )
+            out[folded:, :] = jnp.concatenate([tail[:, columns]] * fold, axis=1)
+
+    def merge_body(*refs):
+        query_refs, refs = refs[:query_devices], refs[query_devices:]
+        chunk_refs, (merged_out,) = refs[:ranks], refs[ranks:]
+        residual, tail = merged_chunk(query_refs, chunk_refs)
         merged_out[:width, :] = residual
-        merged_out[width:, :] = jnp.concatenate(
-            [row_max, row_total, row_delta, jnp.zeros((TAIL - 3, chunk), jnp.float32)], axis=0
-        )
+        merged_out[width:, :] = tail
+
+    def join_pieces(piece_refs, pieces):
+        rank, _, _ = places()
+        for at, ref in enumerate(piece_refs):
+            pieces[rank ^ (at % ranks), at // ranks] = ref[...]
+        joined = []
+        for at in range(ranks):
+            for turn in range(query_devices):
+                groups = [
+                    pieces[at, turn, :folded, group * piece : (group + 1) * piece]
+                    for group in range(fold)
+                ]
+                joined.append(
+                    jnp.concatenate(groups + [pieces[at, turn, folded:, :piece]], axis=0)
+                )
+        return jnp.concatenate(joined, axis=1)
+
+    def join_chunks(merged_refs, chunks):
+        rank, _, _ = places()
+        for turn, ref in enumerate(merged_refs):
+            chunks[rank ^ turn] = ref[...]
+        return jnp.concatenate([chunks[at] for at in range(ranks)], axis=1)
 
     def backward_body(weights_ref, max_ref, *refs):
-        state_refs, refs = parts_of(refs[: len(states)]), refs[len(states) :]
+        state_refs, refs = pages_of(refs[: len(states)]), refs[len(states) :]
         query_refs, refs = refs[:query_devices], refs[query_devices:]
-        merged_refs, refs = refs[:ranks], refs[ranks:]
-        grad_outs, (squares_out, chunks) = refs[:2], refs[2:]
-        rank, _, _ = places()
-        for turn in range(ranks):
-            chunks[rank ^ turn] = merged_refs[turn][...]
-        joined = jnp.concatenate([chunks[at] for at in range(ranks)], axis=1)
+        merged_refs, refs = refs[: len(all_merged)], refs[len(all_merged) :]
+        grad_outs, (squares_out, received) = refs[:2], refs[2:]
+        if len(states) == CORES:
+            joined = join_pieces(merged_refs, received)
+        else:
+            joined = join_chunks(merged_refs, received)
         residual = joined[:width, :]
         row_max, row_total, row_delta = (
             joined[width + at : width + at + 1, :] for at in range(3)
@@ -415,26 +480,28 @@
 
     out_masks = list(itertools.product(range(query_devices), range(CORES)))
 
-    def to_output(packs, mask):
-        if mask == (0, 0):
-            return packs[0]
-        return exchange(packs[mask[1]], page=mask[1], query=mask[0])
+    def to_device(value, **masks):
+        masks = {axis: mask for axis, mask in masks.items() if mask}
+        return exchange(value, **masks) if masks else value
 
     for repeat in range(STEPS):
         last = repeat == STEPS - 1
         if repeat == 0:
-            *chunk_parts, weights, maxima = call(
+            chunk_parts = call(
                 first_body,
-                forward_shapes,
+                [chunk_shape] * ranks,
                 "forward",
                 2 * matmul_cost,
-                states + query_parts,
+                states + own_queries,
                 chunk_scratch,
+            )
+            weights, maxima = call(
+                weights_body, weight_shapes, "weights", matmul_cost, states + query_parts
             )
         else:
             new_state, *chunk_parts, weights, maxima = call(
                 next_body,
-                [(CORES * packed_rows, width)] + forward_shapes,
+                [(CORES * packed_rows, width)] + [chunk_shape] * ranks + weight_shapes,
                 "update_forward",
                 2 * matmul_cost,
                 states + query_parts + grads + tiles,
@@ -449,16 +516,27 @@
             new_states = states + [
                 exchange(states[0], query=turn) for turn in range(1, query_devices)
             ]
-        (merged,) = call(
-            merge_body,
-            [chunk_shape],
-            "merge",
-            2**20,
-            query_parts + chunk_parts[:1] + list(arrived.values()),
-        )
-        all_merged = [merged] + [
-            exchange(merged, page=CORES * turn) for turn in range(1, ranks)
-        ]
+        chunk_parts = [chunk_parts[0]] + list(arrived.values())
+        if repeat == 0:
+            pieces = call(
+                first_merge_body,
+                [piece_shape] * query_devices,
+                "first_merge",
+                2**20,
+                own_queries + chunk_parts,
+            )
+            all_merged = [
+                to_device(pieces[turn], page=CORES * shift, query=turn)
+                for turn in range(query_devices)
+                for shift in range(ranks)
+            ]
+            received = pltpu.VMEM((ranks, query_devices) + piece_shape, jnp.float32)
+        else:
+            (merged,) = call(
+                merge_body, [chunk_shape], "merge", 2**20, query_parts + chunk_parts
+            )
+            all_merged = [to_device(merged, page=CORES * shift) for shift in range(ranks)]
+            received = chunk_scratch[0]
         if repeat:
             (for_mate,) = call(
                 mate_body,
@@ -475,11 +553,13 @@
             "backward",
             3 * matmul_cost,
             [weights, maxima] + states + query_parts + all_merged,
-            scratch=chunk_scratch,
+            scratch=[received],
         )
         grads = [own_grad, mate_grad]
         if last:
-            all_grads = [to_output(grads, mask) for mask in out_masks]
+            all_grads = [
+                to_device(grads[flip], page=flip, query=turn) for turn, flip in out_masks
+            ]
         tiles = [
             lax.all_to_all(
                 squares, ("page", "query", "head"), split_axis=0, concat_axis=0, tiled=True

time: 84.4 us -> 88 us (1.043)
  waiting for transfers between devices: 23.4 us -> 16.1 us
  starting transfers between devices: 23.6 us -> 30.2 us
  Pallas kernels: 10.9 us -> 12.8 us
  blocking collectives: 25.5 us -> 26.7 us
  local copies, waits for them, and re-layouts: 0.03 us -> 1.06 us
    ppermute x19 -> x23, waiting for transfers between devices: 23.4 us -> 16.1 us  [exchange(): return lax.ppermute(value, axes, pairs)]
    ppermute x19 -> x23, starting transfers between devices: 23.6 us -> 30.2 us  [exchange(): return lax.ppermute(value, axes, pairs)]
    pallas_call x10 -> x11, Pallas kernels: 10.9 us -> 12.8 us  [call(): pl.pallas_call(without_after, out_shape=[jax.ShapeDtypeStruct(shape, jnp....]
    all_to_all x2, blocking collectives: 25.5 us -> 26.7 us  [direct_per_device(): lax.all_to_all(squares, ('page', 'query', 'head'), split_axis=0, concat_a...]
    unnamed x14, local copies, waits for them, and re-layouts: 0.03 us -> 1.06 us
  transfers between devices with their start and end apart: 19 -> 23, of which waited for: 9 -> 8; matrix products, arithmetic and copies ran while one was open for 0% -> 0% of each run, Pallas kernels for 3% -> 7%
where the time goes in v7:
time: 88 us; the launch traced here: 87.7 us
  starting transfers between devices  30.2 us (34%)
  blocking collectives  26.7 us (30%)
  waiting for transfers between devices  16.1 us (18%)
  Pallas kernels  12.8 us (15%)
  local copies, waits for them, and re-layouts  1.06 us (1%)
    ppermute x23, starting transfers between devices, exchange(): return lax.ppermute(value, axes, pairs)  30.2 us
    all_to_all x2, blocking collectives, direct_per_device(): lax.all_to_all(squares, ('page', 'query', 'head'), split_axis=0, concat_a...  26.7 us
    ppermute x23, waiting for transfers between devices, exchange(): return lax.ppermute(value, axes, pairs)  16.1 us
    pallas_call x11, Pallas kernels, call(): pl.pallas_call(without_after, out_shape=[jax.ShapeDtypeStruct(shape, jnp....  12.8 us
  transfers between devices with their start and end apart: 23, of which 8 were waited for; matrix products, arithmetic and copies ran while one was open for 0% of the time, Pallas kernels for 7%

profile of v7, /device:TPU:0, one launch (start us, length us, event | category | flops | bytes accessed | tf_op | source)
XLA Modules:
  0.0 87.7 jit_solution(345421415679147870)
XLA Ops:
  0.7 2.1 %pack.1 = f32[1040,128]{1,0:T(8,128)} custom-call(f32[4,256,128]{2,1,0:T(8,128)} %refs_0_.3, f32[4,256,128]{2,1,0:T(8,128)} %refs_1_.3, f32[4,256]{1,0:T(4,128)} %refs_2_.3, s32[8]{0:T(128)} %refs_3_.3), custom_call_target="tpu_custom_call" | custom-call | flops 1048576 | bytes 1048576 | tf_op jit(solution)/shard_map/pack/pallas_call | solution.py:67
  2.8 0.5 collective-permute-start
  3.3 0.0 copy-start.3
  3.3 1.0 %copy-done.3 = f32[4,256,128]{2,1,0:T(8,128)S(1)} copy-done((f32[4,256,128]{2,1,0:T(8,128)S(1)}, f32[4,256,128]{2,1,0:T(8,128)}, u32[]{:S(2)}) %copy-start.3) | copy-done | bytes 524312
  4.4 1.2 %own.1 = (f32[1040,128]{1,0:T(8,128)S(1)}, f32[328,128]{1,0:T(8,128)S(1)}, f32[328,128]{1,0:T(8,128)S(1)}) custom-call(f32[4,256,128]{2,1,0:T(8,128)S(1)} %copy-done.2, f32[4,256,128]{2,1,0:T(8,128)S(1)} %copy-done, f32[4,256,128]{2,1,0:T(8,128)S(1)} %copy-done.1, f32[4,256]{1,0:T(4,128)S(1)} %copy-done.4, f32[4,256,128]{2,1,0:T(8,128)S(1)} %copy-done.3, ...), custom_call_target="tpu_custom_call" | custom-call | flops 16777216 | bytes 1048576 | tf_op jit(solution)/shard_map/own/pallas_call | solution.py:67
  5.6 2.6 %collective-permute-start.1 = (f32[328,128]{1,0:T(8,128)S(1)}, f32[328,128]{1,0:T(8,128)S(1)}, u32[]{:S(2)}, u32[]{:S(2)}) collective-permute-start(f32[328,128]{1,0:T(8,128)S(1)} %get-tuple-element.29.refs_3_.refs_1_), channel_id=1, source_target_pairs={{0,2},{2,0},{1,3},{3,1},{4,6},{6,4},{5,7},{7,5},{8,10},{10,8},{9,1... | collective-permute-start | bytes 503816 | tf_op jit(solution)/shard_map/ppermute | solution.py:39
  8.2 0.0 collective-permute-done.refs_1_.refs_3_
  8.2 1.6 %forward.1 = (f32[136,128]{1,0:T(8,128)S(1)}, f32[136,128]{1,0:T(8,128)S(1)}, f32[136,128]{1,0:T(8,128)S(1)}, f32[136,128]{1,0:T(8,128)S(1)}) custom-call(f32[1040,128]{1,0:T(8,128)S(1)} %get-tuple-element.27.refs_0_.refs_2_, f32[1040,128]{1,0:T(8,128)S(1)} %collective-permute-done.refs_1_.refs_3_, ...), custom_call_target="tpu_custom_call" | custom-call | flops 402653184 | bytes 1048576 | tf_op jit(solution)/shard_map/forward/pallas_call | solution.py:67
  9.8 3.6 %collective-permute-start.2 = (f32[136,128]{1,0:T(8,128)S(1)}, f32[136,128]{1,0:T(8,128)S(1)}, u32[]{:S(2)}, u32[]{:S(2)}) collective-permute-start(f32[136,128]{1,0:T(8,128)S(1)} %get-tuple-element.33), channel_id=1, source_target_pairs={{0,24},{4,28},{8,16},{12,20},{16,8},{20,12},{24,0},{28,4},{1,25},{... | collective-permute-start | bytes 208904 | tf_op jit(solution)/shard_map/ppermute | solution.py:39
  13.4 0.0 collective-permute-start.3
  13.4 0.8 collective-permute-start.4
  14.2 2.1 %collective-permute-done.2.refs_3_ = f32[136,128]{1,0:T(8,128)S(1)} collective-permute-done((f32[136,128]{1,0:T(8,128)S(1)}, f32[136,128]{1,0:T(8,128)S(1)}, u32[]{:S(2)}, u32[]{:S(2)}) %collective-permute-start.2) | collective-permute-done | bytes 69664 | tf_op jit(solution)/shard_map/ppermute | solution.py:39
  16.3 3.3 %collective-permute-done.3.refs_4_ = f32[136,128]{1,0:T(8,128)S(1)} collective-permute-done((f32[136,128]{1,0:T(8,128)S(1)}, f32[136,128]{1,0:T(8,128)S(1)}, u32[]{:S(2)}, u32[]{:S(2)}) %collective-permute-start.3) | collective-permute-done | bytes 69664 | tf_op jit(solution)/shard_map/ppermute | solution.py:39
  19.7 0.0 collective-permute-done.4.refs_5_
  19.7 0.2 first_merge.1
  19.8 2.5 %collective-permute-start.7 = (f32[72,128]{1,0:T(8,128)S(1)}, f32[72,128]{1,0:T(8,128)S(1)}, u32[]{:S(2)}, u32[]{:S(2)}) collective-permute-start(f32[72,128]{1,0:T(8,128)S(1)} %get-tuple-element.36.refs_6_), channel_id=1, source_target_pairs={{0,24},{4,28},{8,16},{12,20},{16,8},{20,12},{24,0},{28,4},{1,25},{... | collective-permute-start | bytes 110600 | tf_op jit(solution)/shard_map/ppermute | solution.py:39
  22.4 0.1 collective-permute-start.6
  22.5 1.8 %collective-permute-start.5 = (f32[72,128]{1,0:T(8,128)S(1)}, f32[72,128]{1,0:T(8,128)S(1)}, u32[]{:S(2)}, u32[]{:S(2)}) collective-permute-start(f32[72,128]{1,0:T(8,128)S(1)} %get-tuple-element.36.refs_6_), channel_id=1, source_target_pairs={{0,8},{4,12},{8,0},{12,4},{16,24},{20,28},{24,16},{28,20},{1,9},{5... | collective-permute-start | bytes 110600 | tf_op jit(solution)/shard_map/ppermute | solution.py:39
  24.3 2.4 %collective-permute-start.11 = (f32[72,128]{1,0:T(8,128)S(1)}, f32[72,128]{1,0:T(8,128)S(1)}, u32[]{:S(2)}, u32[]{:S(2)}) collective-permute-start(f32[72,128]{1,0:T(8,128)S(1)} %get-tuple-element.37), channel_id=1, source_target_pairs={{0,26},{2,24},{4,30},{6,28},{8,18},{10,16},{12,22},{14,20},{16,10}... | collective-permute-start | bytes 110600 | tf_op jit(solution)/shard_map/ppermute | solution.py:39
  26.7 0.0 collective-permute-done.1.refs_3_.refs_5_.refs_1_.refs_4_
  26.7 0.2 collective-permute-start.10
  26.9 0.0 collective-permute-done.7.refs_9_
  26.9 2.7 %collective-permute-start.9 = (f32[72,128]{1,0:T(8,128)S(1)}, f32[72,128]{1,0:T(8,128)S(1)}, u32[]{:S(2)}, u32[]{:S(2)}) collective-permute-start(f32[72,128]{1,0:T(8,128)S(1)} %get-tuple-element.37), channel_id=1, source_target_pairs={{0,10},{2,8},{4,14},{6,12},{8,2},{10,0},{12,6},{14,4},{16,26},{18,... | collective-permute-start | bytes 110600 | tf_op jit(solution)/shard_map/ppermute | solution.py:39
  29.5 1.5 %collective-permute-start.8 = (f32[72,128]{1,0:T(8,128)S(1)}, f32[72,128]{1,0:T(8,128)S(1)}, u32[]{:S(2)}, u32[]{:S(2)}) collective-permute-start(f32[72,128]{1,0:T(8,128)S(1)} %get-tuple-element.37), channel_id=1, source_target_pairs={{0,2},{2,0},{1,3},{3,1},{4,6},{6,4},{5,7},{7,5},{8,10},{10,8},{9,1... | collective-permute-start | bytes 110600 | tf_op jit(solution)/shard_map/ppermute | solution.py:39
  31.1 0.7 weights.1
  31.8 0.6 collective-permute-done.10.refs_12_
  32.5 1.0 %collective-permute-done.8.refs_10_ = f32[72,128]{1,0:T(8,128)S(1)} collective-permute-done((f32[72,128]{1,0:T(8,128)S(1)}, f32[72,128]{1,0:T(8,128)S(1)}, u32[]{:S(2)}, u32[]{:S(2)}) %collective-permute-start.8) | collective-permute-done | bytes 36896 | tf_op jit(solution)/shard_map/ppermute | solution.py:39
  33.5 2.3 %backward.2 = (f32[520,128]{1,0:T(8,128)S(1)}, f32[520,128]{1,0:T(8,128)S(1)}, f32[32,8,128]{2,1,0:T(8,128)S(1)}) custom-call(f32[512,512]{1,0:T(8,128)S(1)} %get-tuple-element.30.refs_0_, f32[8,512]{1,0:T(8,128)S(1)} %get-tuple-element.31.refs_1_, f32[1040,128]{1,0:T(8,128)S(1)} %get-tuple-element.27.refs_0_.refs_2_, ...), custom_call_target="tpu_custom_call" | custom-call | flops 603979776 | bytes 1048576 | tf_op jit(solution)/shard_map/backward/pallas_call | solution.py:67
  35.8 12.9 %all_to_all.10.refs_6_ = f32[32,8,128]{2,1,0:T(8,128)S(1)} all-to-all(f32[32,8,128]{2,1,0:T(8,128)S(1)} %get-tuple-element.40), channel_id=1, replica_groups=mesh['page'=8,'query'=2,'head'=2] {'page','query','head'}, dimensions={0} | all-to-all | bytes 262144 | tf_op jit(solution)/shard_map/all_to_all | solution.py:564
  48.7 1.3 %update_forward.1 = (f32[1040,128]{1,0:T(8,128)S(1)}, f32[136,128]{1,0:T(8,128)S(1)}, f32[136,128]{1,0:T(8,128)S(1)}, f32[136,128]{1,0:T(8,128)S(1)}, f32[136,12...) custom-call(f32[1040,128]{1,0:T(8,128)S(1)} %get-tuple-element.27.refs_0_.refs_2_, ...), custom_call_target="tpu_custom_call" | custom-call | flops 402653184 | bytes 1048576 | tf_op jit(solution)/shard_map/update_forward/pallas_call | solution.py:67
  50.1 0.3 collective-permute-start.12
  50.4 1.4 %collective-permute-start.13 = (f32[136,128]{1,0:T(8,128)S(1)}, f32[136,128]{1,0:T(8,128)S(1)}, u32[]{:S(2)}, u32[]{:S(2)}) collective-permute-start(f32[136,128]{1,0:T(8,128)S(1)} %get-tuple-element.43), channel_id=1, source_target_pairs={{0,24},{4,28},{8,16},{12,20},{16,8},{20,12},{24,0},{28,4},{1,25},{... | collective-permute-start | bytes 208904 | tf_op jit(solution)/shard_map/ppermute | solution.py:39
  51.8 0.8 collective-permute-start.14
  52.5 2.2 %collective-permute-start.15 = (f32[136,128]{1,0:T(8,128)S(1)}, f32[136,128]{1,0:T(8,128)S(1)}, u32[]{:S(2)}, u32[]{:S(2)}) collective-permute-start(f32[136,128]{1,0:T(8,128)S(1)} %get-tuple-element.45), channel_id=1, source_target_pairs={{0,8},{4,12},{8,0},{12,4},{16,24},{20,28},{24,16},{28,20},{1,9},{5... | collective-permute-start | bytes 208904 | tf_op jit(solution)/shard_map/ppermute | solution.py:39
  54.8 2.5 %collective-permute-done.13.refs_3_ = f32[136,128]{1,0:T(8,128)S(1)} collective-permute-done((f32[136,128]{1,0:T(8,128)S(1)}, f32[136,128]{1,0:T(8,128)S(1)}, u32[]{:S(2)}, u32[]{:S(2)}) %collective-permute-start.13) | collective-permute-done | bytes 69664 | tf_op jit(solution)/shard_map/ppermute | solution.py:39
  57.3 2.0 %collective-permute-done.14.refs_4_ = f32[136,128]{1,0:T(8,128)S(1)} collective-permute-done((f32[136,128]{1,0:T(8,128)S(1)}, f32[136,128]{1,0:T(8,128)S(1)}, u32[]{:S(2)}, u32[]{:S(2)}) %collective-permute-start.14) | collective-permute-done | bytes 69664 | tf_op jit(solution)/shard_map/ppermute | solution.py:39
  59.3 0.1 merge.1.refs_5_
  59.4 1.7 %collective-permute-start.18 = (f32[136,128]{1,0:T(8,128)S(1)}, f32[136,128]{1,0:T(8,128)S(1)}, u32[]{:S(2)}, u32[]{:S(2)}) collective-permute-start(f32[136,128]{1,0:T(8,128)S(1)} %merge.1.refs_5_), channel_id=1, source_target_pairs={{0,24},{4,28},{8,16},{12,20},{16,8},{20,12},{24,0},{28,4},{1,25},{... | collective-permute-start | bytes 208904 | tf_op jit(solution)/shard_map/ppermute | solution.py:39
  61.1 2.8 %collective-permute-start.16 = (f32[136,128]{1,0:T(8,128)S(1)}, f32[136,128]{1,0:T(8,128)S(1)}, u32[]{:S(2)}, u32[]{:S(2)}) collective-permute-start(f32[136,128]{1,0:T(8,128)S(1)} %merge.1.refs_5_), channel_id=1, source_target_pairs={{0,8},{4,12},{8,0},{12,4},{16,24},{20,28},{24,16},{28,20},{1,9},{5... | collective-permute-start | bytes 208904 | tf_op jit(solution)/shard_map/ppermute | solution.py:39
  63.9 2.5 %collective-permute-done.18.refs_4_.refs_8_ = f32[136,128]{1,0:T(8,128)S(1)} collective-permute-done((f32[136,128]{1,0:T(8,128)S(1)}, f32[136,128]{1,0:T(8,128)S(1)}, u32[]{:S(2)}, u32[]{:S(2)}) %collective-permute-start.18) | collective-permute-done | bytes 69664 | tf_op jit(solution)/shard_map/ppermute | solution.py:39
  66.4 2.0 %collective-permute-done.17.refs_3_.refs_7_ = f32[136,128]{1,0:T(8,128)S(1)} collective-permute-done((f32[136,128]{1,0:T(8,128)S(1)}, f32[136,128]{1,0:T(8,128)S(1)}, u32[]{:S(2)}, u32[]{:S(2)}) %collective-permute-start.17) | collective-permute-done | bytes 69664 | tf_op jit(solution)/shard_map/ppermute | solution.py:39
  68.4 0.1 collective-permute-start.19
  68.5 2.1 %backward.3 = (f32[520,128]{1,0:T(8,128)S(1)}, f32[520,128]{1,0:T(8,128)S(1)}, f32[32,8,128]{2,1,0:T(8,128)S(1)}) custom-call(f32[512,512]{1,0:T(8,128)S(1)} %get-tuple-element.46.refs_0_, f32[8,512]{1,0:T(8,128)S(1)} %get-tuple-element.47.refs_1_, f32[1040,128]{1,0:T(8,128)S(1)} %get-tuple-element.41.refs_0_.refs_2_, ...), custom_call_target="tpu_custom_call" | custom-call | flops 603979776 | bytes 1048576 | tf_op jit(solution)/shard_map/backward/pallas_call | solution.py:67
  70.6 0.9 %collective-permute-start.21 = (f32[520,128]{1,0:T(8,128)S(1)}, f32[520,128]{1,0:T(8,128)S(1)}, u32[]{:S(2)}, u32[]{:S(2)}) collective-permute-start(f32[520,128]{1,0:T(8,128)S(1)} %get-tuple-element.48.refs_3_), channel_id=1, source_target_pairs={{0,2},{2,0},{1,3},{3,1},{4,6},{6,4},{5,7},{7,5},{8,10},{10,8},{9,1... | collective-permute-start | bytes 798728 | tf_op jit(solution)/shard_map/ppermute | solution.py:39
  71.6 1.0 %collective-permute-start.22 = (f32[520,128]{1,0:T(8,128)S(1)}, f32[520,128]{1,0:T(8,128)S(1)}, u32[]{:S(2)}, u32[]{:S(2)}) collective-permute-start(f32[520,128]{1,0:T(8,128)S(1)} %get-tuple-element.49), channel_id=1, source_target_pairs={{0,6},{2,4},{4,2},{6,0},{8,14},{10,12},{12,10},{14,8},{16,22},{18,... | collective-permute-start | bytes 798728 | tf_op jit(solution)/shard_map/ppermute | solution.py:39
  72.5 0.3 collective-permute-start.20
  72.9 13.7 %all_to_all.11.refs_7_ = f32[32,8,128]{2,1,0:T(8,128)S(1)} all-to-all(f32[32,8,128]{2,1,0:T(8,128)S(1)} %get-tuple-element.50), channel_id=1, replica_groups=mesh['page'=8,'query'=2,'head'=2] {'page','query','head'}, dimensions={0} | all-to-all | bytes 262144 | tf_op jit(solution)/shard_map/all_to_all | solution.py:564
  86.6 1.2 %last_update.1 = (f32[4,256,128]{2,1,0:T(8,128)}, f32[4,256,128]{2,1,0:T(8,128)}, f32[4,256]{1,0:T(4,128)}) custom-call(f32[1040,128]{1,0:T(8,128)S(1)} %get-tuple-element.41.refs_0_.refs_2_, f32[1040,128]{1,0:T(8,128)S(1)} %collective-permute-done.12.refs_1_, f32[1040,128]{1,0:T(8,128)S(1)} %collective-permute-done.19.refs_2_, ...), custom_call_target="tpu_custom_call" | custom-call | flops 1048576 | bytes 1048576 | tf_op jit(solution)/shard_map/last_update/pallas_call | solution.py:67
  (25 shorter events, 0.1 us)
Async XLA Ops:
  0.6 2.7 %copy-start.6 = (s32[8]{0:T(128)S(1)}, s32[8]{0:T(128)}, u32[]{:S(2)}) copy-start(s32[8]{0:T(128)} %refs_3_.3) | copy-start | bytes 100
  0.6 2.7 %copy-start.4 = (f32[4,256]{1,0:T(4,128)S(1)}, f32[4,256]{1,0:T(4,128)}, u32[]{:S(2)}) copy-start(f32[4,256]{1,0:T(4,128)} %refs_2_.3) | copy-start | bytes 12292
  0.7 2.6 %copy-start.1 = (f32[4,256,128]{2,1,0:T(8,128)S(1)}, f32[4,256,128]{2,1,0:T(8,128)}, u32[]{:S(2)}) copy-start(f32[4,256,128]{2,1,0:T(8,128)} %refs_1_.3) | copy-start | bytes 1572868
  0.7 2.6 %copy-start = (f32[4,256,128]{2,1,0:T(8,128)S(1)}, f32[4,256,128]{2,1,0:T(8,128)}, u32[]{:S(2)}) copy-start(f32[4,256,128]{2,1,0:T(8,128)} %refs_0_.3) | copy-start | bytes 1572868
  0.7 2.6 %copy-start.5 = (s32[4,256]{1,0:T(4,128)S(1)}, s32[4,256]{1,0:T(4,128)}, u32[]{:S(2)}) copy-start(s32[4,256]{1,0:T(4,128)} %refs_5_.1) | copy-start | bytes 12292
  0.7 2.6 %copy-start.2 = (f32[4,256,128]{2,1,0:T(8,128)S(1)}, f32[4,256,128]{2,1,0:T(8,128)}, u32[]{:S(2)}) copy-start(f32[4,256,128]{2,1,0:T(8,128)} %refs_0_.2) | copy-start | bytes 1572868
  2.8 5.4 %collective-permute-start = (f32[1040,128]{1,0:T(8,128)}, f32[1040,128]{1,0:T(8,128)S(1)}, u32[]{:S(2)}, u32[]{:S(2)}) collective-permute-start(f32[1040,128]{1,0:T(8,128)} %pack.1), channel_id=1, source_target_pairs={{0,4},{4,0},{8,12},{12,8},{16,20},{20,16},{24,28},{28,24},{1,5},{5... | collective-permute-start | bytes 1597448 | tf_op jit(solution)/shard_map/ppermute | solution.py:39
  3.3 1.0 %copy-start.3 = (f32[4,256,128]{2,1,0:T(8,128)S(1)}, f32[4,256,128]{2,1,0:T(8,128)}, u32[]{:S(2)}) copy-start(f32[4,256,128]{2,1,0:T(8,128)} %refs_4_.1) | copy-start | bytes 1572868
  5.6 21.1 %collective-permute-start.1 = (f32[328,128]{1,0:T(8,128)S(1)}, f32[328,128]{1,0:T(8,128)S(1)}, u32[]{:S(2)}, u32[]{:S(2)}) collective-permute-start(f32[328,128]{1,0:T(8,128)S(1)} %get-tuple-element.29.refs_3_.refs_1_), channel_id=1, source_target_pairs={{0,2},{2,0},{1,3},{3,1},{4,6},{6,4},{5,7},{7,5},{8,10},{10,8},{9,1... | collective-permute-start | bytes 503816 | tf_op jit(solution)/shard_map/ppermute | solution.py:39
  9.8 6.5 %collective-permute-start.2 = (f32[136,128]{1,0:T(8,128)S(1)}, f32[136,128]{1,0:T(8,128)S(1)}, u32[]{:S(2)}, u32[]{:S(2)}) collective-permute-start(f32[136,128]{1,0:T(8,128)S(1)} %get-tuple-element.33), channel_id=1, source_target_pairs={{0,24},{4,28},{8,16},{12,20},{16,8},{20,12},{24,0},{28,4},{1,25},{... | collective-permute-start | bytes 208904 | tf_op jit(solution)/shard_map/ppermute | solution.py:39
  13.4 6.2 %collective-permute-start.3 = (f32[136,128]{1,0:T(8,128)S(1)}, f32[136,128]{1,0:T(8,128)S(1)}, u32[]{:S(2)}, u32[]{:S(2)}) collective-permute-start(f32[136,128]{1,0:T(8,128)S(1)} %get-tuple-element.34), channel_id=1, source_target_pairs={{0,16},{4,20},{8,24},{12,28},{16,0},{20,4},{24,8},{28,12},{1,17},{... | collective-permute-start | bytes 208904 | tf_op jit(solution)/shard_map/ppermute | solution.py:39
  13.4 6.2 %collective-permute-start.4 = (f32[136,128]{1,0:T(8,128)S(1)}, f32[136,128]{1,0:T(8,128)S(1)}, u32[]{:S(2)}, u32[]{:S(2)}) collective-permute-start(f32[136,128]{1,0:T(8,128)S(1)} %get-tuple-element.35), channel_id=1, source_target_pairs={{0,8},{4,12},{8,0},{12,4},{16,24},{20,28},{24,16},{28,20},{1,9},{5... | collective-permute-start | bytes 208904 | tf_op jit(solution)/shard_map/ppermute | solution.py:39
  19.8 7.0 %collective-permute-start.7 = (f32[72,128]{1,0:T(8,128)S(1)}, f32[72,128]{1,0:T(8,128)S(1)}, u32[]{:S(2)}, u32[]{:S(2)}) collective-permute-start(f32[72,128]{1,0:T(8,128)S(1)} %get-tuple-element.36.refs_6_), channel_id=1, source_target_pairs={{0,24},{4,28},{8,16},{12,20},{16,8},{20,12},{24,0},{28,4},{1,25},{... | collective-permute-start | bytes 110600 | tf_op jit(solution)/shard_map/ppermute | solution.py:39
  22.4 7.2 %collective-permute-start.6 = (f32[72,128]{1,0:T(8,128)S(1)}, f32[72,128]{1,0:T(8,128)S(1)}, u32[]{:S(2)}, u32[]{:S(2)}) collective-permute-start(f32[72,128]{1,0:T(8,128)S(1)} %get-tuple-element.36.refs_6_), channel_id=1, source_target_pairs={{0,16},{4,20},{8,24},{12,28},{16,0},{20,4},{24,8},{28,12},{1,17},{... | collective-permute-start | bytes 110600 | tf_op jit(solution)/shard_map/ppermute | solution.py:39
  22.5 9.3 %collective-permute-start.5 = (f32[72,128]{1,0:T(8,128)S(1)}, f32[72,128]{1,0:T(8,128)S(1)}, u32[]{:S(2)}, u32[]{:S(2)}) collective-permute-start(f32[72,128]{1,0:T(8,128)S(1)} %get-tuple-element.36.refs_6_), channel_id=1, source_target_pairs={{0,8},{4,12},{8,0},{12,4},{16,24},{20,28},{24,16},{28,20},{1,9},{5... | collective-permute-start | bytes 110600 | tf_op jit(solution)/shard_map/ppermute | solution.py:39
  24.3 7.5 %collective-permute-start.11 = (f32[72,128]{1,0:T(8,128)S(1)}, f32[72,128]{1,0:T(8,128)S(1)}, u32[]{:S(2)}, u32[]{:S(2)}) collective-permute-start(f32[72,128]{1,0:T(8,128)S(1)} %get-tuple-element.37), channel_id=1, source_target_pairs={{0,26},{2,24},{4,30},{6,28},{8,18},{10,16},{12,22},{14,20},{16,10}... | collective-permute-start | bytes 110600 | tf_op jit(solution)/shard_map/ppermute | solution.py:39
  26.7 5.8 %collective-permute-start.10 = (f32[72,128]{1,0:T(8,128)S(1)}, f32[72,128]{1,0:T(8,128)S(1)}, u32[]{:S(2)}, u32[]{:S(2)}) collective-permute-start(f32[72,128]{1,0:T(8,128)S(1)} %get-tuple-element.37), channel_id=1, source_target_pairs={{0,18},{2,16},{4,22},{6,20},{8,26},{10,24},{12,30},{14,28},{16,2},... | collective-permute-start | bytes 110600 | tf_op jit(solution)/shard_map/ppermute | solution.py:39
  26.9 5.6 %collective-permute-start.9 = (f32[72,128]{1,0:T(8,128)S(1)}, f32[72,128]{1,0:T(8,128)S(1)}, u32[]{:S(2)}, u32[]{:S(2)}) collective-permute-start(f32[72,128]{1,0:T(8,128)S(1)} %get-tuple-element.37), channel_id=1, source_target_pairs={{0,10},{2,8},{4,14},{6,12},{8,2},{10,0},{12,6},{14,4},{16,26},{18,... | collective-permute-start | bytes 110600 | tf_op jit(solution)/shard_map/ppermute | solution.py:39
  29.5 4.0 %collective-permute-start.8 = (f32[72,128]{1,0:T(8,128)S(1)}, f32[72,128]{1,0:T(8,128)S(1)}, u32[]{:S(2)}, u32[]{:S(2)}) collective-permute-start(f32[72,128]{1,0:T(8,128)S(1)} %get-tuple-element.37), channel_id=1, source_target_pairs={{0,2},{2,0},{1,3},{3,1},{4,6},{6,4},{5,7},{7,5},{8,10},{10,8},{9,1... | collective-permute-start | bytes 110600 | tf_op jit(solution)/shard_map/ppermute | solution.py:39
  50.1 18.3 %collective-permute-start.12 = (f32[1040,128]{1,0:T(8,128)S(1)}, f32[1040,128]{1,0:T(8,128)S(1)}, u32[]{:S(2)}, u32[]{:S(2)}) collective-permute-start(f32[1040,128]{1,0:T(8,128)S(1)} %get-tuple-element.41.refs_0_.refs_2_), channel_id=1, source_target_pairs={{0,2},{2,0},{1,3},{3,1},{4,6},{6,4},{5,7},{7,5},{8,10},{10,8},{9,1... | collective-permute-start | bytes 1597448 | tf_op jit(solution)/shard_map/ppermute | solution.py:39
  50.4 6.9 %collective-permute-start.13 = (f32[136,128]{1,0:T(8,128)S(1)}, f32[136,128]{1,0:T(8,128)S(1)}, u32[]{:S(2)}, u32[]{:S(2)}) collective-permute-start(f32[136,128]{1,0:T(8,128)S(1)} %get-tuple-element.43), channel_id=1, source_target_pairs={{0,24},{4,28},{8,16},{12,20},{16,8},{20,12},{24,0},{28,4},{1,25},{... | collective-permute-start | bytes 208904 | tf_op jit(solution)/shard_map/ppermute | solution.py:39
  51.8 7.5 %collective-permute-start.14 = (f32[136,128]{1,0:T(8,128)S(1)}, f32[136,128]{1,0:T(8,128)S(1)}, u32[]{:S(2)}, u32[]{:S(2)}) collective-permute-start(f32[136,128]{1,0:T(8,128)S(1)} %get-tuple-element.44), channel_id=1, source_target_pairs={{0,16},{4,20},{8,24},{12,28},{16,0},{20,4},{24,8},{28,12},{1,17},{... | collective-permute-start | bytes 208904 | tf_op jit(solution)/shard_map/ppermute | solution.py:39
  52.5 6.8 %collective-permute-start.15 = (f32[136,128]{1,0:T(8,128)S(1)}, f32[136,128]{1,0:T(8,128)S(1)}, u32[]{:S(2)}, u32[]{:S(2)}) collective-permute-start(f32[136,128]{1,0:T(8,128)S(1)} %get-tuple-element.45), channel_id=1, source_target_pairs={{0,8},{4,12},{8,0},{12,4},{16,24},{20,28},{24,16},{28,20},{1,9},{5... | collective-permute-start | bytes 208904 | tf_op jit(solution)/shard_map/ppermute | solution.py:39
  59.4 7.0 %collective-permute-start.18 = (f32[136,128]{1,0:T(8,128)S(1)}, f32[136,128]{1,0:T(8,128)S(1)}, u32[]{:S(2)}, u32[]{:S(2)}) collective-permute-start(f32[136,128]{1,0:T(8,128)S(1)} %merge.1.refs_5_), channel_id=1, source_target_pairs={{0,24},{4,28},{8,16},{12,20},{16,8},{20,12},{24,0},{28,4},{1,25},{... | collective-permute-start | bytes 208904 | tf_op jit(solution)/shard_map/ppermute | solution.py:39
  61.1 7.3 %collective-permute-start.17 = (f32[136,128]{1,0:T(8,128)S(1)}, f32[136,128]{1,0:T(8,128)S(1)}, u32[]{:S(2)}, u32[]{:S(2)}) collective-permute-start(f32[136,128]{1,0:T(8,128)S(1)} %merge.1.refs_5_), channel_id=1, source_target_pairs={{0,16},{4,20},{8,24},{12,28},{16,0},{20,4},{24,8},{28,12},{1,17},{... | collective-permute-start | bytes 208904 | tf_op jit(solution)/shard_map/ppermute | solution.py:39
  61.1 7.3 %collective-permute-start.16 = (f32[136,128]{1,0:T(8,128)S(1)}, f32[136,128]{1,0:T(8,128)S(1)}, u32[]{:S(2)}, u32[]{:S(2)}) collective-permute-start(f32[136,128]{1,0:T(8,128)S(1)} %merge.1.refs_5_), channel_id=1, source_target_pairs={{0,8},{4,12},{8,0},{12,4},{16,24},{20,28},{24,16},{28,20},{1,9},{5... | collective-permute-start | bytes 208904 | tf_op jit(solution)/shard_map/ppermute | solution.py:39
  68.4 18.1 %collective-permute-start.19 = (f32[1040,128]{1,0:T(8,128)S(1)}, f32[1040,128]{1,0:T(8,128)S(1)}, u32[]{:S(2)}, u32[]{:S(2)}) collective-permute-start(f32[1040,128]{1,0:T(8,128)S(1)} %mate_parts.1), channel_id=1, source_target_pairs={{0,4},{4,0},{8,12},{12,8},{16,20},{20,16},{24,28},{28,24},{1,5},{5... | collective-permute-start | bytes 1597448 | tf_op jit(solution)/shard_map/ppermute | solution.py:39
  70.6 15.9 %collective-permute-start.21 = (f32[520,128]{1,0:T(8,128)S(1)}, f32[520,128]{1,0:T(8,128)S(1)}, u32[]{:S(2)}, u32[]{:S(2)}) collective-permute-start(f32[520,128]{1,0:T(8,128)S(1)} %get-tuple-element.48.refs_3_), channel_id=1, source_target_pairs={{0,2},{2,0},{1,3},{3,1},{4,6},{6,4},{5,7},{7,5},{8,10},{10,8},{9,1... | collective-permute-start | bytes 798728 | tf_op jit(solution)/shard_map/ppermute | solution.py:39
  71.6 15.0 %collective-permute-start.22 = (f32[520,128]{1,0:T(8,128)S(1)}, f32[520,128]{1,0:T(8,128)S(1)}, u32[]{:S(2)}, u32[]{:S(2)}) collective-permute-start(f32[520,128]{1,0:T(8,128)S(1)} %get-tuple-element.49), channel_id=1, source_target_pairs={{0,6},{2,4},{4,2},{6,0},{8,14},{10,12},{12,10},{14,8},{16,22},{18,... | collective-permute-start | bytes 798728 | tf_op jit(solution)/shard_map/ppermute | solution.py:39
  72.5 14.0 %collective-permute-start.20 = (f32[520,128]{1,0:T(8,128)S(1)}, f32[520,128]{1,0:T(8,128)S(1)}, u32[]{:S(2)}, u32[]{:S(2)}) collective-permute-start(f32[520,128]{1,0:T(8,128)S(1)} %get-tuple-element.49), channel_id=1, source_target_pairs={{0,4},{4,0},{8,12},{12,8},{16,20},{20,16},{24,28},{28,24},{1,5},{5... | collective-permute-start | bytes 798728 | tf_op jit(solution)/shard_map/ppermute | solution.py:39

commit v8 on v6

--- a/solution.py
+++ b/solution.py
@@ -57,8 +57,10 @@
     return one_pass(left[0], right[0]) + cross
 
 
-def call(body, out_shapes, name, cost, operands, scratch=(), after=(), space=pltpu.VMEM, vmem=32):
+def call(body, out_shapes, name, cost, operands, scratch=(), after=(), space=pltpu.VMEM,
+         out_spaces=None, vmem=32):
     spaces = [space] * len(operands) + [pl.ANY] * len(after)
+    out_spaces = out_spaces or [pltpu.VMEM] * len(out_shapes)
     count = len(operands)
 
     def without_after(*refs):
@@ -68,7 +70,7 @@
         without_after,
         out_shape=[jax.ShapeDtypeStruct(shape, jnp.float32) for shape in out_shapes],
         in_specs=[pl.BlockSpec(memory_space=space) for space in spaces],
-        out_specs=[pl.BlockSpec(memory_space=pltpu.VMEM) for _ in out_shapes],
+        out_specs=[pl.BlockSpec(memory_space=out_space) for out_space in out_spaces],
         scratch_shapes=scratch,
         compiler_params=pltpu.CompilerParams(vmem_limit_bytes=vmem * 2**20),
         cost_estimate=pl.CostEstimate(flops=cost, bytes_accessed=2**20, transcendentals=0),
@@ -123,14 +125,14 @@
     slot_rows = compact_keys.shape[1]
     query_devices = lax.axis_size("query")
     head_devices = lax.axis_size("head")
-    ranks = lax.axis_size("page") // CORES
+    ranks = lax.axis_size("rank")
     query_rows = part_rows * query_devices
     chunk, piece = query_rows // ranks, part_rows // ranks
-    slot_total = local_heads * head_devices * slot_rows * lax.axis_size("page")
+    slot_total = local_heads * head_devices * slot_rows * ranks * CORES
     entry_total = slot_total * width
     score_scale = 1.0 / math.sqrt(width)
     slots = CORES * slot_rows
-    devices = ranks * CORES * query_devices * head_devices
+    groups = ranks * query_devices * head_devices
     pos_rows = part_rows // width
     bias_rows = slot_rows // width
     packed_rows = 2 * slot_rows + TAIL
@@ -138,8 +140,7 @@
     matmul_cost = 3 * 2 * slots * query_rows * width
 
     def places():
-        page = lax.axis_index("page")
-        return page // CORES, page % CORES, lax.axis_index("query")
+        return lax.axis_index("rank"), lax.axis_index("core"), lax.axis_index("query")
 
     def pack_queries(head, rank, queries, targets, out):
         rows = pl.ds(pl.multiple_of(rank * piece, piece), piece)
@@ -250,7 +251,7 @@
     query_parts = [own_queries] + [
         exchange(sent_queries[turn - 1], query=turn) for turn in range(1, query_devices)
     ]
-    states = [own_state, exchange(mate_state, page=1)]
+    states = [own_state, exchange(mate_state, core=1)]
 
     def in_columns(parts, axis):
         return jnp.concatenate(
@@ -404,9 +405,14 @@
             grad_outs[at][2 * slot_rows :, :] = grad_bias
             for which, grad in enumerate((grad_keys, grad_values, grad_bias)):
                 squares[which] = squares[which] + jnp.sum(grad * grad, axis=0, keepdims=True)
-        tile = jnp.concatenate(squares + [jnp.zeros((TAIL - 3, width), jnp.float32)], axis=0)
-        for at in range(devices):
-            squares_out[at] = tile
+        squares_out[...] = jnp.concatenate(
+            squares + [jnp.zeros((TAIL - 3, width), jnp.float32)], axis=0
+        )
+
+    def spread_body(own_ref, mate_ref, out_ref):
+        tile = own_ref[...] + mate_ref[...]
+        for at in range(groups):
+            out_ref[at] = tile
 
     def mate_body(*refs):
         *state_refs, out_ref = refs
@@ -418,7 +424,7 @@
     def to_output(packs, mask):
         if mask == (0, 0):
             return packs[0]
-        return exchange(packs[mask[1]], page=mask[1], query=mask[0])
+        return exchange(packs[mask[1]], core=mask[1], query=mask[0])
 
     for repeat in range(STEPS):
         last = repeat == STEPS - 1
@@ -442,7 +448,7 @@
             )
             states = [new_state]
         arrived = {
-            turn: exchange(chunk_parts[turn], page=CORES * turn)
+            turn: exchange(chunk_parts[turn], rank=turn)
             for turn in reversed(range(1, ranks))
         }
         if repeat:
@@ -457,7 +463,7 @@
             query_parts + chunk_parts[:1] + list(arrived.values()),
         )
         all_merged = [merged] + [
-            exchange(merged, page=CORES * turn) for turn in range(1, ranks)
+            exchange(merged, rank=turn) for turn in range(1, ranks)
         ]
         if repeat:
             (for_mate,) = call(
@@ -468,10 +474,10 @@
                 new_states,
                 after=all_merged[1:],
             )
-            from_mate = exchange(for_mate, page=1)
+            from_mate = exchange(for_mate, core=1)
         own_grad, mate_grad, squares = call(
             backward_body,
-            packed_shapes + [(devices, TAIL, width)],
+            packed_shapes + [(TAIL, width)],
             "backward",
             3 * matmul_cost,
             [weights, maxima] + states + query_parts + all_merged,
@@ -480,9 +486,16 @@
         grads = [own_grad, mate_grad]
         if last:
             all_grads = [to_output(grads, mask) for mask in out_masks]
+        (shared,) = call(
+            spread_body,
+            [(groups, TAIL, width)],
+            "spread",
+            2**10,
+            [squares, exchange(squares, core=1)],
+        )
         tiles = [
             lax.all_to_all(
-                squares, ("page", "query", "head"), split_axis=0, concat_axis=0, tiled=True
+                shared, ("rank", "query", "head"), split_axis=0, concat_axis=0, tiled=True
             )
         ]
 
@@ -493,16 +506,28 @@
             for turn, flip in out_masks
         ]
         grad_refs, refs = refs[:local_heads], refs[local_heads:]
-        tile_refs, (keys_out, values_out, bias_out) = refs[: len(tiles)], refs[len(tiles) :]
+        tile_refs, refs = refs[: len(tiles)], refs[len(tiles) :]
+        keys_out, values_out, bias_out, new_keys, new_values, sems = refs
         _, core, me = places()
         sizes = step_sizes(tile_refs)
+        copies = []
         for at, (turn, flip) in enumerate(out_masks):
             keys, values, bias = updated(state_refs[at], grad_refs[at], sizes)
             head = CORES * (me ^ turn) + (core ^ flip)
-            keys_out[head] = keys
-            values_out[head] = values
+            new_keys[at] = keys
+            new_values[at] = values
+            copies += start_all(
+                [
+                    (new_keys.at[at], keys_out.at[head]),
+                    (new_values.at[at], values_out.at[head]),
+                ],
+                sems,
+                len(copies),
+            )
             bias_row = jnp.concatenate([bias[row : row + 1] for row in range(bias_rows)], axis=1)
             bias_out[pl.ds(head, 1), :] = bias_row
+        for copy in copies:
+            copy.wait()
 
     return tuple(
         call(
@@ -511,6 +536,12 @@
             "last_update",
             2**20,
             new_states + [from_mate] + all_grads + tiles,
+            [
+                pltpu.VMEM(compact_keys.shape, jnp.float32),
+                pltpu.VMEM(compact_values.shape, jnp.float32),
+                pltpu.SemaphoreType.DMA((2 * local_heads,)),
+            ],
+            out_spaces=[pl.ANY, pl.ANY, pltpu.VMEM],
         )
     )
 
@@ -639,23 +670,30 @@
 
 
 def solution(mesh):
-    placed = (
-        P("head", "query", None),
-        P("head", "page", None),
-        P("head", "page", None),
-        P("head", "page"),
-        P("head", "query", None),
-        P("head", "query"),
-        P(),
-    )
+    sizes = [mesh.shape[axis] for axis in ("page", "query", "head")]
+    if sizes[0] % CORES == 0:
+        split = [sizes[0] // CORES, CORES] + sizes[1:]
+        split_mesh = jax.sharding.Mesh(
+            mesh.devices.reshape(split), ("rank", "core", "query", "head")
+        )
 
     def program(*args):
-        plan = direct_per_device if direct_plan_fits(mesh, args[0], args[1]) else per_device
+        direct = direct_plan_fits(mesh, args[0], args[1])
+        page = ("rank", "core") if direct else "page"
+        placed = (
+            P("head", "query", None),
+            P("head", page, None),
+            P("head", page, None),
+            P("head", page),
+            P("head", "query", None),
+            P("head", "query"),
+            P(),
+        )
         return jax.shard_map(
-            plan,
-            mesh=mesh,
+            direct_per_device if direct else per_device,
+            mesh=split_mesh if direct else mesh,
             in_specs=placed,
-            out_specs=(P("head", "page", None), P("head", "page", None), P("head", "page")),
+            out_specs=(P("head", page, None), P("head", page, None), P("head", page)),
             check_vma=False,
         )(*args)
 

time: 84.4 us -> 84 us (level)
  blocking collectives: 25.5 us -> 23.7 us
    all_to_all x2, blocking collectives: 25.5 us -> 23.7 us  [direct_per_device(): lax.all_to_all(shared, ('rank', 'query', 'head'), split_axis=0, concat_ax...]
    ppermute x19 -> x21, starting transfers between devices: 23.6 us -> 24.2 us  [exchange(): return lax.ppermute(value, axes, pairs)]
    pallas_call x10 -> x12, Pallas kernels: 10.9 us -> 11.5 us  [call(): pl.pallas_call(without_after, out_shape=[jax.ShapeDtypeStruct(shape, jnp....]
    ppermute x19 -> x21, waiting for transfers between devices: 23.4 us -> 23.5 us  [exchange(): return lax.ppermute(value, axes, pairs)]
  transfers between devices with their start and end apart: 19 -> 21, of which waited for: 9 -> 11; matrix products, arithmetic and copies ran while one was open for 0% -> 0% of each run, Pallas kernels for 3% -> 3%
where the time goes in v8:
time: 84 us; the launch traced here: 83.8 us
  starting transfers between devices  24.2 us (29%)
  blocking collectives  23.7 us (28%)
  waiting for transfers between devices  23.5 us (28%)
  Pallas kernels  11.5 us (14%)
    ppermute x21, starting transfers between devices, exchange(): return lax.ppermute(value, axes, pairs)  24.2 us
    all_to_all x2, blocking collectives, direct_per_device(): lax.all_to_all(shared, ('rank', 'query', 'head'), split_axis=0, concat_ax...  23.7 us
    ppermute x21, waiting for transfers between devices, exchange(): return lax.ppermute(value, axes, pairs)  23.5 us
    pallas_call x12, Pallas kernels, call(): pl.pallas_call(without_after, out_shape=[jax.ShapeDtypeStruct(shape, jnp....  11.5 us
  transfers between devices with their start and end apart: 21, of which 11 were waited for; matrix products, arithmetic and copies ran while one was open for 0% of the time, Pallas kernels for 3%

profile of v8, /device:TPU:0, one launch (start us, length us, event | category | flops | bytes accessed | tf_op | source)
XLA Modules:
  0.0 83.8 jit_solution(11161445031717707750)
XLA Ops:
  0.7 2.0 %pack.1 = (f32[520,128]{1,0:T(8,128)}, f32[328,128]{1,0:T(8,128)}) custom-call(f32[4,256,128]{2,1,0:T(8,128)} %refs_0_.3, f32[4,256,128]{2,1,0:T(8,128)} %refs_1_.3, f32[4,256,128]{2,1,0:T(8,128)} %refs_2_.3, f32[4,256]{1,0:T(4,128)} %refs_3_.3, f32[4,256,128]{2,1,0:T(8,128)} %refs_4_.3, s32[4,256]{1,0:T(4,128)} %refs_5_.3, s32[8]{0:T(128)} %refs_6_.3), custom_call_target="tpu_custom_call" | custom-call | flops 1048576 | bytes 1048576 | tf_op jit(solution)/shard_map/pack/pallas_call | solution.py:69
  2.7 0.0 copy-start.6
  2.7 0.5 collective-permute-start
  3.3 2.6 %collective-permute-start.1 = (f32[328,128]{1,0:T(8,128)}, f32[328,128]{1,0:T(8,128)S(1)}, u32[]{:S(2)}, u32[]{:S(2)}) collective-permute-start(f32[328,128]{1,0:T(8,128)} %get-tuple-element.29), channel_id=1, source_target_pairs={{0,2},{2,0},{1,3},{3,1},{4,6},{6,4},{5,7},{7,5},{8,10},{10,8},{9,1... | collective-permute-start | bytes 503816 | tf_op jit(solution)/shard_map/ppermute | solution.py:39
  5.9 0.7 own.1
  6.6 4.4 %collective-permute-done.1.refs_3_.refs_1_.refs_5_.refs_4_ = f32[328,128]{1,0:T(8,128)S(1)} collective-permute-done((f32[328,128]{1,0:T(8,128)}, f32[328,128]{1,0:T(8,128)S(1)}, u32[]{:S(2)}, u32[]{:S(2)}) %collective-permute-start.1) | collective-permute-done | bytes 167968 | tf_op jit(solution)/shard_map/ppermute | solution.py:39
  10.9 1.3 %forward.1 = (f32[136,128]{1,0:T(8,128)S(1)}, f32[136,128]{1,0:T(8,128)S(1)}, f32[136,128]{1,0:T(8,128)S(1)}, f32[136,128]{1,0:T(8,128)S(1)}, f32[512,512]{1,0:T(8,128)S(1)}, /*index=5*/f32[8,512]{1,0:T(8,128)S(1)}) custom-call(f32[520,128]{1,0:T(8,128)S(1)} %get-tuple-element.26.refs_0_.refs_2_, f32[520,128]{1,0:T(8,128)S(1)} %collective-permute-done.refs_1_.refs_3_, ...), custom_call_target="tpu_custom_call" | custom-call | flops 402653184 | bytes 1048576 | tf_op jit(solution)/shard_map/forward/pallas_call | solution.py:69
  12.2 3.9 %collective-permute-start.2 = (f32[136,128]{1,0:T(8,128)S(1)}, f32[136,128]{1,0:T(8,128)S(1)}, u32[]{:S(2)}, u32[]{:S(2)}) collective-permute-start(f32[136,128]{1,0:T(8,128)S(1)} %get-tuple-element.33), channel_id=1, source_target_pairs={{0,24},{8,16},{16,8},{24,0},{1,25},{9,17},{17,9},{25,1},{2,26},{10... | collective-permute-start | bytes 208904 | tf_op jit(solution)/shard_map/ppermute | solution.py:39
  16.1 0.0 collective-permute-start.3
  16.1 0.6 collective-permute-start.4
  16.8 2.1 %collective-permute-done.2.refs_3_ = f32[136,128]{1,0:T(8,128)S(1)} collective-permute-done((f32[136,128]{1,0:T(8,128)S(1)}, f32[136,128]{1,0:T(8,128)S(1)}, u32[]{:S(2)}, u32[]{:S(2)}) %collective-permute-start.2) | collective-permute-done | bytes 69664 | tf_op jit(solution)/shard_map/ppermute | solution.py:39
  18.9 3.0 %collective-permute-done.3.refs_4_ = f32[136,128]{1,0:T(8,128)S(1)} collective-permute-done((f32[136,128]{1,0:T(8,128)S(1)}, f32[136,128]{1,0:T(8,128)S(1)}, u32[]{:S(2)}, u32[]{:S(2)}) %collective-permute-start.3) | collective-permute-done | bytes 69664 | tf_op jit(solution)/shard_map/ppermute | solution.py:39
  21.9 0.0 collective-permute-done.4.refs_5_
  21.9 0.1 merge.2.refs_6_
  22.0 2.8 %collective-permute-start.7 = (f32[136,128]{1,0:T(8,128)S(1)}, f32[136,128]{1,0:T(8,128)S(1)}, u32[]{:S(2)}, u32[]{:S(2)}) collective-permute-start(f32[136,128]{1,0:T(8,128)S(1)} %merge.2.refs_6_), channel_id=1, source_target_pairs={{0,24},{8,16},{16,8},{24,0},{1,25},{9,17},{17,9},{25,1},{2,26},{10... | collective-permute-start | bytes 208904 | tf_op jit(solution)/shard_map/ppermute | solution.py:39
  24.8 1.7 %collective-permute-start.5 = (f32[136,128]{1,0:T(8,128)S(1)}, f32[136,128]{1,0:T(8,128)S(1)}, u32[]{:S(2)}, u32[]{:S(2)}) collective-permute-start(f32[136,128]{1,0:T(8,128)S(1)} %merge.2.refs_6_), channel_id=1, source_target_pairs={{0,8},{8,0},{16,24},{24,16},{1,9},{9,1},{17,25},{25,17},{2,10},{10... | collective-permute-start | bytes 208904 | tf_op jit(solution)/shard_map/ppermute | solution.py:39
  26.4 2.5 %collective-permute-done.7.refs_9_ = f32[136,128]{1,0:T(8,128)S(1)} collective-permute-done((f32[136,128]{1,0:T(8,128)S(1)}, f32[136,128]{1,0:T(8,128)S(1)}, u32[]{:S(2)}, u32[]{:S(2)}) %collective-permute-start.7) | collective-permute-done | bytes 69664 | tf_op jit(solution)/shard_map/ppermute | solution.py:39
  28.9 2.4 %collective-permute-done.6.refs_8_ = f32[136,128]{1,0:T(8,128)S(1)} collective-permute-done((f32[136,128]{1,0:T(8,128)S(1)}, f32[136,128]{1,0:T(8,128)S(1)}, u32[]{:S(2)}, u32[]{:S(2)}) %collective-permute-start.6) | collective-permute-done | bytes 69664 | tf_op jit(solution)/shard_map/ppermute | solution.py:39
  31.3 2.1 %backward.2 = (f32[520,128]{1,0:T(8,128)S(1)}, f32[520,128]{1,0:T(8,128)S(1)}, f32[8,128]{1,0:T(8,128)S(1)}) custom-call(f32[512,512]{1,0:T(8,128)S(1)} %get-tuple-element.30.refs_0_, f32[8,512]{1,0:T(8,128)S(1)} %get-tuple-element.31.refs_1_, f32[520,128]{1,0:T(8,128)S(1)} %get-tuple-element.26.refs_0_.refs_2_, ...), custom_call_target="tpu_custom_call" | custom-call | flops 603979776 | bytes 1048576 | tf_op jit(solution)/shard_map/backward/pallas_call | solution.py:69
  33.4 0.1 collective-permute-start.8
  33.5 1.2 %collective-permute-done.8.refs_1_ = f32[8,128]{1,0:T(8,128)S(1)} collective-permute-done((f32[8,128]{1,0:T(8,128)S(1)}, f32[8,128]{1,0:T(8,128)S(1)}, u32[]{:S(2)}, u32[]{:S(2)}) %collective-permute-start.8) | collective-permute-done | bytes 4128 | tf_op jit(solution)/shard_map/ppermute | solution.py:39
  34.7 11.9 %all_to_all.10.refs_6_ = f32[16,8,128]{2,1,0:T(8,128)S(1)} all-to-all(f32[16,8,128]{2,1,0:T(8,128)S(1)} %spread.2), channel_id=1, replica_groups=mesh['rank'=4,'core'=2,'query'=2,'head'=2] {'rank','query','head'}, dimensions={0} | all-to-all | bytes 131072 | tf_op jit(solution)/shard_map/all_to_all | solution.py:497
  46.6 1.3 %update_forward.1 = (f32[1040,128]{1,0:T(8,128)S(1)}, f32[136,128]{1,0:T(8,128)S(1)}, f32[136,128]{1,0:T(8,128)S(1)}, f32[136,128]{1,0:T(8,128)S(1)}, f32[136,12...) custom-call(f32[520,128]{1,0:T(8,128)S(1)} %get-tuple-element.26.refs_0_.refs_2_, ...), custom_call_target="tpu_custom_call" | custom-call | flops 402653184 | bytes 1048576 | tf_op jit(solution)/shard_map/update_forward/pallas_call | solution.py:69
  47.9 0.7 collective-permute-start.9
  48.6 0.9 %collective-permute-start.10 = (f32[136,128]{1,0:T(8,128)S(1)}, f32[136,128]{1,0:T(8,128)S(1)}, u32[]{:S(2)}, u32[]{:S(2)}) collective-permute-start(f32[136,128]{1,0:T(8,128)S(1)} %get-tuple-element.41), channel_id=1, source_target_pairs={{0,24},{8,16},{16,8},{24,0},{1,25},{9,17},{17,9},{25,1},{2,26},{10... | collective-permute-start | bytes 208904 | tf_op jit(solution)/shard_map/ppermute | solution.py:39
  49.5 1.2 %collective-permute-start.11 = (f32[136,128]{1,0:T(8,128)S(1)}, f32[136,128]{1,0:T(8,128)S(1)}, u32[]{:S(2)}, u32[]{:S(2)}) collective-permute-start(f32[136,128]{1,0:T(8,128)S(1)} %get-tuple-element.42), channel_id=1, source_target_pairs={{0,16},{8,24},{16,0},{24,8},{1,17},{9,25},{17,1},{25,9},{2,18},{10... | collective-permute-start | bytes 208904 | tf_op jit(solution)/shard_map/ppermute | solution.py:39
  50.7 2.3 %collective-permute-start.12 = (f32[136,128]{1,0:T(8,128)S(1)}, f32[136,128]{1,0:T(8,128)S(1)}, u32[]{:S(2)}, u32[]{:S(2)}) collective-permute-start(f32[136,128]{1,0:T(8,128)S(1)} %get-tuple-element.43), channel_id=1, source_target_pairs={{0,8},{8,0},{16,24},{24,16},{1,9},{9,1},{17,25},{25,17},{2,10},{10... | collective-permute-start | bytes 208904 | tf_op jit(solution)/shard_map/ppermute | solution.py:39
  53.0 1.8 %collective-permute-done.10.refs_3_ = f32[136,128]{1,0:T(8,128)S(1)} collective-permute-done((f32[136,128]{1,0:T(8,128)S(1)}, f32[136,128]{1,0:T(8,128)S(1)}, u32[]{:S(2)}, u32[]{:S(2)}) %collective-permute-start.10) | collective-permute-done | bytes 69664 | tf_op jit(solution)/shard_map/ppermute | solution.py:39
  54.8 1.6 %collective-permute-done.11.refs_4_ = f32[136,128]{1,0:T(8,128)S(1)} collective-permute-done((f32[136,128]{1,0:T(8,128)S(1)}, f32[136,128]{1,0:T(8,128)S(1)}, u32[]{:S(2)}, u32[]{:S(2)}) %collective-permute-start.11) | collective-permute-done | bytes 69664 | tf_op jit(solution)/shard_map/ppermute | solution.py:39
  56.4 0.0 collective-permute-done.12.refs_5_
  56.4 0.1 merge.3.refs_5_
  56.5 1.6 %collective-permute-start.15 = (f32[136,128]{1,0:T(8,128)S(1)}, f32[136,128]{1,0:T(8,128)S(1)}, u32[]{:S(2)}, u32[]{:S(2)}) collective-permute-start(f32[136,128]{1,0:T(8,128)S(1)} %merge.3.refs_5_), channel_id=1, source_target_pairs={{0,24},{8,16},{16,8},{24,0},{1,25},{9,17},{17,9},{25,1},{2,26},{10... | collective-permute-start | bytes 208904 | tf_op jit(solution)/shard_map/ppermute | solution.py:39
  58.2 0.8 collective-permute-start.14
  58.9 2.0 %collective-permute-start.13 = (f32[136,128]{1,0:T(8,128)S(1)}, f32[136,128]{1,0:T(8,128)S(1)}, u32[]{:S(2)}, u32[]{:S(2)}) collective-permute-start(f32[136,128]{1,0:T(8,128)S(1)} %merge.3.refs_5_), channel_id=1, source_target_pairs={{0,8},{8,0},{16,24},{24,16},{1,9},{9,1},{17,25},{25,17},{2,10},{10... | collective-permute-start | bytes 208904 | tf_op jit(solution)/shard_map/ppermute | solution.py:39
  61.0 2.5 %collective-permute-done.15.refs_4_.refs_8_ = f32[136,128]{1,0:T(8,128)S(1)} collective-permute-done((f32[136,128]{1,0:T(8,128)S(1)}, f32[136,128]{1,0:T(8,128)S(1)}, u32[]{:S(2)}, u32[]{:S(2)}) %collective-permute-start.15) | collective-permute-done | bytes 69664 | tf_op jit(solution)/shard_map/ppermute | solution.py:39
  63.5 1.0 %collective-permute-done.14.refs_3_.refs_7_ = f32[136,128]{1,0:T(8,128)S(1)} collective-permute-done((f32[136,128]{1,0:T(8,128)S(1)}, f32[136,128]{1,0:T(8,128)S(1)}, u32[]{:S(2)}, u32[]{:S(2)}) %collective-permute-start.14) | collective-permute-done | bytes 69664 | tf_op jit(solution)/shard_map/ppermute | solution.py:39
  64.5 0.0 collective-permute-done.13.refs_2_.refs_6_
  64.5 0.0 collective-permute-done.9.refs_1_
  64.6 0.1 collective-permute-start.16
  64.6 2.1 %backward.3 = (f32[520,128]{1,0:T(8,128)S(1)}, f32[520,128]{1,0:T(8,128)S(1)}, f32[8,128]{1,0:T(8,128)S(1)}) custom-call(f32[512,512]{1,0:T(8,128)S(1)} %get-tuple-element.44.refs_0_, f32[8,512]{1,0:T(8,128)S(1)} %get-tuple-element.45.refs_1_, f32[1040,128]{1,0:T(8,128)S(1)} %get-tuple-element.39.refs_0_.refs_2_, ...), custom_call_target="tpu_custom_call" | custom-call | flops 603979776 | bytes 1048576 | tf_op jit(solution)/shard_map/backward/pallas_call | solution.py:69
  66.7 1.2 %collective-permute-start.18 = (f32[520,128]{1,0:T(8,128)S(1)}, f32[520,128]{1,0:T(8,128)S(1)}, u32[]{:S(2)}, u32[]{:S(2)}) collective-permute-start(f32[520,128]{1,0:T(8,128)S(1)} %get-tuple-element.46.refs_3_), channel_id=1, source_target_pairs={{0,2},{2,0},{4,6},{6,4},{1,3},{3,1},{5,7},{7,5},{8,10},{10,8},{12,... | collective-permute-start | bytes 798728 | tf_op jit(solution)/shard_map/ppermute | solution.py:39
  67.9 0.7 collective-permute-start.19
  68.7 0.3 collective-permute-start.17
  69.0 0.2 collective-permute-start.20
  69.2 1.0 %collective-permute-done.20.refs_1_ = f32[8,128]{1,0:T(8,128)S(1)} collective-permute-done((f32[8,128]{1,0:T(8,128)S(1)}, f32[8,128]{1,0:T(8,128)S(1)}, u32[]{:S(2)}, u32[]{:S(2)}) %collective-permute-start.20) | collective-permute-done | bytes 4128 | tf_op jit(solution)/shard_map/ppermute | solution.py:39
  70.2 11.8 %all_to_all.11.refs_7_ = f32[16,8,128]{2,1,0:T(8,128)S(1)} all-to-all(f32[16,8,128]{2,1,0:T(8,128)S(1)} %spread.3), channel_id=1, replica_groups=mesh['rank'=4,'core'=2,'query'=2,'head'=2] {'rank','query','head'}, dimensions={0} | all-to-all | bytes 131072 | tf_op jit(solution)/shard_map/all_to_all | solution.py:497
  82.0 0.0 collective-permute-done.16.refs_2_
  82.0 1.7 %last_update.1 = (f32[4,256,128]{2,1,0:T(8,128)}, f32[4,256,128]{2,1,0:T(8,128)}, f32[4,256]{1,0:T(4,128)}) custom-call(f32[1040,128]{1,0:T(8,128)S(1)} %get-tuple-element.39.refs_0_.refs_2_, f32[1040,128]{1,0:T(8,128)S(1)} %collective-permute-done.9.refs_1_, f32[1040,128]{1,0:T(8,128)S(1)} %collective-permute-done.16.refs_2_, ...), custom_call_target="tpu_custom_call" | custom-call | flops 1048576 | bytes 1048576 | tf_op jit(solution)/shard_map/last_update/pallas_call | solution.py:69
  (22 shorter events, 0.1 us)
Async XLA Ops:
  0.6 5.2 %copy-start.3 = (f32[4,256,128]{2,1,0:T(8,128)S(1)}, f32[4,256,128]{2,1,0:T(8,128)}, u32[]{:S(2)}) copy-start(f32[4,256,128]{2,1,0:T(8,128)} %refs_4_.3) | copy-start | bytes 1572868
  0.6 5.2 %copy-start.2 = (f32[4,256,128]{2,1,0:T(8,128)S(1)}, f32[4,256,128]{2,1,0:T(8,128)}, u32[]{:S(2)}) copy-start(f32[4,256,128]{2,1,0:T(8,128)} %refs_2_.3) | copy-start | bytes 1572868
  0.7 5.2 %copy-start.1 = (f32[4,256,128]{2,1,0:T(8,128)S(1)}, f32[4,256,128]{2,1,0:T(8,128)}, u32[]{:S(2)}) copy-start(f32[4,256,128]{2,1,0:T(8,128)} %refs_1_.3) | copy-start | bytes 1572868
  0.7 5.2 %copy-start = (f32[4,256,128]{2,1,0:T(8,128)S(1)}, f32[4,256,128]{2,1,0:T(8,128)}, u32[]{:S(2)}) copy-start(f32[4,256,128]{2,1,0:T(8,128)} %refs_0_.3) | copy-start | bytes 1572868
  0.7 5.2 %copy-start.4 = (f32[4,256]{1,0:T(4,128)S(1)}, f32[4,256]{1,0:T(4,128)}, u32[]{:S(2)}) copy-start(f32[4,256]{1,0:T(4,128)} %refs_3_.3) | copy-start | bytes 12292
  0.7 5.2 %copy-start.5 = (s32[4,256]{1,0:T(4,128)S(1)}, s32[4,256]{1,0:T(4,128)}, u32[]{:S(2)}) copy-start(s32[4,256]{1,0:T(4,128)} %refs_5_.3) | copy-start | bytes 12292
  2.7 3.2 %copy-start.6 = (s32[8]{0:T(128)S(1)}, s32[8]{0:T(128)}, u32[]{:S(2)}) copy-start(s32[8]{0:T(128)} %refs_6_.3) | copy-start | bytes 100
  2.7 8.2 %collective-permute-start = (f32[520,128]{1,0:T(8,128)}, f32[520,128]{1,0:T(8,128)S(1)}, u32[]{:S(2)}, u32[]{:S(2)}) collective-permute-start(f32[520,128]{1,0:T(8,128)} %get-tuple-element.27), channel_id=1, source_target_pairs={{0,4},{4,0},{1,5},{5,1},{2,6},{6,2},{3,7},{7,3},{8,12},{12,8},{9,1... | collective-permute-start | bytes 798728 | tf_op jit(solution)/shard_map/ppermute | solution.py:39
  3.3 7.7 %collective-permute-start.1 = (f32[328,128]{1,0:T(8,128)}, f32[328,128]{1,0:T(8,128)S(1)}, u32[]{:S(2)}, u32[]{:S(2)}) collective-permute-start(f32[328,128]{1,0:T(8,128)} %get-tuple-element.29), channel_id=1, source_target_pairs={{0,2},{2,0},{1,3},{3,1},{4,6},{6,4},{5,7},{7,5},{8,10},{10,8},{9,1... | collective-permute-start | bytes 503816 | tf_op jit(solution)/shard_map/ppermute | solution.py:39
  12.2 6.7 %collective-permute-start.2 = (f32[136,128]{1,0:T(8,128)S(1)}, f32[136,128]{1,0:T(8,128)S(1)}, u32[]{:S(2)}, u32[]{:S(2)}) collective-permute-start(f32[136,128]{1,0:T(8,128)S(1)} %get-tuple-element.33), channel_id=1, source_target_pairs={{0,24},{8,16},{16,8},{24,0},{1,25},{9,17},{17,9},{25,1},{2,26},{10... | collective-permute-start | bytes 208904 | tf_op jit(solution)/shard_map/ppermute | solution.py:39
  16.1 5.7 %collective-permute-start.3 = (f32[136,128]{1,0:T(8,128)S(1)}, f32[136,128]{1,0:T(8,128)S(1)}, u32[]{:S(2)}, u32[]{:S(2)}) collective-permute-start(f32[136,128]{1,0:T(8,128)S(1)} %get-tuple-element.34), channel_id=1, source_target_pairs={{0,16},{8,24},{16,0},{24,8},{1,17},{9,25},{17,1},{25,9},{2,18},{10... | collective-permute-start | bytes 208904 | tf_op jit(solution)/shard_map/ppermute | solution.py:39
  16.1 5.7 %collective-permute-start.4 = (f32[136,128]{1,0:T(8,128)S(1)}, f32[136,128]{1,0:T(8,128)S(1)}, u32[]{:S(2)}, u32[]{:S(2)}) collective-permute-start(f32[136,128]{1,0:T(8,128)S(1)} %get-tuple-element.35), channel_id=1, source_target_pairs={{0,8},{8,0},{16,24},{24,16},{1,9},{9,1},{17,25},{25,17},{2,10},{10... | collective-permute-start | bytes 208904 | tf_op jit(solution)/shard_map/ppermute | solution.py:39
  22.0 7.0 %collective-permute-start.7 = (f32[136,128]{1,0:T(8,128)S(1)}, f32[136,128]{1,0:T(8,128)S(1)}, u32[]{:S(2)}, u32[]{:S(2)}) collective-permute-start(f32[136,128]{1,0:T(8,128)S(1)} %merge.2.refs_6_), channel_id=1, source_target_pairs={{0,24},{8,16},{16,8},{24,0},{1,25},{9,17},{17,9},{25,1},{2,26},{10... | collective-permute-start | bytes 208904 | tf_op jit(solution)/shard_map/ppermute | solution.py:39
  24.8 6.5 %collective-permute-start.6 = (f32[136,128]{1,0:T(8,128)S(1)}, f32[136,128]{1,0:T(8,128)S(1)}, u32[]{:S(2)}, u32[]{:S(2)}) collective-permute-start(f32[136,128]{1,0:T(8,128)S(1)} %merge.2.refs_6_), channel_id=1, source_target_pairs={{0,16},{8,24},{16,0},{24,8},{1,17},{9,25},{17,1},{25,9},{2,18},{10... | collective-permute-start | bytes 208904 | tf_op jit(solution)/shard_map/ppermute | solution.py:39
  24.8 6.5 %collective-permute-start.5 = (f32[136,128]{1,0:T(8,128)S(1)}, f32[136,128]{1,0:T(8,128)S(1)}, u32[]{:S(2)}, u32[]{:S(2)}) collective-permute-start(f32[136,128]{1,0:T(8,128)S(1)} %merge.2.refs_6_), channel_id=1, source_target_pairs={{0,8},{8,0},{16,24},{24,16},{1,9},{9,1},{17,25},{25,17},{2,10},{10... | collective-permute-start | bytes 208904 | tf_op jit(solution)/shard_map/ppermute | solution.py:39
  33.4 1.2 %collective-permute-start.8 = (f32[8,128]{1,0:T(8,128)S(1)}, f32[8,128]{1,0:T(8,128)S(1)}, u32[]{:S(2)}, u32[]{:S(2)}) collective-permute-start(f32[8,128]{1,0:T(8,128)S(1)} %get-tuple-element.38.refs_0_), channel_id=1, source_target_pairs={{0,4},{4,0},{1,5},{5,1},{2,6},{6,2},{3,7},{7,3},{8,12},{12,8},{9,1... | collective-permute-start | bytes 12296 | tf_op jit(solution)/shard_map/ppermute | solution.py:39
  47.9 16.6 %collective-permute-start.9 = (f32[1040,128]{1,0:T(8,128)S(1)}, f32[1040,128]{1,0:T(8,128)S(1)}, u32[]{:S(2)}, u32[]{:S(2)}) collective-permute-start(f32[1040,128]{1,0:T(8,128)S(1)} %get-tuple-element.39.refs_0_.refs_2_), channel_id=1, source_target_pairs={{0,2},{2,0},{1,3},{3,1},{4,6},{6,4},{5,7},{7,5},{8,10},{10,8},{9,1... | collective-permute-start | bytes 1597448 | tf_op jit(solution)/shard_map/ppermute | solution.py:39
  48.6 6.2 %collective-permute-start.10 = (f32[136,128]{1,0:T(8,128)S(1)}, f32[136,128]{1,0:T(8,128)S(1)}, u32[]{:S(2)}, u32[]{:S(2)}) collective-permute-start(f32[136,128]{1,0:T(8,128)S(1)} %get-tuple-element.41), channel_id=1, source_target_pairs={{0,24},{8,16},{16,8},{24,0},{1,25},{9,17},{17,9},{25,1},{2,26},{10... | collective-permute-start | bytes 208904 | tf_op jit(solution)/shard_map/ppermute | solution.py:39
  49.5 6.9 %collective-permute-start.11 = (f32[136,128]{1,0:T(8,128)S(1)}, f32[136,128]{1,0:T(8,128)S(1)}, u32[]{:S(2)}, u32[]{:S(2)}) collective-permute-start(f32[136,128]{1,0:T(8,128)S(1)} %get-tuple-element.42), channel_id=1, source_target_pairs={{0,16},{8,24},{16,0},{24,8},{1,17},{9,25},{17,1},{25,9},{2,18},{10... | collective-permute-start | bytes 208904 | tf_op jit(solution)/shard_map/ppermute | solution.py:39
  50.7 5.7 %collective-permute-start.12 = (f32[136,128]{1,0:T(8,128)S(1)}, f32[136,128]{1,0:T(8,128)S(1)}, u32[]{:S(2)}, u32[]{:S(2)}) collective-permute-start(f32[136,128]{1,0:T(8,128)S(1)} %get-tuple-element.43), channel_id=1, source_target_pairs={{0,8},{8,0},{16,24},{24,16},{1,9},{9,1},{17,25},{25,17},{2,10},{10... | collective-permute-start | bytes 208904 | tf_op jit(solution)/shard_map/ppermute | solution.py:39
  56.5 7.0 %collective-permute-start.15 = (f32[136,128]{1,0:T(8,128)S(1)}, f32[136,128]{1,0:T(8,128)S(1)}, u32[]{:S(2)}, u32[]{:S(2)}) collective-permute-start(f32[136,128]{1,0:T(8,128)S(1)} %merge.3.refs_5_), channel_id=1, source_target_pairs={{0,24},{8,16},{16,8},{24,0},{1,25},{9,17},{17,9},{25,1},{2,26},{10... | collective-permute-start | bytes 208904 | tf_op jit(solution)/shard_map/ppermute | solution.py:39
  58.2 6.4 %collective-permute-start.14 = (f32[136,128]{1,0:T(8,128)S(1)}, f32[136,128]{1,0:T(8,128)S(1)}, u32[]{:S(2)}, u32[]{:S(2)}) collective-permute-start(f32[136,128]{1,0:T(8,128)S(1)} %merge.3.refs_5_), channel_id=1, source_target_pairs={{0,16},{8,24},{16,0},{24,8},{1,17},{9,25},{17,1},{25,9},{2,18},{10... | collective-permute-start | bytes 208904 | tf_op jit(solution)/shard_map/ppermute | solution.py:39
  58.9 5.6 %collective-permute-start.13 = (f32[136,128]{1,0:T(8,128)S(1)}, f32[136,128]{1,0:T(8,128)S(1)}, u32[]{:S(2)}, u32[]{:S(2)}) collective-permute-start(f32[136,128]{1,0:T(8,128)S(1)} %merge.3.refs_5_), channel_id=1, source_target_pairs={{0,8},{8,0},{16,24},{24,16},{1,9},{9,1},{17,25},{25,17},{2,10},{10... | collective-permute-start | bytes 208904 | tf_op jit(solution)/shard_map/ppermute | solution.py:39
  64.6 17.5 %collective-permute-start.16 = (f32[1040,128]{1,0:T(8,128)S(1)}, f32[1040,128]{1,0:T(8,128)S(1)}, u32[]{:S(2)}, u32[]{:S(2)}) collective-permute-start(f32[1040,128]{1,0:T(8,128)S(1)} %mate_parts.1), channel_id=1, source_target_pairs={{0,4},{4,0},{1,5},{5,1},{2,6},{6,2},{3,7},{7,3},{8,12},{12,8},{9,1... | collective-permute-start | bytes 1597448 | tf_op jit(solution)/shard_map/ppermute | solution.py:39
  66.7 15.3 %collective-permute-start.18 = (f32[520,128]{1,0:T(8,128)S(1)}, f32[520,128]{1,0:T(8,128)S(1)}, u32[]{:S(2)}, u32[]{:S(2)}) collective-permute-start(f32[520,128]{1,0:T(8,128)S(1)} %get-tuple-element.46.refs_3_), channel_id=1, source_target_pairs={{0,2},{2,0},{4,6},{6,4},{1,3},{3,1},{5,7},{7,5},{8,10},{10,8},{12,... | collective-permute-start | bytes 798728 | tf_op jit(solution)/shard_map/ppermute | solution.py:39
  67.9 14.1 %collective-permute-start.19 = (f32[520,128]{1,0:T(8,128)S(1)}, f32[520,128]{1,0:T(8,128)S(1)}, u32[]{:S(2)}, u32[]{:S(2)}) collective-permute-start(f32[520,128]{1,0:T(8,128)S(1)} %get-tuple-element.47), channel_id=1, source_target_pairs={{0,6},{2,4},{4,2},{6,0},{1,7},{3,5},{5,3},{7,1},{8,14},{10,12},{12... | collective-permute-start | bytes 798728 | tf_op jit(solution)/shard_map/ppermute | solution.py:39
  68.7 13.4 %collective-permute-start.17 = (f32[520,128]{1,0:T(8,128)S(1)}, f32[520,128]{1,0:T(8,128)S(1)}, u32[]{:S(2)}, u32[]{:S(2)}) collective-permute-start(f32[520,128]{1,0:T(8,128)S(1)} %get-tuple-element.47), channel_id=1, source_target_pairs={{0,4},{2,6},{4,0},{6,2},{1,5},{3,7},{5,1},{7,3},{8,12},{10,14},{12... | collective-permute-start | bytes 798728 | tf_op jit(solution)/shard_map/ppermute | solution.py:39
  69.0 1.2 %collective-permute-start.20 = (f32[8,128]{1,0:T(8,128)S(1)}, f32[8,128]{1,0:T(8,128)S(1)}, u32[]{:S(2)}, u32[]{:S(2)}) collective-permute-start(f32[8,128]{1,0:T(8,128)S(1)} %get-tuple-element.48.refs_0_), channel_id=1, source_target_pairs={{0,4},{4,0},{1,5},{5,1},{2,6},{6,2},{3,7},{7,3},{8,12},{12,8},{9,1... | collective-permute-start | bytes 12296 | tf_op jit(solution)/shard_map/ppermute | solution.py:39

commit v9 on v6

--- a/solution.py
+++ b/solution.py
@@ -141,6 +141,10 @@
         page = lax.axis_index("page")
         return page // CORES, page % CORES, lax.axis_index("query")
 
+    def to_device(value, **masks):
+        masks = {axis: mask for axis, mask in masks.items() if mask}
+        return exchange(value, **masks) if masks else value
+
     def pack_queries(head, rank, queries, targets, out):
         rows = pl.ds(pl.multiple_of(rank * piece, piece), piece)
         return [
@@ -247,9 +251,12 @@
         small_scratch + [pltpu.SemaphoreType.DMA((7,))],
         space=pl.ANY,
     )
-    query_parts = [own_queries] + [
-        exchange(sent_queries[turn - 1], query=turn) for turn in range(1, query_devices)
+    packs = [own_queries] + list(sent_queries)
+    query_parts_of = [
+        [to_device(packs[part], query=turn ^ part) for part in range(query_devices)]
+        for turn in range(query_devices)
     ]
+    query_parts = query_parts_of[0]
     states = [own_state, exchange(mate_state, page=1)]
 
     def in_columns(parts, axis):
@@ -288,14 +295,13 @@
             state_ref[value_end:, :] - sizes[2] * grad_ref[value_end:, :],
         )
 
-    def forward(state_refs, query_refs, chunk_outs, weights_out, max_out, chunks):
-        rank, _, _ = places()
+    def all_weights(state_refs, query_refs):
         all_queries = read_queries(query_refs)
         position_row = in_columns(
             [tail_as_row(ref, part_rows + piece, pos_rows) for ref in query_refs], 1
         )
         all_scores, all_visible = [], []
-        for at, ref in enumerate(state_refs):
+        for ref in state_refs:
             scores = dot(halves(ref[:slot_rows, :]), all_queries, 1, 1) * score_scale
             bias = row_as_column(tail_as_row(ref, 2 * slot_rows, bias_rows), width)
             scores = scores + jnp.concatenate([bias] * (query_rows // width), axis=1)
@@ -306,15 +312,27 @@
         row_max = jnp.max(all_scores[0], axis=0, keepdims=True)
         for scores in all_scores[1:]:
             row_max = jnp.maximum(row_max, jnp.max(scores, axis=0, keepdims=True))
+        weights = [
+            jnp.where(visible, jnp.exp(scores - row_max), 0.0)
+            for scores, visible in zip(all_scores, all_visible)
+        ]
+        return weights, row_max
+
+    def store_weights(weights, row_max, weights_out, max_out):
+        for at, part in enumerate(weights):
+            weights_out[at * slot_rows : (at + 1) * slot_rows, :] = part
+        max_out[...] = jnp.broadcast_to(row_max, (TAIL, query_rows))
+
+    def forward(state_refs, query_refs, chunk_outs, weights_out, max_out, chunks):
+        rank, _, _ = places()
+        weights, row_max = all_weights(state_refs, query_refs)
+        store_weights(weights, row_max, weights_out, max_out)
         row_total = jnp.zeros_like(row_max)
         row_sum = jnp.zeros((width, query_rows), jnp.float32)
-        for at, ref in enumerate(state_refs):
-            weights = jnp.where(all_visible[at], jnp.exp(all_scores[at] - row_max), 0.0)
-            weights_out[at * slot_rows : (at + 1) * slot_rows, :] = weights
-            row_total = row_total + jnp.sum(weights, axis=0, keepdims=True)
+        for ref, part in zip(state_refs, weights):
+            row_total = row_total + jnp.sum(part, axis=0, keepdims=True)
             values = halves(ref[slot_rows : 2 * slot_rows, :])
-            row_sum = row_sum + dot(values, halves(weights), 0, 0)
-        max_out[...] = jnp.broadcast_to(row_max, (TAIL, query_rows))
+            row_sum = row_sum + dot(values, halves(part), 0, 0)
         tail = jnp.concatenate(
             [row_max, row_total, jnp.zeros((TAIL - 2, query_rows), jnp.float32)], axis=0
         )
@@ -326,7 +344,8 @@
             chunk_outs[turn][...] = chunks[rank ^ turn]
 
     chunk_shape = (width + TAIL, chunk)
-    forward_shapes = [chunk_shape] * ranks + [(slots, query_rows), (TAIL, query_rows)]
+    weight_shapes = [(slots, query_rows), (TAIL, query_rows)]
+    forward_shapes = [chunk_shape] * ranks + weight_shapes
     chunk_scratch = [pltpu.VMEM((ranks,) + chunk_shape, jnp.float32)]
 
     def first_body(*refs):
@@ -373,40 +392,73 @@
             [row_max, row_total, row_delta, jnp.zeros((TAIL - 3, chunk), jnp.float32)], axis=0
         )
 
+    def join_chunks(merged_refs, chunks):
+        rank, _, _ = places()
+        for turn, ref in enumerate(merged_refs):
+            chunks[rank ^ turn] = ref[...]
+        return jnp.concatenate([chunks[at] for at in range(ranks)], axis=1)
+
+    def join_body(*refs):
+        *merged_refs, joined_out, chunks = refs
+        joined_out[...] = join_chunks(merged_refs, chunks)
+
+    def gradients_of(joined, max_ref, query_refs):
+        residual = halves(joined[:width, :])
+        row_max, row_total, row_delta = (
+            joined[width + at : width + at + 1, :] for at in range(3)
+        )
+        all_queries = read_queries(query_refs)
+        factor = jnp.exp(max_ref[0:1, :] - row_max) / row_total
+        ones = jnp.ones((TAIL, query_rows), jnp.bfloat16)
+        ones = (ones, jnp.zeros_like(ones))
+
+        def gradients(at, state_ref, weights_ref, out):
+            attention = weights_ref[at * slot_rows : (at + 1) * slot_rows, :] * factor
+            grad_values = dot(halves(attention), residual, 1, 1)
+            grad_probs = dot(halves(state_ref[slot_rows : 2 * slot_rows, :]), residual, 1, 0)
+            grad_scores = halves(attention * (grad_probs - row_delta))
+            grad_keys = dot(grad_scores, all_queries, 1, 0) * score_scale
+            grad_bias = row_as_tail(dot(ones, grad_scores, 1, 1)[0:1, :], width)
+            out[:slot_rows, :] = grad_keys
+            out[slot_rows : 2 * slot_rows, :] = grad_values
+            out[2 * slot_rows :, :] = grad_bias
+            return [
+                jnp.sum(grad * grad, axis=0, keepdims=True)
+                for grad in (grad_keys, grad_values, grad_bias)
+            ]
+
+        return gradients
+
     def backward_body(weights_ref, max_ref, *refs):
         state_refs, refs = parts_of(refs[: len(states)]), refs[len(states) :]
         query_refs, refs = refs[:query_devices], refs[query_devices:]
-        merged_refs, refs = refs[:ranks], refs[ranks:]
-        grad_outs, (squares_out, chunks) = refs[:2], refs[2:]
-        rank, _, _ = places()
-        for turn in range(ranks):
-            chunks[rank ^ turn] = merged_refs[turn][...]
-        joined = jnp.concatenate([chunks[at] for at in range(ranks)], axis=1)
-        residual = joined[:width, :]
-        row_max, row_total, row_delta = (
-            joined[width + at : width + at + 1, :] for at in range(3)
-        )
-        all_queries = read_queries(query_refs)
-        residual = halves(residual)
-        factor = jnp.exp(max_ref[0:1, :] - row_max) / row_total
-        ones = jnp.ones((TAIL, query_rows), jnp.bfloat16)
-        ones = (ones, jnp.zeros_like(ones))
-        squares = [jnp.zeros((1, width), jnp.float32)] * 3
-        for at, ref in enumerate(state_refs):
-            attention = weights_ref[at * slot_rows : (at + 1) * slot_rows, :] * factor
-            grad_values = dot(halves(attention), residual, 1, 1)
-            grad_probs = dot(halves(ref[slot_rows : 2 * slot_rows, :]), residual, 1, 0)
-            grad_scores = halves(attention * (grad_probs - row_delta))
-            grad_keys = dot(grad_scores, all_queries, 1, 0) * score_scale
-            grad_bias = row_as_tail(dot(ones, grad_scores, 1, 1)[0:1, :], width)
-            grad_outs[at][:slot_rows, :] = grad_keys
-            grad_outs[at][slot_rows : 2 * slot_rows, :] = grad_values
-            grad_outs[at][2 * slot_rows :, :] = grad_bias
-            for which, grad in enumerate((grad_keys, grad_values, grad_bias)):
-                squares[which] = squares[which] + jnp.sum(grad * grad, axis=0, keepdims=True)
-        tile = jnp.concatenate(squares + [jnp.zeros((TAIL - 3, width), jnp.float32)], axis=0)
+        merged_refs, refs = refs[: len(all_merged)], refs[len(all_merged) :]
+        grad_outs, (squares_out, *scratch) = refs[:2], refs[2:]
+        joined = join_chunks(merged_refs, *scratch) if scratch else merged_refs[0][...]
+        gradients = gradients_of(joined, max_ref, query_refs)
+        squares = [
+            gradients(at, ref, weights_ref, grad_outs[at]) for at, ref in enumerate(state_refs)
+        ]
+        tile = jnp.concatenate(
+            [sum(parts) for parts in zip(*squares)]
+            + [jnp.zeros((TAIL - 3, width), jnp.float32)],
+            axis=0,
+        )
         for at in range(devices):
             squares_out[at] = tile
+
+    def weights_body(state_ref, *refs):
+        query_refs, (weights_out, max_out) = refs[:query_devices], refs[query_devices:]
+        weights, row_max = all_weights(parts_of([state_ref]), query_refs)
+        store_weights(weights, row_max, weights_out, max_out)
+
+    def page_body(at):
+        def body(weights_ref, max_ref, state_ref, joined_ref, *refs):
+            query_refs, (grad_out,) = refs[:query_devices], refs[query_devices:]
+            gradients = gradients_of(joined_ref[...], max_ref, query_refs)
+            gradients(at, part_of(state_ref, at), weights_ref, grad_out)
+
+        return body
 
     def mate_body(*refs):
         *state_refs, out_ref = refs
@@ -414,11 +466,6 @@
             out_ref[pl.ds(at * packed_rows, packed_rows), :] = part_of(ref, 1)[...]
 
     out_masks = list(itertools.product(range(query_devices), range(CORES)))
-
-    def to_output(packs, mask):
-        if mask == (0, 0):
-            return packs[0]
-        return exchange(packs[mask[1]], page=mask[1], query=mask[0])
 
     for repeat in range(STEPS):
         last = repeat == STEPS - 1
@@ -459,32 +506,69 @@
         all_merged = [merged] + [
             exchange(merged, page=CORES * turn) for turn in range(1, ranks)
         ]
-        if repeat:
-            (for_mate,) = call(
-                mate_body,
-                [(query_devices * packed_rows, width)],
-                "mate_parts",
+        if last and repeat:
+            other_weights = [
+                call(
+                    weights_body,
+                    weight_shapes,
+                    "other_weights",
+                    matmul_cost,
+                    [new_states[turn]] + query_parts_of[turn],
+                )
+                for turn in range(1, query_devices)
+            ]
+            all_merged = call(
+                join_body,
+                [(width + TAIL, query_rows)],
+                "join",
                 2**20,
-                new_states,
-                after=all_merged[1:],
+                all_merged,
+                chunk_scratch,
+                after=[head_weights[1] for head_weights in other_weights],
             )
-            from_mate = exchange(for_mate, page=1)
+            all_joined = [
+                to_device(all_merged[0], query=turn) for turn in range(query_devices)
+            ]
         own_grad, mate_grad, squares = call(
             backward_body,
             packed_shapes + [(devices, TAIL, width)],
             "backward",
             3 * matmul_cost,
-            [weights, maxima] + states + query_parts + all_merged,
-            scratch=chunk_scratch,
+            [weights, maxima] + states + query_parts + list(all_merged),
+            scratch=() if last and repeat else chunk_scratch,
+            after=[part for parts in query_parts_of[1:] for part in parts],
         )
         grads = [own_grad, mate_grad]
-        if last:
-            all_grads = [to_output(grads, mask) for mask in out_masks]
         tiles = [
             lax.all_to_all(
                 squares, ("page", "query", "head"), split_axis=0, concat_axis=0, tiled=True
             )
         ]
+
+    all_grads = [own_grad, exchange(mate_grad, page=1)]
+    for turn in range(1, query_devices):
+        operands = list(other_weights[turn - 1]) + [new_states[turn], all_joined[turn]]
+        page_grads = [
+            call(
+                page_body(at),
+                [(packed_rows, width)],
+                "other_backward",
+                3 * matmul_cost // 2,
+                operands + query_parts_of[turn],
+                after=[squares],
+            )[0]
+            for at in reversed(range(CORES))
+        ]
+        all_grads += [page_grads[1], exchange(page_grads[0], page=1)]
+    (for_mate,) = call(
+        mate_body,
+        [(query_devices * packed_rows, width)],
+        "mate_parts",
+        2**20,
+        new_states,
+        after=all_joined[1:] + [squares],
+    )
+    from_mate = exchange(for_mate, page=1)
 
     def last_body(*refs):
         state_refs, (mate_ref, *refs) = refs[:query_devices], refs[query_devices:]

time: 84.4 us -> 91.8 us (1.088)
  blocking collectives: 25.5 us -> 12.6 us
  waiting for transfers between devices: 23.4 us -> 33.2 us
  Pallas kernels: 10.9 us -> 17.3 us
  starting transfers between devices: 23.6 us -> 26.7 us
  local copies, waits for them, and re-layouts: 0.03 us -> 0.99 us
    all_to_all x2 -> x1, blocking collectives: 25.5 us -> 12.6 us  [direct_per_device(): lax.all_to_all(squares, ('page', 'query', 'head'), split_axis=0, concat_a...]
    all_to_all x0 -> x1, waiting for transfers between devices: none -> 7.22 us  [direct_per_device(): lax.all_to_all(squares, ('page', 'query', 'head'), split_axis=0, concat_a...]
    pallas_call x10 -> x14, Pallas kernels: 10.9 us -> 17.3 us  [call(): pl.pallas_call(without_after, out_shape=[jax.ShapeDtypeStruct(shape, jnp....]
    all_to_all x0 -> x1, starting transfers between devices: none -> 3.29 us  [direct_per_device(): lax.all_to_all(squares, ('page', 'query', 'head'), split_axis=0, concat_a...]
    ppermute x19 -> x20, waiting for transfers between devices: 23.4 us -> 25.9 us  [exchange(): return lax.ppermute(value, axes, pairs)]
    unnamed x14 -> x20, local copies, waits for them, and re-layouts: 0.03 us -> 0.99 us
    ppermute x19 -> x20, starting transfers between devices: 23.6 us -> 23.4 us  [exchange(): return lax.ppermute(value, axes, pairs)]
  transfers between devices with their start and end apart: 19 -> 21, of which waited for: 9 -> 11; matrix products, arithmetic and copies ran while one was open for 0% -> 0% of each run, Pallas kernels for 3% -> 10%
where the time goes in v9:
time: 91.8 us; the launch traced here: 91.5 us
  waiting for transfers between devices  33.2 us (36%)
  starting transfers between devices  26.7 us (29%)
  Pallas kernels  17.3 us (19%)
  blocking collectives  12.6 us (14%)
  local copies, waits for them, and re-layouts  0.99 us (1%)
    ppermute x20, waiting for transfers between devices, exchange(): return lax.ppermute(value, axes, pairs)  25.9 us
    ppermute x20, starting transfers between devices, exchange(): return lax.ppermute(value, axes, pairs)  23.4 us
    pallas_call x14, Pallas kernels, call(): pl.pallas_call(without_after, out_shape=[jax.ShapeDtypeStruct(shape, jnp....  17.3 us
    all_to_all x1, blocking collectives, direct_per_device(): lax.all_to_all(squares, ('page', 'query', 'head'), split_axis=0, concat_a...  12.6 us
    all_to_all x1, waiting for transfers between devices, direct_per_device(): lax.all_to_all(squares, ('page', 'query', 'head'), split_axis=0, concat_a...  7.22 us
    all_to_all x1, starting transfers between devices, direct_per_device(): lax.all_to_all(squares, ('page', 'query', 'head'), split_axis=0, concat_a...  3.29 us
  transfers between devices with their start and end apart: 21, of which 11 were waited for; matrix products, arithmetic and copies ran while one was open for 0% of the time, Pallas kernels for 10%

profile of v9, /device:TPU:0, one launch (start us, length us, event | category | flops | bytes accessed | tf_op | source)
XLA Modules:
  0.0 91.5 jit_solution(9474614162942617220)
XLA Ops:
  0.7 2.0 %pack.1 = (f32[520,128]{1,0:T(8,128)}, f32[328,128]{1,0:T(8,128)}) custom-call(f32[4,256,128]{2,1,0:T(8,128)} %refs_0_.3, f32[4,256,128]{2,1,0:T(8,128)} %refs_1_.3, f32[4,256,128]{2,1,0:T(8,128)} %refs_2_.3, f32[4,256]{1,0:T(4,128)} %refs_3_.3, f32[4,256,128]{2,1,0:T(8,128)} %refs_4_.3, s32[4,256]{1,0:T(4,128)} %refs_5_.3, s32[8]{0:T(128)} %refs_6_.3), custom_call_target="tpu_custom_call" | custom-call | flops 1048576 | bytes 1048576 | tf_op jit(solution)/shard_map/pack/pallas_call | solution.py:67
  2.7 0.0 copy-start.9
  2.7 0.5 collective-permute-start
  3.3 2.6 %collective-permute-start.1 = (f32[328,128]{1,0:T(8,128)}, f32[328,128]{1,0:T(8,128)S(1)}, u32[]{:S(2)}, u32[]{:S(2)}) collective-permute-start(f32[328,128]{1,0:T(8,128)} %get-tuple-element.31.refs_11_.refs_2_.refs_7_.refs_5_), channel_id=1, source_target_pairs={{0,2},{2,0},{1,3},{3,1},{4,6},{6,4},{5,7},{7,5},{8,10},{10,8},{9,1... | collective-permute-start | bytes 503816 | tf_op jit(solution)/shard_map/ppermute | solution.py:39
  5.9 0.7 own.1
  6.6 0.5 collective-permute-start.8
  7.0 4.2 %collective-permute-done.1.refs_3_.refs_1_.refs_5_.refs_4_ = f32[328,128]{1,0:T(8,128)S(1)} collective-permute-done((f32[328,128]{1,0:T(8,128)}, f32[328,128]{1,0:T(8,128)S(1)}, u32[]{:S(2)}, u32[]{:S(2)}) %collective-permute-start.1) | collective-permute-done | bytes 167968 | tf_op jit(solution)/shard_map/ppermute | solution.py:39
  11.2 0.0 collective-permute-done.refs_1_.refs_3_
  11.2 1.2 %forward.1 = (f32[136,128]{1,0:T(8,128)S(1)}, f32[136,128]{1,0:T(8,128)S(1)}, f32[136,128]{1,0:T(8,128)S(1)}, f32[136,128]{1,0:T(8,128)S(1)}, f32[512,512]{1,0:T(8,128)S(1)}, /*index=5*/f32[8,512]{1,0:T(8,128)S(1)}) custom-call(f32[520,128]{1,0:T(8,128)S(1)} %get-tuple-element.28.refs_0_.refs_2_, f32[520,128]{1,0:T(8,128)S(1)} %collective-permute-done.refs_1_.refs_3_, ...), custom_call_target="tpu_custom_call" | custom-call | flops 402653184 | bytes 1048576 | tf_op jit(solution)/shard_map/forward/pallas_call | solution.py:67
  12.4 4.1 %collective-permute-start.2 = (f32[136,128]{1,0:T(8,128)S(1)}, f32[136,128]{1,0:T(8,128)S(1)}, u32[]{:S(2)}, u32[]{:S(2)}) collective-permute-start(f32[136,128]{1,0:T(8,128)S(1)} %get-tuple-element.35), channel_id=1, source_target_pairs={{0,24},{4,28},{8,16},{12,20},{16,8},{20,12},{24,0},{28,4},{1,25},{... | collective-permute-start | bytes 208904 | tf_op jit(solution)/shard_map/ppermute | solution.py:39
  16.6 0.6 collective-permute-start.4
  17.2 2.4 %collective-permute-done.2.refs_3_ = f32[136,128]{1,0:T(8,128)S(1)} collective-permute-done((f32[136,128]{1,0:T(8,128)S(1)}, f32[136,128]{1,0:T(8,128)S(1)}, u32[]{:S(2)}, u32[]{:S(2)}) %collective-permute-start.2) | collective-permute-done | bytes 69664 | tf_op jit(solution)/shard_map/ppermute | solution.py:39
  19.6 2.4 %collective-permute-done.3.refs_4_ = f32[136,128]{1,0:T(8,128)S(1)} collective-permute-done((f32[136,128]{1,0:T(8,128)S(1)}, f32[136,128]{1,0:T(8,128)S(1)}, u32[]{:S(2)}, u32[]{:S(2)}) %collective-permute-start.3) | collective-permute-done | bytes 69664 | tf_op jit(solution)/shard_map/ppermute | solution.py:39
  22.0 0.1 merge.2.refs_6_
  22.1 2.6 %collective-permute-start.7 = (f32[136,128]{1,0:T(8,128)S(1)}, f32[136,128]{1,0:T(8,128)S(1)}, u32[]{:S(2)}, u32[]{:S(2)}) collective-permute-start(f32[136,128]{1,0:T(8,128)S(1)} %merge.2.refs_6_), channel_id=1, source_target_pairs={{0,24},{4,28},{8,16},{12,20},{16,8},{20,12},{24,0},{28,4},{1,25},{... | collective-permute-start | bytes 208904 | tf_op jit(solution)/shard_map/ppermute | solution.py:39
  24.7 1.8 %collective-permute-start.5 = (f32[136,128]{1,0:T(8,128)S(1)}, f32[136,128]{1,0:T(8,128)S(1)}, u32[]{:S(2)}, u32[]{:S(2)}) collective-permute-start(f32[136,128]{1,0:T(8,128)S(1)} %merge.2.refs_6_), channel_id=1, source_target_pairs={{0,8},{4,12},{8,0},{12,4},{16,24},{20,28},{24,16},{28,20},{1,9},{5... | collective-permute-start | bytes 208904 | tf_op jit(solution)/shard_map/ppermute | solution.py:39
  26.6 0.0 collective-permute-done.8.refs_10_.refs_1_.refs_6_.refs_4_
  26.6 2.4 %collective-permute-done.7.refs_9_ = f32[136,128]{1,0:T(8,128)S(1)} collective-permute-done((f32[136,128]{1,0:T(8,128)S(1)}, f32[136,128]{1,0:T(8,128)S(1)}, u32[]{:S(2)}, u32[]{:S(2)}) %collective-permute-start.7) | collective-permute-done | bytes 69664 | tf_op jit(solution)/shard_map/ppermute | solution.py:39
  29.0 1.4 %collective-permute-done.6.refs_8_ = f32[136,128]{1,0:T(8,128)S(1)} collective-permute-done((f32[136,128]{1,0:T(8,128)S(1)}, f32[136,128]{1,0:T(8,128)S(1)}, u32[]{:S(2)}, u32[]{:S(2)}) %collective-permute-start.6) | collective-permute-done | bytes 69664 | tf_op jit(solution)/shard_map/ppermute | solution.py:39
  30.4 0.0 collective-permute-done.5.refs_7_
  30.4 2.1 %backward.2 = (f32[520,128]{1,0:T(8,128)S(1)}, f32[520,128]{1,0:T(8,128)S(1)}, f32[32,8,128]{2,1,0:T(8,128)S(1)}) custom-call(f32[512,512]{1,0:T(8,128)S(1)} %get-tuple-element.32.refs_0_, f32[8,512]{1,0:T(8,128)S(1)} %get-tuple-element.33.refs_1_, f32[520,128]{1,0:T(8,128)S(1)} %get-tuple-element.28.refs_0_.refs_2_, ...), custom_call_target="tpu_custom_call" | custom-call | flops 603979776 | bytes 1048576 | tf_op jit(solution)/shard_map/backward/pallas_call | solution.py:67
  32.5 12.6 %all_to_all.10.refs_6_ = f32[32,8,128]{2,1,0:T(8,128)S(1)} all-to-all(f32[32,8,128]{2,1,0:T(8,128)S(1)} %get-tuple-element.40), channel_id=1, replica_groups=mesh['page'=8,'query'=2,'head'=2] {'page','query','head'}, dimensions={0} | all-to-all | bytes 262144 | tf_op jit(solution)/shard_map/all_to_all | solution.py:543
  45.1 1.3 %update_forward.1 = (f32[1040,128]{1,0:T(8,128)S(1)}, f32[136,128]{1,0:T(8,128)S(1)}, f32[136,128]{1,0:T(8,128)S(1)}, f32[136,128]{1,0:T(8,128)S(1)}, f32[136,12...) custom-call(f32[520,128]{1,0:T(8,128)S(1)} %get-tuple-element.28.refs_0_.refs_2_, ...), custom_call_target="tpu_custom_call" | custom-call | flops 402653184 | bytes 1048576 | tf_op jit(solution)/shard_map/update_forward/pallas_call | solution.py:67
  46.4 0.3 collective-permute-start.9
  46.7 1.4 %collective-permute-start.10 = (f32[136,128]{1,0:T(8,128)S(1)}, f32[136,128]{1,0:T(8,128)S(1)}, u32[]{:S(2)}, u32[]{:S(2)}) collective-permute-start(f32[136,128]{1,0:T(8,128)S(1)} %get-tuple-element.43), channel_id=1, source_target_pairs={{0,24},{4,28},{8,16},{12,20},{16,8},{20,12},{24,0},{28,4},{1,25},{... | collective-permute-start | bytes 208904 | tf_op jit(solution)/shard_map/ppermute | solution.py:39
  48.1 0.8 collective-permute-start.11
  48.9 2.2 %collective-permute-start.12 = (f32[136,128]{1,0:T(8,128)S(1)}, f32[136,128]{1,0:T(8,128)S(1)}, u32[]{:S(2)}, u32[]{:S(2)}) collective-permute-start(f32[136,128]{1,0:T(8,128)S(1)} %get-tuple-element.45), channel_id=1, source_target_pairs={{0,8},{4,12},{8,0},{12,4},{16,24},{20,28},{24,16},{28,20},{1,9},{5... | collective-permute-start | bytes 208904 | tf_op jit(solution)/shard_map/ppermute | solution.py:39
  51.1 2.5 %collective-permute-done.10.refs_3_ = f32[136,128]{1,0:T(8,128)S(1)} collective-permute-done((f32[136,128]{1,0:T(8,128)S(1)}, f32[136,128]{1,0:T(8,128)S(1)}, u32[]{:S(2)}, u32[]{:S(2)}) %collective-permute-start.10) | collective-permute-done | bytes 69664 | tf_op jit(solution)/shard_map/ppermute | solution.py:39
  53.6 2.0 %collective-permute-done.11.refs_4_ = f32[136,128]{1,0:T(8,128)S(1)} collective-permute-done((f32[136,128]{1,0:T(8,128)S(1)}, f32[136,128]{1,0:T(8,128)S(1)}, u32[]{:S(2)}, u32[]{:S(2)}) %collective-permute-start.11) | collective-permute-done | bytes 69664 | tf_op jit(solution)/shard_map/ppermute | solution.py:39
  55.7 0.1 merge.3.refs_0_
  55.8 1.7 %collective-permute-start.15 = (f32[136,128]{1,0:T(8,128)S(1)}, f32[136,128]{1,0:T(8,128)S(1)}, u32[]{:S(2)}, u32[]{:S(2)}) collective-permute-start(f32[136,128]{1,0:T(8,128)S(1)} %merge.3.refs_0_), channel_id=1, source_target_pairs={{0,24},{4,28},{8,16},{12,20},{16,8},{20,12},{24,0},{28,4},{1,25},{... | collective-permute-start | bytes 208904 | tf_op jit(solution)/shard_map/ppermute | solution.py:39
  57.4 2.8 %collective-permute-start.13 = (f32[136,128]{1,0:T(8,128)S(1)}, f32[136,128]{1,0:T(8,128)S(1)}, u32[]{:S(2)}, u32[]{:S(2)}) collective-permute-start(f32[136,128]{1,0:T(8,128)S(1)} %merge.3.refs_0_), channel_id=1, source_target_pairs={{0,8},{4,12},{8,0},{12,4},{16,24},{20,28},{24,16},{28,20},{1,9},{5... | collective-permute-start | bytes 208904 | tf_op jit(solution)/shard_map/ppermute | solution.py:39
  60.2 0.7 other_weights.1
  61.0 1.8 %collective-permute-done.15.refs_3_ = f32[136,128]{1,0:T(8,128)S(1)} collective-permute-done((f32[136,128]{1,0:T(8,128)S(1)}, f32[136,128]{1,0:T(8,128)S(1)}, u32[]{:S(2)}, u32[]{:S(2)}) %collective-permute-start.15) | collective-permute-done | bytes 69664 | tf_op jit(solution)/shard_map/ppermute | solution.py:39
  62.7 2.0 %collective-permute-done.14.refs_2_ = f32[136,128]{1,0:T(8,128)S(1)} collective-permute-done((f32[136,128]{1,0:T(8,128)S(1)}, f32[136,128]{1,0:T(8,128)S(1)}, u32[]{:S(2)}, u32[]{:S(2)}) %collective-permute-start.14) | collective-permute-done | bytes 69664 | tf_op jit(solution)/shard_map/ppermute | solution.py:39
  64.7 0.1 join.1.refs_5_
  64.8 0.9 %collective-permute-start.16 = (f32[136,512]{1,0:T(8,128)S(1)}, f32[136,512]{1,0:T(8,128)S(1)}, u32[]{:S(2)}, u32[]{:S(2)}) collective-permute-start(f32[136,512]{1,0:T(8,128)S(1)} %join.1.refs_5_), channel_id=1, source_target_pairs={{0,2},{2,0},{1,3},{3,1},{4,6},{6,4},{5,7},{7,5},{8,10},{10,8},{9,1... | collective-permute-start | bytes 835592 | tf_op jit(solution)/shard_map/ppermute | solution.py:39
  65.7 2.8 %backward.3 = (f32[520,128]{1,0:T(8,128)S(1)}, f32[520,128]{1,0:T(8,128)}, f32[32,8,128]{2,1,0:T(8,128)}) custom-call(f32[512,512]{1,0:T(8,128)S(1)} %get-tuple-element.47.refs_0_, f32[8,512]{1,0:T(8,128)S(1)} %get-tuple-element.48.refs_1_, f32[1040,128]{1,0:T(8,128)S(1)} %get-tuple-element.41.refs_2_.refs_0_, ...), custom_call_target="tpu_custom_call" | custom-call | flops 603979776 | bytes 1048576 | tf_op jit(solution)/shard_map/backward/pallas_call | solution.py:67
  68.5 4.9 %collective-permute-done.16.refs_2_.refs_3_ = f32[136,512]{1,0:T(8,128)S(1)} collective-permute-done((f32[136,512]{1,0:T(8,128)S(1)}, f32[136,512]{1,0:T(8,128)S(1)}, u32[]{:S(2)}, u32[]{:S(2)}) %collective-permute-start.16) | collective-permute-done | bytes 278560 | tf_op jit(solution)/shard_map/ppermute | solution.py:39
  73.4 0.8 mate_parts.1
  74.3 0.5 collective-permute-start.18
  74.8 1.9 %other_backward.3 = f32[520,128]{1,0:T(8,128)} custom-call(f32[512,512]{1,0:T(8,128)S(1)} %get-tuple-element.52.refs_0_, f32[8,512]{1,0:T(8,128)S(1)} %get-tuple-element.46.refs_4_.refs_1_, f32[1040,128]{1,0:T(8,128)S(1)} %collective-permute-done.9.refs_0_.refs_1_.refs_2_, f32[136,512]{1,0:T(8,128)S(1)} %collective-permute-done.16.refs_2_.refs_3_, ...), custom_call_target="tpu_custom_call" | custom-call | flops 301989888 | bytes 1048576 | tf_op jit(solution)/shard_map/other_backward/pallas_call | solution.py:67
  76.7 3.3 %all-to-all-start.1 = ((f32[32,8,128]{2,1,0:T(8,128)}), f32[32,8,128]{2,1,0:T(8,128)}, u32[]{:S(2)}, u32[]{:S(2)}) async-start(f32[32,8,128]{2,1,0:T(8,128)} %get-tuple-element.49.refs_3_.refs_6_), calls=%async_computation.1 | async-start | bytes 262144 | tf_op jit(solution)/shard_map/all_to_all | solution.py:543
  80.0 1.2 %other_backward.2.refs_5_ = f32[520,128]{1,0:T(8,128)S(1)} custom-call(f32[512,512]{1,0:T(8,128)S(1)} %get-tuple-element.52.refs_0_, f32[8,512]{1,0:T(8,128)S(1)} %get-tuple-element.46.refs_4_.refs_1_, f32[1040,128]{1,0:T(8,128)S(1)} %collective-permute-done.9.refs_0_.refs_1_.refs_2_, f32[136,512]{1,0:T(8,128)S(1)} %collective-permute-done.16.refs_2_.refs_3_, ...), custom_call_target="tpu_custom_call" | custom-call | flops 301989888 | bytes 1048576 | tf_op jit(solution)/shard_map/other_backward/pallas_call | solution.py:67
  81.1 7.2 %all-to-all-done.1.refs_7_ = f32[32,8,128]{2,1,0:T(8,128)} async-done(((f32[32,8,128]{2,1,0:T(8,128)}), f32[32,8,128]{2,1,0:T(8,128)}, u32[]{:S(2)}, u32[]{:S(2)}) %all-to-all-start.1) | async-done | bytes 131104 | tf_op jit(solution)/shard_map/all_to_all | solution.py:543
  88.4 0.0 copy-start.6
  88.4 0.9 %copy-done.6 = f32[520,128]{1,0:T(8,128)S(1)} copy-done((f32[520,128]{1,0:T(8,128)S(1)}, f32[520,128]{1,0:T(8,128)}, u32[]{:S(2)}) %copy-start.6) | copy-done | bytes 266264
  89.3 2.2 %last_update.1 = (f32[4,256,128]{2,1,0:T(8,128)}, f32[4,256,128]{2,1,0:T(8,128)}, f32[4,256]{1,0:T(4,128)}) custom-call(f32[1040,128]{1,0:T(8,128)S(1)} %get-tuple-element.41.refs_2_.refs_0_, f32[1040,128]{1,0:T(8,128)S(1)} %collective-permute-done.9.refs_0_.refs_1_.refs_2_, f32[1040,128]{1,0:T(8,128)S(1)} %collective-permute-done.17.refs_2_, ...), custom_call_target="tpu_custom_call" | custom-call | flops 1048576 | bytes 1048576 | tf_op jit(solution)/shard_map/last_update/pallas_call | solution.py:67
  (29 shorter events, 0.1 us)
Async XLA Ops:
  0.6 5.2 %copy-start.4 = (f32[4,256,128]{2,1,0:T(8,128)S(1)}, f32[4,256,128]{2,1,0:T(8,128)}, u32[]{:S(2)}) copy-start(f32[4,256,128]{2,1,0:T(8,128)} %refs_4_.3) | copy-start | bytes 1572868
  0.6 5.2 %copy-start.3 = (f32[4,256,128]{2,1,0:T(8,128)S(1)}, f32[4,256,128]{2,1,0:T(8,128)}, u32[]{:S(2)}) copy-start(f32[4,256,128]{2,1,0:T(8,128)} %refs_2_.3) | copy-start | bytes 1572868
  0.7 5.2 %copy-start.2 = (f32[4,256,128]{2,1,0:T(8,128)S(1)}, f32[4,256,128]{2,1,0:T(8,128)}, u32[]{:S(2)}) copy-start(f32[4,256,128]{2,1,0:T(8,128)} %refs_1_.3) | copy-start | bytes 1572868
  0.7 5.2 %copy-start.1 = (f32[4,256,128]{2,1,0:T(8,128)S(1)}, f32[4,256,128]{2,1,0:T(8,128)}, u32[]{:S(2)}) copy-start(f32[4,256,128]{2,1,0:T(8,128)} %refs_0_.3) | copy-start | bytes 1572868
  0.7 5.2 %copy-start.7 = (f32[4,256]{1,0:T(4,128)S(1)}, f32[4,256]{1,0:T(4,128)}, u32[]{:S(2)}) copy-start(f32[4,256]{1,0:T(4,128)} %refs_3_.3) | copy-start | bytes 12292
  0.7 5.2 %copy-start.8 = (s32[4,256]{1,0:T(4,128)S(1)}, s32[4,256]{1,0:T(4,128)}, u32[]{:S(2)}) copy-start(s32[4,256]{1,0:T(4,128)} %refs_5_.3) | copy-start | bytes 12292
  2.7 3.2 %copy-start.9 = (s32[8]{0:T(128)S(1)}, s32[8]{0:T(128)}, u32[]{:S(2)}) copy-start(s32[8]{0:T(128)} %refs_6_.3) | copy-start | bytes 100
  2.7 8.5 %collective-permute-start = (f32[520,128]{1,0:T(8,128)}, f32[520,128]{1,0:T(8,128)S(1)}, u32[]{:S(2)}, u32[]{:S(2)}) collective-permute-start(f32[520,128]{1,0:T(8,128)} %get-tuple-element.29), channel_id=1, source_target_pairs={{0,4},{4,0},{8,12},{12,8},{16,20},{20,16},{24,28},{28,24},{1,5},{5... | collective-permute-start | bytes 798728 | tf_op jit(solution)/shard_map/ppermute | solution.py:39
  3.3 7.9 %collective-permute-start.1 = (f32[328,128]{1,0:T(8,128)}, f32[328,128]{1,0:T(8,128)S(1)}, u32[]{:S(2)}, u32[]{:S(2)}) collective-permute-start(f32[328,128]{1,0:T(8,128)} %get-tuple-element.31.refs_11_.refs_2_.refs_7_.refs_5_), channel_id=1, source_target_pairs={{0,2},{2,0},{1,3},{3,1},{4,6},{6,4},{5,7},{7,5},{8,10},{10,8},{9,1... | collective-permute-start | bytes 503816 | tf_op jit(solution)/shard_map/ppermute | solution.py:39
  6.6 20.0 %collective-permute-start.8 = (f32[328,128]{1,0:T(8,128)S(1)}, f32[328,128]{1,0:T(8,128)S(1)}, u32[]{:S(2)}, u32[]{:S(2)}) collective-permute-start(f32[328,128]{1,0:T(8,128)S(1)} %get-tuple-element.30.refs_2_.refs_0_.refs_4_.refs_3_), channel_id=1, source_target_pairs={{0,2},{2,0},{1,3},{3,1},{4,6},{6,4},{5,7},{7,5},{8,10},{10,8},{9,1... | collective-permute-start | bytes 503816 | tf_op jit(solution)/shard_map/ppermute | solution.py:39
  12.4 7.1 %collective-permute-start.2 = (f32[136,128]{1,0:T(8,128)S(1)}, f32[136,128]{1,0:T(8,128)S(1)}, u32[]{:S(2)}, u32[]{:S(2)}) collective-permute-start(f32[136,128]{1,0:T(8,128)S(1)} %get-tuple-element.35), channel_id=1, source_target_pairs={{0,24},{4,28},{8,16},{12,20},{16,8},{20,12},{24,0},{28,4},{1,25},{... | collective-permute-start | bytes 208904 | tf_op jit(solution)/shard_map/ppermute | solution.py:39
  16.6 5.5 %collective-permute-start.3 = (f32[136,128]{1,0:T(8,128)S(1)}, f32[136,128]{1,0:T(8,128)S(1)}, u32[]{:S(2)}, u32[]{:S(2)}) collective-permute-start(f32[136,128]{1,0:T(8,128)S(1)} %get-tuple-element.36), channel_id=1, source_target_pairs={{0,16},{4,20},{8,24},{12,28},{16,0},{20,4},{24,8},{28,12},{1,17},{... | collective-permute-start | bytes 208904 | tf_op jit(solution)/shard_map/ppermute | solution.py:39
  16.6 5.5 %collective-permute-start.4 = (f32[136,128]{1,0:T(8,128)S(1)}, f32[136,128]{1,0:T(8,128)S(1)}, u32[]{:S(2)}, u32[]{:S(2)}) collective-permute-start(f32[136,128]{1,0:T(8,128)S(1)} %get-tuple-element.37), channel_id=1, source_target_pairs={{0,8},{4,12},{8,0},{12,4},{16,24},{20,28},{24,16},{28,20},{1,9},{5... | collective-permute-start | bytes 208904 | tf_op jit(solution)/shard_map/ppermute | solution.py:39
  22.0 8.3 %copy-start = (f32[328,128]{1,0:T(8,128)S(1)}, f32[328,128]{1,0:T(8,128)}, u32[]{:S(2)}) copy-start(f32[328,128]{1,0:T(8,128)} %get-tuple-element.31.refs_11_.refs_2_.refs_7_.refs_5_) | copy-start | bytes 503812
  22.1 6.8 %collective-permute-start.7 = (f32[136,128]{1,0:T(8,128)S(1)}, f32[136,128]{1,0:T(8,128)S(1)}, u32[]{:S(2)}, u32[]{:S(2)}) collective-permute-start(f32[136,128]{1,0:T(8,128)S(1)} %merge.2.refs_6_), channel_id=1, source_target_pairs={{0,24},{4,28},{8,16},{12,20},{16,8},{20,12},{24,0},{28,4},{1,25},{... | collective-permute-start | bytes 208904 | tf_op jit(solution)/shard_map/ppermute | solution.py:39
  24.7 5.6 %collective-permute-start.6 = (f32[136,128]{1,0:T(8,128)S(1)}, f32[136,128]{1,0:T(8,128)S(1)}, u32[]{:S(2)}, u32[]{:S(2)}) collective-permute-start(f32[136,128]{1,0:T(8,128)S(1)} %merge.2.refs_6_), channel_id=1, source_target_pairs={{0,16},{4,20},{8,24},{12,28},{16,0},{20,4},{24,8},{28,12},{1,17},{... | collective-permute-start | bytes 208904 | tf_op jit(solution)/shard_map/ppermute | solution.py:39
  24.7 5.6 %collective-permute-start.5 = (f32[136,128]{1,0:T(8,128)S(1)}, f32[136,128]{1,0:T(8,128)S(1)}, u32[]{:S(2)}, u32[]{:S(2)}) collective-permute-start(f32[136,128]{1,0:T(8,128)S(1)} %merge.2.refs_6_), channel_id=1, source_target_pairs={{0,8},{4,12},{8,0},{12,4},{16,24},{20,28},{24,16},{28,20},{1,9},{5... | collective-permute-start | bytes 208904 | tf_op jit(solution)/shard_map/ppermute | solution.py:39
  46.4 13.8 %collective-permute-start.9 = (f32[1040,128]{1,0:T(8,128)S(1)}, f32[1040,128]{1,0:T(8,128)S(1)}, u32[]{:S(2)}, u32[]{:S(2)}) collective-permute-start(f32[1040,128]{1,0:T(8,128)S(1)} %get-tuple-element.41.refs_2_.refs_0_), channel_id=1, source_target_pairs={{0,2},{2,0},{1,3},{3,1},{4,6},{6,4},{5,7},{7,5},{8,10},{10,8},{9,1... | collective-permute-start | bytes 1597448 | tf_op jit(solution)/shard_map/ppermute | solution.py:39
  46.7 6.9 %collective-permute-start.10 = (f32[136,128]{1,0:T(8,128)S(1)}, f32[136,128]{1,0:T(8,128)S(1)}, u32[]{:S(2)}, u32[]{:S(2)}) collective-permute-start(f32[136,128]{1,0:T(8,128)S(1)} %get-tuple-element.43), channel_id=1, source_target_pairs={{0,24},{4,28},{8,16},{12,20},{16,8},{20,12},{24,0},{28,4},{1,25},{... | collective-permute-start | bytes 208904 | tf_op jit(solution)/shard_map/ppermute | solution.py:39
  48.1 7.5 %collective-permute-start.11 = (f32[136,128]{1,0:T(8,128)S(1)}, f32[136,128]{1,0:T(8,128)S(1)}, u32[]{:S(2)}, u32[]{:S(2)}) collective-permute-start(f32[136,128]{1,0:T(8,128)S(1)} %get-tuple-element.44), channel_id=1, source_target_pairs={{0,16},{4,20},{8,24},{12,28},{16,0},{20,4},{24,8},{28,12},{1,17},{... | collective-permute-start | bytes 208904 | tf_op jit(solution)/shard_map/ppermute | solution.py:39
  48.9 6.8 %collective-permute-start.12 = (f32[136,128]{1,0:T(8,128)S(1)}, f32[136,128]{1,0:T(8,128)S(1)}, u32[]{:S(2)}, u32[]{:S(2)}) collective-permute-start(f32[136,128]{1,0:T(8,128)S(1)} %get-tuple-element.45), channel_id=1, source_target_pairs={{0,8},{4,12},{8,0},{12,4},{16,24},{20,28},{24,16},{28,20},{1,9},{5... | collective-permute-start | bytes 208904 | tf_op jit(solution)/shard_map/ppermute | solution.py:39
  55.8 7.0 %collective-permute-start.15 = (f32[136,128]{1,0:T(8,128)S(1)}, f32[136,128]{1,0:T(8,128)S(1)}, u32[]{:S(2)}, u32[]{:S(2)}) collective-permute-start(f32[136,128]{1,0:T(8,128)S(1)} %merge.3.refs_0_), channel_id=1, source_target_pairs={{0,24},{4,28},{8,16},{12,20},{16,8},{20,12},{24,0},{28,4},{1,25},{... | collective-permute-start | bytes 208904 | tf_op jit(solution)/shard_map/ppermute | solution.py:39
  57.4 7.3 %collective-permute-start.14 = (f32[136,128]{1,0:T(8,128)S(1)}, f32[136,128]{1,0:T(8,128)S(1)}, u32[]{:S(2)}, u32[]{:S(2)}) collective-permute-start(f32[136,128]{1,0:T(8,128)S(1)} %merge.3.refs_0_), channel_id=1, source_target_pairs={{0,16},{4,20},{8,24},{12,28},{16,0},{20,4},{24,8},{28,12},{1,17},{... | collective-permute-start | bytes 208904 | tf_op jit(solution)/shard_map/ppermute | solution.py:39
  57.4 7.3 %collective-permute-start.13 = (f32[136,128]{1,0:T(8,128)S(1)}, f32[136,128]{1,0:T(8,128)S(1)}, u32[]{:S(2)}, u32[]{:S(2)}) collective-permute-start(f32[136,128]{1,0:T(8,128)S(1)} %merge.3.refs_0_), channel_id=1, source_target_pairs={{0,8},{4,12},{8,0},{12,4},{16,24},{20,28},{24,16},{28,20},{1,9},{5... | collective-permute-start | bytes 208904 | tf_op jit(solution)/shard_map/ppermute | solution.py:39
  64.8 8.6 %collective-permute-start.16 = (f32[136,512]{1,0:T(8,128)S(1)}, f32[136,512]{1,0:T(8,128)S(1)}, u32[]{:S(2)}, u32[]{:S(2)}) collective-permute-start(f32[136,512]{1,0:T(8,128)S(1)} %join.1.refs_5_), channel_id=1, source_target_pairs={{0,2},{2,0},{1,3},{3,1},{4,6},{6,4},{5,7},{7,5},{8,10},{10,8},{9,1... | collective-permute-start | bytes 835592 | tf_op jit(solution)/shard_map/ppermute | solution.py:39
  68.5 5.7 %copy-start.5 = (f32[520,128]{1,0:T(8,128)}, f32[520,128]{1,0:T(8,128)S(1)}, u32[]{:S(2)}) copy-start(f32[520,128]{1,0:T(8,128)S(1)} %get-tuple-element.50.refs_3_) | copy-start | bytes 798724
  74.3 14.1 %collective-permute-start.17 = (f32[1040,128]{1,0:T(8,128)}, f32[1040,128]{1,0:T(8,128)S(1)}, u32[]{:S(2)}, u32[]{:S(2)}) collective-permute-start(f32[1040,128]{1,0:T(8,128)} %mate_parts.1), channel_id=1, source_target_pairs={{0,4},{4,0},{8,12},{12,8},{16,20},{20,16},{24,28},{28,24},{1,5},{5... | collective-permute-start | bytes 1597448 | tf_op jit(solution)/shard_map/ppermute | solution.py:39
  74.3 14.1 %collective-permute-start.18 = (f32[520,128]{1,0:T(8,128)}, f32[520,128]{1,0:T(8,128)}, u32[]{:S(2)}, u32[]{:S(2)}) collective-permute-start(f32[520,128]{1,0:T(8,128)} %get-tuple-element.51), channel_id=1, source_target_pairs={{0,4},{4,0},{8,12},{12,8},{16,20},{20,16},{24,28},{28,24},{1,5},{5... | collective-permute-start | bytes 798728 | tf_op jit(solution)/shard_map/ppermute | solution.py:39
  76.7 11.7 %collective-permute-start.19 = (f32[520,128]{1,0:T(8,128)}, f32[520,128]{1,0:T(8,128)}, u32[]{:S(2)}, u32[]{:S(2)}) collective-permute-start(f32[520,128]{1,0:T(8,128)} %other_backward.3), channel_id=1, source_target_pairs={{0,4},{4,0},{8,12},{12,8},{16,20},{20,16},{24,28},{28,24},{1,5},{5... | collective-permute-start | bytes 798728 | tf_op jit(solution)/shard_map/ppermute | solution.py:39
  76.7 11.7 %all-to-all-start.1 = ((f32[32,8,128]{2,1,0:T(8,128)}), f32[32,8,128]{2,1,0:T(8,128)}, u32[]{:S(2)}, u32[]{:S(2)}) async-start(f32[32,8,128]{2,1,0:T(8,128)} %get-tuple-element.49.refs_3_.refs_6_), calls=%async_computation.1 | async-start | bytes 262144 | tf_op jit(solution)/shard_map/all_to_all | solution.py:543
  88.4 1.0 %copy-start.6 = (f32[520,128]{1,0:T(8,128)S(1)}, f32[520,128]{1,0:T(8,128)}, u32[]{:S(2)}) copy-start(f32[520,128]{1,0:T(8,128)} %copy-done.5) | copy-start | bytes 798724

commit v10 on v9

--- a/solution.py
+++ b/solution.py
@@ -71,7 +71,9 @@
         out_specs=[pl.BlockSpec(memory_space=pltpu.VMEM) for _ in out_shapes],
         scratch_shapes=scratch,
         compiler_params=pltpu.CompilerParams(vmem_limit_bytes=vmem * 2**20),
-        cost_estimate=pl.CostEstimate(flops=cost, bytes_accessed=2**20, transcendentals=0),
+        cost_estimate=pl.CostEstimate(
+            flops=cost, bytes_accessed=min(cost, 2**20), transcendentals=0
+        ),
         name=name,
     )(*operands, *after)
 
@@ -295,26 +297,27 @@
             state_ref[value_end:, :] - sizes[2] * grad_ref[value_end:, :],
         )
 
+    def read_positions(query_refs):
+        return in_columns(
+            [tail_as_row(ref, part_rows + piece, pos_rows) for ref in query_refs], 1
+        )
+
+    def page_scores(ref, all_queries, positions):
+        scores = dot(halves(ref[:slot_rows, :]), all_queries, 1, 1) * score_scale
+        bias = row_as_column(tail_as_row(ref, 2 * slot_rows, bias_rows), width)
+        scores = scores + jnp.concatenate([bias] * (query_rows // width), axis=1)
+        page_start = ref[packed_rows - 1 : packed_rows, 0:1]
+        visible = jnp.broadcast_to(positions >= page_start, scores.shape)
+        return jnp.where(visible, scores, MASKED), visible
+
     def all_weights(state_refs, query_refs):
-        all_queries = read_queries(query_refs)
-        position_row = in_columns(
-            [tail_as_row(ref, part_rows + piece, pos_rows) for ref in query_refs], 1
-        )
-        all_scores, all_visible = [], []
-        for ref in state_refs:
-            scores = dot(halves(ref[:slot_rows, :]), all_queries, 1, 1) * score_scale
-            bias = row_as_column(tail_as_row(ref, 2 * slot_rows, bias_rows), width)
-            scores = scores + jnp.concatenate([bias] * (query_rows // width), axis=1)
-            page_start = ref[packed_rows - 1 : packed_rows, 0:1]
-            visible = jnp.broadcast_to(position_row >= page_start, scores.shape)
-            all_scores.append(jnp.where(visible, scores, MASKED))
-            all_visible.append(visible)
-        row_max = jnp.max(all_scores[0], axis=0, keepdims=True)
-        for scores in all_scores[1:]:
+        all_queries, positions = read_queries(query_refs), read_positions(query_refs)
+        pages = [page_scores(ref, all_queries, positions) for ref in state_refs]
+        row_max = jnp.max(pages[0][0], axis=0, keepdims=True)
+        for scores, _ in pages[1:]:
             row_max = jnp.maximum(row_max, jnp.max(scores, axis=0, keepdims=True))
         weights = [
-            jnp.where(visible, jnp.exp(scores - row_max), 0.0)
-            for scores, visible in zip(all_scores, all_visible)
+            jnp.where(visible, jnp.exp(scores - row_max), 0.0) for scores, visible in pages
         ]
         return weights, row_max
 
@@ -402,32 +405,28 @@
         *merged_refs, joined_out, chunks = refs
         joined_out[...] = join_chunks(merged_refs, chunks)
 
-    def gradients_of(joined, max_ref, query_refs):
-        residual = halves(joined[:width, :])
+    def page_gradients(weights, factor, state_ref, all_queries, residual, row_delta, out):
+        attention = weights * factor
+        grad_values = dot(halves(attention), residual, 1, 1)
+        grad_probs = dot(halves(state_ref[slot_rows : 2 * slot_rows, :]), residual, 1, 0)
+        grad_scores = halves(attention * (grad_probs - row_delta))
+        grad_keys = dot(grad_scores, all_queries, 1, 0) * score_scale
+        ones = jnp.ones((TAIL, query_rows), jnp.bfloat16)
+        grad_bias = dot((ones, jnp.zeros_like(ones)), grad_scores, 1, 1)[0:1, :]
+        grad_bias = row_as_tail(grad_bias, width)
+        out[:slot_rows, :] = grad_keys
+        out[slot_rows : 2 * slot_rows, :] = grad_values
+        out[2 * slot_rows :, :] = grad_bias
+        return [
+            jnp.sum(grad * grad, axis=0, keepdims=True)
+            for grad in (grad_keys, grad_values, grad_bias)
+        ]
+
+    def split_joined(joined):
         row_max, row_total, row_delta = (
             joined[width + at : width + at + 1, :] for at in range(3)
         )
-        all_queries = read_queries(query_refs)
-        factor = jnp.exp(max_ref[0:1, :] - row_max) / row_total
-        ones = jnp.ones((TAIL, query_rows), jnp.bfloat16)
-        ones = (ones, jnp.zeros_like(ones))
-
-        def gradients(at, state_ref, weights_ref, out):
-            attention = weights_ref[at * slot_rows : (at + 1) * slot_rows, :] * factor
-            grad_values = dot(halves(attention), residual, 1, 1)
-            grad_probs = dot(halves(state_ref[slot_rows : 2 * slot_rows, :]), residual, 1, 0)
-            grad_scores = halves(attention * (grad_probs - row_delta))
-            grad_keys = dot(grad_scores, all_queries, 1, 0) * score_scale
-            grad_bias = row_as_tail(dot(ones, grad_scores, 1, 1)[0:1, :], width)
-            out[:slot_rows, :] = grad_keys
-            out[slot_rows : 2 * slot_rows, :] = grad_values
-            out[2 * slot_rows :, :] = grad_bias
-            return [
-                jnp.sum(grad * grad, axis=0, keepdims=True)
-                for grad in (grad_keys, grad_values, grad_bias)
-            ]
-
-        return gradients
+        return halves(joined[:width, :]), row_max, row_total, row_delta
 
     def backward_body(weights_ref, max_ref, *refs):
         state_refs, refs = parts_of(refs[: len(states)]), refs[len(states) :]
@@ -435,10 +434,15 @@
         merged_refs, refs = refs[: len(all_merged)], refs[len(all_merged) :]
         grad_outs, (squares_out, *scratch) = refs[:2], refs[2:]
         joined = join_chunks(merged_refs, *scratch) if scratch else merged_refs[0][...]
-        gradients = gradients_of(joined, max_ref, query_refs)
-        squares = [
-            gradients(at, ref, weights_ref, grad_outs[at]) for at, ref in enumerate(state_refs)
-        ]
+        residual, row_max, row_total, row_delta = split_joined(joined)
+        all_queries = read_queries(query_refs)
+        factor = jnp.exp(max_ref[0:1, :] - row_max) / row_total
+        squares = []
+        for at, (ref, out) in enumerate(zip(state_refs, grad_outs)):
+            weights = weights_ref[at * slot_rows : (at + 1) * slot_rows, :]
+            squares.append(
+                page_gradients(weights, factor, ref, all_queries, residual, row_delta, out)
+            )
         tile = jnp.concatenate(
             [sum(parts) for parts in zip(*squares)]
             + [jnp.zeros((TAIL - 3, width), jnp.float32)],
@@ -447,16 +451,17 @@
         for at in range(devices):
             squares_out[at] = tile
 
-    def weights_body(state_ref, *refs):
-        query_refs, (weights_out, max_out) = refs[:query_devices], refs[query_devices:]
-        weights, row_max = all_weights(parts_of([state_ref]), query_refs)
-        store_weights(weights, row_max, weights_out, max_out)
-
     def page_body(at):
-        def body(weights_ref, max_ref, state_ref, joined_ref, *refs):
+        def body(state_ref, joined_ref, *refs):
             query_refs, (grad_out,) = refs[:query_devices], refs[query_devices:]
-            gradients = gradients_of(joined_ref[...], max_ref, query_refs)
-            gradients(at, part_of(state_ref, at), weights_ref, grad_out)
+            residual, row_max, row_total, row_delta = split_joined(joined_ref[...])
+            all_queries = read_queries(query_refs)
+            ref = part_of(state_ref, at)
+            scores, visible = page_scores(ref, all_queries, read_positions(query_refs))
+            weights = jnp.where(visible, jnp.exp(scores - row_max), 0.0)
+            page_gradients(
+                weights, 1.0 / row_total, ref, all_queries, residual, row_delta, grad_out
+            )
 
         return body
 
@@ -507,24 +512,8 @@
             exchange(merged, page=CORES * turn) for turn in range(1, ranks)
         ]
         if last and repeat:
-            other_weights = [
-                call(
-                    weights_body,
-                    weight_shapes,
-                    "other_weights",
-                    matmul_cost,
-                    [new_states[turn]] + query_parts_of[turn],
-                )
-                for turn in range(1, query_devices)
-            ]
             all_merged = call(
-                join_body,
-                [(width + TAIL, query_rows)],
-                "join",
-                2**20,
-                all_merged,
-                chunk_scratch,
-                after=[head_weights[1] for head_weights in other_weights],
+                join_body, [(width + TAIL, query_rows)], "join", 2**20, all_merged, chunk_scratch
             )
             all_joined = [
                 to_device(all_merged[0], query=turn) for turn in range(query_devices)
@@ -547,13 +536,13 @@
 
     all_grads = [own_grad, exchange(mate_grad, page=1)]
     for turn in range(1, query_devices):
-        operands = list(other_weights[turn - 1]) + [new_states[turn], all_joined[turn]]
+        operands = [new_states[turn], all_joined[turn]]
         page_grads = [
             call(
                 page_body(at),
                 [(packed_rows, width)],
                 "other_backward",
-                3 * matmul_cost // 2,
+                0,
                 operands + query_parts_of[turn],
                 after=[squares],
             )[0]
@@ -564,7 +553,7 @@
         mate_body,
         [(query_devices * packed_rows, width)],
         "mate_parts",
-        2**20,
+        0,
         new_states,
         after=all_joined[1:] + [squares],
     )

time: 91.8 us -> 90.1 us (0.981)
  Pallas kernels: 17.3 us -> 15.5 us
    pallas_call x14 -> x13, Pallas kernels: 17.3 us -> 15.5 us  [call(): pl.pallas_call(without_after, out_shape=[jax.ShapeDtypeStruct(shape, jnp....]
  transfers between devices with their start and end apart: 21 -> 21, of which waited for: 11 -> 11; matrix products, arithmetic and copies ran while one was open for 0% -> 0% of each run, Pallas kernels for 10% -> 9%
where the time goes in v10:
time: 90.1 us; the launch traced here: 89.9 us
  waiting for transfers between devices  33.7 us (37%)
  starting transfers between devices  26.3 us (29%)
  Pallas kernels  15.5 us (17%)
  blocking collectives  12.6 us (14%)
  local copies, waits for them, and re-layouts  0.99 us (1%)
    ppermute x20, waiting for transfers between devices, exchange(): return lax.ppermute(value, axes, pairs)  26.7 us
    ppermute x20, starting transfers between devices, exchange(): return lax.ppermute(value, axes, pairs)  23.6 us
    pallas_call x13, Pallas kernels, call(): pl.pallas_call(without_after, out_shape=[jax.ShapeDtypeStruct(shape, jnp....  15.5 us
    all_to_all x1, blocking collectives, direct_per_device(): lax.all_to_all(squares, ('page', 'query', 'head'), split_axis=0, concat_a...  12.6 us
    all_to_all x1, waiting for transfers between devices, direct_per_device(): lax.all_to_all(squares, ('page', 'query', 'head'), split_axis=0, concat_a...  7 us
    all_to_all x1, starting transfers between devices, direct_per_device(): lax.all_to_all(squares, ('page', 'query', 'head'), split_axis=0, concat_a...  2.72 us
  transfers between devices with their start and end apart: 21, of which 11 were waited for; matrix products, arithmetic and copies ran while one was open for 0% of the time, Pallas kernels for 9%

profile of v10, /device:TPU:0, one launch (start us, length us, event | category | flops | bytes accessed | tf_op | source)
XLA Modules:
  0.0 89.9 jit_solution(6293935726504897240)
XLA Ops:
  0.7 2.0 %pack.1 = (f32[520,128]{1,0:T(8,128)}, f32[328,128]{1,0:T(8,128)}) custom-call(f32[4,256,128]{2,1,0:T(8,128)} %refs_0_.3, f32[4,256,128]{2,1,0:T(8,128)} %refs_1_.3, f32[4,256,128]{2,1,0:T(8,128)} %refs_2_.3, f32[4,256]{1,0:T(4,128)} %refs_3_.3, f32[4,256,128]{2,1,0:T(8,128)} %refs_4_.3, s32[4,256]{1,0:T(4,128)} %refs_5_.3, s32[8]{0:T(128)} %refs_6_.3), custom_call_target="tpu_custom_call" | custom-call | flops 1048576 | bytes 1048576 | tf_op jit(solution)/shard_map/pack/pallas_call | solution.py:67
  2.7 0.0 copy-start.9
  2.7 0.5 collective-permute-start
  3.3 2.6 %collective-permute-start.1 = (f32[328,128]{1,0:T(8,128)}, f32[328,128]{1,0:T(8,128)S(1)}, u32[]{:S(2)}, u32[]{:S(2)}) collective-permute-start(f32[328,128]{1,0:T(8,128)} %get-tuple-element.29.refs_11_.refs_7_.refs_3_), channel_id=1, source_target_pairs={{0,2},{2,0},{1,3},{3,1},{4,6},{6,4},{5,7},{7,5},{8,10},{10,8},{9,1... | collective-permute-start | bytes 503816 | tf_op jit(solution)/shard_map/ppermute | solution.py:39
  5.9 0.7 own.1
  6.6 0.5 collective-permute-start.8
  7.0 4.2 %collective-permute-done.1.refs_3_.refs_1_.refs_5_.refs_4_ = f32[328,128]{1,0:T(8,128)S(1)} collective-permute-done((f32[328,128]{1,0:T(8,128)}, f32[328,128]{1,0:T(8,128)S(1)}, u32[]{:S(2)}, u32[]{:S(2)}) %collective-permute-start.1) | collective-permute-done | bytes 167968 | tf_op jit(solution)/shard_map/ppermute | solution.py:39
  11.2 0.0 collective-permute-done.refs_1_.refs_3_
  11.2 1.2 %forward.1 = (f32[136,128]{1,0:T(8,128)S(1)}, f32[136,128]{1,0:T(8,128)S(1)}, f32[136,128]{1,0:T(8,128)S(1)}, f32[136,128]{1,0:T(8,128)S(1)}, f32[512,512]{1,0:T(8,128)S(1)}, /*index=5*/f32[8,512]{1,0:T(8,128)S(1)}) custom-call(f32[520,128]{1,0:T(8,128)S(1)} %get-tuple-element.26.refs_0_.refs_2_, f32[520,128]{1,0:T(8,128)S(1)} %collective-permute-done.refs_1_.refs_3_, ...), custom_call_target="tpu_custom_call" | custom-call | flops 402653184 | bytes 1048576 | tf_op jit(solution)/shard_map/forward/pallas_call | solution.py:67
  12.4 4.1 %collective-permute-start.2 = (f32[136,128]{1,0:T(8,128)S(1)}, f32[136,128]{1,0:T(8,128)S(1)}, u32[]{:S(2)}, u32[]{:S(2)}) collective-permute-start(f32[136,128]{1,0:T(8,128)S(1)} %get-tuple-element.33), channel_id=1, source_target_pairs={{0,24},{4,28},{8,16},{12,20},{16,8},{20,12},{24,0},{28,4},{1,25},{... | collective-permute-start | bytes 208904 | tf_op jit(solution)/shard_map/ppermute | solution.py:39
  16.6 0.6 collective-permute-start.4
  17.2 2.4 %collective-permute-done.2.refs_3_ = f32[136,128]{1,0:T(8,128)S(1)} collective-permute-done((f32[136,128]{1,0:T(8,128)S(1)}, f32[136,128]{1,0:T(8,128)S(1)}, u32[]{:S(2)}, u32[]{:S(2)}) %collective-permute-start.2) | collective-permute-done | bytes 69664 | tf_op jit(solution)/shard_map/ppermute | solution.py:39
  19.6 2.4 %collective-permute-done.3.refs_4_ = f32[136,128]{1,0:T(8,128)S(1)} collective-permute-done((f32[136,128]{1,0:T(8,128)S(1)}, f32[136,128]{1,0:T(8,128)S(1)}, u32[]{:S(2)}, u32[]{:S(2)}) %collective-permute-start.3) | collective-permute-done | bytes 69664 | tf_op jit(solution)/shard_map/ppermute | solution.py:39
  22.0 0.1 merge.2.refs_6_
  22.1 2.6 %collective-permute-start.7 = (f32[136,128]{1,0:T(8,128)S(1)}, f32[136,128]{1,0:T(8,128)S(1)}, u32[]{:S(2)}, u32[]{:S(2)}) collective-permute-start(f32[136,128]{1,0:T(8,128)S(1)} %merge.2.refs_6_), channel_id=1, source_target_pairs={{0,24},{4,28},{8,16},{12,20},{16,8},{20,12},{24,0},{28,4},{1,25},{... | collective-permute-start | bytes 208904 | tf_op jit(solution)/shard_map/ppermute | solution.py:39
  24.7 1.8 %collective-permute-start.5 = (f32[136,128]{1,0:T(8,128)S(1)}, f32[136,128]{1,0:T(8,128)S(1)}, u32[]{:S(2)}, u32[]{:S(2)}) collective-permute-start(f32[136,128]{1,0:T(8,128)S(1)} %merge.2.refs_6_), channel_id=1, source_target_pairs={{0,8},{4,12},{8,0},{12,4},{16,24},{20,28},{24,16},{28,20},{1,9},{5... | collective-permute-start | bytes 208904 | tf_op jit(solution)/shard_map/ppermute | solution.py:39
  26.6 0.0 collective-permute-done.8.refs_10_.refs_6_.refs_2_
  26.6 2.4 %collective-permute-done.7.refs_9_ = f32[136,128]{1,0:T(8,128)S(1)} collective-permute-done((f32[136,128]{1,0:T(8,128)S(1)}, f32[136,128]{1,0:T(8,128)S(1)}, u32[]{:S(2)}, u32[]{:S(2)}) %collective-permute-start.7) | collective-permute-done | bytes 69664 | tf_op jit(solution)/shard_map/ppermute | solution.py:39
  29.0 1.4 %collective-permute-done.6.refs_8_ = f32[136,128]{1,0:T(8,128)S(1)} collective-permute-done((f32[136,128]{1,0:T(8,128)S(1)}, f32[136,128]{1,0:T(8,128)S(1)}, u32[]{:S(2)}, u32[]{:S(2)}) %collective-permute-start.6) | collective-permute-done | bytes 69664 | tf_op jit(solution)/shard_map/ppermute | solution.py:39
  30.4 0.0 collective-permute-done.5.refs_7_
  30.4 2.1 %backward.2 = (f32[520,128]{1,0:T(8,128)S(1)}, f32[520,128]{1,0:T(8,128)S(1)}, f32[32,8,128]{2,1,0:T(8,128)S(1)}) custom-call(f32[512,512]{1,0:T(8,128)S(1)} %get-tuple-element.30.refs_0_, f32[8,512]{1,0:T(8,128)S(1)} %get-tuple-element.31.refs_1_, f32[520,128]{1,0:T(8,128)S(1)} %get-tuple-element.26.refs_0_.refs_2_, ...), custom_call_target="tpu_custom_call" | custom-call | flops 603979776 | bytes 1048576 | tf_op jit(solution)/shard_map/backward/pallas_call | solution.py:67
  32.5 12.6 %all_to_all.10.refs_6_ = f32[32,8,128]{2,1,0:T(8,128)S(1)} all-to-all(f32[32,8,128]{2,1,0:T(8,128)S(1)} %get-tuple-element.38), channel_id=1, replica_groups=mesh['page'=8,'query'=2,'head'=2] {'page','query','head'}, dimensions={0} | all-to-all | bytes 262144 | tf_op jit(solution)/shard_map/all_to_all | solution.py:532
  45.1 1.3 %update_forward.1 = (f32[1040,128]{1,0:T(8,128)S(1)}, f32[136,128]{1,0:T(8,128)S(1)}, f32[136,128]{1,0:T(8,128)S(1)}, f32[136,128]{1,0:T(8,128)S(1)}, f32[136,12...) custom-call(f32[520,128]{1,0:T(8,128)S(1)} %get-tuple-element.26.refs_0_.refs_2_, ...), custom_call_target="tpu_custom_call" | custom-call | flops 402653184 | bytes 1048576 | tf_op jit(solution)/shard_map/update_forward/pallas_call | solution.py:67
  46.4 0.3 collective-permute-start.9
  46.7 1.4 %collective-permute-start.10 = (f32[136,128]{1,0:T(8,128)S(1)}, f32[136,128]{1,0:T(8,128)S(1)}, u32[]{:S(2)}, u32[]{:S(2)}) collective-permute-start(f32[136,128]{1,0:T(8,128)S(1)} %get-tuple-element.41), channel_id=1, source_target_pairs={{0,24},{4,28},{8,16},{12,20},{16,8},{20,12},{24,0},{28,4},{1,25},{... | collective-permute-start | bytes 208904 | tf_op jit(solution)/shard_map/ppermute | solution.py:39
  48.1 0.8 collective-permute-start.11
  48.9 2.2 %collective-permute-start.12 = (f32[136,128]{1,0:T(8,128)S(1)}, f32[136,128]{1,0:T(8,128)S(1)}, u32[]{:S(2)}, u32[]{:S(2)}) collective-permute-start(f32[136,128]{1,0:T(8,128)S(1)} %get-tuple-element.43), channel_id=1, source_target_pairs={{0,8},{4,12},{8,0},{12,4},{16,24},{20,28},{24,16},{28,20},{1,9},{5... | collective-permute-start | bytes 208904 | tf_op jit(solution)/shard_map/ppermute | solution.py:39
  51.1 2.5 %collective-permute-done.10.refs_3_ = f32[136,128]{1,0:T(8,128)S(1)} collective-permute-done((f32[136,128]{1,0:T(8,128)S(1)}, f32[136,128]{1,0:T(8,128)S(1)}, u32[]{:S(2)}, u32[]{:S(2)}) %collective-permute-start.10) | collective-permute-done | bytes 69664 | tf_op jit(solution)/shard_map/ppermute | solution.py:39
  53.6 2.0 %collective-permute-done.11.refs_4_ = f32[136,128]{1,0:T(8,128)S(1)} collective-permute-done((f32[136,128]{1,0:T(8,128)S(1)}, f32[136,128]{1,0:T(8,128)S(1)}, u32[]{:S(2)}, u32[]{:S(2)}) %collective-permute-start.11) | collective-permute-done | bytes 69664 | tf_op jit(solution)/shard_map/ppermute | solution.py:39
  55.7 0.1 merge.3.refs_0_
  55.8 1.7 %collective-permute-start.15 = (f32[136,128]{1,0:T(8,128)S(1)}, f32[136,128]{1,0:T(8,128)S(1)}, u32[]{:S(2)}, u32[]{:S(2)}) collective-permute-start(f32[136,128]{1,0:T(8,128)S(1)} %merge.3.refs_0_), channel_id=1, source_target_pairs={{0,24},{4,28},{8,16},{12,20},{16,8},{20,12},{24,0},{28,4},{1,25},{... | collective-permute-start | bytes 208904 | tf_op jit(solution)/shard_map/ppermute | solution.py:39
  57.4 2.8 %collective-permute-start.13 = (f32[136,128]{1,0:T(8,128)S(1)}, f32[136,128]{1,0:T(8,128)S(1)}, u32[]{:S(2)}, u32[]{:S(2)}) collective-permute-start(f32[136,128]{1,0:T(8,128)S(1)} %merge.3.refs_0_), channel_id=1, source_target_pairs={{0,8},{4,12},{8,0},{12,4},{16,24},{20,28},{24,16},{28,20},{1,9},{5... | collective-permute-start | bytes 208904 | tf_op jit(solution)/shard_map/ppermute | solution.py:39
  60.2 2.5 %collective-permute-done.15.refs_3_ = f32[136,128]{1,0:T(8,128)S(1)} collective-permute-done((f32[136,128]{1,0:T(8,128)S(1)}, f32[136,128]{1,0:T(8,128)S(1)}, u32[]{:S(2)}, u32[]{:S(2)}) %collective-permute-start.15) | collective-permute-done | bytes 69664 | tf_op jit(solution)/shard_map/ppermute | solution.py:39
  62.7 2.0 %collective-permute-done.14.refs_2_ = f32[136,128]{1,0:T(8,128)S(1)} collective-permute-done((f32[136,128]{1,0:T(8,128)S(1)}, f32[136,128]{1,0:T(8,128)S(1)}, u32[]{:S(2)}, u32[]{:S(2)}) %collective-permute-start.14) | collective-permute-done | bytes 69664 | tf_op jit(solution)/shard_map/ppermute | solution.py:39
  64.7 0.1 join.1.refs_5_
  64.8 0.9 %collective-permute-start.16 = (f32[136,512]{1,0:T(8,128)S(1)}, f32[136,512]{1,0:T(8,128)S(1)}, u32[]{:S(2)}, u32[]{:S(2)}) collective-permute-start(f32[136,512]{1,0:T(8,128)S(1)} %join.1.refs_5_), channel_id=1, source_target_pairs={{0,2},{2,0},{1,3},{3,1},{4,6},{6,4},{5,7},{7,5},{8,10},{10,8},{9,1... | collective-permute-start | bytes 835592 | tf_op jit(solution)/shard_map/ppermute | solution.py:39
  65.7 2.8 %backward.3 = (f32[520,128]{1,0:T(8,128)S(1)}, f32[520,128]{1,0:T(8,128)}, f32[32,8,128]{2,1,0:T(8,128)}) custom-call(f32[512,512]{1,0:T(8,128)S(1)} %get-tuple-element.44.refs_0_, f32[8,512]{1,0:T(8,128)S(1)} %get-tuple-element.45.refs_1_, f32[1040,128]{1,0:T(8,128)S(1)} %get-tuple-element.39.refs_2_.refs_0_, ...), custom_call_target="tpu_custom_call" | custom-call | flops 603979776 | bytes 1048576 | tf_op jit(solution)/shard_map/backward/pallas_call | solution.py:67
  68.6 4.9 %collective-permute-done.16.refs_2_.refs_1_ = f32[136,512]{1,0:T(8,128)S(1)} collective-permute-done((f32[136,512]{1,0:T(8,128)S(1)}, f32[136,512]{1,0:T(8,128)S(1)}, u32[]{:S(2)}, u32[]{:S(2)}) %collective-permute-start.16) | collective-permute-done | bytes 278560 | tf_op jit(solution)/shard_map/ppermute | solution.py:39
  73.5 0.1 collective-permute-start.17
  73.6 0.5 collective-permute-start.18
  74.1 1.4 %other_backward.3 = f32[520,128]{1,0:T(8,128)S(1)} custom-call(f32[1040,128]{1,0:T(8,128)S(1)} %collective-permute-done.9.refs_1_.refs_0_, f32[136,512]{1,0:T(8,128)S(1)} %collective-permute-done.16.refs_2_.refs_1_, f32[328,128]{1,0:T(8,128)S(1)} %collective-permute-done.8.refs_10_.refs_6_.refs_2_, f32[328,128]{1,0:T(8,128)S(1)} %copy-done, ...), custom_call_target="tpu_custom_call" | custom-call | tf_op jit(solution)/shard_map/other_backward/pallas_call | solution.py:67
  75.5 0.1 collective-permute-start.19
  75.6 2.7 %all-to-all-start.1 = ((f32[32,8,128]{2,1,0:T(8,128)}), f32[32,8,128]{2,1,0:T(8,128)S(1)}, u32[]{:S(2)}, u32[]{:S(2)}) async-start(f32[32,8,128]{2,1,0:T(8,128)} %get-tuple-element.46.refs_3_.refs_4_), calls=%async_computation.1 | async-start | bytes 262144 | tf_op jit(solution)/shard_map/all_to_all | solution.py:532
  78.3 1.4 %other_backward.2.refs_5_ = f32[520,128]{1,0:T(8,128)S(1)} custom-call(f32[1040,128]{1,0:T(8,128)S(1)} %collective-permute-done.9.refs_1_.refs_0_, f32[136,512]{1,0:T(8,128)S(1)} %collective-permute-done.16.refs_2_.refs_1_, f32[328,128]{1,0:T(8,128)S(1)} %collective-permute-done.8.refs_10_.refs_6_.refs_2_, f32[328,128]{1,0:T(8,128)S(1)} %copy-done, ...), custom_call_target="tpu_custom_call" | custom-call | tf_op jit(solution)/shard_map/other_backward/pallas_call | solution.py:67
  79.7 7.0 %all-to-all-done.1.refs_7_ = f32[32,8,128]{2,1,0:T(8,128)S(1)} async-done(((f32[32,8,128]{2,1,0:T(8,128)}), f32[32,8,128]{2,1,0:T(8,128)S(1)}, u32[]{:S(2)}, u32[]{:S(2)}) %all-to-all-start.1) | async-done | bytes 131104 | tf_op jit(solution)/shard_map/all_to_all | solution.py:532
  86.7 0.0 copy-start.6
  86.7 0.9 %copy-done.6 = f32[520,128]{1,0:T(8,128)S(1)} copy-done((f32[520,128]{1,0:T(8,128)S(1)}, f32[520,128]{1,0:T(8,128)}, u32[]{:S(2)}) %copy-start.6) | copy-done | bytes 266264
  87.7 2.2 %last_update.1 = (f32[4,256,128]{2,1,0:T(8,128)}, f32[4,256,128]{2,1,0:T(8,128)}, f32[4,256]{1,0:T(4,128)}) custom-call(f32[1040,128]{1,0:T(8,128)S(1)} %get-tuple-element.39.refs_2_.refs_0_, f32[1040,128]{1,0:T(8,128)S(1)} %collective-permute-done.9.refs_1_.refs_0_, f32[1040,128]{1,0:T(8,128)S(1)} %collective-permute-done.17.refs_2_, ...), custom_call_target="tpu_custom_call" | custom-call | flops 1048576 | bytes 1048576 | tf_op jit(solution)/shard_map/last_update/pallas_call | solution.py:67
  (28 shorter events, 0.1 us)
Async XLA Ops:
  0.6 5.2 %copy-start.4 = (f32[4,256,128]{2,1,0:T(8,128)S(1)}, f32[4,256,128]{2,1,0:T(8,128)}, u32[]{:S(2)}) copy-start(f32[4,256,128]{2,1,0:T(8,128)} %refs_4_.3) | copy-start | bytes 1572868
  0.6 5.2 %copy-start.3 = (f32[4,256,128]{2,1,0:T(8,128)S(1)}, f32[4,256,128]{2,1,0:T(8,128)}, u32[]{:S(2)}) copy-start(f32[4,256,128]{2,1,0:T(8,128)} %refs_2_.3) | copy-start | bytes 1572868
  0.7 5.2 %copy-start.2 = (f32[4,256,128]{2,1,0:T(8,128)S(1)}, f32[4,256,128]{2,1,0:T(8,128)}, u32[]{:S(2)}) copy-start(f32[4,256,128]{2,1,0:T(8,128)} %refs_1_.3) | copy-start | bytes 1572868
  0.7 5.2 %copy-start.1 = (f32[4,256,128]{2,1,0:T(8,128)S(1)}, f32[4,256,128]{2,1,0:T(8,128)}, u32[]{:S(2)}) copy-start(f32[4,256,128]{2,1,0:T(8,128)} %refs_0_.3) | copy-start | bytes 1572868
  0.7 5.2 %copy-start.7 = (f32[4,256]{1,0:T(4,128)S(1)}, f32[4,256]{1,0:T(4,128)}, u32[]{:S(2)}) copy-start(f32[4,256]{1,0:T(4,128)} %refs_3_.3) | copy-start | bytes 12292
  0.7 5.2 %copy-start.8 = (s32[4,256]{1,0:T(4,128)S(1)}, s32[4,256]{1,0:T(4,128)}, u32[]{:S(2)}) copy-start(s32[4,256]{1,0:T(4,128)} %refs_5_.3) | copy-start | bytes 12292
  2.7 3.2 %copy-start.9 = (s32[8]{0:T(128)S(1)}, s32[8]{0:T(128)}, u32[]{:S(2)}) copy-start(s32[8]{0:T(128)} %refs_6_.3) | copy-start | bytes 100
  2.7 8.5 %collective-permute-start = (f32[520,128]{1,0:T(8,128)}, f32[520,128]{1,0:T(8,128)S(1)}, u32[]{:S(2)}, u32[]{:S(2)}) collective-permute-start(f32[520,128]{1,0:T(8,128)} %get-tuple-element.27), channel_id=1, source_target_pairs={{0,4},{4,0},{8,12},{12,8},{16,20},{20,16},{24,28},{28,24},{1,5},{5... | collective-permute-start | bytes 798728 | tf_op jit(solution)/shard_map/ppermute | solution.py:39
  3.3 7.9 %collective-permute-start.1 = (f32[328,128]{1,0:T(8,128)}, f32[328,128]{1,0:T(8,128)S(1)}, u32[]{:S(2)}, u32[]{:S(2)}) collective-permute-start(f32[328,128]{1,0:T(8,128)} %get-tuple-element.29.refs_11_.refs_7_.refs_3_), channel_id=1, source_target_pairs={{0,2},{2,0},{1,3},{3,1},{4,6},{6,4},{5,7},{7,5},{8,10},{10,8},{9,1... | collective-permute-start | bytes 503816 | tf_op jit(solution)/shard_map/ppermute | solution.py:39
  6.6 20.0 %collective-permute-start.8 = (f32[328,128]{1,0:T(8,128)S(1)}, f32[328,128]{1,0:T(8,128)S(1)}, u32[]{:S(2)}, u32[]{:S(2)}) collective-permute-start(f32[328,128]{1,0:T(8,128)S(1)} %get-tuple-element.28.refs_2_.refs_0_.refs_4_.refs_3_), channel_id=1, source_target_pairs={{0,2},{2,0},{1,3},{3,1},{4,6},{6,4},{5,7},{7,5},{8,10},{10,8},{9,1... | collective-permute-start | bytes 503816 | tf_op jit(solution)/shard_map/ppermute | solution.py:39
  12.4 7.1 %collective-permute-start.2 = (f32[136,128]{1,0:T(8,128)S(1)}, f32[136,128]{1,0:T(8,128)S(1)}, u32[]{:S(2)}, u32[]{:S(2)}) collective-permute-start(f32[136,128]{1,0:T(8,128)S(1)} %get-tuple-element.33), channel_id=1, source_target_pairs={{0,24},{4,28},{8,16},{12,20},{16,8},{20,12},{24,0},{28,4},{1,25},{... | collective-permute-start | bytes 208904 | tf_op jit(solution)/shard_map/ppermute | solution.py:39
  16.6 5.5 %collective-permute-start.3 = (f32[136,128]{1,0:T(8,128)S(1)}, f32[136,128]{1,0:T(8,128)S(1)}, u32[]{:S(2)}, u32[]{:S(2)}) collective-permute-start(f32[136,128]{1,0:T(8,128)S(1)} %get-tuple-element.34), channel_id=1, source_target_pairs={{0,16},{4,20},{8,24},{12,28},{16,0},{20,4},{24,8},{28,12},{1,17},{... | collective-permute-start | bytes 208904 | tf_op jit(solution)/shard_map/ppermute | solution.py:39
  16.6 5.5 %collective-permute-start.4 = (f32[136,128]{1,0:T(8,128)S(1)}, f32[136,128]{1,0:T(8,128)S(1)}, u32[]{:S(2)}, u32[]{:S(2)}) collective-permute-start(f32[136,128]{1,0:T(8,128)S(1)} %get-tuple-element.35), channel_id=1, source_target_pairs={{0,8},{4,12},{8,0},{12,4},{16,24},{20,28},{24,16},{28,20},{1,9},{5... | collective-permute-start | bytes 208904 | tf_op jit(solution)/shard_map/ppermute | solution.py:39
  22.0 8.3 %copy-start = (f32[328,128]{1,0:T(8,128)S(1)}, f32[328,128]{1,0:T(8,128)}, u32[]{:S(2)}) copy-start(f32[328,128]{1,0:T(8,128)} %get-tuple-element.29.refs_11_.refs_7_.refs_3_) | copy-start | bytes 503812
  22.1 6.8 %collective-permute-start.7 = (f32[136,128]{1,0:T(8,128)S(1)}, f32[136,128]{1,0:T(8,128)S(1)}, u32[]{:S(2)}, u32[]{:S(2)}) collective-permute-start(f32[136,128]{1,0:T(8,128)S(1)} %merge.2.refs_6_), channel_id=1, source_target_pairs={{0,24},{4,28},{8,16},{12,20},{16,8},{20,12},{24,0},{28,4},{1,25},{... | collective-permute-start | bytes 208904 | tf_op jit(solution)/shard_map/ppermute | solution.py:39
  24.7 5.6 %collective-permute-start.6 = (f32[136,128]{1,0:T(8,128)S(1)}, f32[136,128]{1,0:T(8,128)S(1)}, u32[]{:S(2)}, u32[]{:S(2)}) collective-permute-start(f32[136,128]{1,0:T(8,128)S(1)} %merge.2.refs_6_), channel_id=1, source_target_pairs={{0,16},{4,20},{8,24},{12,28},{16,0},{20,4},{24,8},{28,12},{1,17},{... | collective-permute-start | bytes 208904 | tf_op jit(solution)/shard_map/ppermute | solution.py:39
  24.7 5.6 %collective-permute-start.5 = (f32[136,128]{1,0:T(8,128)S(1)}, f32[136,128]{1,0:T(8,128)S(1)}, u32[]{:S(2)}, u32[]{:S(2)}) collective-permute-start(f32[136,128]{1,0:T(8,128)S(1)} %merge.2.refs_6_), channel_id=1, source_target_pairs={{0,8},{4,12},{8,0},{12,4},{16,24},{20,28},{24,16},{28,20},{1,9},{5... | collective-permute-start | bytes 208904 | tf_op jit(solution)/shard_map/ppermute | solution.py:39
  46.4 27.0 %collective-permute-start.9 = (f32[1040,128]{1,0:T(8,128)S(1)}, f32[1040,128]{1,0:T(8,128)S(1)}, u32[]{:S(2)}, u32[]{:S(2)}) collective-permute-start(f32[1040,128]{1,0:T(8,128)S(1)} %get-tuple-element.39.refs_2_.refs_0_), channel_id=1, source_target_pairs={{0,2},{2,0},{1,3},{3,1},{4,6},{6,4},{5,7},{7,5},{8,10},{10,8},{9,1... | collective-permute-start | bytes 1597448 | tf_op jit(solution)/shard_map/ppermute | solution.py:39
  46.7 6.9 %collective-permute-start.10 = (f32[136,128]{1,0:T(8,128)S(1)}, f32[136,128]{1,0:T(8,128)S(1)}, u32[]{:S(2)}, u32[]{:S(2)}) collective-permute-start(f32[136,128]{1,0:T(8,128)S(1)} %get-tuple-element.41), channel_id=1, source_target_pairs={{0,24},{4,28},{8,16},{12,20},{16,8},{20,12},{24,0},{28,4},{1,25},{... | collective-permute-start | bytes 208904 | tf_op jit(solution)/shard_map/ppermute | solution.py:39
  48.1 7.5 %collective-permute-start.11 = (f32[136,128]{1,0:T(8,128)S(1)}, f32[136,128]{1,0:T(8,128)S(1)}, u32[]{:S(2)}, u32[]{:S(2)}) collective-permute-start(f32[136,128]{1,0:T(8,128)S(1)} %get-tuple-element.42), channel_id=1, source_target_pairs={{0,16},{4,20},{8,24},{12,28},{16,0},{20,4},{24,8},{28,12},{1,17},{... | collective-permute-start | bytes 208904 | tf_op jit(solution)/shard_map/ppermute | solution.py:39
  48.9 6.8 %collective-permute-start.12 = (f32[136,128]{1,0:T(8,128)S(1)}, f32[136,128]{1,0:T(8,128)S(1)}, u32[]{:S(2)}, u32[]{:S(2)}) collective-permute-start(f32[136,128]{1,0:T(8,128)S(1)} %get-tuple-element.43), channel_id=1, source_target_pairs={{0,8},{4,12},{8,0},{12,4},{16,24},{20,28},{24,16},{28,20},{1,9},{5... | collective-permute-start | bytes 208904 | tf_op jit(solution)/shard_map/ppermute | solution.py:39
  55.8 7.0 %collective-permute-start.15 = (f32[136,128]{1,0:T(8,128)S(1)}, f32[136,128]{1,0:T(8,128)S(1)}, u32[]{:S(2)}, u32[]{:S(2)}) collective-permute-start(f32[136,128]{1,0:T(8,128)S(1)} %merge.3.refs_0_), channel_id=1, source_target_pairs={{0,24},{4,28},{8,16},{12,20},{16,8},{20,12},{24,0},{28,4},{1,25},{... | collective-permute-start | bytes 208904 | tf_op jit(solution)/shard_map/ppermute | solution.py:39
  57.4 7.3 %collective-permute-start.14 = (f32[136,128]{1,0:T(8,128)S(1)}, f32[136,128]{1,0:T(8,128)S(1)}, u32[]{:S(2)}, u32[]{:S(2)}) collective-permute-start(f32[136,128]{1,0:T(8,128)S(1)} %merge.3.refs_0_), channel_id=1, source_target_pairs={{0,16},{4,20},{8,24},{12,28},{16,0},{20,4},{24,8},{28,12},{1,17},{... | collective-permute-start | bytes 208904 | tf_op jit(solution)/shard_map/ppermute | solution.py:39
  57.4 7.3 %collective-permute-start.13 = (f32[136,128]{1,0:T(8,128)S(1)}, f32[136,128]{1,0:T(8,128)S(1)}, u32[]{:S(2)}, u32[]{:S(2)}) collective-permute-start(f32[136,128]{1,0:T(8,128)S(1)} %merge.3.refs_0_), channel_id=1, source_target_pairs={{0,8},{4,12},{8,0},{12,4},{16,24},{20,28},{24,16},{28,20},{1,9},{5... | collective-permute-start | bytes 208904 | tf_op jit(solution)/shard_map/ppermute | solution.py:39
  64.8 8.6 %collective-permute-start.16 = (f32[136,512]{1,0:T(8,128)S(1)}, f32[136,512]{1,0:T(8,128)S(1)}, u32[]{:S(2)}, u32[]{:S(2)}) collective-permute-start(f32[136,512]{1,0:T(8,128)S(1)} %join.1.refs_5_), channel_id=1, source_target_pairs={{0,2},{2,0},{1,3},{3,1},{4,6},{6,4},{5,7},{7,5},{8,10},{10,8},{9,1... | collective-permute-start | bytes 835592 | tf_op jit(solution)/shard_map/ppermute | solution.py:39
  68.6 4.9 %copy-start.5 = (f32[520,128]{1,0:T(8,128)}, f32[520,128]{1,0:T(8,128)S(1)}, u32[]{:S(2)}) copy-start(f32[520,128]{1,0:T(8,128)S(1)} %get-tuple-element.47.refs_3_) | copy-start | bytes 798724
  73.5 13.2 %collective-permute-start.17 = (f32[1040,128]{1,0:T(8,128)S(1)}, f32[1040,128]{1,0:T(8,128)S(1)}, u32[]{:S(2)}, u32[]{:S(2)}) collective-permute-start(f32[1040,128]{1,0:T(8,128)S(1)} %mate_parts.1), channel_id=1, source_target_pairs={{0,4},{4,0},{8,12},{12,8},{16,20},{20,16},{24,28},{28,24},{1,5},{5... | collective-permute-start | bytes 1597448 | tf_op jit(solution)/shard_map/ppermute | solution.py:39
  73.6 13.2 %collective-permute-start.18 = (f32[520,128]{1,0:T(8,128)}, f32[520,128]{1,0:T(8,128)}, u32[]{:S(2)}, u32[]{:S(2)}) collective-permute-start(f32[520,128]{1,0:T(8,128)} %get-tuple-element.48), channel_id=1, source_target_pairs={{0,4},{4,0},{8,12},{12,8},{16,20},{20,16},{24,28},{28,24},{1,5},{5... | collective-permute-start | bytes 798728 | tf_op jit(solution)/shard_map/ppermute | solution.py:39
  75.5 11.3 %collective-permute-start.19 = (f32[520,128]{1,0:T(8,128)S(1)}, f32[520,128]{1,0:T(8,128)}, u32[]{:S(2)}, u32[]{:S(2)}) collective-permute-start(f32[520,128]{1,0:T(8,128)S(1)} %other_backward.3), channel_id=1, source_target_pairs={{0,4},{4,0},{8,12},{12,8},{16,20},{20,16},{24,28},{28,24},{1,5},{5... | collective-permute-start | bytes 798728 | tf_op jit(solution)/shard_map/ppermute | solution.py:39
  75.6 11.1 %all-to-all-start.1 = ((f32[32,8,128]{2,1,0:T(8,128)}), f32[32,8,128]{2,1,0:T(8,128)S(1)}, u32[]{:S(2)}, u32[]{:S(2)}) async-start(f32[32,8,128]{2,1,0:T(8,128)} %get-tuple-element.46.refs_3_.refs_4_), calls=%async_computation.1 | async-start | bytes 262144 | tf_op jit(solution)/shard_map/all_to_all | solution.py:532
  86.7 1.0 %copy-start.6 = (f32[520,128]{1,0:T(8,128)S(1)}, f32[520,128]{1,0:T(8,128)}, u32[]{:S(2)}) copy-start(f32[520,128]{1,0:T(8,128)} %copy-done.5) | copy-start | bytes 798724

commit v11 on v10

--- a/solution.py
+++ b/solution.py
@@ -66,7 +66,10 @@
 
     return pl.pallas_call(
         without_after,
-        out_shape=[jax.ShapeDtypeStruct(shape, jnp.float32) for shape in out_shapes],
+        out_shape=[
+            shape if hasattr(shape, "dtype") else jax.ShapeDtypeStruct(shape, jnp.float32)
+            for shape in out_shapes
+        ],
         in_specs=[pl.BlockSpec(memory_space=space) for space in spaces],
         out_specs=[pl.BlockSpec(memory_space=pltpu.VMEM) for _ in out_shapes],
         scratch_shapes=scratch,
@@ -310,8 +313,7 @@
         visible = jnp.broadcast_to(positions >= page_start, scores.shape)
         return jnp.where(visible, scores, MASKED), visible
 
-    def all_weights(state_refs, query_refs):
-        all_queries, positions = read_queries(query_refs), read_positions(query_refs)
+    def all_weights(state_refs, all_queries, positions):
         pages = [page_scores(ref, all_queries, positions) for ref in state_refs]
         row_max = jnp.max(pages[0][0], axis=0, keepdims=True)
         for scores, _ in pages[1:]:
@@ -326,9 +328,9 @@
             weights_out[at * slot_rows : (at + 1) * slot_rows, :] = part
         max_out[...] = jnp.broadcast_to(row_max, (TAIL, query_rows))
 
-    def forward(state_refs, query_refs, chunk_outs, weights_out, max_out, chunks):
+    def forward(state_refs, all_queries, positions, chunk_outs, weights_out, max_out, chunks):
         rank, _, _ = places()
-        weights, row_max = all_weights(state_refs, query_refs)
+        weights, row_max = all_weights(state_refs, all_queries, positions)
         store_weights(weights, row_max, weights_out, max_out)
         row_total = jnp.zeros_like(row_max)
         row_sum = jnp.zeros((width, query_rows), jnp.float32)
@@ -355,11 +357,21 @@
         state_refs, refs = refs[:2], refs[2:]
         query_refs, refs = refs[:query_devices], refs[query_devices:]
         chunk_outs, refs = refs[:ranks], refs[ranks:]
-        forward(state_refs, query_refs, chunk_outs, *refs)
+        forward(
+            state_refs, read_queries(query_refs), read_positions(query_refs), chunk_outs, *refs
+        )
+
+    def split_body(*refs):
+        query_refs, (high_out, low_out, positions_out) = refs[:query_devices], refs[query_devices:]
+        high_out[...], low_out[...] = read_queries(query_refs)
+        positions_out[...] = jnp.broadcast_to(read_positions(query_refs), (TAIL, query_rows))
+
+    half_shape = jax.ShapeDtypeStruct((query_rows, width), jnp.bfloat16)
+    split_shapes = [half_shape, half_shape, (TAIL, query_rows)]
 
     def next_body(*refs):
         state_refs, refs = refs[:2], refs[2:]
-        query_refs, refs = refs[:query_devices], refs[query_devices:]
+        (high_ref, low_ref, positions_ref), refs = refs[:3], refs[3:]
         grad_refs, refs = refs[:2], refs[2:]
         tile_refs, refs = refs[: len(tiles)], refs[len(tiles) :]
         state_outs, refs = parts_of(refs[:1]), refs[1:]
@@ -370,7 +382,9 @@
             state_outs[at][:slot_rows, :] = keys
             state_outs[at][slot_rows : 2 * slot_rows, :] = values
             state_outs[at][2 * slot_rows :, :] = bias
-        forward(state_outs, query_refs, chunk_outs, *refs)
+        forward(
+            state_outs, (high_ref[...], low_ref[...]), positions_ref[0:1, :], chunk_outs, *refs
+        )
 
     def merge_body(*refs):
         query_refs, refs = refs[:query_devices], refs[query_devices:]
@@ -430,12 +444,15 @@
 
     def backward_body(weights_ref, max_ref, *refs):
         state_refs, refs = parts_of(refs[: len(states)]), refs[len(states) :]
-        query_refs, refs = refs[:query_devices], refs[query_devices:]
+        query_refs, refs = refs[: len(head_queries)], refs[len(head_queries) :]
         merged_refs, refs = refs[: len(all_merged)], refs[len(all_merged) :]
         grad_outs, (squares_out, *scratch) = refs[:2], refs[2:]
         joined = join_chunks(merged_refs, *scratch) if scratch else merged_refs[0][...]
         residual, row_max, row_total, row_delta = split_joined(joined)
-        all_queries = read_queries(query_refs)
+        if head_queries is query_parts:
+            all_queries = read_queries(query_refs)
+        else:
+            all_queries = (query_refs[0][...], query_refs[1][...])
         factor = jnp.exp(max_ref[0:1, :] - row_max) / row_total
         squares = []
         for at, (ref, out) in enumerate(zip(state_refs, grad_outs)):
@@ -474,6 +491,7 @@
 
     for repeat in range(STEPS):
         last = repeat == STEPS - 1
+        head_queries = split_queries[:2] if repeat else query_parts
         if repeat == 0:
             *chunk_parts, weights, maxima = call(
                 first_body,
@@ -489,7 +507,7 @@
                 [(CORES * packed_rows, width)] + forward_shapes,
                 "update_forward",
                 2 * matmul_cost,
-                states + query_parts + grads + tiles,
+                states + split_queries + grads + tiles,
                 chunk_scratch,
             )
             states = [new_state]
@@ -523,41 +541,45 @@
             packed_shapes + [(devices, TAIL, width)],
             "backward",
             3 * matmul_cost,
-            [weights, maxima] + states + query_parts + list(all_merged),
+            [weights, maxima] + states + head_queries + list(all_merged),
             scratch=() if last and repeat else chunk_scratch,
             after=[part for parts in query_parts_of[1:] for part in parts],
         )
         grads = [own_grad, mate_grad]
+        if repeat == 0:
+            split_queries = call(
+                split_body, split_shapes, "split_queries", 2**28, query_parts, after=[squares]
+            )
+            split_queries = list(split_queries)
         tiles = [
             lax.all_to_all(
                 squares, ("page", "query", "head"), split_axis=0, concat_axis=0, tiled=True
             )
         ]
 
+    (for_mate,) = call(
+        mate_body,
+        [(query_devices * packed_rows, width)],
+        "mate_parts",
+        2**28,
+        new_states,
+        after=[squares],
+    )
+    from_mate = exchange(for_mate, page=1)
     all_grads = [own_grad, exchange(mate_grad, page=1)]
     for turn in range(1, query_devices):
-        operands = [new_states[turn], all_joined[turn]]
         page_grads = [
             call(
                 page_body(at),
                 [(packed_rows, width)],
                 "other_backward",
-                0,
-                operands + query_parts_of[turn],
-                after=[squares],
+                3 * matmul_cost // 2,
+                [new_states[turn], all_joined[turn]] + query_parts_of[turn],
+                after=tiles,
             )[0]
             for at in reversed(range(CORES))
         ]
         all_grads += [page_grads[1], exchange(page_grads[0], page=1)]
-    (for_mate,) = call(
-        mate_body,
-        [(query_devices * packed_rows, width)],
-        "mate_parts",
-        0,
-        new_states,
-        after=all_joined[1:] + [squares],
-    )
-    from_mate = exchange(for_mate, page=1)
 
     def last_body(*refs):
         state_refs, (mate_ref, *refs) = refs[:query_devices], refs[query_devices:]

time: 90.1 us -> 85.7 us (0.951)
  blocking collectives: 12.6 us -> 0 us
  waiting for transfers between devices: 33.7 us -> 38 us
  starting transfers between devices: 26.3 us -> 30.4 us
  local copies, waits for them, and re-layouts: 0.99 us -> 0.04 us
    all_to_all x1 -> x0, blocking collectives: 12.6 us -> none  [direct_per_device(): lax.all_to_all(squares, ('page', 'query', 'head'), split_axis=0, concat_a...]
    all_to_all x1 -> x2, waiting for transfers between devices: 7 us -> 16.1 us  [direct_per_device(): lax.all_to_all(squares, ('page', 'query', 'head'), split_axis=0, concat_a...]
    ppermute x20, waiting for transfers between devices: 26.7 us -> 21.9 us  [exchange(): return lax.ppermute(value, axes, pairs)]
    all_to_all x1 -> x2, starting transfers between devices: 2.72 us -> 6.95 us  [direct_per_device(): lax.all_to_all(squares, ('page', 'query', 'head'), split_axis=0, concat_a...]
    unnamed x20 -> x18, local copies, waits for them, and re-layouts: 0.99 us -> 0.04 us
    pallas_call x13 -> x14, Pallas kernels: 15.5 us -> 16.1 us  [call(): pl.pallas_call(without_after, out_shape=[shape if hasattr(shape, 'dtype')...]
  transfers between devices with their start and end apart: 21 -> 22, of which waited for: 11 -> 12; matrix products, arithmetic and copies ran while one was open for 0% -> 0% of each run, Pallas kernels for 9% -> 9%
where the time goes in v11:
time: 85.7 us; the launch traced here: 85.4 us
  waiting for transfers between devices  38 us (44%)
  starting transfers between devices  30.4 us (35%)
  Pallas kernels  16.1 us (19%)
    ppermute x20, starting transfers between devices, exchange(): return lax.ppermute(value, axes, pairs)  23.5 us
    ppermute x20, waiting for transfers between devices, exchange(): return lax.ppermute(value, axes, pairs)  21.9 us
    pallas_call x14, Pallas kernels, call(): pl.pallas_call(without_after, out_shape=[shape if hasattr(shape, 'dtype')...  16.1 us
    all_to_all x2, waiting for transfers between devices, direct_per_device(): lax.all_to_all(squares, ('page', 'query', 'head'), split_axis=0, concat_a...  16.1 us
    all_to_all x2, starting transfers between devices, direct_per_device(): lax.all_to_all(squares, ('page', 'query', 'head'), split_axis=0, concat_a...  6.95 us
  transfers between devices with their start and end apart: 22, of which 12 were waited for; matrix products, arithmetic and copies ran while one was open for 0% of the time, Pallas kernels for 9%

profile of v11, /device:TPU:0, one launch (start us, length us, event | category | flops | bytes accessed | tf_op | source)
XLA Modules:
  0.0 85.4 jit_solution(17482382146762709850)
XLA Ops:
  0.7 2.0 %pack.1 = (f32[520,128]{1,0:T(8,128)}, f32[328,128]{1,0:T(8,128)}) custom-call(f32[4,256,128]{2,1,0:T(8,128)} %refs_0_.3, f32[4,256,128]{2,1,0:T(8,128)} %refs_1_.3, f32[4,256,128]{2,1,0:T(8,128)} %refs_2_.3, f32[4,256]{1,0:T(4,128)} %refs_3_.3, f32[4,256,128]{2,1,0:T(8,128)} %refs_4_.3, s32[4,256]{1,0:T(4,128)} %refs_5_.3, s32[8]{0:T(128)} %refs_6_.3), custom_call_target="tpu_custom_call" | custom-call | flops 1048576 | bytes 1048576 | tf_op jit(solution)/shard_map/pack/pallas_call | solution.py:67
  2.7 0.0 copy-start.7
  2.7 0.5 collective-permute-start
  3.3 2.6 %collective-permute-start.1 = (f32[328,128]{1,0:T(8,128)}, f32[328,128]{1,0:T(8,128)S(1)}, u32[]{:S(2)}, u32[]{:S(2)}) collective-permute-start(f32[328,128]{1,0:T(8,128)} %get-tuple-element.32.refs_11_.refs_7_.refs_3_), channel_id=1, source_target_pairs={{0,2},{2,0},{1,3},{3,1},{4,6},{6,4},{5,7},{7,5},{8,10},{10,8},{9,1... | collective-permute-start | bytes 503816 | tf_op jit(solution)/shard_map/ppermute | solution.py:39
  5.9 0.7 own.1
  6.6 0.5 collective-permute-start.8
  7.0 4.2 %collective-permute-done.1.refs_3_.refs_1_.refs_5_ = f32[328,128]{1,0:T(8,128)S(1)} collective-permute-done((f32[328,128]{1,0:T(8,128)}, f32[328,128]{1,0:T(8,128)S(1)}, u32[]{:S(2)}, u32[]{:S(2)}) %collective-permute-start.1) | collective-permute-done | bytes 167968 | tf_op jit(solution)/shard_map/ppermute | solution.py:39
  11.2 0.0 collective-permute-done.refs_1_.refs_3_
  11.2 1.2 %forward.1 = (f32[136,128]{1,0:T(8,128)S(1)}, f32[136,128]{1,0:T(8,128)S(1)}, f32[136,128]{1,0:T(8,128)S(1)}, f32[136,128]{1,0:T(8,128)S(1)}, f32[512,512]{1,0:T(8,128)S(1)}, /*index=5*/f32[8,512]{1,0:T(8,128)S(1)}) custom-call(f32[520,128]{1,0:T(8,128)S(1)} %get-tuple-element.29.refs_0_.refs_2_, f32[520,128]{1,0:T(8,128)S(1)} %collective-permute-done.refs_1_.refs_3_, ...), custom_call_target="tpu_custom_call" | custom-call | flops 402653184 | bytes 1048576 | tf_op jit(solution)/shard_map/forward/pallas_call | solution.py:67
  12.4 4.1 %collective-permute-start.2 = (f32[136,128]{1,0:T(8,128)S(1)}, f32[136,128]{1,0:T(8,128)S(1)}, u32[]{:S(2)}, u32[]{:S(2)}) collective-permute-start(f32[136,128]{1,0:T(8,128)S(1)} %get-tuple-element.36), channel_id=1, source_target_pairs={{0,24},{4,28},{8,16},{12,20},{16,8},{20,12},{24,0},{28,4},{1,25},{... | collective-permute-start | bytes 208904 | tf_op jit(solution)/shard_map/ppermute | solution.py:39
  16.6 0.0 collective-permute-start.3
  16.6 0.6 collective-permute-start.4
  17.2 2.4 %collective-permute-done.2.refs_3_ = f32[136,128]{1,0:T(8,128)S(1)} collective-permute-done((f32[136,128]{1,0:T(8,128)S(1)}, f32[136,128]{1,0:T(8,128)S(1)}, u32[]{:S(2)}, u32[]{:S(2)}) %collective-permute-start.2) | collective-permute-done | bytes 69664 | tf_op jit(solution)/shard_map/ppermute | solution.py:39
  19.6 2.4 %collective-permute-done.3.refs_4_ = f32[136,128]{1,0:T(8,128)S(1)} collective-permute-done((f32[136,128]{1,0:T(8,128)S(1)}, f32[136,128]{1,0:T(8,128)S(1)}, u32[]{:S(2)}, u32[]{:S(2)}) %collective-permute-start.3) | collective-permute-done | bytes 69664 | tf_op jit(solution)/shard_map/ppermute | solution.py:39
  22.0 0.0 collective-permute-done.4.refs_5_
  22.0 0.1 merge.2.refs_6_
  22.1 2.6 %collective-permute-start.7 = (f32[136,128]{1,0:T(8,128)S(1)}, f32[136,128]{1,0:T(8,128)S(1)}, u32[]{:S(2)}, u32[]{:S(2)}) collective-permute-start(f32[136,128]{1,0:T(8,128)S(1)} %merge.2.refs_6_), channel_id=1, source_target_pairs={{0,24},{4,28},{8,16},{12,20},{16,8},{20,12},{24,0},{28,4},{1,25},{... | collective-permute-start | bytes 208904 | tf_op jit(solution)/shard_map/ppermute | solution.py:39
  24.7 1.8 %collective-permute-start.5 = (f32[136,128]{1,0:T(8,128)S(1)}, f32[136,128]{1,0:T(8,128)S(1)}, u32[]{:S(2)}, u32[]{:S(2)}) collective-permute-start(f32[136,128]{1,0:T(8,128)S(1)} %merge.2.refs_6_), channel_id=1, source_target_pairs={{0,8},{4,12},{8,0},{12,4},{16,24},{20,28},{24,16},{28,20},{1,9},{5... | collective-permute-start | bytes 208904 | tf_op jit(solution)/shard_map/ppermute | solution.py:39
  26.6 0.0 collective-permute-done.8.refs_10_.refs_6_.refs_2_
  26.6 2.4 %collective-permute-done.7.refs_9_ = f32[136,128]{1,0:T(8,128)S(1)} collective-permute-done((f32[136,128]{1,0:T(8,128)S(1)}, f32[136,128]{1,0:T(8,128)S(1)}, u32[]{:S(2)}, u32[]{:S(2)}) %collective-permute-start.7) | collective-permute-done | bytes 69664 | tf_op jit(solution)/shard_map/ppermute | solution.py:39
  29.0 1.4 %collective-permute-done.6.refs_8_ = f32[136,128]{1,0:T(8,128)S(1)} collective-permute-done((f32[136,128]{1,0:T(8,128)S(1)}, f32[136,128]{1,0:T(8,128)S(1)}, u32[]{:S(2)}, u32[]{:S(2)}) %collective-permute-start.6) | collective-permute-done | bytes 69664 | tf_op jit(solution)/shard_map/ppermute | solution.py:39
  30.4 2.8 %backward.2 = (f32[520,128]{1,0:T(8,128)S(1)}, f32[520,128]{1,0:T(8,128)S(1)}, f32[32,8,128]{2,1,0:T(8,128)}) custom-call(f32[512,512]{1,0:T(8,128)S(1)} %get-tuple-element.33.refs_0_, f32[8,512]{1,0:T(8,128)S(1)} %get-tuple-element.34.refs_1_, f32[520,128]{1,0:T(8,128)S(1)} %get-tuple-element.29.refs_0_.refs_2_, ...), custom_call_target="tpu_custom_call" | custom-call | flops 603979776 | bytes 1048576 | tf_op jit(solution)/shard_map/backward/pallas_call | solution.py:67
  33.1 4.4 %all-to-all-start = ((f32[32,8,128]{2,1,0:T(8,128)}), f32[32,8,128]{2,1,0:T(8,128)S(1)}, u32[]{:S(2)}, u32[]{:S(2)}) async-start(f32[32,8,128]{2,1,0:T(8,128)} %get-tuple-element.39.refs_2_), calls=%async_computation | async-start | bytes 262144 | tf_op jit(solution)/shard_map/all_to_all | solution.py:555
  37.5 0.1 split_queries.1
  37.6 8.3 %all-to-all-done.refs_7_ = f32[32,8,128]{2,1,0:T(8,128)S(1)} async-done(((f32[32,8,128]{2,1,0:T(8,128)}), f32[32,8,128]{2,1,0:T(8,128)S(1)}, u32[]{:S(2)}, u32[]{:S(2)}) %all-to-all-start) | async-done | bytes 131104 | tf_op jit(solution)/shard_map/all_to_all | solution.py:555
  45.9 1.3 %update_forward.1 = (f32[1040,128]{1,0:T(8,128)S(1)}, f32[136,128]{1,0:T(8,128)S(1)}, f32[136,128]{1,0:T(8,128)S(1)}, f32[136,128]{1,0:T(8,128)S(1)}, f32[136,12...) custom-call(f32[520,128]{1,0:T(8,128)S(1)} %get-tuple-element.29.refs_0_.refs_2_, ...), custom_call_target="tpu_custom_call" | custom-call | flops 402653184 | bytes 1048576 | tf_op jit(solution)/shard_map/update_forward/pallas_call | solution.py:67
  47.3 0.3 collective-permute-start.9
  47.6 1.4 %collective-permute-start.10 = (f32[136,128]{1,0:T(8,128)S(1)}, f32[136,128]{1,0:T(8,128)S(1)}, u32[]{:S(2)}, u32[]{:S(2)}) collective-permute-start(f32[136,128]{1,0:T(8,128)S(1)} %get-tuple-element.49), channel_id=1, source_target_pairs={{0,24},{4,28},{8,16},{12,20},{16,8},{20,12},{24,0},{28,4},{1,25},{... | collective-permute-start | bytes 208904 | tf_op jit(solution)/shard_map/ppermute | solution.py:39
  49.0 0.8 collective-permute-start.11
  49.7 2.2 %collective-permute-start.12 = (f32[136,128]{1,0:T(8,128)S(1)}, f32[136,128]{1,0:T(8,128)S(1)}, u32[]{:S(2)}, u32[]{:S(2)}) collective-permute-start(f32[136,128]{1,0:T(8,128)S(1)} %get-tuple-element.51), channel_id=1, source_target_pairs={{0,8},{4,12},{8,0},{12,4},{16,24},{20,28},{24,16},{28,20},{1,9},{5... | collective-permute-start | bytes 208904 | tf_op jit(solution)/shard_map/ppermute | solution.py:39
  52.0 2.5 %collective-permute-done.10.refs_3_ = f32[136,128]{1,0:T(8,128)S(1)} collective-permute-done((f32[136,128]{1,0:T(8,128)S(1)}, f32[136,128]{1,0:T(8,128)S(1)}, u32[]{:S(2)}, u32[]{:S(2)}) %collective-permute-start.10) | collective-permute-done | bytes 69664 | tf_op jit(solution)/shard_map/ppermute | solution.py:39
  54.5 2.0 %collective-permute-done.11.refs_4_ = f32[136,128]{1,0:T(8,128)S(1)} collective-permute-done((f32[136,128]{1,0:T(8,128)S(1)}, f32[136,128]{1,0:T(8,128)S(1)}, u32[]{:S(2)}, u32[]{:S(2)}) %collective-permute-start.11) | collective-permute-done | bytes 69664 | tf_op jit(solution)/shard_map/ppermute | solution.py:39
  56.5 0.1 merge.3.refs_0_
  56.6 1.7 %collective-permute-start.15 = (f32[136,128]{1,0:T(8,128)S(1)}, f32[136,128]{1,0:T(8,128)S(1)}, u32[]{:S(2)}, u32[]{:S(2)}) collective-permute-start(f32[136,128]{1,0:T(8,128)S(1)} %merge.3.refs_0_), channel_id=1, source_target_pairs={{0,24},{4,28},{8,16},{12,20},{16,8},{20,12},{24,0},{28,4},{1,25},{... | collective-permute-start | bytes 208904 | tf_op jit(solution)/shard_map/ppermute | solution.py:39
  58.3 2.8 %collective-permute-start.13 = (f32[136,128]{1,0:T(8,128)S(1)}, f32[136,128]{1,0:T(8,128)S(1)}, u32[]{:S(2)}, u32[]{:S(2)}) collective-permute-start(f32[136,128]{1,0:T(8,128)S(1)} %merge.3.refs_0_), channel_id=1, source_target_pairs={{0,8},{4,12},{8,0},{12,4},{16,24},{20,28},{24,16},{28,20},{1,9},{5... | collective-permute-start | bytes 208904 | tf_op jit(solution)/shard_map/ppermute | solution.py:39
  61.1 2.5 %collective-permute-done.15.refs_3_ = f32[136,128]{1,0:T(8,128)S(1)} collective-permute-done((f32[136,128]{1,0:T(8,128)S(1)}, f32[136,128]{1,0:T(8,128)S(1)}, u32[]{:S(2)}, u32[]{:S(2)}) %collective-permute-start.15) | collective-permute-done | bytes 69664 | tf_op jit(solution)/shard_map/ppermute | solution.py:39
  63.6 2.0 %collective-permute-done.14.refs_2_ = f32[136,128]{1,0:T(8,128)S(1)} collective-permute-done((f32[136,128]{1,0:T(8,128)S(1)}, f32[136,128]{1,0:T(8,128)S(1)}, u32[]{:S(2)}, u32[]{:S(2)}) %collective-permute-start.14) | collective-permute-done | bytes 69664 | tf_op jit(solution)/shard_map/ppermute | solution.py:39
  65.6 0.1 join.1.refs_5_
  65.7 0.9 %collective-permute-start.18 = (f32[136,512]{1,0:T(8,128)S(1)}, f32[136,512]{1,0:T(8,128)S(1)}, u32[]{:S(2)}, u32[]{:S(2)}) collective-permute-start(f32[136,512]{1,0:T(8,128)S(1)} %join.1.refs_5_), channel_id=1, source_target_pairs={{0,2},{2,0},{1,3},{3,1},{4,6},{6,4},{5,7},{7,5},{8,10},{10,8},{9,1... | collective-permute-start | bytes 835592 | tf_op jit(solution)/shard_map/ppermute | solution.py:39
  66.6 2.8 %backward.3 = (f32[520,128]{1,0:T(8,128)S(1)}, f32[520,128]{1,0:T(8,128)S(1)}, f32[32,8,128]{2,1,0:T(8,128)}) custom-call(f32[512,512]{1,0:T(8,128)S(1)} %get-tuple-element.46.refs_0_, f32[8,512]{1,0:T(8,128)S(1)} %get-tuple-element.47.refs_1_, f32[1040,128]{1,0:T(8,128)S(1)} %get-tuple-element.45.refs_2_.refs_0_, ...), custom_call_target="tpu_custom_call" | custom-call | flops 603979776 | bytes 1048576 | tf_op jit(solution)/shard_map/backward/pallas_call | solution.py:67
  69.3 2.6 %all-to-all-start.1 = ((f32[32,8,128]{2,1,0:T(8,128)}), f32[32,8,128]{2,1,0:T(8,128)S(1)}, u32[]{:S(2)}, u32[]{:S(2)}) async-start(f32[32,8,128]{2,1,0:T(8,128)} %get-tuple-element.52.refs_2_), calls=%async_computation.1 | async-start | bytes 262144 | tf_op jit(solution)/shard_map/all_to_all | solution.py:555
  72.0 0.3 collective-permute-start.16
  72.3 0.3 collective-permute-start.17
  72.6 7.8 %all-to-all-done.1.refs_4_.refs_7_ = f32[32,8,128]{2,1,0:T(8,128)S(1)} async-done(((f32[32,8,128]{2,1,0:T(8,128)}), f32[32,8,128]{2,1,0:T(8,128)S(1)}, u32[]{:S(2)}, u32[]{:S(2)}) %all-to-all-start.1) | async-done | bytes 131104 | tf_op jit(solution)/shard_map/all_to_all | solution.py:555
  80.3 1.4 %other_backward.3 = f32[520,128]{1,0:T(8,128)S(1)} custom-call(f32[1040,128]{1,0:T(8,128)S(1)} %collective-permute-done.9.refs_1_.refs_0_, f32[136,512]{1,0:T(8,128)S(1)} %collective-permute-done.18.refs_1_, f32[328,128]{1,0:T(8,128)S(1)} %collective-permute-done.8.refs_10_.refs_6_.refs_2_, f32[328,128]{1,0:T(8,128)S(1)} %copy-done, ...), custom_call_target="tpu_custom_call" | custom-call | flops 301989888 | bytes 1048576 | tf_op jit(solution)/shard_map/other_backward/pallas_call | solution.py:67
  81.7 1.4 %other_backward.2.refs_5_ = f32[520,128]{1,0:T(8,128)S(1)} custom-call(f32[1040,128]{1,0:T(8,128)S(1)} %collective-permute-done.9.refs_1_.refs_0_, f32[136,512]{1,0:T(8,128)S(1)} %collective-permute-done.18.refs_1_, f32[328,128]{1,0:T(8,128)S(1)} %collective-permute-done.8.refs_10_.refs_6_.refs_2_, f32[328,128]{1,0:T(8,128)S(1)} %copy-done, ...), custom_call_target="tpu_custom_call" | custom-call | flops 301989888 | bytes 1048576 | tf_op jit(solution)/shard_map/other_backward/pallas_call | solution.py:67
  83.2 0.1 collective-permute-done.19.refs_6_
  83.3 2.1 %last_update.1 = (f32[4,256,128]{2,1,0:T(8,128)}, f32[4,256,128]{2,1,0:T(8,128)}, f32[4,256]{1,0:T(4,128)}) custom-call(f32[1040,128]{1,0:T(8,128)S(1)} %get-tuple-element.45.refs_2_.refs_0_, f32[1040,128]{1,0:T(8,128)S(1)} %collective-permute-done.9.refs_1_.refs_0_, f32[1040,128]{1,0:T(8,128)S(1)} %collective-permute-done.16.refs_2_, ...), custom_call_target="tpu_custom_call" | custom-call | flops 1048576 | bytes 1048576 | tf_op jit(solution)/shard_map/last_update/pallas_call | solution.py:67
  (28 shorter events, 0.1 us)
Async XLA Ops:
  0.6 5.2 %copy-start.4 = (f32[4,256,128]{2,1,0:T(8,128)S(1)}, f32[4,256,128]{2,1,0:T(8,128)}, u32[]{:S(2)}) copy-start(f32[4,256,128]{2,1,0:T(8,128)} %refs_4_.3) | copy-start | bytes 1572868
  0.6 5.2 %copy-start.3 = (f32[4,256,128]{2,1,0:T(8,128)S(1)}, f32[4,256,128]{2,1,0:T(8,128)}, u32[]{:S(2)}) copy-start(f32[4,256,128]{2,1,0:T(8,128)} %refs_2_.3) | copy-start | bytes 1572868
  0.7 5.2 %copy-start.2 = (f32[4,256,128]{2,1,0:T(8,128)S(1)}, f32[4,256,128]{2,1,0:T(8,128)}, u32[]{:S(2)}) copy-start(f32[4,256,128]{2,1,0:T(8,128)} %refs_1_.3) | copy-start | bytes 1572868
  0.7 5.2 %copy-start.1 = (f32[4,256,128]{2,1,0:T(8,128)S(1)}, f32[4,256,128]{2,1,0:T(8,128)}, u32[]{:S(2)}) copy-start(f32[4,256,128]{2,1,0:T(8,128)} %refs_0_.3) | copy-start | bytes 1572868
  0.7 5.2 %copy-start.5 = (f32[4,256]{1,0:T(4,128)S(1)}, f32[4,256]{1,0:T(4,128)}, u32[]{:S(2)}) copy-start(f32[4,256]{1,0:T(4,128)} %refs_3_.3) | copy-start | bytes 12292
  0.7 5.2 %copy-start.6 = (s32[4,256]{1,0:T(4,128)S(1)}, s32[4,256]{1,0:T(4,128)}, u32[]{:S(2)}) copy-start(s32[4,256]{1,0:T(4,128)} %refs_5_.3) | copy-start | bytes 12292
  2.7 3.2 %copy-start.7 = (s32[8]{0:T(128)S(1)}, s32[8]{0:T(128)}, u32[]{:S(2)}) copy-start(s32[8]{0:T(128)} %refs_6_.3) | copy-start | bytes 100
  2.7 8.5 %collective-permute-start = (f32[520,128]{1,0:T(8,128)}, f32[520,128]{1,0:T(8,128)S(1)}, u32[]{:S(2)}, u32[]{:S(2)}) collective-permute-start(f32[520,128]{1,0:T(8,128)} %get-tuple-element.30), channel_id=1, source_target_pairs={{0,4},{4,0},{8,12},{12,8},{16,20},{20,16},{24,28},{28,24},{1,5},{5... | collective-permute-start | bytes 798728 | tf_op jit(solution)/shard_map/ppermute | solution.py:39
  3.3 7.9 %collective-permute-start.1 = (f32[328,128]{1,0:T(8,128)}, f32[328,128]{1,0:T(8,128)S(1)}, u32[]{:S(2)}, u32[]{:S(2)}) collective-permute-start(f32[328,128]{1,0:T(8,128)} %get-tuple-element.32.refs_11_.refs_7_.refs_3_), channel_id=1, source_target_pairs={{0,2},{2,0},{1,3},{3,1},{4,6},{6,4},{5,7},{7,5},{8,10},{10,8},{9,1... | collective-permute-start | bytes 503816 | tf_op jit(solution)/shard_map/ppermute | solution.py:39
  6.6 20.0 %collective-permute-start.8 = (f32[328,128]{1,0:T(8,128)S(1)}, f32[328,128]{1,0:T(8,128)S(1)}, u32[]{:S(2)}, u32[]{:S(2)}) collective-permute-start(f32[328,128]{1,0:T(8,128)S(1)} %get-tuple-element.31.refs_2_.refs_0_.refs_4_), channel_id=1, source_target_pairs={{0,2},{2,0},{1,3},{3,1},{4,6},{6,4},{5,7},{7,5},{8,10},{10,8},{9,1... | collective-permute-start | bytes 503816 | tf_op jit(solution)/shard_map/ppermute | solution.py:39
  12.4 7.1 %collective-permute-start.2 = (f32[136,128]{1,0:T(8,128)S(1)}, f32[136,128]{1,0:T(8,128)S(1)}, u32[]{:S(2)}, u32[]{:S(2)}) collective-permute-start(f32[136,128]{1,0:T(8,128)S(1)} %get-tuple-element.36), channel_id=1, source_target_pairs={{0,24},{4,28},{8,16},{12,20},{16,8},{20,12},{24,0},{28,4},{1,25},{... | collective-permute-start | bytes 208904 | tf_op jit(solution)/shard_map/ppermute | solution.py:39
  16.6 5.5 %collective-permute-start.3 = (f32[136,128]{1,0:T(8,128)S(1)}, f32[136,128]{1,0:T(8,128)S(1)}, u32[]{:S(2)}, u32[]{:S(2)}) collective-permute-start(f32[136,128]{1,0:T(8,128)S(1)} %get-tuple-element.37), channel_id=1, source_target_pairs={{0,16},{4,20},{8,24},{12,28},{16,0},{20,4},{24,8},{28,12},{1,17},{... | collective-permute-start | bytes 208904 | tf_op jit(solution)/shard_map/ppermute | solution.py:39
  16.6 5.5 %collective-permute-start.4 = (f32[136,128]{1,0:T(8,128)S(1)}, f32[136,128]{1,0:T(8,128)S(1)}, u32[]{:S(2)}, u32[]{:S(2)}) collective-permute-start(f32[136,128]{1,0:T(8,128)S(1)} %get-tuple-element.38), channel_id=1, source_target_pairs={{0,8},{4,12},{8,0},{12,4},{16,24},{20,28},{24,16},{28,20},{1,9},{5... | collective-permute-start | bytes 208904 | tf_op jit(solution)/shard_map/ppermute | solution.py:39
  22.0 8.3 %copy-start = (f32[328,128]{1,0:T(8,128)S(1)}, f32[328,128]{1,0:T(8,128)}, u32[]{:S(2)}) copy-start(f32[328,128]{1,0:T(8,128)} %get-tuple-element.32.refs_11_.refs_7_.refs_3_) | copy-start | bytes 503812
  22.1 6.8 %collective-permute-start.7 = (f32[136,128]{1,0:T(8,128)S(1)}, f32[136,128]{1,0:T(8,128)S(1)}, u32[]{:S(2)}, u32[]{:S(2)}) collective-permute-start(f32[136,128]{1,0:T(8,128)S(1)} %merge.2.refs_6_), channel_id=1, source_target_pairs={{0,24},{4,28},{8,16},{12,20},{16,8},{20,12},{24,0},{28,4},{1,25},{... | collective-permute-start | bytes 208904 | tf_op jit(solution)/shard_map/ppermute | solution.py:39
  24.7 5.6 %collective-permute-start.6 = (f32[136,128]{1,0:T(8,128)S(1)}, f32[136,128]{1,0:T(8,128)S(1)}, u32[]{:S(2)}, u32[]{:S(2)}) collective-permute-start(f32[136,128]{1,0:T(8,128)S(1)} %merge.2.refs_6_), channel_id=1, source_target_pairs={{0,16},{4,20},{8,24},{12,28},{16,0},{20,4},{24,8},{28,12},{1,17},{... | collective-permute-start | bytes 208904 | tf_op jit(solution)/shard_map/ppermute | solution.py:39
  24.7 5.6 %collective-permute-start.5 = (f32[136,128]{1,0:T(8,128)S(1)}, f32[136,128]{1,0:T(8,128)S(1)}, u32[]{:S(2)}, u32[]{:S(2)}) collective-permute-start(f32[136,128]{1,0:T(8,128)S(1)} %merge.2.refs_6_), channel_id=1, source_target_pairs={{0,8},{4,12},{8,0},{12,4},{16,24},{20,28},{24,16},{28,20},{1,9},{5... | collective-permute-start | bytes 208904 | tf_op jit(solution)/shard_map/ppermute | solution.py:39
  33.1 12.8 %all-to-all-start = ((f32[32,8,128]{2,1,0:T(8,128)}), f32[32,8,128]{2,1,0:T(8,128)S(1)}, u32[]{:S(2)}, u32[]{:S(2)}) async-start(f32[32,8,128]{2,1,0:T(8,128)} %get-tuple-element.39.refs_2_), calls=%async_computation | async-start | bytes 262144 | tf_op jit(solution)/shard_map/all_to_all | solution.py:555
  47.3 24.7 %collective-permute-start.9 = (f32[1040,128]{1,0:T(8,128)S(1)}, f32[1040,128]{1,0:T(8,128)S(1)}, u32[]{:S(2)}, u32[]{:S(2)}) collective-permute-start(f32[1040,128]{1,0:T(8,128)S(1)} %get-tuple-element.45.refs_2_.refs_0_), channel_id=1, source_target_pairs={{0,2},{2,0},{1,3},{3,1},{4,6},{6,4},{5,7},{7,5},{8,10},{10,8},{9,1... | collective-permute-start | bytes 1597448 | tf_op jit(solution)/shard_map/ppermute | solution.py:39
  47.6 6.9 %collective-permute-start.10 = (f32[136,128]{1,0:T(8,128)S(1)}, f32[136,128]{1,0:T(8,128)S(1)}, u32[]{:S(2)}, u32[]{:S(2)}) collective-permute-start(f32[136,128]{1,0:T(8,128)S(1)} %get-tuple-element.49), channel_id=1, source_target_pairs={{0,24},{4,28},{8,16},{12,20},{16,8},{20,12},{24,0},{28,4},{1,25},{... | collective-permute-start | bytes 208904 | tf_op jit(solution)/shard_map/ppermute | solution.py:39
  49.0 7.5 %collective-permute-start.11 = (f32[136,128]{1,0:T(8,128)S(1)}, f32[136,128]{1,0:T(8,128)S(1)}, u32[]{:S(2)}, u32[]{:S(2)}) collective-permute-start(f32[136,128]{1,0:T(8,128)S(1)} %get-tuple-element.50), channel_id=1, source_target_pairs={{0,16},{4,20},{8,24},{12,28},{16,0},{20,4},{24,8},{28,12},{1,17},{... | collective-permute-start | bytes 208904 | tf_op jit(solution)/shard_map/ppermute | solution.py:39
  49.7 6.8 %collective-permute-start.12 = (f32[136,128]{1,0:T(8,128)S(1)}, f32[136,128]{1,0:T(8,128)S(1)}, u32[]{:S(2)}, u32[]{:S(2)}) collective-permute-start(f32[136,128]{1,0:T(8,128)S(1)} %get-tuple-element.51), channel_id=1, source_target_pairs={{0,8},{4,12},{8,0},{12,4},{16,24},{20,28},{24,16},{28,20},{1,9},{5... | collective-permute-start | bytes 208904 | tf_op jit(solution)/shard_map/ppermute | solution.py:39
  56.6 7.0 %collective-permute-start.15 = (f32[136,128]{1,0:T(8,128)S(1)}, f32[136,128]{1,0:T(8,128)S(1)}, u32[]{:S(2)}, u32[]{:S(2)}) collective-permute-start(f32[136,128]{1,0:T(8,128)S(1)} %merge.3.refs_0_), channel_id=1, source_target_pairs={{0,24},{4,28},{8,16},{12,20},{16,8},{20,12},{24,0},{28,4},{1,25},{... | collective-permute-start | bytes 208904 | tf_op jit(solution)/shard_map/ppermute | solution.py:39
  58.3 7.3 %collective-permute-start.14 = (f32[136,128]{1,0:T(8,128)S(1)}, f32[136,128]{1,0:T(8,128)S(1)}, u32[]{:S(2)}, u32[]{:S(2)}) collective-permute-start(f32[136,128]{1,0:T(8,128)S(1)} %merge.3.refs_0_), channel_id=1, source_target_pairs={{0,16},{4,20},{8,24},{12,28},{16,0},{20,4},{24,8},{28,12},{1,17},{... | collective-permute-start | bytes 208904 | tf_op jit(solution)/shard_map/ppermute | solution.py:39
  58.3 7.3 %collective-permute-start.13 = (f32[136,128]{1,0:T(8,128)S(1)}, f32[136,128]{1,0:T(8,128)S(1)}, u32[]{:S(2)}, u32[]{:S(2)}) collective-permute-start(f32[136,128]{1,0:T(8,128)S(1)} %merge.3.refs_0_), channel_id=1, source_target_pairs={{0,8},{4,12},{8,0},{12,4},{16,24},{20,28},{24,16},{28,20},{1,9},{5... | collective-permute-start | bytes 208904 | tf_op jit(solution)/shard_map/ppermute | solution.py:39
  65.7 14.7 %collective-permute-start.18 = (f32[136,512]{1,0:T(8,128)S(1)}, f32[136,512]{1,0:T(8,128)S(1)}, u32[]{:S(2)}, u32[]{:S(2)}) collective-permute-start(f32[136,512]{1,0:T(8,128)S(1)} %join.1.refs_5_), channel_id=1, source_target_pairs={{0,2},{2,0},{1,3},{3,1},{4,6},{6,4},{5,7},{7,5},{8,10},{10,8},{9,1... | collective-permute-start | bytes 835592 | tf_op jit(solution)/shard_map/ppermute | solution.py:39
  69.3 2.6 %copy-start.8 = (f32[520,128]{1,0:T(8,128)}, f32[520,128]{1,0:T(8,128)S(1)}, u32[]{:S(2)}) copy-start(f32[520,128]{1,0:T(8,128)S(1)} %get-tuple-element.54) | copy-start | bytes 798724
  69.3 11.0 %all-to-all-start.1 = ((f32[32,8,128]{2,1,0:T(8,128)}), f32[32,8,128]{2,1,0:T(8,128)S(1)}, u32[]{:S(2)}, u32[]{:S(2)}) async-start(f32[32,8,128]{2,1,0:T(8,128)} %get-tuple-element.52.refs_2_), calls=%async_computation.1 | async-start | bytes 262144 | tf_op jit(solution)/shard_map/all_to_all | solution.py:555
  72.0 11.3 %collective-permute-start.16 = (f32[1040,128]{1,0:T(8,128)S(1)}, f32[1040,128]{1,0:T(8,128)S(1)}, u32[]{:S(2)}, u32[]{:S(2)}) collective-permute-start(f32[1040,128]{1,0:T(8,128)S(1)} %mate_parts.1), channel_id=1, source_target_pairs={{0,4},{4,0},{8,12},{12,8},{16,20},{20,16},{24,28},{28,24},{1,5},{5... | collective-permute-start | bytes 1597448 | tf_op jit(solution)/shard_map/ppermute | solution.py:39
  72.3 10.9 %collective-permute-start.17 = (f32[520,128]{1,0:T(8,128)}, f32[520,128]{1,0:T(8,128)}, u32[]{:S(2)}, u32[]{:S(2)}) collective-permute-start(f32[520,128]{1,0:T(8,128)} %copy-done.8), channel_id=1, source_target_pairs={{0,4},{4,0},{8,12},{12,8},{16,20},{20,16},{24,28},{28,24},{1,5},{5... | collective-permute-start | bytes 798728 | tf_op jit(solution)/shard_map/ppermute | solution.py:39
  81.7 1.6 %collective-permute-start.19 = (f32[520,128]{1,0:T(8,128)S(1)}, f32[520,128]{1,0:T(8,128)S(1)}, u32[]{:S(2)}, u32[]{:S(2)}) collective-permute-start(f32[520,128]{1,0:T(8,128)S(1)} %other_backward.3), channel_id=1, source_target_pairs={{0,4},{4,0},{8,12},{12,8},{16,20},{20,16},{24,28},{28,24},{1,5},{5... | collective-permute-start | bytes 798728 | tf_op jit(solution)/shard_map/ppermute | solution.py:39

commit v12 on v6

--- a/solution.py
+++ b/solution.py
@@ -130,7 +130,6 @@
     entry_total = slot_total * width
     score_scale = 1.0 / math.sqrt(width)
     slots = CORES * slot_rows
-    devices = ranks * CORES * query_devices * head_devices
     pos_rows = part_rows // width
     bias_rows = slot_rows // width
     packed_rows = 2 * slot_rows + TAIL
@@ -404,9 +403,9 @@
             grad_outs[at][2 * slot_rows :, :] = grad_bias
             for which, grad in enumerate((grad_keys, grad_values, grad_bias)):
                 squares[which] = squares[which] + jnp.sum(grad * grad, axis=0, keepdims=True)
-        tile = jnp.concatenate(squares + [jnp.zeros((TAIL - 3, width), jnp.float32)], axis=0)
-        for at in range(devices):
-            squares_out[at] = tile
+        squares_out[...] = jnp.concatenate(
+            squares + [jnp.zeros((TAIL - 3, width), jnp.float32)], axis=0
+        )
 
     def mate_body(*refs):
         *state_refs, out_ref = refs
@@ -471,7 +470,7 @@
             from_mate = exchange(for_mate, page=1)
         own_grad, mate_grad, squares = call(
             backward_body,
-            packed_shapes + [(devices, TAIL, width)],
+            packed_shapes + [(TAIL, width)],
             "backward",
             3 * matmul_cost,
             [weights, maxima] + states + query_parts + all_merged,
@@ -480,11 +479,7 @@
         grads = [own_grad, mate_grad]
         if last:
             all_grads = [to_output(grads, mask) for mask in out_masks]
-        tiles = [
-            lax.all_to_all(
-                squares, ("page", "query", "head"), split_axis=0, concat_axis=0, tiled=True
-            )
-        ]
+        tiles = [lax.all_gather(squares, ("page", "query", "head"))]
 
     def last_body(*refs):
         state_refs, (mate_ref, *refs) = refs[:query_devices], refs[query_devices:]

time: 84.4 us -> 190 us (2.25)
  blocking collectives: 25.5 us -> 133 us
    all_gather x0 -> x2, blocking collectives: none -> 133 us  [direct_per_device(): tiles = [lax.all_gather(squares, ('page', 'query', 'head'))]]
    all_to_all x2 -> x0, blocking collectives: 25.5 us -> none  [direct_per_device(): lax.all_to_all(squares, ('page', 'query', 'head'), split_axis=0, concat_a...]
    ppermute x19, waiting for transfers between devices: 23.4 us -> 21.5 us  [exchange(): return lax.ppermute(value, axes, pairs)]
  transfers between devices with their start and end apart: 19 -> 19, of which waited for: 9 -> 9; matrix products, arithmetic and copies ran while one was open for 0% -> 0% of each run, Pallas kernels for 3% -> 2%
where the time goes in v12:
time: 190 us
  blocking collectives  133 us (70%)
  starting transfers between devices  23.9 us (13%)
  waiting for transfers between devices  21.5 us (11%)
  Pallas kernels  10.9 us (6%)
    all_gather x2, blocking collectives, direct_per_device(): tiles = [lax.all_gather(squares, ('page', 'query', 'head'))]  133 us
    ppermute x19, starting transfers between devices, exchange(): return lax.ppermute(value, axes, pairs)  23.9 us
    ppermute x19, waiting for transfers between devices, exchange(): return lax.ppermute(value, axes, pairs)  21.5 us
    pallas_call x10, Pallas kernels, call(): pl.pallas_call(without_after, out_shape=[jax.ShapeDtypeStruct(shape, jnp....  10.9 us
  transfers between devices with their start and end apart: 19, of which 9 were waited for; matrix products, arithmetic and copies ran while one was open for 0% of the time, Pallas kernels for 2%

profile of v12, /device:TPU:0, one launch (start us, length us, event | category | flops | bytes accessed | tf_op | source)
XLA Modules:
  0.0 190.1 jit_solution(13734592121700860152)
XLA Ops:
  0.7 2.0 %pack.1 = (f32[520,128]{1,0:T(8,128)}, f32[328,128]{1,0:T(8,128)}) custom-call(f32[4,256,128]{2,1,0:T(8,128)} %refs_0_.3, f32[4,256,128]{2,1,0:T(8,128)} %refs_1_.3, f32[4,256,128]{2,1,0:T(8,128)} %refs_2_.3, f32[4,256]{1,0:T(4,128)} %refs_3_.3, f32[4,256,128]{2,1,0:T(8,128)} %refs_4_.3, s32[4,256]{1,0:T(4,128)} %refs_5_.3, s32[8]{0:T(128)} %refs_6_.3), custom_call_target="tpu_custom_call" | custom-call | flops 1048576 | bytes 1048576 | tf_op jit(solution)/shard_map/pack/pallas_call | solution.py:67
  2.7 0.0 copy-start.6
  2.7 0.5 collective-permute-start
  3.3 2.6 %collective-permute-start.1 = (f32[328,128]{1,0:T(8,128)}, f32[328,128]{1,0:T(8,128)S(1)}, u32[]{:S(2)}, u32[]{:S(2)}) collective-permute-start(f32[328,128]{1,0:T(8,128)} %get-tuple-element.29), channel_id=1, source_target_pairs={{0,2},{2,0},{1,3},{3,1},{4,6},{6,4},{5,7},{7,5},{8,10},{10,8},{9,1... | collective-permute-start | bytes 503816 | tf_op jit(solution)/shard_map/ppermute | solution.py:39
  5.9 0.7 own.1
  6.6 4.4 %collective-permute-done.1.refs_3_.refs_1_.refs_5_.refs_4_ = f32[328,128]{1,0:T(8,128)S(1)} collective-permute-done((f32[328,128]{1,0:T(8,128)}, f32[328,128]{1,0:T(8,128)S(1)}, u32[]{:S(2)}, u32[]{:S(2)}) %collective-permute-start.1) | collective-permute-done | bytes 167968 | tf_op jit(solution)/shard_map/ppermute | solution.py:39
  10.9 0.0 collective-permute-done.refs_1_.refs_3_
  10.9 1.2 forward.1
  12.2 3.9 %collective-permute-start.2 = (f32[136,128]{1,0:T(8,128)S(1)}, f32[136,128]{1,0:T(8,128)S(1)}, u32[]{:S(2)}, u32[]{:S(2)}) collective-permute-start(f32[136,128]{1,0:T(8,128)S(1)} %get-tuple-element.33), channel_id=1, source_target_pairs={{0,24},{4,28},{8,16},{12,20},{16,8},{20,12},{24,0},{28,4},{1,25},{... | collective-permute-start | bytes 208904 | tf_op jit(solution)/shard_map/ppermute | solution.py:39
  16.1 0.0 collective-permute-start.3
  16.1 0.6 collective-permute-start.4
  16.7 2.1 %collective-permute-done.2.refs_3_ = f32[136,128]{1,0:T(8,128)S(1)} collective-permute-done((f32[136,128]{1,0:T(8,128)S(1)}, f32[136,128]{1,0:T(8,128)S(1)}, u32[]{:S(2)}, u32[]{:S(2)}) %collective-permute-start.2) | collective-permute-done | bytes 69664 | tf_op jit(solution)/shard_map/ppermute | solution.py:39
  18.9 3.0 %collective-permute-done.3.refs_4_ = f32[136,128]{1,0:T(8,128)S(1)} collective-permute-done((f32[136,128]{1,0:T(8,128)S(1)}, f32[136,128]{1,0:T(8,128)S(1)}, u32[]{:S(2)}, u32[]{:S(2)}) %collective-permute-start.3) | collective-permute-done | bytes 69664 | tf_op jit(solution)/shard_map/ppermute | solution.py:39
  21.8 0.0 collective-permute-done.4.refs_5_
  21.8 0.1 merge.2.refs_6_
  22.0 2.8 %collective-permute-start.7 = (f32[136,128]{1,0:T(8,128)S(1)}, f32[136,128]{1,0:T(8,128)S(1)}, u32[]{:S(2)}, u32[]{:S(2)}) collective-permute-start(f32[136,128]{1,0:T(8,128)S(1)} %merge.2.refs_6_), channel_id=1, source_target_pairs={{0,24},{4,28},{8,16},{12,20},{16,8},{20,12},{24,0},{28,4},{1,25},{... | collective-permute-start | bytes 208904 | tf_op jit(solution)/shard_map/ppermute | solution.py:39
  24.7 0.0 collective-permute-start.6
  24.7 1.7 collective-permute-start.5
  26.4 2.5 %collective-permute-done.7.refs_9_ = f32[136,128]{1,0:T(8,128)S(1)} collective-permute-done((f32[136,128]{1,0:T(8,128)S(1)}, f32[136,128]{1,0:T(8,128)S(1)}, u32[]{:S(2)}, u32[]{:S(2)}) %collective-permute-start.7) | collective-permute-done | bytes 69664 | tf_op jit(solution)/shard_map/ppermute | solution.py:39
  28.9 2.4 %collective-permute-done.6.refs_8_ = f32[136,128]{1,0:T(8,128)S(1)} collective-permute-done((f32[136,128]{1,0:T(8,128)S(1)}, f32[136,128]{1,0:T(8,128)S(1)}, u32[]{:S(2)}, u32[]{:S(2)}) %collective-permute-start.6) | collective-permute-done | bytes 69664 | tf_op jit(solution)/shard_map/ppermute | solution.py:39
  31.3 0.0 collective-permute-done.5.refs_7_
  31.3 2.1 %backward.2 = (f32[520,128]{1,0:T(8,128)S(1)}, f32[520,128]{1,0:T(8,128)S(1)}, f32[8,128]{1,0:T(8,128)S(1)}) custom-call(f32[512,512]{1,0:T(8,128)S(1)} %get-tuple-element.30.refs_0_, f32[8,512]{1,0:T(8,128)S(1)} %get-tuple-element.31.refs_1_, f32[520,128]{1,0:T(8,128)S(1)} %get-tuple-element.26.refs_0_.refs_2_, ...), custom_call_target="tpu_custom_call" | custom-call | flops 603979776 | bytes 1048576 | tf_op jit(solution)/shard_map/backward/pallas_call | solution.py:67
  33.4 65.8 %all-gather = f32[256,128]{1,0:T(8,128)S(1)} all-gather(f32[8,128]{1,0:T(8,128)S(1)} %get-tuple-element.38), channel_id=2, replica_groups=mesh['page'=8,'query'=2,'head'=2] {'page','query','head'}, dimensions={0}, use_global_device_ids=true | all-gather | bytes 135168 | tf_op jit(solution)/shard_map/all_gather | solution.py:482
  99.2 1.3 update_forward.1
  100.5 0.1 collective-permute-start.8
  100.6 0.1 collective-permute-start.9
  100.7 0.1 collective-permute-start.10
  100.7 4.3 %collective-permute-start.11 = (f32[136,128]{1,0:T(8,128)S(1)}, f32[136,128]{1,0:T(8,128)S(1)}, u32[]{:S(2)}, u32[]{:S(2)}) collective-permute-start(f32[136,128]{1,0:T(8,128)S(1)} %get-tuple-element.43), channel_id=1, source_target_pairs={{0,8},{4,12},{8,0},{12,4},{16,24},{20,28},{24,16},{28,20},{1,9},{5... | collective-permute-start | bytes 208904 | tf_op jit(solution)/shard_map/ppermute | solution.py:39
  105.0 1.9 collective-permute-done.9.refs_3_
  106.9 0.0 collective-permute-done.10.refs_4_
  106.9 0.7 collective-permute-done.11.refs_5_
  107.6 0.1 merge.3.refs_5_
  107.7 4.2 %collective-permute-start.14 = (f32[136,128]{1,0:T(8,128)S(1)}, f32[136,128]{1,0:T(8,128)S(1)}, u32[]{:S(2)}, u32[]{:S(2)}) collective-permute-start(f32[136,128]{1,0:T(8,128)S(1)} %merge.3.refs_5_), channel_id=1, source_target_pairs={{0,24},{4,28},{8,16},{12,20},{16,8},{20,12},{24,0},{28,4},{1,25},{... | collective-permute-start | bytes 208904 | tf_op jit(solution)/shard_map/ppermute | solution.py:39
  111.9 0.0 collective-permute-start.13
  111.9 0.6 collective-permute-start.12
  112.5 1.7 collective-permute-done.14.refs_4_.refs_8_
  114.3 2.8 %collective-permute-done.13.refs_3_.refs_7_ = f32[136,128]{1,0:T(8,128)S(1)} collective-permute-done((f32[136,128]{1,0:T(8,128)S(1)}, f32[136,128]{1,0:T(8,128)S(1)}, u32[]{:S(2)}, u32[]{:S(2)}) %collective-permute-start.13) | collective-permute-done | bytes 69664 | tf_op jit(solution)/shard_map/ppermute | solution.py:39
  117.1 0.0 collective-permute-done.8.refs_1_
  117.1 0.1 collective-permute-start.15
  117.2 2.1 %backward.3 = (f32[520,128]{1,0:T(8,128)S(1)}, f32[520,128]{1,0:T(8,128)S(1)}, f32[8,128]{1,0:T(8,128)S(1)}) custom-call(f32[512,512]{1,0:T(8,128)S(1)} %get-tuple-element.44.refs_0_, f32[8,512]{1,0:T(8,128)S(1)} %get-tuple-element.45.refs_1_, f32[1040,128]{1,0:T(8,128)S(1)} %get-tuple-element.39.refs_0_.refs_2_, ...), custom_call_target="tpu_custom_call" | custom-call | flops 603979776 | bytes 1048576 | tf_op jit(solution)/shard_map/backward/pallas_call | solution.py:67
  119.3 2.1 %collective-permute-start.17 = (f32[520,128]{1,0:T(8,128)S(1)}, f32[520,128]{1,0:T(8,128)S(1)}, u32[]{:S(2)}, u32[]{:S(2)}) collective-permute-start(f32[520,128]{1,0:T(8,128)S(1)} %get-tuple-element.46.refs_3_), channel_id=1, source_target_pairs={{0,2},{2,0},{4,6},{6,4},{8,10},{10,8},{12,14},{14,12},{16,18},{18,... | collective-permute-start | bytes 798728 | tf_op jit(solution)/shard_map/ppermute | solution.py:39
  121.4 0.2 collective-permute-start.18
  121.6 0.1 collective-permute-start.16
  121.7 67.2 %all-gather.1 = f32[256,128]{1,0:T(8,128)S(1)} all-gather(f32[8,128]{1,0:T(8,128)S(1)} %get-tuple-element.48), channel_id=3, replica_groups=mesh['page'=8,'query'=2,'head'=2] {'page','query','head'}, dimensions={0}, use_global_device_ids=true | all-gather | bytes 135168 | tf_op jit(solution)/shard_map/all_gather | solution.py:482
  188.9 0.0 collective-permute-done.18.refs_6_
  188.9 0.0 collective-permute-done.16.refs_4_
  188.9 0.0 collective-permute-done.15.refs_2_
  188.9 1.1 last_update.1
  (16 shorter events, 0.1 us)
Async XLA Ops:
  0.6 5.2 %copy-start.3 = (f32[4,256,128]{2,1,0:T(8,128)S(1)}, f32[4,256,128]{2,1,0:T(8,128)}, u32[]{:S(2)}) copy-start(f32[4,256,128]{2,1,0:T(8,128)} %refs_4_.3) | copy-start | bytes 1572868
  0.6 5.2 %copy-start.2 = (f32[4,256,128]{2,1,0:T(8,128)S(1)}, f32[4,256,128]{2,1,0:T(8,128)}, u32[]{:S(2)}) copy-start(f32[4,256,128]{2,1,0:T(8,128)} %refs_2_.3) | copy-start | bytes 1572868
  0.7 5.2 %copy-start.1 = (f32[4,256,128]{2,1,0:T(8,128)S(1)}, f32[4,256,128]{2,1,0:T(8,128)}, u32[]{:S(2)}) copy-start(f32[4,256,128]{2,1,0:T(8,128)} %refs_1_.3) | copy-start | bytes 1572868
  0.7 5.2 %copy-start = (f32[4,256,128]{2,1,0:T(8,128)S(1)}, f32[4,256,128]{2,1,0:T(8,128)}, u32[]{:S(2)}) copy-start(f32[4,256,128]{2,1,0:T(8,128)} %refs_0_.3) | copy-start | bytes 1572868
  0.7 5.2 %copy-start.4 = (f32[4,256]{1,0:T(4,128)S(1)}, f32[4,256]{1,0:T(4,128)}, u32[]{:S(2)}) copy-start(f32[4,256]{1,0:T(4,128)} %refs_3_.3) | copy-start | bytes 12292
  0.7 5.2 %copy-start.5 = (s32[4,256]{1,0:T(4,128)S(1)}, s32[4,256]{1,0:T(4,128)}, u32[]{:S(2)}) copy-start(s32[4,256]{1,0:T(4,128)} %refs_5_.3) | copy-start | bytes 12292
  2.7 3.2 %copy-start.6 = (s32[8]{0:T(128)S(1)}, s32[8]{0:T(128)}, u32[]{:S(2)}) copy-start(s32[8]{0:T(128)} %refs_6_.3) | copy-start | bytes 100
  2.7 8.2 %collective-permute-start = (f32[520,128]{1,0:T(8,128)}, f32[520,128]{1,0:T(8,128)S(1)}, u32[]{:S(2)}, u32[]{:S(2)}) collective-permute-start(f32[520,128]{1,0:T(8,128)} %get-tuple-element.27), channel_id=1, source_target_pairs={{0,4},{4,0},{8,12},{12,8},{16,20},{20,16},{24,28},{28,24},{1,5},{5... | collective-permute-start | bytes 798728 | tf_op jit(solution)/shard_map/ppermute | solution.py:39
  3.3 7.7 %collective-permute-start.1 = (f32[328,128]{1,0:T(8,128)}, f32[328,128]{1,0:T(8,128)S(1)}, u32[]{:S(2)}, u32[]{:S(2)}) collective-permute-start(f32[328,128]{1,0:T(8,128)} %get-tuple-element.29), channel_id=1, source_target_pairs={{0,2},{2,0},{1,3},{3,1},{4,6},{6,4},{5,7},{7,5},{8,10},{10,8},{9,1... | collective-permute-start | bytes 503816 | tf_op jit(solution)/shard_map/ppermute | solution.py:39
  12.2 6.7 %collective-permute-start.2 = (f32[136,128]{1,0:T(8,128)S(1)}, f32[136,128]{1,0:T(8,128)S(1)}, u32[]{:S(2)}, u32[]{:S(2)}) collective-permute-start(f32[136,128]{1,0:T(8,128)S(1)} %get-tuple-element.33), channel_id=1, source_target_pairs={{0,24},{4,28},{8,16},{12,20},{16,8},{20,12},{24,0},{28,4},{1,25},{... | collective-permute-start | bytes 208904 | tf_op jit(solution)/shard_map/ppermute | solution.py:39
  16.1 5.7 %collective-permute-start.3 = (f32[136,128]{1,0:T(8,128)S(1)}, f32[136,128]{1,0:T(8,128)S(1)}, u32[]{:S(2)}, u32[]{:S(2)}) collective-permute-start(f32[136,128]{1,0:T(8,128)S(1)} %get-tuple-element.34), channel_id=1, source_target_pairs={{0,16},{4,20},{8,24},{12,28},{16,0},{20,4},{24,8},{28,12},{1,17},{... | collective-permute-start | bytes 208904 | tf_op jit(solution)/shard_map/ppermute | solution.py:39
  16.1 5.7 %collective-permute-start.4 = (f32[136,128]{1,0:T(8,128)S(1)}, f32[136,128]{1,0:T(8,128)S(1)}, u32[]{:S(2)}, u32[]{:S(2)}) collective-permute-start(f32[136,128]{1,0:T(8,128)S(1)} %get-tuple-element.35), channel_id=1, source_target_pairs={{0,8},{4,12},{8,0},{12,4},{16,24},{20,28},{24,16},{28,20},{1,9},{5... | collective-permute-start | bytes 208904 | tf_op jit(solution)/shard_map/ppermute | solution.py:39
  22.0 7.0 %collective-permute-start.7 = (f32[136,128]{1,0:T(8,128)S(1)}, f32[136,128]{1,0:T(8,128)S(1)}, u32[]{:S(2)}, u32[]{:S(2)}) collective-permute-start(f32[136,128]{1,0:T(8,128)S(1)} %merge.2.refs_6_), channel_id=1, source_target_pairs={{0,24},{4,28},{8,16},{12,20},{16,8},{20,12},{24,0},{28,4},{1,25},{... | collective-permute-start | bytes 208904 | tf_op jit(solution)/shard_map/ppermute | solution.py:39
  24.7 6.5 %collective-permute-start.6 = (f32[136,128]{1,0:T(8,128)S(1)}, f32[136,128]{1,0:T(8,128)S(1)}, u32[]{:S(2)}, u32[]{:S(2)}) collective-permute-start(f32[136,128]{1,0:T(8,128)S(1)} %merge.2.refs_6_), channel_id=1, source_target_pairs={{0,16},{4,20},{8,24},{12,28},{16,0},{20,4},{24,8},{28,12},{1,17},{... | collective-permute-start | bytes 208904 | tf_op jit(solution)/shard_map/ppermute | solution.py:39
  24.7 6.5 %collective-permute-start.5 = (f32[136,128]{1,0:T(8,128)S(1)}, f32[136,128]{1,0:T(8,128)S(1)}, u32[]{:S(2)}, u32[]{:S(2)}) collective-permute-start(f32[136,128]{1,0:T(8,128)S(1)} %merge.2.refs_6_), channel_id=1, source_target_pairs={{0,8},{4,12},{8,0},{12,4},{16,24},{20,28},{24,16},{28,20},{1,9},{5... | collective-permute-start | bytes 208904 | tf_op jit(solution)/shard_map/ppermute | solution.py:39
  100.5 16.6 %collective-permute-start.8 = (f32[1040,128]{1,0:T(8,128)S(1)}, f32[1040,128]{1,0:T(8,128)S(1)}, u32[]{:S(2)}, u32[]{:S(2)}) collective-permute-start(f32[1040,128]{1,0:T(8,128)S(1)} %get-tuple-element.39.refs_0_.refs_2_), channel_id=1, source_target_pairs={{0,2},{2,0},{1,3},{3,1},{4,6},{6,4},{5,7},{7,5},{8,10},{10,8},{9,1... | collective-permute-start | bytes 1597448 | tf_op jit(solution)/shard_map/ppermute | solution.py:39
  100.6 6.3 %collective-permute-start.9 = (f32[136,128]{1,0:T(8,128)S(1)}, f32[136,128]{1,0:T(8,128)S(1)}, u32[]{:S(2)}, u32[]{:S(2)}) collective-permute-start(f32[136,128]{1,0:T(8,128)S(1)} %get-tuple-element.41), channel_id=1, source_target_pairs={{0,24},{4,28},{8,16},{12,20},{16,8},{20,12},{24,0},{28,4},{1,25},{... | collective-permute-start | bytes 208904 | tf_op jit(solution)/shard_map/ppermute | solution.py:39
  100.7 6.2 %collective-permute-start.10 = (f32[136,128]{1,0:T(8,128)S(1)}, f32[136,128]{1,0:T(8,128)S(1)}, u32[]{:S(2)}, u32[]{:S(2)}) collective-permute-start(f32[136,128]{1,0:T(8,128)S(1)} %get-tuple-element.42), channel_id=1, source_target_pairs={{0,16},{4,20},{8,24},{12,28},{16,0},{20,4},{24,8},{28,12},{1,17},{... | collective-permute-start | bytes 208904 | tf_op jit(solution)/shard_map/ppermute | solution.py:39
  100.7 6.8 %collective-permute-start.11 = (f32[136,128]{1,0:T(8,128)S(1)}, f32[136,128]{1,0:T(8,128)S(1)}, u32[]{:S(2)}, u32[]{:S(2)}) collective-permute-start(f32[136,128]{1,0:T(8,128)S(1)} %get-tuple-element.43), channel_id=1, source_target_pairs={{0,8},{4,12},{8,0},{12,4},{16,24},{20,28},{24,16},{28,20},{1,9},{5... | collective-permute-start | bytes 208904 | tf_op jit(solution)/shard_map/ppermute | solution.py:39
  107.7 6.6 %collective-permute-start.14 = (f32[136,128]{1,0:T(8,128)S(1)}, f32[136,128]{1,0:T(8,128)S(1)}, u32[]{:S(2)}, u32[]{:S(2)}) collective-permute-start(f32[136,128]{1,0:T(8,128)S(1)} %merge.3.refs_5_), channel_id=1, source_target_pairs={{0,24},{4,28},{8,16},{12,20},{16,8},{20,12},{24,0},{28,4},{1,25},{... | collective-permute-start | bytes 208904 | tf_op jit(solution)/shard_map/ppermute | solution.py:39
  111.9 5.2 %collective-permute-start.13 = (f32[136,128]{1,0:T(8,128)S(1)}, f32[136,128]{1,0:T(8,128)S(1)}, u32[]{:S(2)}, u32[]{:S(2)}) collective-permute-start(f32[136,128]{1,0:T(8,128)S(1)} %merge.3.refs_5_), channel_id=1, source_target_pairs={{0,16},{4,20},{8,24},{12,28},{16,0},{20,4},{24,8},{28,12},{1,17},{... | collective-permute-start | bytes 208904 | tf_op jit(solution)/shard_map/ppermute | solution.py:39
  111.9 5.2 %collective-permute-start.12 = (f32[136,128]{1,0:T(8,128)S(1)}, f32[136,128]{1,0:T(8,128)S(1)}, u32[]{:S(2)}, u32[]{:S(2)}) collective-permute-start(f32[136,128]{1,0:T(8,128)S(1)} %merge.3.refs_5_), channel_id=1, source_target_pairs={{0,8},{4,12},{8,0},{12,4},{16,24},{20,28},{24,16},{28,20},{1,9},{5... | collective-permute-start | bytes 208904 | tf_op jit(solution)/shard_map/ppermute | solution.py:39
  117.1 71.8 %collective-permute-start.15 = (f32[1040,128]{1,0:T(8,128)S(1)}, f32[1040,128]{1,0:T(8,128)S(1)}, u32[]{:S(2)}, u32[]{:S(2)}) collective-permute-start(f32[1040,128]{1,0:T(8,128)S(1)} %mate_parts.1), channel_id=1, source_target_pairs={{0,4},{4,0},{8,12},{12,8},{16,20},{20,16},{24,28},{28,24},{1,5},{5... | collective-permute-start | bytes 1597448 | tf_op jit(solution)/shard_map/ppermute | solution.py:39
  119.3 69.6 %collective-permute-start.17 = (f32[520,128]{1,0:T(8,128)S(1)}, f32[520,128]{1,0:T(8,128)S(1)}, u32[]{:S(2)}, u32[]{:S(2)}) collective-permute-start(f32[520,128]{1,0:T(8,128)S(1)} %get-tuple-element.46.refs_3_), channel_id=1, source_target_pairs={{0,2},{2,0},{4,6},{6,4},{8,10},{10,8},{12,14},{14,12},{16,18},{18,... | collective-permute-start | bytes 798728 | tf_op jit(solution)/shard_map/ppermute | solution.py:39
  121.4 67.5 %collective-permute-start.18 = (f32[520,128]{1,0:T(8,128)S(1)}, f32[520,128]{1,0:T(8,128)S(1)}, u32[]{:S(2)}, u32[]{:S(2)}) collective-permute-start(f32[520,128]{1,0:T(8,128)S(1)} %get-tuple-element.47), channel_id=1, source_target_pairs={{0,6},{2,4},{4,2},{6,0},{8,14},{10,12},{12,10},{14,8},{16,22},{18,... | collective-permute-start | bytes 798728 | tf_op jit(solution)/shard_map/ppermute | solution.py:39
  121.6 67.3 %collective-permute-start.16 = (f32[520,128]{1,0:T(8,128)S(1)}, f32[520,128]{1,0:T(8,128)S(1)}, u32[]{:S(2)}, u32[]{:S(2)}) collective-permute-start(f32[520,128]{1,0:T(8,128)S(1)} %get-tuple-element.47), channel_id=1, source_target_pairs={{0,4},{2,6},{4,0},{6,2},{8,12},{10,14},{12,8},{14,10},{16,20},{18,... | collective-permute-start | bytes 798728 | tf_op jit(solution)/shard_map/ppermute | solution.py:39

commit v13 on v6

--- a/solution.py
+++ b/solution.py
@@ -110,6 +110,7 @@
         part_rows * query_devices % ranks == 0
         and chunk % 128 == 0
         and part_rows % (8 * ranks) == 0
+        and (part_rows // ranks % 128 == 0 or 1024 % (part_rows // ranks * 8) == 0)
         and slot_rows % width == 0
         and part_rows % width == 0
         and max(slot_rows, part_rows) < TAIL * width
@@ -134,7 +135,7 @@
     pos_rows = part_rows // width
     bias_rows = slot_rows // width
     packed_rows = 2 * slot_rows + TAIL
-    packed_shapes = [(packed_rows, width)] * 2
+    packed_shapes = [(packed_rows, width)] * CORES
     matmul_cost = 3 * 2 * slots * query_rows * width
 
     def places():
@@ -252,19 +253,6 @@
     ]
     states = [own_state, exchange(mate_state, page=1)]
 
-    def in_columns(parts, axis):
-        return jnp.concatenate(
-            [
-                lax.slice_in_dim(part, at * piece, (at + 1) * piece, axis=axis)
-                for at in range(ranks)
-                for part in parts
-            ],
-            axis=axis,
-        )
-
-    def read_queries(query_refs):
-        return halves(in_columns([ref[:part_rows, :] for ref in query_refs], 0))
-
     def part_of(ref, at):
         return ref.at[pl.ds(at * packed_rows, packed_rows)]
 
@@ -288,17 +276,32 @@
             state_ref[value_end:, :] - sizes[2] * grad_ref[value_end:, :],
         )
 
-    def forward(state_refs, query_refs, chunk_outs, weights_out, max_out, chunks):
+    fold = max(1, 128 // piece)
+    folded, columns = width // fold, fold * piece
+    piece_shape = (folded + TAIL, columns)
+    piece_scratch = [pltpu.VMEM((ranks,) + piece_shape, jnp.float32)]
+
+    def fold_rows(value):
+        groups = [value[at * folded : (at + 1) * folded, :] for at in range(fold)]
+        return jnp.concatenate(groups, axis=1)
+
+    def unfold_rows(value):
+        groups = [value[:, at * piece : (at + 1) * piece] for at in range(fold)]
+        return jnp.concatenate(groups, axis=0)
+
+    def rows_tail(rows):
+        empty = jnp.zeros((TAIL - len(rows), columns), jnp.float32)
+        return jnp.concatenate(rows + [empty], axis=0)
+
+    def forward(state_refs, query_ref, piece_outs, weights_out, max_out, pieces):
         rank, _, _ = places()
-        all_queries = read_queries(query_refs)
-        position_row = in_columns(
-            [tail_as_row(ref, part_rows + piece, pos_rows) for ref in query_refs], 1
-        )
+        queries = halves(query_ref[:part_rows, :])
+        position_row = tail_as_row(query_ref, part_rows + piece, pos_rows)
         all_scores, all_visible = [], []
-        for at, ref in enumerate(state_refs):
-            scores = dot(halves(ref[:slot_rows, :]), all_queries, 1, 1) * score_scale
+        for ref in state_refs:
+            scores = dot(halves(ref[:slot_rows, :]), queries, 1, 1) * score_scale
             bias = row_as_column(tail_as_row(ref, 2 * slot_rows, bias_rows), width)
-            scores = scores + jnp.concatenate([bias] * (query_rows // width), axis=1)
+            scores = scores + jnp.concatenate([bias] * (part_rows // width), axis=1)
             page_start = ref[packed_rows - 1 : packed_rows, 0:1]
             visible = jnp.broadcast_to(position_row >= page_start, scores.shape)
             all_scores.append(jnp.where(visible, scores, MASKED))
@@ -307,106 +310,113 @@
         for scores in all_scores[1:]:
             row_max = jnp.maximum(row_max, jnp.max(scores, axis=0, keepdims=True))
         row_total = jnp.zeros_like(row_max)
-        row_sum = jnp.zeros((width, query_rows), jnp.float32)
+        row_sum = jnp.zeros((width, part_rows), jnp.float32)
         for at, ref in enumerate(state_refs):
             weights = jnp.where(all_visible[at], jnp.exp(all_scores[at] - row_max), 0.0)
             weights_out[at * slot_rows : (at + 1) * slot_rows, :] = weights
             row_total = row_total + jnp.sum(weights, axis=0, keepdims=True)
             values = halves(ref[slot_rows : 2 * slot_rows, :])
             row_sum = row_sum + dot(values, halves(weights), 0, 0)
-        max_out[...] = jnp.broadcast_to(row_max, (TAIL, query_rows))
-        tail = jnp.concatenate(
-            [row_max, row_total, jnp.zeros((TAIL - 2, query_rows), jnp.float32)], axis=0
-        )
+        max_out[...] = jnp.broadcast_to(row_max, (TAIL, part_rows))
         for at in range(ranks):
-            columns = slice(at * chunk, (at + 1) * chunk)
-            chunks[at, :width, :] = row_sum[:, columns]
-            chunks[at, width:, :] = tail[:, columns]
+            own = slice(at * piece, (at + 1) * piece)
+            pieces[at, :folded, :] = fold_rows(row_sum[:, own])
+            pieces[at, folded:, :] = rows_tail(
+                [jnp.concatenate([row[:, own]] * fold, axis=1) for row in (row_max, row_total)]
+            )
         for turn in range(ranks):
-            chunk_outs[turn][...] = chunks[rank ^ turn]
-
-    chunk_shape = (width + TAIL, chunk)
-    forward_shapes = [chunk_shape] * ranks + [(slots, query_rows), (TAIL, query_rows)]
-    chunk_scratch = [pltpu.VMEM((ranks,) + chunk_shape, jnp.float32)]
-
-    def first_body(*refs):
-        state_refs, refs = refs[:2], refs[2:]
-        query_refs, refs = refs[:query_devices], refs[query_devices:]
-        chunk_outs, refs = refs[:ranks], refs[ranks:]
-        forward(state_refs, query_refs, chunk_outs, *refs)
-
-    def next_body(*refs):
-        state_refs, refs = refs[:2], refs[2:]
-        query_refs, refs = refs[:query_devices], refs[query_devices:]
-        grad_refs, refs = refs[:2], refs[2:]
+            piece_outs[turn][...] = pieces[rank ^ turn]
+
+    forward_shapes = [piece_shape] * ranks + [(slots, part_rows), (TAIL, part_rows)]
+
+    def forward_body(*refs):
+        state_refs, refs = parts_of(refs[: len(states)]), refs[len(states) :]
+        query_ref, *refs = refs
+        forward(state_refs, query_ref, refs[:ranks], *refs[ranks:])
+
+    def update_body(*refs):
+        state_refs, (query_ref, *refs) = refs[:CORES], refs[CORES:]
+        grad_refs, refs = refs[:CORES], refs[CORES:]
         tile_refs, refs = refs[: len(tiles)], refs[len(tiles) :]
         state_outs, refs = parts_of(refs[:1]), refs[1:]
-        chunk_outs, refs = refs[:ranks], refs[ranks:]
         sizes = step_sizes(tile_refs)
-        for at in range(2):
-            keys, values, bias = updated(state_refs[at], grad_refs[at], sizes)
-            state_outs[at][:slot_rows, :] = keys
-            state_outs[at][slot_rows : 2 * slot_rows, :] = values
-            state_outs[at][2 * slot_rows :, :] = bias
-        forward(state_outs, query_refs, chunk_outs, *refs)
-
-    def merge_body(*refs):
-        query_refs, refs = refs[:query_devices], refs[query_devices:]
-        chunk_refs, (merged_out,) = refs[:ranks], refs[ranks:]
-        targets = jnp.concatenate(
-            [ref[part_rows : part_rows + piece, :] for ref in query_refs], axis=0
-        )
-        row_max = chunk_refs[0][width : width + 1, :]
-        for ref in chunk_refs[1:]:
-            row_max = jnp.maximum(row_max, ref[width : width + 1, :])
+        for state_ref, grad_ref, out in zip(state_refs, grad_refs, state_outs):
+            keys, values, bias = updated(state_ref, grad_ref, sizes)
+            out[:slot_rows, :] = keys
+            out[slot_rows : 2 * slot_rows, :] = values
+            out[2 * slot_rows :, :] = bias
+        forward(state_outs, query_ref, refs[:ranks], *refs[ranks:])
+
+    def merge_body(query_ref, *refs):
+        piece_refs, (merged_out,) = refs[:ranks], refs[ranks:]
+        targets = fold_rows(query_ref[part_rows : part_rows + piece, :].T)
+        row_max = piece_refs[0][folded : folded + 1, :]
+        for ref in piece_refs[1:]:
+            row_max = jnp.maximum(row_max, ref[folded : folded + 1, :])
         row_total = jnp.zeros_like(row_max)
-        row_sum = jnp.zeros((width, chunk), jnp.float32)
-        for ref in chunk_refs:
-            factor = jnp.exp(ref[width : width + 1, :] - row_max)
-            row_total = row_total + ref[width + 1 : width + 2, :] * factor
-            row_sum = row_sum + ref[:width, :] * factor
+        row_sum = jnp.zeros((folded, columns), jnp.float32)
+        for ref in piece_refs:
+            factor = jnp.exp(ref[folded : folded + 1, :] - row_max)
+            row_total = row_total + ref[folded + 1 : folded + 2, :] * factor
+            row_sum = row_sum + ref[:folded, :] * factor
         output = row_sum / row_total
-        residual = output - targets.T
+        residual = output - targets
         row_delta = jnp.sum(residual * output, axis=0, keepdims=True)
-        merged_out[:width, :] = residual
-        merged_out[width:, :] = jnp.concatenate(
-            [row_max, row_total, row_delta, jnp.zeros((TAIL - 3, chunk), jnp.float32)], axis=0
-        )
-
-    def backward_body(weights_ref, max_ref, *refs):
-        state_refs, refs = parts_of(refs[: len(states)]), refs[len(states) :]
-        query_refs, refs = refs[:query_devices], refs[query_devices:]
-        merged_refs, refs = refs[:ranks], refs[ranks:]
-        grad_outs, (squares_out, chunks) = refs[:2], refs[2:]
-        rank, _, _ = places()
-        for turn in range(ranks):
-            chunks[rank ^ turn] = merged_refs[turn][...]
-        joined = jnp.concatenate([chunks[at] for at in range(ranks)], axis=1)
-        residual = joined[:width, :]
-        row_max, row_total, row_delta = (
-            joined[width + at : width + at + 1, :] for at in range(3)
-        )
-        all_queries = read_queries(query_refs)
-        residual = halves(residual)
-        factor = jnp.exp(max_ref[0:1, :] - row_max) / row_total
-        ones = jnp.ones((TAIL, query_rows), jnp.bfloat16)
-        ones = (ones, jnp.zeros_like(ones))
-        squares = [jnp.zeros((1, width), jnp.float32)] * 3
-        for at, ref in enumerate(state_refs):
-            attention = weights_ref[at * slot_rows : (at + 1) * slot_rows, :] * factor
-            grad_values = dot(halves(attention), residual, 1, 1)
-            grad_probs = dot(halves(ref[slot_rows : 2 * slot_rows, :]), residual, 1, 0)
-            grad_scores = halves(attention * (grad_probs - row_delta))
-            grad_keys = dot(grad_scores, all_queries, 1, 0) * score_scale
-            grad_bias = row_as_tail(dot(ones, grad_scores, 1, 1)[0:1, :], width)
-            grad_outs[at][:slot_rows, :] = grad_keys
-            grad_outs[at][slot_rows : 2 * slot_rows, :] = grad_values
-            grad_outs[at][2 * slot_rows :, :] = grad_bias
-            for which, grad in enumerate((grad_keys, grad_values, grad_bias)):
-                squares[which] = squares[which] + jnp.sum(grad * grad, axis=0, keepdims=True)
-        tile = jnp.concatenate(squares + [jnp.zeros((TAIL - 3, width), jnp.float32)], axis=0)
-        for at in range(devices):
-            squares_out[at] = tile
+        row_delta = sum(row_delta[:, at * piece : (at + 1) * piece] for at in range(fold))
+        merged_out[:folded, :] = residual
+        merged_out[folded:, :] = rows_tail(
+            [row_max, row_total, jnp.concatenate([row_delta] * fold, axis=1)]
+        )
+
+    def backward_of(part):
+        def body(weights_ref, max_ref, *refs):
+            state_refs, refs = parts_of(refs[: len(states)]), refs[len(states) :]
+            query_ref, *refs = refs
+            merged_refs, refs = refs[:ranks], refs[ranks:]
+            before_refs, refs = (refs[:CORES], refs[CORES:]) if part else ([], refs)
+            grad_outs, refs = refs[:CORES], refs[CORES:]
+            *squares_out, pieces = refs
+            rank, _, _ = places()
+            for turn, ref in enumerate(merged_refs):
+                pieces[rank ^ turn] = ref[...]
+            residual = halves(
+                jnp.concatenate([unfold_rows(pieces[at, :folded, :]) for at in range(ranks)], 1)
+            )
+            row_max, row_total, row_delta = (
+                jnp.concatenate(
+                    [pieces[at, folded + row : folded + row + 1, :piece] for at in range(ranks)], 1
+                )
+                for row in range(3)
+            )
+            queries = halves(query_ref[:part_rows, :])
+            factor = jnp.exp(max_ref[0:1, :] - row_max) / row_total
+            ones = jnp.ones((TAIL, part_rows), jnp.bfloat16)
+            ones = (ones, jnp.zeros_like(ones))
+            squares = [jnp.zeros((1, width), jnp.float32)] * 3
+            for at, ref in enumerate(state_refs):
+                attention = weights_ref[at * slot_rows : (at + 1) * slot_rows, :] * factor
+                grad_values = dot(halves(attention), residual, 1, 1)
+                grad_probs = dot(halves(ref[slot_rows : 2 * slot_rows, :]), residual, 1, 0)
+                grad_scores = halves(attention * (grad_probs - row_delta))
+                grad_keys = dot(grad_scores, queries, 1, 0) * score_scale
+                grad_bias = row_as_tail(dot(ones, grad_scores, 1, 1)[0:1, :], width)
+                first, last = 0, 0
+                for which, grad in enumerate((grad_keys, grad_values, grad_bias)):
+                    first, last = last, last + grad.shape[0]
+                    if part:
+                        grad = grad + before_refs[at][first:last, :]
+                    grad_outs[at][first:last, :] = grad
+                    squares[which] = squares[which] + jnp.sum(
+                        grad * grad, axis=0, keepdims=True
+                    )
+            if squares_out:
+                tile = jnp.concatenate(
+                    squares + [jnp.zeros((TAIL - 3, width), jnp.float32)], axis=0
+                )
+                for at in range(devices):
+                    squares_out[0][at] = tile
+
+        return body
 
     def mate_body(*refs):
         *state_refs, out_ref = refs
@@ -422,62 +432,73 @@
 
     for repeat in range(STEPS):
         last = repeat == STEPS - 1
-        if repeat == 0:
-            *chunk_parts, weights, maxima = call(
-                first_body,
-                forward_shapes,
-                "forward",
-                2 * matmul_cost,
-                states + query_parts,
-                chunk_scratch,
+        part_sums, all_weights = [], []
+        for part, query_part in enumerate(query_parts):
+            if repeat and part == 0:
+                new_state, *outs = call(
+                    update_body,
+                    [(CORES * packed_rows, width)] + forward_shapes,
+                    "update_forward",
+                    2 * matmul_cost // query_devices,
+                    states + [query_part] + grads + tiles,
+                    piece_scratch,
+                )
+                states = [new_state]
+            else:
+                outs = call(
+                    forward_body,
+                    forward_shapes,
+                    "forward",
+                    2 * matmul_cost // query_devices,
+                    states + [query_part],
+                    piece_scratch,
+                )
+            part_sums.append(
+                [
+                    exchange(outs[turn], page=CORES * turn) if turn else outs[0]
+                    for turn in range(ranks)
+                ]
             )
-        else:
-            new_state, *chunk_parts, weights, maxima = call(
-                next_body,
-                [(CORES * packed_rows, width)] + forward_shapes,
-                "update_forward",
-                2 * matmul_cost,
-                states + query_parts + grads + tiles,
-                chunk_scratch,
-            )
-            states = [new_state]
-        arrived = {
-            turn: exchange(chunk_parts[turn], page=CORES * turn)
-            for turn in reversed(range(1, ranks))
-        }
+            all_weights.append(list(outs[ranks:]))
         if repeat:
             new_states = states + [
                 exchange(states[0], query=turn) for turn in range(1, query_devices)
             ]
-        (merged,) = call(
-            merge_body,
-            [chunk_shape],
-            "merge",
-            2**20,
-            query_parts + chunk_parts[:1] + list(arrived.values()),
-        )
-        all_merged = [merged] + [
-            exchange(merged, page=CORES * turn) for turn in range(1, ranks)
-        ]
-        if repeat:
-            (for_mate,) = call(
-                mate_body,
-                [(query_devices * packed_rows, width)],
-                "mate_parts",
-                2**20,
-                new_states,
-                after=all_merged[1:],
+        all_merged = []
+        for query_part, sums in zip(query_parts, part_sums):
+            before = [parts[0] for parts in all_merged[-1:]]
+            (merged,) = call(
+                merge_body, [piece_shape], "merge", 2**20, [query_part] + sums, after=before
             )
-            from_mate = exchange(for_mate, page=1)
-        own_grad, mate_grad, squares = call(
-            backward_body,
-            packed_shapes + [(devices, TAIL, width)],
-            "backward",
-            3 * matmul_cost,
-            [weights, maxima] + states + query_parts + all_merged,
-            scratch=chunk_scratch,
-        )
-        grads = [own_grad, mate_grad]
+            all_merged.append(
+                [
+                    exchange(merged, page=CORES * turn) if turn else merged
+                    for turn in range(ranks)
+                ]
+            )
+        grads = []
+        for part, query_part in enumerate(query_parts):
+            ends = part == query_devices - 1
+            *grads, squares = list(
+                call(
+                    backward_of(part),
+                    packed_shapes + [(devices, TAIL, width)] * ends,
+                    "backward",
+                    3 * matmul_cost // query_devices,
+                    all_weights[part] + states + [query_part] + all_merged[part] + grads,
+                    scratch=piece_scratch,
+                )
+            ) + [None] * (not ends)
+            if repeat and part == 0:
+                (for_mate,) = call(
+                    mate_body,
+                    [(query_devices * packed_rows, width)],
+                    "mate_parts",
+                    2**20,
+                    new_states,
+                    after=grads[:1],
+                )
+                from_mate = exchange(for_mate, page=1)
         if last:
             all_grads = [to_output(grads, mask) for mask in out_masks]
         tiles = [

time: 84.4 us -> 96 us (1.14)
  starting transfers between devices: 23.6 us -> 41 us
  waiting for transfers between devices: 23.4 us -> 15.2 us
  Pallas kernels: 10.9 us -> 15 us
  blocking collectives: 25.5 us -> 23.7 us
    ppermute x19 -> x31, starting transfers between devices: 23.6 us -> 41 us  [exchange(): return lax.ppermute(value, axes, pairs)]
    ppermute x19 -> x31, waiting for transfers between devices: 23.4 us -> 15.2 us  [exchange(): return lax.ppermute(value, axes, pairs)]
    pallas_call x10 -> x16, Pallas kernels: 10.9 us -> 15 us  [call(): pl.pallas_call(without_after, out_shape=[jax.ShapeDtypeStruct(shape, jnp....]
    all_to_all x2, blocking collectives: 25.5 us -> 23.7 us  [direct_per_device(): lax.all_to_all(squares, ('page', 'query', 'head'), split_axis=0, concat_a...]
  transfers between devices with their start and end apart: 19 -> 31, of which waited for: 9 -> 11; matrix products, arithmetic and copies ran while one was open for 0% -> 0% of each run, Pallas kernels for 3% -> 10%
where the time goes in v13:
time: 96 us; the launch traced here: 95.8 us
  starting transfers between devices  41 us (43%)
  blocking collectives  23.7 us (25%)
  waiting for transfers between devices  15.2 us (16%)
  Pallas kernels  15 us (16%)
    ppermute x31, starting transfers between devices, exchange(): return lax.ppermute(value, axes, pairs)  41 us
    all_to_all x2, blocking collectives, direct_per_device(): lax.all_to_all(squares, ('page', 'query', 'head'), split_axis=0, concat_a...  23.7 us
    ppermute x31, waiting for transfers between devices, exchange(): return lax.ppermute(value, axes, pairs)  15.2 us
    pallas_call x16, Pallas kernels, call(): pl.pallas_call(without_after, out_shape=[jax.ShapeDtypeStruct(shape, jnp....  15 us
  transfers between devices with their start and end apart: 31, of which 11 were waited for; matrix products, arithmetic and copies ran while one was open for 0% of the time, Pallas kernels for 10%

profile of v13, /device:TPU:0, one launch (start us, length us, event | category | flops | bytes accessed | tf_op | source)
XLA Modules:
  0.0 95.8 jit_solution(17144360233271872402)
XLA Ops:
  0.7 2.0 %pack.1 = (f32[520,128]{1,0:T(8,128)}, f32[328,128]{1,0:T(8,128)}) custom-call(f32[4,256,128]{2,1,0:T(8,128)} %refs_0_.3, f32[4,256,128]{2,1,0:T(8,128)} %refs_1_.3, f32[4,256,128]{2,1,0:T(8,128)} %refs_2_.3, f32[4,256]{1,0:T(4,128)} %refs_3_.3, f32[4,256,128]{2,1,0:T(8,128)} %refs_4_.3, s32[4,256]{1,0:T(4,128)} %refs_5_.3, s32[8]{0:T(128)} %refs_6_.3), custom_call_target="tpu_custom_call" | custom-call | flops 1048576 | bytes 1048576 | tf_op jit(solution)/shard_map/pack/pallas_call | solution.py:67
  2.7 0.5 collective-permute-start
  3.3 2.6 %collective-permute-start.1 = (f32[328,128]{1,0:T(8,128)}, f32[328,128]{1,0:T(8,128)S(1)}, u32[]{:S(2)}, u32[]{:S(2)}) collective-permute-start(f32[328,128]{1,0:T(8,128)} %get-tuple-element.45), channel_id=1, source_target_pairs={{0,2},{2,0},{1,3},{3,1},{4,6},{6,4},{5,7},{7,5},{8,10},{10,8},{9,1... | collective-permute-start | bytes 503816 | tf_op jit(solution)/shard_map/ppermute | solution.py:39
  5.9 0.7 own.1
  6.6 1.0 %forward.4 = (f32[72,128]{1,0:T(8,128)S(1)}, f32[72,128]{1,0:T(8,128)S(1)}, f32[72,128]{1,0:T(8,128)S(1)}, f32[72,128]{1,0:T(8,128)S(1)}, f32[512,256]{1,0:T(8,128)S(1)}, /*index=5*/f32[8,256]{1,0:T(8,128)S(1)}) custom-call(f32[520,128]{1,0:T(8,128)S(1)} %get-tuple-element.42.refs_0_.refs_2_, f32[520,128]{1,0:T(8,128)S(1)} %collective-permute-done.refs_1_.refs_3_, ...), custom_call_target="tpu_custom_call" | custom-call | flops 201326592 | bytes 1048576 | tf_op jit(solution)/shard_map/forward/pallas_call | solution.py:67
  7.6 1.6 %collective-permute-start.5 = (f32[72,128]{1,0:T(8,128)S(1)}, f32[72,128]{1,0:T(8,128)S(1)}, u32[]{:S(2)}, u32[]{:S(2)}) collective-permute-start(f32[72,128]{1,0:T(8,128)S(1)} %get-tuple-element.53), channel_id=1, source_target_pairs={{0,8},{4,12},{8,0},{12,4},{16,24},{20,28},{24,16},{28,20},{1,9},{5... | collective-permute-start | bytes 110600 | tf_op jit(solution)/shard_map/ppermute | solution.py:39
  9.2 2.6 %collective-permute-start.6 = (f32[72,128]{1,0:T(8,128)S(1)}, f32[72,128]{1,0:T(8,128)S(1)}, u32[]{:S(2)}, u32[]{:S(2)}) collective-permute-start(f32[72,128]{1,0:T(8,128)S(1)} %get-tuple-element.54), channel_id=1, source_target_pairs={{0,16},{4,20},{8,24},{12,28},{16,0},{20,4},{24,8},{28,12},{1,17},{... | collective-permute-start | bytes 110600 | tf_op jit(solution)/shard_map/ppermute | solution.py:39
  12.0 1.0 %forward.3 = (f32[72,128]{1,0:T(8,128)S(1)}, f32[72,128]{1,0:T(8,128)S(1)}, f32[72,128]{1,0:T(8,128)S(1)}, f32[72,128]{1,0:T(8,128)S(1)}, f32[512,256]{1,0:T(8,128)S(1)}, /*index=5*/f32[8,256]{1,0:T(8,128)S(1)}) custom-call(f32[520,128]{1,0:T(8,128)S(1)} %get-tuple-element.42.refs_0_.refs_2_, f32[520,128]{1,0:T(8,128)S(1)} %collective-permute-done.refs_1_.refs_3_, ...), custom_call_target="tpu_custom_call" | custom-call | flops 201326592 | bytes 1048576 | tf_op jit(solution)/shard_map/forward/pallas_call | solution.py:67
  13.1 0.8 collective-permute-start.2
  13.8 3.5 %collective-permute-start.3 = (f32[72,128]{1,0:T(8,128)S(1)}, f32[72,128]{1,0:T(8,128)S(1)}, u32[]{:S(2)}, u32[]{:S(2)}) collective-permute-start(f32[72,128]{1,0:T(8,128)S(1)} %get-tuple-element.50), channel_id=1, source_target_pairs={{0,16},{4,20},{8,24},{12,28},{16,0},{20,4},{24,8},{28,12},{1,17},{... | collective-permute-start | bytes 110600 | tf_op jit(solution)/shard_map/ppermute | solution.py:39
  17.5 0.6 collective-permute-done.7.refs_4_
  18.4 3.1 %collective-permute-start.13 = (f32[72,128]{1,0:T(8,128)S(1)}, f32[72,128]{1,0:T(8,128)S(1)}, u32[]{:S(2)}, u32[]{:S(2)}) collective-permute-start(f32[72,128]{1,0:T(8,128)S(1)} %merge.4.refs_5_), channel_id=1, source_target_pairs={{0,24},{4,28},{8,16},{12,20},{16,8},{20,12},{24,0},{28,4},{1,25},{... | collective-permute-start | bytes 110600 | tf_op jit(solution)/shard_map/ppermute | solution.py:39
  21.5 1.3 %collective-permute-start.11 = (f32[72,128]{1,0:T(8,128)S(1)}, f32[72,128]{1,0:T(8,128)S(1)}, u32[]{:S(2)}, u32[]{:S(2)}) collective-permute-start(f32[72,128]{1,0:T(8,128)S(1)} %merge.4.refs_5_), channel_id=1, source_target_pairs={{0,8},{4,12},{8,0},{12,4},{16,24},{20,28},{24,16},{28,20},{1,9},{5... | collective-permute-start | bytes 110600 | tf_op jit(solution)/shard_map/ppermute | solution.py:39
  23.1 0.3 merge.5.refs_5_
  23.4 2.8 %collective-permute-start.10 = (f32[72,128]{1,0:T(8,128)S(1)}, f32[72,128]{1,0:T(8,128)S(1)}, u32[]{:S(2)}, u32[]{:S(2)}) collective-permute-start(f32[72,128]{1,0:T(8,128)S(1)} %merge.5.refs_5_), channel_id=1, source_target_pairs={{0,24},{4,28},{8,16},{12,20},{16,8},{20,12},{24,0},{28,4},{1,25},{... | collective-permute-start | bytes 110600 | tf_op jit(solution)/shard_map/ppermute | solution.py:39
  26.2 1.6 %collective-permute-start.8 = (f32[72,128]{1,0:T(8,128)S(1)}, f32[72,128]{1,0:T(8,128)S(1)}, u32[]{:S(2)}, u32[]{:S(2)}) collective-permute-start(f32[72,128]{1,0:T(8,128)S(1)} %merge.5.refs_5_), channel_id=1, source_target_pairs={{0,8},{4,12},{8,0},{12,4},{16,24},{20,28},{24,16},{28,20},{1,9},{5... | collective-permute-start | bytes 110600 | tf_op jit(solution)/shard_map/ppermute | solution.py:39
  27.8 1.4 %backward.4 = (f32[520,128]{1,0:T(8,128)S(1)}, f32[520,128]{1,0:T(8,128)S(1)}) custom-call(f32[512,256]{1,0:T(8,128)S(1)} %get-tuple-element.56.refs_0_, f32[8,256]{1,0:T(8,128)S(1)} %get-tuple-element.57.refs_1_, f32[520,128]{1,0:T(8,128)S(1)} %get-tuple-element.42.refs_0_.refs_2_, f32[520,128]{1,0:T(8,128)S(1)} %collective-permute-done.refs_1_.refs_3_, ...), custom_call_target="tpu_custom_call" | custom-call | flops 301989888 | bytes 1048576 | tf_op jit(solution)/shard_map/backward/pallas_call | solution.py:67
  29.2 1.9 %collective-permute-done.9.refs_7_ = f32[72,128]{1,0:T(8,128)S(1)} collective-permute-done((f32[72,128]{1,0:T(8,128)S(1)}, f32[72,128]{1,0:T(8,128)S(1)}, u32[]{:S(2)}, u32[]{:S(2)}) %collective-permute-start.9) | collective-permute-done | bytes 36896 | tf_op jit(solution)/shard_map/ppermute | solution.py:39
  31.0 1.5 %backward.5 = (f32[520,128]{1,0:T(8,128)S(1)}, f32[520,128]{1,0:T(8,128)S(1)}, f32[32,8,128]{2,1,0:T(8,128)S(1)}) custom-call(f32[512,256]{1,0:T(8,128)S(1)} %get-tuple-element.46.refs_0_, f32[8,256]{1,0:T(8,128)S(1)} %get-tuple-element.47.refs_1_, f32[520,128]{1,0:T(8,128)S(1)} %get-tuple-element.42.refs_0_.refs_2_, ...), custom_call_target="tpu_custom_call" | custom-call | flops 301989888 | bytes 1048576 | tf_op jit(solution)/shard_map/backward/pallas_call | solution.py:67
  32.6 11.9 %all_to_all.10.refs_5_ = f32[32,8,128]{2,1,0:T(8,128)S(1)} all-to-all(f32[32,8,128]{2,1,0:T(8,128)S(1)} %get-tuple-element.62), channel_id=1, replica_groups=mesh['page'=8,'query'=2,'head'=2] {'page','query','head'}, dimensions={0} | all-to-all | bytes 262144 | tf_op jit(solution)/shard_map/all_to_all | solution.py:505
  44.5 1.1 %update_forward.1 = (f32[1040,128]{1,0:T(8,128)S(1)}, f32[72,128]{1,0:T(8,128)S(1)}, f32[72,128]{1,0:T(8,128)S(1)}, f32[72,128]{1,0:T(8,128)S(1)}, f32[72,128]{1...) custom-call(f32[520,128]{1,0:T(8,128)S(1)} %get-tuple-element.42.refs_0_.refs_2_, ...), custom_call_target="tpu_custom_call" | custom-call | flops 201326592 | bytes 1048576 | tf_op jit(solution)/shard_map/update_forward/pallas_call | solution.py:67
  45.6 0.3 collective-permute-start.14
  45.9 0.7 collective-permute-start.15
  46.6 1.3 %collective-permute-start.16 = (f32[72,128]{1,0:T(8,128)S(1)}, f32[72,128]{1,0:T(8,128)S(1)}, u32[]{:S(2)}, u32[]{:S(2)}) collective-permute-start(f32[72,128]{1,0:T(8,128)S(1)} %get-tuple-element.68), channel_id=1, source_target_pairs={{0,16},{4,20},{8,24},{12,28},{16,0},{20,4},{24,8},{28,12},{1,17},{... | collective-permute-start | bytes 110600 | tf_op jit(solution)/shard_map/ppermute | solution.py:39
  47.9 2.4 %collective-permute-start.17 = (f32[72,128]{1,0:T(8,128)S(1)}, f32[72,128]{1,0:T(8,128)S(1)}, u32[]{:S(2)}, u32[]{:S(2)}) collective-permute-start(f32[72,128]{1,0:T(8,128)S(1)} %get-tuple-element.69), channel_id=1, source_target_pairs={{0,24},{4,28},{8,16},{12,20},{16,8},{20,12},{24,0},{28,4},{1,25},{... | collective-permute-start | bytes 110600 | tf_op jit(solution)/shard_map/ppermute | solution.py:39
  50.3 1.2 %collective-permute-done.16.refs_3_ = f32[72,128]{1,0:T(8,128)S(1)} collective-permute-done((f32[72,128]{1,0:T(8,128)S(1)}, f32[72,128]{1,0:T(8,128)S(1)}, u32[]{:S(2)}, u32[]{:S(2)}) %collective-permute-start.16) | collective-permute-done | bytes 36896 | tf_op jit(solution)/shard_map/ppermute | solution.py:39
  51.5 2.2 %collective-permute-done.17.refs_4_ = f32[72,128]{1,0:T(8,128)S(1)} collective-permute-done((f32[72,128]{1,0:T(8,128)S(1)}, f32[72,128]{1,0:T(8,128)S(1)}, u32[]{:S(2)}, u32[]{:S(2)}) %collective-permute-start.17) | collective-permute-done | bytes 36896 | tf_op jit(solution)/shard_map/ppermute | solution.py:39
  53.9 2.5 %collective-permute-start.20 = (f32[72,128]{1,0:T(8,128)S(1)}, f32[72,128]{1,0:T(8,128)S(1)}, u32[]{:S(2)}, u32[]{:S(2)}) collective-permute-start(f32[72,128]{1,0:T(8,128)S(1)} %merge.6.refs_4_.refs_5_), channel_id=1, source_target_pairs={{0,24},{4,28},{8,16},{12,20},{16,8},{20,12},{24,0},{28,4},{1,25},{... | collective-permute-start | bytes 110600 | tf_op jit(solution)/shard_map/ppermute | solution.py:39
  56.4 1.9 %collective-permute-start.18 = (f32[72,128]{1,0:T(8,128)S(1)}, f32[72,128]{1,0:T(8,128)S(1)}, u32[]{:S(2)}, u32[]{:S(2)}) collective-permute-start(f32[72,128]{1,0:T(8,128)S(1)} %merge.6.refs_4_.refs_5_), channel_id=1, source_target_pairs={{0,8},{4,12},{8,0},{12,4},{16,24},{20,28},{24,16},{28,20},{1,9},{5... | collective-permute-start | bytes 110600 | tf_op jit(solution)/shard_map/ppermute | solution.py:39
  58.3 1.5 %collective-permute-done.20.refs_7_ = f32[72,128]{1,0:T(8,128)S(1)} collective-permute-done((f32[72,128]{1,0:T(8,128)S(1)}, f32[72,128]{1,0:T(8,128)S(1)}, u32[]{:S(2)}, u32[]{:S(2)}) %collective-permute-start.20) | collective-permute-done | bytes 36896 | tf_op jit(solution)/shard_map/ppermute | solution.py:39
  59.9 1.4 %collective-permute-done.19.refs_6_ = f32[72,128]{1,0:T(8,128)S(1)} collective-permute-done((f32[72,128]{1,0:T(8,128)S(1)}, f32[72,128]{1,0:T(8,128)S(1)}, u32[]{:S(2)}, u32[]{:S(2)}) %collective-permute-start.19) | collective-permute-done | bytes 36896 | tf_op jit(solution)/shard_map/ppermute | solution.py:39
  61.2 1.4 %backward.6 = (f32[520,128]{1,0:T(8,128)S(1)}, f32[520,128]{1,0:T(8,128)S(1)}) custom-call(f32[512,256]{1,0:T(8,128)S(1)} %get-tuple-element.64.refs_0_, f32[8,256]{1,0:T(8,128)S(1)} %get-tuple-element.65.refs_1_, f32[1040,128]{1,0:T(8,128)S(1)} %get-tuple-element.63.refs_2_.refs_0_, f32[328,128]{1,0:T(8,128)S(1)} %get-tuple-element.44.refs_2_.refs_0_.refs_4_.refs_3_, ...), custom_call_target="tpu_custom_call" | custom-call | flops 301989888 | bytes 1048576 | tf_op jit(solution)/shard_map/backward/pallas_call | solution.py:67
  62.7 1.0 %forward.5 = (f32[72,128]{1,0:T(8,128)S(1)}, f32[72,128]{1,0:T(8,128)S(1)}, f32[72,128]{1,0:T(8,128)S(1)}, f32[72,128]{1,0:T(8,128)S(1)}, f32[512,256]{1,0:T(8,128)S(1)}, /*index=5*/f32[8,256]{1,0:T(8,128)S(1)}) custom-call(f32[1040,128]{1,0:T(8,128)S(1)} %get-tuple-element.63.refs_2_.refs_0_, ...), custom_call_target="tpu_custom_call" | custom-call | flops 201326592 | bytes 1048576 | tf_op jit(solution)/shard_map/forward/pallas_call | solution.py:67
  63.8 1.1 %collective-permute-start.22 = (f32[72,128]{1,0:T(8,128)S(1)}, f32[72,128]{1,0:T(8,128)S(1)}, u32[]{:S(2)}, u32[]{:S(2)}) collective-permute-start(f32[72,128]{1,0:T(8,128)S(1)} %get-tuple-element.74), channel_id=1, source_target_pairs={{0,8},{4,12},{8,0},{12,4},{16,24},{20,28},{24,16},{28,20},{1,9},{5... | collective-permute-start | bytes 110600 | tf_op jit(solution)/shard_map/ppermute | solution.py:39
  64.9 1.4 %collective-permute-start.23 = (f32[72,128]{1,0:T(8,128)S(1)}, f32[72,128]{1,0:T(8,128)S(1)}, u32[]{:S(2)}, u32[]{:S(2)}) collective-permute-start(f32[72,128]{1,0:T(8,128)S(1)} %get-tuple-element.75), channel_id=1, source_target_pairs={{0,16},{4,20},{8,24},{12,28},{16,0},{20,4},{24,8},{28,12},{1,17},{... | collective-permute-start | bytes 110600 | tf_op jit(solution)/shard_map/ppermute | solution.py:39
  66.2 2.0 %collective-permute-start.24 = (f32[72,128]{1,0:T(8,128)S(1)}, f32[72,128]{1,0:T(8,128)S(1)}, u32[]{:S(2)}, u32[]{:S(2)}) collective-permute-start(f32[72,128]{1,0:T(8,128)S(1)} %get-tuple-element.76), channel_id=1, source_target_pairs={{0,24},{4,28},{8,16},{12,20},{16,8},{20,12},{24,0},{28,4},{1,25},{... | collective-permute-start | bytes 110600 | tf_op jit(solution)/shard_map/ppermute | solution.py:39
  68.2 2.3 %collective-permute-done.23.refs_3_ = f32[72,128]{1,0:T(8,128)S(1)} collective-permute-done((f32[72,128]{1,0:T(8,128)S(1)}, f32[72,128]{1,0:T(8,128)S(1)}, u32[]{:S(2)}, u32[]{:S(2)}) %collective-permute-start.23) | collective-permute-done | bytes 36896 | tf_op jit(solution)/shard_map/ppermute | solution.py:39
  70.5 1.5 %collective-permute-done.24.refs_4_ = f32[72,128]{1,0:T(8,128)S(1)} collective-permute-done((f32[72,128]{1,0:T(8,128)S(1)}, f32[72,128]{1,0:T(8,128)S(1)}, u32[]{:S(2)}, u32[]{:S(2)}) %collective-permute-start.24) | collective-permute-done | bytes 36896 | tf_op jit(solution)/shard_map/ppermute | solution.py:39
  72.0 0.3 merge.7.refs_4_
  72.3 2.0 %collective-permute-start.27 = (f32[72,128]{1,0:T(8,128)S(1)}, f32[72,128]{1,0:T(8,128)S(1)}, u32[]{:S(2)}, u32[]{:S(2)}) collective-permute-start(f32[72,128]{1,0:T(8,128)S(1)} %merge.7.refs_4_), channel_id=1, source_target_pairs={{0,24},{4,28},{8,16},{12,20},{16,8},{20,12},{24,0},{28,4},{1,25},{... | collective-permute-start | bytes 110600 | tf_op jit(solution)/shard_map/ppermute | solution.py:39
  74.3 2.4 %collective-permute-start.25 = (f32[72,128]{1,0:T(8,128)S(1)}, f32[72,128]{1,0:T(8,128)S(1)}, u32[]{:S(2)}, u32[]{:S(2)}) collective-permute-start(f32[72,128]{1,0:T(8,128)S(1)} %merge.7.refs_4_), channel_id=1, source_target_pairs={{0,8},{4,12},{8,0},{12,4},{16,24},{20,28},{24,16},{28,20},{1,9},{5... | collective-permute-start | bytes 110600 | tf_op jit(solution)/shard_map/ppermute | solution.py:39
  76.7 1.8 %collective-permute-done.27.refs_7_ = f32[72,128]{1,0:T(8,128)S(1)} collective-permute-done((f32[72,128]{1,0:T(8,128)S(1)}, f32[72,128]{1,0:T(8,128)S(1)}, u32[]{:S(2)}, u32[]{:S(2)}) %collective-permute-start.27) | collective-permute-done | bytes 36896 | tf_op jit(solution)/shard_map/ppermute | solution.py:39
  78.5 0.7 collective-permute-done.26.refs_6_
  79.2 1.5 %backward.7 = (f32[520,128]{1,0:T(8,128)S(1)}, f32[520,128]{1,0:T(8,128)S(1)}, f32[32,8,128]{2,1,0:T(8,128)S(1)}) custom-call(f32[512,256]{1,0:T(8,128)S(1)} %get-tuple-element.71.refs_0_, f32[8,256]{1,0:T(8,128)S(1)} %get-tuple-element.72.refs_1_, f32[1040,128]{1,0:T(8,128)S(1)} %get-tuple-element.63.refs_2_.refs_0_, ...), custom_call_target="tpu_custom_call" | custom-call | flops 301989888 | bytes 1048576 | tf_op jit(solution)/shard_map/backward/pallas_call | solution.py:67
  80.7 1.8 %collective-permute-start.29 = (f32[520,128]{1,0:T(8,128)S(1)}, f32[520,128]{1,0:T(8,128)S(1)}, u32[]{:S(2)}, u32[]{:S(2)}) collective-permute-start(f32[520,128]{1,0:T(8,128)S(1)} %get-tuple-element.78.refs_3_), channel_id=1, source_target_pairs={{0,2},{2,0},{4,6},{6,4},{8,10},{10,8},{12,14},{14,12},{16,18},{18,... | collective-permute-start | bytes 798728 | tf_op jit(solution)/shard_map/ppermute | solution.py:39
  82.5 0.4 collective-permute-start.28
  82.9 11.8 %all_to_all.11.refs_7_ = f32[32,8,128]{2,1,0:T(8,128)S(1)} all-to-all(f32[32,8,128]{2,1,0:T(8,128)S(1)} %get-tuple-element.80), channel_id=1, replica_groups=mesh['page'=8,'query'=2,'head'=2] {'page','query','head'}, dimensions={0} | all-to-all | bytes 262144 | tf_op jit(solution)/shard_map/all_to_all | solution.py:505
  94.7 1.2 %last_update.1 = (f32[4,256,128]{2,1,0:T(8,128)}, f32[4,256,128]{2,1,0:T(8,128)}, f32[4,256]{1,0:T(4,128)}) custom-call(f32[1040,128]{1,0:T(8,128)S(1)} %get-tuple-element.63.refs_2_.refs_0_, f32[1040,128]{1,0:T(8,128)S(1)} %collective-permute-done.14.refs_1_, f32[1040,128]{1,0:T(8,128)S(1)} %collective-permute-done.21.refs_2_, ...), custom_call_target="tpu_custom_call" | custom-call | flops 1048576 | bytes 1048576 | tf_op jit(solution)/shard_map/last_update/pallas_call | solution.py:67
  (46 shorter events, 1.5 us)
Async XLA Ops:
  0.6 5.2 %copy-start.3 = (f32[4,256,128]{2,1,0:T(8,128)S(1)}, f32[4,256,128]{2,1,0:T(8,128)}, u32[]{:S(2)}) copy-start(f32[4,256,128]{2,1,0:T(8,128)} %refs_4_.3) | copy-start | bytes 1572868
  0.6 5.2 %copy-start.2 = (f32[4,256,128]{2,1,0:T(8,128)S(1)}, f32[4,256,128]{2,1,0:T(8,128)}, u32[]{:S(2)}) copy-start(f32[4,256,128]{2,1,0:T(8,128)} %refs_2_.3) | copy-start | bytes 1572868
  0.7 5.2 %copy-start.1 = (f32[4,256,128]{2,1,0:T(8,128)S(1)}, f32[4,256,128]{2,1,0:T(8,128)}, u32[]{:S(2)}) copy-start(f32[4,256,128]{2,1,0:T(8,128)} %refs_1_.3) | copy-start | bytes 1572868
  0.7 5.2 %copy-start = (f32[4,256,128]{2,1,0:T(8,128)S(1)}, f32[4,256,128]{2,1,0:T(8,128)}, u32[]{:S(2)}) copy-start(f32[4,256,128]{2,1,0:T(8,128)} %refs_0_.3) | copy-start | bytes 1572868
  0.7 5.2 %copy-start.4 = (f32[4,256]{1,0:T(4,128)S(1)}, f32[4,256]{1,0:T(4,128)}, u32[]{:S(2)}) copy-start(f32[4,256]{1,0:T(4,128)} %refs_3_.3) | copy-start | bytes 12292
  0.7 5.2 %copy-start.5 = (s32[4,256]{1,0:T(4,128)S(1)}, s32[4,256]{1,0:T(4,128)}, u32[]{:S(2)}) copy-start(s32[4,256]{1,0:T(4,128)} %refs_5_.3) | copy-start | bytes 12292
  2.7 3.2 %copy-start.6 = (s32[8]{0:T(128)S(1)}, s32[8]{0:T(128)}, u32[]{:S(2)}) copy-start(s32[8]{0:T(128)} %refs_6_.3) | copy-start | bytes 100
  2.7 3.8 %collective-permute-start = (f32[520,128]{1,0:T(8,128)}, f32[520,128]{1,0:T(8,128)S(1)}, u32[]{:S(2)}, u32[]{:S(2)}) collective-permute-start(f32[520,128]{1,0:T(8,128)} %get-tuple-element.43), channel_id=1, source_target_pairs={{0,4},{4,0},{8,12},{12,8},{16,20},{20,16},{24,28},{28,24},{1,5},{5... | collective-permute-start | bytes 798728 | tf_op jit(solution)/shard_map/ppermute | solution.py:39
  3.3 8.8 %collective-permute-start.1 = (f32[328,128]{1,0:T(8,128)}, f32[328,128]{1,0:T(8,128)S(1)}, u32[]{:S(2)}, u32[]{:S(2)}) collective-permute-start(f32[328,128]{1,0:T(8,128)} %get-tuple-element.45), channel_id=1, source_target_pairs={{0,2},{2,0},{1,3},{3,1},{4,6},{6,4},{5,7},{7,5},{8,10},{10,8},{9,1... | collective-permute-start | bytes 503816 | tf_op jit(solution)/shard_map/ppermute | solution.py:39
  7.6 9.7 %collective-permute-start.5 = (f32[72,128]{1,0:T(8,128)S(1)}, f32[72,128]{1,0:T(8,128)S(1)}, u32[]{:S(2)}, u32[]{:S(2)}) collective-permute-start(f32[72,128]{1,0:T(8,128)S(1)} %get-tuple-element.53), channel_id=1, source_target_pairs={{0,8},{4,12},{8,0},{12,4},{16,24},{20,28},{24,16},{28,20},{1,9},{5... | collective-permute-start | bytes 110600 | tf_op jit(solution)/shard_map/ppermute | solution.py:39
  9.2 8.3 %collective-permute-start.6 = (f32[72,128]{1,0:T(8,128)S(1)}, f32[72,128]{1,0:T(8,128)S(1)}, u32[]{:S(2)}, u32[]{:S(2)}) collective-permute-start(f32[72,128]{1,0:T(8,128)S(1)} %get-tuple-element.54), channel_id=1, source_target_pairs={{0,16},{4,20},{8,24},{12,28},{16,0},{20,4},{24,8},{28,12},{1,17},{... | collective-permute-start | bytes 110600 | tf_op jit(solution)/shard_map/ppermute | solution.py:39
  11.8 6.2 %collective-permute-start.7 = (f32[72,128]{1,0:T(8,128)S(1)}, f32[72,128]{1,0:T(8,128)S(1)}, u32[]{:S(2)}, u32[]{:S(2)}) collective-permute-start(f32[72,128]{1,0:T(8,128)S(1)} %get-tuple-element.55), channel_id=1, source_target_pairs={{0,24},{4,28},{8,16},{12,20},{16,8},{20,12},{24,0},{28,4},{1,25},{... | collective-permute-start | bytes 110600 | tf_op jit(solution)/shard_map/ppermute | solution.py:39
  13.1 8.4 %collective-permute-start.2 = (f32[72,128]{1,0:T(8,128)S(1)}, f32[72,128]{1,0:T(8,128)S(1)}, u32[]{:S(2)}, u32[]{:S(2)}) collective-permute-start(f32[72,128]{1,0:T(8,128)S(1)} %get-tuple-element.49), channel_id=1, source_target_pairs={{0,8},{4,12},{8,0},{12,4},{16,24},{20,28},{24,16},{28,20},{1,9},{5... | collective-permute-start | bytes 110600 | tf_op jit(solution)/shard_map/ppermute | solution.py:39
  13.8 9.0 %collective-permute-start.3 = (f32[72,128]{1,0:T(8,128)S(1)}, f32[72,128]{1,0:T(8,128)S(1)}, u32[]{:S(2)}, u32[]{:S(2)}) collective-permute-start(f32[72,128]{1,0:T(8,128)S(1)} %get-tuple-element.50), channel_id=1, source_target_pairs={{0,16},{4,20},{8,24},{12,28},{16,0},{20,4},{24,8},{28,12},{1,17},{... | collective-permute-start | bytes 110600 | tf_op jit(solution)/shard_map/ppermute | solution.py:39
  17.3 5.8 %collective-permute-start.4 = (f32[72,128]{1,0:T(8,128)S(1)}, f32[72,128]{1,0:T(8,128)S(1)}, u32[]{:S(2)}, u32[]{:S(2)}) collective-permute-start(f32[72,128]{1,0:T(8,128)S(1)} %get-tuple-element.51), channel_id=1, source_target_pairs={{0,24},{4,28},{8,16},{12,20},{16,8},{20,12},{24,0},{28,4},{1,25},{... | collective-permute-start | bytes 110600 | tf_op jit(solution)/shard_map/ppermute | solution.py:39
  18.4 7.8 %collective-permute-start.13 = (f32[72,128]{1,0:T(8,128)S(1)}, f32[72,128]{1,0:T(8,128)S(1)}, u32[]{:S(2)}, u32[]{:S(2)}) collective-permute-start(f32[72,128]{1,0:T(8,128)S(1)} %merge.4.refs_5_), channel_id=1, source_target_pairs={{0,24},{4,28},{8,16},{12,20},{16,8},{20,12},{24,0},{28,4},{1,25},{... | collective-permute-start | bytes 110600 | tf_op jit(solution)/shard_map/ppermute | solution.py:39
  21.5 6.3 %collective-permute-start.12 = (f32[72,128]{1,0:T(8,128)S(1)}, f32[72,128]{1,0:T(8,128)S(1)}, u32[]{:S(2)}, u32[]{:S(2)}) collective-permute-start(f32[72,128]{1,0:T(8,128)S(1)} %merge.4.refs_5_), channel_id=1, source_target_pairs={{0,16},{4,20},{8,24},{12,28},{16,0},{20,4},{24,8},{28,12},{1,17},{... | collective-permute-start | bytes 110600 | tf_op jit(solution)/shard_map/ppermute | solution.py:39
  21.5 6.3 %collective-permute-start.11 = (f32[72,128]{1,0:T(8,128)S(1)}, f32[72,128]{1,0:T(8,128)S(1)}, u32[]{:S(2)}, u32[]{:S(2)}) collective-permute-start(f32[72,128]{1,0:T(8,128)S(1)} %merge.4.refs_5_), channel_id=1, source_target_pairs={{0,8},{4,12},{8,0},{12,4},{16,24},{20,28},{24,16},{28,20},{1,9},{5... | collective-permute-start | bytes 110600 | tf_op jit(solution)/shard_map/ppermute | solution.py:39
  23.4 5.8 %collective-permute-start.10 = (f32[72,128]{1,0:T(8,128)S(1)}, f32[72,128]{1,0:T(8,128)S(1)}, u32[]{:S(2)}, u32[]{:S(2)}) collective-permute-start(f32[72,128]{1,0:T(8,128)S(1)} %merge.5.refs_5_), channel_id=1, source_target_pairs={{0,24},{4,28},{8,16},{12,20},{16,8},{20,12},{24,0},{28,4},{1,25},{... | collective-permute-start | bytes 110600 | tf_op jit(solution)/shard_map/ppermute | solution.py:39
  26.2 4.9 %collective-permute-start.9 = (f32[72,128]{1,0:T(8,128)S(1)}, f32[72,128]{1,0:T(8,128)S(1)}, u32[]{:S(2)}, u32[]{:S(2)}) collective-permute-start(f32[72,128]{1,0:T(8,128)S(1)} %merge.5.refs_5_), channel_id=1, source_target_pairs={{0,16},{4,20},{8,24},{12,28},{16,0},{20,4},{24,8},{28,12},{1,17},{... | collective-permute-start | bytes 110600 | tf_op jit(solution)/shard_map/ppermute | solution.py:39
  26.2 4.9 %collective-permute-start.8 = (f32[72,128]{1,0:T(8,128)S(1)}, f32[72,128]{1,0:T(8,128)S(1)}, u32[]{:S(2)}, u32[]{:S(2)}) collective-permute-start(f32[72,128]{1,0:T(8,128)S(1)} %merge.5.refs_5_), channel_id=1, source_target_pairs={{0,8},{4,12},{8,0},{12,4},{16,24},{20,28},{24,16},{28,20},{1,9},{5... | collective-permute-start | bytes 110600 | tf_op jit(solution)/shard_map/ppermute | solution.py:39
  45.6 17.0 %collective-permute-start.14 = (f32[1040,128]{1,0:T(8,128)S(1)}, f32[1040,128]{1,0:T(8,128)S(1)}, u32[]{:S(2)}, u32[]{:S(2)}) collective-permute-start(f32[1040,128]{1,0:T(8,128)S(1)} %get-tuple-element.63.refs_2_.refs_0_), channel_id=1, source_target_pairs={{0,2},{2,0},{1,3},{3,1},{4,6},{6,4},{5,7},{7,5},{8,10},{10,8},{9,1... | collective-permute-start | bytes 1597448 | tf_op jit(solution)/shard_map/ppermute | solution.py:39
  45.9 4.4 %collective-permute-start.15 = (f32[72,128]{1,0:T(8,128)S(1)}, f32[72,128]{1,0:T(8,128)S(1)}, u32[]{:S(2)}, u32[]{:S(2)}) collective-permute-start(f32[72,128]{1,0:T(8,128)S(1)} %get-tuple-element.67), channel_id=1, source_target_pairs={{0,8},{4,12},{8,0},{12,4},{16,24},{20,28},{24,16},{28,20},{1,9},{5... | collective-permute-start | bytes 110600 | tf_op jit(solution)/shard_map/ppermute | solution.py:39
  46.6 4.9 %collective-permute-start.16 = (f32[72,128]{1,0:T(8,128)S(1)}, f32[72,128]{1,0:T(8,128)S(1)}, u32[]{:S(2)}, u32[]{:S(2)}) collective-permute-start(f32[72,128]{1,0:T(8,128)S(1)} %get-tuple-element.68), channel_id=1, source_target_pairs={{0,16},{4,20},{8,24},{12,28},{16,0},{20,4},{24,8},{28,12},{1,17},{... | collective-permute-start | bytes 110600 | tf_op jit(solution)/shard_map/ppermute | solution.py:39
  47.9 5.8 %collective-permute-start.17 = (f32[72,128]{1,0:T(8,128)S(1)}, f32[72,128]{1,0:T(8,128)S(1)}, u32[]{:S(2)}, u32[]{:S(2)}) collective-permute-start(f32[72,128]{1,0:T(8,128)S(1)} %get-tuple-element.69), channel_id=1, source_target_pairs={{0,24},{4,28},{8,16},{12,20},{16,8},{20,12},{24,0},{28,4},{1,25},{... | collective-permute-start | bytes 110600 | tf_op jit(solution)/shard_map/ppermute | solution.py:39
  53.9 5.9 %collective-permute-start.20 = (f32[72,128]{1,0:T(8,128)S(1)}, f32[72,128]{1,0:T(8,128)S(1)}, u32[]{:S(2)}, u32[]{:S(2)}) collective-permute-start(f32[72,128]{1,0:T(8,128)S(1)} %merge.6.refs_4_.refs_5_), channel_id=1, source_target_pairs={{0,24},{4,28},{8,16},{12,20},{16,8},{20,12},{24,0},{28,4},{1,25},{... | collective-permute-start | bytes 110600 | tf_op jit(solution)/shard_map/ppermute | solution.py:39
  56.4 4.9 %collective-permute-start.19 = (f32[72,128]{1,0:T(8,128)S(1)}, f32[72,128]{1,0:T(8,128)S(1)}, u32[]{:S(2)}, u32[]{:S(2)}) collective-permute-start(f32[72,128]{1,0:T(8,128)S(1)} %merge.6.refs_4_.refs_5_), channel_id=1, source_target_pairs={{0,16},{4,20},{8,24},{12,28},{16,0},{20,4},{24,8},{28,12},{1,17},{... | collective-permute-start | bytes 110600 | tf_op jit(solution)/shard_map/ppermute | solution.py:39
  56.4 4.9 %collective-permute-start.18 = (f32[72,128]{1,0:T(8,128)S(1)}, f32[72,128]{1,0:T(8,128)S(1)}, u32[]{:S(2)}, u32[]{:S(2)}) collective-permute-start(f32[72,128]{1,0:T(8,128)S(1)} %merge.6.refs_4_.refs_5_), channel_id=1, source_target_pairs={{0,8},{4,12},{8,0},{12,4},{16,24},{20,28},{24,16},{28,20},{1,9},{5... | collective-permute-start | bytes 110600 | tf_op jit(solution)/shard_map/ppermute | solution.py:39
  62.7 32.0 %collective-permute-start.21 = (f32[1040,128]{1,0:T(8,128)S(1)}, f32[1040,128]{1,0:T(8,128)S(1)}, u32[]{:S(2)}, u32[]{:S(2)}) collective-permute-start(f32[1040,128]{1,0:T(8,128)S(1)} %mate_parts.1), channel_id=1, source_target_pairs={{0,4},{4,0},{8,12},{12,8},{16,20},{20,16},{24,28},{28,24},{1,5},{5... | collective-permute-start | bytes 1597448 | tf_op jit(solution)/shard_map/ppermute | solution.py:39
  63.8 4.5 %collective-permute-start.22 = (f32[72,128]{1,0:T(8,128)S(1)}, f32[72,128]{1,0:T(8,128)S(1)}, u32[]{:S(2)}, u32[]{:S(2)}) collective-permute-start(f32[72,128]{1,0:T(8,128)S(1)} %get-tuple-element.74), channel_id=1, source_target_pairs={{0,8},{4,12},{8,0},{12,4},{16,24},{20,28},{24,16},{28,20},{1,9},{5... | collective-permute-start | bytes 110600 | tf_op jit(solution)/shard_map/ppermute | solution.py:39
  64.9 5.7 %collective-permute-start.23 = (f32[72,128]{1,0:T(8,128)S(1)}, f32[72,128]{1,0:T(8,128)S(1)}, u32[]{:S(2)}, u32[]{:S(2)}) collective-permute-start(f32[72,128]{1,0:T(8,128)S(1)} %get-tuple-element.75), channel_id=1, source_target_pairs={{0,16},{4,20},{8,24},{12,28},{16,0},{20,4},{24,8},{28,12},{1,17},{... | collective-permute-start | bytes 110600 | tf_op jit(solution)/shard_map/ppermute | solution.py:39
  66.2 5.8 %collective-permute-start.24 = (f32[72,128]{1,0:T(8,128)S(1)}, f32[72,128]{1,0:T(8,128)S(1)}, u32[]{:S(2)}, u32[]{:S(2)}) collective-permute-start(f32[72,128]{1,0:T(8,128)S(1)} %get-tuple-element.76), channel_id=1, source_target_pairs={{0,24},{4,28},{8,16},{12,20},{16,8},{20,12},{24,0},{28,4},{1,25},{... | collective-permute-start | bytes 110600 | tf_op jit(solution)/shard_map/ppermute | solution.py:39
  72.3 6.2 %collective-permute-start.27 = (f32[72,128]{1,0:T(8,128)S(1)}, f32[72,128]{1,0:T(8,128)S(1)}, u32[]{:S(2)}, u32[]{:S(2)}) collective-permute-start(f32[72,128]{1,0:T(8,128)S(1)} %merge.7.refs_4_), channel_id=1, source_target_pairs={{0,24},{4,28},{8,16},{12,20},{16,8},{20,12},{24,0},{28,4},{1,25},{... | collective-permute-start | bytes 110600 | tf_op jit(solution)/shard_map/ppermute | solution.py:39
  74.3 4.9 %collective-permute-start.26 = (f32[72,128]{1,0:T(8,128)S(1)}, f32[72,128]{1,0:T(8,128)S(1)}, u32[]{:S(2)}, u32[]{:S(2)}) collective-permute-start(f32[72,128]{1,0:T(8,128)S(1)} %merge.7.refs_4_), channel_id=1, source_target_pairs={{0,16},{4,20},{8,24},{12,28},{16,0},{20,4},{24,8},{28,12},{1,17},{... | collective-permute-start | bytes 110600 | tf_op jit(solution)/shard_map/ppermute | solution.py:39
  74.3 4.9 %collective-permute-start.25 = (f32[72,128]{1,0:T(8,128)S(1)}, f32[72,128]{1,0:T(8,128)S(1)}, u32[]{:S(2)}, u32[]{:S(2)}) collective-permute-start(f32[72,128]{1,0:T(8,128)S(1)} %merge.7.refs_4_), channel_id=1, source_target_pairs={{0,8},{4,12},{8,0},{12,4},{16,24},{20,28},{24,16},{28,20},{1,9},{5... | collective-permute-start | bytes 110600 | tf_op jit(solution)/shard_map/ppermute | solution.py:39
  80.7 14.0 %collective-permute-start.29 = (f32[520,128]{1,0:T(8,128)S(1)}, f32[520,128]{1,0:T(8,128)S(1)}, u32[]{:S(2)}, u32[]{:S(2)}) collective-permute-start(f32[520,128]{1,0:T(8,128)S(1)} %get-tuple-element.78.refs_3_), channel_id=1, source_target_pairs={{0,2},{2,0},{4,6},{6,4},{8,10},{10,8},{12,14},{14,12},{16,18},{18,... | collective-permute-start | bytes 798728 | tf_op jit(solution)/shard_map/ppermute | solution.py:39
  82.5 12.2 %collective-permute-start.30 = (f32[520,128]{1,0:T(8,128)S(1)}, f32[520,128]{1,0:T(8,128)S(1)}, u32[]{:S(2)}, u32[]{:S(2)}) collective-permute-start(f32[520,128]{1,0:T(8,128)S(1)} %get-tuple-element.79), channel_id=1, source_target_pairs={{0,6},{2,4},{4,2},{6,0},{8,14},{10,12},{12,10},{14,8},{16,22},{18,... | collective-permute-start | bytes 798728 | tf_op jit(solution)/shard_map/ppermute | solution.py:39
  82.5 12.2 %collective-permute-start.28 = (f32[520,128]{1,0:T(8,128)S(1)}, f32[520,128]{1,0:T(8,128)S(1)}, u32[]{:S(2)}, u32[]{:S(2)}) collective-permute-start(f32[520,128]{1,0:T(8,128)S(1)} %get-tuple-element.79), channel_id=1, source_target_pairs={{0,4},{2,6},{4,0},{6,2},{8,12},{10,14},{12,8},{14,10},{16,20},{18,... | collective-permute-start | bytes 798728 | tf_op jit(solution)/shard_map/ppermute | solution.py:39

commit v14 on v6

--- a/solution.py
+++ b/solution.py
@@ -110,6 +110,7 @@
         part_rows * query_devices % ranks == 0
         and chunk % 128 == 0
         and part_rows % (8 * ranks) == 0
+        and (part_rows // ranks % 128 == 0 or 1024 % (part_rows // ranks * 8) == 0)
         and slot_rows % width == 0
         and part_rows % width == 0
         and max(slot_rows, part_rows) < TAIL * width
@@ -329,11 +330,60 @@
     forward_shapes = [chunk_shape] * ranks + [(slots, query_rows), (TAIL, query_rows)]
     chunk_scratch = [pltpu.VMEM((ranks,) + chunk_shape, jnp.float32)]
 
-    def first_body(*refs):
-        state_refs, refs = refs[:2], refs[2:]
-        query_refs, refs = refs[:query_devices], refs[query_devices:]
-        chunk_outs, refs = refs[:ranks], refs[ranks:]
-        forward(state_refs, query_refs, chunk_outs, *refs)
+    fold = max(1, 128 // piece)
+    folded, columns = width // fold, fold * piece
+    piece_shape = (folded + TAIL, columns)
+    piece_scratch = [pltpu.VMEM((ranks,) + piece_shape, jnp.float32)]
+
+    def fold_rows(value):
+        groups = [value[at * folded : (at + 1) * folded, :] for at in range(fold)]
+        return jnp.concatenate(groups, axis=1)
+
+    def unfold_rows(value):
+        groups = [value[:, at * piece : (at + 1) * piece] for at in range(fold)]
+        return jnp.concatenate(groups, axis=0)
+
+    def rows_tail(rows):
+        empty = jnp.zeros((TAIL - len(rows), columns), jnp.float32)
+        return jnp.concatenate(rows + [empty], axis=0)
+
+    def part_body(*refs):
+        state_refs, (query_ref, *refs) = refs[:CORES], refs[CORES:]
+        piece_outs, (weights_out, max_out, pieces) = refs[:ranks], refs[ranks:]
+        rank, _, _ = places()
+        queries = halves(query_ref[:part_rows, :])
+        position_row = tail_as_row(query_ref, part_rows + piece, pos_rows)
+        all_scores, all_visible = [], []
+        for ref in state_refs:
+            scores = dot(halves(ref[:slot_rows, :]), queries, 1, 1) * score_scale
+            bias = row_as_column(tail_as_row(ref, 2 * slot_rows, bias_rows), width)
+            scores = scores + jnp.concatenate([bias] * (part_rows // width), axis=1)
+            page_start = ref[packed_rows - 1 : packed_rows, 0:1]
+            visible = jnp.broadcast_to(position_row >= page_start, scores.shape)
+            all_scores.append(jnp.where(visible, scores, MASKED))
+            all_visible.append(visible)
+        row_max = jnp.max(all_scores[0], axis=0, keepdims=True)
+        for scores in all_scores[1:]:
+            row_max = jnp.maximum(row_max, jnp.max(scores, axis=0, keepdims=True))
+        row_total = jnp.zeros_like(row_max)
+        row_sum = jnp.zeros((width, part_rows), jnp.float32)
+        for at, ref in enumerate(state_refs):
+            weights = jnp.where(all_visible[at], jnp.exp(all_scores[at] - row_max), 0.0)
+            weights_out[at * slot_rows : (at + 1) * slot_rows, :] = weights
+            row_total = row_total + jnp.sum(weights, axis=0, keepdims=True)
+            values = halves(ref[slot_rows : 2 * slot_rows, :])
+            row_sum = row_sum + dot(values, halves(weights), 0, 0)
+        max_out[...] = jnp.broadcast_to(row_max, (TAIL, part_rows))
+        for at in range(ranks):
+            own = slice(at * piece, (at + 1) * piece)
+            pieces[at, :folded, :] = fold_rows(row_sum[:, own])
+            pieces[at, folded:, :] = rows_tail(
+                [jnp.concatenate([row[:, own]] * fold, axis=1) for row in (row_max, row_total)]
+            )
+        for turn in range(ranks):
+            piece_outs[turn][...] = pieces[rank ^ turn]
+
+    part_shapes = [piece_shape] * ranks + [(slots, part_rows), (TAIL, part_rows)]
 
     def next_body(*refs):
         state_refs, refs = refs[:2], refs[2:]
@@ -350,30 +400,57 @@
             state_outs[at][2 * slot_rows :, :] = bias
         forward(state_outs, query_refs, chunk_outs, *refs)
 
-    def merge_body(*refs):
-        query_refs, refs = refs[:query_devices], refs[query_devices:]
-        chunk_refs, (merged_out,) = refs[:ranks], refs[ranks:]
+    def merged_chunk(query_refs, sums, maxima, totals, out):
         targets = jnp.concatenate(
             [ref[part_rows : part_rows + piece, :] for ref in query_refs], axis=0
         )
-        row_max = chunk_refs[0][width : width + 1, :]
-        for ref in chunk_refs[1:]:
-            row_max = jnp.maximum(row_max, ref[width : width + 1, :])
+        row_max = maxima[0]
+        for other in maxima[1:]:
+            row_max = jnp.maximum(row_max, other)
         row_total = jnp.zeros_like(row_max)
         row_sum = jnp.zeros((width, chunk), jnp.float32)
-        for ref in chunk_refs:
-            factor = jnp.exp(ref[width : width + 1, :] - row_max)
-            row_total = row_total + ref[width + 1 : width + 2, :] * factor
-            row_sum = row_sum + ref[:width, :] * factor
+        for part_sum, part_max, part_total in zip(sums, maxima, totals):
+            factor = jnp.exp(part_max - row_max)
+            row_total = row_total + part_total * factor
+            row_sum = row_sum + part_sum * factor
         output = row_sum / row_total
         residual = output - targets.T
         row_delta = jnp.sum(residual * output, axis=0, keepdims=True)
-        merged_out[:width, :] = residual
-        merged_out[width:, :] = jnp.concatenate(
+        out[:width, :] = residual
+        out[width:, :] = jnp.concatenate(
             [row_max, row_total, row_delta, jnp.zeros((TAIL - 3, chunk), jnp.float32)], axis=0
         )
 
-    def backward_body(weights_ref, max_ref, *refs):
+    def first_merge_body(*refs):
+        query_refs, (*piece_refs, merged_out) = refs[:query_devices], refs[query_devices:]
+
+        def joined(read):
+            return [
+                jnp.concatenate([read(ref) for ref in piece_refs[turn::ranks]], axis=1)
+                for turn in range(ranks)
+            ]
+
+        merged_chunk(
+            query_refs,
+            joined(lambda ref: unfold_rows(ref[:folded, :])),
+            joined(lambda ref: ref[folded : folded + 1, :piece]),
+            joined(lambda ref: ref[folded + 1 : folded + 2, :piece]),
+            merged_out,
+        )
+
+    def merge_body(*refs):
+        query_refs, (*chunk_refs, merged_out) = refs[:query_devices], refs[query_devices:]
+        merged_chunk(
+            query_refs,
+            [ref[:width, :] for ref in chunk_refs],
+            [ref[width : width + 1, :] for ref in chunk_refs],
+            [ref[width + 1 : width + 2, :] for ref in chunk_refs],
+            merged_out,
+        )
+
+    def backward_body(*refs):
+        weights_refs, refs = refs[: len(weights)], refs[len(weights) :]
+        max_refs, refs = refs[: len(weights)], refs[len(weights) :]
         state_refs, refs = parts_of(refs[: len(states)]), refs[len(states) :]
         query_refs, refs = refs[:query_devices], refs[query_devices:]
         merged_refs, refs = refs[:ranks], refs[ranks:]
@@ -381,19 +458,34 @@
         rank, _, _ = places()
         for turn in range(ranks):
             chunks[rank ^ turn] = merged_refs[turn][...]
-        joined = jnp.concatenate([chunks[at] for at in range(ranks)], axis=1)
+        if len(weights_refs) == 1:
+            joined = jnp.concatenate([chunks[at] for at in range(ranks)], axis=1)
+            all_queries = read_queries(query_refs)
+        else:
+            joined = jnp.concatenate(
+                [
+                    chunks[at, :, part * piece : (part + 1) * piece]
+                    for part in range(query_devices)
+                    for at in range(ranks)
+                ],
+                axis=1,
+            )
+            all_queries = halves(
+                jnp.concatenate([ref[:part_rows, :] for ref in query_refs], axis=0)
+            )
         residual = joined[:width, :]
         row_max, row_total, row_delta = (
             joined[width + at : width + at + 1, :] for at in range(3)
         )
-        all_queries = read_queries(query_refs)
         residual = halves(residual)
-        factor = jnp.exp(max_ref[0:1, :] - row_max) / row_total
+        maxima = jnp.concatenate([ref[0:1, :] for ref in max_refs], axis=1)
+        factor = jnp.exp(maxima - row_max) / row_total
         ones = jnp.ones((TAIL, query_rows), jnp.bfloat16)
         ones = (ones, jnp.zeros_like(ones))
         squares = [jnp.zeros((1, width), jnp.float32)] * 3
         for at, ref in enumerate(state_refs):
-            attention = weights_ref[at * slot_rows : (at + 1) * slot_rows, :] * factor
+            rows = slice(at * slot_rows, (at + 1) * slot_rows)
+            attention = jnp.concatenate([part[rows, :] for part in weights_refs], axis=1) * factor
             grad_values = dot(halves(attention), residual, 1, 1)
             grad_probs = dot(halves(ref[slot_rows : 2 * slot_rows, :]), residual, 1, 0)
             grad_scores = halves(attention * (grad_probs - row_delta))
@@ -423,16 +515,24 @@
     for repeat in range(STEPS):
         last = repeat == STEPS - 1
         if repeat == 0:
-            *chunk_parts, weights, maxima = call(
-                first_body,
-                forward_shapes,
-                "forward",
-                2 * matmul_cost,
-                states + query_parts,
-                chunk_scratch,
-            )
+            sums, weights, maxima = [], [], []
+            for query_part in query_parts:
+                *pieces, part_weights, part_max = call(
+                    part_body,
+                    part_shapes,
+                    "forward",
+                    2 * matmul_cost // query_devices,
+                    states + [query_part],
+                    piece_scratch,
+                    after=maxima[-1:],
+                )
+                sums += pieces[:1] + [
+                    exchange(pieces[turn], page=CORES * turn) for turn in range(1, ranks)
+                ]
+                weights.append(part_weights)
+                maxima.append(part_max)
         else:
-            new_state, *chunk_parts, weights, maxima = call(
+            new_state, *chunk_parts, part_weights, part_max = call(
                 next_body,
                 [(CORES * packed_rows, width)] + forward_shapes,
                 "update_forward",
@@ -440,21 +540,21 @@
                 states + query_parts + grads + tiles,
                 chunk_scratch,
             )
-            states = [new_state]
-        arrived = {
-            turn: exchange(chunk_parts[turn], page=CORES * turn)
-            for turn in reversed(range(1, ranks))
-        }
-        if repeat:
+            states, weights, maxima = [new_state], [part_weights], [part_max]
+            arrived = {
+                turn: exchange(chunk_parts[turn], page=CORES * turn)
+                for turn in reversed(range(1, ranks))
+            }
+            sums = chunk_parts[:1] + list(arrived.values())
             new_states = states + [
                 exchange(states[0], query=turn) for turn in range(1, query_devices)
             ]
         (merged,) = call(
-            merge_body,
+            merge_body if repeat else first_merge_body,
             [chunk_shape],
             "merge",
             2**20,
-            query_parts + chunk_parts[:1] + list(arrived.values()),
+            query_parts + sums,
         )
         all_merged = [merged] + [
             exchange(merged, page=CORES * turn) for turn in range(1, ranks)
@@ -474,7 +574,7 @@
             packed_shapes + [(devices, TAIL, width)],
             "backward",
             3 * matmul_cost,
-            [weights, maxima] + states + query_parts + all_merged,
+            weights + maxima + states + query_parts + all_merged,
             scratch=chunk_scratch,
         )
         grads = [own_grad, mate_grad]

time: 84.4 us -> 83.8 us (level)
  waiting for transfers between devices: 23.4 us -> 17.3 us
  starting transfers between devices: 23.6 us -> 27.9 us
  Pallas kernels: 10.9 us -> 11.9 us
    ppermute x19 -> x22, waiting for transfers between devices: 23.4 us -> 17.3 us  [exchange(): return lax.ppermute(value, axes, pairs)]
    ppermute x19 -> x22, starting transfers between devices: 23.6 us -> 27.9 us  [exchange(): return lax.ppermute(value, axes, pairs)]
    pallas_call x10 -> x11, Pallas kernels: 10.9 us -> 11.9 us  [call(): pl.pallas_call(without_after, out_shape=[jax.ShapeDtypeStruct(shape, jnp....]
  transfers between devices with their start and end apart: 19 -> 22, of which waited for: 9 -> 9; matrix products, arithmetic and copies ran while one was open for 0% -> 0% of each run, Pallas kernels for 3% -> 6%
where the time goes in v14:
time: 83.8 us; the launch traced here: 83.6 us
  starting transfers between devices  27.9 us (33%)
  blocking collectives  25.6 us (31%)
  waiting for transfers between devices  17.3 us (21%)
  Pallas kernels  11.9 us (14%)
    ppermute x22, starting transfers between devices, exchange(): return lax.ppermute(value, axes, pairs)  27.9 us
    all_to_all x2, blocking collectives, direct_per_device(): lax.all_to_all(squares, ('page', 'query', 'head'), split_axis=0, concat_a...  25.6 us
    ppermute x22, waiting for transfers between devices, exchange(): return lax.ppermute(value, axes, pairs)  17.3 us
    pallas_call x11, Pallas kernels, call(): pl.pallas_call(without_after, out_shape=[jax.ShapeDtypeStruct(shape, jnp....  11.9 us
  transfers between devices with their start and end apart: 22, of which 9 were waited for; matrix products, arithmetic and copies ran while one was open for 0% of the time, Pallas kernels for 6%

profile of v14, /device:TPU:0, one launch (start us, length us, event | category | flops | bytes accessed | tf_op | source)
XLA Modules:
  0.0 83.6 jit_solution(3806473045642053556)
XLA Ops:
  0.7 2.0 %pack.1 = (f32[520,128]{1,0:T(8,128)}, f32[328,128]{1,0:T(8,128)}) custom-call(f32[4,256,128]{2,1,0:T(8,128)} %refs_0_.3, f32[4,256,128]{2,1,0:T(8,128)} %refs_1_.3, f32[4,256,128]{2,1,0:T(8,128)} %refs_2_.3, f32[4,256]{1,0:T(4,128)} %refs_3_.3, f32[4,256,128]{2,1,0:T(8,128)} %refs_4_.3, s32[4,256]{1,0:T(4,128)} %refs_5_.3, s32[8]{0:T(128)} %refs_6_.3), custom_call_target="tpu_custom_call" | custom-call | flops 1048576 | bytes 1048576 | tf_op jit(solution)/shard_map/pack/pallas_call | solution.py:67
  2.7 0.0 copy-start.6
  2.7 0.5 collective-permute-start
  3.3 2.6 %collective-permute-start.1 = (f32[328,128]{1,0:T(8,128)}, f32[328,128]{1,0:T(8,128)S(1)}, u32[]{:S(2)}, u32[]{:S(2)}) collective-permute-start(f32[328,128]{1,0:T(8,128)} %get-tuple-element.35), channel_id=1, source_target_pairs={{0,2},{2,0},{1,3},{3,1},{4,6},{6,4},{5,7},{7,5},{8,10},{10,8},{9,1... | collective-permute-start | bytes 503816 | tf_op jit(solution)/shard_map/ppermute | solution.py:39
  5.9 0.7 own.1
  6.6 0.0 collective-permute-done.refs_1_.refs_5_
  6.6 1.0 %forward.2 = (f32[72,128]{1,0:T(8,128)S(1)}, f32[72,128]{1,0:T(8,128)S(1)}, f32[72,128]{1,0:T(8,128)S(1)}, f32[72,128]{1,0:T(8,128)S(1)}, f32[512,256]{1,0:T(8,128)S(1)}, /*index=5*/f32[8,256]{1,0:T(8,128)S(1)}) custom-call(f32[520,128]{1,0:T(8,128)S(1)} %get-tuple-element.32.refs_0_.refs_4_, f32[520,128]{1,0:T(8,128)S(1)} %collective-permute-done.refs_1_.refs_5_, ...), custom_call_target="tpu_custom_call" | custom-call | flops 201326592 | bytes 1048576 | tf_op jit(solution)/shard_map/forward/pallas_call | solution.py:67
  7.6 1.6 %collective-permute-start.2 = (f32[72,128]{1,0:T(8,128)S(1)}, f32[72,128]{1,0:T(8,128)S(1)}, u32[]{:S(2)}, u32[]{:S(2)}) collective-permute-start(f32[72,128]{1,0:T(8,128)S(1)} %get-tuple-element.41), channel_id=1, source_target_pairs={{0,8},{4,12},{8,0},{12,4},{16,24},{20,28},{24,16},{28,20},{1,9},{5... | collective-permute-start | bytes 110600 | tf_op jit(solution)/shard_map/ppermute | solution.py:39
  9.2 2.6 %collective-permute-start.3 = (f32[72,128]{1,0:T(8,128)S(1)}, f32[72,128]{1,0:T(8,128)S(1)}, u32[]{:S(2)}, u32[]{:S(2)}) collective-permute-start(f32[72,128]{1,0:T(8,128)S(1)} %get-tuple-element.42), channel_id=1, source_target_pairs={{0,16},{4,20},{8,24},{12,28},{16,0},{20,4},{24,8},{28,12},{1,17},{... | collective-permute-start | bytes 110600 | tf_op jit(solution)/shard_map/ppermute | solution.py:39
  11.8 0.2 collective-permute-start.4
  12.0 0.0 collective-permute-done.1.refs_2_.refs_1_.refs_7_.refs_3_.refs_4_
  12.0 1.0 %forward.3 = (f32[72,128]{1,0:T(8,128)S(1)}, f32[72,128]{1,0:T(8,128)S(1)}, f32[72,128]{1,0:T(8,128)S(1)}, f32[72,128]{1,0:T(8,128)S(1)}, f32[512,256]{1,0:T(8,128)S(1)}, /*index=5*/f32[8,256]{1,0:T(8,128)S(1)}) custom-call(f32[520,128]{1,0:T(8,128)S(1)} %get-tuple-element.32.refs_0_.refs_4_, f32[520,128]{1,0:T(8,128)S(1)} %collective-permute-done.refs_1_.refs_5_, ...), custom_call_target="tpu_custom_call" | custom-call | flops 201326592 | bytes 1048576 | tf_op jit(solution)/shard_map/forward/pallas_call | solution.py:67
  13.1 0.8 collective-permute-start.5
  13.8 3.5 %collective-permute-start.6 = (f32[72,128]{1,0:T(8,128)S(1)}, f32[72,128]{1,0:T(8,128)S(1)}, u32[]{:S(2)}, u32[]{:S(2)}) collective-permute-start(f32[72,128]{1,0:T(8,128)S(1)} %get-tuple-element.46), channel_id=1, source_target_pairs={{0,16},{4,20},{8,24},{12,28},{16,0},{20,4},{24,8},{28,12},{1,17},{... | collective-permute-start | bytes 110600 | tf_op jit(solution)/shard_map/ppermute | solution.py:39
  17.3 0.0 collective-permute-done.2.refs_3_
  17.3 0.2 collective-permute-start.7
  17.5 0.0 collective-permute-done.3.refs_4_
  17.5 0.6 collective-permute-done.4.refs_5_
  18.1 0.0 collective-permute-done.5.refs_7_
  18.1 1.6 %collective-permute-done.6.refs_8_ = f32[72,128]{1,0:T(8,128)S(1)} collective-permute-done((f32[72,128]{1,0:T(8,128)S(1)}, f32[72,128]{1,0:T(8,128)S(1)}, u32[]{:S(2)}, u32[]{:S(2)}) %collective-permute-start.6) | collective-permute-done | bytes 36896 | tf_op jit(solution)/shard_map/ppermute | solution.py:39
  19.7 3.4 %collective-permute-done.7.refs_9_ = f32[72,128]{1,0:T(8,128)S(1)} collective-permute-done((f32[72,128]{1,0:T(8,128)S(1)}, f32[72,128]{1,0:T(8,128)S(1)}, u32[]{:S(2)}, u32[]{:S(2)}) %collective-permute-start.7) | collective-permute-done | bytes 36896 | tf_op jit(solution)/shard_map/ppermute | solution.py:39
  23.1 0.3 merge.2.refs_8_
  23.3 0.5 collective-permute-start.10
  23.8 0.0 collective-permute-start.9
  23.8 4.0 %collective-permute-start.8 = (f32[136,128]{1,0:T(8,128)S(1)}, f32[136,128]{1,0:T(8,128)S(1)}, u32[]{:S(2)}, u32[]{:S(2)}) collective-permute-start(f32[136,128]{1,0:T(8,128)S(1)} %merge.2.refs_8_), channel_id=1, source_target_pairs={{0,8},{4,12},{8,0},{12,4},{16,24},{20,28},{24,16},{28,20},{1,9},{5... | collective-permute-start | bytes 208904 | tf_op jit(solution)/shard_map/ppermute | solution.py:39
  27.8 1.8 %collective-permute-done.10.refs_11_ = f32[136,128]{1,0:T(8,128)S(1)} collective-permute-done((f32[136,128]{1,0:T(8,128)S(1)}, f32[136,128]{1,0:T(8,128)S(1)}, u32[]{:S(2)}, u32[]{:S(2)}) %collective-permute-start.10) | collective-permute-done | bytes 69664 | tf_op jit(solution)/shard_map/ppermute | solution.py:39
  29.6 0.9 %collective-permute-done.9.refs_10_ = f32[136,128]{1,0:T(8,128)S(1)} collective-permute-done((f32[136,128]{1,0:T(8,128)S(1)}, f32[136,128]{1,0:T(8,128)S(1)}, u32[]{:S(2)}, u32[]{:S(2)}) %collective-permute-start.9) | collective-permute-done | bytes 69664 | tf_op jit(solution)/shard_map/ppermute | solution.py:39
  30.5 2.2 %backward.2 = (f32[520,128]{1,0:T(8,128)S(1)}, f32[520,128]{1,0:T(8,128)S(1)}, f32[32,8,128]{2,1,0:T(8,128)S(1)}) custom-call(f32[512,256]{1,0:T(8,128)S(1)} %get-tuple-element.36.refs_0_, f32[512,256]{1,0:T(8,128)S(1)} %get-tuple-element.38.refs_1_, f32[8,256]{1,0:T(8,128)S(1)} %get-tuple-element.37.refs_3_.refs_2_, ...), custom_call_target="tpu_custom_call" | custom-call | flops 603979776 | bytes 1048576 | tf_op jit(solution)/shard_map/backward/pallas_call | solution.py:67
  32.7 11.9 %all_to_all.10.refs_6_ = f32[32,8,128]{2,1,0:T(8,128)S(1)} all-to-all(f32[32,8,128]{2,1,0:T(8,128)S(1)} %get-tuple-element.50), channel_id=1, replica_groups=mesh['page'=8,'query'=2,'head'=2] {'page','query','head'}, dimensions={0} | all-to-all | bytes 262144 | tf_op jit(solution)/shard_map/all_to_all | solution.py:584
  44.6 1.3 %update_forward.1 = (f32[1040,128]{1,0:T(8,128)S(1)}, f32[136,128]{1,0:T(8,128)S(1)}, f32[136,128]{1,0:T(8,128)S(1)}, f32[136,128]{1,0:T(8,128)S(1)}, f32[136,12...) custom-call(f32[520,128]{1,0:T(8,128)S(1)} %get-tuple-element.32.refs_0_.refs_4_, ...), custom_call_target="tpu_custom_call" | custom-call | flops 402653184 | bytes 1048576 | tf_op jit(solution)/shard_map/update_forward/pallas_call | solution.py:67
  46.0 0.3 collective-permute-start.11
  46.3 1.4 %collective-permute-start.12 = (f32[136,128]{1,0:T(8,128)S(1)}, f32[136,128]{1,0:T(8,128)S(1)}, u32[]{:S(2)}, u32[]{:S(2)}) collective-permute-start(f32[136,128]{1,0:T(8,128)S(1)} %get-tuple-element.53), channel_id=1, source_target_pairs={{0,24},{4,28},{8,16},{12,20},{16,8},{20,12},{24,0},{28,4},{1,25},{... | collective-permute-start | bytes 208904 | tf_op jit(solution)/shard_map/ppermute | solution.py:39
  47.7 0.8 collective-permute-start.13
  48.4 2.2 %collective-permute-start.14 = (f32[136,128]{1,0:T(8,128)S(1)}, f32[136,128]{1,0:T(8,128)S(1)}, u32[]{:S(2)}, u32[]{:S(2)}) collective-permute-start(f32[136,128]{1,0:T(8,128)S(1)} %get-tuple-element.55), channel_id=1, source_target_pairs={{0,8},{4,12},{8,0},{12,4},{16,24},{20,28},{24,16},{28,20},{1,9},{5... | collective-permute-start | bytes 208904 | tf_op jit(solution)/shard_map/ppermute | solution.py:39
  50.7 2.5 %collective-permute-done.12.refs_3_ = f32[136,128]{1,0:T(8,128)S(1)} collective-permute-done((f32[136,128]{1,0:T(8,128)S(1)}, f32[136,128]{1,0:T(8,128)S(1)}, u32[]{:S(2)}, u32[]{:S(2)}) %collective-permute-start.12) | collective-permute-done | bytes 69664 | tf_op jit(solution)/shard_map/ppermute | solution.py:39
  53.2 2.0 %collective-permute-done.13.refs_4_ = f32[136,128]{1,0:T(8,128)S(1)} collective-permute-done((f32[136,128]{1,0:T(8,128)S(1)}, f32[136,128]{1,0:T(8,128)S(1)}, u32[]{:S(2)}, u32[]{:S(2)}) %collective-permute-start.13) | collective-permute-done | bytes 69664 | tf_op jit(solution)/shard_map/ppermute | solution.py:39
  55.2 0.1 merge.3.refs_5_
  55.3 1.7 %collective-permute-start.17 = (f32[136,128]{1,0:T(8,128)S(1)}, f32[136,128]{1,0:T(8,128)S(1)}, u32[]{:S(2)}, u32[]{:S(2)}) collective-permute-start(f32[136,128]{1,0:T(8,128)S(1)} %merge.3.refs_5_), channel_id=1, source_target_pairs={{0,24},{4,28},{8,16},{12,20},{16,8},{20,12},{24,0},{28,4},{1,25},{... | collective-permute-start | bytes 208904 | tf_op jit(solution)/shard_map/ppermute | solution.py:39
  57.0 2.8 %collective-permute-start.15 = (f32[136,128]{1,0:T(8,128)S(1)}, f32[136,128]{1,0:T(8,128)S(1)}, u32[]{:S(2)}, u32[]{:S(2)}) collective-permute-start(f32[136,128]{1,0:T(8,128)S(1)} %merge.3.refs_5_), channel_id=1, source_target_pairs={{0,8},{4,12},{8,0},{12,4},{16,24},{20,28},{24,16},{28,20},{1,9},{5... | collective-permute-start | bytes 208904 | tf_op jit(solution)/shard_map/ppermute | solution.py:39
  59.8 2.5 %collective-permute-done.17.refs_4_.refs_8_ = f32[136,128]{1,0:T(8,128)S(1)} collective-permute-done((f32[136,128]{1,0:T(8,128)S(1)}, f32[136,128]{1,0:T(8,128)S(1)}, u32[]{:S(2)}, u32[]{:S(2)}) %collective-permute-start.17) | collective-permute-done | bytes 69664 | tf_op jit(solution)/shard_map/ppermute | solution.py:39
  62.3 2.0 %collective-permute-done.16.refs_3_.refs_7_ = f32[136,128]{1,0:T(8,128)S(1)} collective-permute-done((f32[136,128]{1,0:T(8,128)S(1)}, f32[136,128]{1,0:T(8,128)S(1)}, u32[]{:S(2)}, u32[]{:S(2)}) %collective-permute-start.16) | collective-permute-done | bytes 69664 | tf_op jit(solution)/shard_map/ppermute | solution.py:39
  64.3 0.1 collective-permute-start.18
  64.4 2.1 %backward.3 = (f32[520,128]{1,0:T(8,128)S(1)}, f32[520,128]{1,0:T(8,128)S(1)}, f32[32,8,128]{2,1,0:T(8,128)S(1)}) custom-call(f32[512,512]{1,0:T(8,128)S(1)} %get-tuple-element.56.refs_0_, f32[8,512]{1,0:T(8,128)S(1)} %get-tuple-element.57.refs_1_, f32[1040,128]{1,0:T(8,128)S(1)} %get-tuple-element.51.refs_0_.refs_2_, ...), custom_call_target="tpu_custom_call" | custom-call | flops 603979776 | bytes 1048576 | tf_op jit(solution)/shard_map/backward/pallas_call | solution.py:67
  66.5 0.9 %collective-permute-start.20 = (f32[520,128]{1,0:T(8,128)S(1)}, f32[520,128]{1,0:T(8,128)S(1)}, u32[]{:S(2)}, u32[]{:S(2)}) collective-permute-start(f32[520,128]{1,0:T(8,128)S(1)} %get-tuple-element.58.refs_3_), channel_id=1, source_target_pairs={{0,2},{2,0},{4,6},{6,4},{8,10},{10,8},{12,14},{14,12},{16,18},{18,... | collective-permute-start | bytes 798728 | tf_op jit(solution)/shard_map/ppermute | solution.py:39
  67.5 1.0 %collective-permute-start.21 = (f32[520,128]{1,0:T(8,128)S(1)}, f32[520,128]{1,0:T(8,128)S(1)}, u32[]{:S(2)}, u32[]{:S(2)}) collective-permute-start(f32[520,128]{1,0:T(8,128)S(1)} %get-tuple-element.59), channel_id=1, source_target_pairs={{0,6},{2,4},{4,2},{6,0},{8,14},{10,12},{12,10},{14,8},{16,22},{18,... | collective-permute-start | bytes 798728 | tf_op jit(solution)/shard_map/ppermute | solution.py:39
  68.4 0.3 collective-permute-start.19
  68.7 13.7 %all_to_all.11.refs_7_ = f32[32,8,128]{2,1,0:T(8,128)S(1)} all-to-all(f32[32,8,128]{2,1,0:T(8,128)S(1)} %get-tuple-element.60), channel_id=1, replica_groups=mesh['page'=8,'query'=2,'head'=2] {'page','query','head'}, dimensions={0} | all-to-all | bytes 262144 | tf_op jit(solution)/shard_map/all_to_all | solution.py:584
  82.5 1.2 %last_update.1 = (f32[4,256,128]{2,1,0:T(8,128)}, f32[4,256,128]{2,1,0:T(8,128)}, f32[4,256]{1,0:T(4,128)}) custom-call(f32[1040,128]{1,0:T(8,128)S(1)} %get-tuple-element.51.refs_0_.refs_2_, f32[1040,128]{1,0:T(8,128)S(1)} %collective-permute-done.11.refs_1_, f32[1040,128]{1,0:T(8,128)S(1)} %collective-permute-done.18.refs_2_, ...), custom_call_target="tpu_custom_call" | custom-call | flops 1048576 | bytes 1048576 | tf_op jit(solution)/shard_map/last_update/pallas_call | solution.py:67
  (23 shorter events, 0.1 us)
Async XLA Ops:
  0.6 5.2 %copy-start.3 = (f32[4,256,128]{2,1,0:T(8,128)S(1)}, f32[4,256,128]{2,1,0:T(8,128)}, u32[]{:S(2)}) copy-start(f32[4,256,128]{2,1,0:T(8,128)} %refs_4_.3) | copy-start | bytes 1572868
  0.6 5.2 %copy-start.2 = (f32[4,256,128]{2,1,0:T(8,128)S(1)}, f32[4,256,128]{2,1,0:T(8,128)}, u32[]{:S(2)}) copy-start(f32[4,256,128]{2,1,0:T(8,128)} %refs_2_.3) | copy-start | bytes 1572868
  0.7 5.2 %copy-start.1 = (f32[4,256,128]{2,1,0:T(8,128)S(1)}, f32[4,256,128]{2,1,0:T(8,128)}, u32[]{:S(2)}) copy-start(f32[4,256,128]{2,1,0:T(8,128)} %refs_1_.3) | copy-start | bytes 1572868
  0.7 5.2 %copy-start = (f32[4,256,128]{2,1,0:T(8,128)S(1)}, f32[4,256,128]{2,1,0:T(8,128)}, u32[]{:S(2)}) copy-start(f32[4,256,128]{2,1,0:T(8,128)} %refs_0_.3) | copy-start | bytes 1572868
  0.7 5.2 %copy-start.4 = (f32[4,256]{1,0:T(4,128)S(1)}, f32[4,256]{1,0:T(4,128)}, u32[]{:S(2)}) copy-start(f32[4,256]{1,0:T(4,128)} %refs_3_.3) | copy-start | bytes 12292
  0.7 5.2 %copy-start.5 = (s32[4,256]{1,0:T(4,128)S(1)}, s32[4,256]{1,0:T(4,128)}, u32[]{:S(2)}) copy-start(s32[4,256]{1,0:T(4,128)} %refs_5_.3) | copy-start | bytes 12292
  2.7 3.2 %copy-start.6 = (s32[8]{0:T(128)S(1)}, s32[8]{0:T(128)}, u32[]{:S(2)}) copy-start(s32[8]{0:T(128)} %refs_6_.3) | copy-start | bytes 100
  2.7 3.8 %collective-permute-start = (f32[520,128]{1,0:T(8,128)}, f32[520,128]{1,0:T(8,128)S(1)}, u32[]{:S(2)}, u32[]{:S(2)}) collective-permute-start(f32[520,128]{1,0:T(8,128)} %get-tuple-element.33), channel_id=1, source_target_pairs={{0,4},{4,0},{8,12},{12,8},{16,20},{20,16},{24,28},{28,24},{1,5},{5... | collective-permute-start | bytes 798728 | tf_op jit(solution)/shard_map/ppermute | solution.py:39
  3.3 8.8 %collective-permute-start.1 = (f32[328,128]{1,0:T(8,128)}, f32[328,128]{1,0:T(8,128)S(1)}, u32[]{:S(2)}, u32[]{:S(2)}) collective-permute-start(f32[328,128]{1,0:T(8,128)} %get-tuple-element.35), channel_id=1, source_target_pairs={{0,2},{2,0},{1,3},{3,1},{4,6},{6,4},{5,7},{7,5},{8,10},{10,8},{9,1... | collective-permute-start | bytes 503816 | tf_op jit(solution)/shard_map/ppermute | solution.py:39
  7.6 9.7 %collective-permute-start.2 = (f32[72,128]{1,0:T(8,128)S(1)}, f32[72,128]{1,0:T(8,128)S(1)}, u32[]{:S(2)}, u32[]{:S(2)}) collective-permute-start(f32[72,128]{1,0:T(8,128)S(1)} %get-tuple-element.41), channel_id=1, source_target_pairs={{0,8},{4,12},{8,0},{12,4},{16,24},{20,28},{24,16},{28,20},{1,9},{5... | collective-permute-start | bytes 110600 | tf_op jit(solution)/shard_map/ppermute | solution.py:39
  9.2 8.3 %collective-permute-start.3 = (f32[72,128]{1,0:T(8,128)S(1)}, f32[72,128]{1,0:T(8,128)S(1)}, u32[]{:S(2)}, u32[]{:S(2)}) collective-permute-start(f32[72,128]{1,0:T(8,128)S(1)} %get-tuple-element.42), channel_id=1, source_target_pairs={{0,16},{4,20},{8,24},{12,28},{16,0},{20,4},{24,8},{28,12},{1,17},{... | collective-permute-start | bytes 110600 | tf_op jit(solution)/shard_map/ppermute | solution.py:39
  11.8 6.2 %collective-permute-start.4 = (f32[72,128]{1,0:T(8,128)S(1)}, f32[72,128]{1,0:T(8,128)S(1)}, u32[]{:S(2)}, u32[]{:S(2)}) collective-permute-start(f32[72,128]{1,0:T(8,128)S(1)} %get-tuple-element.43), channel_id=1, source_target_pairs={{0,24},{4,28},{8,16},{12,20},{16,8},{20,12},{24,0},{28,4},{1,25},{... | collective-permute-start | bytes 110600 | tf_op jit(solution)/shard_map/ppermute | solution.py:39
  13.1 5.0 %collective-permute-start.5 = (f32[72,128]{1,0:T(8,128)S(1)}, f32[72,128]{1,0:T(8,128)S(1)}, u32[]{:S(2)}, u32[]{:S(2)}) collective-permute-start(f32[72,128]{1,0:T(8,128)S(1)} %get-tuple-element.45), channel_id=1, source_target_pairs={{0,8},{4,12},{8,0},{12,4},{16,24},{20,28},{24,16},{28,20},{1,9},{5... | collective-permute-start | bytes 110600 | tf_op jit(solution)/shard_map/ppermute | solution.py:39
  13.8 5.8 %collective-permute-start.6 = (f32[72,128]{1,0:T(8,128)S(1)}, f32[72,128]{1,0:T(8,128)S(1)}, u32[]{:S(2)}, u32[]{:S(2)}) collective-permute-start(f32[72,128]{1,0:T(8,128)S(1)} %get-tuple-element.46), channel_id=1, source_target_pairs={{0,16},{4,20},{8,24},{12,28},{16,0},{20,4},{24,8},{28,12},{1,17},{... | collective-permute-start | bytes 110600 | tf_op jit(solution)/shard_map/ppermute | solution.py:39
  17.3 5.8 %collective-permute-start.7 = (f32[72,128]{1,0:T(8,128)S(1)}, f32[72,128]{1,0:T(8,128)S(1)}, u32[]{:S(2)}, u32[]{:S(2)}) collective-permute-start(f32[72,128]{1,0:T(8,128)S(1)} %get-tuple-element.47), channel_id=1, source_target_pairs={{0,24},{4,28},{8,16},{12,20},{16,8},{20,12},{24,0},{28,4},{1,25},{... | collective-permute-start | bytes 110600 | tf_op jit(solution)/shard_map/ppermute | solution.py:39
  23.3 6.3 %collective-permute-start.10 = (f32[136,128]{1,0:T(8,128)S(1)}, f32[136,128]{1,0:T(8,128)S(1)}, u32[]{:S(2)}, u32[]{:S(2)}) collective-permute-start(f32[136,128]{1,0:T(8,128)S(1)} %merge.2.refs_8_), channel_id=1, source_target_pairs={{0,24},{4,28},{8,16},{12,20},{16,8},{20,12},{24,0},{28,4},{1,25},{... | collective-permute-start | bytes 208904 | tf_op jit(solution)/shard_map/ppermute | solution.py:39
  23.8 6.7 %collective-permute-start.9 = (f32[136,128]{1,0:T(8,128)S(1)}, f32[136,128]{1,0:T(8,128)S(1)}, u32[]{:S(2)}, u32[]{:S(2)}) collective-permute-start(f32[136,128]{1,0:T(8,128)S(1)} %merge.2.refs_8_), channel_id=1, source_target_pairs={{0,16},{4,20},{8,24},{12,28},{16,0},{20,4},{24,8},{28,12},{1,17},{... | collective-permute-start | bytes 208904 | tf_op jit(solution)/shard_map/ppermute | solution.py:39
  23.8 6.7 %collective-permute-start.8 = (f32[136,128]{1,0:T(8,128)S(1)}, f32[136,128]{1,0:T(8,128)S(1)}, u32[]{:S(2)}, u32[]{:S(2)}) collective-permute-start(f32[136,128]{1,0:T(8,128)S(1)} %merge.2.refs_8_), channel_id=1, source_target_pairs={{0,8},{4,12},{8,0},{12,4},{16,24},{20,28},{24,16},{28,20},{1,9},{5... | collective-permute-start | bytes 208904 | tf_op jit(solution)/shard_map/ppermute | solution.py:39
  46.0 18.3 %collective-permute-start.11 = (f32[1040,128]{1,0:T(8,128)S(1)}, f32[1040,128]{1,0:T(8,128)S(1)}, u32[]{:S(2)}, u32[]{:S(2)}) collective-permute-start(f32[1040,128]{1,0:T(8,128)S(1)} %get-tuple-element.51.refs_0_.refs_2_), channel_id=1, source_target_pairs={{0,2},{2,0},{1,3},{3,1},{4,6},{6,4},{5,7},{7,5},{8,10},{10,8},{9,1... | collective-permute-start | bytes 1597448 | tf_op jit(solution)/shard_map/ppermute | solution.py:39
  46.3 6.9 %collective-permute-start.12 = (f32[136,128]{1,0:T(8,128)S(1)}, f32[136,128]{1,0:T(8,128)S(1)}, u32[]{:S(2)}, u32[]{:S(2)}) collective-permute-start(f32[136,128]{1,0:T(8,128)S(1)} %get-tuple-element.53), channel_id=1, source_target_pairs={{0,24},{4,28},{8,16},{12,20},{16,8},{20,12},{24,0},{28,4},{1,25},{... | collective-permute-start | bytes 208904 | tf_op jit(solution)/shard_map/ppermute | solution.py:39
  47.7 7.5 %collective-permute-start.13 = (f32[136,128]{1,0:T(8,128)S(1)}, f32[136,128]{1,0:T(8,128)S(1)}, u32[]{:S(2)}, u32[]{:S(2)}) collective-permute-start(f32[136,128]{1,0:T(8,128)S(1)} %get-tuple-element.54), channel_id=1, source_target_pairs={{0,16},{4,20},{8,24},{12,28},{16,0},{20,4},{24,8},{28,12},{1,17},{... | collective-permute-start | bytes 208904 | tf_op jit(solution)/shard_map/ppermute | solution.py:39
  48.4 6.8 %collective-permute-start.14 = (f32[136,128]{1,0:T(8,128)S(1)}, f32[136,128]{1,0:T(8,128)S(1)}, u32[]{:S(2)}, u32[]{:S(2)}) collective-permute-start(f32[136,128]{1,0:T(8,128)S(1)} %get-tuple-element.55), channel_id=1, source_target_pairs={{0,8},{4,12},{8,0},{12,4},{16,24},{20,28},{24,16},{28,20},{1,9},{5... | collective-permute-start | bytes 208904 | tf_op jit(solution)/shard_map/ppermute | solution.py:39
  55.3 7.0 %collective-permute-start.17 = (f32[136,128]{1,0:T(8,128)S(1)}, f32[136,128]{1,0:T(8,128)S(1)}, u32[]{:S(2)}, u32[]{:S(2)}) collective-permute-start(f32[136,128]{1,0:T(8,128)S(1)} %merge.3.refs_5_), channel_id=1, source_target_pairs={{0,24},{4,28},{8,16},{12,20},{16,8},{20,12},{24,0},{28,4},{1,25},{... | collective-permute-start | bytes 208904 | tf_op jit(solution)/shard_map/ppermute | solution.py:39
  57.0 7.3 %collective-permute-start.16 = (f32[136,128]{1,0:T(8,128)S(1)}, f32[136,128]{1,0:T(8,128)S(1)}, u32[]{:S(2)}, u32[]{:S(2)}) collective-permute-start(f32[136,128]{1,0:T(8,128)S(1)} %merge.3.refs_5_), channel_id=1, source_target_pairs={{0,16},{4,20},{8,24},{12,28},{16,0},{20,4},{24,8},{28,12},{1,17},{... | collective-permute-start | bytes 208904 | tf_op jit(solution)/shard_map/ppermute | solution.py:39
  57.0 7.3 %collective-permute-start.15 = (f32[136,128]{1,0:T(8,128)S(1)}, f32[136,128]{1,0:T(8,128)S(1)}, u32[]{:S(2)}, u32[]{:S(2)}) collective-permute-start(f32[136,128]{1,0:T(8,128)S(1)} %merge.3.refs_5_), channel_id=1, source_target_pairs={{0,8},{4,12},{8,0},{12,4},{16,24},{20,28},{24,16},{28,20},{1,9},{5... | collective-permute-start | bytes 208904 | tf_op jit(solution)/shard_map/ppermute | solution.py:39
  64.3 18.2 %collective-permute-start.18 = (f32[1040,128]{1,0:T(8,128)S(1)}, f32[1040,128]{1,0:T(8,128)S(1)}, u32[]{:S(2)}, u32[]{:S(2)}) collective-permute-start(f32[1040,128]{1,0:T(8,128)S(1)} %mate_parts.1), channel_id=1, source_target_pairs={{0,4},{4,0},{8,12},{12,8},{16,20},{20,16},{24,28},{28,24},{1,5},{5... | collective-permute-start | bytes 1597448 | tf_op jit(solution)/shard_map/ppermute | solution.py:39
  66.5 15.9 %collective-permute-start.20 = (f32[520,128]{1,0:T(8,128)S(1)}, f32[520,128]{1,0:T(8,128)S(1)}, u32[]{:S(2)}, u32[]{:S(2)}) collective-permute-start(f32[520,128]{1,0:T(8,128)S(1)} %get-tuple-element.58.refs_3_), channel_id=1, source_target_pairs={{0,2},{2,0},{4,6},{6,4},{8,10},{10,8},{12,14},{14,12},{16,18},{18,... | collective-permute-start | bytes 798728 | tf_op jit(solution)/shard_map/ppermute | solution.py:39
  67.5 15.0 %collective-permute-start.21 = (f32[520,128]{1,0:T(8,128)S(1)}, f32[520,128]{1,0:T(8,128)S(1)}, u32[]{:S(2)}, u32[]{:S(2)}) collective-permute-start(f32[520,128]{1,0:T(8,128)S(1)} %get-tuple-element.59), channel_id=1, source_target_pairs={{0,6},{2,4},{4,2},{6,0},{8,14},{10,12},{12,10},{14,8},{16,22},{18,... | collective-permute-start | bytes 798728 | tf_op jit(solution)/shard_map/ppermute | solution.py:39
  68.4 14.0 %collective-permute-start.19 = (f32[520,128]{1,0:T(8,128)S(1)}, f32[520,128]{1,0:T(8,128)S(1)}, u32[]{:S(2)}, u32[]{:S(2)}) collective-permute-start(f32[520,128]{1,0:T(8,128)S(1)} %get-tuple-element.59), channel_id=1, source_target_pairs={{0,4},{2,6},{4,0},{6,2},{8,12},{10,14},{12,8},{14,10},{16,20},{18,... | collective-permute-start | bytes 798728 | tf_op jit(solution)/shard_map/ppermute | solution.py:39

commit v15 on v14

--- a/solution.py
+++ b/solution.py
@@ -483,7 +483,7 @@
         ones = jnp.ones((TAIL, query_rows), jnp.bfloat16)
         ones = (ones, jnp.zeros_like(ones))
         squares = [jnp.zeros((1, width), jnp.float32)] * 3
-        for at, ref in enumerate(state_refs):
+        for at, (ref, out) in enumerate(zip(state_refs, grad_outs)):
             rows = slice(at * slot_rows, (at + 1) * slot_rows)
             attention = jnp.concatenate([part[rows, :] for part in weights_refs], axis=1) * factor
             grad_values = dot(halves(attention), residual, 1, 1)
@@ -491,9 +491,9 @@
             grad_scores = halves(attention * (grad_probs - row_delta))
             grad_keys = dot(grad_scores, all_queries, 1, 0) * score_scale
             grad_bias = row_as_tail(dot(ones, grad_scores, 1, 1)[0:1, :], width)
-            grad_outs[at][:slot_rows, :] = grad_keys
-            grad_outs[at][slot_rows : 2 * slot_rows, :] = grad_values
-            grad_outs[at][2 * slot_rows :, :] = grad_bias
+            out[:slot_rows, :] = grad_keys
+            out[slot_rows : 2 * slot_rows, :] = grad_values
+            out[2 * slot_rows :, :] = grad_bias
             for which, grad in enumerate((grad_keys, grad_values, grad_bias)):
                 squares[which] = squares[which] + jnp.sum(grad * grad, axis=0, keepdims=True)
         tile = jnp.concatenate(squares + [jnp.zeros((TAIL - 3, width), jnp.float32)], axis=0)
@@ -526,9 +526,11 @@
                     piece_scratch,
                     after=maxima[-1:],
                 )
-                sums += pieces[:1] + [
-                    exchange(pieces[turn], page=CORES * turn) for turn in range(1, ranks)
-                ]
+                arrived = {
+                    turn: exchange(pieces[turn], page=CORES * turn)
+                    for turn in reversed(range(1, ranks))
+                }
+                sums += list(arrived.values()) + pieces[:1]
                 weights.append(part_weights)
                 maxima.append(part_max)
         else:

time: 83.8 us -> 83.2 us (level)
  waiting for transfers between devices: 17.3 us -> 16.3 us
    ppermute x22, waiting for transfers between devices: 17.3 us -> 16.3 us  [exchange(): return lax.ppermute(value, axes, pairs)]
  transfers between devices with their start and end apart: 22 -> 22, of which waited for: 9 -> 8; matrix products, arithmetic and copies ran while one was open for 0% -> 0% of each run, Pallas kernels for 6% -> 6%
where the time goes in v15:
time: 83.2 us; the launch traced here: 83 us
  starting transfers between devices  27.9 us (34%)
  blocking collectives  26 us (31%)
  waiting for transfers between devices  16.3 us (20%)
  Pallas kernels  11.9 us (14%)
    ppermute x22, starting transfers between devices, exchange(): return lax.ppermute(value, axes, pairs)  27.9 us
    all_to_all x2, blocking collectives, direct_per_device(): lax.all_to_all(squares, ('page', 'query', 'head'), split_axis=0, concat_a...  26 us
    ppermute x22, waiting for transfers between devices, exchange(): return lax.ppermute(value, axes, pairs)  16.3 us
    pallas_call x11, Pallas kernels, call(): pl.pallas_call(without_after, out_shape=[jax.ShapeDtypeStruct(shape, jnp....  11.9 us
  transfers between devices with their start and end apart: 22, of which 8 were waited for; matrix products, arithmetic and copies ran while one was open for 0% of the time, Pallas kernels for 6%

profile of v15, /device:TPU:0, one launch (start us, length us, event | category | flops | bytes accessed | tf_op | source)
XLA Modules:
  0.0 83.0 jit_solution(1226500737021934650)
XLA Ops:
  0.7 2.0 %pack.1 = (f32[520,128]{1,0:T(8,128)}, f32[328,128]{1,0:T(8,128)}) custom-call(f32[4,256,128]{2,1,0:T(8,128)} %refs_0_.3, f32[4,256,128]{2,1,0:T(8,128)} %refs_1_.3, f32[4,256,128]{2,1,0:T(8,128)} %refs_2_.3, f32[4,256]{1,0:T(4,128)} %refs_3_.3, f32[4,256,128]{2,1,0:T(8,128)} %refs_4_.3, s32[4,256]{1,0:T(4,128)} %refs_5_.3, s32[8]{0:T(128)} %refs_6_.3), custom_call_target="tpu_custom_call" | custom-call | flops 1048576 | bytes 1048576 | tf_op jit(solution)/shard_map/pack/pallas_call | solution.py:67
  2.7 0.0 copy-start.6
  2.7 0.5 collective-permute-start
  3.3 2.6 %collective-permute-start.1 = (f32[328,128]{1,0:T(8,128)}, f32[328,128]{1,0:T(8,128)S(1)}, u32[]{:S(2)}, u32[]{:S(2)}) collective-permute-start(f32[328,128]{1,0:T(8,128)} %get-tuple-element.35), channel_id=1, source_target_pairs={{0,2},{2,0},{1,3},{3,1},{4,6},{6,4},{5,7},{7,5},{8,10},{10,8},{9,1... | collective-permute-start | bytes 503816 | tf_op jit(solution)/shard_map/ppermute | solution.py:39
  5.9 0.7 own.1
  6.6 0.0 collective-permute-done.refs_1_.refs_5_
  6.6 1.0 %forward.2 = (f32[72,128]{1,0:T(8,128)S(1)}, f32[72,128]{1,0:T(8,128)S(1)}, f32[72,128]{1,0:T(8,128)S(1)}, f32[72,128]{1,0:T(8,128)S(1)}, f32[512,256]{1,0:T(8,128)S(1)}, /*index=5*/f32[8,256]{1,0:T(8,128)S(1)}) custom-call(f32[520,128]{1,0:T(8,128)S(1)} %get-tuple-element.32.refs_0_.refs_4_, f32[520,128]{1,0:T(8,128)S(1)} %collective-permute-done.refs_1_.refs_5_, ...), custom_call_target="tpu_custom_call" | custom-call | flops 201326592 | bytes 1048576 | tf_op jit(solution)/shard_map/forward/pallas_call | solution.py:67
  7.6 3.7 %collective-permute-start.2 = (f32[72,128]{1,0:T(8,128)S(1)}, f32[72,128]{1,0:T(8,128)S(1)}, u32[]{:S(2)}, u32[]{:S(2)}) collective-permute-start(f32[72,128]{1,0:T(8,128)S(1)} %get-tuple-element.40), channel_id=1, source_target_pairs={{0,24},{4,28},{8,16},{12,20},{16,8},{20,12},{24,0},{28,4},{1,25},{... | collective-permute-start | bytes 110600 | tf_op jit(solution)/shard_map/ppermute | solution.py:39
  11.3 0.8 collective-permute-start.4
  12.0 1.0 %forward.3 = (f32[72,128]{1,0:T(8,128)S(1)}, f32[72,128]{1,0:T(8,128)S(1)}, f32[72,128]{1,0:T(8,128)S(1)}, f32[72,128]{1,0:T(8,128)S(1)}, f32[512,256]{1,0:T(8,128)S(1)}, /*index=5*/f32[8,256]{1,0:T(8,128)S(1)}) custom-call(f32[520,128]{1,0:T(8,128)S(1)} %get-tuple-element.32.refs_0_.refs_4_, f32[520,128]{1,0:T(8,128)S(1)} %collective-permute-done.refs_1_.refs_5_, ...), custom_call_target="tpu_custom_call" | custom-call | flops 201326592 | bytes 1048576 | tf_op jit(solution)/shard_map/forward/pallas_call | solution.py:67
  13.1 3.7 %collective-permute-start.5 = (f32[72,128]{1,0:T(8,128)S(1)}, f32[72,128]{1,0:T(8,128)S(1)}, u32[]{:S(2)}, u32[]{:S(2)}) collective-permute-start(f32[72,128]{1,0:T(8,128)S(1)} %get-tuple-element.44), channel_id=1, source_target_pairs={{0,24},{4,28},{8,16},{12,20},{16,8},{20,12},{24,0},{28,4},{1,25},{... | collective-permute-start | bytes 110600 | tf_op jit(solution)/shard_map/ppermute | solution.py:39
  16.7 0.0 collective-permute-start.6
  16.7 0.8 collective-permute-start.7
  17.5 0.0 collective-permute-done.4.refs_4_
  17.5 1.5 %collective-permute-done.5.refs_6_ = f32[72,128]{1,0:T(8,128)S(1)} collective-permute-done((f32[72,128]{1,0:T(8,128)S(1)}, f32[72,128]{1,0:T(8,128)S(1)}, u32[]{:S(2)}, u32[]{:S(2)}) %collective-permute-start.5) | collective-permute-done | bytes 36896 | tf_op jit(solution)/shard_map/ppermute | solution.py:39
  19.0 2.6 %collective-permute-done.6.refs_7_ = f32[72,128]{1,0:T(8,128)S(1)} collective-permute-done((f32[72,128]{1,0:T(8,128)S(1)}, f32[72,128]{1,0:T(8,128)S(1)}, u32[]{:S(2)}, u32[]{:S(2)}) %collective-permute-start.6) | collective-permute-done | bytes 36896 | tf_op jit(solution)/shard_map/ppermute | solution.py:39
  21.6 0.3 merge.2.refs_8_
  21.9 1.5 %collective-permute-start.10 = (f32[136,128]{1,0:T(8,128)S(1)}, f32[136,128]{1,0:T(8,128)S(1)}, u32[]{:S(2)}, u32[]{:S(2)}) collective-permute-start(f32[136,128]{1,0:T(8,128)S(1)} %merge.2.refs_8_), channel_id=1, source_target_pairs={{0,24},{4,28},{8,16},{12,20},{16,8},{20,12},{24,0},{28,4},{1,25},{... | collective-permute-start | bytes 208904 | tf_op jit(solution)/shard_map/ppermute | solution.py:39
  23.4 0.6 collective-permute-start.9
  24.0 2.3 %collective-permute-start.8 = (f32[136,128]{1,0:T(8,128)S(1)}, f32[136,128]{1,0:T(8,128)S(1)}, u32[]{:S(2)}, u32[]{:S(2)}) collective-permute-start(f32[136,128]{1,0:T(8,128)S(1)} %merge.2.refs_8_), channel_id=1, source_target_pairs={{0,8},{4,12},{8,0},{12,4},{16,24},{20,28},{24,16},{28,20},{1,9},{5... | collective-permute-start | bytes 208904 | tf_op jit(solution)/shard_map/ppermute | solution.py:39
  26.3 1.8 %collective-permute-done.10.refs_11_ = f32[136,128]{1,0:T(8,128)S(1)} collective-permute-done((f32[136,128]{1,0:T(8,128)S(1)}, f32[136,128]{1,0:T(8,128)S(1)}, u32[]{:S(2)}, u32[]{:S(2)}) %collective-permute-start.10) | collective-permute-done | bytes 69664 | tf_op jit(solution)/shard_map/ppermute | solution.py:39
  28.1 1.5 %collective-permute-done.9.refs_10_ = f32[136,128]{1,0:T(8,128)S(1)} collective-permute-done((f32[136,128]{1,0:T(8,128)S(1)}, f32[136,128]{1,0:T(8,128)S(1)}, u32[]{:S(2)}, u32[]{:S(2)}) %collective-permute-start.9) | collective-permute-done | bytes 69664 | tf_op jit(solution)/shard_map/ppermute | solution.py:39
  29.5 0.0 collective-permute-done.8.refs_9_
  29.5 2.2 %backward.2 = (f32[520,128]{1,0:T(8,128)S(1)}, f32[520,128]{1,0:T(8,128)S(1)}, f32[32,8,128]{2,1,0:T(8,128)S(1)}) custom-call(f32[512,256]{1,0:T(8,128)S(1)} %get-tuple-element.36.refs_0_, f32[512,256]{1,0:T(8,128)S(1)} %get-tuple-element.38.refs_1_, f32[8,256]{1,0:T(8,128)S(1)} %get-tuple-element.37.refs_3_.refs_2_, ...), custom_call_target="tpu_custom_call" | custom-call | flops 603979776 | bytes 1048576 | tf_op jit(solution)/shard_map/backward/pallas_call | solution.py:67
  31.8 12.3 %all_to_all.10.refs_6_ = f32[32,8,128]{2,1,0:T(8,128)S(1)} all-to-all(f32[32,8,128]{2,1,0:T(8,128)S(1)} %get-tuple-element.50), channel_id=1, replica_groups=mesh['page'=8,'query'=2,'head'=2] {'page','query','head'}, dimensions={0} | all-to-all | bytes 262144 | tf_op jit(solution)/shard_map/all_to_all | solution.py:586
  44.0 1.3 %update_forward.1 = (f32[1040,128]{1,0:T(8,128)S(1)}, f32[136,128]{1,0:T(8,128)S(1)}, f32[136,128]{1,0:T(8,128)S(1)}, f32[136,128]{1,0:T(8,128)S(1)}, f32[136,12...) custom-call(f32[520,128]{1,0:T(8,128)S(1)} %get-tuple-element.32.refs_0_.refs_4_, ...), custom_call_target="tpu_custom_call" | custom-call | flops 402653184 | bytes 1048576 | tf_op jit(solution)/shard_map/update_forward/pallas_call | solution.py:67
  45.4 0.3 collective-permute-start.11
  45.7 1.4 %collective-permute-start.12 = (f32[136,128]{1,0:T(8,128)S(1)}, f32[136,128]{1,0:T(8,128)S(1)}, u32[]{:S(2)}, u32[]{:S(2)}) collective-permute-start(f32[136,128]{1,0:T(8,128)S(1)} %get-tuple-element.53), channel_id=1, source_target_pairs={{0,24},{4,28},{8,16},{12,20},{16,8},{20,12},{24,0},{28,4},{1,25},{... | collective-permute-start | bytes 208904 | tf_op jit(solution)/shard_map/ppermute | solution.py:39
  47.1 0.8 collective-permute-start.13
  47.8 2.2 %collective-permute-start.14 = (f32[136,128]{1,0:T(8,128)S(1)}, f32[136,128]{1,0:T(8,128)S(1)}, u32[]{:S(2)}, u32[]{:S(2)}) collective-permute-start(f32[136,128]{1,0:T(8,128)S(1)} %get-tuple-element.55), channel_id=1, source_target_pairs={{0,8},{4,12},{8,0},{12,4},{16,24},{20,28},{24,16},{28,20},{1,9},{5... | collective-permute-start | bytes 208904 | tf_op jit(solution)/shard_map/ppermute | solution.py:39
  50.1 2.5 %collective-permute-done.12.refs_3_ = f32[136,128]{1,0:T(8,128)S(1)} collective-permute-done((f32[136,128]{1,0:T(8,128)S(1)}, f32[136,128]{1,0:T(8,128)S(1)}, u32[]{:S(2)}, u32[]{:S(2)}) %collective-permute-start.12) | collective-permute-done | bytes 69664 | tf_op jit(solution)/shard_map/ppermute | solution.py:39
  52.6 2.0 %collective-permute-done.13.refs_4_ = f32[136,128]{1,0:T(8,128)S(1)} collective-permute-done((f32[136,128]{1,0:T(8,128)S(1)}, f32[136,128]{1,0:T(8,128)S(1)}, u32[]{:S(2)}, u32[]{:S(2)}) %collective-permute-start.13) | collective-permute-done | bytes 69664 | tf_op jit(solution)/shard_map/ppermute | solution.py:39
  54.6 0.0 collective-permute-done.14.refs_5_
  54.6 0.1 merge.3.refs_5_
  54.7 1.7 %collective-permute-start.17 = (f32[136,128]{1,0:T(8,128)S(1)}, f32[136,128]{1,0:T(8,128)S(1)}, u32[]{:S(2)}, u32[]{:S(2)}) collective-permute-start(f32[136,128]{1,0:T(8,128)S(1)} %merge.3.refs_5_), channel_id=1, source_target_pairs={{0,24},{4,28},{8,16},{12,20},{16,8},{20,12},{24,0},{28,4},{1,25},{... | collective-permute-start | bytes 208904 | tf_op jit(solution)/shard_map/ppermute | solution.py:39
  56.4 0.0 collective-permute-start.16
  56.4 2.8 %collective-permute-start.15 = (f32[136,128]{1,0:T(8,128)S(1)}, f32[136,128]{1,0:T(8,128)S(1)}, u32[]{:S(2)}, u32[]{:S(2)}) collective-permute-start(f32[136,128]{1,0:T(8,128)S(1)} %merge.3.refs_5_), channel_id=1, source_target_pairs={{0,8},{4,12},{8,0},{12,4},{16,24},{20,28},{24,16},{28,20},{1,9},{5... | collective-permute-start | bytes 208904 | tf_op jit(solution)/shard_map/ppermute | solution.py:39
  59.2 2.5 %collective-permute-done.17.refs_4_.refs_8_ = f32[136,128]{1,0:T(8,128)S(1)} collective-permute-done((f32[136,128]{1,0:T(8,128)S(1)}, f32[136,128]{1,0:T(8,128)S(1)}, u32[]{:S(2)}, u32[]{:S(2)}) %collective-permute-start.17) | collective-permute-done | bytes 69664 | tf_op jit(solution)/shard_map/ppermute | solution.py:39
  61.7 2.0 %collective-permute-done.16.refs_3_.refs_7_ = f32[136,128]{1,0:T(8,128)S(1)} collective-permute-done((f32[136,128]{1,0:T(8,128)S(1)}, f32[136,128]{1,0:T(8,128)S(1)}, u32[]{:S(2)}, u32[]{:S(2)}) %collective-permute-start.16) | collective-permute-done | bytes 69664 | tf_op jit(solution)/shard_map/ppermute | solution.py:39
  63.7 0.0 collective-permute-done.15.refs_2_.refs_6_
  63.7 0.0 collective-permute-done.11.refs_1_
  63.7 0.1 collective-permute-start.18
  63.8 2.1 %backward.3 = (f32[520,128]{1,0:T(8,128)S(1)}, f32[520,128]{1,0:T(8,128)S(1)}, f32[32,8,128]{2,1,0:T(8,128)S(1)}) custom-call(f32[512,512]{1,0:T(8,128)S(1)} %get-tuple-element.56.refs_0_, f32[8,512]{1,0:T(8,128)S(1)} %get-tuple-element.57.refs_1_, f32[1040,128]{1,0:T(8,128)S(1)} %get-tuple-element.51.refs_0_.refs_2_, ...), custom_call_target="tpu_custom_call" | custom-call | flops 603979776 | bytes 1048576 | tf_op jit(solution)/shard_map/backward/pallas_call | solution.py:67
  66.0 0.9 %collective-permute-start.20 = (f32[520,128]{1,0:T(8,128)S(1)}, f32[520,128]{1,0:T(8,128)S(1)}, u32[]{:S(2)}, u32[]{:S(2)}) collective-permute-start(f32[520,128]{1,0:T(8,128)S(1)} %get-tuple-element.58.refs_3_), channel_id=1, source_target_pairs={{0,2},{2,0},{4,6},{6,4},{8,10},{10,8},{12,14},{14,12},{16,18},{18,... | collective-permute-start | bytes 798728 | tf_op jit(solution)/shard_map/ppermute | solution.py:39
  66.9 1.0 %collective-permute-start.21 = (f32[520,128]{1,0:T(8,128)S(1)}, f32[520,128]{1,0:T(8,128)S(1)}, u32[]{:S(2)}, u32[]{:S(2)}) collective-permute-start(f32[520,128]{1,0:T(8,128)S(1)} %get-tuple-element.59), channel_id=1, source_target_pairs={{0,6},{2,4},{4,2},{6,0},{8,14},{10,12},{12,10},{14,8},{16,22},{18,... | collective-permute-start | bytes 798728 | tf_op jit(solution)/shard_map/ppermute | solution.py:39
  67.8 0.3 collective-permute-start.19
  68.2 13.7 %all_to_all.11.refs_7_ = f32[32,8,128]{2,1,0:T(8,128)S(1)} all-to-all(f32[32,8,128]{2,1,0:T(8,128)S(1)} %get-tuple-element.60), channel_id=1, replica_groups=mesh['page'=8,'query'=2,'head'=2] {'page','query','head'}, dimensions={0} | all-to-all | bytes 262144 | tf_op jit(solution)/shard_map/all_to_all | solution.py:586
  81.9 1.2 %last_update.1 = (f32[4,256,128]{2,1,0:T(8,128)}, f32[4,256,128]{2,1,0:T(8,128)}, f32[4,256]{1,0:T(4,128)}) custom-call(f32[1040,128]{1,0:T(8,128)S(1)} %get-tuple-element.51.refs_0_.refs_2_, f32[1040,128]{1,0:T(8,128)S(1)} %collective-permute-done.11.refs_1_, f32[1040,128]{1,0:T(8,128)S(1)} %collective-permute-done.18.refs_2_, ...), custom_call_target="tpu_custom_call" | custom-call | flops 1048576 | bytes 1048576 | tf_op jit(solution)/shard_map/last_update/pallas_call | solution.py:67
  (23 shorter events, 0.1 us)
Async XLA Ops:
  0.6 5.2 %copy-start.3 = (f32[4,256,128]{2,1,0:T(8,128)S(1)}, f32[4,256,128]{2,1,0:T(8,128)}, u32[]{:S(2)}) copy-start(f32[4,256,128]{2,1,0:T(8,128)} %refs_4_.3) | copy-start | bytes 1572868
  0.6 5.2 %copy-start.2 = (f32[4,256,128]{2,1,0:T(8,128)S(1)}, f32[4,256,128]{2,1,0:T(8,128)}, u32[]{:S(2)}) copy-start(f32[4,256,128]{2,1,0:T(8,128)} %refs_2_.3) | copy-start | bytes 1572868
  0.7 5.2 %copy-start.1 = (f32[4,256,128]{2,1,0:T(8,128)S(1)}, f32[4,256,128]{2,1,0:T(8,128)}, u32[]{:S(2)}) copy-start(f32[4,256,128]{2,1,0:T(8,128)} %refs_1_.3) | copy-start | bytes 1572868
  0.7 5.2 %copy-start = (f32[4,256,128]{2,1,0:T(8,128)S(1)}, f32[4,256,128]{2,1,0:T(8,128)}, u32[]{:S(2)}) copy-start(f32[4,256,128]{2,1,0:T(8,128)} %refs_0_.3) | copy-start | bytes 1572868
  0.7 5.2 %copy-start.4 = (f32[4,256]{1,0:T(4,128)S(1)}, f32[4,256]{1,0:T(4,128)}, u32[]{:S(2)}) copy-start(f32[4,256]{1,0:T(4,128)} %refs_3_.3) | copy-start | bytes 12292
  0.7 5.2 %copy-start.5 = (s32[4,256]{1,0:T(4,128)S(1)}, s32[4,256]{1,0:T(4,128)}, u32[]{:S(2)}) copy-start(s32[4,256]{1,0:T(4,128)} %refs_5_.3) | copy-start | bytes 12292
  2.7 3.2 %copy-start.6 = (s32[8]{0:T(128)S(1)}, s32[8]{0:T(128)}, u32[]{:S(2)}) copy-start(s32[8]{0:T(128)} %refs_6_.3) | copy-start | bytes 100
  2.7 3.8 %collective-permute-start = (f32[520,128]{1,0:T(8,128)}, f32[520,128]{1,0:T(8,128)S(1)}, u32[]{:S(2)}, u32[]{:S(2)}) collective-permute-start(f32[520,128]{1,0:T(8,128)} %get-tuple-element.33), channel_id=1, source_target_pairs={{0,4},{4,0},{8,12},{12,8},{16,20},{20,16},{24,28},{28,24},{1,5},{5... | collective-permute-start | bytes 798728 | tf_op jit(solution)/shard_map/ppermute | solution.py:39
  3.3 8.8 %collective-permute-start.1 = (f32[328,128]{1,0:T(8,128)}, f32[328,128]{1,0:T(8,128)S(1)}, u32[]{:S(2)}, u32[]{:S(2)}) collective-permute-start(f32[328,128]{1,0:T(8,128)} %get-tuple-element.35), channel_id=1, source_target_pairs={{0,2},{2,0},{1,3},{3,1},{4,6},{6,4},{5,7},{7,5},{8,10},{10,8},{9,1... | collective-permute-start | bytes 503816 | tf_op jit(solution)/shard_map/ppermute | solution.py:39
  7.6 9.2 %collective-permute-start.2 = (f32[72,128]{1,0:T(8,128)S(1)}, f32[72,128]{1,0:T(8,128)S(1)}, u32[]{:S(2)}, u32[]{:S(2)}) collective-permute-start(f32[72,128]{1,0:T(8,128)S(1)} %get-tuple-element.40), channel_id=1, source_target_pairs={{0,24},{4,28},{8,16},{12,20},{16,8},{20,12},{24,0},{28,4},{1,25},{... | collective-permute-start | bytes 110600 | tf_op jit(solution)/shard_map/ppermute | solution.py:39
  11.3 6.3 %collective-permute-start.3 = (f32[72,128]{1,0:T(8,128)S(1)}, f32[72,128]{1,0:T(8,128)S(1)}, u32[]{:S(2)}, u32[]{:S(2)}) collective-permute-start(f32[72,128]{1,0:T(8,128)S(1)} %get-tuple-element.41), channel_id=1, source_target_pairs={{0,16},{4,20},{8,24},{12,28},{16,0},{20,4},{24,8},{28,12},{1,17},{... | collective-permute-start | bytes 110600 | tf_op jit(solution)/shard_map/ppermute | solution.py:39
  11.3 6.3 %collective-permute-start.4 = (f32[72,128]{1,0:T(8,128)S(1)}, f32[72,128]{1,0:T(8,128)S(1)}, u32[]{:S(2)}, u32[]{:S(2)}) collective-permute-start(f32[72,128]{1,0:T(8,128)S(1)} %get-tuple-element.42), channel_id=1, source_target_pairs={{0,8},{4,12},{8,0},{12,4},{16,24},{20,28},{24,16},{28,20},{1,9},{5... | collective-permute-start | bytes 110600 | tf_op jit(solution)/shard_map/ppermute | solution.py:39
  13.1 5.9 %collective-permute-start.5 = (f32[72,128]{1,0:T(8,128)S(1)}, f32[72,128]{1,0:T(8,128)S(1)}, u32[]{:S(2)}, u32[]{:S(2)}) collective-permute-start(f32[72,128]{1,0:T(8,128)S(1)} %get-tuple-element.44), channel_id=1, source_target_pairs={{0,24},{4,28},{8,16},{12,20},{16,8},{20,12},{24,0},{28,4},{1,25},{... | collective-permute-start | bytes 110600 | tf_op jit(solution)/shard_map/ppermute | solution.py:39
  16.7 4.9 %collective-permute-start.6 = (f32[72,128]{1,0:T(8,128)S(1)}, f32[72,128]{1,0:T(8,128)S(1)}, u32[]{:S(2)}, u32[]{:S(2)}) collective-permute-start(f32[72,128]{1,0:T(8,128)S(1)} %get-tuple-element.45), channel_id=1, source_target_pairs={{0,16},{4,20},{8,24},{12,28},{16,0},{20,4},{24,8},{28,12},{1,17},{... | collective-permute-start | bytes 110600 | tf_op jit(solution)/shard_map/ppermute | solution.py:39
  16.7 4.9 %collective-permute-start.7 = (f32[72,128]{1,0:T(8,128)S(1)}, f32[72,128]{1,0:T(8,128)S(1)}, u32[]{:S(2)}, u32[]{:S(2)}) collective-permute-start(f32[72,128]{1,0:T(8,128)S(1)} %get-tuple-element.46), channel_id=1, source_target_pairs={{0,8},{4,12},{8,0},{12,4},{16,24},{20,28},{24,16},{28,20},{1,9},{5... | collective-permute-start | bytes 110600 | tf_op jit(solution)/shard_map/ppermute | solution.py:39
  21.9 6.2 %collective-permute-start.10 = (f32[136,128]{1,0:T(8,128)S(1)}, f32[136,128]{1,0:T(8,128)S(1)}, u32[]{:S(2)}, u32[]{:S(2)}) collective-permute-start(f32[136,128]{1,0:T(8,128)S(1)} %merge.2.refs_8_), channel_id=1, source_target_pairs={{0,24},{4,28},{8,16},{12,20},{16,8},{20,12},{24,0},{28,4},{1,25},{... | collective-permute-start | bytes 208904 | tf_op jit(solution)/shard_map/ppermute | solution.py:39
  23.4 6.1 %collective-permute-start.9 = (f32[136,128]{1,0:T(8,128)S(1)}, f32[136,128]{1,0:T(8,128)S(1)}, u32[]{:S(2)}, u32[]{:S(2)}) collective-permute-start(f32[136,128]{1,0:T(8,128)S(1)} %merge.2.refs_8_), channel_id=1, source_target_pairs={{0,16},{4,20},{8,24},{12,28},{16,0},{20,4},{24,8},{28,12},{1,17},{... | collective-permute-start | bytes 208904 | tf_op jit(solution)/shard_map/ppermute | solution.py:39
  24.0 5.5 %collective-permute-start.8 = (f32[136,128]{1,0:T(8,128)S(1)}, f32[136,128]{1,0:T(8,128)S(1)}, u32[]{:S(2)}, u32[]{:S(2)}) collective-permute-start(f32[136,128]{1,0:T(8,128)S(1)} %merge.2.refs_8_), channel_id=1, source_target_pairs={{0,8},{4,12},{8,0},{12,4},{16,24},{20,28},{24,16},{28,20},{1,9},{5... | collective-permute-start | bytes 208904 | tf_op jit(solution)/shard_map/ppermute | solution.py:39
  45.4 18.3 %collective-permute-start.11 = (f32[1040,128]{1,0:T(8,128)S(1)}, f32[1040,128]{1,0:T(8,128)S(1)}, u32[]{:S(2)}, u32[]{:S(2)}) collective-permute-start(f32[1040,128]{1,0:T(8,128)S(1)} %get-tuple-element.51.refs_0_.refs_2_), channel_id=1, source_target_pairs={{0,2},{2,0},{1,3},{3,1},{4,6},{6,4},{5,7},{7,5},{8,10},{10,8},{9,1... | collective-permute-start | bytes 1597448 | tf_op jit(solution)/shard_map/ppermute | solution.py:39
  45.7 6.9 %collective-permute-start.12 = (f32[136,128]{1,0:T(8,128)S(1)}, f32[136,128]{1,0:T(8,128)S(1)}, u32[]{:S(2)}, u32[]{:S(2)}) collective-permute-start(f32[136,128]{1,0:T(8,128)S(1)} %get-tuple-element.53), channel_id=1, source_target_pairs={{0,24},{4,28},{8,16},{12,20},{16,8},{20,12},{24,0},{28,4},{1,25},{... | collective-permute-start | bytes 208904 | tf_op jit(solution)/shard_map/ppermute | solution.py:39
  47.1 7.5 %collective-permute-start.13 = (f32[136,128]{1,0:T(8,128)S(1)}, f32[136,128]{1,0:T(8,128)S(1)}, u32[]{:S(2)}, u32[]{:S(2)}) collective-permute-start(f32[136,128]{1,0:T(8,128)S(1)} %get-tuple-element.54), channel_id=1, source_target_pairs={{0,16},{4,20},{8,24},{12,28},{16,0},{20,4},{24,8},{28,12},{1,17},{... | collective-permute-start | bytes 208904 | tf_op jit(solution)/shard_map/ppermute | solution.py:39
  47.8 6.8 %collective-permute-start.14 = (f32[136,128]{1,0:T(8,128)S(1)}, f32[136,128]{1,0:T(8,128)S(1)}, u32[]{:S(2)}, u32[]{:S(2)}) collective-permute-start(f32[136,128]{1,0:T(8,128)S(1)} %get-tuple-element.55), channel_id=1, source_target_pairs={{0,8},{4,12},{8,0},{12,4},{16,24},{20,28},{24,16},{28,20},{1,9},{5... | collective-permute-start | bytes 208904 | tf_op jit(solution)/shard_map/ppermute | solution.py:39
  54.7 7.0 %collective-permute-start.17 = (f32[136,128]{1,0:T(8,128)S(1)}, f32[136,128]{1,0:T(8,128)S(1)}, u32[]{:S(2)}, u32[]{:S(2)}) collective-permute-start(f32[136,128]{1,0:T(8,128)S(1)} %merge.3.refs_5_), channel_id=1, source_target_pairs={{0,24},{4,28},{8,16},{12,20},{16,8},{20,12},{24,0},{28,4},{1,25},{... | collective-permute-start | bytes 208904 | tf_op jit(solution)/shard_map/ppermute | solution.py:39
  56.4 7.3 %collective-permute-start.16 = (f32[136,128]{1,0:T(8,128)S(1)}, f32[136,128]{1,0:T(8,128)S(1)}, u32[]{:S(2)}, u32[]{:S(2)}) collective-permute-start(f32[136,128]{1,0:T(8,128)S(1)} %merge.3.refs_5_), channel_id=1, source_target_pairs={{0,16},{4,20},{8,24},{12,28},{16,0},{20,4},{24,8},{28,12},{1,17},{... | collective-permute-start | bytes 208904 | tf_op jit(solution)/shard_map/ppermute | solution.py:39
  56.4 7.3 %collective-permute-start.15 = (f32[136,128]{1,0:T(8,128)S(1)}, f32[136,128]{1,0:T(8,128)S(1)}, u32[]{:S(2)}, u32[]{:S(2)}) collective-permute-start(f32[136,128]{1,0:T(8,128)S(1)} %merge.3.refs_5_), channel_id=1, source_target_pairs={{0,8},{4,12},{8,0},{12,4},{16,24},{20,28},{24,16},{28,20},{1,9},{5... | collective-permute-start | bytes 208904 | tf_op jit(solution)/shard_map/ppermute | solution.py:39
  63.7 18.2 %collective-permute-start.18 = (f32[1040,128]{1,0:T(8,128)S(1)}, f32[1040,128]{1,0:T(8,128)S(1)}, u32[]{:S(2)}, u32[]{:S(2)}) collective-permute-start(f32[1040,128]{1,0:T(8,128)S(1)} %mate_parts.1), channel_id=1, source_target_pairs={{0,4},{4,0},{8,12},{12,8},{16,20},{20,16},{24,28},{28,24},{1,5},{5... | collective-permute-start | bytes 1597448 | tf_op jit(solution)/shard_map/ppermute | solution.py:39
  66.0 15.9 %collective-permute-start.20 = (f32[520,128]{1,0:T(8,128)S(1)}, f32[520,128]{1,0:T(8,128)S(1)}, u32[]{:S(2)}, u32[]{:S(2)}) collective-permute-start(f32[520,128]{1,0:T(8,128)S(1)} %get-tuple-element.58.refs_3_), channel_id=1, source_target_pairs={{0,2},{2,0},{4,6},{6,4},{8,10},{10,8},{12,14},{14,12},{16,18},{18,... | collective-permute-start | bytes 798728 | tf_op jit(solution)/shard_map/ppermute | solution.py:39
  66.9 15.0 %collective-permute-start.21 = (f32[520,128]{1,0:T(8,128)S(1)}, f32[520,128]{1,0:T(8,128)S(1)}, u32[]{:S(2)}, u32[]{:S(2)}) collective-permute-start(f32[520,128]{1,0:T(8,128)S(1)} %get-tuple-element.59), channel_id=1, source_target_pairs={{0,6},{2,4},{4,2},{6,0},{8,14},{10,12},{12,10},{14,8},{16,22},{18,... | collective-permute-start | bytes 798728 | tf_op jit(solution)/shard_map/ppermute | solution.py:39
  67.8 14.0 %collective-permute-start.19 = (f32[520,128]{1,0:T(8,128)S(1)}, f32[520,128]{1,0:T(8,128)S(1)}, u32[]{:S(2)}, u32[]{:S(2)}) collective-permute-start(f32[520,128]{1,0:T(8,128)S(1)} %get-tuple-element.59), channel_id=1, source_target_pairs={{0,4},{2,6},{4,0},{6,2},{8,12},{10,14},{12,8},{14,10},{16,20},{18,... | collective-permute-start | bytes 798728 | tf_op jit(solution)/shard_map/ppermute | solution.py:39

commit v16 on v15

--- a/solution.py
+++ b/solution.py
@@ -273,12 +273,11 @@
         return refs if len(refs) == CORES else [part_of(refs[0], at) for at in range(CORES)]
 
     def step_sizes(tile_refs):
-        tile = jnp.sum(tile_refs[0][...], axis=0)
-        sums = jnp.sum(tile, axis=1, keepdims=True)
+        row = jnp.sum(tile_refs[0][...], axis=0)
         return (
-            RATE_KEYS / jnp.sqrt(sums[0:1] / entry_total + EPSILON),
-            RATE_VALUES / jnp.sqrt(sums[1:2] / entry_total + EPSILON),
-            RATE_BIAS / jnp.sqrt(sums[2:3] / slot_total + EPSILON),
+            RATE_KEYS / jnp.sqrt(row[:, 0:1] / entry_total + EPSILON),
+            RATE_VALUES / jnp.sqrt(row[:, 1:2] / entry_total + EPSILON),
+            RATE_BIAS / jnp.sqrt(row[:, 2:3] / slot_total + EPSILON),
         )
 
     def updated(state_ref, grad_ref, sizes):
@@ -496,9 +495,12 @@
             out[2 * slot_rows :, :] = grad_bias
             for which, grad in enumerate((grad_keys, grad_values, grad_bias)):
                 squares[which] = squares[which] + jnp.sum(grad * grad, axis=0, keepdims=True)
-        tile = jnp.concatenate(squares + [jnp.zeros((TAIL - 3, width), jnp.float32)], axis=0)
+        lanes = lax.broadcasted_iota(jnp.int32, (1, width), 1)
+        row = jnp.zeros((1, width), jnp.float32)
+        for which, square in enumerate(squares):
+            row = jnp.where(lanes == which, jnp.sum(square, axis=1, keepdims=True), row)
         for at in range(devices):
-            squares_out[at] = tile
+            squares_out[at] = row
 
     def mate_body(*refs):
         *state_refs, out_ref = refs
@@ -573,7 +575,7 @@
             from_mate = exchange(for_mate, page=1)
         own_grad, mate_grad, squares = call(
             backward_body,
-            packed_shapes + [(devices, TAIL, width)],
+            packed_shapes + [(devices, 1, width)],
             "backward",
             3 * matmul_cost,
             weights + maxima + states + query_parts + all_merged,

time: 83.2 us -> 79.9 us (0.960)
  blocking collectives: 26 us -> 23.6 us
  waiting for transfers between devices: 16.3 us -> 15.1 us
    all_to_all x2, blocking collectives: 26 us -> 23.6 us  [direct_per_device(): lax.all_to_all(squares, ('page', 'query', 'head'), split_axis=0, concat_a...]
    ppermute x22, waiting for transfers between devices: 16.3 us -> 15.1 us  [exchange(): return lax.ppermute(value, axes, pairs)]
where the time goes in v16:
time: 79.9 us; the launch traced here: 79.8 us
  starting transfers between devices  28.2 us (35%)
  blocking collectives  23.6 us (30%)
  waiting for transfers between devices  15.1 us (19%)
  Pallas kernels  12 us (15%)
  between operations  0.86 us (1%)
    ppermute x22, starting transfers between devices, exchange(): return lax.ppermute(value, axes, pairs)  28.2 us
    all_to_all x2, blocking collectives, direct_per_device(): lax.all_to_all(squares, ('page', 'query', 'head'), split_axis=0, concat_a...  23.6 us
    ppermute x22, waiting for transfers between devices, exchange(): return lax.ppermute(value, axes, pairs)  15.1 us
    pallas_call x11, Pallas kernels, call(): pl.pallas_call(without_after, out_shape=[jax.ShapeDtypeStruct(shape, jnp....  12 us
  transfers between devices with their start and end apart: 22, of which 8 were waited for; matrix products, arithmetic and copies ran while one was open for 0% of the time, Pallas kernels for 6%

profile of v16, /device:TPU:0, one launch (start us, length us, event | category | flops | bytes accessed | tf_op | source)
XLA Modules:
  0.0 79.8 jit_solution(6648743050022014981)
XLA Ops:
  0.7 2.0 %pack.1 = (f32[520,128]{1,0:T(8,128)}, f32[328,128]{1,0:T(8,128)}) custom-call(f32[4,256,128]{2,1,0:T(8,128)} %refs_0_.3, f32[4,256,128]{2,1,0:T(8,128)} %refs_1_.3, f32[4,256,128]{2,1,0:T(8,128)} %refs_2_.3, f32[4,256]{1,0:T(4,128)} %refs_3_.3, f32[4,256,128]{2,1,0:T(8,128)} %refs_4_.3, s32[4,256]{1,0:T(4,128)} %refs_5_.3, s32[8]{0:T(128)} %refs_6_.3), custom_call_target="tpu_custom_call" | custom-call | flops 1048576 | bytes 1048576 | tf_op jit(solution)/shard_map/pack/pallas_call | solution.py:67
  2.7 0.0 copy-start.6
  2.7 0.5 collective-permute-start
  3.3 2.6 %collective-permute-start.1 = (f32[328,128]{1,0:T(8,128)}, f32[328,128]{1,0:T(8,128)S(1)}, u32[]{:S(2)}, u32[]{:S(2)}) collective-permute-start(f32[328,128]{1,0:T(8,128)} %get-tuple-element.35), channel_id=1, source_target_pairs={{0,2},{2,0},{1,3},{3,1},{4,6},{6,4},{5,7},{7,5},{8,10},{10,8},{9,1... | collective-permute-start | bytes 503816 | tf_op jit(solution)/shard_map/ppermute | solution.py:39
  5.9 0.7 own.1
  6.6 1.0 %forward.2 = (f32[72,128]{1,0:T(8,128)S(1)}, f32[72,128]{1,0:T(8,128)S(1)}, f32[72,128]{1,0:T(8,128)S(1)}, f32[72,128]{1,0:T(8,128)S(1)}, f32[512,256]{1,0:T(8,128)S(1)}, /*index=5*/f32[8,256]{1,0:T(8,128)S(1)}) custom-call(f32[520,128]{1,0:T(8,128)S(1)} %get-tuple-element.32.refs_0_.refs_4_, f32[520,128]{1,0:T(8,128)S(1)} %collective-permute-done.refs_1_.refs_5_, ...), custom_call_target="tpu_custom_call" | custom-call | flops 201326592 | bytes 1048576 | tf_op jit(solution)/shard_map/forward/pallas_call | solution.py:67
  7.6 3.7 %collective-permute-start.2 = (f32[72,128]{1,0:T(8,128)S(1)}, f32[72,128]{1,0:T(8,128)S(1)}, u32[]{:S(2)}, u32[]{:S(2)}) collective-permute-start(f32[72,128]{1,0:T(8,128)S(1)} %get-tuple-element.40), channel_id=1, source_target_pairs={{0,24},{4,28},{8,16},{12,20},{16,8},{20,12},{24,0},{28,4},{1,25},{... | collective-permute-start | bytes 110600 | tf_op jit(solution)/shard_map/ppermute | solution.py:39
  11.3 0.0 collective-permute-start.3
  11.3 0.8 collective-permute-start.4
  12.0 0.0 collective-permute-done.1.refs_2_.refs_1_.refs_7_.refs_3_.refs_4_
  12.0 1.0 %forward.3 = (f32[72,128]{1,0:T(8,128)S(1)}, f32[72,128]{1,0:T(8,128)S(1)}, f32[72,128]{1,0:T(8,128)S(1)}, f32[72,128]{1,0:T(8,128)S(1)}, f32[512,256]{1,0:T(8,128)S(1)}, /*index=5*/f32[8,256]{1,0:T(8,128)S(1)}) custom-call(f32[520,128]{1,0:T(8,128)S(1)} %get-tuple-element.32.refs_0_.refs_4_, f32[520,128]{1,0:T(8,128)S(1)} %collective-permute-done.refs_1_.refs_5_, ...), custom_call_target="tpu_custom_call" | custom-call | flops 201326592 | bytes 1048576 | tf_op jit(solution)/shard_map/forward/pallas_call | solution.py:67
  13.1 3.7 %collective-permute-start.5 = (f32[72,128]{1,0:T(8,128)S(1)}, f32[72,128]{1,0:T(8,128)S(1)}, u32[]{:S(2)}, u32[]{:S(2)}) collective-permute-start(f32[72,128]{1,0:T(8,128)S(1)} %get-tuple-element.44), channel_id=1, source_target_pairs={{0,24},{4,28},{8,16},{12,20},{16,8},{20,12},{24,0},{28,4},{1,25},{... | collective-permute-start | bytes 110600 | tf_op jit(solution)/shard_map/ppermute | solution.py:39
  16.7 0.0 collective-permute-start.6
  16.7 0.0 collective-permute-done.2.refs_2_
  16.7 0.8 collective-permute-start.7
  17.5 0.0 collective-permute-done.3.refs_3_
  17.5 0.0 collective-permute-done.4.refs_4_
  17.5 1.5 %collective-permute-done.5.refs_6_ = f32[72,128]{1,0:T(8,128)S(1)} collective-permute-done((f32[72,128]{1,0:T(8,128)S(1)}, f32[72,128]{1,0:T(8,128)S(1)}, u32[]{:S(2)}, u32[]{:S(2)}) %collective-permute-start.5) | collective-permute-done | bytes 36896 | tf_op jit(solution)/shard_map/ppermute | solution.py:39
  19.0 2.6 %collective-permute-done.6.refs_7_ = f32[72,128]{1,0:T(8,128)S(1)} collective-permute-done((f32[72,128]{1,0:T(8,128)S(1)}, f32[72,128]{1,0:T(8,128)S(1)}, u32[]{:S(2)}, u32[]{:S(2)}) %collective-permute-start.6) | collective-permute-done | bytes 36896 | tf_op jit(solution)/shard_map/ppermute | solution.py:39
  21.6 0.3 merge.2.refs_8_
  21.9 1.5 %collective-permute-start.10 = (f32[136,128]{1,0:T(8,128)S(1)}, f32[136,128]{1,0:T(8,128)S(1)}, u32[]{:S(2)}, u32[]{:S(2)}) collective-permute-start(f32[136,128]{1,0:T(8,128)S(1)} %merge.2.refs_8_), channel_id=1, source_target_pairs={{0,24},{4,28},{8,16},{12,20},{16,8},{20,12},{24,0},{28,4},{1,25},{... | collective-permute-start | bytes 208904 | tf_op jit(solution)/shard_map/ppermute | solution.py:39
  23.4 0.6 collective-permute-start.9
  24.0 2.3 %collective-permute-start.8 = (f32[136,128]{1,0:T(8,128)S(1)}, f32[136,128]{1,0:T(8,128)S(1)}, u32[]{:S(2)}, u32[]{:S(2)}) collective-permute-start(f32[136,128]{1,0:T(8,128)S(1)} %merge.2.refs_8_), channel_id=1, source_target_pairs={{0,8},{4,12},{8,0},{12,4},{16,24},{20,28},{24,16},{28,20},{1,9},{5... | collective-permute-start | bytes 208904 | tf_op jit(solution)/shard_map/ppermute | solution.py:39
  26.3 1.8 %collective-permute-done.10.refs_11_ = f32[136,128]{1,0:T(8,128)S(1)} collective-permute-done((f32[136,128]{1,0:T(8,128)S(1)}, f32[136,128]{1,0:T(8,128)S(1)}, u32[]{:S(2)}, u32[]{:S(2)}) %collective-permute-start.10) | collective-permute-done | bytes 69664 | tf_op jit(solution)/shard_map/ppermute | solution.py:39
  28.1 1.5 %collective-permute-done.9.refs_10_ = f32[136,128]{1,0:T(8,128)S(1)} collective-permute-done((f32[136,128]{1,0:T(8,128)S(1)}, f32[136,128]{1,0:T(8,128)S(1)}, u32[]{:S(2)}, u32[]{:S(2)}) %collective-permute-start.9) | collective-permute-done | bytes 69664 | tf_op jit(solution)/shard_map/ppermute | solution.py:39
  29.5 0.0 collective-permute-done.8.refs_9_
  29.5 2.3 %backward.2 = (f32[520,128]{1,0:T(8,128)S(1)}, f32[520,128]{1,0:T(8,128)S(1)}, f32[32,1,128]{2,1,0:T(1,128)S(1)}) custom-call(f32[512,256]{1,0:T(8,128)S(1)} %get-tuple-element.36.refs_0_, f32[512,256]{1,0:T(8,128)S(1)} %get-tuple-element.38.refs_1_, f32[8,256]{1,0:T(8,128)S(1)} %get-tuple-element.37.refs_3_.refs_2_, ...), custom_call_target="tpu_custom_call" | custom-call | flops 603979776 | bytes 1048576 | tf_op jit(solution)/shard_map/backward/pallas_call | solution.py:67
  31.8 11.1 %all_to_all.10.refs_6_ = f32[32,1,128]{2,1,0:T(1,128)S(1)} all-to-all(f32[32,1,128]{2,1,0:T(1,128)S(1)} %get-tuple-element.50), channel_id=1, replica_groups=mesh['page'=8,'query'=2,'head'=2] {'page','query','head'}, dimensions={0} | all-to-all | bytes 32768 | tf_op jit(solution)/shard_map/all_to_all | solution.py:588
  42.9 1.3 %update_forward.1 = (f32[1040,128]{1,0:T(8,128)S(1)}, f32[136,128]{1,0:T(8,128)S(1)}, f32[136,128]{1,0:T(8,128)S(1)}, f32[136,128]{1,0:T(8,128)S(1)}, f32[136,12...) custom-call(f32[520,128]{1,0:T(8,128)S(1)} %get-tuple-element.32.refs_0_.refs_4_, ...), custom_call_target="tpu_custom_call" | custom-call | flops 402653184 | bytes 1048576 | tf_op jit(solution)/shard_map/update_forward/pallas_call | solution.py:67
  44.2 0.6 collective-permute-start.11
  44.8 0.6 collective-permute-start.12
  45.3 1.5 %collective-permute-start.13 = (f32[136,128]{1,0:T(8,128)S(1)}, f32[136,128]{1,0:T(8,128)S(1)}, u32[]{:S(2)}, u32[]{:S(2)}) collective-permute-start(f32[136,128]{1,0:T(8,128)S(1)} %get-tuple-element.54), channel_id=1, source_target_pairs={{0,16},{4,20},{8,24},{12,28},{16,0},{20,4},{24,8},{28,12},{1,17},{... | collective-permute-start | bytes 208904 | tf_op jit(solution)/shard_map/ppermute | solution.py:39
  46.8 2.4 %collective-permute-start.14 = (f32[136,128]{1,0:T(8,128)S(1)}, f32[136,128]{1,0:T(8,128)S(1)}, u32[]{:S(2)}, u32[]{:S(2)}) collective-permute-start(f32[136,128]{1,0:T(8,128)S(1)} %get-tuple-element.55), channel_id=1, source_target_pairs={{0,8},{4,12},{8,0},{12,4},{16,24},{20,28},{24,16},{28,20},{1,9},{5... | collective-permute-start | bytes 208904 | tf_op jit(solution)/shard_map/ppermute | solution.py:39
  49.2 2.5 %collective-permute-done.12.refs_3_ = f32[136,128]{1,0:T(8,128)S(1)} collective-permute-done((f32[136,128]{1,0:T(8,128)S(1)}, f32[136,128]{1,0:T(8,128)S(1)}, u32[]{:S(2)}, u32[]{:S(2)}) %collective-permute-start.12) | collective-permute-done | bytes 69664 | tf_op jit(solution)/shard_map/ppermute | solution.py:39
  51.7 1.7 %collective-permute-done.13.refs_4_ = f32[136,128]{1,0:T(8,128)S(1)} collective-permute-done((f32[136,128]{1,0:T(8,128)S(1)}, f32[136,128]{1,0:T(8,128)S(1)}, u32[]{:S(2)}, u32[]{:S(2)}) %collective-permute-start.13) | collective-permute-done | bytes 69664 | tf_op jit(solution)/shard_map/ppermute | solution.py:39
  53.3 0.1 merge.3.refs_5_
  53.5 1.2 %collective-permute-start.17 = (f32[136,128]{1,0:T(8,128)S(1)}, f32[136,128]{1,0:T(8,128)S(1)}, u32[]{:S(2)}, u32[]{:S(2)}) collective-permute-start(f32[136,128]{1,0:T(8,128)S(1)} %merge.3.refs_5_), channel_id=1, source_target_pairs={{0,24},{4,28},{8,16},{12,20},{16,8},{20,12},{24,0},{28,4},{1,25},{... | collective-permute-start | bytes 208904 | tf_op jit(solution)/shard_map/ppermute | solution.py:39
  54.7 0.4 collective-permute-start.16
  55.1 2.8 %collective-permute-start.15 = (f32[136,128]{1,0:T(8,128)S(1)}, f32[136,128]{1,0:T(8,128)S(1)}, u32[]{:S(2)}, u32[]{:S(2)}) collective-permute-start(f32[136,128]{1,0:T(8,128)S(1)} %merge.3.refs_5_), channel_id=1, source_target_pairs={{0,8},{4,12},{8,0},{12,4},{16,24},{20,28},{24,16},{28,20},{1,9},{5... | collective-permute-start | bytes 208904 | tf_op jit(solution)/shard_map/ppermute | solution.py:39
  57.9 2.4 %collective-permute-done.17.refs_4_.refs_8_ = f32[136,128]{1,0:T(8,128)S(1)} collective-permute-done((f32[136,128]{1,0:T(8,128)S(1)}, f32[136,128]{1,0:T(8,128)S(1)}, u32[]{:S(2)}, u32[]{:S(2)}) %collective-permute-start.17) | collective-permute-done | bytes 69664 | tf_op jit(solution)/shard_map/ppermute | solution.py:39
  60.3 1.2 %collective-permute-done.16.refs_3_.refs_7_ = f32[136,128]{1,0:T(8,128)S(1)} collective-permute-done((f32[136,128]{1,0:T(8,128)S(1)}, f32[136,128]{1,0:T(8,128)S(1)}, u32[]{:S(2)}, u32[]{:S(2)}) %collective-permute-start.16) | collective-permute-done | bytes 69664 | tf_op jit(solution)/shard_map/ppermute | solution.py:39
  61.5 0.1 collective-permute-start.18
  61.6 2.2 %backward.3 = (f32[520,128]{1,0:T(8,128)S(1)}, f32[520,128]{1,0:T(8,128)S(1)}, f32[32,1,128]{2,1,0:T(1,128)S(1)}) custom-call(f32[512,512]{1,0:T(8,128)S(1)} %get-tuple-element.56.refs_0_, f32[8,512]{1,0:T(8,128)S(1)} %get-tuple-element.57.refs_1_, f32[1040,128]{1,0:T(8,128)S(1)} %get-tuple-element.51.refs_0_.refs_2_, ...), custom_call_target="tpu_custom_call" | custom-call | flops 603979776 | bytes 1048576 | tf_op jit(solution)/shard_map/backward/pallas_call | solution.py:67
  63.9 1.2 %collective-permute-start.20 = (f32[520,128]{1,0:T(8,128)S(1)}, f32[520,128]{1,0:T(8,128)S(1)}, u32[]{:S(2)}, u32[]{:S(2)}) collective-permute-start(f32[520,128]{1,0:T(8,128)S(1)} %get-tuple-element.58.refs_3_), channel_id=1, source_target_pairs={{0,2},{2,0},{4,6},{6,4},{8,10},{10,8},{12,14},{14,12},{16,18},{18,... | collective-permute-start | bytes 798728 | tf_op jit(solution)/shard_map/ppermute | solution.py:39
  65.1 0.7 collective-permute-start.21
  65.8 0.3 collective-permute-start.19
  66.1 12.5 %all_to_all.11.refs_7_ = f32[32,1,128]{2,1,0:T(1,128)S(1)} all-to-all(f32[32,1,128]{2,1,0:T(1,128)S(1)} %get-tuple-element.60), channel_id=1, replica_groups=mesh['page'=8,'query'=2,'head'=2] {'page','query','head'}, dimensions={0} | all-to-all | bytes 32768 | tf_op jit(solution)/shard_map/all_to_all | solution.py:588
  78.6 1.2 %last_update.1 = (f32[4,256,128]{2,1,0:T(8,128)}, f32[4,256,128]{2,1,0:T(8,128)}, f32[4,256]{1,0:T(4,128)}) custom-call(f32[1040,128]{1,0:T(8,128)S(1)} %get-tuple-element.51.refs_0_.refs_2_, f32[1040,128]{1,0:T(8,128)S(1)} %collective-permute-done.11.refs_1_, f32[1040,128]{1,0:T(8,128)S(1)} %collective-permute-done.18.refs_2_, ...), custom_call_target="tpu_custom_call" | custom-call | flops 1048576 | bytes 1048576 | tf_op jit(solution)/shard_map/last_update/pallas_call | solution.py:67
  (23 shorter events, 0.1 us)
Async XLA Ops:
  0.6 5.2 %copy-start.3 = (f32[4,256,128]{2,1,0:T(8,128)S(1)}, f32[4,256,128]{2,1,0:T(8,128)}, u32[]{:S(2)}) copy-start(f32[4,256,128]{2,1,0:T(8,128)} %refs_4_.3) | copy-start | bytes 1572868
  0.6 5.2 %copy-start.2 = (f32[4,256,128]{2,1,0:T(8,128)S(1)}, f32[4,256,128]{2,1,0:T(8,128)}, u32[]{:S(2)}) copy-start(f32[4,256,128]{2,1,0:T(8,128)} %refs_2_.3) | copy-start | bytes 1572868
  0.7 5.2 %copy-start.1 = (f32[4,256,128]{2,1,0:T(8,128)S(1)}, f32[4,256,128]{2,1,0:T(8,128)}, u32[]{:S(2)}) copy-start(f32[4,256,128]{2,1,0:T(8,128)} %refs_1_.3) | copy-start | bytes 1572868
  0.7 5.2 %copy-start = (f32[4,256,128]{2,1,0:T(8,128)S(1)}, f32[4,256,128]{2,1,0:T(8,128)}, u32[]{:S(2)}) copy-start(f32[4,256,128]{2,1,0:T(8,128)} %refs_0_.3) | copy-start | bytes 1572868
  0.7 5.2 %copy-start.4 = (f32[4,256]{1,0:T(4,128)S(1)}, f32[4,256]{1,0:T(4,128)}, u32[]{:S(2)}) copy-start(f32[4,256]{1,0:T(4,128)} %refs_3_.3) | copy-start | bytes 12292
  0.7 5.2 %copy-start.5 = (s32[4,256]{1,0:T(4,128)S(1)}, s32[4,256]{1,0:T(4,128)}, u32[]{:S(2)}) copy-start(s32[4,256]{1,0:T(4,128)} %refs_5_.3) | copy-start | bytes 12292
  2.7 3.2 %copy-start.6 = (s32[8]{0:T(128)S(1)}, s32[8]{0:T(128)}, u32[]{:S(2)}) copy-start(s32[8]{0:T(128)} %refs_6_.3) | copy-start | bytes 100
  2.7 3.8 %collective-permute-start = (f32[520,128]{1,0:T(8,128)}, f32[520,128]{1,0:T(8,128)S(1)}, u32[]{:S(2)}, u32[]{:S(2)}) collective-permute-start(f32[520,128]{1,0:T(8,128)} %get-tuple-element.33), channel_id=1, source_target_pairs={{0,4},{4,0},{8,12},{12,8},{16,20},{20,16},{24,28},{28,24},{1,5},{5... | collective-permute-start | bytes 798728 | tf_op jit(solution)/shard_map/ppermute | solution.py:39
  3.3 8.8 %collective-permute-start.1 = (f32[328,128]{1,0:T(8,128)}, f32[328,128]{1,0:T(8,128)S(1)}, u32[]{:S(2)}, u32[]{:S(2)}) collective-permute-start(f32[328,128]{1,0:T(8,128)} %get-tuple-element.35), channel_id=1, source_target_pairs={{0,2},{2,0},{1,3},{3,1},{4,6},{6,4},{5,7},{7,5},{8,10},{10,8},{9,1... | collective-permute-start | bytes 503816 | tf_op jit(solution)/shard_map/ppermute | solution.py:39
  7.6 9.2 %collective-permute-start.2 = (f32[72,128]{1,0:T(8,128)S(1)}, f32[72,128]{1,0:T(8,128)S(1)}, u32[]{:S(2)}, u32[]{:S(2)}) collective-permute-start(f32[72,128]{1,0:T(8,128)S(1)} %get-tuple-element.40), channel_id=1, source_target_pairs={{0,24},{4,28},{8,16},{12,20},{16,8},{20,12},{24,0},{28,4},{1,25},{... | collective-permute-start | bytes 110600 | tf_op jit(solution)/shard_map/ppermute | solution.py:39
  11.3 6.3 %collective-permute-start.3 = (f32[72,128]{1,0:T(8,128)S(1)}, f32[72,128]{1,0:T(8,128)S(1)}, u32[]{:S(2)}, u32[]{:S(2)}) collective-permute-start(f32[72,128]{1,0:T(8,128)S(1)} %get-tuple-element.41), channel_id=1, source_target_pairs={{0,16},{4,20},{8,24},{12,28},{16,0},{20,4},{24,8},{28,12},{1,17},{... | collective-permute-start | bytes 110600 | tf_op jit(solution)/shard_map/ppermute | solution.py:39
  11.3 6.3 %collective-permute-start.4 = (f32[72,128]{1,0:T(8,128)S(1)}, f32[72,128]{1,0:T(8,128)S(1)}, u32[]{:S(2)}, u32[]{:S(2)}) collective-permute-start(f32[72,128]{1,0:T(8,128)S(1)} %get-tuple-element.42), channel_id=1, source_target_pairs={{0,8},{4,12},{8,0},{12,4},{16,24},{20,28},{24,16},{28,20},{1,9},{5... | collective-permute-start | bytes 110600 | tf_op jit(solution)/shard_map/ppermute | solution.py:39
  13.1 5.9 %collective-permute-start.5 = (f32[72,128]{1,0:T(8,128)S(1)}, f32[72,128]{1,0:T(8,128)S(1)}, u32[]{:S(2)}, u32[]{:S(2)}) collective-permute-start(f32[72,128]{1,0:T(8,128)S(1)} %get-tuple-element.44), channel_id=1, source_target_pairs={{0,24},{4,28},{8,16},{12,20},{16,8},{20,12},{24,0},{28,4},{1,25},{... | collective-permute-start | bytes 110600 | tf_op jit(solution)/shard_map/ppermute | solution.py:39
  16.7 4.9 %collective-permute-start.6 = (f32[72,128]{1,0:T(8,128)S(1)}, f32[72,128]{1,0:T(8,128)S(1)}, u32[]{:S(2)}, u32[]{:S(2)}) collective-permute-start(f32[72,128]{1,0:T(8,128)S(1)} %get-tuple-element.45), channel_id=1, source_target_pairs={{0,16},{4,20},{8,24},{12,28},{16,0},{20,4},{24,8},{28,12},{1,17},{... | collective-permute-start | bytes 110600 | tf_op jit(solution)/shard_map/ppermute | solution.py:39
  16.7 4.9 %collective-permute-start.7 = (f32[72,128]{1,0:T(8,128)S(1)}, f32[72,128]{1,0:T(8,128)S(1)}, u32[]{:S(2)}, u32[]{:S(2)}) collective-permute-start(f32[72,128]{1,0:T(8,128)S(1)} %get-tuple-element.46), channel_id=1, source_target_pairs={{0,8},{4,12},{8,0},{12,4},{16,24},{20,28},{24,16},{28,20},{1,9},{5... | collective-permute-start | bytes 110600 | tf_op jit(solution)/shard_map/ppermute | solution.py:39
  21.9 6.2 %collective-permute-start.10 = (f32[136,128]{1,0:T(8,128)S(1)}, f32[136,128]{1,0:T(8,128)S(1)}, u32[]{:S(2)}, u32[]{:S(2)}) collective-permute-start(f32[136,128]{1,0:T(8,128)S(1)} %merge.2.refs_8_), channel_id=1, source_target_pairs={{0,24},{4,28},{8,16},{12,20},{16,8},{20,12},{24,0},{28,4},{1,25},{... | collective-permute-start | bytes 208904 | tf_op jit(solution)/shard_map/ppermute | solution.py:39
  23.4 6.1 %collective-permute-start.9 = (f32[136,128]{1,0:T(8,128)S(1)}, f32[136,128]{1,0:T(8,128)S(1)}, u32[]{:S(2)}, u32[]{:S(2)}) collective-permute-start(f32[136,128]{1,0:T(8,128)S(1)} %merge.2.refs_8_), channel_id=1, source_target_pairs={{0,16},{4,20},{8,24},{12,28},{16,0},{20,4},{24,8},{28,12},{1,17},{... | collective-permute-start | bytes 208904 | tf_op jit(solution)/shard_map/ppermute | solution.py:39
  24.0 5.5 %collective-permute-start.8 = (f32[136,128]{1,0:T(8,128)S(1)}, f32[136,128]{1,0:T(8,128)S(1)}, u32[]{:S(2)}, u32[]{:S(2)}) collective-permute-start(f32[136,128]{1,0:T(8,128)S(1)} %merge.2.refs_8_), channel_id=1, source_target_pairs={{0,8},{4,12},{8,0},{12,4},{16,24},{20,28},{24,16},{28,20},{1,9},{5... | collective-permute-start | bytes 208904 | tf_op jit(solution)/shard_map/ppermute | solution.py:39
  44.2 17.3 %collective-permute-start.11 = (f32[1040,128]{1,0:T(8,128)S(1)}, f32[1040,128]{1,0:T(8,128)S(1)}, u32[]{:S(2)}, u32[]{:S(2)}) collective-permute-start(f32[1040,128]{1,0:T(8,128)S(1)} %get-tuple-element.51.refs_0_.refs_2_), channel_id=1, source_target_pairs={{0,2},{2,0},{1,3},{3,1},{4,6},{6,4},{5,7},{7,5},{8,10},{10,8},{9,1... | collective-permute-start | bytes 1597448 | tf_op jit(solution)/shard_map/ppermute | solution.py:39
  44.8 6.9 %collective-permute-start.12 = (f32[136,128]{1,0:T(8,128)S(1)}, f32[136,128]{1,0:T(8,128)S(1)}, u32[]{:S(2)}, u32[]{:S(2)}) collective-permute-start(f32[136,128]{1,0:T(8,128)S(1)} %get-tuple-element.53), channel_id=1, source_target_pairs={{0,24},{4,28},{8,16},{12,20},{16,8},{20,12},{24,0},{28,4},{1,25},{... | collective-permute-start | bytes 208904 | tf_op jit(solution)/shard_map/ppermute | solution.py:39
  45.3 8.0 %collective-permute-start.13 = (f32[136,128]{1,0:T(8,128)S(1)}, f32[136,128]{1,0:T(8,128)S(1)}, u32[]{:S(2)}, u32[]{:S(2)}) collective-permute-start(f32[136,128]{1,0:T(8,128)S(1)} %get-tuple-element.54), channel_id=1, source_target_pairs={{0,16},{4,20},{8,24},{12,28},{16,0},{20,4},{24,8},{28,12},{1,17},{... | collective-permute-start | bytes 208904 | tf_op jit(solution)/shard_map/ppermute | solution.py:39
  46.8 6.5 %collective-permute-start.14 = (f32[136,128]{1,0:T(8,128)S(1)}, f32[136,128]{1,0:T(8,128)S(1)}, u32[]{:S(2)}, u32[]{:S(2)}) collective-permute-start(f32[136,128]{1,0:T(8,128)S(1)} %get-tuple-element.55), channel_id=1, source_target_pairs={{0,8},{4,12},{8,0},{12,4},{16,24},{20,28},{24,16},{28,20},{1,9},{5... | collective-permute-start | bytes 208904 | tf_op jit(solution)/shard_map/ppermute | solution.py:39
  53.5 6.9 %collective-permute-start.17 = (f32[136,128]{1,0:T(8,128)S(1)}, f32[136,128]{1,0:T(8,128)S(1)}, u32[]{:S(2)}, u32[]{:S(2)}) collective-permute-start(f32[136,128]{1,0:T(8,128)S(1)} %merge.3.refs_5_), channel_id=1, source_target_pairs={{0,24},{4,28},{8,16},{12,20},{16,8},{20,12},{24,0},{28,4},{1,25},{... | collective-permute-start | bytes 208904 | tf_op jit(solution)/shard_map/ppermute | solution.py:39
  54.7 6.8 %collective-permute-start.16 = (f32[136,128]{1,0:T(8,128)S(1)}, f32[136,128]{1,0:T(8,128)S(1)}, u32[]{:S(2)}, u32[]{:S(2)}) collective-permute-start(f32[136,128]{1,0:T(8,128)S(1)} %merge.3.refs_5_), channel_id=1, source_target_pairs={{0,16},{4,20},{8,24},{12,28},{16,0},{20,4},{24,8},{28,12},{1,17},{... | collective-permute-start | bytes 208904 | tf_op jit(solution)/shard_map/ppermute | solution.py:39
  55.1 6.4 %collective-permute-start.15 = (f32[136,128]{1,0:T(8,128)S(1)}, f32[136,128]{1,0:T(8,128)S(1)}, u32[]{:S(2)}, u32[]{:S(2)}) collective-permute-start(f32[136,128]{1,0:T(8,128)S(1)} %merge.3.refs_5_), channel_id=1, source_target_pairs={{0,8},{4,12},{8,0},{12,4},{16,24},{20,28},{24,16},{28,20},{1,9},{5... | collective-permute-start | bytes 208904 | tf_op jit(solution)/shard_map/ppermute | solution.py:39
  61.5 17.0 %collective-permute-start.18 = (f32[1040,128]{1,0:T(8,128)S(1)}, f32[1040,128]{1,0:T(8,128)S(1)}, u32[]{:S(2)}, u32[]{:S(2)}) collective-permute-start(f32[1040,128]{1,0:T(8,128)S(1)} %mate_parts.1), channel_id=1, source_target_pairs={{0,4},{4,0},{8,12},{12,8},{16,20},{20,16},{24,28},{28,24},{1,5},{5... | collective-permute-start | bytes 1597448 | tf_op jit(solution)/shard_map/ppermute | solution.py:39
  63.9 14.7 %collective-permute-start.20 = (f32[520,128]{1,0:T(8,128)S(1)}, f32[520,128]{1,0:T(8,128)S(1)}, u32[]{:S(2)}, u32[]{:S(2)}) collective-permute-start(f32[520,128]{1,0:T(8,128)S(1)} %get-tuple-element.58.refs_3_), channel_id=1, source_target_pairs={{0,2},{2,0},{4,6},{6,4},{8,10},{10,8},{12,14},{14,12},{16,18},{18,... | collective-permute-start | bytes 798728 | tf_op jit(solution)/shard_map/ppermute | solution.py:39
  65.1 13.5 %collective-permute-start.21 = (f32[520,128]{1,0:T(8,128)S(1)}, f32[520,128]{1,0:T(8,128)S(1)}, u32[]{:S(2)}, u32[]{:S(2)}) collective-permute-start(f32[520,128]{1,0:T(8,128)S(1)} %get-tuple-element.59), channel_id=1, source_target_pairs={{0,6},{2,4},{4,2},{6,0},{8,14},{10,12},{12,10},{14,8},{16,22},{18,... | collective-permute-start | bytes 798728 | tf_op jit(solution)/shard_map/ppermute | solution.py:39
  65.8 12.8 %collective-permute-start.19 = (f32[520,128]{1,0:T(8,128)S(1)}, f32[520,128]{1,0:T(8,128)S(1)}, u32[]{:S(2)}, u32[]{:S(2)}) collective-permute-start(f32[520,128]{1,0:T(8,128)S(1)} %get-tuple-element.59), channel_id=1, source_target_pairs={{0,4},{2,6},{4,0},{6,2},{8,12},{10,14},{12,8},{14,10},{16,20},{18,... | collective-permute-start | bytes 798728 | tf_op jit(solution)/shard_map/ppermute | solution.py:39

commit v17 on v16

--- a/solution.py
+++ b/solution.py
@@ -142,6 +142,10 @@
         page = lax.axis_index("page")
         return page // CORES, page % CORES, lax.axis_index("query")
 
+    def to_device(value, **masks):
+        masks = {axis: mask for axis, mask in masks.items() if mask}
+        return exchange(value, **masks) if masks else value
+
     def pack_queries(head, rank, queries, targets, out):
         rows = pl.ds(pl.multiple_of(rank * piece, piece), piece)
         return [
@@ -248,9 +252,12 @@
         small_scratch + [pltpu.SemaphoreType.DMA((7,))],
         space=pl.ANY,
     )
-    query_parts = [own_queries] + [
-        exchange(sent_queries[turn - 1], query=turn) for turn in range(1, query_devices)
-    ]
+    packs = [own_queries] + list(sent_queries)
+
+    def query_part(turn, part):
+        return to_device(packs[part], query=turn ^ part)
+
+    query_parts = [query_part(0, part) for part in range(query_devices)]
     states = [own_state, exchange(mate_state, page=1)]
 
     def in_columns(parts, axis):
@@ -288,20 +295,26 @@
             state_ref[value_end:, :] - sizes[2] * grad_ref[value_end:, :],
         )
 
+    def page_scores(ref, queries, positions):
+        scores = dot(halves(ref[:slot_rows, :]), queries, 1, 1) * score_scale
+        bias = row_as_column(tail_as_row(ref, 2 * slot_rows, bias_rows), width)
+        scores = scores + jnp.concatenate([bias] * (positions.shape[1] // width), axis=1)
+        page_start = ref[packed_rows - 1 : packed_rows, 0:1]
+        visible = jnp.broadcast_to(positions >= page_start, scores.shape)
+        return jnp.where(visible, scores, MASKED), visible
+
+    def read_positions(query_refs):
+        return in_columns(
+            [tail_as_row(ref, part_rows + piece, pos_rows) for ref in query_refs], 1
+        )
+
     def forward(state_refs, query_refs, chunk_outs, weights_out, max_out, chunks):
         rank, _, _ = places()
-        all_queries = read_queries(query_refs)
-        position_row = in_columns(
-            [tail_as_row(ref, part_rows + piece, pos_rows) for ref in query_refs], 1
-        )
+        all_queries, positions = read_queries(query_refs), read_positions(query_refs)
         all_scores, all_visible = [], []
         for at, ref in enumerate(state_refs):
-            scores = dot(halves(ref[:slot_rows, :]), all_queries, 1, 1) * score_scale
-            bias = row_as_column(tail_as_row(ref, 2 * slot_rows, bias_rows), width)
-            scores = scores + jnp.concatenate([bias] * (query_rows // width), axis=1)
-            page_start = ref[packed_rows - 1 : packed_rows, 0:1]
-            visible = jnp.broadcast_to(position_row >= page_start, scores.shape)
-            all_scores.append(jnp.where(visible, scores, MASKED))
+            scores, visible = page_scores(ref, all_queries, positions)
+            all_scores.append(scores)
             all_visible.append(visible)
         row_max = jnp.max(all_scores[0], axis=0, keepdims=True)
         for scores in all_scores[1:]:
@@ -354,12 +367,8 @@
         position_row = tail_as_row(query_ref, part_rows + piece, pos_rows)
         all_scores, all_visible = [], []
         for ref in state_refs:
-            scores = dot(halves(ref[:slot_rows, :]), queries, 1, 1) * score_scale
-            bias = row_as_column(tail_as_row(ref, 2 * slot_rows, bias_rows), width)
-            scores = scores + jnp.concatenate([bias] * (part_rows // width), axis=1)
-            page_start = ref[packed_rows - 1 : packed_rows, 0:1]
-            visible = jnp.broadcast_to(position_row >= page_start, scores.shape)
-            all_scores.append(jnp.where(visible, scores, MASKED))
+            scores, visible = page_scores(ref, queries, position_row)
+            all_scores.append(scores)
             all_visible.append(visible)
         row_max = jnp.max(all_scores[0], axis=0, keepdims=True)
         for scores in all_scores[1:]:
@@ -389,6 +398,7 @@
         query_refs, refs = refs[:query_devices], refs[query_devices:]
         grad_refs, refs = refs[:2], refs[2:]
         tile_refs, refs = refs[: len(tiles)], refs[len(tiles) :]
+        refs[0][CORES * packed_rows :, :] = query_refs[0][...]
         state_outs, refs = parts_of(refs[:1]), refs[1:]
         chunk_outs, refs = refs[:ranks], refs[ranks:]
         sizes = step_sizes(tile_refs)
@@ -447,53 +457,70 @@
             merged_out,
         )
 
+    def page_gradients(weights, factor, state_ref, all_queries, residual, row_delta, out):
+        attention = weights * factor
+        grad_values = dot(halves(attention), residual, 1, 1)
+        grad_probs = dot(halves(state_ref[slot_rows : 2 * slot_rows, :]), residual, 1, 0)
+        grad_scores = halves(attention * (grad_probs - row_delta))
+        grad_keys = dot(grad_scores, all_queries, 1, 0) * score_scale
+        ones = jnp.ones((TAIL, query_rows), jnp.bfloat16)
+        grad_bias = dot((ones, jnp.zeros_like(ones)), grad_scores, 1, 1)[0:1, :]
+        grad_bias = row_as_tail(grad_bias, width)
+        out[:slot_rows, :] = grad_keys
+        out[slot_rows : 2 * slot_rows, :] = grad_values
+        out[2 * slot_rows :, :] = grad_bias
+        return grad_keys, grad_values, grad_bias
+
+    def split_merged(joined):
+        row_max, row_total, row_delta = (
+            joined[width + at : width + at + 1, :] for at in range(3)
+        )
+        return halves(joined[:width, :]), row_max, row_total, row_delta
+
+    def read_chunks(merged_refs, chunks):
+        rank, _, _ = places()
+        for turn, ref in enumerate(merged_refs):
+            chunks[rank ^ turn] = ref[...]
+        return [chunks[at] for at in range(ranks)]
+
+    def join_body(*refs):
+        *merged_refs, joined_out, chunks = refs
+        joined_out[...] = jnp.concatenate(read_chunks(merged_refs, chunks), axis=1)
+
     def backward_body(*refs):
         weights_refs, refs = refs[: len(weights)], refs[len(weights) :]
         max_refs, refs = refs[: len(weights)], refs[len(weights) :]
         state_refs, refs = parts_of(refs[: len(states)]), refs[len(states) :]
         query_refs, refs = refs[:query_devices], refs[query_devices:]
-        merged_refs, refs = refs[:ranks], refs[ranks:]
-        grad_outs, (squares_out, chunks) = refs[:2], refs[2:]
-        rank, _, _ = places()
-        for turn in range(ranks):
-            chunks[rank ^ turn] = merged_refs[turn][...]
-        if len(weights_refs) == 1:
-            joined = jnp.concatenate([chunks[at] for at in range(ranks)], axis=1)
+        merged_refs, refs = refs[: len(all_merged)], refs[len(all_merged) :]
+        grad_outs, (squares_out, *scratch) = refs[:2], refs[2:]
+        if len(states) < CORES:
+            joined = merged_refs[0][...]
             all_queries = read_queries(query_refs)
         else:
+            chunks = read_chunks(merged_refs, *scratch)
             joined = jnp.concatenate(
                 [
-                    chunks[at, :, part * piece : (part + 1) * piece]
+                    value[:, part * piece : (part + 1) * piece]
                     for part in range(query_devices)
-                    for at in range(ranks)
+                    for value in chunks
                 ],
                 axis=1,
             )
             all_queries = halves(
                 jnp.concatenate([ref[:part_rows, :] for ref in query_refs], axis=0)
             )
-        residual = joined[:width, :]
-        row_max, row_total, row_delta = (
-            joined[width + at : width + at + 1, :] for at in range(3)
-        )
-        residual = halves(residual)
+        residual, row_max, row_total, row_delta = split_merged(joined)
         maxima = jnp.concatenate([ref[0:1, :] for ref in max_refs], axis=1)
         factor = jnp.exp(maxima - row_max) / row_total
-        ones = jnp.ones((TAIL, query_rows), jnp.bfloat16)
-        ones = (ones, jnp.zeros_like(ones))
         squares = [jnp.zeros((1, width), jnp.float32)] * 3
         for at, (ref, out) in enumerate(zip(state_refs, grad_outs)):
             rows = slice(at * slot_rows, (at + 1) * slot_rows)
-            attention = jnp.concatenate([part[rows, :] for part in weights_refs], axis=1) * factor
-            grad_values = dot(halves(attention), residual, 1, 1)
-            grad_probs = dot(halves(ref[slot_rows : 2 * slot_rows, :]), residual, 1, 0)
-            grad_scores = halves(attention * (grad_probs - row_delta))
-            grad_keys = dot(grad_scores, all_queries, 1, 0) * score_scale
-            grad_bias = row_as_tail(dot(ones, grad_scores, 1, 1)[0:1, :], width)
-            out[:slot_rows, :] = grad_keys
-            out[slot_rows : 2 * slot_rows, :] = grad_values
-            out[2 * slot_rows :, :] = grad_bias
-            for which, grad in enumerate((grad_keys, grad_values, grad_bias)):
+            page_weights = jnp.concatenate([part[rows, :] for part in weights_refs], axis=1)
+            grads = page_gradients(
+                page_weights, factor, ref, all_queries, residual, row_delta, out
+            )
+            for which, grad in enumerate(grads):
                 squares[which] = squares[which] + jnp.sum(grad * grad, axis=0, keepdims=True)
         lanes = lax.broadcasted_iota(jnp.int32, (1, width), 1)
         row = jnp.zeros((1, width), jnp.float32)
@@ -502,29 +529,37 @@
         for at in range(devices):
             squares_out[at] = row
 
+    def page_body(turn, at):
+        def body(state_ref, joined_ref, *refs):
+            *pack_refs, grad_out = refs
+            query_refs = [state_ref.at[pl.ds(CORES * packed_rows, query_shape[0])]] + pack_refs
+            residual, row_max, row_total, row_delta = split_merged(joined_ref[...])
+            all_queries = read_queries(query_refs)
+            ref = part_of(state_ref, at)
+            scores, visible = page_scores(ref, all_queries, read_positions(query_refs))
+            weights = jnp.where(visible, jnp.exp(scores - row_max), 0.0)
+            page_gradients(
+                weights, 1.0 / row_total, ref, all_queries, residual, row_delta, grad_out
+            )
+
+        return body
+
     def mate_body(*refs):
         *state_refs, out_ref = refs
         for at, ref in enumerate(state_refs):
             out_ref[pl.ds(at * packed_rows, packed_rows), :] = part_of(ref, 1)[...]
 
-    out_masks = list(itertools.product(range(query_devices), range(CORES)))
-
-    def to_output(packs, mask):
-        if mask == (0, 0):
-            return packs[0]
-        return exchange(packs[mask[1]], page=mask[1], query=mask[0])
-
     for repeat in range(STEPS):
         last = repeat == STEPS - 1
         if repeat == 0:
             sums, weights, maxima = [], [], []
-            for query_part in query_parts:
+            for query_pack in query_parts:
                 *pieces, part_weights, part_max = call(
                     part_body,
                     part_shapes,
                     "forward",
                     2 * matmul_cost // query_devices,
-                    states + [query_part],
+                    states + [query_pack],
                     piece_scratch,
                     after=maxima[-1:],
                 )
@@ -538,7 +573,7 @@
         else:
             new_state, *chunk_parts, part_weights, part_max = call(
                 next_body,
-                [(CORES * packed_rows, width)] + forward_shapes,
+                [(CORES * packed_rows + query_shape[0], width)] + forward_shapes,
                 "update_forward",
                 2 * matmul_cost,
                 states + query_parts + grads + tiles,
@@ -563,32 +598,56 @@
         all_merged = [merged] + [
             exchange(merged, page=CORES * turn) for turn in range(1, ranks)
         ]
-        if repeat:
-            (for_mate,) = call(
-                mate_body,
-                [(query_devices * packed_rows, width)],
-                "mate_parts",
-                2**20,
-                new_states,
-                after=all_merged[1:],
+        if last:
+            all_merged = call(
+                join_body, [(width + TAIL, query_rows)], "join", 2**20, all_merged, chunk_scratch
             )
-            from_mate = exchange(for_mate, page=1)
+            all_joined = [
+                to_device(all_merged[0], query=turn) for turn in range(query_devices)
+            ]
         own_grad, mate_grad, squares = call(
             backward_body,
             packed_shapes + [(devices, 1, width)],
             "backward",
             3 * matmul_cost,
-            weights + maxima + states + query_parts + all_merged,
-            scratch=chunk_scratch,
+            weights + maxima + states + query_parts + list(all_merged),
+            scratch=() if last else chunk_scratch,
         )
         grads = [own_grad, mate_grad]
-        if last:
-            all_grads = [to_output(grads, mask) for mask in out_masks]
         tiles = [
             lax.all_to_all(
                 squares, ("page", "query", "head"), split_axis=0, concat_axis=0, tiled=True
             )
         ]
+
+    (for_mate,) = call(
+        mate_body,
+        [(query_devices * packed_rows, width)],
+        "mate_parts",
+        2**20,
+        new_states,
+        after=tiles,
+    )
+    from_mate = exchange(for_mate, page=1)
+    all_grads = [own_grad, exchange(mate_grad, page=1)]
+    for turn in range(1, query_devices):
+        parts = [
+            packs[part] if part == turn else query_part(turn, part)
+            for part in range(1, query_devices)
+        ]
+        page_grads = [
+            call(
+                page_body(turn, at),
+                packed_shapes[:1],
+                "other_backward",
+                3 * matmul_cost // 2,
+                [new_states[turn], all_joined[turn]] + parts,
+                after=tiles,
+            )[0]
+            for at in reversed(range(CORES))
+        ]
+        all_grads += [page_grads[1], exchange(page_grads[0], page=1)]
+    out_masks = list(itertools.product(range(query_devices), range(CORES)))
 
     def last_body(*refs):
         state_refs, (mate_ref, *refs) = refs[:query_devices], refs[query_devices:]

time: 79.9 us -> 80 us (level)
  Pallas kernels: 12 us -> 14.9 us
  blocking collectives: 23.6 us -> 20.9 us
    pallas_call x11 -> x14, Pallas kernels: 12 us -> 14.9 us  [call(): pl.pallas_call(without_after, out_shape=[jax.ShapeDtypeStruct(shape, jnp....]
    all_to_all x2, blocking collectives: 23.6 us -> 20.9 us  [direct_per_device(): lax.all_to_all(squares, ('page', 'query', 'head'), split_axis=0, concat_a...]
  transfers between devices with their start and end apart: 22 -> 22, of which waited for: 8 -> 9; matrix products, arithmetic and copies ran while one was open for 0% -> 0% of each run, Pallas kernels for 6% -> 10%
where the time goes in v17:
time: 80 us; the launch traced here: 79.8 us
  starting transfers between devices  27.7 us (35%)
  blocking collectives  20.9 us (26%)
  waiting for transfers between devices  15.2 us (19%)
  Pallas kernels  14.9 us (19%)
  between operations  0.86 us (1%)
    ppermute x22, starting transfers between devices, exchange(): return lax.ppermute(value, axes, pairs)  27.7 us
    all_to_all x2, blocking collectives, direct_per_device(): lax.all_to_all(squares, ('page', 'query', 'head'), split_axis=0, concat_a...  20.9 us
    ppermute x22, waiting for transfers between devices, exchange(): return lax.ppermute(value, axes, pairs)  15.2 us
    pallas_call x14, Pallas kernels, call(): pl.pallas_call(without_after, out_shape=[jax.ShapeDtypeStruct(shape, jnp....  14.9 us
  transfers between devices with their start and end apart: 22, of which 9 were waited for; matrix products, arithmetic and copies ran while one was open for 0% of the time, Pallas kernels for 10%

profile of v17, /device:TPU:0, one launch (start us, length us, event | category | flops | bytes accessed | tf_op | source)
XLA Modules:
  0.0 79.8 jit_solution(2372707707814064505)
XLA Ops:
  0.7 2.0 %pack.1 = (f32[520,128]{1,0:T(8,128)}, f32[328,128]{1,0:T(8,128)}) custom-call(f32[4,256,128]{2,1,0:T(8,128)} %refs_0_.3, f32[4,256,128]{2,1,0:T(8,128)} %refs_1_.3, f32[4,256,128]{2,1,0:T(8,128)} %refs_2_.3, f32[4,256]{1,0:T(4,128)} %refs_3_.3, f32[4,256,128]{2,1,0:T(8,128)} %refs_4_.3, s32[4,256]{1,0:T(4,128)} %refs_5_.3, s32[8]{0:T(128)} %refs_6_.3), custom_call_target="tpu_custom_call" | custom-call | flops 1048576 | bytes 1048576 | tf_op jit(solution)/shard_map/pack/pallas_call | solution.py:67
  2.7 0.0 copy-start.7
  2.7 0.5 collective-permute-start
  3.3 2.6 %collective-permute-start.1 = (f32[328,128]{1,0:T(8,128)}, f32[328,128]{1,0:T(8,128)S(1)}, u32[]{:S(2)}, u32[]{:S(2)}) collective-permute-start(f32[328,128]{1,0:T(8,128)} %get-tuple-element.35.refs_2_), channel_id=1, source_target_pairs={{0,2},{2,0},{1,3},{3,1},{4,6},{6,4},{5,7},{7,5},{8,10},{10,8},{9,1... | collective-permute-start | bytes 503816 | tf_op jit(solution)/shard_map/ppermute | solution.py:39
  5.9 0.7 own.1
  6.6 0.0 collective-permute-done.refs_1_.refs_5_
  6.6 1.0 %forward.2 = (f32[72,128]{1,0:T(8,128)S(1)}, f32[72,128]{1,0:T(8,128)S(1)}, f32[72,128]{1,0:T(8,128)S(1)}, f32[72,128]{1,0:T(8,128)S(1)}, f32[512,256]{1,0:T(8,128)S(1)}, /*index=5*/f32[8,256]{1,0:T(8,128)S(1)}) custom-call(f32[520,128]{1,0:T(8,128)S(1)} %get-tuple-element.32.refs_0_.refs_4_, f32[520,128]{1,0:T(8,128)S(1)} %collective-permute-done.refs_1_.refs_5_, ...), custom_call_target="tpu_custom_call" | custom-call | flops 201326592 | bytes 1048576 | tf_op jit(solution)/shard_map/forward/pallas_call | solution.py:67
  7.6 3.7 %collective-permute-start.2 = (f32[72,128]{1,0:T(8,128)S(1)}, f32[72,128]{1,0:T(8,128)S(1)}, u32[]{:S(2)}, u32[]{:S(2)}) collective-permute-start(f32[72,128]{1,0:T(8,128)S(1)} %get-tuple-element.40), channel_id=1, source_target_pairs={{0,24},{4,28},{8,16},{12,20},{16,8},{20,12},{24,0},{28,4},{1,25},{... | collective-permute-start | bytes 110600 | tf_op jit(solution)/shard_map/ppermute | solution.py:39
  11.3 0.0 collective-permute-start.3
  11.3 0.8 collective-permute-start.4
  12.0 0.0 collective-permute-done.1.refs_2_.refs_1_.refs_7_.refs_3_.refs_4_
  12.0 1.0 %forward.3 = (f32[72,128]{1,0:T(8,128)S(1)}, f32[72,128]{1,0:T(8,128)S(1)}, f32[72,128]{1,0:T(8,128)S(1)}, f32[72,128]{1,0:T(8,128)S(1)}, f32[512,256]{1,0:T(8,128)S(1)}, /*index=5*/f32[8,256]{1,0:T(8,128)S(1)}) custom-call(f32[520,128]{1,0:T(8,128)S(1)} %get-tuple-element.32.refs_0_.refs_4_, f32[520,128]{1,0:T(8,128)S(1)} %collective-permute-done.refs_1_.refs_5_, ...), custom_call_target="tpu_custom_call" | custom-call | flops 201326592 | bytes 1048576 | tf_op jit(solution)/shard_map/forward/pallas_call | solution.py:67
  13.1 3.7 %collective-permute-start.5 = (f32[72,128]{1,0:T(8,128)S(1)}, f32[72,128]{1,0:T(8,128)S(1)}, u32[]{:S(2)}, u32[]{:S(2)}) collective-permute-start(f32[72,128]{1,0:T(8,128)S(1)} %get-tuple-element.44), channel_id=1, source_target_pairs={{0,24},{4,28},{8,16},{12,20},{16,8},{20,12},{24,0},{28,4},{1,25},{... | collective-permute-start | bytes 110600 | tf_op jit(solution)/shard_map/ppermute | solution.py:39
  16.7 0.8 collective-permute-start.7
  17.5 1.5 %collective-permute-done.5.refs_6_ = f32[72,128]{1,0:T(8,128)S(1)} collective-permute-done((f32[72,128]{1,0:T(8,128)S(1)}, f32[72,128]{1,0:T(8,128)S(1)}, u32[]{:S(2)}, u32[]{:S(2)}) %collective-permute-start.5) | collective-permute-done | bytes 36896 | tf_op jit(solution)/shard_map/ppermute | solution.py:39
  19.0 2.6 %collective-permute-done.6.refs_7_ = f32[72,128]{1,0:T(8,128)S(1)} collective-permute-done((f32[72,128]{1,0:T(8,128)S(1)}, f32[72,128]{1,0:T(8,128)S(1)}, u32[]{:S(2)}, u32[]{:S(2)}) %collective-permute-start.6) | collective-permute-done | bytes 36896 | tf_op jit(solution)/shard_map/ppermute | solution.py:39
  21.6 0.3 merge.2.refs_8_
  21.9 1.5 %collective-permute-start.10 = (f32[136,128]{1,0:T(8,128)S(1)}, f32[136,128]{1,0:T(8,128)S(1)}, u32[]{:S(2)}, u32[]{:S(2)}) collective-permute-start(f32[136,128]{1,0:T(8,128)S(1)} %merge.2.refs_8_), channel_id=1, source_target_pairs={{0,24},{4,28},{8,16},{12,20},{16,8},{20,12},{24,0},{28,4},{1,25},{... | collective-permute-start | bytes 208904 | tf_op jit(solution)/shard_map/ppermute | solution.py:39
  23.4 0.6 collective-permute-start.9
  24.0 2.3 %collective-permute-start.8 = (f32[136,128]{1,0:T(8,128)S(1)}, f32[136,128]{1,0:T(8,128)S(1)}, u32[]{:S(2)}, u32[]{:S(2)}) collective-permute-start(f32[136,128]{1,0:T(8,128)S(1)} %merge.2.refs_8_), channel_id=1, source_target_pairs={{0,8},{4,12},{8,0},{12,4},{16,24},{20,28},{24,16},{28,20},{1,9},{5... | collective-permute-start | bytes 208904 | tf_op jit(solution)/shard_map/ppermute | solution.py:39
  26.3 1.8 %collective-permute-done.10.refs_11_ = f32[136,128]{1,0:T(8,128)S(1)} collective-permute-done((f32[136,128]{1,0:T(8,128)S(1)}, f32[136,128]{1,0:T(8,128)S(1)}, u32[]{:S(2)}, u32[]{:S(2)}) %collective-permute-start.10) | collective-permute-done | bytes 69664 | tf_op jit(solution)/shard_map/ppermute | solution.py:39
  28.1 1.5 %collective-permute-done.9.refs_10_ = f32[136,128]{1,0:T(8,128)S(1)} collective-permute-done((f32[136,128]{1,0:T(8,128)S(1)}, f32[136,128]{1,0:T(8,128)S(1)}, u32[]{:S(2)}, u32[]{:S(2)}) %collective-permute-start.9) | collective-permute-done | bytes 69664 | tf_op jit(solution)/shard_map/ppermute | solution.py:39
  29.5 2.3 %backward.2 = (f32[520,128]{1,0:T(8,128)S(1)}, f32[520,128]{1,0:T(8,128)S(1)}, f32[32,1,128]{2,1,0:T(1,128)S(1)}) custom-call(f32[512,256]{1,0:T(8,128)S(1)} %get-tuple-element.36.refs_0_, f32[512,256]{1,0:T(8,128)S(1)} %get-tuple-element.38.refs_1_, f32[8,256]{1,0:T(8,128)S(1)} %get-tuple-element.37.refs_3_.refs_2_, ...), custom_call_target="tpu_custom_call" | custom-call | flops 603979776 | bytes 1048576 | tf_op jit(solution)/shard_map/backward/pallas_call | solution.py:67
  31.8 11.1 %all_to_all.10.refs_6_ = f32[32,1,128]{2,1,0:T(1,128)S(1)} all-to-all(f32[32,1,128]{2,1,0:T(1,128)S(1)} %get-tuple-element.50), channel_id=1, replica_groups=mesh['page'=8,'query'=2,'head'=2] {'page','query','head'}, dimensions={0} | all-to-all | bytes 32768 | tf_op jit(solution)/shard_map/all_to_all | solution.py:618
  42.9 1.3 %update_forward.1 = (f32[1368,128]{1,0:T(8,128)S(1)}, f32[136,128]{1,0:T(8,128)S(1)}, f32[136,128]{1,0:T(8,128)S(1)}, f32[136,128]{1,0:T(8,128)S(1)}, f32[136,12...) custom-call(f32[520,128]{1,0:T(8,128)S(1)} %get-tuple-element.32.refs_0_.refs_4_, ...), custom_call_target="tpu_custom_call" | custom-call | flops 402653184 | bytes 1048576 | tf_op jit(solution)/shard_map/update_forward/pallas_call | solution.py:67
  44.2 0.6 collective-permute-start.11
  44.8 0.6 collective-permute-start.12
  45.3 1.5 %collective-permute-start.13 = (f32[136,128]{1,0:T(8,128)S(1)}, f32[136,128]{1,0:T(8,128)S(1)}, u32[]{:S(2)}, u32[]{:S(2)}) collective-permute-start(f32[136,128]{1,0:T(8,128)S(1)} %get-tuple-element.56), channel_id=1, source_target_pairs={{0,16},{4,20},{8,24},{12,28},{16,0},{20,4},{24,8},{28,12},{1,17},{... | collective-permute-start | bytes 208904 | tf_op jit(solution)/shard_map/ppermute | solution.py:39
  46.8 2.3 %collective-permute-start.14 = (f32[136,128]{1,0:T(8,128)S(1)}, f32[136,128]{1,0:T(8,128)S(1)}, u32[]{:S(2)}, u32[]{:S(2)}) collective-permute-start(f32[136,128]{1,0:T(8,128)S(1)} %get-tuple-element.57), channel_id=1, source_target_pairs={{0,8},{4,12},{8,0},{12,4},{16,24},{20,28},{24,16},{28,20},{1,9},{5... | collective-permute-start | bytes 208904 | tf_op jit(solution)/shard_map/ppermute | solution.py:39
  49.1 2.5 %collective-permute-done.12.refs_3_ = f32[136,128]{1,0:T(8,128)S(1)} collective-permute-done((f32[136,128]{1,0:T(8,128)S(1)}, f32[136,128]{1,0:T(8,128)S(1)}, u32[]{:S(2)}, u32[]{:S(2)}) %collective-permute-start.12) | collective-permute-done | bytes 69664 | tf_op jit(solution)/shard_map/ppermute | solution.py:39
  51.7 1.7 %collective-permute-done.13.refs_4_ = f32[136,128]{1,0:T(8,128)S(1)} collective-permute-done((f32[136,128]{1,0:T(8,128)S(1)}, f32[136,128]{1,0:T(8,128)S(1)}, u32[]{:S(2)}, u32[]{:S(2)}) %collective-permute-start.13) | collective-permute-done | bytes 69664 | tf_op jit(solution)/shard_map/ppermute | solution.py:39
  53.3 0.1 merge.3.refs_0_
  53.4 1.2 %collective-permute-start.17 = (f32[136,128]{1,0:T(8,128)S(1)}, f32[136,128]{1,0:T(8,128)S(1)}, u32[]{:S(2)}, u32[]{:S(2)}) collective-permute-start(f32[136,128]{1,0:T(8,128)S(1)} %merge.3.refs_0_), channel_id=1, source_target_pairs={{0,24},{4,28},{8,16},{12,20},{16,8},{20,12},{24,0},{28,4},{1,25},{... | collective-permute-start | bytes 208904 | tf_op jit(solution)/shard_map/ppermute | solution.py:39
  54.7 0.4 collective-permute-start.16
  55.1 2.8 %collective-permute-start.15 = (f32[136,128]{1,0:T(8,128)S(1)}, f32[136,128]{1,0:T(8,128)S(1)}, u32[]{:S(2)}, u32[]{:S(2)}) collective-permute-start(f32[136,128]{1,0:T(8,128)S(1)} %merge.3.refs_0_), channel_id=1, source_target_pairs={{0,8},{4,12},{8,0},{12,4},{16,24},{20,28},{24,16},{28,20},{1,9},{5... | collective-permute-start | bytes 208904 | tf_op jit(solution)/shard_map/ppermute | solution.py:39
  57.9 2.4 %collective-permute-done.17.refs_3_ = f32[136,128]{1,0:T(8,128)S(1)} collective-permute-done((f32[136,128]{1,0:T(8,128)S(1)}, f32[136,128]{1,0:T(8,128)S(1)}, u32[]{:S(2)}, u32[]{:S(2)}) %collective-permute-start.17) | collective-permute-done | bytes 69664 | tf_op jit(solution)/shard_map/ppermute | solution.py:39
  60.3 1.1 %collective-permute-done.16.refs_2_ = f32[136,128]{1,0:T(8,128)S(1)} collective-permute-done((f32[136,128]{1,0:T(8,128)S(1)}, f32[136,128]{1,0:T(8,128)S(1)}, u32[]{:S(2)}, u32[]{:S(2)}) %collective-permute-start.16) | collective-permute-done | bytes 69664 | tf_op jit(solution)/shard_map/ppermute | solution.py:39
  61.5 0.1 join.1.refs_5_
  61.5 1.2 %collective-permute-start.20 = (f32[136,512]{1,0:T(8,128)S(1)}, f32[136,512]{1,0:T(8,128)S(1)}, u32[]{:S(2)}, u32[]{:S(2)}) collective-permute-start(f32[136,512]{1,0:T(8,128)S(1)} %join.1.refs_5_), channel_id=1, source_target_pairs={{0,2},{2,0},{1,3},{3,1},{4,6},{6,4},{5,7},{7,5},{8,10},{10,8},{9,1... | collective-permute-start | bytes 835592 | tf_op jit(solution)/shard_map/ppermute | solution.py:39
  62.7 2.1 %backward.3 = (f32[520,128]{1,0:T(8,128)S(1)}, f32[520,128]{1,0:T(8,128)S(1)}, f32[32,1,128]{2,1,0:T(1,128)S(1)}) custom-call(f32[512,512]{1,0:T(8,128)S(1)} %get-tuple-element.52.refs_0_, f32[8,512]{1,0:T(8,128)S(1)} %get-tuple-element.53.refs_1_, f32[1368,128]{1,0:T(8,128)S(1)} %get-tuple-element.51.refs_2_.refs_0_, ...), custom_call_target="tpu_custom_call" | custom-call | flops 603979776 | bytes 1048576 | tf_op jit(solution)/shard_map/backward/pallas_call | solution.py:67
  64.9 9.9 %all_to_all.11.refs_2_.refs_3_.refs_7_ = f32[32,1,128]{2,1,0:T(1,128)S(1)} all-to-all(f32[32,1,128]{2,1,0:T(1,128)S(1)} %get-tuple-element.58), channel_id=1, replica_groups=mesh['page'=8,'query'=2,'head'=2] {'page','query','head'}, dimensions={0} | all-to-all | bytes 32768 | tf_op jit(solution)/shard_map/all_to_all | solution.py:618
  74.8 0.1 collective-permute-start.18
  74.9 0.5 collective-permute-start.19
  75.4 0.3 copy-done.4
  75.7 1.4 %other_backward.3 = f32[520,128]{1,0:T(8,128)S(1)} custom-call(f32[1368,128]{1,0:T(8,128)S(1)} %collective-permute-done.11.refs_1_.refs_0_, f32[136,512]{1,0:T(8,128)S(1)} %collective-permute-done.20.refs_1_, f32[328,128]{1,0:T(8,128)S(1)} %copy-done.4, f32[32,1,128]{2,1,0:T(1,128)S(1)} %all_to_all.11.refs_2_.refs_3_.refs_7_), custom_call_target="tpu_custom_call" | custom-call | flops 301989888 | bytes 1048576 | tf_op jit(solution)/shard_map/other_backward/pallas_call | solution.py:67
  77.1 1.4 %other_backward.2.refs_5_ = f32[520,128]{1,0:T(8,128)S(1)} custom-call(f32[1368,128]{1,0:T(8,128)S(1)} %collective-permute-done.11.refs_1_.refs_0_, f32[136,512]{1,0:T(8,128)S(1)} %collective-permute-done.20.refs_1_, f32[328,128]{1,0:T(8,128)S(1)} %copy-done.4, f32[32,1,128]{2,1,0:T(1,128)S(1)} %all_to_all.11.refs_2_.refs_3_.refs_7_), custom_call_target="tpu_custom_call" | custom-call | flops 301989888 | bytes 1048576 | tf_op jit(solution)/shard_map/other_backward/pallas_call | solution.py:67
  78.5 0.1 collective-permute-done.21.refs_6_
  78.7 1.2 %last_update.1 = (f32[4,256,128]{2,1,0:T(8,128)}, f32[4,256,128]{2,1,0:T(8,128)}, f32[4,256]{1,0:T(4,128)}) custom-call(f32[1368,128]{1,0:T(8,128)S(1)} %get-tuple-element.51.refs_2_.refs_0_, f32[1368,128]{1,0:T(8,128)S(1)} %collective-permute-done.11.refs_1_.refs_0_, f32[1040,128]{1,0:T(8,128)S(1)} %collective-permute-done.18.refs_2_, ...), custom_call_target="tpu_custom_call" | custom-call | flops 1048576 | bytes 1048576 | tf_op jit(solution)/shard_map/last_update/pallas_call | solution.py:67
  (28 shorter events, 0.1 us)
Async XLA Ops:
  0.6 5.2 %copy-start.3 = (f32[4,256,128]{2,1,0:T(8,128)S(1)}, f32[4,256,128]{2,1,0:T(8,128)}, u32[]{:S(2)}) copy-start(f32[4,256,128]{2,1,0:T(8,128)} %refs_4_.3) | copy-start | bytes 1572868
  0.6 5.2 %copy-start.2 = (f32[4,256,128]{2,1,0:T(8,128)S(1)}, f32[4,256,128]{2,1,0:T(8,128)}, u32[]{:S(2)}) copy-start(f32[4,256,128]{2,1,0:T(8,128)} %refs_2_.3) | copy-start | bytes 1572868
  0.7 5.2 %copy-start.1 = (f32[4,256,128]{2,1,0:T(8,128)S(1)}, f32[4,256,128]{2,1,0:T(8,128)}, u32[]{:S(2)}) copy-start(f32[4,256,128]{2,1,0:T(8,128)} %refs_1_.3) | copy-start | bytes 1572868
  0.7 5.2 %copy-start = (f32[4,256,128]{2,1,0:T(8,128)S(1)}, f32[4,256,128]{2,1,0:T(8,128)}, u32[]{:S(2)}) copy-start(f32[4,256,128]{2,1,0:T(8,128)} %refs_0_.3) | copy-start | bytes 1572868
  0.7 5.2 %copy-start.5 = (f32[4,256]{1,0:T(4,128)S(1)}, f32[4,256]{1,0:T(4,128)}, u32[]{:S(2)}) copy-start(f32[4,256]{1,0:T(4,128)} %refs_3_.3) | copy-start | bytes 12292
  0.7 5.2 %copy-start.6 = (s32[4,256]{1,0:T(4,128)S(1)}, s32[4,256]{1,0:T(4,128)}, u32[]{:S(2)}) copy-start(s32[4,256]{1,0:T(4,128)} %refs_5_.3) | copy-start | bytes 12292
  2.7 3.2 %copy-start.7 = (s32[8]{0:T(128)S(1)}, s32[8]{0:T(128)}, u32[]{:S(2)}) copy-start(s32[8]{0:T(128)} %refs_6_.3) | copy-start | bytes 100
  2.7 3.8 %collective-permute-start = (f32[520,128]{1,0:T(8,128)}, f32[520,128]{1,0:T(8,128)S(1)}, u32[]{:S(2)}, u32[]{:S(2)}) collective-permute-start(f32[520,128]{1,0:T(8,128)} %get-tuple-element.33), channel_id=1, source_target_pairs={{0,4},{4,0},{8,12},{12,8},{16,20},{20,16},{24,28},{28,24},{1,5},{5... | collective-permute-start | bytes 798728 | tf_op jit(solution)/shard_map/ppermute | solution.py:39
  3.3 8.8 %collective-permute-start.1 = (f32[328,128]{1,0:T(8,128)}, f32[328,128]{1,0:T(8,128)S(1)}, u32[]{:S(2)}, u32[]{:S(2)}) collective-permute-start(f32[328,128]{1,0:T(8,128)} %get-tuple-element.35.refs_2_), channel_id=1, source_target_pairs={{0,2},{2,0},{1,3},{3,1},{4,6},{6,4},{5,7},{7,5},{8,10},{10,8},{9,1... | collective-permute-start | bytes 503816 | tf_op jit(solution)/shard_map/ppermute | solution.py:39
  7.6 9.2 %collective-permute-start.2 = (f32[72,128]{1,0:T(8,128)S(1)}, f32[72,128]{1,0:T(8,128)S(1)}, u32[]{:S(2)}, u32[]{:S(2)}) collective-permute-start(f32[72,128]{1,0:T(8,128)S(1)} %get-tuple-element.40), channel_id=1, source_target_pairs={{0,24},{4,28},{8,16},{12,20},{16,8},{20,12},{24,0},{28,4},{1,25},{... | collective-permute-start | bytes 110600 | tf_op jit(solution)/shard_map/ppermute | solution.py:39
  11.3 6.3 %collective-permute-start.3 = (f32[72,128]{1,0:T(8,128)S(1)}, f32[72,128]{1,0:T(8,128)S(1)}, u32[]{:S(2)}, u32[]{:S(2)}) collective-permute-start(f32[72,128]{1,0:T(8,128)S(1)} %get-tuple-element.41), channel_id=1, source_target_pairs={{0,16},{4,20},{8,24},{12,28},{16,0},{20,4},{24,8},{28,12},{1,17},{... | collective-permute-start | bytes 110600 | tf_op jit(solution)/shard_map/ppermute | solution.py:39
  11.3 6.3 %collective-permute-start.4 = (f32[72,128]{1,0:T(8,128)S(1)}, f32[72,128]{1,0:T(8,128)S(1)}, u32[]{:S(2)}, u32[]{:S(2)}) collective-permute-start(f32[72,128]{1,0:T(8,128)S(1)} %get-tuple-element.42), channel_id=1, source_target_pairs={{0,8},{4,12},{8,0},{12,4},{16,24},{20,28},{24,16},{28,20},{1,9},{5... | collective-permute-start | bytes 110600 | tf_op jit(solution)/shard_map/ppermute | solution.py:39
  13.1 5.9 %collective-permute-start.5 = (f32[72,128]{1,0:T(8,128)S(1)}, f32[72,128]{1,0:T(8,128)S(1)}, u32[]{:S(2)}, u32[]{:S(2)}) collective-permute-start(f32[72,128]{1,0:T(8,128)S(1)} %get-tuple-element.44), channel_id=1, source_target_pairs={{0,24},{4,28},{8,16},{12,20},{16,8},{20,12},{24,0},{28,4},{1,25},{... | collective-permute-start | bytes 110600 | tf_op jit(solution)/shard_map/ppermute | solution.py:39
  16.7 4.9 %collective-permute-start.6 = (f32[72,128]{1,0:T(8,128)S(1)}, f32[72,128]{1,0:T(8,128)S(1)}, u32[]{:S(2)}, u32[]{:S(2)}) collective-permute-start(f32[72,128]{1,0:T(8,128)S(1)} %get-tuple-element.45), channel_id=1, source_target_pairs={{0,16},{4,20},{8,24},{12,28},{16,0},{20,4},{24,8},{28,12},{1,17},{... | collective-permute-start | bytes 110600 | tf_op jit(solution)/shard_map/ppermute | solution.py:39
  16.7 4.9 %collective-permute-start.7 = (f32[72,128]{1,0:T(8,128)S(1)}, f32[72,128]{1,0:T(8,128)S(1)}, u32[]{:S(2)}, u32[]{:S(2)}) collective-permute-start(f32[72,128]{1,0:T(8,128)S(1)} %get-tuple-element.46), channel_id=1, source_target_pairs={{0,8},{4,12},{8,0},{12,4},{16,24},{20,28},{24,16},{28,20},{1,9},{5... | collective-permute-start | bytes 110600 | tf_op jit(solution)/shard_map/ppermute | solution.py:39
  21.9 6.2 %collective-permute-start.10 = (f32[136,128]{1,0:T(8,128)S(1)}, f32[136,128]{1,0:T(8,128)S(1)}, u32[]{:S(2)}, u32[]{:S(2)}) collective-permute-start(f32[136,128]{1,0:T(8,128)S(1)} %merge.2.refs_8_), channel_id=1, source_target_pairs={{0,24},{4,28},{8,16},{12,20},{16,8},{20,12},{24,0},{28,4},{1,25},{... | collective-permute-start | bytes 208904 | tf_op jit(solution)/shard_map/ppermute | solution.py:39
  23.4 6.1 %collective-permute-start.9 = (f32[136,128]{1,0:T(8,128)S(1)}, f32[136,128]{1,0:T(8,128)S(1)}, u32[]{:S(2)}, u32[]{:S(2)}) collective-permute-start(f32[136,128]{1,0:T(8,128)S(1)} %merge.2.refs_8_), channel_id=1, source_target_pairs={{0,16},{4,20},{8,24},{12,28},{16,0},{20,4},{24,8},{28,12},{1,17},{... | collective-permute-start | bytes 208904 | tf_op jit(solution)/shard_map/ppermute | solution.py:39
  24.0 5.5 %collective-permute-start.8 = (f32[136,128]{1,0:T(8,128)S(1)}, f32[136,128]{1,0:T(8,128)S(1)}, u32[]{:S(2)}, u32[]{:S(2)}) collective-permute-start(f32[136,128]{1,0:T(8,128)S(1)} %merge.2.refs_8_), channel_id=1, source_target_pairs={{0,8},{4,12},{8,0},{12,4},{16,24},{20,28},{24,16},{28,20},{1,9},{5... | collective-permute-start | bytes 208904 | tf_op jit(solution)/shard_map/ppermute | solution.py:39
  44.2 30.6 %collective-permute-start.11 = (f32[1368,128]{1,0:T(8,128)S(1)}, f32[1368,128]{1,0:T(8,128)S(1)}, u32[]{:S(2)}, u32[]{:S(2)}) collective-permute-start(f32[1368,128]{1,0:T(8,128)S(1)} %get-tuple-element.51.refs_2_.refs_0_), channel_id=1, source_target_pairs={{0,2},{2,0},{1,3},{3,1},{4,6},{6,4},{5,7},{7,5},{8,10},{10,8},{9,1... | collective-permute-start | bytes 2101256 | tf_op jit(solution)/shard_map/ppermute | solution.py:39
  44.8 6.9 %collective-permute-start.12 = (f32[136,128]{1,0:T(8,128)S(1)}, f32[136,128]{1,0:T(8,128)S(1)}, u32[]{:S(2)}, u32[]{:S(2)}) collective-permute-start(f32[136,128]{1,0:T(8,128)S(1)} %get-tuple-element.55), channel_id=1, source_target_pairs={{0,24},{4,28},{8,16},{12,20},{16,8},{20,12},{24,0},{28,4},{1,25},{... | collective-permute-start | bytes 208904 | tf_op jit(solution)/shard_map/ppermute | solution.py:39
  45.3 8.0 %collective-permute-start.13 = (f32[136,128]{1,0:T(8,128)S(1)}, f32[136,128]{1,0:T(8,128)S(1)}, u32[]{:S(2)}, u32[]{:S(2)}) collective-permute-start(f32[136,128]{1,0:T(8,128)S(1)} %get-tuple-element.56), channel_id=1, source_target_pairs={{0,16},{4,20},{8,24},{12,28},{16,0},{20,4},{24,8},{28,12},{1,17},{... | collective-permute-start | bytes 208904 | tf_op jit(solution)/shard_map/ppermute | solution.py:39
  46.8 6.5 %collective-permute-start.14 = (f32[136,128]{1,0:T(8,128)S(1)}, f32[136,128]{1,0:T(8,128)S(1)}, u32[]{:S(2)}, u32[]{:S(2)}) collective-permute-start(f32[136,128]{1,0:T(8,128)S(1)} %get-tuple-element.57), channel_id=1, source_target_pairs={{0,8},{4,12},{8,0},{12,4},{16,24},{20,28},{24,16},{28,20},{1,9},{5... | collective-permute-start | bytes 208904 | tf_op jit(solution)/shard_map/ppermute | solution.py:39
  53.4 6.9 %collective-permute-start.17 = (f32[136,128]{1,0:T(8,128)S(1)}, f32[136,128]{1,0:T(8,128)S(1)}, u32[]{:S(2)}, u32[]{:S(2)}) collective-permute-start(f32[136,128]{1,0:T(8,128)S(1)} %merge.3.refs_0_), channel_id=1, source_target_pairs={{0,24},{4,28},{8,16},{12,20},{16,8},{20,12},{24,0},{28,4},{1,25},{... | collective-permute-start | bytes 208904 | tf_op jit(solution)/shard_map/ppermute | solution.py:39
  54.7 6.8 %collective-permute-start.16 = (f32[136,128]{1,0:T(8,128)S(1)}, f32[136,128]{1,0:T(8,128)S(1)}, u32[]{:S(2)}, u32[]{:S(2)}) collective-permute-start(f32[136,128]{1,0:T(8,128)S(1)} %merge.3.refs_0_), channel_id=1, source_target_pairs={{0,16},{4,20},{8,24},{12,28},{16,0},{20,4},{24,8},{28,12},{1,17},{... | collective-permute-start | bytes 208904 | tf_op jit(solution)/shard_map/ppermute | solution.py:39
  55.1 6.4 %collective-permute-start.15 = (f32[136,128]{1,0:T(8,128)S(1)}, f32[136,128]{1,0:T(8,128)S(1)}, u32[]{:S(2)}, u32[]{:S(2)}) collective-permute-start(f32[136,128]{1,0:T(8,128)S(1)} %merge.3.refs_0_), channel_id=1, source_target_pairs={{0,8},{4,12},{8,0},{12,4},{16,24},{20,28},{24,16},{28,20},{1,9},{5... | collective-permute-start | bytes 208904 | tf_op jit(solution)/shard_map/ppermute | solution.py:39
  61.5 13.8 %collective-permute-start.20 = (f32[136,512]{1,0:T(8,128)S(1)}, f32[136,512]{1,0:T(8,128)S(1)}, u32[]{:S(2)}, u32[]{:S(2)}) collective-permute-start(f32[136,512]{1,0:T(8,128)S(1)} %join.1.refs_5_), channel_id=1, source_target_pairs={{0,2},{2,0},{1,3},{3,1},{4,6},{6,4},{5,7},{7,5},{8,10},{10,8},{9,1... | collective-permute-start | bytes 835592 | tf_op jit(solution)/shard_map/ppermute | solution.py:39
  74.8 0.9 %copy-start.4 = (f32[328,128]{1,0:T(8,128)S(1)}, f32[328,128]{1,0:T(8,128)}, u32[]{:S(2)}) copy-start(f32[328,128]{1,0:T(8,128)} %get-tuple-element.35.refs_2_) | copy-start | bytes 503812
  74.8 3.8 %collective-permute-start.18 = (f32[1040,128]{1,0:T(8,128)S(1)}, f32[1040,128]{1,0:T(8,128)S(1)}, u32[]{:S(2)}, u32[]{:S(2)}) collective-permute-start(f32[1040,128]{1,0:T(8,128)S(1)} %mate_parts.1), channel_id=1, source_target_pairs={{0,4},{4,0},{8,12},{12,8},{16,20},{20,16},{24,28},{28,24},{1,5},{5... | collective-permute-start | bytes 1597448 | tf_op jit(solution)/shard_map/ppermute | solution.py:39
  74.9 3.6 %collective-permute-start.19 = (f32[520,128]{1,0:T(8,128)S(1)}, f32[520,128]{1,0:T(8,128)S(1)}, u32[]{:S(2)}, u32[]{:S(2)}) collective-permute-start(f32[520,128]{1,0:T(8,128)S(1)} %get-tuple-element.60), channel_id=1, source_target_pairs={{0,4},{4,0},{8,12},{12,8},{16,20},{20,16},{24,28},{28,24},{1,5},{5... | collective-permute-start | bytes 798728 | tf_op jit(solution)/shard_map/ppermute | solution.py:39
  77.1 1.6 %collective-permute-start.21 = (f32[520,128]{1,0:T(8,128)S(1)}, f32[520,128]{1,0:T(8,128)S(1)}, u32[]{:S(2)}, u32[]{:S(2)}) collective-permute-start(f32[520,128]{1,0:T(8,128)S(1)} %other_backward.3), channel_id=1, source_target_pairs={{0,4},{4,0},{8,12},{12,8},{16,20},{20,16},{24,28},{28,24},{1,5},{5... | collective-permute-start | bytes 798728 | tf_op jit(solution)/shard_map/ppermute | solution.py:39

commit v18 on v17

--- a/solution.py
+++ b/solution.py
@@ -287,13 +287,16 @@
             RATE_BIAS / jnp.sqrt(row[:, 2:3] / slot_total + EPSILON),
         )
 
-    def updated(state_ref, grad_ref, sizes):
-        key_end, value_end = slot_rows, 2 * slot_rows
-        return (
-            state_ref[:key_end, :] - sizes[0] * grad_ref[:key_end, :],
-            state_ref[key_end:value_end, :] - sizes[1] * grad_ref[key_end:value_end, :],
-            state_ref[value_end:, :] - sizes[2] * grad_ref[value_end:, :],
-        )
+    def read_pack(ref):
+        return ref[:slot_rows, :], ref[slot_rows : 2 * slot_rows, :], ref[2 * slot_rows :, :]
+
+    def store_pack(ref, values):
+        ref[:slot_rows, :] = values[0]
+        ref[slot_rows : 2 * slot_rows, :] = values[1]
+        ref[2 * slot_rows :, :] = values[2]
+
+    def updated(state, grads, sizes):
+        return [value - size * grad for value, grad, size in zip(state, grads, sizes)]
 
     def page_scores(ref, queries, positions):
         scores = dot(halves(ref[:slot_rows, :]), queries, 1, 1) * score_scale
@@ -403,10 +406,8 @@
         chunk_outs, refs = refs[:ranks], refs[ranks:]
         sizes = step_sizes(tile_refs)
         for at in range(2):
-            keys, values, bias = updated(state_refs[at], grad_refs[at], sizes)
-            state_outs[at][:slot_rows, :] = keys
-            state_outs[at][slot_rows : 2 * slot_rows, :] = values
-            state_outs[at][2 * slot_rows :, :] = bias
+            state = read_pack(state_refs[at])
+            store_pack(state_outs[at], updated(state, read_pack(grad_refs[at]), sizes))
         forward(state_outs, query_refs, chunk_outs, *refs)
 
     def merged_chunk(query_refs, sums, maxima, totals, out):
@@ -457,7 +458,7 @@
             merged_out,
         )
 
-    def page_gradients(weights, factor, state_ref, all_queries, residual, row_delta, out):
+    def page_gradients(weights, factor, state_ref, all_queries, residual, row_delta):
         attention = weights * factor
         grad_values = dot(halves(attention), residual, 1, 1)
         grad_probs = dot(halves(state_ref[slot_rows : 2 * slot_rows, :]), residual, 1, 0)
@@ -465,11 +466,7 @@
         grad_keys = dot(grad_scores, all_queries, 1, 0) * score_scale
         ones = jnp.ones((TAIL, query_rows), jnp.bfloat16)
         grad_bias = dot((ones, jnp.zeros_like(ones)), grad_scores, 1, 1)[0:1, :]
-        grad_bias = row_as_tail(grad_bias, width)
-        out[:slot_rows, :] = grad_keys
-        out[slot_rows : 2 * slot_rows, :] = grad_values
-        out[2 * slot_rows :, :] = grad_bias
-        return grad_keys, grad_values, grad_bias
+        return grad_keys, grad_values, row_as_tail(grad_bias, width)
 
     def split_merged(joined):
         row_max, row_total, row_delta = (
@@ -517,9 +514,8 @@
         for at, (ref, out) in enumerate(zip(state_refs, grad_outs)):
             rows = slice(at * slot_rows, (at + 1) * slot_rows)
             page_weights = jnp.concatenate([part[rows, :] for part in weights_refs], axis=1)
-            grads = page_gradients(
-                page_weights, factor, ref, all_queries, residual, row_delta, out
-            )
+            grads = page_gradients(page_weights, factor, ref, all_queries, residual, row_delta)
+            store_pack(out, grads)
             for which, grad in enumerate(grads):
                 squares[which] = squares[which] + jnp.sum(grad * grad, axis=0, keepdims=True)
         lanes = lax.broadcasted_iota(jnp.int32, (1, width), 1)
@@ -529,25 +525,27 @@
         for at in range(devices):
             squares_out[at] = row
 
-    def page_body(turn, at):
-        def body(state_ref, joined_ref, *refs):
-            *pack_refs, grad_out = refs
-            query_refs = [state_ref.at[pl.ds(CORES * packed_rows, query_shape[0])]] + pack_refs
-            residual, row_max, row_total, row_delta = split_merged(joined_ref[...])
-            all_queries = read_queries(query_refs)
-            ref = part_of(state_ref, at)
-            scores, visible = page_scores(ref, all_queries, read_positions(query_refs))
-            weights = jnp.where(visible, jnp.exp(scores - row_max), 0.0)
-            page_gradients(
-                weights, 1.0 / row_total, ref, all_queries, residual, row_delta, grad_out
-            )
+    def page_body(at):
+        def body(tile_ref, grad_ref, own_state_ref, *refs):
+            state_refs, refs = refs[: query_devices - 1], refs[query_devices - 1 :]
+            joined_refs, (*pack_refs, out) = refs[: query_devices - 1], refs[query_devices - 1 :]
+            sizes = step_sizes([tile_ref])
+            state = read_pack(part_of(own_state_ref, at))
+            store_pack(part_of(out, 0), updated(state, read_pack(grad_ref), sizes))
+            for turn, (state_ref, joined_ref) in enumerate(zip(state_refs, joined_refs), 1):
+                query_refs = [state_ref.at[pl.ds(CORES * packed_rows, query_shape[0])]]
+                query_refs += pack_refs[(turn - 1) * (query_devices - 1) :][: query_devices - 1]
+                residual, row_max, row_total, row_delta = split_merged(joined_ref[...])
+                all_queries = read_queries(query_refs)
+                ref = part_of(state_ref, at)
+                scores, visible = page_scores(ref, all_queries, read_positions(query_refs))
+                weights = jnp.where(visible, jnp.exp(scores - row_max), 0.0)
+                grads = page_gradients(
+                    weights, 1.0 / row_total, ref, all_queries, residual, row_delta
+                )
+                store_pack(part_of(out, turn), updated(read_pack(ref), grads, sizes))
 
         return body
-
-    def mate_body(*refs):
-        *state_refs, out_ref = refs
-        for at, ref in enumerate(state_refs):
-            out_ref[pl.ds(at * packed_rows, packed_rows), :] = part_of(ref, 1)[...]
 
     for repeat in range(STEPS):
         last = repeat == STEPS - 1
@@ -620,47 +618,29 @@
             )
         ]
 
-    (for_mate,) = call(
-        mate_body,
-        [(query_devices * packed_rows, width)],
-        "mate_parts",
-        2**20,
-        new_states,
-        after=tiles,
-    )
-    from_mate = exchange(for_mate, page=1)
-    all_grads = [own_grad, exchange(mate_grad, page=1)]
-    for turn in range(1, query_devices):
-        parts = [
-            packs[part] if part == turn else query_part(turn, part)
-            for part in range(1, query_devices)
-        ]
-        page_grads = [
-            call(
-                page_body(turn, at),
-                packed_shapes[:1],
-                "other_backward",
-                3 * matmul_cost // 2,
-                [new_states[turn], all_joined[turn]] + parts,
-                after=tiles,
-            )[0]
-            for at in reversed(range(CORES))
-        ]
-        all_grads += [page_grads[1], exchange(page_grads[0], page=1)]
-    out_masks = list(itertools.product(range(query_devices), range(CORES)))
+    other_packs = [
+        packs[part] if part == turn else query_part(turn, part)
+        for turn in range(1, query_devices)
+        for part in range(1, query_devices)
+    ]
+    operands = new_states + all_joined[1:] + other_packs
+    pages = []
+    for at, grad in ((1, mate_grad), (0, own_grad)):
+        pages += call(
+            page_body(at),
+            [(query_devices * packed_rows, width)],
+            "page_update",
+            3 * matmul_cost // 2,
+            tiles + [grad] + operands,
+            after=pages,
+        )
+    pages = [pages[1], exchange(pages[0], page=1)]
 
     def last_body(*refs):
-        state_refs, (mate_ref, *refs) = refs[:query_devices], refs[query_devices:]
-        state_refs = [
-            part_of(mate_ref, turn) if flip else part_of(state_refs[turn], 0)
-            for turn, flip in out_masks
-        ]
-        grad_refs, refs = refs[:local_heads], refs[local_heads:]
-        tile_refs, (keys_out, values_out, bias_out) = refs[: len(tiles)], refs[len(tiles) :]
+        page_refs, (keys_out, values_out, bias_out) = refs[:CORES], refs[CORES:]
         _, core, me = places()
-        sizes = step_sizes(tile_refs)
-        for at, (turn, flip) in enumerate(out_masks):
-            keys, values, bias = updated(state_refs[at], grad_refs[at], sizes)
+        for turn, flip in itertools.product(range(query_devices), range(CORES)):
+            keys, values, bias = read_pack(part_of(page_refs[flip], turn))
             head = CORES * (me ^ turn) + (core ^ flip)
             keys_out[head] = keys
             values_out[head] = values
@@ -671,9 +651,9 @@
         call(
             last_body,
             [compact_keys.shape, compact_values.shape, slot_bias.shape],
-            "last_update",
+            "unpack",
             2**20,
-            new_states + [from_mate] + all_grads + tiles,
+            pages,
         )
     )
 

time: 80 us -> 79.4 us (level)
    ppermute x22 -> x20, starting transfers between devices: 27.7 us -> 27.1 us  [exchange(): return lax.ppermute(value, axes, pairs)]
    ppermute x22 -> x20, waiting for transfers between devices: 15.2 us -> 15.5 us  [exchange(): return lax.ppermute(value, axes, pairs)]
    pallas_call x14 -> x13, Pallas kernels: 14.9 us -> 14.8 us  [call(): pl.pallas_call(without_after, out_shape=[jax.ShapeDtypeStruct(shape, jnp....]
  transfers between devices with their start and end apart: 22 -> 20, of which waited for: 9 -> 9; matrix products, arithmetic and copies ran while one was open for 0% -> 0% of each run, Pallas kernels for 10% -> 8%
where the time goes in v18:
time: 79.4 us; the launch traced here: 79.2 us
  starting transfers between devices  27.1 us (34%)
  blocking collectives  20.9 us (26%)
  waiting for transfers between devices  15.5 us (20%)
  Pallas kernels  14.8 us (19%)
  between operations  0.85 us (1%)
    ppermute x20, starting transfers between devices, exchange(): return lax.ppermute(value, axes, pairs)  27.1 us
    all_to_all x2, blocking collectives, direct_per_device(): lax.all_to_all(squares, ('page', 'query', 'head'), split_axis=0, concat_a...  20.9 us
    ppermute x20, waiting for transfers between devices, exchange(): return lax.ppermute(value, axes, pairs)  15.5 us
    pallas_call x13, Pallas kernels, call(): pl.pallas_call(without_after, out_shape=[jax.ShapeDtypeStruct(shape, jnp....  14.8 us
  transfers between devices with their start and end apart: 20, of which 9 were waited for; matrix products, arithmetic and copies ran while one was open for 0% of the time, Pallas kernels for 8%

profile of v18, /device:TPU:0, one launch (start us, length us, event | category | flops | bytes accessed | tf_op | source)
XLA Modules:
  0.0 79.2 jit_solution(8275502808281914933)
XLA Ops:
  0.7 2.0 %pack.1 = (f32[520,128]{1,0:T(8,128)}, f32[328,128]{1,0:T(8,128)}) custom-call(f32[4,256,128]{2,1,0:T(8,128)} %refs_0_.3, f32[4,256,128]{2,1,0:T(8,128)} %refs_1_.3, f32[4,256,128]{2,1,0:T(8,128)} %refs_2_.3, f32[4,256]{1,0:T(4,128)} %refs_3_.3, f32[4,256,128]{2,1,0:T(8,128)} %refs_4_.3, s32[4,256]{1,0:T(4,128)} %refs_5_.3, s32[8]{0:T(128)} %refs_6_.3), custom_call_target="tpu_custom_call" | custom-call | flops 1048576 | bytes 1048576 | tf_op jit(solution)/shard_map/pack/pallas_call | solution.py:67
  2.7 0.0 copy-start.7
  2.7 0.5 collective-permute-start
  3.3 2.6 %collective-permute-start.1 = (f32[328,128]{1,0:T(8,128)}, f32[328,128]{1,0:T(8,128)S(1)}, u32[]{:S(2)}, u32[]{:S(2)}) collective-permute-start(f32[328,128]{1,0:T(8,128)} %get-tuple-element.35.refs_5_), channel_id=1, source_target_pairs={{0,2},{2,0},{1,3},{3,1},{4,6},{6,4},{5,7},{7,5},{8,10},{10,8},{9,1... | collective-permute-start | bytes 503816 | tf_op jit(solution)/shard_map/ppermute | solution.py:39
  5.9 0.7 own.1
  6.6 1.0 %forward.2 = (f32[72,128]{1,0:T(8,128)S(1)}, f32[72,128]{1,0:T(8,128)S(1)}, f32[72,128]{1,0:T(8,128)S(1)}, f32[72,128]{1,0:T(8,128)S(1)}, f32[512,256]{1,0:T(8,128)S(1)}, /*index=5*/f32[8,256]{1,0:T(8,128)S(1)}) custom-call(f32[520,128]{1,0:T(8,128)S(1)} %get-tuple-element.32.refs_0_.refs_4_, f32[520,128]{1,0:T(8,128)S(1)} %collective-permute-done.refs_1_.refs_5_, ...), custom_call_target="tpu_custom_call" | custom-call | flops 201326592 | bytes 1048576 | tf_op jit(solution)/shard_map/forward/pallas_call | solution.py:67
  7.6 3.7 %collective-permute-start.2 = (f32[72,128]{1,0:T(8,128)S(1)}, f32[72,128]{1,0:T(8,128)S(1)}, u32[]{:S(2)}, u32[]{:S(2)}) collective-permute-start(f32[72,128]{1,0:T(8,128)S(1)} %get-tuple-element.40), channel_id=1, source_target_pairs={{0,24},{4,28},{8,16},{12,20},{16,8},{20,12},{24,0},{28,4},{1,25},{... | collective-permute-start | bytes 110600 | tf_op jit(solution)/shard_map/ppermute | solution.py:39
  11.3 0.0 collective-permute-start.3
  11.3 0.8 collective-permute-start.4
  12.0 1.0 %forward.3 = (f32[72,128]{1,0:T(8,128)S(1)}, f32[72,128]{1,0:T(8,128)S(1)}, f32[72,128]{1,0:T(8,128)S(1)}, f32[72,128]{1,0:T(8,128)S(1)}, f32[512,256]{1,0:T(8,128)S(1)}, /*index=5*/f32[8,256]{1,0:T(8,128)S(1)}) custom-call(f32[520,128]{1,0:T(8,128)S(1)} %get-tuple-element.32.refs_0_.refs_4_, f32[520,128]{1,0:T(8,128)S(1)} %collective-permute-done.refs_1_.refs_5_, ...), custom_call_target="tpu_custom_call" | custom-call | flops 201326592 | bytes 1048576 | tf_op jit(solution)/shard_map/forward/pallas_call | solution.py:67
  13.1 3.7 %collective-permute-start.5 = (f32[72,128]{1,0:T(8,128)S(1)}, f32[72,128]{1,0:T(8,128)S(1)}, u32[]{:S(2)}, u32[]{:S(2)}) collective-permute-start(f32[72,128]{1,0:T(8,128)S(1)} %get-tuple-element.44), channel_id=1, source_target_pairs={{0,24},{4,28},{8,16},{12,20},{16,8},{20,12},{24,0},{28,4},{1,25},{... | collective-permute-start | bytes 110600 | tf_op jit(solution)/shard_map/ppermute | solution.py:39
  16.7 0.0 collective-permute-start.6
  16.7 0.0 collective-permute-done.2.refs_2_
  16.7 0.8 collective-permute-start.7
  17.5 0.0 collective-permute-done.3.refs_3_
  17.5 0.0 collective-permute-done.4.refs_4_
  17.5 1.5 %collective-permute-done.5.refs_6_ = f32[72,128]{1,0:T(8,128)S(1)} collective-permute-done((f32[72,128]{1,0:T(8,128)S(1)}, f32[72,128]{1,0:T(8,128)S(1)}, u32[]{:S(2)}, u32[]{:S(2)}) %collective-permute-start.5) | collective-permute-done | bytes 36896 | tf_op jit(solution)/shard_map/ppermute | solution.py:39
  19.0 2.6 %collective-permute-done.6.refs_7_ = f32[72,128]{1,0:T(8,128)S(1)} collective-permute-done((f32[72,128]{1,0:T(8,128)S(1)}, f32[72,128]{1,0:T(8,128)S(1)}, u32[]{:S(2)}, u32[]{:S(2)}) %collective-permute-start.6) | collective-permute-done | bytes 36896 | tf_op jit(solution)/shard_map/ppermute | solution.py:39
  21.6 0.3 merge.2.refs_8_
  21.9 1.5 %collective-permute-start.10 = (f32[136,128]{1,0:T(8,128)S(1)}, f32[136,128]{1,0:T(8,128)S(1)}, u32[]{:S(2)}, u32[]{:S(2)}) collective-permute-start(f32[136,128]{1,0:T(8,128)S(1)} %merge.2.refs_8_), channel_id=1, source_target_pairs={{0,24},{4,28},{8,16},{12,20},{16,8},{20,12},{24,0},{28,4},{1,25},{... | collective-permute-start | bytes 208904 | tf_op jit(solution)/shard_map/ppermute | solution.py:39
  23.4 0.6 collective-permute-start.9
  24.0 2.3 %collective-permute-start.8 = (f32[136,128]{1,0:T(8,128)S(1)}, f32[136,128]{1,0:T(8,128)S(1)}, u32[]{:S(2)}, u32[]{:S(2)}) collective-permute-start(f32[136,128]{1,0:T(8,128)S(1)} %merge.2.refs_8_), channel_id=1, source_target_pairs={{0,8},{4,12},{8,0},{12,4},{16,24},{20,28},{24,16},{28,20},{1,9},{5... | collective-permute-start | bytes 208904 | tf_op jit(solution)/shard_map/ppermute | solution.py:39
  26.3 1.8 %collective-permute-done.10.refs_11_ = f32[136,128]{1,0:T(8,128)S(1)} collective-permute-done((f32[136,128]{1,0:T(8,128)S(1)}, f32[136,128]{1,0:T(8,128)S(1)}, u32[]{:S(2)}, u32[]{:S(2)}) %collective-permute-start.10) | collective-permute-done | bytes 69664 | tf_op jit(solution)/shard_map/ppermute | solution.py:39
  28.1 1.5 %collective-permute-done.9.refs_10_ = f32[136,128]{1,0:T(8,128)S(1)} collective-permute-done((f32[136,128]{1,0:T(8,128)S(1)}, f32[136,128]{1,0:T(8,128)S(1)}, u32[]{:S(2)}, u32[]{:S(2)}) %collective-permute-start.9) | collective-permute-done | bytes 69664 | tf_op jit(solution)/shard_map/ppermute | solution.py:39
  29.5 2.3 %backward.2 = (f32[520,128]{1,0:T(8,128)S(1)}, f32[520,128]{1,0:T(8,128)S(1)}, f32[32,1,128]{2,1,0:T(1,128)S(1)}) custom-call(f32[512,256]{1,0:T(8,128)S(1)} %get-tuple-element.36.refs_0_, f32[512,256]{1,0:T(8,128)S(1)} %get-tuple-element.38.refs_1_, f32[8,256]{1,0:T(8,128)S(1)} %get-tuple-element.37.refs_3_.refs_2_, ...), custom_call_target="tpu_custom_call" | custom-call | flops 603979776 | bytes 1048576 | tf_op jit(solution)/shard_map/backward/pallas_call | solution.py:67
  31.8 11.1 %all_to_all.10.refs_6_ = f32[32,1,128]{2,1,0:T(1,128)S(1)} all-to-all(f32[32,1,128]{2,1,0:T(1,128)S(1)} %get-tuple-element.50), channel_id=1, replica_groups=mesh['page'=8,'query'=2,'head'=2] {'page','query','head'}, dimensions={0} | all-to-all | bytes 32768 | tf_op jit(solution)/shard_map/all_to_all | solution.py:616
  42.9 1.3 %update_forward.1 = (f32[1368,128]{1,0:T(8,128)S(1)}, f32[136,128]{1,0:T(8,128)S(1)}, f32[136,128]{1,0:T(8,128)S(1)}, f32[136,128]{1,0:T(8,128)S(1)}, f32[136,12...) custom-call(f32[520,128]{1,0:T(8,128)S(1)} %get-tuple-element.32.refs_0_.refs_4_, ...), custom_call_target="tpu_custom_call" | custom-call | flops 402653184 | bytes 1048576 | tf_op jit(solution)/shard_map/update_forward/pallas_call | solution.py:67
  44.2 0.6 collective-permute-start.17
  44.8 0.6 collective-permute-start.11
  45.3 1.5 %collective-permute-start.12 = (f32[136,128]{1,0:T(8,128)S(1)}, f32[136,128]{1,0:T(8,128)S(1)}, u32[]{:S(2)}, u32[]{:S(2)}) collective-permute-start(f32[136,128]{1,0:T(8,128)S(1)} %get-tuple-element.56), channel_id=1, source_target_pairs={{0,16},{4,20},{8,24},{12,28},{16,0},{20,4},{24,8},{28,12},{1,17},{... | collective-permute-start | bytes 208904 | tf_op jit(solution)/shard_map/ppermute | solution.py:39
  46.8 2.3 %collective-permute-start.13 = (f32[136,128]{1,0:T(8,128)S(1)}, f32[136,128]{1,0:T(8,128)S(1)}, u32[]{:S(2)}, u32[]{:S(2)}) collective-permute-start(f32[136,128]{1,0:T(8,128)S(1)} %get-tuple-element.57), channel_id=1, source_target_pairs={{0,8},{4,12},{8,0},{12,4},{16,24},{20,28},{24,16},{28,20},{1,9},{5... | collective-permute-start | bytes 208904 | tf_op jit(solution)/shard_map/ppermute | solution.py:39
  49.1 2.5 %collective-permute-done.11.refs_3_ = f32[136,128]{1,0:T(8,128)S(1)} collective-permute-done((f32[136,128]{1,0:T(8,128)S(1)}, f32[136,128]{1,0:T(8,128)S(1)}, u32[]{:S(2)}, u32[]{:S(2)}) %collective-permute-start.11) | collective-permute-done | bytes 69664 | tf_op jit(solution)/shard_map/ppermute | solution.py:39
  51.7 1.7 %collective-permute-done.12.refs_4_ = f32[136,128]{1,0:T(8,128)S(1)} collective-permute-done((f32[136,128]{1,0:T(8,128)S(1)}, f32[136,128]{1,0:T(8,128)S(1)}, u32[]{:S(2)}, u32[]{:S(2)}) %collective-permute-start.12) | collective-permute-done | bytes 69664 | tf_op jit(solution)/shard_map/ppermute | solution.py:39
  53.3 0.1 merge.3.refs_0_
  53.5 1.2 %collective-permute-start.16 = (f32[136,128]{1,0:T(8,128)S(1)}, f32[136,128]{1,0:T(8,128)S(1)}, u32[]{:S(2)}, u32[]{:S(2)}) collective-permute-start(f32[136,128]{1,0:T(8,128)S(1)} %merge.3.refs_0_), channel_id=1, source_target_pairs={{0,24},{4,28},{8,16},{12,20},{16,8},{20,12},{24,0},{28,4},{1,25},{... | collective-permute-start | bytes 208904 | tf_op jit(solution)/shard_map/ppermute | solution.py:39
  54.7 0.4 collective-permute-start.15
  55.1 2.8 %collective-permute-start.14 = (f32[136,128]{1,0:T(8,128)S(1)}, f32[136,128]{1,0:T(8,128)S(1)}, u32[]{:S(2)}, u32[]{:S(2)}) collective-permute-start(f32[136,128]{1,0:T(8,128)S(1)} %merge.3.refs_0_), channel_id=1, source_target_pairs={{0,8},{4,12},{8,0},{12,4},{16,24},{20,28},{24,16},{28,20},{1,9},{5... | collective-permute-start | bytes 208904 | tf_op jit(solution)/shard_map/ppermute | solution.py:39
  57.9 2.4 %collective-permute-done.16.refs_3_ = f32[136,128]{1,0:T(8,128)S(1)} collective-permute-done((f32[136,128]{1,0:T(8,128)S(1)}, f32[136,128]{1,0:T(8,128)S(1)}, u32[]{:S(2)}, u32[]{:S(2)}) %collective-permute-start.16) | collective-permute-done | bytes 69664 | tf_op jit(solution)/shard_map/ppermute | solution.py:39
  60.3 1.1 %collective-permute-done.15.refs_2_ = f32[136,128]{1,0:T(8,128)S(1)} collective-permute-done((f32[136,128]{1,0:T(8,128)S(1)}, f32[136,128]{1,0:T(8,128)S(1)}, u32[]{:S(2)}, u32[]{:S(2)}) %collective-permute-start.15) | collective-permute-done | bytes 69664 | tf_op jit(solution)/shard_map/ppermute | solution.py:39
  61.5 0.1 join.1.refs_5_
  61.6 1.2 %collective-permute-start.18 = (f32[136,512]{1,0:T(8,128)S(1)}, f32[136,512]{1,0:T(8,128)S(1)}, u32[]{:S(2)}, u32[]{:S(2)}) collective-permute-start(f32[136,512]{1,0:T(8,128)S(1)} %join.1.refs_5_), channel_id=1, source_target_pairs={{0,2},{2,0},{1,3},{3,1},{4,6},{6,4},{5,7},{7,5},{8,10},{10,8},{9,1... | collective-permute-start | bytes 835592 | tf_op jit(solution)/shard_map/ppermute | solution.py:39
  62.8 2.1 %backward.3 = (f32[520,128]{1,0:T(8,128)S(1)}, f32[520,128]{1,0:T(8,128)S(1)}, f32[32,1,128]{2,1,0:T(1,128)S(1)}) custom-call(f32[512,512]{1,0:T(8,128)S(1)} %get-tuple-element.51.refs_0_, f32[8,512]{1,0:T(8,128)S(1)} %get-tuple-element.52.refs_1_, f32[1368,128]{1,0:T(8,128)S(1)} %get-tuple-element.53.refs_2_, ...), custom_call_target="tpu_custom_call" | custom-call | flops 603979776 | bytes 1048576 | tf_op jit(solution)/shard_map/backward/pallas_call | solution.py:67
  64.9 9.9 %all_to_all.11.refs_0_ = f32[32,1,128]{2,1,0:T(1,128)S(1)} all-to-all(f32[32,1,128]{2,1,0:T(1,128)S(1)} %get-tuple-element.58), channel_id=1, replica_groups=mesh['page'=8,'query'=2,'head'=2] {'page','query','head'}, dimensions={0} | all-to-all | bytes 32768 | tf_op jit(solution)/shard_map/all_to_all | solution.py:616
  74.8 1.5 %page_update.2.refs_6_ = f32[1040,128]{1,0:T(8,128)S(1)} custom-call(f32[32,1,128]{2,1,0:T(1,128)S(1)} %all_to_all.11.refs_0_, f32[520,128]{1,0:T(8,128)S(1)} %get-tuple-element.60.refs_1_, f32[1368,128]{1,0:T(8,128)S(1)} %get-tuple-element.53.refs_2_, f32[1368,128]{1,0:T(8,128)S(1)} %collective-permute-done.17.refs_3_, ...), custom_call_target="tpu_custom_call" | custom-call | flops 301989888 | bytes 1048576 | tf_op jit(solution)/shard_map/page_update/pallas_call | solution.py:67
  76.3 0.0 collective-permute-start.19
  76.3 1.5 %page_update.3.refs_0_ = f32[1040,128]{1,0:T(8,128)S(1)} custom-call(f32[32,1,128]{2,1,0:T(1,128)S(1)} %all_to_all.11.refs_0_, f32[520,128]{1,0:T(8,128)S(1)} %get-tuple-element.59.refs_1_, f32[1368,128]{1,0:T(8,128)S(1)} %get-tuple-element.53.refs_2_, f32[1368,128]{1,0:T(8,128)S(1)} %collective-permute-done.17.refs_3_, ...), custom_call_target="tpu_custom_call" | custom-call | flops 301989888 | bytes 1048576 | tf_op jit(solution)/shard_map/page_update/pallas_call | solution.py:67
  77.7 0.4 collective-permute-done.19.refs_1_
  78.2 1.0 %unpack.1 = (f32[4,256,128]{2,1,0:T(8,128)}, f32[4,256,128]{2,1,0:T(8,128)}, f32[4,256]{1,0:T(4,128)}) custom-call(f32[1040,128]{1,0:T(8,128)S(1)} %page_update.3.refs_0_, f32[1040,128]{1,0:T(8,128)S(1)} %collective-permute-done.19.refs_1_), custom_call_target="tpu_custom_call" | custom-call | flops 1048576 | bytes 1048576 | tf_op jit(solution)/shard_map/unpack/pallas_call | solution.py:67
  (23 shorter events, 0.1 us)
Async XLA Ops:
  0.6 5.2 %copy-start.3 = (f32[4,256,128]{2,1,0:T(8,128)S(1)}, f32[4,256,128]{2,1,0:T(8,128)}, u32[]{:S(2)}) copy-start(f32[4,256,128]{2,1,0:T(8,128)} %refs_4_.3) | copy-start | bytes 1572868
  0.6 5.2 %copy-start.2 = (f32[4,256,128]{2,1,0:T(8,128)S(1)}, f32[4,256,128]{2,1,0:T(8,128)}, u32[]{:S(2)}) copy-start(f32[4,256,128]{2,1,0:T(8,128)} %refs_2_.3) | copy-start | bytes 1572868
  0.7 5.2 %copy-start.1 = (f32[4,256,128]{2,1,0:T(8,128)S(1)}, f32[4,256,128]{2,1,0:T(8,128)}, u32[]{:S(2)}) copy-start(f32[4,256,128]{2,1,0:T(8,128)} %refs_1_.3) | copy-start | bytes 1572868
  0.7 5.2 %copy-start = (f32[4,256,128]{2,1,0:T(8,128)S(1)}, f32[4,256,128]{2,1,0:T(8,128)}, u32[]{:S(2)}) copy-start(f32[4,256,128]{2,1,0:T(8,128)} %refs_0_.3) | copy-start | bytes 1572868
  0.7 5.2 %copy-start.5 = (f32[4,256]{1,0:T(4,128)S(1)}, f32[4,256]{1,0:T(4,128)}, u32[]{:S(2)}) copy-start(f32[4,256]{1,0:T(4,128)} %refs_3_.3) | copy-start | bytes 12292
  0.7 5.2 %copy-start.6 = (s32[4,256]{1,0:T(4,128)S(1)}, s32[4,256]{1,0:T(4,128)}, u32[]{:S(2)}) copy-start(s32[4,256]{1,0:T(4,128)} %refs_5_.3) | copy-start | bytes 12292
  2.7 3.2 %copy-start.7 = (s32[8]{0:T(128)S(1)}, s32[8]{0:T(128)}, u32[]{:S(2)}) copy-start(s32[8]{0:T(128)} %refs_6_.3) | copy-start | bytes 100
  2.7 3.8 %collective-permute-start = (f32[520,128]{1,0:T(8,128)}, f32[520,128]{1,0:T(8,128)S(1)}, u32[]{:S(2)}, u32[]{:S(2)}) collective-permute-start(f32[520,128]{1,0:T(8,128)} %get-tuple-element.33), channel_id=1, source_target_pairs={{0,4},{4,0},{8,12},{12,8},{16,20},{20,16},{24,28},{28,24},{1,5},{5... | collective-permute-start | bytes 798728 | tf_op jit(solution)/shard_map/ppermute | solution.py:39
  3.3 8.8 %collective-permute-start.1 = (f32[328,128]{1,0:T(8,128)}, f32[328,128]{1,0:T(8,128)S(1)}, u32[]{:S(2)}, u32[]{:S(2)}) collective-permute-start(f32[328,128]{1,0:T(8,128)} %get-tuple-element.35.refs_5_), channel_id=1, source_target_pairs={{0,2},{2,0},{1,3},{3,1},{4,6},{6,4},{5,7},{7,5},{8,10},{10,8},{9,1... | collective-permute-start | bytes 503816 | tf_op jit(solution)/shard_map/ppermute | solution.py:39
  7.6 9.2 %collective-permute-start.2 = (f32[72,128]{1,0:T(8,128)S(1)}, f32[72,128]{1,0:T(8,128)S(1)}, u32[]{:S(2)}, u32[]{:S(2)}) collective-permute-start(f32[72,128]{1,0:T(8,128)S(1)} %get-tuple-element.40), channel_id=1, source_target_pairs={{0,24},{4,28},{8,16},{12,20},{16,8},{20,12},{24,0},{28,4},{1,25},{... | collective-permute-start | bytes 110600 | tf_op jit(solution)/shard_map/ppermute | solution.py:39
  11.3 6.3 %collective-permute-start.3 = (f32[72,128]{1,0:T(8,128)S(1)}, f32[72,128]{1,0:T(8,128)S(1)}, u32[]{:S(2)}, u32[]{:S(2)}) collective-permute-start(f32[72,128]{1,0:T(8,128)S(1)} %get-tuple-element.41), channel_id=1, source_target_pairs={{0,16},{4,20},{8,24},{12,28},{16,0},{20,4},{24,8},{28,12},{1,17},{... | collective-permute-start | bytes 110600 | tf_op jit(solution)/shard_map/ppermute | solution.py:39
  11.3 6.3 %collective-permute-start.4 = (f32[72,128]{1,0:T(8,128)S(1)}, f32[72,128]{1,0:T(8,128)S(1)}, u32[]{:S(2)}, u32[]{:S(2)}) collective-permute-start(f32[72,128]{1,0:T(8,128)S(1)} %get-tuple-element.42), channel_id=1, source_target_pairs={{0,8},{4,12},{8,0},{12,4},{16,24},{20,28},{24,16},{28,20},{1,9},{5... | collective-permute-start | bytes 110600 | tf_op jit(solution)/shard_map/ppermute | solution.py:39
  13.1 5.9 %collective-permute-start.5 = (f32[72,128]{1,0:T(8,128)S(1)}, f32[72,128]{1,0:T(8,128)S(1)}, u32[]{:S(2)}, u32[]{:S(2)}) collective-permute-start(f32[72,128]{1,0:T(8,128)S(1)} %get-tuple-element.44), channel_id=1, source_target_pairs={{0,24},{4,28},{8,16},{12,20},{16,8},{20,12},{24,0},{28,4},{1,25},{... | collective-permute-start | bytes 110600 | tf_op jit(solution)/shard_map/ppermute | solution.py:39
  16.7 4.9 %collective-permute-start.6 = (f32[72,128]{1,0:T(8,128)S(1)}, f32[72,128]{1,0:T(8,128)S(1)}, u32[]{:S(2)}, u32[]{:S(2)}) collective-permute-start(f32[72,128]{1,0:T(8,128)S(1)} %get-tuple-element.45), channel_id=1, source_target_pairs={{0,16},{4,20},{8,24},{12,28},{16,0},{20,4},{24,8},{28,12},{1,17},{... | collective-permute-start | bytes 110600 | tf_op jit(solution)/shard_map/ppermute | solution.py:39
  16.7 4.9 %collective-permute-start.7 = (f32[72,128]{1,0:T(8,128)S(1)}, f32[72,128]{1,0:T(8,128)S(1)}, u32[]{:S(2)}, u32[]{:S(2)}) collective-permute-start(f32[72,128]{1,0:T(8,128)S(1)} %get-tuple-element.46), channel_id=1, source_target_pairs={{0,8},{4,12},{8,0},{12,4},{16,24},{20,28},{24,16},{28,20},{1,9},{5... | collective-permute-start | bytes 110600 | tf_op jit(solution)/shard_map/ppermute | solution.py:39
  21.9 6.2 %collective-permute-start.10 = (f32[136,128]{1,0:T(8,128)S(1)}, f32[136,128]{1,0:T(8,128)S(1)}, u32[]{:S(2)}, u32[]{:S(2)}) collective-permute-start(f32[136,128]{1,0:T(8,128)S(1)} %merge.2.refs_8_), channel_id=1, source_target_pairs={{0,24},{4,28},{8,16},{12,20},{16,8},{20,12},{24,0},{28,4},{1,25},{... | collective-permute-start | bytes 208904 | tf_op jit(solution)/shard_map/ppermute | solution.py:39
  23.4 6.1 %collective-permute-start.9 = (f32[136,128]{1,0:T(8,128)S(1)}, f32[136,128]{1,0:T(8,128)S(1)}, u32[]{:S(2)}, u32[]{:S(2)}) collective-permute-start(f32[136,128]{1,0:T(8,128)S(1)} %merge.2.refs_8_), channel_id=1, source_target_pairs={{0,16},{4,20},{8,24},{12,28},{16,0},{20,4},{24,8},{28,12},{1,17},{... | collective-permute-start | bytes 208904 | tf_op jit(solution)/shard_map/ppermute | solution.py:39
  24.0 5.5 %collective-permute-start.8 = (f32[136,128]{1,0:T(8,128)S(1)}, f32[136,128]{1,0:T(8,128)S(1)}, u32[]{:S(2)}, u32[]{:S(2)}) collective-permute-start(f32[136,128]{1,0:T(8,128)S(1)} %merge.2.refs_8_), channel_id=1, source_target_pairs={{0,8},{4,12},{8,0},{12,4},{16,24},{20,28},{24,16},{28,20},{1,9},{5... | collective-permute-start | bytes 208904 | tf_op jit(solution)/shard_map/ppermute | solution.py:39
  44.2 30.6 %collective-permute-start.17 = (f32[1368,128]{1,0:T(8,128)S(1)}, f32[1368,128]{1,0:T(8,128)S(1)}, u32[]{:S(2)}, u32[]{:S(2)}) collective-permute-start(f32[1368,128]{1,0:T(8,128)S(1)} %get-tuple-element.53.refs_2_), channel_id=1, source_target_pairs={{0,2},{2,0},{1,3},{3,1},{4,6},{6,4},{5,7},{7,5},{8,10},{10,8},{9,1... | collective-permute-start | bytes 2101256 | tf_op jit(solution)/shard_map/ppermute | solution.py:39
  44.8 6.9 %collective-permute-start.11 = (f32[136,128]{1,0:T(8,128)S(1)}, f32[136,128]{1,0:T(8,128)S(1)}, u32[]{:S(2)}, u32[]{:S(2)}) collective-permute-start(f32[136,128]{1,0:T(8,128)S(1)} %get-tuple-element.55), channel_id=1, source_target_pairs={{0,24},{4,28},{8,16},{12,20},{16,8},{20,12},{24,0},{28,4},{1,25},{... | collective-permute-start | bytes 208904 | tf_op jit(solution)/shard_map/ppermute | solution.py:39
  45.3 8.0 %collective-permute-start.12 = (f32[136,128]{1,0:T(8,128)S(1)}, f32[136,128]{1,0:T(8,128)S(1)}, u32[]{:S(2)}, u32[]{:S(2)}) collective-permute-start(f32[136,128]{1,0:T(8,128)S(1)} %get-tuple-element.56), channel_id=1, source_target_pairs={{0,16},{4,20},{8,24},{12,28},{16,0},{20,4},{24,8},{28,12},{1,17},{... | collective-permute-start | bytes 208904 | tf_op jit(solution)/shard_map/ppermute | solution.py:39
  46.8 6.5 %collective-permute-start.13 = (f32[136,128]{1,0:T(8,128)S(1)}, f32[136,128]{1,0:T(8,128)S(1)}, u32[]{:S(2)}, u32[]{:S(2)}) collective-permute-start(f32[136,128]{1,0:T(8,128)S(1)} %get-tuple-element.57), channel_id=1, source_target_pairs={{0,8},{4,12},{8,0},{12,4},{16,24},{20,28},{24,16},{28,20},{1,9},{5... | collective-permute-start | bytes 208904 | tf_op jit(solution)/shard_map/ppermute | solution.py:39
  53.5 6.9 %collective-permute-start.16 = (f32[136,128]{1,0:T(8,128)S(1)}, f32[136,128]{1,0:T(8,128)S(1)}, u32[]{:S(2)}, u32[]{:S(2)}) collective-permute-start(f32[136,128]{1,0:T(8,128)S(1)} %merge.3.refs_0_), channel_id=1, source_target_pairs={{0,24},{4,28},{8,16},{12,20},{16,8},{20,12},{24,0},{28,4},{1,25},{... | collective-permute-start | bytes 208904 | tf_op jit(solution)/shard_map/ppermute | solution.py:39
  54.7 6.8 %collective-permute-start.15 = (f32[136,128]{1,0:T(8,128)S(1)}, f32[136,128]{1,0:T(8,128)S(1)}, u32[]{:S(2)}, u32[]{:S(2)}) collective-permute-start(f32[136,128]{1,0:T(8,128)S(1)} %merge.3.refs_0_), channel_id=1, source_target_pairs={{0,16},{4,20},{8,24},{12,28},{16,0},{20,4},{24,8},{28,12},{1,17},{... | collective-permute-start | bytes 208904 | tf_op jit(solution)/shard_map/ppermute | solution.py:39
  55.1 6.4 %collective-permute-start.14 = (f32[136,128]{1,0:T(8,128)S(1)}, f32[136,128]{1,0:T(8,128)S(1)}, u32[]{:S(2)}, u32[]{:S(2)}) collective-permute-start(f32[136,128]{1,0:T(8,128)S(1)} %merge.3.refs_0_), channel_id=1, source_target_pairs={{0,8},{4,12},{8,0},{12,4},{16,24},{20,28},{24,16},{28,20},{1,9},{5... | collective-permute-start | bytes 208904 | tf_op jit(solution)/shard_map/ppermute | solution.py:39
  61.6 13.2 %collective-permute-start.18 = (f32[136,512]{1,0:T(8,128)S(1)}, f32[136,512]{1,0:T(8,128)S(1)}, u32[]{:S(2)}, u32[]{:S(2)}) collective-permute-start(f32[136,512]{1,0:T(8,128)S(1)} %join.1.refs_5_), channel_id=1, source_target_pairs={{0,2},{2,0},{1,3},{3,1},{4,6},{6,4},{5,7},{7,5},{8,10},{10,8},{9,1... | collective-permute-start | bytes 835592 | tf_op jit(solution)/shard_map/ppermute | solution.py:39
  62.8 12.0 %copy-start.4 = (f32[328,128]{1,0:T(8,128)S(1)}, f32[328,128]{1,0:T(8,128)}, u32[]{:S(2)}) copy-start(f32[328,128]{1,0:T(8,128)} %get-tuple-element.35.refs_5_) | copy-start | bytes 503812
  76.3 1.9 %collective-permute-start.19 = (f32[1040,128]{1,0:T(8,128)S(1)}, f32[1040,128]{1,0:T(8,128)S(1)}, u32[]{:S(2)}, u32[]{:S(2)}) collective-permute-start(f32[1040,128]{1,0:T(8,128)S(1)} %page_update.2.refs_6_), channel_id=1, source_target_pairs={{0,4},{4,0},{8,12},{12,8},{16,20},{20,16},{24,28},{28,24},{1,5},{5... | collective-permute-start | bytes 1597448 | tf_op jit(solution)/shard_map/ppermute | solution.py:39

commit v19 on v18

--- a/solution.py
+++ b/solution.py
@@ -44,17 +44,35 @@
     return high, (value - high.astype(jnp.float32)).astype(jnp.bfloat16)
 
 
-def dot(left, right, left_dim, right_dim):
-    def one_pass(left_half, right_half):
-        return lax.dot_general(
-            left_half,
-            right_half,
-            (((left_dim,), (right_dim,)), ((), ())),
-            preferred_element_type=jnp.float32,
-        )
-
-    cross = one_pass(left[0], right[1]) + one_pass(left[1], right[0])
-    return one_pass(left[0], right[0]) + cross
+def one_pass(left, right, left_dim, right_dim):
+    return lax.dot_general(
+        left,
+        right,
+        (((left_dim,), (right_dim,)), ((), ())),
+        preferred_element_type=jnp.float32,
+    )
+
+
+def dot_deep(left, right, left_dim, right_dim):
+    left = jnp.concatenate([left[0], left[1], left[0]], axis=left_dim)
+    right = jnp.concatenate([right[0], right[0], right[1]], axis=right_dim)
+    return one_pass(left, right, left_dim, right_dim)
+
+
+def dot_narrow(left, right, left_dim, right_dim):
+    both = one_pass(
+        left[0], jnp.concatenate(right, axis=1 - right_dim), left_dim, right_dim
+    )
+    count = both.shape[1] // 2
+    cross = both[:, count:] + one_pass(left[1], right[0], left_dim, right_dim)
+    return both[:, :count] + cross
+
+
+def dot_low(left, right, left_dim, right_dim):
+    both = one_pass(jnp.concatenate(left, axis=1 - left_dim), right[0], left_dim, right_dim)
+    count = both.shape[0] // 2
+    cross = both[count:, :] + one_pass(left[0], right[1], left_dim, right_dim)
+    return both[:count, :] + cross
 
 
 def call(body, out_shapes, name, cost, operands, scratch=(), after=(), space=pltpu.VMEM, vmem=32):
@@ -91,6 +109,16 @@
     for at in range(0, row.shape[1], width):
         parts.append(jnp.broadcast_to(row[:, at : at + width], (width, width)).T)
     return jnp.concatenate(parts, axis=0)
+
+
+def column_sums(value, width):
+    groups = [value[:, at : at + width] for at in range(0, value.shape[1], width)]
+    partial = sum(groups[1:], groups[0])
+    blocks = [
+        jnp.sum(partial[at : at + width, :].T, axis=0, keepdims=True)
+        for at in range(0, value.shape[0], width)
+    ]
+    return jnp.concatenate(blocks, axis=1)
 
 
 def direct_plan_fits(mesh, queries, compact_keys):
@@ -299,7 +327,7 @@
         return [value - size * grad for value, grad, size in zip(state, grads, sizes)]
 
     def page_scores(ref, queries, positions):
-        scores = dot(halves(ref[:slot_rows, :]), queries, 1, 1) * score_scale
+        scores = dot_deep(halves(ref[:slot_rows, :]), queries, 1, 1) * score_scale
         bias = row_as_column(tail_as_row(ref, 2 * slot_rows, bias_rows), width)
         scores = scores + jnp.concatenate([bias] * (positions.shape[1] // width), axis=1)
         page_start = ref[packed_rows - 1 : packed_rows, 0:1]
@@ -329,7 +357,7 @@
             weights_out[at * slot_rows : (at + 1) * slot_rows, :] = weights
             row_total = row_total + jnp.sum(weights, axis=0, keepdims=True)
             values = halves(ref[slot_rows : 2 * slot_rows, :])
-            row_sum = row_sum + dot(values, halves(weights), 0, 0)
+            row_sum = row_sum + dot_low(values, halves(weights), 0, 0)
         max_out[...] = jnp.broadcast_to(row_max, (TAIL, query_rows))
         tail = jnp.concatenate(
             [row_max, row_total, jnp.zeros((TAIL - 2, query_rows), jnp.float32)], axis=0
@@ -383,7 +411,7 @@
             weights_out[at * slot_rows : (at + 1) * slot_rows, :] = weights
             row_total = row_total + jnp.sum(weights, axis=0, keepdims=True)
             values = halves(ref[slot_rows : 2 * slot_rows, :])
-            row_sum = row_sum + dot(values, halves(weights), 0, 0)
+            row_sum = row_sum + dot_low(values, halves(weights), 0, 0)
         max_out[...] = jnp.broadcast_to(row_max, (TAIL, part_rows))
         for at in range(ranks):
             own = slice(at * piece, (at + 1) * piece)
@@ -460,12 +488,11 @@
 
     def page_gradients(weights, factor, state_ref, all_queries, residual, row_delta):
         attention = weights * factor
-        grad_values = dot(halves(attention), residual, 1, 1)
-        grad_probs = dot(halves(state_ref[slot_rows : 2 * slot_rows, :]), residual, 1, 0)
-        grad_scores = halves(attention * (grad_probs - row_delta))
-        grad_keys = dot(grad_scores, all_queries, 1, 0) * score_scale
-        ones = jnp.ones((TAIL, query_rows), jnp.bfloat16)
-        grad_bias = dot((ones, jnp.zeros_like(ones)), grad_scores, 1, 1)[0:1, :]
+        grad_values = dot_narrow(halves(attention), residual, 1, 1)
+        grad_probs = dot_deep(halves(state_ref[slot_rows : 2 * slot_rows, :]), residual, 1, 0)
+        grad_scores = attention * (grad_probs - row_delta)
+        grad_keys = dot_narrow(halves(grad_scores), all_queries, 1, 0) * score_scale
+        grad_bias = column_sums(grad_scores, width)
         return grad_keys, grad_values, row_as_tail(grad_bias, width)
 
     def split_merged(joined):

time: 79.4 us -> 76.9 us (0.969)
  Pallas kernels: 14.8 us -> 11.8 us
    pallas_call x13, Pallas kernels: 14.8 us -> 11.8 us  [call(): pl.pallas_call(without_after, out_shape=[jax.ShapeDtypeStruct(shape, jnp....]
  transfers between devices with their start and end apart: 20 -> 20, of which waited for: 9 -> 9; matrix products, arithmetic and copies ran while one was open for 0% -> 0% of each run, Pallas kernels for 8% -> 6%
where the time goes in v19:
time: 76.9 us; the launch traced here: 76.7 us
  starting transfers between devices  27.2 us (35%)
  blocking collectives  20.9 us (27%)
  waiting for transfers between devices  16 us (21%)
  Pallas kernels  11.8 us (15%)
  between operations  0.82 us (1%)
    ppermute x20, starting transfers between devices, exchange(): return lax.ppermute(value, axes, pairs)  27.2 us
    all_to_all x2, blocking collectives, direct_per_device(): lax.all_to_all(squares, ('page', 'query', 'head'), split_axis=0, concat_a...  20.9 us
    ppermute x20, waiting for transfers between devices, exchange(): return lax.ppermute(value, axes, pairs)  16 us
    pallas_call x13, Pallas kernels, call(): pl.pallas_call(without_after, out_shape=[jax.ShapeDtypeStruct(shape, jnp....  11.8 us
  transfers between devices with their start and end apart: 20, of which 9 were waited for; matrix products, arithmetic and copies ran while one was open for 0% of the time, Pallas kernels for 6%

profile of v19, /device:TPU:0, one launch (start us, length us, event | category | flops | bytes accessed | tf_op | source)
XLA Modules:
  0.0 76.7 jit_solution(17634782385588076216)
XLA Ops:
  0.7 2.0 %pack.1 = (f32[520,128]{1,0:T(8,128)}, f32[328,128]{1,0:T(8,128)}) custom-call(f32[4,256,128]{2,1,0:T(8,128)} %refs_0_.3, f32[4,256,128]{2,1,0:T(8,128)} %refs_1_.3, f32[4,256,128]{2,1,0:T(8,128)} %refs_2_.3, f32[4,256]{1,0:T(4,128)} %refs_3_.3, f32[4,256,128]{2,1,0:T(8,128)} %refs_4_.3, s32[4,256]{1,0:T(4,128)} %refs_5_.3, s32[8]{0:T(128)} %refs_6_.3), custom_call_target="tpu_custom_call" | custom-call | flops 1048576 | bytes 1048576 | tf_op jit(solution)/shard_map/pack/pallas_call | solution.py:85
  2.7 0.0 copy-start.7
  2.7 0.5 collective-permute-start
  3.3 2.6 %collective-permute-start.1 = (f32[328,128]{1,0:T(8,128)}, f32[328,128]{1,0:T(8,128)S(1)}, u32[]{:S(2)}, u32[]{:S(2)}) collective-permute-start(f32[328,128]{1,0:T(8,128)} %get-tuple-element.35.refs_5_), channel_id=1, source_target_pairs={{0,2},{2,0},{1,3},{3,1},{4,6},{6,4},{5,7},{7,5},{8,10},{10,8},{9,1... | collective-permute-start | bytes 503816 | tf_op jit(solution)/shard_map/ppermute | solution.py:39
  5.9 0.7 own.1
  6.6 0.9 %forward.2 = (f32[72,128]{1,0:T(8,128)S(1)}, f32[72,128]{1,0:T(8,128)S(1)}, f32[72,128]{1,0:T(8,128)S(1)}, f32[72,128]{1,0:T(8,128)S(1)}, f32[512,256]{1,0:T(8,128)S(1)}, /*index=5*/f32[8,256]{1,0:T(8,128)S(1)}) custom-call(f32[520,128]{1,0:T(8,128)S(1)} %get-tuple-element.32.refs_0_.refs_4_, f32[520,128]{1,0:T(8,128)S(1)} %collective-permute-done.refs_1_.refs_5_, ...), custom_call_target="tpu_custom_call" | custom-call | flops 201326592 | bytes 1048576 | tf_op jit(solution)/shard_map/forward/pallas_call | solution.py:85
  7.5 3.7 %collective-permute-start.2 = (f32[72,128]{1,0:T(8,128)S(1)}, f32[72,128]{1,0:T(8,128)S(1)}, u32[]{:S(2)}, u32[]{:S(2)}) collective-permute-start(f32[72,128]{1,0:T(8,128)S(1)} %get-tuple-element.40), channel_id=1, source_target_pairs={{0,24},{4,28},{8,16},{12,20},{16,8},{20,12},{24,0},{28,4},{1,25},{... | collective-permute-start | bytes 110600 | tf_op jit(solution)/shard_map/ppermute | solution.py:39
  11.2 0.0 collective-permute-start.3
  11.2 0.8 %collective-permute-start.4 = (f32[72,128]{1,0:T(8,128)S(1)}, f32[72,128]{1,0:T(8,128)S(1)}, u32[]{:S(2)}, u32[]{:S(2)}) collective-permute-start(f32[72,128]{1,0:T(8,128)S(1)} %get-tuple-element.42), channel_id=1, source_target_pairs={{0,8},{4,12},{8,0},{12,4},{16,24},{20,28},{24,16},{28,20},{1,9},{5... | collective-permute-start | bytes 110600 | tf_op jit(solution)/shard_map/ppermute | solution.py:39
  12.0 0.0 collective-permute-done.1.refs_2_.refs_1_.refs_7_.refs_3_.refs_4_
  12.0 0.9 %forward.3 = (f32[72,128]{1,0:T(8,128)S(1)}, f32[72,128]{1,0:T(8,128)S(1)}, f32[72,128]{1,0:T(8,128)S(1)}, f32[72,128]{1,0:T(8,128)S(1)}, f32[512,256]{1,0:T(8,128)S(1)}, /*index=5*/f32[8,256]{1,0:T(8,128)S(1)}) custom-call(f32[520,128]{1,0:T(8,128)S(1)} %get-tuple-element.32.refs_0_.refs_4_, f32[520,128]{1,0:T(8,128)S(1)} %collective-permute-done.refs_1_.refs_5_, ...), custom_call_target="tpu_custom_call" | custom-call | flops 201326592 | bytes 1048576 | tf_op jit(solution)/shard_map/forward/pallas_call | solution.py:85
  12.9 3.7 %collective-permute-start.5 = (f32[72,128]{1,0:T(8,128)S(1)}, f32[72,128]{1,0:T(8,128)S(1)}, u32[]{:S(2)}, u32[]{:S(2)}) collective-permute-start(f32[72,128]{1,0:T(8,128)S(1)} %get-tuple-element.44), channel_id=1, source_target_pairs={{0,24},{4,28},{8,16},{12,20},{16,8},{20,12},{24,0},{28,4},{1,25},{... | collective-permute-start | bytes 110600 | tf_op jit(solution)/shard_map/ppermute | solution.py:39
  16.6 0.0 collective-permute-start.6
  16.6 0.0 collective-permute-done.2.refs_2_
  16.6 0.8 %collective-permute-start.7 = (f32[72,128]{1,0:T(8,128)S(1)}, f32[72,128]{1,0:T(8,128)S(1)}, u32[]{:S(2)}, u32[]{:S(2)}) collective-permute-start(f32[72,128]{1,0:T(8,128)S(1)} %get-tuple-element.46), channel_id=1, source_target_pairs={{0,8},{4,12},{8,0},{12,4},{16,24},{20,28},{24,16},{28,20},{1,9},{5... | collective-permute-start | bytes 110600 | tf_op jit(solution)/shard_map/ppermute | solution.py:39
  17.3 0.0 collective-permute-done.3.refs_3_
  17.3 1.5 %collective-permute-done.5.refs_6_ = f32[72,128]{1,0:T(8,128)S(1)} collective-permute-done((f32[72,128]{1,0:T(8,128)S(1)}, f32[72,128]{1,0:T(8,128)S(1)}, u32[]{:S(2)}, u32[]{:S(2)}) %collective-permute-start.5) | collective-permute-done | bytes 36896 | tf_op jit(solution)/shard_map/ppermute | solution.py:39
  18.8 2.6 %collective-permute-done.6.refs_7_ = f32[72,128]{1,0:T(8,128)S(1)} collective-permute-done((f32[72,128]{1,0:T(8,128)S(1)}, f32[72,128]{1,0:T(8,128)S(1)}, u32[]{:S(2)}, u32[]{:S(2)}) %collective-permute-start.6) | collective-permute-done | bytes 36896 | tf_op jit(solution)/shard_map/ppermute | solution.py:39
  21.4 0.3 merge.2.refs_8_
  21.7 1.5 %collective-permute-start.10 = (f32[136,128]{1,0:T(8,128)S(1)}, f32[136,128]{1,0:T(8,128)S(1)}, u32[]{:S(2)}, u32[]{:S(2)}) collective-permute-start(f32[136,128]{1,0:T(8,128)S(1)} %merge.2.refs_8_), channel_id=1, source_target_pairs={{0,24},{4,28},{8,16},{12,20},{16,8},{20,12},{24,0},{28,4},{1,25},{... | collective-permute-start | bytes 208904 | tf_op jit(solution)/shard_map/ppermute | solution.py:39
  23.2 0.6 collective-permute-start.9
  23.8 2.3 %collective-permute-start.8 = (f32[136,128]{1,0:T(8,128)S(1)}, f32[136,128]{1,0:T(8,128)S(1)}, u32[]{:S(2)}, u32[]{:S(2)}) collective-permute-start(f32[136,128]{1,0:T(8,128)S(1)} %merge.2.refs_8_), channel_id=1, source_target_pairs={{0,8},{4,12},{8,0},{12,4},{16,24},{20,28},{24,16},{28,20},{1,9},{5... | collective-permute-start | bytes 208904 | tf_op jit(solution)/shard_map/ppermute | solution.py:39
  26.1 1.8 %collective-permute-done.10.refs_11_ = f32[136,128]{1,0:T(8,128)S(1)} collective-permute-done((f32[136,128]{1,0:T(8,128)S(1)}, f32[136,128]{1,0:T(8,128)S(1)}, u32[]{:S(2)}, u32[]{:S(2)}) %collective-permute-start.10) | collective-permute-done | bytes 69664 | tf_op jit(solution)/shard_map/ppermute | solution.py:39
  27.9 1.5 %collective-permute-done.9.refs_10_ = f32[136,128]{1,0:T(8,128)S(1)} collective-permute-done((f32[136,128]{1,0:T(8,128)S(1)}, f32[136,128]{1,0:T(8,128)S(1)}, u32[]{:S(2)}, u32[]{:S(2)}) %collective-permute-start.9) | collective-permute-done | bytes 69664 | tf_op jit(solution)/shard_map/ppermute | solution.py:39
  29.3 1.4 %backward.2 = (f32[520,128]{1,0:T(8,128)S(1)}, f32[520,128]{1,0:T(8,128)S(1)}, f32[32,1,128]{2,1,0:T(1,128)S(1)}) custom-call(f32[512,256]{1,0:T(8,128)S(1)} %get-tuple-element.36.refs_0_, f32[512,256]{1,0:T(8,128)S(1)} %get-tuple-element.38.refs_1_, f32[8,256]{1,0:T(8,128)S(1)} %get-tuple-element.37.refs_3_.refs_2_, ...), custom_call_target="tpu_custom_call" | custom-call | flops 603979776 | bytes 1048576 | tf_op jit(solution)/shard_map/backward/pallas_call | solution.py:85
  30.7 11.1 %all_to_all.10.refs_6_ = f32[32,1,128]{2,1,0:T(1,128)S(1)} all-to-all(f32[32,1,128]{2,1,0:T(1,128)S(1)} %get-tuple-element.50), channel_id=1, replica_groups=mesh['page'=8,'query'=2,'head'=2] {'page','query','head'}, dimensions={0} | all-to-all | bytes 32768 | tf_op jit(solution)/shard_map/all_to_all | solution.py:643
  41.8 1.1 %update_forward.1 = (f32[1368,128]{1,0:T(8,128)S(1)}, f32[136,128]{1,0:T(8,128)S(1)}, f32[136,128]{1,0:T(8,128)S(1)}, f32[136,128]{1,0:T(8,128)S(1)}, f32[136,12...) custom-call(f32[520,128]{1,0:T(8,128)S(1)} %get-tuple-element.32.refs_0_.refs_4_, ...), custom_call_target="tpu_custom_call" | custom-call | flops 402653184 | bytes 1048576 | tf_op jit(solution)/shard_map/update_forward/pallas_call | solution.py:85
  42.9 0.6 collective-permute-start.17
  43.5 0.6 collective-permute-start.11
  44.0 1.5 %collective-permute-start.12 = (f32[136,128]{1,0:T(8,128)S(1)}, f32[136,128]{1,0:T(8,128)S(1)}, u32[]{:S(2)}, u32[]{:S(2)}) collective-permute-start(f32[136,128]{1,0:T(8,128)S(1)} %get-tuple-element.56), channel_id=1, source_target_pairs={{0,16},{4,20},{8,24},{12,28},{16,0},{20,4},{24,8},{28,12},{1,17},{... | collective-permute-start | bytes 208904 | tf_op jit(solution)/shard_map/ppermute | solution.py:39
  45.5 2.4 %collective-permute-start.13 = (f32[136,128]{1,0:T(8,128)S(1)}, f32[136,128]{1,0:T(8,128)S(1)}, u32[]{:S(2)}, u32[]{:S(2)}) collective-permute-start(f32[136,128]{1,0:T(8,128)S(1)} %get-tuple-element.57), channel_id=1, source_target_pairs={{0,8},{4,12},{8,0},{12,4},{16,24},{20,28},{24,16},{28,20},{1,9},{5... | collective-permute-start | bytes 208904 | tf_op jit(solution)/shard_map/ppermute | solution.py:39
  47.9 2.5 %collective-permute-done.11.refs_3_ = f32[136,128]{1,0:T(8,128)S(1)} collective-permute-done((f32[136,128]{1,0:T(8,128)S(1)}, f32[136,128]{1,0:T(8,128)S(1)}, u32[]{:S(2)}, u32[]{:S(2)}) %collective-permute-start.11) | collective-permute-done | bytes 69664 | tf_op jit(solution)/shard_map/ppermute | solution.py:39
  50.4 1.7 %collective-permute-done.12.refs_4_ = f32[136,128]{1,0:T(8,128)S(1)} collective-permute-done((f32[136,128]{1,0:T(8,128)S(1)}, f32[136,128]{1,0:T(8,128)S(1)}, u32[]{:S(2)}, u32[]{:S(2)}) %collective-permute-start.12) | collective-permute-done | bytes 69664 | tf_op jit(solution)/shard_map/ppermute | solution.py:39
  52.1 0.1 merge.3.refs_0_
  52.2 1.2 %collective-permute-start.16 = (f32[136,128]{1,0:T(8,128)S(1)}, f32[136,128]{1,0:T(8,128)S(1)}, u32[]{:S(2)}, u32[]{:S(2)}) collective-permute-start(f32[136,128]{1,0:T(8,128)S(1)} %merge.3.refs_0_), channel_id=1, source_target_pairs={{0,24},{4,28},{8,16},{12,20},{16,8},{20,12},{24,0},{28,4},{1,25},{... | collective-permute-start | bytes 208904 | tf_op jit(solution)/shard_map/ppermute | solution.py:39
  53.4 0.4 collective-permute-start.15
  53.8 2.8 %collective-permute-start.14 = (f32[136,128]{1,0:T(8,128)S(1)}, f32[136,128]{1,0:T(8,128)S(1)}, u32[]{:S(2)}, u32[]{:S(2)}) collective-permute-start(f32[136,128]{1,0:T(8,128)S(1)} %merge.3.refs_0_), channel_id=1, source_target_pairs={{0,8},{4,12},{8,0},{12,4},{16,24},{20,28},{24,16},{28,20},{1,9},{5... | collective-permute-start | bytes 208904 | tf_op jit(solution)/shard_map/ppermute | solution.py:39
  56.6 2.4 %collective-permute-done.16.refs_3_ = f32[136,128]{1,0:T(8,128)S(1)} collective-permute-done((f32[136,128]{1,0:T(8,128)S(1)}, f32[136,128]{1,0:T(8,128)S(1)}, u32[]{:S(2)}, u32[]{:S(2)}) %collective-permute-start.16) | collective-permute-done | bytes 69664 | tf_op jit(solution)/shard_map/ppermute | solution.py:39
  59.1 1.1 %collective-permute-done.15.refs_2_ = f32[136,128]{1,0:T(8,128)S(1)} collective-permute-done((f32[136,128]{1,0:T(8,128)S(1)}, f32[136,128]{1,0:T(8,128)S(1)}, u32[]{:S(2)}, u32[]{:S(2)}) %collective-permute-start.15) | collective-permute-done | bytes 69664 | tf_op jit(solution)/shard_map/ppermute | solution.py:39
  60.2 0.1 join.1.refs_5_
  60.3 1.2 %collective-permute-start.18 = (f32[136,512]{1,0:T(8,128)S(1)}, f32[136,512]{1,0:T(8,128)S(1)}, u32[]{:S(2)}, u32[]{:S(2)}) collective-permute-start(f32[136,512]{1,0:T(8,128)S(1)} %join.1.refs_5_), channel_id=1, source_target_pairs={{0,2},{2,0},{1,3},{3,1},{4,6},{6,4},{5,7},{7,5},{8,10},{10,8},{9,1... | collective-permute-start | bytes 835592 | tf_op jit(solution)/shard_map/ppermute | solution.py:39
  61.5 1.3 %backward.3 = (f32[520,128]{1,0:T(8,128)S(1)}, f32[520,128]{1,0:T(8,128)S(1)}, f32[32,1,128]{2,1,0:T(1,128)S(1)}) custom-call(f32[512,512]{1,0:T(8,128)S(1)} %get-tuple-element.51.refs_0_, f32[8,512]{1,0:T(8,128)S(1)} %get-tuple-element.52.refs_1_, f32[1368,128]{1,0:T(8,128)S(1)} %get-tuple-element.53.refs_2_, ...), custom_call_target="tpu_custom_call" | custom-call | flops 603979776 | bytes 1048576 | tf_op jit(solution)/shard_map/backward/pallas_call | solution.py:85
  62.8 9.9 %all_to_all.11.refs_0_ = f32[32,1,128]{2,1,0:T(1,128)S(1)} all-to-all(f32[32,1,128]{2,1,0:T(1,128)S(1)} %get-tuple-element.58), channel_id=1, replica_groups=mesh['page'=8,'query'=2,'head'=2] {'page','query','head'}, dimensions={0} | all-to-all | bytes 32768 | tf_op jit(solution)/shard_map/all_to_all | solution.py:643
  72.6 1.0 %page_update.2.refs_6_ = f32[1040,128]{1,0:T(8,128)S(1)} custom-call(f32[32,1,128]{2,1,0:T(1,128)S(1)} %all_to_all.11.refs_0_, f32[520,128]{1,0:T(8,128)S(1)} %get-tuple-element.60.refs_1_, f32[1368,128]{1,0:T(8,128)S(1)} %get-tuple-element.53.refs_2_, f32[1368,128]{1,0:T(8,128)S(1)} %collective-permute-done.17.refs_3_, ...), custom_call_target="tpu_custom_call" | custom-call | flops 301989888 | bytes 1048576 | tf_op jit(solution)/shard_map/page_update/pallas_call | solution.py:85
  73.6 0.1 collective-permute-start.19
  73.7 1.0 %page_update.3.refs_0_ = f32[1040,128]{1,0:T(8,128)S(1)} custom-call(f32[32,1,128]{2,1,0:T(1,128)S(1)} %all_to_all.11.refs_0_, f32[520,128]{1,0:T(8,128)S(1)} %get-tuple-element.59.refs_1_, f32[1368,128]{1,0:T(8,128)S(1)} %get-tuple-element.53.refs_2_, f32[1368,128]{1,0:T(8,128)S(1)} %collective-permute-done.17.refs_3_, ...), custom_call_target="tpu_custom_call" | custom-call | flops 301989888 | bytes 1048576 | tf_op jit(solution)/shard_map/page_update/pallas_call | solution.py:85
  74.7 0.9 %collective-permute-done.19.refs_1_ = f32[1040,128]{1,0:T(8,128)S(1)} collective-permute-done((f32[1040,128]{1,0:T(8,128)S(1)}, f32[1040,128]{1,0:T(8,128)S(1)}, u32[]{:S(2)}, u32[]{:S(2)}) %collective-permute-start.19) | collective-permute-done | bytes 532512 | tf_op jit(solution)/shard_map/ppermute | solution.py:39
  75.6 1.0 %unpack.1 = (f32[4,256,128]{2,1,0:T(8,128)}, f32[4,256,128]{2,1,0:T(8,128)}, f32[4,256]{1,0:T(4,128)}) custom-call(f32[1040,128]{1,0:T(8,128)S(1)} %page_update.3.refs_0_, f32[1040,128]{1,0:T(8,128)S(1)} %collective-permute-done.19.refs_1_), custom_call_target="tpu_custom_call" | custom-call | flops 1048576 | bytes 1048576 | tf_op jit(solution)/shard_map/unpack/pallas_call | solution.py:85
  (23 shorter events, 0.1 us)
Async XLA Ops:
  0.6 5.2 %copy-start.3 = (f32[4,256,128]{2,1,0:T(8,128)S(1)}, f32[4,256,128]{2,1,0:T(8,128)}, u32[]{:S(2)}) copy-start(f32[4,256,128]{2,1,0:T(8,128)} %refs_4_.3) | copy-start | bytes 1572868
  0.6 5.2 %copy-start.2 = (f32[4,256,128]{2,1,0:T(8,128)S(1)}, f32[4,256,128]{2,1,0:T(8,128)}, u32[]{:S(2)}) copy-start(f32[4,256,128]{2,1,0:T(8,128)} %refs_2_.3) | copy-start | bytes 1572868
  0.7 5.2 %copy-start.1 = (f32[4,256,128]{2,1,0:T(8,128)S(1)}, f32[4,256,128]{2,1,0:T(8,128)}, u32[]{:S(2)}) copy-start(f32[4,256,128]{2,1,0:T(8,128)} %refs_1_.3) | copy-start | bytes 1572868
  0.7 5.2 %copy-start = (f32[4,256,128]{2,1,0:T(8,128)S(1)}, f32[4,256,128]{2,1,0:T(8,128)}, u32[]{:S(2)}) copy-start(f32[4,256,128]{2,1,0:T(8,128)} %refs_0_.3) | copy-start | bytes 1572868
  0.7 5.2 %copy-start.5 = (f32[4,256]{1,0:T(4,128)S(1)}, f32[4,256]{1,0:T(4,128)}, u32[]{:S(2)}) copy-start(f32[4,256]{1,0:T(4,128)} %refs_3_.3) | copy-start | bytes 12292
  0.7 5.2 %copy-start.6 = (s32[4,256]{1,0:T(4,128)S(1)}, s32[4,256]{1,0:T(4,128)}, u32[]{:S(2)}) copy-start(s32[4,256]{1,0:T(4,128)} %refs_5_.3) | copy-start | bytes 12292
  2.7 3.2 %copy-start.7 = (s32[8]{0:T(128)S(1)}, s32[8]{0:T(128)}, u32[]{:S(2)}) copy-start(s32[8]{0:T(128)} %refs_6_.3) | copy-start | bytes 100
  2.7 3.8 %collective-permute-start = (f32[520,128]{1,0:T(8,128)}, f32[520,128]{1,0:T(8,128)S(1)}, u32[]{:S(2)}, u32[]{:S(2)}) collective-permute-start(f32[520,128]{1,0:T(8,128)} %get-tuple-element.33), channel_id=1, source_target_pairs={{0,4},{4,0},{8,12},{12,8},{16,20},{20,16},{24,28},{28,24},{1,5},{5... | collective-permute-start | bytes 798728 | tf_op jit(solution)/shard_map/ppermute | solution.py:39
  3.3 8.7 %collective-permute-start.1 = (f32[328,128]{1,0:T(8,128)}, f32[328,128]{1,0:T(8,128)S(1)}, u32[]{:S(2)}, u32[]{:S(2)}) collective-permute-start(f32[328,128]{1,0:T(8,128)} %get-tuple-element.35.refs_5_), channel_id=1, source_target_pairs={{0,2},{2,0},{1,3},{3,1},{4,6},{6,4},{5,7},{7,5},{8,10},{10,8},{9,1... | collective-permute-start | bytes 503816 | tf_op jit(solution)/shard_map/ppermute | solution.py:39
  7.5 9.1 %collective-permute-start.2 = (f32[72,128]{1,0:T(8,128)S(1)}, f32[72,128]{1,0:T(8,128)S(1)}, u32[]{:S(2)}, u32[]{:S(2)}) collective-permute-start(f32[72,128]{1,0:T(8,128)S(1)} %get-tuple-element.40), channel_id=1, source_target_pairs={{0,24},{4,28},{8,16},{12,20},{16,8},{20,12},{24,0},{28,4},{1,25},{... | collective-permute-start | bytes 110600 | tf_op jit(solution)/shard_map/ppermute | solution.py:39
  11.2 6.2 %collective-permute-start.3 = (f32[72,128]{1,0:T(8,128)S(1)}, f32[72,128]{1,0:T(8,128)S(1)}, u32[]{:S(2)}, u32[]{:S(2)}) collective-permute-start(f32[72,128]{1,0:T(8,128)S(1)} %get-tuple-element.41), channel_id=1, source_target_pairs={{0,16},{4,20},{8,24},{12,28},{16,0},{20,4},{24,8},{28,12},{1,17},{... | collective-permute-start | bytes 110600 | tf_op jit(solution)/shard_map/ppermute | solution.py:39
  11.2 6.2 %collective-permute-start.4 = (f32[72,128]{1,0:T(8,128)S(1)}, f32[72,128]{1,0:T(8,128)S(1)}, u32[]{:S(2)}, u32[]{:S(2)}) collective-permute-start(f32[72,128]{1,0:T(8,128)S(1)} %get-tuple-element.42), channel_id=1, source_target_pairs={{0,8},{4,12},{8,0},{12,4},{16,24},{20,28},{24,16},{28,20},{1,9},{5... | collective-permute-start | bytes 110600 | tf_op jit(solution)/shard_map/ppermute | solution.py:39
  12.9 5.9 %collective-permute-start.5 = (f32[72,128]{1,0:T(8,128)S(1)}, f32[72,128]{1,0:T(8,128)S(1)}, u32[]{:S(2)}, u32[]{:S(2)}) collective-permute-start(f32[72,128]{1,0:T(8,128)S(1)} %get-tuple-element.44), channel_id=1, source_target_pairs={{0,24},{4,28},{8,16},{12,20},{16,8},{20,12},{24,0},{28,4},{1,25},{... | collective-permute-start | bytes 110600 | tf_op jit(solution)/shard_map/ppermute | solution.py:39
  16.6 4.9 %collective-permute-start.6 = (f32[72,128]{1,0:T(8,128)S(1)}, f32[72,128]{1,0:T(8,128)S(1)}, u32[]{:S(2)}, u32[]{:S(2)}) collective-permute-start(f32[72,128]{1,0:T(8,128)S(1)} %get-tuple-element.45), channel_id=1, source_target_pairs={{0,16},{4,20},{8,24},{12,28},{16,0},{20,4},{24,8},{28,12},{1,17},{... | collective-permute-start | bytes 110600 | tf_op jit(solution)/shard_map/ppermute | solution.py:39
  16.6 4.9 %collective-permute-start.7 = (f32[72,128]{1,0:T(8,128)S(1)}, f32[72,128]{1,0:T(8,128)S(1)}, u32[]{:S(2)}, u32[]{:S(2)}) collective-permute-start(f32[72,128]{1,0:T(8,128)S(1)} %get-tuple-element.46), channel_id=1, source_target_pairs={{0,8},{4,12},{8,0},{12,4},{16,24},{20,28},{24,16},{28,20},{1,9},{5... | collective-permute-start | bytes 110600 | tf_op jit(solution)/shard_map/ppermute | solution.py:39
  21.7 6.2 %collective-permute-start.10 = (f32[136,128]{1,0:T(8,128)S(1)}, f32[136,128]{1,0:T(8,128)S(1)}, u32[]{:S(2)}, u32[]{:S(2)}) collective-permute-start(f32[136,128]{1,0:T(8,128)S(1)} %merge.2.refs_8_), channel_id=1, source_target_pairs={{0,24},{4,28},{8,16},{12,20},{16,8},{20,12},{24,0},{28,4},{1,25},{... | collective-permute-start | bytes 208904 | tf_op jit(solution)/shard_map/ppermute | solution.py:39
  23.2 6.1 %collective-permute-start.9 = (f32[136,128]{1,0:T(8,128)S(1)}, f32[136,128]{1,0:T(8,128)S(1)}, u32[]{:S(2)}, u32[]{:S(2)}) collective-permute-start(f32[136,128]{1,0:T(8,128)S(1)} %merge.2.refs_8_), channel_id=1, source_target_pairs={{0,16},{4,20},{8,24},{12,28},{16,0},{20,4},{24,8},{28,12},{1,17},{... | collective-permute-start | bytes 208904 | tf_op jit(solution)/shard_map/ppermute | solution.py:39
  23.8 5.5 %collective-permute-start.8 = (f32[136,128]{1,0:T(8,128)S(1)}, f32[136,128]{1,0:T(8,128)S(1)}, u32[]{:S(2)}, u32[]{:S(2)}) collective-permute-start(f32[136,128]{1,0:T(8,128)S(1)} %merge.2.refs_8_), channel_id=1, source_target_pairs={{0,8},{4,12},{8,0},{12,4},{16,24},{20,28},{24,16},{28,20},{1,9},{5... | collective-permute-start | bytes 208904 | tf_op jit(solution)/shard_map/ppermute | solution.py:39
  42.9 29.7 %collective-permute-start.17 = (f32[1368,128]{1,0:T(8,128)S(1)}, f32[1368,128]{1,0:T(8,128)S(1)}, u32[]{:S(2)}, u32[]{:S(2)}) collective-permute-start(f32[1368,128]{1,0:T(8,128)S(1)} %get-tuple-element.53.refs_2_), channel_id=1, source_target_pairs={{0,2},{2,0},{1,3},{3,1},{4,6},{6,4},{5,7},{7,5},{8,10},{10,8},{9,1... | collective-permute-start | bytes 2101256 | tf_op jit(solution)/shard_map/ppermute | solution.py:39
  43.5 6.9 %collective-permute-start.11 = (f32[136,128]{1,0:T(8,128)S(1)}, f32[136,128]{1,0:T(8,128)S(1)}, u32[]{:S(2)}, u32[]{:S(2)}) collective-permute-start(f32[136,128]{1,0:T(8,128)S(1)} %get-tuple-element.55), channel_id=1, source_target_pairs={{0,24},{4,28},{8,16},{12,20},{16,8},{20,12},{24,0},{28,4},{1,25},{... | collective-permute-start | bytes 208904 | tf_op jit(solution)/shard_map/ppermute | solution.py:39
  44.0 8.0 %collective-permute-start.12 = (f32[136,128]{1,0:T(8,128)S(1)}, f32[136,128]{1,0:T(8,128)S(1)}, u32[]{:S(2)}, u32[]{:S(2)}) collective-permute-start(f32[136,128]{1,0:T(8,128)S(1)} %get-tuple-element.56), channel_id=1, source_target_pairs={{0,16},{4,20},{8,24},{12,28},{16,0},{20,4},{24,8},{28,12},{1,17},{... | collective-permute-start | bytes 208904 | tf_op jit(solution)/shard_map/ppermute | solution.py:39
  45.5 6.5 %collective-permute-start.13 = (f32[136,128]{1,0:T(8,128)S(1)}, f32[136,128]{1,0:T(8,128)S(1)}, u32[]{:S(2)}, u32[]{:S(2)}) collective-permute-start(f32[136,128]{1,0:T(8,128)S(1)} %get-tuple-element.57), channel_id=1, source_target_pairs={{0,8},{4,12},{8,0},{12,4},{16,24},{20,28},{24,16},{28,20},{1,9},{5... | collective-permute-start | bytes 208904 | tf_op jit(solution)/shard_map/ppermute | solution.py:39
  52.2 6.9 %collective-permute-start.16 = (f32[136,128]{1,0:T(8,128)S(1)}, f32[136,128]{1,0:T(8,128)S(1)}, u32[]{:S(2)}, u32[]{:S(2)}) collective-permute-start(f32[136,128]{1,0:T(8,128)S(1)} %merge.3.refs_0_), channel_id=1, source_target_pairs={{0,24},{4,28},{8,16},{12,20},{16,8},{20,12},{24,0},{28,4},{1,25},{... | collective-permute-start | bytes 208904 | tf_op jit(solution)/shard_map/ppermute | solution.py:39
  53.4 6.8 %collective-permute-start.15 = (f32[136,128]{1,0:T(8,128)S(1)}, f32[136,128]{1,0:T(8,128)S(1)}, u32[]{:S(2)}, u32[]{:S(2)}) collective-permute-start(f32[136,128]{1,0:T(8,128)S(1)} %merge.3.refs_0_), channel_id=1, source_target_pairs={{0,16},{4,20},{8,24},{12,28},{16,0},{20,4},{24,8},{28,12},{1,17},{... | collective-permute-start | bytes 208904 | tf_op jit(solution)/shard_map/ppermute | solution.py:39
  53.8 6.4 %collective-permute-start.14 = (f32[136,128]{1,0:T(8,128)S(1)}, f32[136,128]{1,0:T(8,128)S(1)}, u32[]{:S(2)}, u32[]{:S(2)}) collective-permute-start(f32[136,128]{1,0:T(8,128)S(1)} %merge.3.refs_0_), channel_id=1, source_target_pairs={{0,8},{4,12},{8,0},{12,4},{16,24},{20,28},{24,16},{28,20},{1,9},{5... | collective-permute-start | bytes 208904 | tf_op jit(solution)/shard_map/ppermute | solution.py:39
  60.3 12.3 %collective-permute-start.18 = (f32[136,512]{1,0:T(8,128)S(1)}, f32[136,512]{1,0:T(8,128)S(1)}, u32[]{:S(2)}, u32[]{:S(2)}) collective-permute-start(f32[136,512]{1,0:T(8,128)S(1)} %join.1.refs_5_), channel_id=1, source_target_pairs={{0,2},{2,0},{1,3},{3,1},{4,6},{6,4},{5,7},{7,5},{8,10},{10,8},{9,1... | collective-permute-start | bytes 835592 | tf_op jit(solution)/shard_map/ppermute | solution.py:39
  61.5 11.1 %copy-start.4 = (f32[328,128]{1,0:T(8,128)S(1)}, f32[328,128]{1,0:T(8,128)}, u32[]{:S(2)}) copy-start(f32[328,128]{1,0:T(8,128)} %get-tuple-element.35.refs_5_) | copy-start | bytes 503812
  73.6 2.0 %collective-permute-start.19 = (f32[1040,128]{1,0:T(8,128)S(1)}, f32[1040,128]{1,0:T(8,128)S(1)}, u32[]{:S(2)}, u32[]{:S(2)}) collective-permute-start(f32[1040,128]{1,0:T(8,128)S(1)} %page_update.2.refs_6_), channel_id=1, source_target_pairs={{0,4},{4,0},{8,12},{12,8},{16,20},{20,16},{24,28},{28,24},{1,5},{5... | collective-permute-start | bytes 1597448 | tf_op jit(solution)/shard_map/ppermute | solution.py:39

commit v20 on v19

--- a/solution.py
+++ b/solution.py
@@ -88,7 +88,7 @@
         in_specs=[pl.BlockSpec(memory_space=space) for space in spaces],
         out_specs=[pl.BlockSpec(memory_space=pltpu.VMEM) for _ in out_shapes],
         scratch_shapes=scratch,
-        compiler_params=pltpu.CompilerParams(vmem_limit_bytes=vmem * 2**20),
+        compiler_params=pltpu.CompilerParams(vmem_limit_bytes=int(vmem * 2**20)),
         cost_estimate=pl.CostEstimate(flops=cost, bytes_accessed=2**20, transcendentals=0),
         name=name,
     )(*operands, *after)
@@ -133,6 +133,8 @@
     if local_heads != CORES * query_devices:
         return False
     ranks = pages // CORES
+    if ranks < 4 or query_devices != 2:
+        return False
     chunk = part_rows * query_devices // ranks
     return (
         part_rows * query_devices % ranks == 0
@@ -174,12 +176,8 @@
         masks = {axis: mask for axis, mask in masks.items() if mask}
         return exchange(value, **masks) if masks else value
 
-    def pack_queries(head, rank, queries, targets, out):
-        rows = pl.ds(pl.multiple_of(rank * piece, piece), piece)
-        return [
-            (queries.at[head], out.at[pl.ds(0, part_rows)]),
-            (targets.at[head, rows], out.at[pl.ds(part_rows, piece)]),
-        ]
+    def target_rows(head, rank, targets, out):
+        return (targets.at[head, pl.ds(pl.multiple_of(rank * piece, piece), piece)], out)
 
     def pack_state(head, keys, values, out):
         return [
@@ -206,87 +204,79 @@
             [tail[: TAIL - 1], jnp.full((1, width), page_start, jnp.float32)], axis=0
         )
 
-    def send_body(
-        queries, keys, values, biases, targets, positions, assignment, state_out, *refs
+    def send_body(queries, keys, values, state_out, *refs):
+        query_outs, (sems,) = refs[: query_devices - 1], refs[query_devices - 1 :]
+        _, core, me = places()
+        copies = [
+            (queries.at[CORES * (me ^ turn) + core], out) for turn, out in enumerate(query_outs, 1)
+        ]
+        copies += pack_state(CORES * me + (core ^ 1), keys, values, state_out)
+        for copy in start_all(copies, sems):
+            copy.wait()
+
+    def own_body(
+        queries, keys, values, biases, targets, positions, assignment, state_out, query_out,
+        mate_tail_out, *refs
     ):
-        query_outs = refs[: query_devices - 1]
-        bias_ref, positions_ref, assignment_ref, sems = refs[query_devices - 1 :]
+        rest_outs, refs = refs[: query_devices - 1], refs[query_devices - 1 :]
+        bias_ref, positions_ref, assignment_ref, sems = refs
         rank, core, me = places()
-        heads = [CORES * (me ^ turn) + core for turn in range(1, query_devices)]
-        mate_head = CORES * me + (core ^ 1)
+        head, page = CORES * me + core, CORES * rank + core
         small = start_all(
             [(assignment, assignment_ref), (positions, positions_ref), (biases, bias_ref)], sems
         )
-        copies = pack_state(mate_head, keys, values, state_out)
-        for head, out in zip(heads, query_outs):
-            copies += pack_queries(head, rank, queries, targets, out)
+        copies = pack_state(head, keys, values, state_out)
+        copies.append((queries.at[head], query_out.at[pl.ds(0, part_rows)]))
+        copies.append(target_rows(head, rank, targets, query_out.at[pl.ds(part_rows, piece)]))
+        for turn, out in enumerate(rest_outs, 1):
+            other = CORES * (me ^ turn) + core
+            copies.append(target_rows(other, rank, targets, out.at[pl.ds(0, piece)]))
         copies = start_all(copies, sems, 3)
         for copy in small:
             copy.wait()
-        state_out[2 * slot_rows :, :] = state_tail(
-            mate_head, CORES * rank + core, bias_ref, assignment_ref
-        )
-        for head, out in zip(heads, query_outs):
-            out[part_rows + piece :, :] = position_tail(head, positions_ref)
+        state_out[2 * slot_rows :, :] = state_tail(head, page, bias_ref, assignment_ref)
+        mate_tail_out[...] = state_tail(head ^ 1, page, bias_ref, assignment_ref)
+        query_out[part_rows + piece :, :] = position_tail(head, positions_ref)
+        for turn, out in enumerate(rest_outs, 1):
+            other = CORES * (me ^ turn) + core
+            out[piece:, :] = position_tail(other, positions_ref)
         for copy in copies:
             copy.wait()
 
-    def own_body(
-        queries, keys, values, biases, targets, positions, assignment, state_out, query_out, *refs
-    ):
-        bias_ref, positions_ref, assignment_ref, sems = refs
-        rank, core, me = places()
-        head = CORES * me + core
-        small = start_all(
-            [(assignment, assignment_ref), (positions, positions_ref), (biases, bias_ref)], sems
-        )
-        copies = pack_state(head, keys, values, state_out)
-        copies += pack_queries(head, rank, queries, targets, query_out)
-        copies = start_all(copies, sems, 3)
-        for copy in small:
-            copy.wait()
-        state_out[2 * slot_rows :, :] = state_tail(
-            head, CORES * rank + core, bias_ref, assignment_ref
-        )
-        query_out[part_rows + piece :, :] = position_tail(head, positions_ref)
-        for copy in copies:
-            copy.wait()
-
     state_shape, query_shape = (packed_rows, width), (part_rows + piece + TAIL, width)
-    small_scratch = [
-        pltpu.VMEM(slot_bias.shape, jnp.float32),
-        pltpu.VMEM(positions.shape, jnp.int32),
-        pltpu.SMEM(assignment.shape, jnp.int32),
-    ]
-    arguments = [
-        queries, compact_keys, compact_values, slot_bias, targets, positions, assignment
-    ]
-    mate_state, *sent_queries = call(
+    rest_shape = (piece + TAIL, width)
+    mate_slots, *sent_queries = call(
         send_body,
-        [state_shape] + [query_shape] * (query_devices - 1),
+        [(2 * slot_rows, width)] + [(part_rows, width)] * (query_devices - 1),
         "pack",
         2**20,
-        arguments,
-        small_scratch + [pltpu.SemaphoreType.DMA((3 + 2 * query_devices,))],
+        [queries, compact_keys, compact_values],
+        [pltpu.SemaphoreType.DMA((query_devices + 1,))],
+        after=[slot_bias, targets, positions, assignment],
         space=pl.ANY,
         vmem=60,
     )
-    own_state, own_queries = call(
+    own_state, own_queries, mate_tail, *sent_rests = call(
         own_body,
-        [state_shape, query_shape],
+        [state_shape, query_shape, (TAIL, width)] + [rest_shape] * (query_devices - 1),
         "own",
         2**24,
-        arguments,
-        small_scratch + [pltpu.SemaphoreType.DMA((7,))],
+        [queries, compact_keys, compact_values, slot_bias, targets, positions, assignment],
+        [
+            pltpu.VMEM(slot_bias.shape, jnp.float32),
+            pltpu.VMEM(positions.shape, jnp.int32),
+            pltpu.SMEM(assignment.shape, jnp.int32),
+            pltpu.SemaphoreType.DMA((6 + query_devices,)),
+        ],
         space=pl.ANY,
     )
-    packs = [own_queries] + list(sent_queries)
-
-    def query_part(turn, part):
-        return to_device(packs[part], query=turn ^ part)
-
-    query_parts = [query_part(0, part) for part in range(query_devices)]
-    states = [own_state, exchange(mate_state, page=1)]
+    arrived_queries = [
+        exchange(sent_queries[turn - 1], query=turn) for turn in range(1, query_devices)
+    ]
+    arrived_rests = [
+        exchange(sent_rests[turn - 1], query=turn) for turn in range(1, query_devices)
+    ]
+    mate_parts = [exchange(mate_slots, page=1), exchange(mate_tail, page=1)]
 
     def in_columns(parts, axis):
         return jnp.concatenate(
@@ -390,9 +380,31 @@
         empty = jnp.zeros((TAIL - len(rows), columns), jnp.float32)
         return jnp.concatenate(rows + [empty], axis=0)
 
-    def part_body(*refs):
-        state_refs, (query_ref, *refs) = refs[:CORES], refs[CORES:]
-        piece_outs, (weights_out, max_out, pieces) = refs[:ranks], refs[ranks:]
+    def part_body(part):
+        def body(own_ref, *refs):
+            if part:
+                (mate_ref, query_rows_ref, rest_ref), refs = refs[:3], refs[3:]
+            else:
+                (slots_ref, tail_ref, query_ref), refs = refs[:3], refs[3:]
+            before_refs, refs = refs[: len(before)], refs[len(before) :]
+            piece_outs, (weights_out, max_out, joined_out, pieces) = refs[:ranks], refs[ranks:]
+            if part:
+                query_ref = joined_out
+                query_ref[:part_rows, :] = query_rows_ref[...]
+                query_ref[part_rows:, :] = rest_ref[...]
+            else:
+                mate_ref = joined_out
+                mate_ref[: 2 * slot_rows, :] = slots_ref[...]
+                mate_ref[2 * slot_rows :, :] = tail_ref[...]
+            part_forward(
+                [own_ref, mate_ref], query_ref, before_refs, piece_outs, weights_out, max_out, pieces
+            )
+
+        return body
+
+    def part_forward(
+        state_refs, query_ref, before_refs, piece_outs, weights_out, max_out, pieces
+    ):
         rank, _, _ = places()
         queries = halves(query_ref[:part_rows, :])
         position_row = tail_as_row(query_ref, part_rows + piece, pos_rows)
@@ -419,10 +431,12 @@
             pieces[at, folded:, :] = rows_tail(
                 [jnp.concatenate([row[:, own]] * fold, axis=1) for row in (row_max, row_total)]
             )
-        for turn in range(ranks):
-            piece_outs[turn][...] = pieces[rank ^ turn]
-
-    part_shapes = [piece_shape] * ranks + [(slots, part_rows), (TAIL, part_rows)]
+        for turn, out in enumerate(piece_outs):
+            out[out.shape[0] - piece_shape[0] :, :] = pieces[rank ^ turn]
+        for at, ref in enumerate(before_refs):
+            out, first = piece_outs[1 + at % (ranks - 2)], at // (ranks - 2) * piece_shape[0]
+            out[first : first + piece_shape[0], :] = ref[...]
+
 
     def next_body(*refs):
         state_refs, refs = refs[:2], refs[2:]
@@ -461,12 +475,18 @@
 
     def first_merge_body(*refs):
         query_refs, (*piece_refs, merged_out) = refs[:query_devices], refs[query_devices:]
+        single, joint = piece_refs[: 2 * query_devices], piece_refs[2 * query_devices :]
+        groups = [single[0::2], single[1::2]]
+        for ref in joint:
+            groups.append(
+                [
+                    ref.at[pl.ds(part * piece_shape[0], piece_shape[0])]
+                    for part in range(query_devices)
+                ]
+            )
 
         def joined(read):
-            return [
-                jnp.concatenate([read(ref) for ref in piece_refs[turn::ranks]], axis=1)
-                for turn in range(ranks)
-            ]
+            return [jnp.concatenate([read(ref) for ref in group], axis=1) for group in groups]
 
         merged_chunk(
             query_refs,
@@ -560,12 +580,17 @@
             state = read_pack(part_of(own_state_ref, at))
             store_pack(part_of(out, 0), updated(state, read_pack(grad_ref), sizes))
             for turn, (state_ref, joined_ref) in enumerate(zip(state_refs, joined_refs), 1):
-                query_refs = [state_ref.at[pl.ds(CORES * packed_rows, query_shape[0])]]
-                query_refs += pack_refs[(turn - 1) * (query_devices - 1) :][: query_devices - 1]
+                query_ref = state_ref.at[pl.ds(CORES * packed_rows, query_shape[0])]
+                rows_ref, rest_ref = pack_refs[2 * turn - 2 : 2 * turn]
+                query_rows = [query_ref[:part_rows, :], rows_ref[...]]
+                positions = [
+                    tail_as_row(query_ref, part_rows + piece, pos_rows),
+                    tail_as_row(rest_ref, piece, pos_rows),
+                ]
                 residual, row_max, row_total, row_delta = split_merged(joined_ref[...])
-                all_queries = read_queries(query_refs)
+                all_queries = halves(in_columns(query_rows, 0))
                 ref = part_of(state_ref, at)
-                scores, visible = page_scores(ref, all_queries, read_positions(query_refs))
+                scores, visible = page_scores(ref, all_queries, in_columns(positions, 1))
                 weights = jnp.where(visible, jnp.exp(scores - row_max), 0.0)
                 grads = page_gradients(
                     weights, 1.0 / row_total, ref, all_queries, residual, row_delta
@@ -577,24 +602,39 @@
     for repeat in range(STEPS):
         last = repeat == STEPS - 1
         if repeat == 0:
-            sums, weights, maxima = [], [], []
-            for query_pack in query_parts:
-                *pieces, part_weights, part_max = call(
-                    part_body,
-                    part_shapes,
+            sums, weights, maxima, nearer, far = [], [], [], [], []
+            for part in range(query_devices):
+                before = nearer if part == query_devices - 1 else []
+                joined_rows = 1 + len(before) // (ranks - 2)
+                near_shape = (joined_rows * piece_shape[0], columns)
+                if part:
+                    inputs = [states[1], arrived_queries[part - 1], arrived_rests[part - 1]]
+                else:
+                    inputs = mate_parts + [own_queries]
+                *pieces, part_weights, part_max, joined = call(
+                    part_body(part),
+                    [piece_shape]
+                    + [near_shape] * (ranks - 2)
+                    + [piece_shape, (slots, part_rows), (TAIL, part_rows)]
+                    + [query_shape if part else state_shape],
                     "forward",
                     2 * matmul_cost // query_devices,
-                    states + [query_pack],
+                    [own_state] + inputs + before,
                     piece_scratch,
-                    after=maxima[-1:],
+                    after=maxima[-1:] + far,
                 )
-                arrived = {
-                    turn: exchange(pieces[turn], page=CORES * turn)
-                    for turn in reversed(range(1, ranks))
-                }
-                sums += list(arrived.values()) + pieces[:1]
+                if part:
+                    query_parts.append(joined)
+                else:
+                    states, query_parts = [own_state, joined], [own_queries]
+                far = [exchange(pieces[-1], page=CORES * (ranks - 1))]
+                nearer = nearer + pieces[1:-1]
+                sums += [pieces[0]] + far
                 weights.append(part_weights)
                 maxima.append(part_max)
+            sums += [
+                exchange(pieces[turn], page=CORES * turn) for turn in reversed(range(1, ranks - 1))
+            ]
         else:
             new_state, *chunk_parts, part_weights, part_max = call(
                 next_body,
@@ -646,9 +686,7 @@
         ]
 
     other_packs = [
-        packs[part] if part == turn else query_part(turn, part)
-        for turn in range(1, query_devices)
-        for part in range(1, query_devices)
+        part for turn in range(1, query_devices) for part in (sent_queries[turn - 1], sent_rests[turn - 1])
     ]
     operands = new_states + all_joined[1:] + other_packs
     pages = []

time: 76.9 us -> 80.1 us (1.042)
  waiting for transfers between devices: 16 us -> 20.1 us
    ppermute x20, waiting for transfers between devices: 16 us -> 20.1 us  [exchange(): return lax.ppermute(value, axes, pairs)]
  transfers between devices with their start and end apart: 20 -> 20, of which waited for: 9 -> 10; matrix products, arithmetic and copies ran while one was open for 0% -> 0% of each run, Pallas kernels for 6% -> 5%
where the time goes in v20:
time: 80.1 us; the launch traced here: 80 us
  starting transfers between devices  27 us (34%)
  blocking collectives  20.3 us (25%)
  waiting for transfers between devices  20.1 us (25%)
  Pallas kernels  11.8 us (15%)
  between operations  0.81 us (1%)
    ppermute x20, starting transfers between devices, exchange(): return lax.ppermute(value, axes, pairs)  27 us
    all_to_all x2, blocking collectives, direct_per_device(): lax.all_to_all(squares, ('page', 'query', 'head'), split_axis=0, concat_a...  20.3 us
    ppermute x20, waiting for transfers between devices, exchange(): return lax.ppermute(value, axes, pairs)  20.1 us
    pallas_call x13, Pallas kernels, call(): pl.pallas_call(without_after, out_shape=[jax.ShapeDtypeStruct(shape, jnp....  11.8 us
  transfers between devices with their start and end apart: 20, of which 10 were waited for; matrix products, arithmetic and copies ran while one was open for 0% of the time, Pallas kernels for 5%

profile of v20, /device:TPU:0, one launch (start us, length us, event | category | flops | bytes accessed | tf_op | source)
XLA Modules:
  0.0 80.0 jit_solution(10063722444072917573)
XLA Ops:
  0.7 1.9 %pack.1 = (f32[512,128]{1,0:T(8,128)}, f32[256,128]{1,0:T(8,128)}) custom-call(f32[4,256,128]{2,1,0:T(8,128)} %refs_0_.3, f32[4,256,128]{2,1,0:T(8,128)} %refs_1_.3, f32[4,256,128]{2,1,0:T(8,128)} %refs_2_.3, f32[4,256]{1,0:T(4,128)} %refs_3_.3, f32[4,256,128]{2,1,0:T(8,128)} %refs_4_.3, s32[4,256]{1,0:T(4,128)} %refs_5_.3, s32[8]{0:T(128)} %refs_6_.3), custom_call_target="tpu_custom_call" | custom-call | flops 1048576 | bytes 1048576 | tf_op jit(solution)/shard_map/pack/pallas_call | solution.py:85
  2.6 0.0 copy-start.7
  2.7 0.5 collective-permute-start
  3.2 2.6 %collective-permute-start.2 = (f32[256,128]{1,0:T(8,128)}, f32[256,128]{1,0:T(8,128)S(1)}, u32[]{:S(2)}, u32[]{:S(2)}) collective-permute-start(f32[256,128]{1,0:T(8,128)} %get-tuple-element.41.refs_5_), channel_id=1, source_target_pairs={{0,2},{2,0},{1,3},{3,1},{4,6},{6,4},{5,7},{7,5},{8,10},{10,8},{9,1... | collective-permute-start | bytes 393224 | tf_op jit(solution)/shard_map/ppermute | solution.py:39
  5.8 0.7 own.1
  6.5 0.2 collective-permute-start.1
  6.8 0.3 collective-permute-start.3
  7.1 0.7 collective-permute-done.1.refs_2_
  7.8 0.0 collective-permute-done.refs_1_
  7.8 0.9 %forward.2 = (f32[72,128]{1,0:T(8,128)S(1)}, f32[72,128]{1,0:T(8,128)S(1)}, f32[72,128]{1,0:T(8,128)S(1)}, f32[72,128]{1,0:T(8,128)S(1)}, f32[512,256]{1,0:T(8,1...) custom-call(f32[520,128]{1,0:T(8,128)S(1)} %get-tuple-element.36.refs_0_.refs_4_, ...), custom_call_target="tpu_custom_call" | custom-call | flops 201326592 | bytes 1048576 | tf_op jit(solution)/shard_map/forward/pallas_call | solution.py:85
  8.7 3.7 %collective-permute-start.4 = (f32[72,128]{1,0:T(8,128)S(1)}, f32[72,128]{1,0:T(8,128)S(1)}, u32[]{:S(2)}, u32[]{:S(2)}) collective-permute-start(f32[72,128]{1,0:T(8,128)S(1)} %get-tuple-element.46), channel_id=1, source_target_pairs={{0,24},{4,28},{8,16},{12,20},{16,8},{20,12},{24,0},{28,4},{1,25},{... | collective-permute-start | bytes 110600 | tf_op jit(solution)/shard_map/ppermute | solution.py:39
  12.4 2.1 %collective-permute-done.4.refs_7_.refs_3_ = f32[72,128]{1,0:T(8,128)S(1)} collective-permute-done((f32[72,128]{1,0:T(8,128)S(1)}, f32[72,128]{1,0:T(8,128)S(1)}, u32[]{:S(2)}, u32[]{:S(2)}) %collective-permute-start.4) | collective-permute-done | bytes 36896 | tf_op jit(solution)/shard_map/ppermute | solution.py:39
  14.5 0.9 %forward.3 = (f32[72,128]{1,0:T(8,128)S(1)}, f32[144,128]{1,0:T(8,128)S(1)}, f32[144,128]{1,0:T(8,128)S(1)}, f32[72,128]{1,0:T(8,128)S(1)}, f32[512,256]{1,0:T(8...) custom-call(f32[520,128]{1,0:T(8,128)S(1)} %get-tuple-element.36.refs_0_.refs_4_, ...), custom_call_target="tpu_custom_call" | custom-call | flops 201326592 | bytes 1048576 | tf_op jit(solution)/shard_map/forward/pallas_call | solution.py:85
  15.5 0.9 %collective-permute-start.6 = (f32[144,128]{1,0:T(8,128)S(1)}, f32[144,128]{1,0:T(8,128)S(1)}, u32[]{:S(2)}, u32[]{:S(2)}) collective-permute-start(f32[144,128]{1,0:T(8,128)S(1)} %get-tuple-element.54), channel_id=1, source_target_pairs={{0,16},{4,20},{8,24},{12,28},{16,0},{20,4},{24,8},{28,12},{1,17},{... | collective-permute-start | bytes 221192 | tf_op jit(solution)/shard_map/ppermute | solution.py:39
  16.3 3.4 %collective-permute-start.7 = (f32[144,128]{1,0:T(8,128)S(1)}, f32[144,128]{1,0:T(8,128)S(1)}, u32[]{:S(2)}, u32[]{:S(2)}) collective-permute-start(f32[144,128]{1,0:T(8,128)S(1)} %get-tuple-element.55), channel_id=1, source_target_pairs={{0,8},{4,12},{8,0},{12,4},{16,24},{20,28},{24,16},{28,20},{1,9},{5... | collective-permute-start | bytes 221192 | tf_op jit(solution)/shard_map/ppermute | solution.py:39
  19.7 0.2 collective-permute-start.5
  19.9 5.6 %collective-permute-done.5.refs_5_ = f32[72,128]{1,0:T(8,128)S(1)} collective-permute-done((f32[72,128]{1,0:T(8,128)S(1)}, f32[72,128]{1,0:T(8,128)S(1)}, u32[]{:S(2)}, u32[]{:S(2)}) %collective-permute-start.5) | collective-permute-done | bytes 36896 | tf_op jit(solution)/shard_map/ppermute | solution.py:39
  25.5 0.0 collective-permute-done.6.refs_6_
  25.6 0.0 collective-permute-done.7.refs_7_
  25.6 0.3 merge.2.refs_8_
  25.8 0.7 collective-permute-start.10
  26.6 3.7 %collective-permute-start.8 = (f32[136,128]{1,0:T(8,128)S(1)}, f32[136,128]{1,0:T(8,128)S(1)}, u32[]{:S(2)}, u32[]{:S(2)}) collective-permute-start(f32[136,128]{1,0:T(8,128)S(1)} %merge.2.refs_8_), channel_id=1, source_target_pairs={{0,8},{4,12},{8,0},{12,4},{16,24},{20,28},{24,16},{28,20},{1,9},{5... | collective-permute-start | bytes 208904 | tf_op jit(solution)/shard_map/ppermute | solution.py:39
  30.3 1.8 %collective-permute-done.10.refs_11_ = f32[136,128]{1,0:T(8,128)S(1)} collective-permute-done((f32[136,128]{1,0:T(8,128)S(1)}, f32[136,128]{1,0:T(8,128)S(1)}, u32[]{:S(2)}, u32[]{:S(2)}) %collective-permute-start.10) | collective-permute-done | bytes 69664 | tf_op jit(solution)/shard_map/ppermute | solution.py:39
  32.1 1.1 %collective-permute-done.9.refs_10_ = f32[136,128]{1,0:T(8,128)S(1)} collective-permute-done((f32[136,128]{1,0:T(8,128)S(1)}, f32[136,128]{1,0:T(8,128)S(1)}, u32[]{:S(2)}, u32[]{:S(2)}) %collective-permute-start.9) | collective-permute-done | bytes 69664 | tf_op jit(solution)/shard_map/ppermute | solution.py:39
  33.3 1.4 %backward.2 = (f32[520,128]{1,0:T(8,128)S(1)}, f32[520,128]{1,0:T(8,128)S(1)}, f32[32,1,128]{2,1,0:T(1,128)S(1)}) custom-call(f32[512,256]{1,0:T(8,128)S(1)} %get-tuple-element.48.refs_0_, f32[512,256]{1,0:T(8,128)S(1)} %get-tuple-element.49.refs_1_, f32[8,256]{1,0:T(8,128)S(1)} %get-tuple-element.45.refs_6_.refs_2_, ...), custom_call_target="tpu_custom_call" | custom-call | flops 603979776 | bytes 1048576 | tf_op jit(solution)/shard_map/backward/pallas_call | solution.py:85
  34.7 10.4 %all_to_all.10.refs_6_ = f32[32,1,128]{2,1,0:T(1,128)S(1)} all-to-all(f32[32,1,128]{2,1,0:T(1,128)S(1)} %get-tuple-element.58), channel_id=1, replica_groups=mesh['page'=8,'query'=2,'head'=2] {'page','query','head'}, dimensions={0} | all-to-all | bytes 32768 | tf_op jit(solution)/shard_map/all_to_all | solution.py:683
  45.1 1.1 %update_forward.1 = (f32[1368,128]{1,0:T(8,128)S(1)}, f32[136,128]{1,0:T(8,128)S(1)}, f32[136,128]{1,0:T(8,128)S(1)}, f32[136,128]{1,0:T(8,128)S(1)}, f32[136,12...) custom-call(f32[520,128]{1,0:T(8,128)S(1)} %get-tuple-element.36.refs_0_.refs_4_, ...), custom_call_target="tpu_custom_call" | custom-call | flops 402653184 | bytes 1048576 | tf_op jit(solution)/shard_map/update_forward/pallas_call | solution.py:85
  46.2 0.6 collective-permute-start.17
  46.8 0.6 collective-permute-start.11
  47.3 1.5 %collective-permute-start.12 = (f32[136,128]{1,0:T(8,128)S(1)}, f32[136,128]{1,0:T(8,128)S(1)}, u32[]{:S(2)}, u32[]{:S(2)}) collective-permute-start(f32[136,128]{1,0:T(8,128)S(1)} %get-tuple-element.64), channel_id=1, source_target_pairs={{0,16},{4,20},{8,24},{12,28},{16,0},{20,4},{24,8},{28,12},{1,17},{... | collective-permute-start | bytes 208904 | tf_op jit(solution)/shard_map/ppermute | solution.py:39
  48.8 2.4 %collective-permute-start.13 = (f32[136,128]{1,0:T(8,128)S(1)}, f32[136,128]{1,0:T(8,128)S(1)}, u32[]{:S(2)}, u32[]{:S(2)}) collective-permute-start(f32[136,128]{1,0:T(8,128)S(1)} %get-tuple-element.65), channel_id=1, source_target_pairs={{0,8},{4,12},{8,0},{12,4},{16,24},{20,28},{24,16},{28,20},{1,9},{5... | collective-permute-start | bytes 208904 | tf_op jit(solution)/shard_map/ppermute | solution.py:39
  51.2 2.5 %collective-permute-done.11.refs_3_ = f32[136,128]{1,0:T(8,128)S(1)} collective-permute-done((f32[136,128]{1,0:T(8,128)S(1)}, f32[136,128]{1,0:T(8,128)S(1)}, u32[]{:S(2)}, u32[]{:S(2)}) %collective-permute-start.11) | collective-permute-done | bytes 69664 | tf_op jit(solution)/shard_map/ppermute | solution.py:39
  53.7 1.7 %collective-permute-done.12.refs_4_ = f32[136,128]{1,0:T(8,128)S(1)} collective-permute-done((f32[136,128]{1,0:T(8,128)S(1)}, f32[136,128]{1,0:T(8,128)S(1)}, u32[]{:S(2)}, u32[]{:S(2)}) %collective-permute-start.12) | collective-permute-done | bytes 69664 | tf_op jit(solution)/shard_map/ppermute | solution.py:39
  55.4 0.1 merge.3.refs_0_
  55.5 1.2 %collective-permute-start.16 = (f32[136,128]{1,0:T(8,128)S(1)}, f32[136,128]{1,0:T(8,128)S(1)}, u32[]{:S(2)}, u32[]{:S(2)}) collective-permute-start(f32[136,128]{1,0:T(8,128)S(1)} %merge.3.refs_0_), channel_id=1, source_target_pairs={{0,24},{4,28},{8,16},{12,20},{16,8},{20,12},{24,0},{28,4},{1,25},{... | collective-permute-start | bytes 208904 | tf_op jit(solution)/shard_map/ppermute | solution.py:39
  56.7 0.4 collective-permute-start.15
  57.1 2.8 %collective-permute-start.14 = (f32[136,128]{1,0:T(8,128)S(1)}, f32[136,128]{1,0:T(8,128)S(1)}, u32[]{:S(2)}, u32[]{:S(2)}) collective-permute-start(f32[136,128]{1,0:T(8,128)S(1)} %merge.3.refs_0_), channel_id=1, source_target_pairs={{0,8},{4,12},{8,0},{12,4},{16,24},{20,28},{24,16},{28,20},{1,9},{5... | collective-permute-start | bytes 208904 | tf_op jit(solution)/shard_map/ppermute | solution.py:39
  59.9 2.4 %collective-permute-done.16.refs_3_ = f32[136,128]{1,0:T(8,128)S(1)} collective-permute-done((f32[136,128]{1,0:T(8,128)S(1)}, f32[136,128]{1,0:T(8,128)S(1)}, u32[]{:S(2)}, u32[]{:S(2)}) %collective-permute-start.16) | collective-permute-done | bytes 69664 | tf_op jit(solution)/shard_map/ppermute | solution.py:39
  62.3 1.1 %collective-permute-done.15.refs_2_ = f32[136,128]{1,0:T(8,128)S(1)} collective-permute-done((f32[136,128]{1,0:T(8,128)S(1)}, f32[136,128]{1,0:T(8,128)S(1)}, u32[]{:S(2)}, u32[]{:S(2)}) %collective-permute-start.15) | collective-permute-done | bytes 69664 | tf_op jit(solution)/shard_map/ppermute | solution.py:39
  63.5 0.1 join.1.refs_5_
  63.6 1.2 %collective-permute-start.18 = (f32[136,512]{1,0:T(8,128)S(1)}, f32[136,512]{1,0:T(8,128)S(1)}, u32[]{:S(2)}, u32[]{:S(2)}) collective-permute-start(f32[136,512]{1,0:T(8,128)S(1)} %join.1.refs_5_), channel_id=1, source_target_pairs={{0,2},{2,0},{1,3},{3,1},{4,6},{6,4},{5,7},{7,5},{8,10},{10,8},{9,1... | collective-permute-start | bytes 835592 | tf_op jit(solution)/shard_map/ppermute | solution.py:39
  64.8 1.3 %backward.3 = (f32[520,128]{1,0:T(8,128)S(1)}, f32[520,128]{1,0:T(8,128)S(1)}, f32[32,1,128]{2,1,0:T(1,128)S(1)}) custom-call(f32[512,512]{1,0:T(8,128)S(1)} %get-tuple-element.59.refs_0_, f32[8,512]{1,0:T(8,128)S(1)} %get-tuple-element.60.refs_1_, f32[1368,128]{1,0:T(8,128)S(1)} %get-tuple-element.61.refs_2_, ...), custom_call_target="tpu_custom_call" | custom-call | flops 603979776 | bytes 1048576 | tf_op jit(solution)/shard_map/backward/pallas_call | solution.py:85
  66.0 9.9 %all_to_all.11.refs_0_ = f32[32,1,128]{2,1,0:T(1,128)S(1)} all-to-all(f32[32,1,128]{2,1,0:T(1,128)S(1)} %get-tuple-element.66), channel_id=1, replica_groups=mesh['page'=8,'query'=2,'head'=2] {'page','query','head'}, dimensions={0} | all-to-all | bytes 32768 | tf_op jit(solution)/shard_map/all_to_all | solution.py:683
  75.9 1.0 %page_update.2.refs_7_ = f32[1040,128]{1,0:T(8,128)S(1)} custom-call(f32[32,1,128]{2,1,0:T(1,128)S(1)} %all_to_all.11.refs_0_, f32[520,128]{1,0:T(8,128)S(1)} %get-tuple-element.68.refs_1_, f32[1368,128]{1,0:T(8,128)S(1)} %get-tuple-element.61.refs_2_, f32[1368,128]{1,0:T(8,128)S(1)} %collective-permute-done.17.refs_3_, ...), custom_call_target="tpu_custom_call" | custom-call | flops 301989888 | bytes 1048576 | tf_op jit(solution)/shard_map/page_update/pallas_call | solution.py:85
  76.9 0.1 collective-permute-start.19
  77.0 1.0 %page_update.3.refs_0_ = f32[1040,128]{1,0:T(8,128)S(1)} custom-call(f32[32,1,128]{2,1,0:T(1,128)S(1)} %all_to_all.11.refs_0_, f32[520,128]{1,0:T(8,128)S(1)} %get-tuple-element.67.refs_1_, f32[1368,128]{1,0:T(8,128)S(1)} %get-tuple-element.61.refs_2_, f32[1368,128]{1,0:T(8,128)S(1)} %collective-permute-done.17.refs_3_, ...), custom_call_target="tpu_custom_call" | custom-call | flops 301989888 | bytes 1048576 | tf_op jit(solution)/shard_map/page_update/pallas_call | solution.py:85
  78.0 0.9 %collective-permute-done.19.refs_1_ = f32[1040,128]{1,0:T(8,128)S(1)} collective-permute-done((f32[1040,128]{1,0:T(8,128)S(1)}, f32[1040,128]{1,0:T(8,128)S(1)}, u32[]{:S(2)}, u32[]{:S(2)}) %collective-permute-start.19) | collective-permute-done | bytes 532512 | tf_op jit(solution)/shard_map/ppermute | solution.py:39
  78.9 1.0 %unpack.1 = (f32[4,256,128]{2,1,0:T(8,128)}, f32[4,256,128]{2,1,0:T(8,128)}, f32[4,256]{1,0:T(4,128)}) custom-call(f32[1040,128]{1,0:T(8,128)S(1)} %page_update.3.refs_0_, f32[1040,128]{1,0:T(8,128)S(1)} %collective-permute-done.19.refs_1_), custom_call_target="tpu_custom_call" | custom-call | flops 1048576 | bytes 1048576 | tf_op jit(solution)/shard_map/unpack/pallas_call | solution.py:85
  (23 shorter events, 0.1 us)
Async XLA Ops:
  0.6 5.1 %copy-start.3 = (f32[4,256,128]{2,1,0:T(8,128)S(1)}, f32[4,256,128]{2,1,0:T(8,128)}, u32[]{:S(2)}) copy-start(f32[4,256,128]{2,1,0:T(8,128)} %refs_4_.3) | copy-start | bytes 1572868
  0.6 5.1 %copy-start.2 = (f32[4,256,128]{2,1,0:T(8,128)S(1)}, f32[4,256,128]{2,1,0:T(8,128)}, u32[]{:S(2)}) copy-start(f32[4,256,128]{2,1,0:T(8,128)} %refs_2_.3) | copy-start | bytes 1572868
  0.7 5.1 %copy-start.1 = (f32[4,256,128]{2,1,0:T(8,128)S(1)}, f32[4,256,128]{2,1,0:T(8,128)}, u32[]{:S(2)}) copy-start(f32[4,256,128]{2,1,0:T(8,128)} %refs_1_.3) | copy-start | bytes 1572868
  0.7 5.1 %copy-start = (f32[4,256,128]{2,1,0:T(8,128)S(1)}, f32[4,256,128]{2,1,0:T(8,128)}, u32[]{:S(2)}) copy-start(f32[4,256,128]{2,1,0:T(8,128)} %refs_0_.3) | copy-start | bytes 1572868
  0.7 5.1 %copy-start.5 = (f32[4,256]{1,0:T(4,128)S(1)}, f32[4,256]{1,0:T(4,128)}, u32[]{:S(2)}) copy-start(f32[4,256]{1,0:T(4,128)} %refs_3_.3) | copy-start | bytes 12292
  0.7 5.1 %copy-start.6 = (s32[4,256]{1,0:T(4,128)S(1)}, s32[4,256]{1,0:T(4,128)}, u32[]{:S(2)}) copy-start(s32[4,256]{1,0:T(4,128)} %refs_5_.3) | copy-start | bytes 12292
  2.6 3.2 %copy-start.7 = (s32[8]{0:T(128)S(1)}, s32[8]{0:T(128)}, u32[]{:S(2)}) copy-start(s32[8]{0:T(128)} %refs_6_.3) | copy-start | bytes 100
  2.7 5.1 %collective-permute-start = (f32[512,128]{1,0:T(8,128)}, f32[512,128]{1,0:T(8,128)S(1)}, u32[]{:S(2)}, u32[]{:S(2)}) collective-permute-start(f32[512,128]{1,0:T(8,128)} %get-tuple-element.37), channel_id=1, source_target_pairs={{0,4},{4,0},{8,12},{12,8},{16,20},{20,16},{24,28},{28,24},{1,5},{5... | collective-permute-start | bytes 786440 | tf_op jit(solution)/shard_map/ppermute | solution.py:39
  3.2 9.2 %collective-permute-start.2 = (f32[256,128]{1,0:T(8,128)}, f32[256,128]{1,0:T(8,128)S(1)}, u32[]{:S(2)}, u32[]{:S(2)}) collective-permute-start(f32[256,128]{1,0:T(8,128)} %get-tuple-element.41.refs_5_), channel_id=1, source_target_pairs={{0,2},{2,0},{1,3},{3,1},{4,6},{6,4},{5,7},{7,5},{8,10},{10,8},{9,1... | collective-permute-start | bytes 393224 | tf_op jit(solution)/shard_map/ppermute | solution.py:39
  6.5 1.2 %collective-permute-start.1 = (f32[8,128]{1,0:T(8,128)S(1)}, f32[8,128]{1,0:T(8,128)S(1)}, u32[]{:S(2)}, u32[]{:S(2)}) collective-permute-start(f32[8,128]{1,0:T(8,128)S(1)} %get-tuple-element.38), channel_id=1, source_target_pairs={{0,4},{4,0},{8,12},{12,8},{16,20},{20,16},{24,28},{28,24},{1,5},{5... | collective-permute-start | bytes 12296 | tf_op jit(solution)/shard_map/ppermute | solution.py:39
  6.8 5.6 %collective-permute-start.3 = (f32[72,128]{1,0:T(8,128)S(1)}, f32[72,128]{1,0:T(8,128)S(1)}, u32[]{:S(2)}, u32[]{:S(2)}) collective-permute-start(f32[72,128]{1,0:T(8,128)S(1)} %get-tuple-element.42.refs_6_), channel_id=1, source_target_pairs={{0,2},{2,0},{1,3},{3,1},{4,6},{6,4},{5,7},{7,5},{8,10},{10,8},{9,1... | collective-permute-start | bytes 110600 | tf_op jit(solution)/shard_map/ppermute | solution.py:39
  8.7 5.8 %collective-permute-start.4 = (f32[72,128]{1,0:T(8,128)S(1)}, f32[72,128]{1,0:T(8,128)S(1)}, u32[]{:S(2)}, u32[]{:S(2)}) collective-permute-start(f32[72,128]{1,0:T(8,128)S(1)} %get-tuple-element.46), channel_id=1, source_target_pairs={{0,24},{4,28},{8,16},{12,20},{16,8},{20,12},{24,0},{28,4},{1,25},{... | collective-permute-start | bytes 110600 | tf_op jit(solution)/shard_map/ppermute | solution.py:39
  15.5 10.1 %collective-permute-start.6 = (f32[144,128]{1,0:T(8,128)S(1)}, f32[144,128]{1,0:T(8,128)S(1)}, u32[]{:S(2)}, u32[]{:S(2)}) collective-permute-start(f32[144,128]{1,0:T(8,128)S(1)} %get-tuple-element.54), channel_id=1, source_target_pairs={{0,16},{4,20},{8,24},{12,28},{16,0},{20,4},{24,8},{28,12},{1,17},{... | collective-permute-start | bytes 221192 | tf_op jit(solution)/shard_map/ppermute | solution.py:39
  16.3 9.2 %collective-permute-start.7 = (f32[144,128]{1,0:T(8,128)S(1)}, f32[144,128]{1,0:T(8,128)S(1)}, u32[]{:S(2)}, u32[]{:S(2)}) collective-permute-start(f32[144,128]{1,0:T(8,128)S(1)} %get-tuple-element.55), channel_id=1, source_target_pairs={{0,8},{4,12},{8,0},{12,4},{16,24},{20,28},{24,16},{28,20},{1,9},{5... | collective-permute-start | bytes 221192 | tf_op jit(solution)/shard_map/ppermute | solution.py:39
  19.7 5.9 %collective-permute-start.5 = (f32[72,128]{1,0:T(8,128)S(1)}, f32[72,128]{1,0:T(8,128)S(1)}, u32[]{:S(2)}, u32[]{:S(2)}) collective-permute-start(f32[72,128]{1,0:T(8,128)S(1)} %get-tuple-element.53), channel_id=1, source_target_pairs={{0,24},{4,28},{8,16},{12,20},{16,8},{20,12},{24,0},{28,4},{1,25},{... | collective-permute-start | bytes 110600 | tf_op jit(solution)/shard_map/ppermute | solution.py:39
  25.8 6.3 %collective-permute-start.10 = (f32[136,128]{1,0:T(8,128)S(1)}, f32[136,128]{1,0:T(8,128)S(1)}, u32[]{:S(2)}, u32[]{:S(2)}) collective-permute-start(f32[136,128]{1,0:T(8,128)S(1)} %merge.2.refs_8_), channel_id=1, source_target_pairs={{0,24},{4,28},{8,16},{12,20},{16,8},{20,12},{24,0},{28,4},{1,25},{... | collective-permute-start | bytes 208904 | tf_op jit(solution)/shard_map/ppermute | solution.py:39
  26.6 6.7 %collective-permute-start.9 = (f32[136,128]{1,0:T(8,128)S(1)}, f32[136,128]{1,0:T(8,128)S(1)}, u32[]{:S(2)}, u32[]{:S(2)}) collective-permute-start(f32[136,128]{1,0:T(8,128)S(1)} %merge.2.refs_8_), channel_id=1, source_target_pairs={{0,16},{4,20},{8,24},{12,28},{16,0},{20,4},{24,8},{28,12},{1,17},{... | collective-permute-start | bytes 208904 | tf_op jit(solution)/shard_map/ppermute | solution.py:39
  26.6 6.7 %collective-permute-start.8 = (f32[136,128]{1,0:T(8,128)S(1)}, f32[136,128]{1,0:T(8,128)S(1)}, u32[]{:S(2)}, u32[]{:S(2)}) collective-permute-start(f32[136,128]{1,0:T(8,128)S(1)} %merge.2.refs_8_), channel_id=1, source_target_pairs={{0,8},{4,12},{8,0},{12,4},{16,24},{20,28},{24,16},{28,20},{1,9},{5... | collective-permute-start | bytes 208904 | tf_op jit(solution)/shard_map/ppermute | solution.py:39
  46.2 29.7 %collective-permute-start.17 = (f32[1368,128]{1,0:T(8,128)S(1)}, f32[1368,128]{1,0:T(8,128)S(1)}, u32[]{:S(2)}, u32[]{:S(2)}) collective-permute-start(f32[1368,128]{1,0:T(8,128)S(1)} %get-tuple-element.61.refs_2_), channel_id=1, source_target_pairs={{0,2},{2,0},{1,3},{3,1},{4,6},{6,4},{5,7},{7,5},{8,10},{10,8},{9,1... | collective-permute-start | bytes 2101256 | tf_op jit(solution)/shard_map/ppermute | solution.py:39
  46.8 6.9 %collective-permute-start.11 = (f32[136,128]{1,0:T(8,128)S(1)}, f32[136,128]{1,0:T(8,128)S(1)}, u32[]{:S(2)}, u32[]{:S(2)}) collective-permute-start(f32[136,128]{1,0:T(8,128)S(1)} %get-tuple-element.63), channel_id=1, source_target_pairs={{0,24},{4,28},{8,16},{12,20},{16,8},{20,12},{24,0},{28,4},{1,25},{... | collective-permute-start | bytes 208904 | tf_op jit(solution)/shard_map/ppermute | solution.py:39
  47.3 8.0 %collective-permute-start.12 = (f32[136,128]{1,0:T(8,128)S(1)}, f32[136,128]{1,0:T(8,128)S(1)}, u32[]{:S(2)}, u32[]{:S(2)}) collective-permute-start(f32[136,128]{1,0:T(8,128)S(1)} %get-tuple-element.64), channel_id=1, source_target_pairs={{0,16},{4,20},{8,24},{12,28},{16,0},{20,4},{24,8},{28,12},{1,17},{... | collective-permute-start | bytes 208904 | tf_op jit(solution)/shard_map/ppermute | solution.py:39
  48.8 6.5 %collective-permute-start.13 = (f32[136,128]{1,0:T(8,128)S(1)}, f32[136,128]{1,0:T(8,128)S(1)}, u32[]{:S(2)}, u32[]{:S(2)}) collective-permute-start(f32[136,128]{1,0:T(8,128)S(1)} %get-tuple-element.65), channel_id=1, source_target_pairs={{0,8},{4,12},{8,0},{12,4},{16,24},{20,28},{24,16},{28,20},{1,9},{5... | collective-permute-start | bytes 208904 | tf_op jit(solution)/shard_map/ppermute | solution.py:39
  55.5 6.9 %collective-permute-start.16 = (f32[136,128]{1,0:T(8,128)S(1)}, f32[136,128]{1,0:T(8,128)S(1)}, u32[]{:S(2)}, u32[]{:S(2)}) collective-permute-start(f32[136,128]{1,0:T(8,128)S(1)} %merge.3.refs_0_), channel_id=1, source_target_pairs={{0,24},{4,28},{8,16},{12,20},{16,8},{20,12},{24,0},{28,4},{1,25},{... | collective-permute-start | bytes 208904 | tf_op jit(solution)/shard_map/ppermute | solution.py:39
  56.7 6.8 %collective-permute-start.15 = (f32[136,128]{1,0:T(8,128)S(1)}, f32[136,128]{1,0:T(8,128)S(1)}, u32[]{:S(2)}, u32[]{:S(2)}) collective-permute-start(f32[136,128]{1,0:T(8,128)S(1)} %merge.3.refs_0_), channel_id=1, source_target_pairs={{0,16},{4,20},{8,24},{12,28},{16,0},{20,4},{24,8},{28,12},{1,17},{... | collective-permute-start | bytes 208904 | tf_op jit(solution)/shard_map/ppermute | solution.py:39
  57.1 6.4 %collective-permute-start.14 = (f32[136,128]{1,0:T(8,128)S(1)}, f32[136,128]{1,0:T(8,128)S(1)}, u32[]{:S(2)}, u32[]{:S(2)}) collective-permute-start(f32[136,128]{1,0:T(8,128)S(1)} %merge.3.refs_0_), channel_id=1, source_target_pairs={{0,8},{4,12},{8,0},{12,4},{16,24},{20,28},{24,16},{28,20},{1,9},{5... | collective-permute-start | bytes 208904 | tf_op jit(solution)/shard_map/ppermute | solution.py:39
  63.6 12.3 %collective-permute-start.18 = (f32[136,512]{1,0:T(8,128)S(1)}, f32[136,512]{1,0:T(8,128)S(1)}, u32[]{:S(2)}, u32[]{:S(2)}) collective-permute-start(f32[136,512]{1,0:T(8,128)S(1)} %join.1.refs_5_), channel_id=1, source_target_pairs={{0,2},{2,0},{1,3},{3,1},{4,6},{6,4},{5,7},{7,5},{8,10},{10,8},{9,1... | collective-permute-start | bytes 835592 | tf_op jit(solution)/shard_map/ppermute | solution.py:39
  64.8 11.1 %copy-start.4 = (f32[256,128]{1,0:T(8,128)S(1)}, f32[256,128]{1,0:T(8,128)}, u32[]{:S(2)}) copy-start(f32[256,128]{1,0:T(8,128)} %get-tuple-element.41.refs_5_) | copy-start | bytes 393220
  76.9 2.0 %collective-permute-start.19 = (f32[1040,128]{1,0:T(8,128)S(1)}, f32[1040,128]{1,0:T(8,128)S(1)}, u32[]{:S(2)}, u32[]{:S(2)}) collective-permute-start(f32[1040,128]{1,0:T(8,128)S(1)} %page_update.2.refs_7_), channel_id=1, source_target_pairs={{0,4},{4,0},{8,12},{12,8},{16,20},{20,16},{24,28},{28,24},{1,5},{5... | collective-permute-start | bytes 1597448 | tf_op jit(solution)/shard_map/ppermute | solution.py:39

commit v21 on v19

--- a/solution.py
+++ b/solution.py
@@ -155,6 +155,7 @@
     ranks = lax.axis_size("page") // CORES
     query_rows = part_rows * query_devices
     chunk, piece = query_rows // ranks, part_rows // ranks
+    turns = [ranks // 2] + [turn for turn in reversed(range(1, ranks)) if turn != ranks // 2]
     slot_total = local_heads * head_devices * slot_rows * lax.axis_size("page")
     entry_total = slot_total * width
     score_scale = 1.0 / math.sqrt(width)
@@ -503,7 +504,7 @@
 
     def read_chunks(merged_refs, chunks):
         rank, _, _ = places()
-        for turn, ref in enumerate(merged_refs):
+        for turn, ref in zip([0] + turns[::-1], merged_refs):
             chunks[rank ^ turn] = ref[...]
         return [chunks[at] for at in range(ranks)]
 
@@ -590,7 +591,7 @@
                 )
                 arrived = {
                     turn: exchange(pieces[turn], page=CORES * turn)
-                    for turn in reversed(range(1, ranks))
+                    for turn in turns
                 }
                 sums += list(arrived.values()) + pieces[:1]
                 weights.append(part_weights)
@@ -607,7 +608,7 @@
             states, weights, maxima = [new_state], [part_weights], [part_max]
             arrived = {
                 turn: exchange(chunk_parts[turn], page=CORES * turn)
-                for turn in reversed(range(1, ranks))
+                for turn in turns
             }
             sums = chunk_parts[:1] + list(arrived.values())
             new_states = states + [
@@ -620,9 +621,7 @@
             2**20,
             query_parts + sums,
         )
-        all_merged = [merged] + [
-            exchange(merged, page=CORES * turn) for turn in range(1, ranks)
-        ]
+        all_merged = [merged] + [exchange(merged, page=CORES * turn) for turn in reversed(turns)]
         if last:
             all_merged = call(
                 join_body, [(width + TAIL, query_rows)], "join", 2**20, all_merged, chunk_scratch

time: 76.9 us -> 75.9 us (0.987)
  starting transfers between devices: 27.2 us -> 24.4 us
  waiting for transfers between devices: 16 us -> 18.7 us
  blocking collectives: 20.9 us -> 20 us
    ppermute x20, starting transfers between devices: 27.2 us -> 24.4 us  [exchange(): return lax.ppermute(value, axes, pairs)]
    ppermute x20, waiting for transfers between devices: 16 us -> 18.7 us  [exchange(): return lax.ppermute(value, axes, pairs)]
    all_to_all x2, blocking collectives: 20.9 us -> 20 us  [direct_per_device(): lax.all_to_all(squares, ('page', 'query', 'head'), split_axis=0, concat_a...]
  transfers between devices with their start and end apart: 20 -> 20, of which waited for: 9 -> 11; matrix products, arithmetic and copies ran while one was open for 0% -> 0% of each run, Pallas kernels for 6% -> 7%
where the time goes in v21:
time: 75.9 us; the launch traced here: 75.7 us
  starting transfers between devices  24.4 us (32%)
  blocking collectives  20 us (26%)
  waiting for transfers between devices  18.7 us (25%)
  Pallas kernels  11.8 us (16%)
  between operations  0.83 us (1%)
    ppermute x20, starting transfers between devices, exchange(): return lax.ppermute(value, axes, pairs)  24.4 us
    all_to_all x2, blocking collectives, direct_per_device(): lax.all_to_all(squares, ('page', 'query', 'head'), split_axis=0, concat_a...  20 us
    ppermute x20, waiting for transfers between devices, exchange(): return lax.ppermute(value, axes, pairs)  18.7 us
    pallas_call x13, Pallas kernels, call(): pl.pallas_call(without_after, out_shape=[jax.ShapeDtypeStruct(shape, jnp....  11.8 us
  transfers between devices with their start and end apart: 20, of which 11 were waited for; matrix products, arithmetic and copies ran while one was open for 0% of the time, Pallas kernels for 7%

profile of v21, /device:TPU:0, one launch (start us, length us, event | category | flops | bytes accessed | tf_op | source)
XLA Modules:
  0.0 75.7 jit_solution(18087074927210481728)
XLA Ops:
  0.7 2.0 %pack.1 = (f32[520,128]{1,0:T(8,128)}, f32[328,128]{1,0:T(8,128)}) custom-call(f32[4,256,128]{2,1,0:T(8,128)} %refs_0_.3, f32[4,256,128]{2,1,0:T(8,128)} %refs_1_.3, f32[4,256,128]{2,1,0:T(8,128)} %refs_2_.3, f32[4,256]{1,0:T(4,128)} %refs_3_.3, f32[4,256,128]{2,1,0:T(8,128)} %refs_4_.3, s32[4,256]{1,0:T(4,128)} %refs_5_.3, s32[8]{0:T(128)} %refs_6_.3), custom_call_target="tpu_custom_call" | custom-call | flops 1048576 | bytes 1048576 | tf_op jit(solution)/shard_map/pack/pallas_call | solution.py:85
  2.7 0.0 copy-start.7
  2.7 0.5 collective-permute-start
  3.3 2.6 %collective-permute-start.1 = (f32[328,128]{1,0:T(8,128)}, f32[328,128]{1,0:T(8,128)S(1)}, u32[]{:S(2)}, u32[]{:S(2)}) collective-permute-start(f32[328,128]{1,0:T(8,128)} %get-tuple-element.35.refs_5_), channel_id=1, source_target_pairs={{0,2},{2,0},{1,3},{3,1},{4,6},{6,4},{5,7},{7,5},{8,10},{10,8},{9,1... | collective-permute-start | bytes 503816 | tf_op jit(solution)/shard_map/ppermute | solution.py:39
  5.9 0.7 own.1
  6.6 0.9 %forward.2 = (f32[72,128]{1,0:T(8,128)S(1)}, f32[72,128]{1,0:T(8,128)S(1)}, f32[72,128]{1,0:T(8,128)S(1)}, f32[72,128]{1,0:T(8,128)S(1)}, f32[512,256]{1,0:T(8,128)S(1)}, /*index=5*/f32[8,256]{1,0:T(8,128)S(1)}) custom-call(f32[520,128]{1,0:T(8,128)S(1)} %get-tuple-element.32.refs_0_.refs_4_, f32[520,128]{1,0:T(8,128)S(1)} %collective-permute-done.refs_1_.refs_5_, ...), custom_call_target="tpu_custom_call" | custom-call | flops 201326592 | bytes 1048576 | tf_op jit(solution)/shard_map/forward/pallas_call | solution.py:85
  7.5 2.7 %collective-permute-start.2 = (f32[72,128]{1,0:T(8,128)S(1)}, f32[72,128]{1,0:T(8,128)S(1)}, u32[]{:S(2)}, u32[]{:S(2)}) collective-permute-start(f32[72,128]{1,0:T(8,128)S(1)} %get-tuple-element.40), channel_id=1, source_target_pairs={{0,16},{4,20},{8,24},{12,28},{16,0},{20,4},{24,8},{28,12},{1,17},{... | collective-permute-start | bytes 110600 | tf_op jit(solution)/shard_map/ppermute | solution.py:39
  10.2 1.3 %collective-permute-start.3 = (f32[72,128]{1,0:T(8,128)S(1)}, f32[72,128]{1,0:T(8,128)S(1)}, u32[]{:S(2)}, u32[]{:S(2)}) collective-permute-start(f32[72,128]{1,0:T(8,128)S(1)} %get-tuple-element.41), channel_id=1, source_target_pairs={{0,24},{4,28},{8,16},{12,20},{16,8},{20,12},{24,0},{28,4},{1,25},{... | collective-permute-start | bytes 110600 | tf_op jit(solution)/shard_map/ppermute | solution.py:39
  11.5 0.2 collective-permute-start.4
  11.7 0.9 %forward.3 = (f32[72,128]{1,0:T(8,128)S(1)}, f32[72,128]{1,0:T(8,128)S(1)}, f32[72,128]{1,0:T(8,128)S(1)}, f32[72,128]{1,0:T(8,128)S(1)}, f32[512,256]{1,0:T(8,128)S(1)}, /*index=5*/f32[8,256]{1,0:T(8,128)S(1)}) custom-call(f32[520,128]{1,0:T(8,128)S(1)} %get-tuple-element.32.refs_0_.refs_4_, f32[520,128]{1,0:T(8,128)S(1)} %collective-permute-done.refs_1_.refs_5_, ...), custom_call_target="tpu_custom_call" | custom-call | flops 201326592 | bytes 1048576 | tf_op jit(solution)/shard_map/forward/pallas_call | solution.py:85
  12.7 2.9 %collective-permute-start.5 = (f32[72,128]{1,0:T(8,128)S(1)}, f32[72,128]{1,0:T(8,128)S(1)}, u32[]{:S(2)}, u32[]{:S(2)}) collective-permute-start(f32[72,128]{1,0:T(8,128)S(1)} %get-tuple-element.44), channel_id=1, source_target_pairs={{0,16},{4,20},{8,24},{12,28},{16,0},{20,4},{24,8},{28,12},{1,17},{... | collective-permute-start | bytes 110600 | tf_op jit(solution)/shard_map/ppermute | solution.py:39
  15.5 1.3 %collective-permute-start.6 = (f32[72,128]{1,0:T(8,128)S(1)}, f32[72,128]{1,0:T(8,128)S(1)}, u32[]{:S(2)}, u32[]{:S(2)}) collective-permute-start(f32[72,128]{1,0:T(8,128)S(1)} %get-tuple-element.45), channel_id=1, source_target_pairs={{0,24},{4,28},{8,16},{12,20},{16,8},{20,12},{24,0},{28,4},{1,25},{... | collective-permute-start | bytes 110600 | tf_op jit(solution)/shard_map/ppermute | solution.py:39
  16.9 0.0 collective-permute-done.2.refs_2_
  16.9 0.0 collective-permute-start.7
  16.9 0.0 collective-permute-done.3.refs_3_
  16.9 0.7 collective-permute-done.5.refs_6_
  17.6 3.7 %collective-permute-done.6.refs_7_ = f32[72,128]{1,0:T(8,128)S(1)} collective-permute-done((f32[72,128]{1,0:T(8,128)S(1)}, f32[72,128]{1,0:T(8,128)S(1)}, u32[]{:S(2)}, u32[]{:S(2)}) %collective-permute-start.6) | collective-permute-done | bytes 36896 | tf_op jit(solution)/shard_map/ppermute | solution.py:39
  21.3 0.3 merge.2.refs_8_
  21.6 1.0 %collective-permute-start.10 = (f32[136,128]{1,0:T(8,128)S(1)}, f32[136,128]{1,0:T(8,128)S(1)}, u32[]{:S(2)}, u32[]{:S(2)}) collective-permute-start(f32[136,128]{1,0:T(8,128)S(1)} %merge.2.refs_8_), channel_id=1, source_target_pairs={{0,16},{4,20},{8,24},{12,28},{16,0},{20,4},{24,8},{28,12},{1,17},{... | collective-permute-start | bytes 208904 | tf_op jit(solution)/shard_map/ppermute | solution.py:39
  22.6 1.3 %collective-permute-start.9 = (f32[136,128]{1,0:T(8,128)S(1)}, f32[136,128]{1,0:T(8,128)S(1)}, u32[]{:S(2)}, u32[]{:S(2)}) collective-permute-start(f32[136,128]{1,0:T(8,128)S(1)} %merge.2.refs_8_), channel_id=1, source_target_pairs={{0,24},{4,28},{8,16},{12,20},{16,8},{20,12},{24,0},{28,4},{1,25},{... | collective-permute-start | bytes 208904 | tf_op jit(solution)/shard_map/ppermute | solution.py:39
  23.9 1.2 %collective-permute-start.8 = (f32[136,128]{1,0:T(8,128)S(1)}, f32[136,128]{1,0:T(8,128)S(1)}, u32[]{:S(2)}, u32[]{:S(2)}) collective-permute-start(f32[136,128]{1,0:T(8,128)S(1)} %merge.2.refs_8_), channel_id=1, source_target_pairs={{0,8},{4,12},{8,0},{12,4},{16,24},{20,28},{24,16},{28,20},{1,9},{5... | collective-permute-start | bytes 208904 | tf_op jit(solution)/shard_map/ppermute | solution.py:39
  25.1 2.1 %collective-permute-done.10.refs_11_ = f32[136,128]{1,0:T(8,128)S(1)} collective-permute-done((f32[136,128]{1,0:T(8,128)S(1)}, f32[136,128]{1,0:T(8,128)S(1)}, u32[]{:S(2)}, u32[]{:S(2)}) %collective-permute-start.10) | collective-permute-done | bytes 69664 | tf_op jit(solution)/shard_map/ppermute | solution.py:39
  27.3 1.5 %collective-permute-done.9.refs_10_ = f32[136,128]{1,0:T(8,128)S(1)} collective-permute-done((f32[136,128]{1,0:T(8,128)S(1)}, f32[136,128]{1,0:T(8,128)S(1)}, u32[]{:S(2)}, u32[]{:S(2)}) %collective-permute-start.9) | collective-permute-done | bytes 69664 | tf_op jit(solution)/shard_map/ppermute | solution.py:39
  28.8 0.2 collective-permute-done.8.refs_9_
  29.0 1.4 %backward.2 = (f32[520,128]{1,0:T(8,128)S(1)}, f32[520,128]{1,0:T(8,128)S(1)}, f32[32,1,128]{2,1,0:T(1,128)S(1)}) custom-call(f32[512,256]{1,0:T(8,128)S(1)} %get-tuple-element.36.refs_0_, f32[512,256]{1,0:T(8,128)S(1)} %get-tuple-element.38.refs_1_, f32[8,256]{1,0:T(8,128)S(1)} %get-tuple-element.37.refs_3_.refs_2_, ...), custom_call_target="tpu_custom_call" | custom-call | flops 603979776 | bytes 1048576 | tf_op jit(solution)/shard_map/backward/pallas_call | solution.py:85
  30.4 10.9 %all_to_all.10.refs_6_ = f32[32,1,128]{2,1,0:T(1,128)S(1)} all-to-all(f32[32,1,128]{2,1,0:T(1,128)S(1)} %get-tuple-element.50), channel_id=1, replica_groups=mesh['page'=8,'query'=2,'head'=2] {'page','query','head'}, dimensions={0} | all-to-all | bytes 32768 | tf_op jit(solution)/shard_map/all_to_all | solution.py:642
  41.3 1.1 %update_forward.1 = (f32[1368,128]{1,0:T(8,128)S(1)}, f32[136,128]{1,0:T(8,128)S(1)}, f32[136,128]{1,0:T(8,128)S(1)}, f32[136,128]{1,0:T(8,128)S(1)}, f32[136,12...) custom-call(f32[520,128]{1,0:T(8,128)S(1)} %get-tuple-element.32.refs_0_.refs_4_, ...), custom_call_target="tpu_custom_call" | custom-call | flops 402653184 | bytes 1048576 | tf_op jit(solution)/shard_map/update_forward/pallas_call | solution.py:85
  42.4 0.6 collective-permute-start.17
  43.0 0.6 collective-permute-start.11
  43.6 2.3 %collective-permute-start.12 = (f32[136,128]{1,0:T(8,128)S(1)}, f32[136,128]{1,0:T(8,128)S(1)}, u32[]{:S(2)}, u32[]{:S(2)}) collective-permute-start(f32[136,128]{1,0:T(8,128)S(1)} %get-tuple-element.56), channel_id=1, source_target_pairs={{0,24},{4,28},{8,16},{12,20},{16,8},{20,12},{24,0},{28,4},{1,25},{... | collective-permute-start | bytes 208904 | tf_op jit(solution)/shard_map/ppermute | solution.py:39
  45.9 0.6 collective-permute-start.13
  46.5 4.5 %collective-permute-done.11.refs_3_ = f32[136,128]{1,0:T(8,128)S(1)} collective-permute-done((f32[136,128]{1,0:T(8,128)S(1)}, f32[136,128]{1,0:T(8,128)S(1)}, u32[]{:S(2)}, u32[]{:S(2)}) %collective-permute-start.11) | collective-permute-done | bytes 69664 | tf_op jit(solution)/shard_map/ppermute | solution.py:39
  51.0 0.3 collective-permute-done.13.refs_5_
  51.3 0.1 merge.3.refs_0_
  51.4 0.6 collective-permute-start.16
  52.0 3.1 %collective-permute-start.15 = (f32[136,128]{1,0:T(8,128)S(1)}, f32[136,128]{1,0:T(8,128)S(1)}, u32[]{:S(2)}, u32[]{:S(2)}) collective-permute-start(f32[136,128]{1,0:T(8,128)S(1)} %merge.3.refs_0_), channel_id=1, source_target_pairs={{0,24},{4,28},{8,16},{12,20},{16,8},{20,12},{24,0},{28,4},{1,25},{... | collective-permute-start | bytes 208904 | tf_op jit(solution)/shard_map/ppermute | solution.py:39
  55.1 3.4 %collective-permute-done.16.refs_3_ = f32[136,128]{1,0:T(8,128)S(1)} collective-permute-done((f32[136,128]{1,0:T(8,128)S(1)}, f32[136,128]{1,0:T(8,128)S(1)}, u32[]{:S(2)}, u32[]{:S(2)}) %collective-permute-start.16) | collective-permute-done | bytes 69664 | tf_op jit(solution)/shard_map/ppermute | solution.py:39
  58.5 0.7 collective-permute-done.15.refs_2_
  59.1 0.7 collective-permute-done.14.refs_1_
  59.8 0.1 join.1.refs_5_
  59.9 1.4 %collective-permute-start.18 = (f32[136,512]{1,0:T(8,128)S(1)}, f32[136,512]{1,0:T(8,128)S(1)}, u32[]{:S(2)}, u32[]{:S(2)}) collective-permute-start(f32[136,512]{1,0:T(8,128)S(1)} %join.1.refs_5_), channel_id=1, source_target_pairs={{0,2},{2,0},{1,3},{3,1},{4,6},{6,4},{5,7},{7,5},{8,10},{10,8},{9,1... | collective-permute-start | bytes 835592 | tf_op jit(solution)/shard_map/ppermute | solution.py:39
  61.3 1.3 %backward.3 = (f32[520,128]{1,0:T(8,128)S(1)}, f32[520,128]{1,0:T(8,128)S(1)}, f32[32,1,128]{2,1,0:T(1,128)S(1)}) custom-call(f32[512,512]{1,0:T(8,128)S(1)} %get-tuple-element.51.refs_0_, f32[8,512]{1,0:T(8,128)S(1)} %get-tuple-element.52.refs_1_, f32[1368,128]{1,0:T(8,128)S(1)} %get-tuple-element.53.refs_2_, ...), custom_call_target="tpu_custom_call" | custom-call | flops 603979776 | bytes 1048576 | tf_op jit(solution)/shard_map/backward/pallas_call | solution.py:85
  62.6 9.0 %all_to_all.11.refs_0_ = f32[32,1,128]{2,1,0:T(1,128)S(1)} all-to-all(f32[32,1,128]{2,1,0:T(1,128)S(1)} %get-tuple-element.58), channel_id=1, replica_groups=mesh['page'=8,'query'=2,'head'=2] {'page','query','head'}, dimensions={0} | all-to-all | bytes 32768 | tf_op jit(solution)/shard_map/all_to_all | solution.py:642
  71.7 1.0 %page_update.2.refs_6_ = f32[1040,128]{1,0:T(8,128)S(1)} custom-call(f32[32,1,128]{2,1,0:T(1,128)S(1)} %all_to_all.11.refs_0_, f32[520,128]{1,0:T(8,128)S(1)} %get-tuple-element.60.refs_1_, f32[1368,128]{1,0:T(8,128)S(1)} %get-tuple-element.53.refs_2_, f32[1368,128]{1,0:T(8,128)S(1)} %collective-permute-done.17.refs_3_, ...), custom_call_target="tpu_custom_call" | custom-call | flops 301989888 | bytes 1048576 | tf_op jit(solution)/shard_map/page_update/pallas_call | solution.py:85
  72.7 0.1 collective-permute-start.19
  72.7 1.0 %page_update.3.refs_0_ = f32[1040,128]{1,0:T(8,128)S(1)} custom-call(f32[32,1,128]{2,1,0:T(1,128)S(1)} %all_to_all.11.refs_0_, f32[520,128]{1,0:T(8,128)S(1)} %get-tuple-element.59.refs_1_, f32[1368,128]{1,0:T(8,128)S(1)} %get-tuple-element.53.refs_2_, f32[1368,128]{1,0:T(8,128)S(1)} %collective-permute-done.17.refs_3_, ...), custom_call_target="tpu_custom_call" | custom-call | flops 301989888 | bytes 1048576 | tf_op jit(solution)/shard_map/page_update/pallas_call | solution.py:85
  73.8 0.9 %collective-permute-done.19.refs_1_ = f32[1040,128]{1,0:T(8,128)S(1)} collective-permute-done((f32[1040,128]{1,0:T(8,128)S(1)}, f32[1040,128]{1,0:T(8,128)S(1)}, u32[]{:S(2)}, u32[]{:S(2)}) %collective-permute-start.19) | collective-permute-done | bytes 532512 | tf_op jit(solution)/shard_map/ppermute | solution.py:39
  74.7 1.0 %unpack.1 = (f32[4,256,128]{2,1,0:T(8,128)}, f32[4,256,128]{2,1,0:T(8,128)}, f32[4,256]{1,0:T(4,128)}) custom-call(f32[1040,128]{1,0:T(8,128)S(1)} %page_update.3.refs_0_, f32[1040,128]{1,0:T(8,128)S(1)} %collective-permute-done.19.refs_1_), custom_call_target="tpu_custom_call" | custom-call | flops 1048576 | bytes 1048576 | tf_op jit(solution)/shard_map/unpack/pallas_call | solution.py:85
  (23 shorter events, 0.1 us)
Async XLA Ops:
  0.6 5.2 %copy-start.3 = (f32[4,256,128]{2,1,0:T(8,128)S(1)}, f32[4,256,128]{2,1,0:T(8,128)}, u32[]{:S(2)}) copy-start(f32[4,256,128]{2,1,0:T(8,128)} %refs_4_.3) | copy-start | bytes 1572868
  0.6 5.2 %copy-start.2 = (f32[4,256,128]{2,1,0:T(8,128)S(1)}, f32[4,256,128]{2,1,0:T(8,128)}, u32[]{:S(2)}) copy-start(f32[4,256,128]{2,1,0:T(8,128)} %refs_2_.3) | copy-start | bytes 1572868
  0.7 5.2 %copy-start.1 = (f32[4,256,128]{2,1,0:T(8,128)S(1)}, f32[4,256,128]{2,1,0:T(8,128)}, u32[]{:S(2)}) copy-start(f32[4,256,128]{2,1,0:T(8,128)} %refs_1_.3) | copy-start | bytes 1572868
  0.7 5.2 %copy-start = (f32[4,256,128]{2,1,0:T(8,128)S(1)}, f32[4,256,128]{2,1,0:T(8,128)}, u32[]{:S(2)}) copy-start(f32[4,256,128]{2,1,0:T(8,128)} %refs_0_.3) | copy-start | bytes 1572868
  0.7 5.2 %copy-start.5 = (f32[4,256]{1,0:T(4,128)S(1)}, f32[4,256]{1,0:T(4,128)}, u32[]{:S(2)}) copy-start(f32[4,256]{1,0:T(4,128)} %refs_3_.3) | copy-start | bytes 12292
  0.7 5.2 %copy-start.6 = (s32[4,256]{1,0:T(4,128)S(1)}, s32[4,256]{1,0:T(4,128)}, u32[]{:S(2)}) copy-start(s32[4,256]{1,0:T(4,128)} %refs_5_.3) | copy-start | bytes 12292
  2.7 3.2 %copy-start.7 = (s32[8]{0:T(128)S(1)}, s32[8]{0:T(128)}, u32[]{:S(2)}) copy-start(s32[8]{0:T(128)} %refs_6_.3) | copy-start | bytes 100
  2.7 3.8 %collective-permute-start = (f32[520,128]{1,0:T(8,128)}, f32[520,128]{1,0:T(8,128)S(1)}, u32[]{:S(2)}, u32[]{:S(2)}) collective-permute-start(f32[520,128]{1,0:T(8,128)} %get-tuple-element.33), channel_id=1, source_target_pairs={{0,4},{4,0},{8,12},{12,8},{16,20},{20,16},{24,28},{28,24},{1,5},{5... | collective-permute-start | bytes 798728 | tf_op jit(solution)/shard_map/ppermute | solution.py:39
  3.3 8.5 %collective-permute-start.1 = (f32[328,128]{1,0:T(8,128)}, f32[328,128]{1,0:T(8,128)S(1)}, u32[]{:S(2)}, u32[]{:S(2)}) collective-permute-start(f32[328,128]{1,0:T(8,128)} %get-tuple-element.35.refs_5_), channel_id=1, source_target_pairs={{0,2},{2,0},{1,3},{3,1},{4,6},{6,4},{5,7},{7,5},{8,10},{10,8},{9,1... | collective-permute-start | bytes 503816 | tf_op jit(solution)/shard_map/ppermute | solution.py:39
  7.5 9.4 %collective-permute-start.2 = (f32[72,128]{1,0:T(8,128)S(1)}, f32[72,128]{1,0:T(8,128)S(1)}, u32[]{:S(2)}, u32[]{:S(2)}) collective-permute-start(f32[72,128]{1,0:T(8,128)S(1)} %get-tuple-element.40), channel_id=1, source_target_pairs={{0,16},{4,20},{8,24},{12,28},{16,0},{20,4},{24,8},{28,12},{1,17},{... | collective-permute-start | bytes 110600 | tf_op jit(solution)/shard_map/ppermute | solution.py:39
  10.2 6.7 %collective-permute-start.3 = (f32[72,128]{1,0:T(8,128)S(1)}, f32[72,128]{1,0:T(8,128)S(1)}, u32[]{:S(2)}, u32[]{:S(2)}) collective-permute-start(f32[72,128]{1,0:T(8,128)S(1)} %get-tuple-element.41), channel_id=1, source_target_pairs={{0,24},{4,28},{8,16},{12,20},{16,8},{20,12},{24,0},{28,4},{1,25},{... | collective-permute-start | bytes 110600 | tf_op jit(solution)/shard_map/ppermute | solution.py:39
  11.5 5.4 %collective-permute-start.4 = (f32[72,128]{1,0:T(8,128)S(1)}, f32[72,128]{1,0:T(8,128)S(1)}, u32[]{:S(2)}, u32[]{:S(2)}) collective-permute-start(f32[72,128]{1,0:T(8,128)S(1)} %get-tuple-element.42), channel_id=1, source_target_pairs={{0,8},{4,12},{8,0},{12,4},{16,24},{20,28},{24,16},{28,20},{1,9},{5... | collective-permute-start | bytes 110600 | tf_op jit(solution)/shard_map/ppermute | solution.py:39
  12.7 4.9 %collective-permute-start.5 = (f32[72,128]{1,0:T(8,128)S(1)}, f32[72,128]{1,0:T(8,128)S(1)}, u32[]{:S(2)}, u32[]{:S(2)}) collective-permute-start(f32[72,128]{1,0:T(8,128)S(1)} %get-tuple-element.44), channel_id=1, source_target_pairs={{0,16},{4,20},{8,24},{12,28},{16,0},{20,4},{24,8},{28,12},{1,17},{... | collective-permute-start | bytes 110600 | tf_op jit(solution)/shard_map/ppermute | solution.py:39
  15.5 5.8 %collective-permute-start.6 = (f32[72,128]{1,0:T(8,128)S(1)}, f32[72,128]{1,0:T(8,128)S(1)}, u32[]{:S(2)}, u32[]{:S(2)}) collective-permute-start(f32[72,128]{1,0:T(8,128)S(1)} %get-tuple-element.45), channel_id=1, source_target_pairs={{0,24},{4,28},{8,16},{12,20},{16,8},{20,12},{24,0},{28,4},{1,25},{... | collective-permute-start | bytes 110600 | tf_op jit(solution)/shard_map/ppermute | solution.py:39
  16.9 4.4 %collective-permute-start.7 = (f32[72,128]{1,0:T(8,128)S(1)}, f32[72,128]{1,0:T(8,128)S(1)}, u32[]{:S(2)}, u32[]{:S(2)}) collective-permute-start(f32[72,128]{1,0:T(8,128)S(1)} %get-tuple-element.46), channel_id=1, source_target_pairs={{0,8},{4,12},{8,0},{12,4},{16,24},{20,28},{24,16},{28,20},{1,9},{5... | collective-permute-start | bytes 110600 | tf_op jit(solution)/shard_map/ppermute | solution.py:39
  21.6 5.7 %collective-permute-start.10 = (f32[136,128]{1,0:T(8,128)S(1)}, f32[136,128]{1,0:T(8,128)S(1)}, u32[]{:S(2)}, u32[]{:S(2)}) collective-permute-start(f32[136,128]{1,0:T(8,128)S(1)} %merge.2.refs_8_), channel_id=1, source_target_pairs={{0,16},{4,20},{8,24},{12,28},{16,0},{20,4},{24,8},{28,12},{1,17},{... | collective-permute-start | bytes 208904 | tf_op jit(solution)/shard_map/ppermute | solution.py:39
  22.6 6.2 %collective-permute-start.9 = (f32[136,128]{1,0:T(8,128)S(1)}, f32[136,128]{1,0:T(8,128)S(1)}, u32[]{:S(2)}, u32[]{:S(2)}) collective-permute-start(f32[136,128]{1,0:T(8,128)S(1)} %merge.2.refs_8_), channel_id=1, source_target_pairs={{0,24},{4,28},{8,16},{12,20},{16,8},{20,12},{24,0},{28,4},{1,25},{... | collective-permute-start | bytes 208904 | tf_op jit(solution)/shard_map/ppermute | solution.py:39
  23.9 5.1 %collective-permute-start.8 = (f32[136,128]{1,0:T(8,128)S(1)}, f32[136,128]{1,0:T(8,128)S(1)}, u32[]{:S(2)}, u32[]{:S(2)}) collective-permute-start(f32[136,128]{1,0:T(8,128)S(1)} %merge.2.refs_8_), channel_id=1, source_target_pairs={{0,8},{4,12},{8,0},{12,4},{16,24},{20,28},{24,16},{28,20},{1,9},{5... | collective-permute-start | bytes 208904 | tf_op jit(solution)/shard_map/ppermute | solution.py:39
  42.4 29.3 %collective-permute-start.17 = (f32[1368,128]{1,0:T(8,128)S(1)}, f32[1368,128]{1,0:T(8,128)S(1)}, u32[]{:S(2)}, u32[]{:S(2)}) collective-permute-start(f32[1368,128]{1,0:T(8,128)S(1)} %get-tuple-element.53.refs_2_), channel_id=1, source_target_pairs={{0,2},{2,0},{1,3},{3,1},{4,6},{6,4},{5,7},{7,5},{8,10},{10,8},{9,1... | collective-permute-start | bytes 2101256 | tf_op jit(solution)/shard_map/ppermute | solution.py:39
  43.0 8.0 %collective-permute-start.11 = (f32[136,128]{1,0:T(8,128)S(1)}, f32[136,128]{1,0:T(8,128)S(1)}, u32[]{:S(2)}, u32[]{:S(2)}) collective-permute-start(f32[136,128]{1,0:T(8,128)S(1)} %get-tuple-element.55), channel_id=1, source_target_pairs={{0,16},{4,20},{8,24},{12,28},{16,0},{20,4},{24,8},{28,12},{1,17},{... | collective-permute-start | bytes 208904 | tf_op jit(solution)/shard_map/ppermute | solution.py:39
  43.6 7.4 %collective-permute-start.12 = (f32[136,128]{1,0:T(8,128)S(1)}, f32[136,128]{1,0:T(8,128)S(1)}, u32[]{:S(2)}, u32[]{:S(2)}) collective-permute-start(f32[136,128]{1,0:T(8,128)S(1)} %get-tuple-element.56), channel_id=1, source_target_pairs={{0,24},{4,28},{8,16},{12,20},{16,8},{20,12},{24,0},{28,4},{1,25},{... | collective-permute-start | bytes 208904 | tf_op jit(solution)/shard_map/ppermute | solution.py:39
  45.9 5.4 %collective-permute-start.13 = (f32[136,128]{1,0:T(8,128)S(1)}, f32[136,128]{1,0:T(8,128)S(1)}, u32[]{:S(2)}, u32[]{:S(2)}) collective-permute-start(f32[136,128]{1,0:T(8,128)S(1)} %get-tuple-element.57), channel_id=1, source_target_pairs={{0,8},{4,12},{8,0},{12,4},{16,24},{20,28},{24,16},{28,20},{1,9},{5... | collective-permute-start | bytes 208904 | tf_op jit(solution)/shard_map/ppermute | solution.py:39
  51.4 7.1 %collective-permute-start.16 = (f32[136,128]{1,0:T(8,128)S(1)}, f32[136,128]{1,0:T(8,128)S(1)}, u32[]{:S(2)}, u32[]{:S(2)}) collective-permute-start(f32[136,128]{1,0:T(8,128)S(1)} %merge.3.refs_0_), channel_id=1, source_target_pairs={{0,16},{4,20},{8,24},{12,28},{16,0},{20,4},{24,8},{28,12},{1,17},{... | collective-permute-start | bytes 208904 | tf_op jit(solution)/shard_map/ppermute | solution.py:39
  52.0 7.2 %collective-permute-start.15 = (f32[136,128]{1,0:T(8,128)S(1)}, f32[136,128]{1,0:T(8,128)S(1)}, u32[]{:S(2)}, u32[]{:S(2)}) collective-permute-start(f32[136,128]{1,0:T(8,128)S(1)} %merge.3.refs_0_), channel_id=1, source_target_pairs={{0,24},{4,28},{8,16},{12,20},{16,8},{20,12},{24,0},{28,4},{1,25},{... | collective-permute-start | bytes 208904 | tf_op jit(solution)/shard_map/ppermute | solution.py:39
  55.1 4.7 %collective-permute-start.14 = (f32[136,128]{1,0:T(8,128)S(1)}, f32[136,128]{1,0:T(8,128)S(1)}, u32[]{:S(2)}, u32[]{:S(2)}) collective-permute-start(f32[136,128]{1,0:T(8,128)S(1)} %merge.3.refs_0_), channel_id=1, source_target_pairs={{0,8},{4,12},{8,0},{12,4},{16,24},{20,28},{24,16},{28,20},{1,9},{5... | collective-permute-start | bytes 208904 | tf_op jit(solution)/shard_map/ppermute | solution.py:39
  59.9 11.8 %collective-permute-start.18 = (f32[136,512]{1,0:T(8,128)S(1)}, f32[136,512]{1,0:T(8,128)S(1)}, u32[]{:S(2)}, u32[]{:S(2)}) collective-permute-start(f32[136,512]{1,0:T(8,128)S(1)} %join.1.refs_5_), channel_id=1, source_target_pairs={{0,2},{2,0},{1,3},{3,1},{4,6},{6,4},{5,7},{7,5},{8,10},{10,8},{9,1... | collective-permute-start | bytes 835592 | tf_op jit(solution)/shard_map/ppermute | solution.py:39
  61.3 10.3 %copy-start.4 = (f32[328,128]{1,0:T(8,128)S(1)}, f32[328,128]{1,0:T(8,128)}, u32[]{:S(2)}) copy-start(f32[328,128]{1,0:T(8,128)} %get-tuple-element.35.refs_5_) | copy-start | bytes 503812
  72.7 2.0 %collective-permute-start.19 = (f32[1040,128]{1,0:T(8,128)S(1)}, f32[1040,128]{1,0:T(8,128)S(1)}, u32[]{:S(2)}, u32[]{:S(2)}) collective-permute-start(f32[1040,128]{1,0:T(8,128)S(1)} %page_update.2.refs_6_), channel_id=1, source_target_pairs={{0,4},{4,0},{8,12},{12,8},{16,20},{20,16},{24,28},{28,24},{1,5},{5... | collective-permute-start | bytes 1597448 | tf_op jit(solution)/shard_map/ppermute | solution.py:39

commit v22 on v21

--- a/solution.py
+++ b/solution.py
@@ -155,7 +155,7 @@
     ranks = lax.axis_size("page") // CORES
     query_rows = part_rows * query_devices
     chunk, piece = query_rows // ranks, part_rows // ranks
-    turns = [ranks // 2] + [turn for turn in reversed(range(1, ranks)) if turn != ranks // 2]
+    turns = [ranks // 2] + [turn for turn in range(1, ranks) if turn != ranks // 2]
     slot_total = local_heads * head_devices * slot_rows * lax.axis_size("page")
     entry_total = slot_total * width
     score_scale = 1.0 / math.sqrt(width)

time: 75.9 us -> 78.8 us (1.038)
  starting transfers between devices: 24.4 us -> 27.5 us
    ppermute x20, starting transfers between devices: 24.4 us -> 27.5 us  [exchange(): return lax.ppermute(value, axes, pairs)]
  transfers between devices with their start and end apart: 20 -> 20, of which waited for: 11 -> 11; matrix products, arithmetic and copies ran while one was open for 0% -> 0% of each run, Pallas kernels for 7% -> 6%
where the time goes in v22:
time: 78.8 us; the launch traced here: 78.7 us
  starting transfers between devices  27.5 us (35%)
  blocking collectives  20.3 us (26%)
  waiting for transfers between devices  18.2 us (23%)
  Pallas kernels  11.8 us (15%)
  between operations  0.82 us (1%)
    ppermute x20, starting transfers between devices, exchange(): return lax.ppermute(value, axes, pairs)  27.5 us
    all_to_all x2, blocking collectives, direct_per_device(): lax.all_to_all(squares, ('page', 'query', 'head'), split_axis=0, concat_a...  20.3 us
    ppermute x20, waiting for transfers between devices, exchange(): return lax.ppermute(value, axes, pairs)  18.2 us
    pallas_call x13, Pallas kernels, call(): pl.pallas_call(without_after, out_shape=[jax.ShapeDtypeStruct(shape, jnp....  11.8 us
  transfers between devices with their start and end apart: 20, of which 11 were waited for; matrix products, arithmetic and copies ran while one was open for 0% of the time, Pallas kernels for 6%

profile of v22, /device:TPU:0, one launch (start us, length us, event | category | flops | bytes accessed | tf_op | source)
XLA Modules:
  0.0 78.7 jit_solution(5116637797409468656)
XLA Ops:
  0.7 2.0 %pack.1 = (f32[520,128]{1,0:T(8,128)}, f32[328,128]{1,0:T(8,128)}) custom-call(f32[4,256,128]{2,1,0:T(8,128)} %refs_0_.3, f32[4,256,128]{2,1,0:T(8,128)} %refs_1_.3, f32[4,256,128]{2,1,0:T(8,128)} %refs_2_.3, f32[4,256]{1,0:T(4,128)} %refs_3_.3, f32[4,256,128]{2,1,0:T(8,128)} %refs_4_.3, s32[4,256]{1,0:T(4,128)} %refs_5_.3, s32[8]{0:T(128)} %refs_6_.3), custom_call_target="tpu_custom_call" | custom-call | flops 1048576 | bytes 1048576 | tf_op jit(solution)/shard_map/pack/pallas_call | solution.py:85
  2.7 0.0 copy-start.7
  2.7 0.5 collective-permute-start
  3.3 2.6 %collective-permute-start.1 = (f32[328,128]{1,0:T(8,128)}, f32[328,128]{1,0:T(8,128)S(1)}, u32[]{:S(2)}, u32[]{:S(2)}) collective-permute-start(f32[328,128]{1,0:T(8,128)} %get-tuple-element.35.refs_5_), channel_id=1, source_target_pairs={{0,2},{2,0},{1,3},{3,1},{4,6},{6,4},{5,7},{7,5},{8,10},{10,8},{9,1... | collective-permute-start | bytes 503816 | tf_op jit(solution)/shard_map/ppermute | solution.py:39
  5.9 0.7 own.1
  6.6 0.9 %forward.2 = (f32[72,128]{1,0:T(8,128)S(1)}, f32[72,128]{1,0:T(8,128)S(1)}, f32[72,128]{1,0:T(8,128)S(1)}, f32[72,128]{1,0:T(8,128)S(1)}, f32[512,256]{1,0:T(8,128)S(1)}, /*index=5*/f32[8,256]{1,0:T(8,128)S(1)}) custom-call(f32[520,128]{1,0:T(8,128)S(1)} %get-tuple-element.32.refs_0_.refs_4_, f32[520,128]{1,0:T(8,128)S(1)} %collective-permute-done.refs_1_.refs_5_, ...), custom_call_target="tpu_custom_call" | custom-call | flops 201326592 | bytes 1048576 | tf_op jit(solution)/shard_map/forward/pallas_call | solution.py:85
  7.5 2.7 %collective-permute-start.2 = (f32[72,128]{1,0:T(8,128)S(1)}, f32[72,128]{1,0:T(8,128)S(1)}, u32[]{:S(2)}, u32[]{:S(2)}) collective-permute-start(f32[72,128]{1,0:T(8,128)S(1)} %get-tuple-element.40), channel_id=1, source_target_pairs={{0,16},{4,20},{8,24},{12,28},{16,0},{20,4},{24,8},{28,12},{1,17},{... | collective-permute-start | bytes 110600 | tf_op jit(solution)/shard_map/ppermute | solution.py:39
  10.2 1.6 %collective-permute-start.3 = (f32[72,128]{1,0:T(8,128)S(1)}, f32[72,128]{1,0:T(8,128)S(1)}, u32[]{:S(2)}, u32[]{:S(2)}) collective-permute-start(f32[72,128]{1,0:T(8,128)S(1)} %get-tuple-element.41), channel_id=1, source_target_pairs={{0,8},{4,12},{8,0},{12,4},{16,24},{20,28},{24,16},{28,20},{1,9},{5... | collective-permute-start | bytes 110600 | tf_op jit(solution)/shard_map/ppermute | solution.py:39
  11.7 0.2 collective-permute-start.4
  12.0 0.9 %forward.3 = (f32[72,128]{1,0:T(8,128)S(1)}, f32[72,128]{1,0:T(8,128)S(1)}, f32[72,128]{1,0:T(8,128)S(1)}, f32[72,128]{1,0:T(8,128)S(1)}, f32[512,256]{1,0:T(8,128)S(1)}, /*index=5*/f32[8,256]{1,0:T(8,128)S(1)}) custom-call(f32[520,128]{1,0:T(8,128)S(1)} %get-tuple-element.32.refs_0_.refs_4_, f32[520,128]{1,0:T(8,128)S(1)} %collective-permute-done.refs_1_.refs_5_, ...), custom_call_target="tpu_custom_call" | custom-call | flops 201326592 | bytes 1048576 | tf_op jit(solution)/shard_map/forward/pallas_call | solution.py:85
  12.9 1.9 %collective-permute-start.5 = (f32[72,128]{1,0:T(8,128)S(1)}, f32[72,128]{1,0:T(8,128)S(1)}, u32[]{:S(2)}, u32[]{:S(2)}) collective-permute-start(f32[72,128]{1,0:T(8,128)S(1)} %get-tuple-element.44), channel_id=1, source_target_pairs={{0,16},{4,20},{8,24},{12,28},{16,0},{20,4},{24,8},{28,12},{1,17},{... | collective-permute-start | bytes 110600 | tf_op jit(solution)/shard_map/ppermute | solution.py:39
  14.8 2.4 %collective-permute-start.6 = (f32[72,128]{1,0:T(8,128)S(1)}, f32[72,128]{1,0:T(8,128)S(1)}, u32[]{:S(2)}, u32[]{:S(2)}) collective-permute-start(f32[72,128]{1,0:T(8,128)S(1)} %get-tuple-element.45), channel_id=1, source_target_pairs={{0,8},{4,12},{8,0},{12,4},{16,24},{20,28},{24,16},{28,20},{1,9},{5... | collective-permute-start | bytes 110600 | tf_op jit(solution)/shard_map/ppermute | solution.py:39
  17.1 0.2 collective-permute-start.7
  17.3 0.5 collective-permute-done.4.refs_4_
  17.8 0.2 collective-permute-done.5.refs_6_
  18.1 1.0 %collective-permute-done.6.refs_7_ = f32[72,128]{1,0:T(8,128)S(1)} collective-permute-done((f32[72,128]{1,0:T(8,128)S(1)}, f32[72,128]{1,0:T(8,128)S(1)}, u32[]{:S(2)}, u32[]{:S(2)}) %collective-permute-start.6) | collective-permute-done | bytes 36896 | tf_op jit(solution)/shard_map/ppermute | solution.py:39
  19.1 4.2 %collective-permute-done.7.refs_8_ = f32[72,128]{1,0:T(8,128)S(1)} collective-permute-done((f32[72,128]{1,0:T(8,128)S(1)}, f32[72,128]{1,0:T(8,128)S(1)}, u32[]{:S(2)}, u32[]{:S(2)}) %collective-permute-start.7) | collective-permute-done | bytes 36896 | tf_op jit(solution)/shard_map/ppermute | solution.py:39
  23.2 0.3 merge.2.refs_8_
  23.5 0.1 collective-permute-start.10
  23.6 0.6 collective-permute-start.9
  24.2 3.8 %collective-permute-start.8 = (f32[136,128]{1,0:T(8,128)S(1)}, f32[136,128]{1,0:T(8,128)S(1)}, u32[]{:S(2)}, u32[]{:S(2)}) collective-permute-start(f32[136,128]{1,0:T(8,128)S(1)} %merge.2.refs_8_), channel_id=1, source_target_pairs={{0,24},{4,28},{8,16},{12,20},{16,8},{20,12},{24,0},{28,4},{1,25},{... | collective-permute-start | bytes 208904 | tf_op jit(solution)/shard_map/ppermute | solution.py:39
  27.9 0.9 %collective-permute-done.10.refs_11_ = f32[136,128]{1,0:T(8,128)S(1)} collective-permute-done((f32[136,128]{1,0:T(8,128)S(1)}, f32[136,128]{1,0:T(8,128)S(1)}, u32[]{:S(2)}, u32[]{:S(2)}) %collective-permute-start.10) | collective-permute-done | bytes 69664 | tf_op jit(solution)/shard_map/ppermute | solution.py:39
  28.8 0.5 collective-permute-done.9.refs_10_
  29.3 1.6 %collective-permute-done.8.refs_9_ = f32[136,128]{1,0:T(8,128)S(1)} collective-permute-done((f32[136,128]{1,0:T(8,128)S(1)}, f32[136,128]{1,0:T(8,128)S(1)}, u32[]{:S(2)}, u32[]{:S(2)}) %collective-permute-start.8) | collective-permute-done | bytes 69664 | tf_op jit(solution)/shard_map/ppermute | solution.py:39
  31.0 1.4 %backward.2 = (f32[520,128]{1,0:T(8,128)S(1)}, f32[520,128]{1,0:T(8,128)S(1)}, f32[32,1,128]{2,1,0:T(1,128)S(1)}) custom-call(f32[512,256]{1,0:T(8,128)S(1)} %get-tuple-element.36.refs_0_, f32[512,256]{1,0:T(8,128)S(1)} %get-tuple-element.38.refs_1_, f32[8,256]{1,0:T(8,128)S(1)} %get-tuple-element.37.refs_3_.refs_2_, ...), custom_call_target="tpu_custom_call" | custom-call | flops 603979776 | bytes 1048576 | tf_op jit(solution)/shard_map/backward/pallas_call | solution.py:85
  32.3 11.4 %all_to_all.10.refs_6_ = f32[32,1,128]{2,1,0:T(1,128)S(1)} all-to-all(f32[32,1,128]{2,1,0:T(1,128)S(1)} %get-tuple-element.50), channel_id=1, replica_groups=mesh['page'=8,'query'=2,'head'=2] {'page','query','head'}, dimensions={0} | all-to-all | bytes 32768 | tf_op jit(solution)/shard_map/all_to_all | solution.py:642
  43.7 1.1 %update_forward.1 = (f32[1368,128]{1,0:T(8,128)S(1)}, f32[136,128]{1,0:T(8,128)S(1)}, f32[136,128]{1,0:T(8,128)S(1)}, f32[136,128]{1,0:T(8,128)S(1)}, f32[136,12...) custom-call(f32[520,128]{1,0:T(8,128)S(1)} %get-tuple-element.32.refs_0_.refs_4_, ...), custom_call_target="tpu_custom_call" | custom-call | flops 402653184 | bytes 1048576 | tf_op jit(solution)/shard_map/update_forward/pallas_call | solution.py:85
  44.8 0.6 collective-permute-start.17
  45.4 0.6 collective-permute-start.11
  46.0 0.5 collective-permute-start.12
  46.6 3.3 %collective-permute-start.13 = (f32[136,128]{1,0:T(8,128)S(1)}, f32[136,128]{1,0:T(8,128)S(1)}, u32[]{:S(2)}, u32[]{:S(2)}) collective-permute-start(f32[136,128]{1,0:T(8,128)S(1)} %get-tuple-element.57), channel_id=1, source_target_pairs={{0,24},{4,28},{8,16},{12,20},{16,8},{20,12},{24,0},{28,4},{1,25},{... | collective-permute-start | bytes 208904 | tf_op jit(solution)/shard_map/ppermute | solution.py:39
  49.8 3.9 %collective-permute-done.11.refs_3_ = f32[136,128]{1,0:T(8,128)S(1)} collective-permute-done((f32[136,128]{1,0:T(8,128)S(1)}, f32[136,128]{1,0:T(8,128)S(1)}, u32[]{:S(2)}, u32[]{:S(2)}) %collective-permute-start.11) | collective-permute-done | bytes 69664 | tf_op jit(solution)/shard_map/ppermute | solution.py:39
  53.7 0.1 merge.3.refs_0_
  53.8 0.4 collective-permute-start.16
  54.2 2.5 %collective-permute-start.15 = (f32[136,128]{1,0:T(8,128)S(1)}, f32[136,128]{1,0:T(8,128)S(1)}, u32[]{:S(2)}, u32[]{:S(2)}) collective-permute-start(f32[136,128]{1,0:T(8,128)S(1)} %merge.3.refs_0_), channel_id=1, source_target_pairs={{0,8},{4,12},{8,0},{12,4},{16,24},{20,28},{24,16},{28,20},{1,9},{5... | collective-permute-start | bytes 208904 | tf_op jit(solution)/shard_map/ppermute | solution.py:39
  56.7 1.6 %collective-permute-start.14 = (f32[136,128]{1,0:T(8,128)S(1)}, f32[136,128]{1,0:T(8,128)S(1)}, u32[]{:S(2)}, u32[]{:S(2)}) collective-permute-start(f32[136,128]{1,0:T(8,128)S(1)} %merge.3.refs_0_), channel_id=1, source_target_pairs={{0,24},{4,28},{8,16},{12,20},{16,8},{20,12},{24,0},{28,4},{1,25},{... | collective-permute-start | bytes 208904 | tf_op jit(solution)/shard_map/ppermute | solution.py:39
  58.3 3.0 %collective-permute-done.16.refs_3_ = f32[136,128]{1,0:T(8,128)S(1)} collective-permute-done((f32[136,128]{1,0:T(8,128)S(1)}, f32[136,128]{1,0:T(8,128)S(1)}, u32[]{:S(2)}, u32[]{:S(2)}) %collective-permute-start.16) | collective-permute-done | bytes 69664 | tf_op jit(solution)/shard_map/ppermute | solution.py:39
  61.2 0.0 collective-permute-done.15.refs_2_
  61.2 1.5 %collective-permute-done.14.refs_1_ = f32[136,128]{1,0:T(8,128)S(1)} collective-permute-done((f32[136,128]{1,0:T(8,128)S(1)}, f32[136,128]{1,0:T(8,128)S(1)}, u32[]{:S(2)}, u32[]{:S(2)}) %collective-permute-start.14) | collective-permute-done | bytes 69664 | tf_op jit(solution)/shard_map/ppermute | solution.py:39
  62.8 0.1 join.1.refs_5_
  62.8 1.6 %collective-permute-start.18 = (f32[136,512]{1,0:T(8,128)S(1)}, f32[136,512]{1,0:T(8,128)S(1)}, u32[]{:S(2)}, u32[]{:S(2)}) collective-permute-start(f32[136,512]{1,0:T(8,128)S(1)} %join.1.refs_5_), channel_id=1, source_target_pairs={{0,2},{2,0},{1,3},{3,1},{4,6},{6,4},{5,7},{7,5},{8,10},{10,8},{9,1... | collective-permute-start | bytes 835592 | tf_op jit(solution)/shard_map/ppermute | solution.py:39
  64.4 1.3 %backward.3 = (f32[520,128]{1,0:T(8,128)S(1)}, f32[520,128]{1,0:T(8,128)S(1)}, f32[32,1,128]{2,1,0:T(1,128)S(1)}) custom-call(f32[512,512]{1,0:T(8,128)S(1)} %get-tuple-element.51.refs_0_, f32[8,512]{1,0:T(8,128)S(1)} %get-tuple-element.52.refs_1_, f32[1368,128]{1,0:T(8,128)S(1)} %get-tuple-element.53.refs_2_, ...), custom_call_target="tpu_custom_call" | custom-call | flops 603979776 | bytes 1048576 | tf_op jit(solution)/shard_map/backward/pallas_call | solution.py:85
  65.7 8.9 %all_to_all.11.refs_0_ = f32[32,1,128]{2,1,0:T(1,128)S(1)} all-to-all(f32[32,1,128]{2,1,0:T(1,128)S(1)} %get-tuple-element.58), channel_id=1, replica_groups=mesh['page'=8,'query'=2,'head'=2] {'page','query','head'}, dimensions={0} | all-to-all | bytes 32768 | tf_op jit(solution)/shard_map/all_to_all | solution.py:642
  74.6 1.0 %page_update.2.refs_6_ = f32[1040,128]{1,0:T(8,128)S(1)} custom-call(f32[32,1,128]{2,1,0:T(1,128)S(1)} %all_to_all.11.refs_0_, f32[520,128]{1,0:T(8,128)S(1)} %get-tuple-element.60.refs_1_, f32[1368,128]{1,0:T(8,128)S(1)} %get-tuple-element.53.refs_2_, f32[1368,128]{1,0:T(8,128)S(1)} %collective-permute-done.17.refs_3_, ...), custom_call_target="tpu_custom_call" | custom-call | flops 301989888 | bytes 1048576 | tf_op jit(solution)/shard_map/page_update/pallas_call | solution.py:85
  75.6 0.1 collective-permute-start.19
  75.7 1.0 %page_update.3.refs_0_ = f32[1040,128]{1,0:T(8,128)S(1)} custom-call(f32[32,1,128]{2,1,0:T(1,128)S(1)} %all_to_all.11.refs_0_, f32[520,128]{1,0:T(8,128)S(1)} %get-tuple-element.59.refs_1_, f32[1368,128]{1,0:T(8,128)S(1)} %get-tuple-element.53.refs_2_, f32[1368,128]{1,0:T(8,128)S(1)} %collective-permute-done.17.refs_3_, ...), custom_call_target="tpu_custom_call" | custom-call | flops 301989888 | bytes 1048576 | tf_op jit(solution)/shard_map/page_update/pallas_call | solution.py:85
  76.7 0.9 %collective-permute-done.19.refs_1_ = f32[1040,128]{1,0:T(8,128)S(1)} collective-permute-done((f32[1040,128]{1,0:T(8,128)S(1)}, f32[1040,128]{1,0:T(8,128)S(1)}, u32[]{:S(2)}, u32[]{:S(2)}) %collective-permute-start.19) | collective-permute-done | bytes 532512 | tf_op jit(solution)/shard_map/ppermute | solution.py:39
  77.6 1.0 %unpack.1 = (f32[4,256,128]{2,1,0:T(8,128)}, f32[4,256,128]{2,1,0:T(8,128)}, f32[4,256]{1,0:T(4,128)}) custom-call(f32[1040,128]{1,0:T(8,128)S(1)} %page_update.3.refs_0_, f32[1040,128]{1,0:T(8,128)S(1)} %collective-permute-done.19.refs_1_), custom_call_target="tpu_custom_call" | custom-call | flops 1048576 | bytes 1048576 | tf_op jit(solution)/shard_map/unpack/pallas_call | solution.py:85
  (23 shorter events, 0.1 us)
Async XLA Ops:
  0.6 5.2 %copy-start.3 = (f32[4,256,128]{2,1,0:T(8,128)S(1)}, f32[4,256,128]{2,1,0:T(8,128)}, u32[]{:S(2)}) copy-start(f32[4,256,128]{2,1,0:T(8,128)} %refs_4_.3) | copy-start | bytes 1572868
  0.6 5.2 %copy-start.2 = (f32[4,256,128]{2,1,0:T(8,128)S(1)}, f32[4,256,128]{2,1,0:T(8,128)}, u32[]{:S(2)}) copy-start(f32[4,256,128]{2,1,0:T(8,128)} %refs_2_.3) | copy-start | bytes 1572868
  0.7 5.2 %copy-start.1 = (f32[4,256,128]{2,1,0:T(8,128)S(1)}, f32[4,256,128]{2,1,0:T(8,128)}, u32[]{:S(2)}) copy-start(f32[4,256,128]{2,1,0:T(8,128)} %refs_1_.3) | copy-start | bytes 1572868
  0.7 5.2 %copy-start = (f32[4,256,128]{2,1,0:T(8,128)S(1)}, f32[4,256,128]{2,1,0:T(8,128)}, u32[]{:S(2)}) copy-start(f32[4,256,128]{2,1,0:T(8,128)} %refs_0_.3) | copy-start | bytes 1572868
  0.7 5.2 %copy-start.5 = (f32[4,256]{1,0:T(4,128)S(1)}, f32[4,256]{1,0:T(4,128)}, u32[]{:S(2)}) copy-start(f32[4,256]{1,0:T(4,128)} %refs_3_.3) | copy-start | bytes 12292
  0.7 5.2 %copy-start.6 = (s32[4,256]{1,0:T(4,128)S(1)}, s32[4,256]{1,0:T(4,128)}, u32[]{:S(2)}) copy-start(s32[4,256]{1,0:T(4,128)} %refs_5_.3) | copy-start | bytes 12292
  2.7 3.2 %copy-start.7 = (s32[8]{0:T(128)S(1)}, s32[8]{0:T(128)}, u32[]{:S(2)}) copy-start(s32[8]{0:T(128)} %refs_6_.3) | copy-start | bytes 100
  2.7 3.8 %collective-permute-start = (f32[520,128]{1,0:T(8,128)}, f32[520,128]{1,0:T(8,128)S(1)}, u32[]{:S(2)}, u32[]{:S(2)}) collective-permute-start(f32[520,128]{1,0:T(8,128)} %get-tuple-element.33), channel_id=1, source_target_pairs={{0,4},{4,0},{8,12},{12,8},{16,20},{20,16},{24,28},{28,24},{1,5},{5... | collective-permute-start | bytes 798728 | tf_op jit(solution)/shard_map/ppermute | solution.py:39
  3.3 8.7 %collective-permute-start.1 = (f32[328,128]{1,0:T(8,128)}, f32[328,128]{1,0:T(8,128)S(1)}, u32[]{:S(2)}, u32[]{:S(2)}) collective-permute-start(f32[328,128]{1,0:T(8,128)} %get-tuple-element.35.refs_5_), channel_id=1, source_target_pairs={{0,2},{2,0},{1,3},{3,1},{4,6},{6,4},{5,7},{7,5},{8,10},{10,8},{9,1... | collective-permute-start | bytes 503816 | tf_op jit(solution)/shard_map/ppermute | solution.py:39
  7.5 9.6 %collective-permute-start.2 = (f32[72,128]{1,0:T(8,128)S(1)}, f32[72,128]{1,0:T(8,128)S(1)}, u32[]{:S(2)}, u32[]{:S(2)}) collective-permute-start(f32[72,128]{1,0:T(8,128)S(1)} %get-tuple-element.40), channel_id=1, source_target_pairs={{0,16},{4,20},{8,24},{12,28},{16,0},{20,4},{24,8},{28,12},{1,17},{... | collective-permute-start | bytes 110600 | tf_op jit(solution)/shard_map/ppermute | solution.py:39
  10.2 7.2 %collective-permute-start.3 = (f32[72,128]{1,0:T(8,128)S(1)}, f32[72,128]{1,0:T(8,128)S(1)}, u32[]{:S(2)}, u32[]{:S(2)}) collective-permute-start(f32[72,128]{1,0:T(8,128)S(1)} %get-tuple-element.41), channel_id=1, source_target_pairs={{0,8},{4,12},{8,0},{12,4},{16,24},{20,28},{24,16},{28,20},{1,9},{5... | collective-permute-start | bytes 110600 | tf_op jit(solution)/shard_map/ppermute | solution.py:39
  11.7 6.1 %collective-permute-start.4 = (f32[72,128]{1,0:T(8,128)S(1)}, f32[72,128]{1,0:T(8,128)S(1)}, u32[]{:S(2)}, u32[]{:S(2)}) collective-permute-start(f32[72,128]{1,0:T(8,128)S(1)} %get-tuple-element.42), channel_id=1, source_target_pairs={{0,24},{4,28},{8,16},{12,20},{16,8},{20,12},{24,0},{28,4},{1,25},{... | collective-permute-start | bytes 110600 | tf_op jit(solution)/shard_map/ppermute | solution.py:39
  12.9 5.2 %collective-permute-start.5 = (f32[72,128]{1,0:T(8,128)S(1)}, f32[72,128]{1,0:T(8,128)S(1)}, u32[]{:S(2)}, u32[]{:S(2)}) collective-permute-start(f32[72,128]{1,0:T(8,128)S(1)} %get-tuple-element.44), channel_id=1, source_target_pairs={{0,16},{4,20},{8,24},{12,28},{16,0},{20,4},{24,8},{28,12},{1,17},{... | collective-permute-start | bytes 110600 | tf_op jit(solution)/shard_map/ppermute | solution.py:39
  14.8 4.3 %collective-permute-start.6 = (f32[72,128]{1,0:T(8,128)S(1)}, f32[72,128]{1,0:T(8,128)S(1)}, u32[]{:S(2)}, u32[]{:S(2)}) collective-permute-start(f32[72,128]{1,0:T(8,128)S(1)} %get-tuple-element.45), channel_id=1, source_target_pairs={{0,8},{4,12},{8,0},{12,4},{16,24},{20,28},{24,16},{28,20},{1,9},{5... | collective-permute-start | bytes 110600 | tf_op jit(solution)/shard_map/ppermute | solution.py:39
  17.1 6.1 %collective-permute-start.7 = (f32[72,128]{1,0:T(8,128)S(1)}, f32[72,128]{1,0:T(8,128)S(1)}, u32[]{:S(2)}, u32[]{:S(2)}) collective-permute-start(f32[72,128]{1,0:T(8,128)S(1)} %get-tuple-element.46), channel_id=1, source_target_pairs={{0,24},{4,28},{8,16},{12,20},{16,8},{20,12},{24,0},{28,4},{1,25},{... | collective-permute-start | bytes 110600 | tf_op jit(solution)/shard_map/ppermute | solution.py:39
  23.5 5.3 %collective-permute-start.10 = (f32[136,128]{1,0:T(8,128)S(1)}, f32[136,128]{1,0:T(8,128)S(1)}, u32[]{:S(2)}, u32[]{:S(2)}) collective-permute-start(f32[136,128]{1,0:T(8,128)S(1)} %merge.2.refs_8_), channel_id=1, source_target_pairs={{0,16},{4,20},{8,24},{12,28},{16,0},{20,4},{24,8},{28,12},{1,17},{... | collective-permute-start | bytes 208904 | tf_op jit(solution)/shard_map/ppermute | solution.py:39
  23.6 5.8 %collective-permute-start.9 = (f32[136,128]{1,0:T(8,128)S(1)}, f32[136,128]{1,0:T(8,128)S(1)}, u32[]{:S(2)}, u32[]{:S(2)}) collective-permute-start(f32[136,128]{1,0:T(8,128)S(1)} %merge.2.refs_8_), channel_id=1, source_target_pairs={{0,8},{4,12},{8,0},{12,4},{16,24},{20,28},{24,16},{28,20},{1,9},{5... | collective-permute-start | bytes 208904 | tf_op jit(solution)/shard_map/ppermute | solution.py:39
  24.2 6.8 %collective-permute-start.8 = (f32[136,128]{1,0:T(8,128)S(1)}, f32[136,128]{1,0:T(8,128)S(1)}, u32[]{:S(2)}, u32[]{:S(2)}) collective-permute-start(f32[136,128]{1,0:T(8,128)S(1)} %merge.2.refs_8_), channel_id=1, source_target_pairs={{0,24},{4,28},{8,16},{12,20},{16,8},{20,12},{24,0},{28,4},{1,25},{... | collective-permute-start | bytes 208904 | tf_op jit(solution)/shard_map/ppermute | solution.py:39
  44.8 29.8 %collective-permute-start.17 = (f32[1368,128]{1,0:T(8,128)S(1)}, f32[1368,128]{1,0:T(8,128)S(1)}, u32[]{:S(2)}, u32[]{:S(2)}) collective-permute-start(f32[1368,128]{1,0:T(8,128)S(1)} %get-tuple-element.53.refs_2_), channel_id=1, source_target_pairs={{0,2},{2,0},{1,3},{3,1},{4,6},{6,4},{5,7},{7,5},{8,10},{10,8},{9,1... | collective-permute-start | bytes 2101256 | tf_op jit(solution)/shard_map/ppermute | solution.py:39
  45.4 8.2 %collective-permute-start.11 = (f32[136,128]{1,0:T(8,128)S(1)}, f32[136,128]{1,0:T(8,128)S(1)}, u32[]{:S(2)}, u32[]{:S(2)}) collective-permute-start(f32[136,128]{1,0:T(8,128)S(1)} %get-tuple-element.55), channel_id=1, source_target_pairs={{0,16},{4,20},{8,24},{12,28},{16,0},{20,4},{24,8},{28,12},{1,17},{... | collective-permute-start | bytes 208904 | tf_op jit(solution)/shard_map/ppermute | solution.py:39
  46.0 7.7 %collective-permute-start.12 = (f32[136,128]{1,0:T(8,128)S(1)}, f32[136,128]{1,0:T(8,128)S(1)}, u32[]{:S(2)}, u32[]{:S(2)}) collective-permute-start(f32[136,128]{1,0:T(8,128)S(1)} %get-tuple-element.56), channel_id=1, source_target_pairs={{0,8},{4,12},{8,0},{12,4},{16,24},{20,28},{24,16},{28,20},{1,9},{5... | collective-permute-start | bytes 208904 | tf_op jit(solution)/shard_map/ppermute | solution.py:39
  46.6 7.1 %collective-permute-start.13 = (f32[136,128]{1,0:T(8,128)S(1)}, f32[136,128]{1,0:T(8,128)S(1)}, u32[]{:S(2)}, u32[]{:S(2)}) collective-permute-start(f32[136,128]{1,0:T(8,128)S(1)} %get-tuple-element.57), channel_id=1, source_target_pairs={{0,24},{4,28},{8,16},{12,20},{16,8},{20,12},{24,0},{28,4},{1,25},{... | collective-permute-start | bytes 208904 | tf_op jit(solution)/shard_map/ppermute | solution.py:39
  53.8 7.4 %collective-permute-start.16 = (f32[136,128]{1,0:T(8,128)S(1)}, f32[136,128]{1,0:T(8,128)S(1)}, u32[]{:S(2)}, u32[]{:S(2)}) collective-permute-start(f32[136,128]{1,0:T(8,128)S(1)} %merge.3.refs_0_), channel_id=1, source_target_pairs={{0,16},{4,20},{8,24},{12,28},{16,0},{20,4},{24,8},{28,12},{1,17},{... | collective-permute-start | bytes 208904 | tf_op jit(solution)/shard_map/ppermute | solution.py:39
  54.2 7.1 %collective-permute-start.15 = (f32[136,128]{1,0:T(8,128)S(1)}, f32[136,128]{1,0:T(8,128)S(1)}, u32[]{:S(2)}, u32[]{:S(2)}) collective-permute-start(f32[136,128]{1,0:T(8,128)S(1)} %merge.3.refs_0_), channel_id=1, source_target_pairs={{0,8},{4,12},{8,0},{12,4},{16,24},{20,28},{24,16},{28,20},{1,9},{5... | collective-permute-start | bytes 208904 | tf_op jit(solution)/shard_map/ppermute | solution.py:39
  56.7 6.1 %collective-permute-start.14 = (f32[136,128]{1,0:T(8,128)S(1)}, f32[136,128]{1,0:T(8,128)S(1)}, u32[]{:S(2)}, u32[]{:S(2)}) collective-permute-start(f32[136,128]{1,0:T(8,128)S(1)} %merge.3.refs_0_), channel_id=1, source_target_pairs={{0,24},{4,28},{8,16},{12,20},{16,8},{20,12},{24,0},{28,4},{1,25},{... | collective-permute-start | bytes 208904 | tf_op jit(solution)/shard_map/ppermute | solution.py:39
  62.8 11.8 %collective-permute-start.18 = (f32[136,512]{1,0:T(8,128)S(1)}, f32[136,512]{1,0:T(8,128)S(1)}, u32[]{:S(2)}, u32[]{:S(2)}) collective-permute-start(f32[136,512]{1,0:T(8,128)S(1)} %join.1.refs_5_), channel_id=1, source_target_pairs={{0,2},{2,0},{1,3},{3,1},{4,6},{6,4},{5,7},{7,5},{8,10},{10,8},{9,1... | collective-permute-start | bytes 835592 | tf_op jit(solution)/shard_map/ppermute | solution.py:39
  64.4 10.2 %copy-start.4 = (f32[328,128]{1,0:T(8,128)S(1)}, f32[328,128]{1,0:T(8,128)}, u32[]{:S(2)}) copy-start(f32[328,128]{1,0:T(8,128)} %get-tuple-element.35.refs_5_) | copy-start | bytes 503812
  75.6 2.0 %collective-permute-start.19 = (f32[1040,128]{1,0:T(8,128)S(1)}, f32[1040,128]{1,0:T(8,128)S(1)}, u32[]{:S(2)}, u32[]{:S(2)}) collective-permute-start(f32[1040,128]{1,0:T(8,128)S(1)} %page_update.2.refs_6_), channel_id=1, source_target_pairs={{0,4},{4,0},{8,12},{12,8},{16,20},{20,16},{24,28},{28,24},{1,5},{5... | collective-permute-start | bytes 1597448 | tf_op jit(solution)/shard_map/ppermute | solution.py:39

commit v23 on v21

--- a/solution.py
+++ b/solution.py
@@ -130,7 +130,7 @@
     width = queries.shape[2]
     if any(size & (size - 1) for size in sizes) or pages < CORES or width % 128:
         return False
-    if local_heads != CORES * query_devices:
+    if local_heads != CORES * query_devices or query_devices < 2:
         return False
     ranks = pages // CORES
     chunk = part_rows * query_devices // ranks
@@ -553,16 +553,21 @@
         for at in range(devices):
             squares_out[at] = row
 
-    def page_body(at):
-        def body(tile_ref, grad_ref, own_state_ref, *refs):
+    def own_update(tile_ref, state_ref, grad_ref, at):
+        state = read_pack(part_of(state_ref, at))
+        return updated(state, read_pack(grad_ref), step_sizes([tile_ref]))
+
+    def own_page_body(tile_ref, state_ref, grad_ref, out):
+        store_pack(out, own_update(tile_ref, state_ref, grad_ref, 1))
+
+    def other_page_body(at):
+        def body(tile_ref, *refs):
             state_refs, refs = refs[: query_devices - 1], refs[query_devices - 1 :]
             joined_refs, (*pack_refs, out) = refs[: query_devices - 1], refs[query_devices - 1 :]
             sizes = step_sizes([tile_ref])
-            state = read_pack(part_of(own_state_ref, at))
-            store_pack(part_of(out, 0), updated(state, read_pack(grad_ref), sizes))
-            for turn, (state_ref, joined_ref) in enumerate(zip(state_refs, joined_refs), 1):
+            for other, (state_ref, joined_ref) in enumerate(zip(state_refs, joined_refs)):
                 query_refs = [state_ref.at[pl.ds(CORES * packed_rows, query_shape[0])]]
-                query_refs += pack_refs[(turn - 1) * (query_devices - 1) :][: query_devices - 1]
+                query_refs += pack_refs[other * (query_devices - 1) :][: query_devices - 1]
                 residual, row_max, row_total, row_delta = split_merged(joined_ref[...])
                 all_queries = read_queries(query_refs)
                 ref = part_of(state_ref, at)
@@ -571,7 +576,7 @@
                 grads = page_gradients(
                     weights, 1.0 / row_total, ref, all_queries, residual, row_delta
                 )
-                store_pack(part_of(out, turn), updated(read_pack(ref), grads, sizes))
+                store_pack(part_of(out, other), updated(read_pack(ref), grads, sizes))
 
         return body
 
@@ -649,29 +654,38 @@
         for turn in range(1, query_devices)
         for part in range(1, query_devices)
     ]
-    operands = new_states + all_joined[1:] + other_packs
-    pages = []
-    for at, grad in ((1, mate_grad), (0, own_grad)):
-        pages += call(
-            page_body(at),
-            [(query_devices * packed_rows, width)],
-            "page_update",
+    (own_for_mate,) = call(
+        own_page_body, packed_shapes[:1], "own_update", 2**20, tiles + states + [mate_grad]
+    )
+    before, others = [own_for_mate], []
+    for at in reversed(range(CORES)):
+        others += call(
+            other_page_body(at),
+            [((query_devices - 1) * packed_rows, width)],
+            "other_update",
             3 * matmul_cost // 2,
-            tiles + [grad] + operands,
-            after=pages,
-        )
-    pages = [pages[1], exchange(pages[0], page=1)]
-
-    def last_body(*refs):
-        page_refs, (keys_out, values_out, bias_out) = refs[:CORES], refs[CORES:]
+            tiles + new_states[1:] + all_joined[1:] + other_packs,
+            after=before,
+        )
+        before = others[-1:]
+    others_for_mate, own_page_others = others
+    from_mate = [exchange(own_for_mate, page=1), exchange(others_for_mate, page=1)]
+
+    def last_body(tile_ref, state_ref, grad_ref, *refs):
+        others_ref, mate_ref, mate_others_ref, keys_out, values_out, bias_out = refs
         _, core, me = places()
         for turn, flip in itertools.product(range(query_devices), range(CORES)):
-            keys, values, bias = read_pack(part_of(page_refs[flip], turn))
+            if turn:
+                values = read_pack(part_of(mate_others_ref if flip else others_ref, turn - 1))
+            elif flip:
+                values = read_pack(mate_ref)
+            else:
+                values = own_update(tile_ref, state_ref, grad_ref, 0)
             head = CORES * (me ^ turn) + (core ^ flip)
-            keys_out[head] = keys
-            values_out[head] = values
-            bias_row = jnp.concatenate([bias[row : row + 1] for row in range(bias_rows)], axis=1)
-            bias_out[pl.ds(head, 1), :] = bias_row
+            keys_out[head] = values[0]
+            values_out[head] = values[1]
+            bias_row = [values[2][row : row + 1] for row in range(bias_rows)]
+            bias_out[pl.ds(head, 1), :] = jnp.concatenate(bias_row, axis=1)
 
     return tuple(
         call(
@@ -679,7 +693,7 @@
             [compact_keys.shape, compact_values.shape, slot_bias.shape],
             "unpack",
             2**20,
-            pages,
+            tiles + states + [own_grad, own_page_others] + from_mate,
         )
     )
 

time: 75.9 us -> 76.5 us (level)
    ppermute x20 -> x21, waiting for transfers between devices: 18.7 us -> 18.3 us  [exchange(): return lax.ppermute(value, axes, pairs)]
    pallas_call x13 -> x14, Pallas kernels: 11.8 us -> 11.9 us  [call(): pl.pallas_call(without_after, out_shape=[jax.ShapeDtypeStruct(shape, jnp....]
    ppermute x20 -> x21, starting transfers between devices: 24.4 us -> 24.5 us  [exchange(): return lax.ppermute(value, axes, pairs)]
  transfers between devices with their start and end apart: 20 -> 21, of which waited for: 11 -> 11; matrix products, arithmetic and copies ran while one was open for 0% -> 0% of each run, Pallas kernels for 7% -> 8%
where the time goes in v23:
time: 76.5 us; the launch traced here: 76.3 us
  starting transfers between devices  24.5 us (32%)
  blocking collectives  20 us (26%)
  waiting for transfers between devices  18.3 us (24%)
  Pallas kernels  11.9 us (16%)
  between operations  0.87 us (1%)
    ppermute x21, starting transfers between devices, exchange(): return lax.ppermute(value, axes, pairs)  24.5 us
    all_to_all x2, blocking collectives, direct_per_device(): lax.all_to_all(squares, ('page', 'query', 'head'), split_axis=0, concat_a...  20 us
    ppermute x21, waiting for transfers between devices, exchange(): return lax.ppermute(value, axes, pairs)  18.3 us
    pallas_call x14, Pallas kernels, call(): pl.pallas_call(without_after, out_shape=[jax.ShapeDtypeStruct(shape, jnp....  11.9 us
  transfers between devices with their start and end apart: 21, of which 11 were waited for; matrix products, arithmetic and copies ran while one was open for 0% of the time, Pallas kernels for 8%

profile of v23, /device:TPU:0, one launch (start us, length us, event | category | flops | bytes accessed | tf_op | source)
XLA Modules:
  0.0 76.3 jit_solution(2489137033158990204)
XLA Ops:
  0.7 2.0 %pack.1 = (f32[520,128]{1,0:T(8,128)}, f32[328,128]{1,0:T(8,128)}) custom-call(f32[4,256,128]{2,1,0:T(8,128)} %refs_0_.3, f32[4,256,128]{2,1,0:T(8,128)} %refs_1_.3, f32[4,256,128]{2,1,0:T(8,128)} %refs_2_.3, f32[4,256]{1,0:T(4,128)} %refs_3_.3, f32[4,256,128]{2,1,0:T(8,128)} %refs_4_.3, s32[4,256]{1,0:T(4,128)} %refs_5_.3, s32[8]{0:T(128)} %refs_6_.3), custom_call_target="tpu_custom_call" | custom-call | flops 1048576 | bytes 1048576 | tf_op jit(solution)/shard_map/pack/pallas_call | solution.py:85
  2.7 0.0 copy-start.7
  2.7 0.5 collective-permute-start
  3.3 2.6 %collective-permute-start.1 = (f32[328,128]{1,0:T(8,128)}, f32[328,128]{1,0:T(8,128)S(1)}, u32[]{:S(2)}, u32[]{:S(2)}) collective-permute-start(f32[328,128]{1,0:T(8,128)} %get-tuple-element.35.refs_3_), channel_id=1, source_target_pairs={{0,2},{2,0},{1,3},{3,1},{4,6},{6,4},{5,7},{7,5},{8,10},{10,8},{9,1... | collective-permute-start | bytes 503816 | tf_op jit(solution)/shard_map/ppermute | solution.py:39
  5.9 0.7 own.1
  6.6 0.9 %forward.2 = (f32[72,128]{1,0:T(8,128)S(1)}, f32[72,128]{1,0:T(8,128)S(1)}, f32[72,128]{1,0:T(8,128)S(1)}, f32[72,128]{1,0:T(8,128)S(1)}, f32[512,256]{1,0:T(8,128)S(1)}, /*index=5*/f32[8,256]{1,0:T(8,128)S(1)}) custom-call(f32[520,128]{1,0:T(8,128)S(1)} %get-tuple-element.32.refs_0_.refs_4_, f32[520,128]{1,0:T(8,128)S(1)} %collective-permute-done.refs_1_.refs_5_, ...), custom_call_target="tpu_custom_call" | custom-call | flops 201326592 | bytes 1048576 | tf_op jit(solution)/shard_map/forward/pallas_call | solution.py:85
  7.5 2.7 %collective-permute-start.2 = (f32[72,128]{1,0:T(8,128)S(1)}, f32[72,128]{1,0:T(8,128)S(1)}, u32[]{:S(2)}, u32[]{:S(2)}) collective-permute-start(f32[72,128]{1,0:T(8,128)S(1)} %get-tuple-element.40), channel_id=1, source_target_pairs={{0,16},{4,20},{8,24},{12,28},{16,0},{20,4},{24,8},{28,12},{1,17},{... | collective-permute-start | bytes 110600 | tf_op jit(solution)/shard_map/ppermute | solution.py:39
  10.2 1.3 %collective-permute-start.3 = (f32[72,128]{1,0:T(8,128)S(1)}, f32[72,128]{1,0:T(8,128)S(1)}, u32[]{:S(2)}, u32[]{:S(2)}) collective-permute-start(f32[72,128]{1,0:T(8,128)S(1)} %get-tuple-element.41), channel_id=1, source_target_pairs={{0,24},{4,28},{8,16},{12,20},{16,8},{20,12},{24,0},{28,4},{1,25},{... | collective-permute-start | bytes 110600 | tf_op jit(solution)/shard_map/ppermute | solution.py:39
  11.5 0.2 collective-permute-start.4
  11.7 0.9 %forward.3 = (f32[72,128]{1,0:T(8,128)S(1)}, f32[72,128]{1,0:T(8,128)S(1)}, f32[72,128]{1,0:T(8,128)S(1)}, f32[72,128]{1,0:T(8,128)S(1)}, f32[512,256]{1,0:T(8,128)S(1)}, /*index=5*/f32[8,256]{1,0:T(8,128)S(1)}) custom-call(f32[520,128]{1,0:T(8,128)S(1)} %get-tuple-element.32.refs_0_.refs_4_, f32[520,128]{1,0:T(8,128)S(1)} %collective-permute-done.refs_1_.refs_5_, ...), custom_call_target="tpu_custom_call" | custom-call | flops 201326592 | bytes 1048576 | tf_op jit(solution)/shard_map/forward/pallas_call | solution.py:85
  12.7 2.9 %collective-permute-start.5 = (f32[72,128]{1,0:T(8,128)S(1)}, f32[72,128]{1,0:T(8,128)S(1)}, u32[]{:S(2)}, u32[]{:S(2)}) collective-permute-start(f32[72,128]{1,0:T(8,128)S(1)} %get-tuple-element.44), channel_id=1, source_target_pairs={{0,16},{4,20},{8,24},{12,28},{16,0},{20,4},{24,8},{28,12},{1,17},{... | collective-permute-start | bytes 110600 | tf_op jit(solution)/shard_map/ppermute | solution.py:39
  15.5 1.3 %collective-permute-start.6 = (f32[72,128]{1,0:T(8,128)S(1)}, f32[72,128]{1,0:T(8,128)S(1)}, u32[]{:S(2)}, u32[]{:S(2)}) collective-permute-start(f32[72,128]{1,0:T(8,128)S(1)} %get-tuple-element.45), channel_id=1, source_target_pairs={{0,24},{4,28},{8,16},{12,20},{16,8},{20,12},{24,0},{28,4},{1,25},{... | collective-permute-start | bytes 110600 | tf_op jit(solution)/shard_map/ppermute | solution.py:39
  16.9 0.7 collective-permute-done.5.refs_6_
  17.6 3.7 %collective-permute-done.6.refs_7_ = f32[72,128]{1,0:T(8,128)S(1)} collective-permute-done((f32[72,128]{1,0:T(8,128)S(1)}, f32[72,128]{1,0:T(8,128)S(1)}, u32[]{:S(2)}, u32[]{:S(2)}) %collective-permute-start.6) | collective-permute-done | bytes 36896 | tf_op jit(solution)/shard_map/ppermute | solution.py:39
  21.3 0.3 merge.2.refs_8_
  21.6 1.0 %collective-permute-start.10 = (f32[136,128]{1,0:T(8,128)S(1)}, f32[136,128]{1,0:T(8,128)S(1)}, u32[]{:S(2)}, u32[]{:S(2)}) collective-permute-start(f32[136,128]{1,0:T(8,128)S(1)} %merge.2.refs_8_), channel_id=1, source_target_pairs={{0,16},{4,20},{8,24},{12,28},{16,0},{20,4},{24,8},{28,12},{1,17},{... | collective-permute-start | bytes 208904 | tf_op jit(solution)/shard_map/ppermute | solution.py:39
  22.6 1.3 %collective-permute-start.9 = (f32[136,128]{1,0:T(8,128)S(1)}, f32[136,128]{1,0:T(8,128)S(1)}, u32[]{:S(2)}, u32[]{:S(2)}) collective-permute-start(f32[136,128]{1,0:T(8,128)S(1)} %merge.2.refs_8_), channel_id=1, source_target_pairs={{0,24},{4,28},{8,16},{12,20},{16,8},{20,12},{24,0},{28,4},{1,25},{... | collective-permute-start | bytes 208904 | tf_op jit(solution)/shard_map/ppermute | solution.py:39
  23.9 1.2 %collective-permute-start.8 = (f32[136,128]{1,0:T(8,128)S(1)}, f32[136,128]{1,0:T(8,128)S(1)}, u32[]{:S(2)}, u32[]{:S(2)}) collective-permute-start(f32[136,128]{1,0:T(8,128)S(1)} %merge.2.refs_8_), channel_id=1, source_target_pairs={{0,8},{4,12},{8,0},{12,4},{16,24},{20,28},{24,16},{28,20},{1,9},{5... | collective-permute-start | bytes 208904 | tf_op jit(solution)/shard_map/ppermute | solution.py:39
  25.1 2.1 %collective-permute-done.10.refs_11_ = f32[136,128]{1,0:T(8,128)S(1)} collective-permute-done((f32[136,128]{1,0:T(8,128)S(1)}, f32[136,128]{1,0:T(8,128)S(1)}, u32[]{:S(2)}, u32[]{:S(2)}) %collective-permute-start.10) | collective-permute-done | bytes 69664 | tf_op jit(solution)/shard_map/ppermute | solution.py:39
  27.3 1.5 %collective-permute-done.9.refs_10_ = f32[136,128]{1,0:T(8,128)S(1)} collective-permute-done((f32[136,128]{1,0:T(8,128)S(1)}, f32[136,128]{1,0:T(8,128)S(1)}, u32[]{:S(2)}, u32[]{:S(2)}) %collective-permute-start.9) | collective-permute-done | bytes 69664 | tf_op jit(solution)/shard_map/ppermute | solution.py:39
  28.8 0.2 collective-permute-done.8.refs_9_
  29.0 1.4 %backward.2 = (f32[520,128]{1,0:T(8,128)S(1)}, f32[520,128]{1,0:T(8,128)S(1)}, f32[32,1,128]{2,1,0:T(1,128)S(1)}) custom-call(f32[512,256]{1,0:T(8,128)S(1)} %get-tuple-element.36.refs_0_, f32[512,256]{1,0:T(8,128)S(1)} %get-tuple-element.38.refs_1_, f32[8,256]{1,0:T(8,128)S(1)} %get-tuple-element.37.refs_3_.refs_2_, ...), custom_call_target="tpu_custom_call" | custom-call | flops 603979776 | bytes 1048576 | tf_op jit(solution)/shard_map/backward/pallas_call | solution.py:85
  30.3 10.9 %all_to_all.10.refs_6_ = f32[32,1,128]{2,1,0:T(1,128)S(1)} all-to-all(f32[32,1,128]{2,1,0:T(1,128)S(1)} %get-tuple-element.50), channel_id=1, replica_groups=mesh['page'=8,'query'=2,'head'=2] {'page','query','head'}, dimensions={0} | all-to-all | bytes 32768 | tf_op jit(solution)/shard_map/all_to_all | solution.py:647
  41.3 1.1 %update_forward.1 = (f32[1368,128]{1,0:T(8,128)S(1)}, f32[136,128]{1,0:T(8,128)S(1)}, f32[136,128]{1,0:T(8,128)S(1)}, f32[136,128]{1,0:T(8,128)S(1)}, f32[136,12...) custom-call(f32[520,128]{1,0:T(8,128)S(1)} %get-tuple-element.32.refs_0_.refs_4_, ...), custom_call_target="tpu_custom_call" | custom-call | flops 402653184 | bytes 1048576 | tf_op jit(solution)/shard_map/update_forward/pallas_call | solution.py:85
  42.4 0.6 collective-permute-start.17
  43.0 0.6 collective-permute-start.11
  43.6 2.3 %collective-permute-start.12 = (f32[136,128]{1,0:T(8,128)S(1)}, f32[136,128]{1,0:T(8,128)S(1)}, u32[]{:S(2)}, u32[]{:S(2)}) collective-permute-start(f32[136,128]{1,0:T(8,128)S(1)} %get-tuple-element.56), channel_id=1, source_target_pairs={{0,24},{4,28},{8,16},{12,20},{16,8},{20,12},{24,0},{28,4},{1,25},{... | collective-permute-start | bytes 208904 | tf_op jit(solution)/shard_map/ppermute | solution.py:39
  45.9 0.6 collective-permute-start.13
  46.5 4.5 %collective-permute-done.11.refs_3_ = f32[136,128]{1,0:T(8,128)S(1)} collective-permute-done((f32[136,128]{1,0:T(8,128)S(1)}, f32[136,128]{1,0:T(8,128)S(1)}, u32[]{:S(2)}, u32[]{:S(2)}) %collective-permute-start.11) | collective-permute-done | bytes 69664 | tf_op jit(solution)/shard_map/ppermute | solution.py:39
  51.0 0.3 collective-permute-done.13.refs_5_
  51.3 0.1 merge.3.refs_0_
  51.4 0.6 collective-permute-start.16
  52.0 3.1 %collective-permute-start.15 = (f32[136,128]{1,0:T(8,128)S(1)}, f32[136,128]{1,0:T(8,128)S(1)}, u32[]{:S(2)}, u32[]{:S(2)}) collective-permute-start(f32[136,128]{1,0:T(8,128)S(1)} %merge.3.refs_0_), channel_id=1, source_target_pairs={{0,24},{4,28},{8,16},{12,20},{16,8},{20,12},{24,0},{28,4},{1,25},{... | collective-permute-start | bytes 208904 | tf_op jit(solution)/shard_map/ppermute | solution.py:39
  55.1 3.4 %collective-permute-done.16.refs_3_ = f32[136,128]{1,0:T(8,128)S(1)} collective-permute-done((f32[136,128]{1,0:T(8,128)S(1)}, f32[136,128]{1,0:T(8,128)S(1)}, u32[]{:S(2)}, u32[]{:S(2)}) %collective-permute-start.16) | collective-permute-done | bytes 69664 | tf_op jit(solution)/shard_map/ppermute | solution.py:39
  58.5 0.6 collective-permute-done.15.refs_2_
  59.1 0.7 collective-permute-done.14.refs_1_
  59.8 0.1 join.1.refs_5_
  59.9 1.4 %collective-permute-start.18 = (f32[136,512]{1,0:T(8,128)S(1)}, f32[136,512]{1,0:T(8,128)S(1)}, u32[]{:S(2)}, u32[]{:S(2)}) collective-permute-start(f32[136,512]{1,0:T(8,128)S(1)} %join.1.refs_5_), channel_id=1, source_target_pairs={{0,2},{2,0},{1,3},{3,1},{4,6},{6,4},{5,7},{7,5},{8,10},{10,8},{9,1... | collective-permute-start | bytes 835592 | tf_op jit(solution)/shard_map/ppermute | solution.py:39
  61.3 1.3 %backward.3 = (f32[520,128]{1,0:T(8,128)S(1)}, f32[520,128]{1,0:T(8,128)S(1)}, f32[32,1,128]{2,1,0:T(1,128)S(1)}) custom-call(f32[512,512]{1,0:T(8,128)S(1)} %get-tuple-element.51.refs_0_, f32[8,512]{1,0:T(8,128)S(1)} %get-tuple-element.52.refs_1_, f32[1368,128]{1,0:T(8,128)S(1)} %get-tuple-element.53.refs_2_.refs_1_, ...), custom_call_target="tpu_custom_call" | custom-call | flops 603979776 | bytes 1048576 | tf_op jit(solution)/shard_map/backward/pallas_call | solution.py:85
  62.6 9.1 %all_to_all.11.refs_0_ = f32[32,1,128]{2,1,0:T(1,128)S(1)} all-to-all(f32[32,1,128]{2,1,0:T(1,128)S(1)} %get-tuple-element.58), channel_id=1, replica_groups=mesh['page'=8,'query'=2,'head'=2] {'page','query','head'}, dimensions={0} | all-to-all | bytes 32768 | tf_op jit(solution)/shard_map/all_to_all | solution.py:647
  71.6 0.2 own_update.1.refs_4_
  71.8 0.1 collective-permute-start.19
  71.9 0.6 copy-done.4
  72.6 1.0 %other_update.2.refs_4_ = f32[520,128]{1,0:T(8,128)S(1)} custom-call(f32[32,1,128]{2,1,0:T(1,128)S(1)} %all_to_all.11.refs_0_, f32[1368,128]{1,0:T(8,128)S(1)} %collective-permute-done.17.refs_1_, f32[136,512]{1,0:T(8,128)S(1)} %collective-permute-done.18.refs_2_, f32[328,128]{1,0:T(8,128)S(1)} %copy-done.4, f32[520,128]{1,0:T(8,128)S(1)} %own_update.1.refs_4_), custom_call_target="tpu_custom_call" | custom-call | flops 301989888 | bytes 1048576 | tf_op jit(solution)/shard_map/other_update/pallas_call | solution.py:85
  73.6 0.1 collective-permute-start.20
  73.7 1.0 %other_update.3.refs_3_ = f32[520,128]{1,0:T(8,128)S(1)} custom-call(f32[32,1,128]{2,1,0:T(1,128)S(1)} %all_to_all.11.refs_0_, f32[1368,128]{1,0:T(8,128)S(1)} %collective-permute-done.17.refs_1_, f32[136,512]{1,0:T(8,128)S(1)} %collective-permute-done.18.refs_2_, f32[328,128]{1,0:T(8,128)S(1)} %copy-done.4, f32[520,128]{1,0:T(8,128)S(1)} %other_update.2.refs_4_), custom_call_target="tpu_custom_call" | custom-call | flops 301989888 | bytes 1048576 | tf_op jit(solution)/shard_map/other_update/pallas_call | solution.py:85
  74.7 0.5 collective-permute-done.20.refs_5_
  75.2 1.1 %unpack.1 = (f32[4,256,128]{2,1,0:T(8,128)}, f32[4,256,128]{2,1,0:T(8,128)}, f32[4,256]{1,0:T(4,128)}) custom-call(f32[32,1,128]{2,1,0:T(1,128)S(1)} %all_to_all.11.refs_0_, f32[1368,128]{1,0:T(8,128)S(1)} %get-tuple-element.53.refs_2_.refs_1_, f32[520,128]{1,0:T(8,128)S(1)} %get-tuple-element.59.refs_2_, f32[520,128]{1,0:T(8,128)S(1)} %other_update.3.refs_3_, ...), custom_call_target="tpu_custom_call" | custom-call | flops 1048576 | bytes 1048576 | tf_op jit(solution)/shard_map/unpack/pallas_call | solution.py:85
  (26 shorter events, 0.1 us)
Async XLA Ops:
  0.6 5.2 %copy-start.3 = (f32[4,256,128]{2,1,0:T(8,128)S(1)}, f32[4,256,128]{2,1,0:T(8,128)}, u32[]{:S(2)}) copy-start(f32[4,256,128]{2,1,0:T(8,128)} %refs_4_.3) | copy-start | bytes 1572868
  0.6 5.2 %copy-start.2 = (f32[4,256,128]{2,1,0:T(8,128)S(1)}, f32[4,256,128]{2,1,0:T(8,128)}, u32[]{:S(2)}) copy-start(f32[4,256,128]{2,1,0:T(8,128)} %refs_2_.3) | copy-start | bytes 1572868
  0.7 5.2 %copy-start.1 = (f32[4,256,128]{2,1,0:T(8,128)S(1)}, f32[4,256,128]{2,1,0:T(8,128)}, u32[]{:S(2)}) copy-start(f32[4,256,128]{2,1,0:T(8,128)} %refs_1_.3) | copy-start | bytes 1572868
  0.7 5.2 %copy-start = (f32[4,256,128]{2,1,0:T(8,128)S(1)}, f32[4,256,128]{2,1,0:T(8,128)}, u32[]{:S(2)}) copy-start(f32[4,256,128]{2,1,0:T(8,128)} %refs_0_.3) | copy-start | bytes 1572868
  0.7 5.2 %copy-start.5 = (f32[4,256]{1,0:T(4,128)S(1)}, f32[4,256]{1,0:T(4,128)}, u32[]{:S(2)}) copy-start(f32[4,256]{1,0:T(4,128)} %refs_3_.3) | copy-start | bytes 12292
  0.7 5.2 %copy-start.6 = (s32[4,256]{1,0:T(4,128)S(1)}, s32[4,256]{1,0:T(4,128)}, u32[]{:S(2)}) copy-start(s32[4,256]{1,0:T(4,128)} %refs_5_.3) | copy-start | bytes 12292
  2.7 3.2 %copy-start.7 = (s32[8]{0:T(128)S(1)}, s32[8]{0:T(128)}, u32[]{:S(2)}) copy-start(s32[8]{0:T(128)} %refs_6_.3) | copy-start | bytes 100
  2.7 3.8 %collective-permute-start = (f32[520,128]{1,0:T(8,128)}, f32[520,128]{1,0:T(8,128)S(1)}, u32[]{:S(2)}, u32[]{:S(2)}) collective-permute-start(f32[520,128]{1,0:T(8,128)} %get-tuple-element.33), channel_id=1, source_target_pairs={{0,4},{4,0},{8,12},{12,8},{16,20},{20,16},{24,28},{28,24},{1,5},{5... | collective-permute-start | bytes 798728 | tf_op jit(solution)/shard_map/ppermute | solution.py:39
  3.3 8.5 %collective-permute-start.1 = (f32[328,128]{1,0:T(8,128)}, f32[328,128]{1,0:T(8,128)S(1)}, u32[]{:S(2)}, u32[]{:S(2)}) collective-permute-start(f32[328,128]{1,0:T(8,128)} %get-tuple-element.35.refs_3_), channel_id=1, source_target_pairs={{0,2},{2,0},{1,3},{3,1},{4,6},{6,4},{5,7},{7,5},{8,10},{10,8},{9,1... | collective-permute-start | bytes 503816 | tf_op jit(solution)/shard_map/ppermute | solution.py:39
  7.5 9.4 %collective-permute-start.2 = (f32[72,128]{1,0:T(8,128)S(1)}, f32[72,128]{1,0:T(8,128)S(1)}, u32[]{:S(2)}, u32[]{:S(2)}) collective-permute-start(f32[72,128]{1,0:T(8,128)S(1)} %get-tuple-element.40), channel_id=1, source_target_pairs={{0,16},{4,20},{8,24},{12,28},{16,0},{20,4},{24,8},{28,12},{1,17},{... | collective-permute-start | bytes 110600 | tf_op jit(solution)/shard_map/ppermute | solution.py:39
  10.2 6.7 %collective-permute-start.3 = (f32[72,128]{1,0:T(8,128)S(1)}, f32[72,128]{1,0:T(8,128)S(1)}, u32[]{:S(2)}, u32[]{:S(2)}) collective-permute-start(f32[72,128]{1,0:T(8,128)S(1)} %get-tuple-element.41), channel_id=1, source_target_pairs={{0,24},{4,28},{8,16},{12,20},{16,8},{20,12},{24,0},{28,4},{1,25},{... | collective-permute-start | bytes 110600 | tf_op jit(solution)/shard_map/ppermute | solution.py:39
  11.5 5.4 %collective-permute-start.4 = (f32[72,128]{1,0:T(8,128)S(1)}, f32[72,128]{1,0:T(8,128)S(1)}, u32[]{:S(2)}, u32[]{:S(2)}) collective-permute-start(f32[72,128]{1,0:T(8,128)S(1)} %get-tuple-element.42), channel_id=1, source_target_pairs={{0,8},{4,12},{8,0},{12,4},{16,24},{20,28},{24,16},{28,20},{1,9},{5... | collective-permute-start | bytes 110600 | tf_op jit(solution)/shard_map/ppermute | solution.py:39
  12.7 4.9 %collective-permute-start.5 = (f32[72,128]{1,0:T(8,128)S(1)}, f32[72,128]{1,0:T(8,128)S(1)}, u32[]{:S(2)}, u32[]{:S(2)}) collective-permute-start(f32[72,128]{1,0:T(8,128)S(1)} %get-tuple-element.44), channel_id=1, source_target_pairs={{0,16},{4,20},{8,24},{12,28},{16,0},{20,4},{24,8},{28,12},{1,17},{... | collective-permute-start | bytes 110600 | tf_op jit(solution)/shard_map/ppermute | solution.py:39
  15.5 5.8 %collective-permute-start.6 = (f32[72,128]{1,0:T(8,128)S(1)}, f32[72,128]{1,0:T(8,128)S(1)}, u32[]{:S(2)}, u32[]{:S(2)}) collective-permute-start(f32[72,128]{1,0:T(8,128)S(1)} %get-tuple-element.45), channel_id=1, source_target_pairs={{0,24},{4,28},{8,16},{12,20},{16,8},{20,12},{24,0},{28,4},{1,25},{... | collective-permute-start | bytes 110600 | tf_op jit(solution)/shard_map/ppermute | solution.py:39
  16.9 4.4 %collective-permute-start.7 = (f32[72,128]{1,0:T(8,128)S(1)}, f32[72,128]{1,0:T(8,128)S(1)}, u32[]{:S(2)}, u32[]{:S(2)}) collective-permute-start(f32[72,128]{1,0:T(8,128)S(1)} %get-tuple-element.46), channel_id=1, source_target_pairs={{0,8},{4,12},{8,0},{12,4},{16,24},{20,28},{24,16},{28,20},{1,9},{5... | collective-permute-start | bytes 110600 | tf_op jit(solution)/shard_map/ppermute | solution.py:39
  21.6 5.7 %collective-permute-start.10 = (f32[136,128]{1,0:T(8,128)S(1)}, f32[136,128]{1,0:T(8,128)S(1)}, u32[]{:S(2)}, u32[]{:S(2)}) collective-permute-start(f32[136,128]{1,0:T(8,128)S(1)} %merge.2.refs_8_), channel_id=1, source_target_pairs={{0,16},{4,20},{8,24},{12,28},{16,0},{20,4},{24,8},{28,12},{1,17},{... | collective-permute-start | bytes 208904 | tf_op jit(solution)/shard_map/ppermute | solution.py:39
  22.6 6.2 %collective-permute-start.9 = (f32[136,128]{1,0:T(8,128)S(1)}, f32[136,128]{1,0:T(8,128)S(1)}, u32[]{:S(2)}, u32[]{:S(2)}) collective-permute-start(f32[136,128]{1,0:T(8,128)S(1)} %merge.2.refs_8_), channel_id=1, source_target_pairs={{0,24},{4,28},{8,16},{12,20},{16,8},{20,12},{24,0},{28,4},{1,25},{... | collective-permute-start | bytes 208904 | tf_op jit(solution)/shard_map/ppermute | solution.py:39
  23.9 5.1 %collective-permute-start.8 = (f32[136,128]{1,0:T(8,128)S(1)}, f32[136,128]{1,0:T(8,128)S(1)}, u32[]{:S(2)}, u32[]{:S(2)}) collective-permute-start(f32[136,128]{1,0:T(8,128)S(1)} %merge.2.refs_8_), channel_id=1, source_target_pairs={{0,8},{4,12},{8,0},{12,4},{16,24},{20,28},{24,16},{28,20},{1,9},{5... | collective-permute-start | bytes 208904 | tf_op jit(solution)/shard_map/ppermute | solution.py:39
  42.4 29.5 %collective-permute-start.17 = (f32[1368,128]{1,0:T(8,128)S(1)}, f32[1368,128]{1,0:T(8,128)S(1)}, u32[]{:S(2)}, u32[]{:S(2)}) collective-permute-start(f32[1368,128]{1,0:T(8,128)S(1)} %get-tuple-element.53.refs_2_.refs_1_), channel_id=1, source_target_pairs={{0,2},{2,0},{1,3},{3,1},{4,6},{6,4},{5,7},{7,5},{8,10},{10,8},{9,1... | collective-permute-start | bytes 2101256 | tf_op jit(solution)/shard_map/ppermute | solution.py:39
  43.0 8.0 %collective-permute-start.11 = (f32[136,128]{1,0:T(8,128)S(1)}, f32[136,128]{1,0:T(8,128)S(1)}, u32[]{:S(2)}, u32[]{:S(2)}) collective-permute-start(f32[136,128]{1,0:T(8,128)S(1)} %get-tuple-element.55), channel_id=1, source_target_pairs={{0,16},{4,20},{8,24},{12,28},{16,0},{20,4},{24,8},{28,12},{1,17},{... | collective-permute-start | bytes 208904 | tf_op jit(solution)/shard_map/ppermute | solution.py:39
  43.6 7.4 %collective-permute-start.12 = (f32[136,128]{1,0:T(8,128)S(1)}, f32[136,128]{1,0:T(8,128)S(1)}, u32[]{:S(2)}, u32[]{:S(2)}) collective-permute-start(f32[136,128]{1,0:T(8,128)S(1)} %get-tuple-element.56), channel_id=1, source_target_pairs={{0,24},{4,28},{8,16},{12,20},{16,8},{20,12},{24,0},{28,4},{1,25},{... | collective-permute-start | bytes 208904 | tf_op jit(solution)/shard_map/ppermute | solution.py:39
  45.9 5.4 %collective-permute-start.13 = (f32[136,128]{1,0:T(8,128)S(1)}, f32[136,128]{1,0:T(8,128)S(1)}, u32[]{:S(2)}, u32[]{:S(2)}) collective-permute-start(f32[136,128]{1,0:T(8,128)S(1)} %get-tuple-element.57), channel_id=1, source_target_pairs={{0,8},{4,12},{8,0},{12,4},{16,24},{20,28},{24,16},{28,20},{1,9},{5... | collective-permute-start | bytes 208904 | tf_op jit(solution)/shard_map/ppermute | solution.py:39
  51.4 7.1 %collective-permute-start.16 = (f32[136,128]{1,0:T(8,128)S(1)}, f32[136,128]{1,0:T(8,128)S(1)}, u32[]{:S(2)}, u32[]{:S(2)}) collective-permute-start(f32[136,128]{1,0:T(8,128)S(1)} %merge.3.refs_0_), channel_id=1, source_target_pairs={{0,16},{4,20},{8,24},{12,28},{16,0},{20,4},{24,8},{28,12},{1,17},{... | collective-permute-start | bytes 208904 | tf_op jit(solution)/shard_map/ppermute | solution.py:39
  52.0 7.2 %collective-permute-start.15 = (f32[136,128]{1,0:T(8,128)S(1)}, f32[136,128]{1,0:T(8,128)S(1)}, u32[]{:S(2)}, u32[]{:S(2)}) collective-permute-start(f32[136,128]{1,0:T(8,128)S(1)} %merge.3.refs_0_), channel_id=1, source_target_pairs={{0,24},{4,28},{8,16},{12,20},{16,8},{20,12},{24,0},{28,4},{1,25},{... | collective-permute-start | bytes 208904 | tf_op jit(solution)/shard_map/ppermute | solution.py:39
  55.1 4.7 %collective-permute-start.14 = (f32[136,128]{1,0:T(8,128)S(1)}, f32[136,128]{1,0:T(8,128)S(1)}, u32[]{:S(2)}, u32[]{:S(2)}) collective-permute-start(f32[136,128]{1,0:T(8,128)S(1)} %merge.3.refs_0_), channel_id=1, source_target_pairs={{0,8},{4,12},{8,0},{12,4},{16,24},{20,28},{24,16},{28,20},{1,9},{5... | collective-permute-start | bytes 208904 | tf_op jit(solution)/shard_map/ppermute | solution.py:39
  59.9 12.0 %collective-permute-start.18 = (f32[136,512]{1,0:T(8,128)S(1)}, f32[136,512]{1,0:T(8,128)S(1)}, u32[]{:S(2)}, u32[]{:S(2)}) collective-permute-start(f32[136,512]{1,0:T(8,128)S(1)} %join.1.refs_5_), channel_id=1, source_target_pairs={{0,2},{2,0},{1,3},{3,1},{4,6},{6,4},{5,7},{7,5},{8,10},{10,8},{9,1... | collective-permute-start | bytes 835592 | tf_op jit(solution)/shard_map/ppermute | solution.py:39
  71.6 0.9 %copy-start.4 = (f32[328,128]{1,0:T(8,128)S(1)}, f32[328,128]{1,0:T(8,128)}, u32[]{:S(2)}) copy-start(f32[328,128]{1,0:T(8,128)} %get-tuple-element.35.refs_3_) | copy-start | bytes 503812
  71.8 2.8 %collective-permute-start.19 = (f32[520,128]{1,0:T(8,128)S(1)}, f32[520,128]{1,0:T(8,128)S(1)}, u32[]{:S(2)}, u32[]{:S(2)}) collective-permute-start(f32[520,128]{1,0:T(8,128)S(1)} %own_update.1.refs_4_), channel_id=1, source_target_pairs={{0,4},{4,0},{8,12},{12,8},{16,20},{20,16},{24,28},{28,24},{1,5},{5... | collective-permute-start | bytes 798728 | tf_op jit(solution)/shard_map/ppermute | solution.py:39
  73.6 1.6 %collective-permute-start.20 = (f32[520,128]{1,0:T(8,128)S(1)}, f32[520,128]{1,0:T(8,128)S(1)}, u32[]{:S(2)}, u32[]{:S(2)}) collective-permute-start(f32[520,128]{1,0:T(8,128)S(1)} %other_update.2.refs_4_), channel_id=1, source_target_pairs={{0,4},{4,0},{8,12},{12,8},{16,20},{20,16},{24,28},{28,24},{1,5},{5... | collective-permute-start | bytes 798728 | tf_op jit(solution)/shard_map/ppermute | solution.py:39

commit v24 on v21

--- a/solution.py
+++ b/solution.py
@@ -75,8 +75,10 @@
     return both[:count, :] + cross
 
 
-def call(body, out_shapes, name, cost, operands, scratch=(), after=(), space=pltpu.VMEM, vmem=32):
-    spaces = [space] * len(operands) + [pl.ANY] * len(after)
+def call(body, out_shapes, name, cost, operands, scratch=(), after=(), space=pltpu.VMEM,
+         spaces=None, out_spaces=None, aliases=None, vmem=32):
+    spaces = (spaces or [space] * len(operands)) + [pl.ANY] * len(after)
+    out_spaces = out_spaces or [pltpu.VMEM] * len(out_shapes)
     count = len(operands)
 
     def without_after(*refs):
@@ -86,7 +88,8 @@
         without_after,
         out_shape=[jax.ShapeDtypeStruct(shape, jnp.float32) for shape in out_shapes],
         in_specs=[pl.BlockSpec(memory_space=space) for space in spaces],
-        out_specs=[pl.BlockSpec(memory_space=pltpu.VMEM) for _ in out_shapes],
+        out_specs=[pl.BlockSpec(memory_space=out_space) for out_space in out_spaces],
+        input_output_aliases=aliases or {},
         scratch_shapes=scratch,
         compiler_params=pltpu.CompilerParams(vmem_limit_bytes=vmem * 2**20),
         cost_estimate=pl.CostEstimate(flops=cost, bytes_accessed=2**20, transcendentals=0),
@@ -660,26 +663,57 @@
             tiles + [grad] + operands,
             after=pages,
         )
-    pages = [pages[1], exchange(pages[0], page=1)]
-
-    def last_body(*refs):
-        page_refs, (keys_out, values_out, bias_out) = refs[:CORES], refs[CORES:]
+    mate_page, own_page = exchange(pages[0], page=1), pages[1]
+
+    def write_page(page_ref, flip, keys_out, values_out, sems):
         _, core, me = places()
-        for turn, flip in itertools.product(range(query_devices), range(CORES)):
-            keys, values, bias = read_pack(part_of(page_refs[flip], turn))
+        copies = []
+        for turn in range(query_devices):
+            keys, values = (
+                page_ref.at[pl.ds(turn * packed_rows + at * slot_rows, slot_rows)]
+                for at in range(2)
+            )
             head = CORES * (me ^ turn) + (core ^ flip)
-            keys_out[head] = keys
-            values_out[head] = values
-            bias_row = jnp.concatenate([bias[row : row + 1] for row in range(bias_rows)], axis=1)
-            bias_out[pl.ds(head, 1), :] = bias_row
-
+            copies += [(keys, keys_out.at[head]), (values, values_out.at[head])]
+        return start_all(copies, sems)
+
+    def own_unpack_body(page_ref, keys_out, values_out, sems):
+        for copy in write_page(page_ref, 0, keys_out, values_out, sems):
+            copy.wait()
+
+    def unpack_body(own_ref, mate_ref, _keys, _values, keys_out, values_out, bias_out, sems):
+        copies = write_page(mate_ref, 1, keys_out, values_out, sems)
+        _, core, me = places()
+        for flip, page_ref in enumerate((own_ref, mate_ref)):
+            for turn in range(query_devices):
+                first = turn * packed_rows + 2 * slot_rows
+                head = CORES * (me ^ turn) + (core ^ flip)
+                bias_out[pl.ds(head, 1), :] = tail_as_row(page_ref, first, bias_rows)
+        for copy in copies:
+            copy.wait()
+
+    result_shapes = [compact_keys.shape, compact_values.shape]
+    unpack_sems = [pltpu.SemaphoreType.DMA((2 * query_devices,))]
+    results = call(
+        own_unpack_body,
+        result_shapes,
+        "unpack_own",
+        2**10,
+        [own_page],
+        unpack_sems,
+        out_spaces=[pl.ANY] * 2,
+    )
     return tuple(
         call(
-            last_body,
-            [compact_keys.shape, compact_values.shape, slot_bias.shape],
+            unpack_body,
+            result_shapes + [slot_bias.shape],
             "unpack",
             2**20,
-            pages,
+            [own_page, mate_page] + list(results),
+            unpack_sems,
+            spaces=[pltpu.VMEM] * 2 + [pl.ANY] * 2,
+            out_spaces=[pl.ANY] * 2 + [pltpu.VMEM],
+            aliases={2: 0, 3: 1},
         )
     )
 

time: 75.9 us -> 76.3 us (level)
  Pallas kernels: 11.8 us -> 13 us
  waiting for transfers between devices: 18.7 us -> 17.8 us
    pallas_call x13 -> x14, Pallas kernels: 11.8 us -> 13 us  [call(): pl.pallas_call(without_after, out_shape=[jax.ShapeDtypeStruct(shape, jnp....]
    ppermute x20, waiting for transfers between devices: 18.7 us -> 17.8 us  [exchange(): return lax.ppermute(value, axes, pairs)]
  transfers between devices with their start and end apart: 20 -> 20, of which waited for: 11 -> 11; matrix products, arithmetic and copies ran while one was open for 0% -> 0% of each run, Pallas kernels for 7% -> 8%
where the time goes in v24:
time: 76.3 us; the launch traced here: 76.1 us
  starting transfers between devices  24.4 us (32%)
  blocking collectives  20 us (26%)
  waiting for transfers between devices  17.8 us (23%)
  Pallas kernels  13 us (17%)
  between operations  0.83 us (1%)
    ppermute x20, starting transfers between devices, exchange(): return lax.ppermute(value, axes, pairs)  24.4 us
    all_to_all x2, blocking collectives, direct_per_device(): lax.all_to_all(squares, ('page', 'query', 'head'), split_axis=0, concat_a...  20 us
    ppermute x20, waiting for transfers between devices, exchange(): return lax.ppermute(value, axes, pairs)  17.8 us
    pallas_call x14, Pallas kernels, call(): pl.pallas_call(without_after, out_shape=[jax.ShapeDtypeStruct(shape, jnp....  13 us
  transfers between devices with their start and end apart: 20, of which 11 were waited for; matrix products, arithmetic and copies ran while one was open for 0% of the time, Pallas kernels for 8%

profile of v24, /device:TPU:0, one launch (start us, length us, event | category | flops | bytes accessed | tf_op | source)
XLA Modules:
  0.0 76.1 jit_solution(6928811305848442559)
XLA Ops:
  0.7 2.0 %pack.1 = (f32[520,128]{1,0:T(8,128)}, f32[328,128]{1,0:T(8,128)}) custom-call(f32[4,256,128]{2,1,0:T(8,128)} %refs_0_.3, f32[4,256,128]{2,1,0:T(8,128)} %refs_1_.3, f32[4,256,128]{2,1,0:T(8,128)} %refs_2_.3, f32[4,256]{1,0:T(4,128)} %refs_3_.3, f32[4,256,128]{2,1,0:T(8,128)} %refs_4_.3, s32[4,256]{1,0:T(4,128)} %refs_5_.3, s32[8]{0:T(128)} %refs_6_.3), custom_call_target="tpu_custom_call" | custom-call | flops 1048576 | bytes 1048576 | tf_op jit(solution)/shard_map/pack/pallas_call | solution.py:87
  2.7 0.0 copy-start.7
  2.7 0.5 collective-permute-start
  3.3 2.6 %collective-permute-start.1 = (f32[328,128]{1,0:T(8,128)}, f32[328,128]{1,0:T(8,128)S(1)}, u32[]{:S(2)}, u32[]{:S(2)}) collective-permute-start(f32[328,128]{1,0:T(8,128)} %get-tuple-element.37.refs_5_), channel_id=1, source_target_pairs={{0,2},{2,0},{1,3},{3,1},{4,6},{6,4},{5,7},{7,5},{8,10},{10,8},{9,1... | collective-permute-start | bytes 503816 | tf_op jit(solution)/shard_map/ppermute | solution.py:39
  5.9 0.7 own.1
  6.6 0.0 collective-permute-done.refs_1_.refs_5_
  6.6 0.9 %forward.2 = (f32[72,128]{1,0:T(8,128)S(1)}, f32[72,128]{1,0:T(8,128)S(1)}, f32[72,128]{1,0:T(8,128)S(1)}, f32[72,128]{1,0:T(8,128)S(1)}, f32[512,256]{1,0:T(8,128)S(1)}, /*index=5*/f32[8,256]{1,0:T(8,128)S(1)}) custom-call(f32[520,128]{1,0:T(8,128)S(1)} %get-tuple-element.34.refs_0_.refs_4_, f32[520,128]{1,0:T(8,128)S(1)} %collective-permute-done.refs_1_.refs_5_, ...), custom_call_target="tpu_custom_call" | custom-call | flops 201326592 | bytes 1048576 | tf_op jit(solution)/shard_map/forward/pallas_call | solution.py:87
  7.5 2.7 %collective-permute-start.2 = (f32[72,128]{1,0:T(8,128)S(1)}, f32[72,128]{1,0:T(8,128)S(1)}, u32[]{:S(2)}, u32[]{:S(2)}) collective-permute-start(f32[72,128]{1,0:T(8,128)S(1)} %get-tuple-element.42), channel_id=1, source_target_pairs={{0,16},{4,20},{8,24},{12,28},{16,0},{20,4},{24,8},{28,12},{1,17},{... | collective-permute-start | bytes 110600 | tf_op jit(solution)/shard_map/ppermute | solution.py:39
  10.2 1.3 %collective-permute-start.3 = (f32[72,128]{1,0:T(8,128)S(1)}, f32[72,128]{1,0:T(8,128)S(1)}, u32[]{:S(2)}, u32[]{:S(2)}) collective-permute-start(f32[72,128]{1,0:T(8,128)S(1)} %get-tuple-element.43), channel_id=1, source_target_pairs={{0,24},{4,28},{8,16},{12,20},{16,8},{20,12},{24,0},{28,4},{1,25},{... | collective-permute-start | bytes 110600 | tf_op jit(solution)/shard_map/ppermute | solution.py:39
  11.5 0.2 collective-permute-start.4
  11.7 0.9 %forward.3 = (f32[72,128]{1,0:T(8,128)S(1)}, f32[72,128]{1,0:T(8,128)S(1)}, f32[72,128]{1,0:T(8,128)S(1)}, f32[72,128]{1,0:T(8,128)S(1)}, f32[512,256]{1,0:T(8,128)S(1)}, /*index=5*/f32[8,256]{1,0:T(8,128)S(1)}) custom-call(f32[520,128]{1,0:T(8,128)S(1)} %get-tuple-element.34.refs_0_.refs_4_, f32[520,128]{1,0:T(8,128)S(1)} %collective-permute-done.refs_1_.refs_5_, ...), custom_call_target="tpu_custom_call" | custom-call | flops 201326592 | bytes 1048576 | tf_op jit(solution)/shard_map/forward/pallas_call | solution.py:87
  12.7 2.9 %collective-permute-start.5 = (f32[72,128]{1,0:T(8,128)S(1)}, f32[72,128]{1,0:T(8,128)S(1)}, u32[]{:S(2)}, u32[]{:S(2)}) collective-permute-start(f32[72,128]{1,0:T(8,128)S(1)} %get-tuple-element.46), channel_id=1, source_target_pairs={{0,16},{4,20},{8,24},{12,28},{16,0},{20,4},{24,8},{28,12},{1,17},{... | collective-permute-start | bytes 110600 | tf_op jit(solution)/shard_map/ppermute | solution.py:39
  15.5 1.3 %collective-permute-start.6 = (f32[72,128]{1,0:T(8,128)S(1)}, f32[72,128]{1,0:T(8,128)S(1)}, u32[]{:S(2)}, u32[]{:S(2)}) collective-permute-start(f32[72,128]{1,0:T(8,128)S(1)} %get-tuple-element.47), channel_id=1, source_target_pairs={{0,24},{4,28},{8,16},{12,20},{16,8},{20,12},{24,0},{28,4},{1,25},{... | collective-permute-start | bytes 110600 | tf_op jit(solution)/shard_map/ppermute | solution.py:39
  16.9 0.0 collective-permute-done.2.refs_2_
  16.9 0.7 collective-permute-done.5.refs_6_
  17.6 3.7 %collective-permute-done.6.refs_7_ = f32[72,128]{1,0:T(8,128)S(1)} collective-permute-done((f32[72,128]{1,0:T(8,128)S(1)}, f32[72,128]{1,0:T(8,128)S(1)}, u32[]{:S(2)}, u32[]{:S(2)}) %collective-permute-start.6) | collective-permute-done | bytes 36896 | tf_op jit(solution)/shard_map/ppermute | solution.py:39
  21.3 0.3 merge.2.refs_8_
  21.6 1.0 %collective-permute-start.10 = (f32[136,128]{1,0:T(8,128)S(1)}, f32[136,128]{1,0:T(8,128)S(1)}, u32[]{:S(2)}, u32[]{:S(2)}) collective-permute-start(f32[136,128]{1,0:T(8,128)S(1)} %merge.2.refs_8_), channel_id=1, source_target_pairs={{0,16},{4,20},{8,24},{12,28},{16,0},{20,4},{24,8},{28,12},{1,17},{... | collective-permute-start | bytes 208904 | tf_op jit(solution)/shard_map/ppermute | solution.py:39
  22.6 1.3 %collective-permute-start.9 = (f32[136,128]{1,0:T(8,128)S(1)}, f32[136,128]{1,0:T(8,128)S(1)}, u32[]{:S(2)}, u32[]{:S(2)}) collective-permute-start(f32[136,128]{1,0:T(8,128)S(1)} %merge.2.refs_8_), channel_id=1, source_target_pairs={{0,24},{4,28},{8,16},{12,20},{16,8},{20,12},{24,0},{28,4},{1,25},{... | collective-permute-start | bytes 208904 | tf_op jit(solution)/shard_map/ppermute | solution.py:39
  23.9 1.2 %collective-permute-start.8 = (f32[136,128]{1,0:T(8,128)S(1)}, f32[136,128]{1,0:T(8,128)S(1)}, u32[]{:S(2)}, u32[]{:S(2)}) collective-permute-start(f32[136,128]{1,0:T(8,128)S(1)} %merge.2.refs_8_), channel_id=1, source_target_pairs={{0,8},{4,12},{8,0},{12,4},{16,24},{20,28},{24,16},{28,20},{1,9},{5... | collective-permute-start | bytes 208904 | tf_op jit(solution)/shard_map/ppermute | solution.py:39
  25.1 2.1 %collective-permute-done.10.refs_11_ = f32[136,128]{1,0:T(8,128)S(1)} collective-permute-done((f32[136,128]{1,0:T(8,128)S(1)}, f32[136,128]{1,0:T(8,128)S(1)}, u32[]{:S(2)}, u32[]{:S(2)}) %collective-permute-start.10) | collective-permute-done | bytes 69664 | tf_op jit(solution)/shard_map/ppermute | solution.py:39
  27.3 1.5 %collective-permute-done.9.refs_10_ = f32[136,128]{1,0:T(8,128)S(1)} collective-permute-done((f32[136,128]{1,0:T(8,128)S(1)}, f32[136,128]{1,0:T(8,128)S(1)}, u32[]{:S(2)}, u32[]{:S(2)}) %collective-permute-start.9) | collective-permute-done | bytes 69664 | tf_op jit(solution)/shard_map/ppermute | solution.py:39
  28.8 0.2 collective-permute-done.8.refs_9_
  29.0 1.4 %backward.2 = (f32[520,128]{1,0:T(8,128)S(1)}, f32[520,128]{1,0:T(8,128)S(1)}, f32[32,1,128]{2,1,0:T(1,128)S(1)}) custom-call(f32[512,256]{1,0:T(8,128)S(1)} %get-tuple-element.38.refs_0_, f32[512,256]{1,0:T(8,128)S(1)} %get-tuple-element.40.refs_1_, f32[8,256]{1,0:T(8,128)S(1)} %get-tuple-element.39.refs_3_.refs_2_, ...), custom_call_target="tpu_custom_call" | custom-call | flops 603979776 | bytes 1048576 | tf_op jit(solution)/shard_map/backward/pallas_call | solution.py:87
  30.4 10.9 %all_to_all.10.refs_6_ = f32[32,1,128]{2,1,0:T(1,128)S(1)} all-to-all(f32[32,1,128]{2,1,0:T(1,128)S(1)} %get-tuple-element.52), channel_id=1, replica_groups=mesh['page'=8,'query'=2,'head'=2] {'page','query','head'}, dimensions={0} | all-to-all | bytes 32768 | tf_op jit(solution)/shard_map/all_to_all | solution.py:645
  41.3 1.1 %update_forward.1 = (f32[1368,128]{1,0:T(8,128)S(1)}, f32[136,128]{1,0:T(8,128)S(1)}, f32[136,128]{1,0:T(8,128)S(1)}, f32[136,128]{1,0:T(8,128)S(1)}, f32[136,12...) custom-call(f32[520,128]{1,0:T(8,128)S(1)} %get-tuple-element.34.refs_0_.refs_4_, ...), custom_call_target="tpu_custom_call" | custom-call | flops 402653184 | bytes 1048576 | tf_op jit(solution)/shard_map/update_forward/pallas_call | solution.py:87
  42.4 0.6 collective-permute-start.17
  43.0 0.6 collective-permute-start.11
  43.6 2.3 %collective-permute-start.12 = (f32[136,128]{1,0:T(8,128)S(1)}, f32[136,128]{1,0:T(8,128)S(1)}, u32[]{:S(2)}, u32[]{:S(2)}) collective-permute-start(f32[136,128]{1,0:T(8,128)S(1)} %get-tuple-element.58), channel_id=1, source_target_pairs={{0,24},{4,28},{8,16},{12,20},{16,8},{20,12},{24,0},{28,4},{1,25},{... | collective-permute-start | bytes 208904 | tf_op jit(solution)/shard_map/ppermute | solution.py:39
  45.9 0.6 collective-permute-start.13
  46.5 4.5 %collective-permute-done.11.refs_3_ = f32[136,128]{1,0:T(8,128)S(1)} collective-permute-done((f32[136,128]{1,0:T(8,128)S(1)}, f32[136,128]{1,0:T(8,128)S(1)}, u32[]{:S(2)}, u32[]{:S(2)}) %collective-permute-start.11) | collective-permute-done | bytes 69664 | tf_op jit(solution)/shard_map/ppermute | solution.py:39
  51.0 0.3 collective-permute-done.13.refs_5_
  51.3 0.1 merge.3.refs_0_
  51.4 0.6 collective-permute-start.16
  52.0 3.1 %collective-permute-start.15 = (f32[136,128]{1,0:T(8,128)S(1)}, f32[136,128]{1,0:T(8,128)S(1)}, u32[]{:S(2)}, u32[]{:S(2)}) collective-permute-start(f32[136,128]{1,0:T(8,128)S(1)} %merge.3.refs_0_), channel_id=1, source_target_pairs={{0,24},{4,28},{8,16},{12,20},{16,8},{20,12},{24,0},{28,4},{1,25},{... | collective-permute-start | bytes 208904 | tf_op jit(solution)/shard_map/ppermute | solution.py:39
  55.1 3.4 %collective-permute-done.16.refs_3_ = f32[136,128]{1,0:T(8,128)S(1)} collective-permute-done((f32[136,128]{1,0:T(8,128)S(1)}, f32[136,128]{1,0:T(8,128)S(1)}, u32[]{:S(2)}, u32[]{:S(2)}) %collective-permute-start.16) | collective-permute-done | bytes 69664 | tf_op jit(solution)/shard_map/ppermute | solution.py:39
  58.5 0.7 collective-permute-done.15.refs_2_
  59.1 0.7 collective-permute-done.14.refs_1_
  59.8 0.1 join.1.refs_5_
  59.9 1.4 %collective-permute-start.18 = (f32[136,512]{1,0:T(8,128)S(1)}, f32[136,512]{1,0:T(8,128)S(1)}, u32[]{:S(2)}, u32[]{:S(2)}) collective-permute-start(f32[136,512]{1,0:T(8,128)S(1)} %join.1.refs_5_), channel_id=1, source_target_pairs={{0,2},{2,0},{1,3},{3,1},{4,6},{6,4},{5,7},{7,5},{8,10},{10,8},{9,1... | collective-permute-start | bytes 835592 | tf_op jit(solution)/shard_map/ppermute | solution.py:39
  61.3 1.3 %backward.3 = (f32[520,128]{1,0:T(8,128)S(1)}, f32[520,128]{1,0:T(8,128)S(1)}, f32[32,1,128]{2,1,0:T(1,128)S(1)}) custom-call(f32[512,512]{1,0:T(8,128)S(1)} %get-tuple-element.53.refs_0_, f32[8,512]{1,0:T(8,128)S(1)} %get-tuple-element.54.refs_1_, f32[1368,128]{1,0:T(8,128)S(1)} %get-tuple-element.55.refs_2_, ...), custom_call_target="tpu_custom_call" | custom-call | flops 603979776 | bytes 1048576 | tf_op jit(solution)/shard_map/backward/pallas_call | solution.py:87
  62.6 9.0 %all_to_all.11.refs_0_ = f32[32,1,128]{2,1,0:T(1,128)S(1)} all-to-all(f32[32,1,128]{2,1,0:T(1,128)S(1)} %get-tuple-element.60), channel_id=1, replica_groups=mesh['page'=8,'query'=2,'head'=2] {'page','query','head'}, dimensions={0} | all-to-all | bytes 32768 | tf_op jit(solution)/shard_map/all_to_all | solution.py:645
  71.7 1.0 %page_update.2.refs_6_ = f32[1040,128]{1,0:T(8,128)S(1)} custom-call(f32[32,1,128]{2,1,0:T(1,128)S(1)} %all_to_all.11.refs_0_, f32[520,128]{1,0:T(8,128)S(1)} %get-tuple-element.62.refs_1_, f32[1368,128]{1,0:T(8,128)S(1)} %get-tuple-element.55.refs_2_, f32[1368,128]{1,0:T(8,128)S(1)} %collective-permute-done.17.refs_3_, ...), custom_call_target="tpu_custom_call" | custom-call | flops 301989888 | bytes 1048576 | tf_op jit(solution)/shard_map/page_update/pallas_call | solution.py:87
  72.7 0.1 collective-permute-start.19
  72.7 1.0 %page_update.3.refs_0_ = f32[1040,128]{1,0:T(8,128)S(1)} custom-call(f32[32,1,128]{2,1,0:T(1,128)S(1)} %all_to_all.11.refs_0_, f32[520,128]{1,0:T(8,128)S(1)} %get-tuple-element.61.refs_1_, f32[1368,128]{1,0:T(8,128)S(1)} %get-tuple-element.55.refs_2_, f32[1368,128]{1,0:T(8,128)S(1)} %collective-permute-done.17.refs_3_, ...), custom_call_target="tpu_custom_call" | custom-call | flops 301989888 | bytes 1048576 | tf_op jit(solution)/shard_map/page_update/pallas_call | solution.py:87
  73.8 0.8 %unpack_own.1 = (f32[4,256,128]{2,1,0:T(8,128)}, f32[4,256,128]{2,1,0:T(8,128)}) custom-call(f32[1040,128]{1,0:T(8,128)S(1)} %page_update.3.refs_0_), custom_call_target="tpu_custom_call" | custom-call | flops 1024 | bytes 1048576 | tf_op jit(solution)/shard_map/unpack_own/pallas_call | solution.py:87
  74.6 0.1 collective-permute-done.19.refs_1_
  74.7 1.4 %unpack.1 = (f32[4,256,128]{2,1,0:T(8,128)}, f32[4,256,128]{2,1,0:T(8,128)}, f32[4,256]{1,0:T(4,128)}) custom-call(f32[1040,128]{1,0:T(8,128)S(1)} %page_update.3.refs_0_, f32[1040,128]{1,0:T(8,128)S(1)} %collective-permute-done.19.refs_1_, f32[4,256,128]{2,1,0:T(8,128)} %get-tuple-element.63.refs_2_, ...), custom_call_target="tpu_custom_call", output_to_operand_aliasing={{0}: (2, {}), {1}: (3, {})} | custom-call | flops 1048576 | bytes 1048576 | tf_op jit(solution)/shard_map/unpack/pallas_call | solution.py:87
  (24 shorter events, 0.1 us)
Async XLA Ops:
  0.6 5.2 %copy-start.3 = (f32[4,256,128]{2,1,0:T(8,128)S(1)}, f32[4,256,128]{2,1,0:T(8,128)}, u32[]{:S(2)}) copy-start(f32[4,256,128]{2,1,0:T(8,128)} %refs_4_.3) | copy-start | bytes 1572868
  0.6 5.2 %copy-start.2 = (f32[4,256,128]{2,1,0:T(8,128)S(1)}, f32[4,256,128]{2,1,0:T(8,128)}, u32[]{:S(2)}) copy-start(f32[4,256,128]{2,1,0:T(8,128)} %refs_2_.3) | copy-start | bytes 1572868
  0.7 5.2 %copy-start.1 = (f32[4,256,128]{2,1,0:T(8,128)S(1)}, f32[4,256,128]{2,1,0:T(8,128)}, u32[]{:S(2)}) copy-start(f32[4,256,128]{2,1,0:T(8,128)} %refs_1_.3) | copy-start | bytes 1572868
  0.7 5.2 %copy-start = (f32[4,256,128]{2,1,0:T(8,128)S(1)}, f32[4,256,128]{2,1,0:T(8,128)}, u32[]{:S(2)}) copy-start(f32[4,256,128]{2,1,0:T(8,128)} %refs_0_.3) | copy-start | bytes 1572868
  0.7 5.2 %copy-start.5 = (f32[4,256]{1,0:T(4,128)S(1)}, f32[4,256]{1,0:T(4,128)}, u32[]{:S(2)}) copy-start(f32[4,256]{1,0:T(4,128)} %refs_3_.3) | copy-start | bytes 12292
  0.7 5.2 %copy-start.6 = (s32[4,256]{1,0:T(4,128)S(1)}, s32[4,256]{1,0:T(4,128)}, u32[]{:S(2)}) copy-start(s32[4,256]{1,0:T(4,128)} %refs_5_.3) | copy-start | bytes 12292
  2.7 3.2 %copy-start.7 = (s32[8]{0:T(128)S(1)}, s32[8]{0:T(128)}, u32[]{:S(2)}) copy-start(s32[8]{0:T(128)} %refs_6_.3) | copy-start | bytes 100
  2.7 3.8 %collective-permute-start = (f32[520,128]{1,0:T(8,128)}, f32[520,128]{1,0:T(8,128)S(1)}, u32[]{:S(2)}, u32[]{:S(2)}) collective-permute-start(f32[520,128]{1,0:T(8,128)} %get-tuple-element.35), channel_id=1, source_target_pairs={{0,4},{4,0},{8,12},{12,8},{16,20},{20,16},{24,28},{28,24},{1,5},{5... | collective-permute-start | bytes 798728 | tf_op jit(solution)/shard_map/ppermute | solution.py:39
  3.3 8.5 %collective-permute-start.1 = (f32[328,128]{1,0:T(8,128)}, f32[328,128]{1,0:T(8,128)S(1)}, u32[]{:S(2)}, u32[]{:S(2)}) collective-permute-start(f32[328,128]{1,0:T(8,128)} %get-tuple-element.37.refs_5_), channel_id=1, source_target_pairs={{0,2},{2,0},{1,3},{3,1},{4,6},{6,4},{5,7},{7,5},{8,10},{10,8},{9,1... | collective-permute-start | bytes 503816 | tf_op jit(solution)/shard_map/ppermute | solution.py:39
  7.5 9.4 %collective-permute-start.2 = (f32[72,128]{1,0:T(8,128)S(1)}, f32[72,128]{1,0:T(8,128)S(1)}, u32[]{:S(2)}, u32[]{:S(2)}) collective-permute-start(f32[72,128]{1,0:T(8,128)S(1)} %get-tuple-element.42), channel_id=1, source_target_pairs={{0,16},{4,20},{8,24},{12,28},{16,0},{20,4},{24,8},{28,12},{1,17},{... | collective-permute-start | bytes 110600 | tf_op jit(solution)/shard_map/ppermute | solution.py:39
  10.2 6.7 %collective-permute-start.3 = (f32[72,128]{1,0:T(8,128)S(1)}, f32[72,128]{1,0:T(8,128)S(1)}, u32[]{:S(2)}, u32[]{:S(2)}) collective-permute-start(f32[72,128]{1,0:T(8,128)S(1)} %get-tuple-element.43), channel_id=1, source_target_pairs={{0,24},{4,28},{8,16},{12,20},{16,8},{20,12},{24,0},{28,4},{1,25},{... | collective-permute-start | bytes 110600 | tf_op jit(solution)/shard_map/ppermute | solution.py:39
  11.5 5.4 %collective-permute-start.4 = (f32[72,128]{1,0:T(8,128)S(1)}, f32[72,128]{1,0:T(8,128)S(1)}, u32[]{:S(2)}, u32[]{:S(2)}) collective-permute-start(f32[72,128]{1,0:T(8,128)S(1)} %get-tuple-element.44), channel_id=1, source_target_pairs={{0,8},{4,12},{8,0},{12,4},{16,24},{20,28},{24,16},{28,20},{1,9},{5... | collective-permute-start | bytes 110600 | tf_op jit(solution)/shard_map/ppermute | solution.py:39
  12.7 4.9 %collective-permute-start.5 = (f32[72,128]{1,0:T(8,128)S(1)}, f32[72,128]{1,0:T(8,128)S(1)}, u32[]{:S(2)}, u32[]{:S(2)}) collective-permute-start(f32[72,128]{1,0:T(8,128)S(1)} %get-tuple-element.46), channel_id=1, source_target_pairs={{0,16},{4,20},{8,24},{12,28},{16,0},{20,4},{24,8},{28,12},{1,17},{... | collective-permute-start | bytes 110600 | tf_op jit(solution)/shard_map/ppermute | solution.py:39
  15.5 5.8 %collective-permute-start.6 = (f32[72,128]{1,0:T(8,128)S(1)}, f32[72,128]{1,0:T(8,128)S(1)}, u32[]{:S(2)}, u32[]{:S(2)}) collective-permute-start(f32[72,128]{1,0:T(8,128)S(1)} %get-tuple-element.47), channel_id=1, source_target_pairs={{0,24},{4,28},{8,16},{12,20},{16,8},{20,12},{24,0},{28,4},{1,25},{... | collective-permute-start | bytes 110600 | tf_op jit(solution)/shard_map/ppermute | solution.py:39
  16.9 4.4 %collective-permute-start.7 = (f32[72,128]{1,0:T(8,128)S(1)}, f32[72,128]{1,0:T(8,128)S(1)}, u32[]{:S(2)}, u32[]{:S(2)}) collective-permute-start(f32[72,128]{1,0:T(8,128)S(1)} %get-tuple-element.48), channel_id=1, source_target_pairs={{0,8},{4,12},{8,0},{12,4},{16,24},{20,28},{24,16},{28,20},{1,9},{5... | collective-permute-start | bytes 110600 | tf_op jit(solution)/shard_map/ppermute | solution.py:39
  21.6 5.7 %collective-permute-start.10 = (f32[136,128]{1,0:T(8,128)S(1)}, f32[136,128]{1,0:T(8,128)S(1)}, u32[]{:S(2)}, u32[]{:S(2)}) collective-permute-start(f32[136,128]{1,0:T(8,128)S(1)} %merge.2.refs_8_), channel_id=1, source_target_pairs={{0,16},{4,20},{8,24},{12,28},{16,0},{20,4},{24,8},{28,12},{1,17},{... | collective-permute-start | bytes 208904 | tf_op jit(solution)/shard_map/ppermute | solution.py:39
  22.6 6.2 %collective-permute-start.9 = (f32[136,128]{1,0:T(8,128)S(1)}, f32[136,128]{1,0:T(8,128)S(1)}, u32[]{:S(2)}, u32[]{:S(2)}) collective-permute-start(f32[136,128]{1,0:T(8,128)S(1)} %merge.2.refs_8_), channel_id=1, source_target_pairs={{0,24},{4,28},{8,16},{12,20},{16,8},{20,12},{24,0},{28,4},{1,25},{... | collective-permute-start | bytes 208904 | tf_op jit(solution)/shard_map/ppermute | solution.py:39
  23.9 5.1 %collective-permute-start.8 = (f32[136,128]{1,0:T(8,128)S(1)}, f32[136,128]{1,0:T(8,128)S(1)}, u32[]{:S(2)}, u32[]{:S(2)}) collective-permute-start(f32[136,128]{1,0:T(8,128)S(1)} %merge.2.refs_8_), channel_id=1, source_target_pairs={{0,8},{4,12},{8,0},{12,4},{16,24},{20,28},{24,16},{28,20},{1,9},{5... | collective-permute-start | bytes 208904 | tf_op jit(solution)/shard_map/ppermute | solution.py:39
  42.4 29.3 %collective-permute-start.17 = (f32[1368,128]{1,0:T(8,128)S(1)}, f32[1368,128]{1,0:T(8,128)S(1)}, u32[]{:S(2)}, u32[]{:S(2)}) collective-permute-start(f32[1368,128]{1,0:T(8,128)S(1)} %get-tuple-element.55.refs_2_), channel_id=1, source_target_pairs={{0,2},{2,0},{1,3},{3,1},{4,6},{6,4},{5,7},{7,5},{8,10},{10,8},{9,1... | collective-permute-start | bytes 2101256 | tf_op jit(solution)/shard_map/ppermute | solution.py:39
  43.0 8.0 %collective-permute-start.11 = (f32[136,128]{1,0:T(8,128)S(1)}, f32[136,128]{1,0:T(8,128)S(1)}, u32[]{:S(2)}, u32[]{:S(2)}) collective-permute-start(f32[136,128]{1,0:T(8,128)S(1)} %get-tuple-element.57), channel_id=1, source_target_pairs={{0,16},{4,20},{8,24},{12,28},{16,0},{20,4},{24,8},{28,12},{1,17},{... | collective-permute-start | bytes 208904 | tf_op jit(solution)/shard_map/ppermute | solution.py:39
  43.6 7.4 %collective-permute-start.12 = (f32[136,128]{1,0:T(8,128)S(1)}, f32[136,128]{1,0:T(8,128)S(1)}, u32[]{:S(2)}, u32[]{:S(2)}) collective-permute-start(f32[136,128]{1,0:T(8,128)S(1)} %get-tuple-element.58), channel_id=1, source_target_pairs={{0,24},{4,28},{8,16},{12,20},{16,8},{20,12},{24,0},{28,4},{1,25},{... | collective-permute-start | bytes 208904 | tf_op jit(solution)/shard_map/ppermute | solution.py:39
  45.9 5.4 %collective-permute-start.13 = (f32[136,128]{1,0:T(8,128)S(1)}, f32[136,128]{1,0:T(8,128)S(1)}, u32[]{:S(2)}, u32[]{:S(2)}) collective-permute-start(f32[136,128]{1,0:T(8,128)S(1)} %get-tuple-element.59), channel_id=1, source_target_pairs={{0,8},{4,12},{8,0},{12,4},{16,24},{20,28},{24,16},{28,20},{1,9},{5... | collective-permute-start | bytes 208904 | tf_op jit(solution)/shard_map/ppermute | solution.py:39
  51.4 7.1 %collective-permute-start.16 = (f32[136,128]{1,0:T(8,128)S(1)}, f32[136,128]{1,0:T(8,128)S(1)}, u32[]{:S(2)}, u32[]{:S(2)}) collective-permute-start(f32[136,128]{1,0:T(8,128)S(1)} %merge.3.refs_0_), channel_id=1, source_target_pairs={{0,16},{4,20},{8,24},{12,28},{16,0},{20,4},{24,8},{28,12},{1,17},{... | collective-permute-start | bytes 208904 | tf_op jit(solution)/shard_map/ppermute | solution.py:39
  52.0 7.2 %collective-permute-start.15 = (f32[136,128]{1,0:T(8,128)S(1)}, f32[136,128]{1,0:T(8,128)S(1)}, u32[]{:S(2)}, u32[]{:S(2)}) collective-permute-start(f32[136,128]{1,0:T(8,128)S(1)} %merge.3.refs_0_), channel_id=1, source_target_pairs={{0,24},{4,28},{8,16},{12,20},{16,8},{20,12},{24,0},{28,4},{1,25},{... | collective-permute-start | bytes 208904 | tf_op jit(solution)/shard_map/ppermute | solution.py:39
  55.1 4.7 %collective-permute-start.14 = (f32[136,128]{1,0:T(8,128)S(1)}, f32[136,128]{1,0:T(8,128)S(1)}, u32[]{:S(2)}, u32[]{:S(2)}) collective-permute-start(f32[136,128]{1,0:T(8,128)S(1)} %merge.3.refs_0_), channel_id=1, source_target_pairs={{0,8},{4,12},{8,0},{12,4},{16,24},{20,28},{24,16},{28,20},{1,9},{5... | collective-permute-start | bytes 208904 | tf_op jit(solution)/shard_map/ppermute | solution.py:39
  59.9 11.8 %collective-permute-start.18 = (f32[136,512]{1,0:T(8,128)S(1)}, f32[136,512]{1,0:T(8,128)S(1)}, u32[]{:S(2)}, u32[]{:S(2)}) collective-permute-start(f32[136,512]{1,0:T(8,128)S(1)} %join.1.refs_5_), channel_id=1, source_target_pairs={{0,2},{2,0},{1,3},{3,1},{4,6},{6,4},{5,7},{7,5},{8,10},{10,8},{9,1... | collective-permute-start | bytes 835592 | tf_op jit(solution)/shard_map/ppermute | solution.py:39
  61.3 10.3 %copy-start.4 = (f32[328,128]{1,0:T(8,128)S(1)}, f32[328,128]{1,0:T(8,128)}, u32[]{:S(2)}) copy-start(f32[328,128]{1,0:T(8,128)} %get-tuple-element.37.refs_5_) | copy-start | bytes 503812
  72.7 2.0 %collective-permute-start.19 = (f32[1040,128]{1,0:T(8,128)S(1)}, f32[1040,128]{1,0:T(8,128)S(1)}, u32[]{:S(2)}, u32[]{:S(2)}) collective-permute-start(f32[1040,128]{1,0:T(8,128)S(1)} %page_update.2.refs_6_), channel_id=1, source_target_pairs={{0,4},{4,0},{8,12},{12,8},{16,20},{20,16},{24,28},{28,24},{1,5},{5... | collective-permute-start | bytes 1597448 | tf_op jit(solution)/shard_map/ppermute | solution.py:39

commit v25 on v21

--- a/solution.py
+++ b/solution.py
@@ -175,13 +175,6 @@
         masks = {axis: mask for axis, mask in masks.items() if mask}
         return exchange(value, **masks) if masks else value
 
-    def pack_queries(head, rank, queries, targets, out):
-        rows = pl.ds(pl.multiple_of(rank * piece, piece), piece)
-        return [
-            (queries.at[head], out.at[pl.ds(0, part_rows)]),
-            (targets.at[head, rows], out.at[pl.ds(part_rows, piece)]),
-        ]
-
     def pack_state(head, keys, values, out):
         return [
             (keys.at[head], out.at[pl.ds(0, slot_rows)]),
@@ -220,7 +213,7 @@
         )
         copies = pack_state(mate_head, keys, values, state_out)
         for head, out in zip(heads, query_outs):
-            copies += pack_queries(head, rank, queries, targets, out)
+            copies.append((queries.at[head], out.at[pl.ds(0, part_rows)]))
         copies = start_all(copies, sems, 3)
         for copy in small:
             copy.wait()
@@ -228,13 +221,14 @@
             mate_head, CORES * rank + core, bias_ref, assignment_ref
         )
         for head, out in zip(heads, query_outs):
-            out[part_rows + piece :, :] = position_tail(head, positions_ref)
+            out[part_rows:, :] = position_tail(head, positions_ref)
         for copy in copies:
             copy.wait()
 
     def own_body(
         queries, keys, values, biases, targets, positions, assignment, state_out, query_out, *refs
     ):
+        target_outs, refs = refs[:query_devices], refs[query_devices:]
         bias_ref, positions_ref, assignment_ref, sems = refs
         rank, core, me = places()
         head = CORES * me + core
@@ -242,18 +236,21 @@
             [(assignment, assignment_ref), (positions, positions_ref), (biases, bias_ref)], sems
         )
         copies = pack_state(head, keys, values, state_out)
-        copies += pack_queries(head, rank, queries, targets, query_out)
+        copies.append((queries.at[head], query_out.at[pl.ds(0, part_rows)]))
+        rows = pl.ds(pl.multiple_of(rank * piece, piece), piece)
+        for turn, out in enumerate(target_outs):
+            copies.append((targets.at[CORES * (me ^ turn) + core, rows], out))
         copies = start_all(copies, sems, 3)
         for copy in small:
             copy.wait()
         state_out[2 * slot_rows :, :] = state_tail(
             head, CORES * rank + core, bias_ref, assignment_ref
         )
-        query_out[part_rows + piece :, :] = position_tail(head, positions_ref)
+        query_out[part_rows:, :] = position_tail(head, positions_ref)
         for copy in copies:
             copy.wait()
 
-    state_shape, query_shape = (packed_rows, width), (part_rows + piece + TAIL, width)
+    state_shape, query_shape = (packed_rows, width), (part_rows + TAIL, width)
     small_scratch = [
         pltpu.VMEM(slot_bias.shape, jnp.float32),
         pltpu.VMEM(positions.shape, jnp.int32),
@@ -272,13 +269,13 @@
         space=pl.ANY,
         vmem=60,
     )
-    own_state, own_queries = call(
+    own_state, own_queries, own_targets, *sent_targets = call(
         own_body,
-        [state_shape, query_shape],
+        [state_shape, query_shape] + [(piece, width)] * query_devices,
         "own",
         2**24,
         arguments,
-        small_scratch + [pltpu.SemaphoreType.DMA((7,))],
+        small_scratch + [pltpu.SemaphoreType.DMA((6 + query_devices,))],
         space=pl.ANY,
     )
     packs = [own_queries] + list(sent_queries)
@@ -337,7 +334,7 @@
 
     def read_positions(query_refs):
         return in_columns(
-            [tail_as_row(ref, part_rows + piece, pos_rows) for ref in query_refs], 1
+            [tail_as_row(ref, part_rows, pos_rows) for ref in query_refs], 1
         )
 
     def forward(state_refs, query_refs, chunk_outs, weights_out, max_out, chunks):
@@ -393,10 +390,14 @@
 
     def part_body(*refs):
         state_refs, (query_ref, *refs) = refs[:CORES], refs[CORES:]
-        piece_outs, (weights_out, max_out, pieces) = refs[:ranks], refs[ranks:]
+        target_refs, refs = refs[: len(passed)], refs[len(passed) :]
+        piece_outs, (weights_out, max_out, *refs) = refs[:ranks], refs[ranks:]
+        *target_outs, pieces = refs
+        for ref, out in zip(target_refs, target_outs):
+            out[...] = ref[...]
         rank, _, _ = places()
         queries = halves(query_ref[:part_rows, :])
-        position_row = tail_as_row(query_ref, part_rows + piece, pos_rows)
+        position_row = tail_as_row(query_ref, part_rows, pos_rows)
         all_scores, all_visible = [], []
         for ref in state_refs:
             scores, visible = page_scores(ref, queries, position_row)
@@ -439,10 +440,8 @@
             store_pack(state_outs[at], updated(state, read_pack(grad_refs[at]), sizes))
         forward(state_outs, query_refs, chunk_outs, *refs)
 
-    def merged_chunk(query_refs, sums, maxima, totals, out):
-        targets = jnp.concatenate(
-            [ref[part_rows : part_rows + piece, :] for ref in query_refs], axis=0
-        )
+    def merged_chunk(target_refs, sums, maxima, totals, out):
+        targets = jnp.concatenate([ref[...] for ref in target_refs], axis=0)
         row_max = maxima[0]
         for other in maxima[1:]:
             row_max = jnp.maximum(row_max, other)
@@ -461,7 +460,7 @@
         )
 
     def first_merge_body(*refs):
-        query_refs, (*piece_refs, merged_out) = refs[:query_devices], refs[query_devices:]
+        target_refs, (*piece_refs, merged_out) = refs[:query_devices], refs[query_devices:]
 
         def joined(read):
             return [
@@ -470,7 +469,7 @@
             ]
 
         merged_chunk(
-            query_refs,
+            target_refs,
             joined(lambda ref: unfold_rows(ref[:folded, :])),
             joined(lambda ref: ref[folded : folded + 1, :piece]),
             joined(lambda ref: ref[folded + 1 : folded + 2, :piece]),
@@ -478,9 +477,9 @@
         )
 
     def merge_body(*refs):
-        query_refs, (*chunk_refs, merged_out) = refs[:query_devices], refs[query_devices:]
+        target_refs, (*chunk_refs, merged_out) = refs[:query_devices], refs[query_devices:]
         merged_chunk(
-            query_refs,
+            target_refs,
             [ref[:width, :] for ref in chunk_refs],
             [ref[width : width + 1, :] for ref in chunk_refs],
             [ref[width + 1 : width + 2, :] for ref in chunk_refs],
@@ -579,16 +578,18 @@
         last = repeat == STEPS - 1
         if repeat == 0:
             sums, weights, maxima = [], [], []
-            for query_pack in query_parts:
-                *pieces, part_weights, part_max = call(
+            for part, query_pack in enumerate(query_parts):
+                passed = list(sent_targets) if part == query_devices - 1 else []
+                outs = call(
                     part_body,
-                    part_shapes,
+                    part_shapes + [(piece, width)] * len(passed),
                     "forward",
                     2 * matmul_cost // query_devices,
-                    states + [query_pack],
+                    states + [query_pack] + passed,
                     piece_scratch,
-                    after=maxima[-1:],
+                    after=maxima[-1:] + sums[:1],
                 )
+                pieces, (part_weights, part_max, *leaving) = list(outs[:ranks]), outs[ranks:]
                 arrived = {
                     turn: exchange(pieces[turn], page=CORES * turn)
                     for turn in turns
@@ -596,6 +597,9 @@
                 sums += list(arrived.values()) + pieces[:1]
                 weights.append(part_weights)
                 maxima.append(part_max)
+            target_parts = [own_targets] + [
+                exchange(rows, query=turn) for turn, rows in enumerate(leaving, 1)
+            ]
         else:
             new_state, *chunk_parts, part_weights, part_max = call(
                 next_body,
@@ -619,7 +623,7 @@
             [chunk_shape],
             "merge",
             2**20,
-            query_parts + sums,
+            target_parts + sums,
         )
         all_merged = [merged] + [exchange(merged, page=CORES * turn) for turn in reversed(turns)]
         if last:

time: 75.9 us -> 78.3 us (1.032)
  starting transfers between devices: 24.4 us -> 26.8 us
    ppermute x20 -> x21, starting transfers between devices: 24.4 us -> 26.8 us  [exchange(): return lax.ppermute(value, axes, pairs)]
    ppermute x20 -> x21, waiting for transfers between devices: 18.7 us -> 19.1 us  [exchange(): return lax.ppermute(value, axes, pairs)]
  transfers between devices with their start and end apart: 20 -> 21, of which waited for: 11 -> 11; matrix products, arithmetic and copies ran while one was open for 0% -> 0% of each run, Pallas kernels for 7% -> 6%
where the time goes in v25:
time: 78.3 us; the launch traced here: 78.1 us
  starting transfers between devices  26.8 us (34%)
  blocking collectives  19.6 us (25%)
  waiting for transfers between devices  19.1 us (24%)
  Pallas kernels  11.8 us (15%)
  between operations  0.82 us (1%)
    ppermute x21, starting transfers between devices, exchange(): return lax.ppermute(value, axes, pairs)  26.8 us
    all_to_all x2, blocking collectives, direct_per_device(): lax.all_to_all(squares, ('page', 'query', 'head'), split_axis=0, concat_a...  19.6 us
    ppermute x21, waiting for transfers between devices, exchange(): return lax.ppermute(value, axes, pairs)  19.1 us
    pallas_call x13, Pallas kernels, call(): pl.pallas_call(without_after, out_shape=[jax.ShapeDtypeStruct(shape, jnp....  11.8 us
  transfers between devices with their start and end apart: 21, of which 11 were waited for; matrix products, arithmetic and copies ran while one was open for 0% of the time, Pallas kernels for 6%

profile of v25, /device:TPU:0, one launch (start us, length us, event | category | flops | bytes accessed | tf_op | source)
XLA Modules:
  0.0 78.1 jit_solution(14922477340473677017)
XLA Ops:
  0.7 2.0 %pack.1 = (f32[520,128]{1,0:T(8,128)}, f32[264,128]{1,0:T(8,128)}) custom-call(f32[4,256,128]{2,1,0:T(8,128)} %refs_0_.3, f32[4,256,128]{2,1,0:T(8,128)} %refs_1_.3, f32[4,256,128]{2,1,0:T(8,128)} %refs_2_.3, f32[4,256]{1,0:T(4,128)} %refs_3_.3, f32[4,256,128]{2,1,0:T(8,128)} %refs_4_.3, s32[4,256]{1,0:T(4,128)} %refs_5_.3, s32[8]{0:T(128)} %refs_6_.3), custom_call_target="tpu_custom_call" | custom-call | flops 1048576 | bytes 1048576 | tf_op jit(solution)/shard_map/pack/pallas_call | solution.py:85
  2.7 0.0 copy-start.7
  2.7 0.5 collective-permute-start
  3.2 2.6 %collective-permute-start.1 = (f32[264,128]{1,0:T(8,128)}, f32[264,128]{1,0:T(8,128)S(1)}, u32[]{:S(2)}, u32[]{:S(2)}) collective-permute-start(f32[264,128]{1,0:T(8,128)} %get-tuple-element.38.refs_5_), channel_id=1, source_target_pairs={{0,2},{2,0},{1,3},{3,1},{4,6},{6,4},{5,7},{7,5},{8,10},{10,8},{9,1... | collective-permute-start | bytes 405512 | tf_op jit(solution)/shard_map/ppermute | solution.py:39
  5.9 0.7 own.1
  6.6 0.0 collective-permute-done.refs_1_.refs_5_
  6.6 0.9 %forward.2 = (f32[72,128]{1,0:T(8,128)S(1)}, f32[72,128]{1,0:T(8,128)S(1)}, f32[72,128]{1,0:T(8,128)S(1)}, f32[72,128]{1,0:T(8,128)S(1)}, f32[512,256]{1,0:T(8,128)S(1)}, /*index=5*/f32[8,256]{1,0:T(8,128)S(1)}) custom-call(f32[520,128]{1,0:T(8,128)S(1)} %get-tuple-element.35.refs_0_.refs_4_, f32[520,128]{1,0:T(8,128)S(1)} %collective-permute-done.refs_1_.refs_5_, ...), custom_call_target="tpu_custom_call" | custom-call | flops 201326592 | bytes 1048576 | tf_op jit(solution)/shard_map/forward/pallas_call | solution.py:85
  7.5 2.7 %collective-permute-start.2 = (f32[72,128]{1,0:T(8,128)S(1)}, f32[72,128]{1,0:T(8,128)S(1)}, u32[]{:S(2)}, u32[]{:S(2)}) collective-permute-start(f32[72,128]{1,0:T(8,128)S(1)} %get-tuple-element.42), channel_id=1, source_target_pairs={{0,16},{4,20},{8,24},{12,28},{16,0},{20,4},{24,8},{28,12},{1,17},{... | collective-permute-start | bytes 110600 | tf_op jit(solution)/shard_map/ppermute | solution.py:39
  10.2 1.3 %collective-permute-start.4 = (f32[72,128]{1,0:T(8,128)S(1)}, f32[72,128]{1,0:T(8,128)S(1)}, u32[]{:S(2)}, u32[]{:S(2)}) collective-permute-start(f32[72,128]{1,0:T(8,128)S(1)} %get-tuple-element.47), channel_id=1, source_target_pairs={{0,24},{4,28},{8,16},{12,20},{16,8},{20,12},{24,0},{28,4},{1,25},{... | collective-permute-start | bytes 110600 | tf_op jit(solution)/shard_map/ppermute | solution.py:39
  11.5 0.2 collective-permute-start.5
  11.8 1.1 %collective-permute-done.2.refs_5_.refs_2_ = f32[72,128]{1,0:T(8,128)S(1)} collective-permute-done((f32[72,128]{1,0:T(8,128)S(1)}, f32[72,128]{1,0:T(8,128)S(1)}, u32[]{:S(2)}, u32[]{:S(2)}) %collective-permute-start.2) | collective-permute-done | bytes 36896 | tf_op jit(solution)/shard_map/ppermute | solution.py:39
  12.9 0.9 %forward.3 = (f32[72,128]{1,0:T(8,128)S(1)}, f32[72,128]{1,0:T(8,128)S(1)}, f32[72,128]{1,0:T(8,128)S(1)}, f32[72,128]{1,0:T(8,128)S(1)}, f32[512,256]{1,0:T(8,1...) custom-call(f32[520,128]{1,0:T(8,128)S(1)} %get-tuple-element.35.refs_0_.refs_4_, ...), custom_call_target="tpu_custom_call" | custom-call | flops 201326592 | bytes 1048576 | tf_op jit(solution)/shard_map/forward/pallas_call | solution.py:85
  13.8 2.4 %collective-permute-start.6 = (f32[72,128]{1,0:T(8,128)S(1)}, f32[72,128]{1,0:T(8,128)S(1)}, u32[]{:S(2)}, u32[]{:S(2)}) collective-permute-start(f32[72,128]{1,0:T(8,128)S(1)} %get-tuple-element.50), channel_id=1, source_target_pairs={{0,16},{4,20},{8,24},{12,28},{16,0},{20,4},{24,8},{28,12},{1,17},{... | collective-permute-start | bytes 110600 | tf_op jit(solution)/shard_map/ppermute | solution.py:39
  16.2 2.4 %collective-permute-start.7 = (f32[72,128]{1,0:T(8,128)S(1)}, f32[72,128]{1,0:T(8,128)S(1)}, u32[]{:S(2)}, u32[]{:S(2)}) collective-permute-start(f32[72,128]{1,0:T(8,128)S(1)} %get-tuple-element.51), channel_id=1, source_target_pairs={{0,24},{4,28},{8,16},{12,20},{16,8},{20,12},{24,0},{28,4},{1,25},{... | collective-permute-start | bytes 110600 | tf_op jit(solution)/shard_map/ppermute | solution.py:39
  18.6 0.5 collective-permute-start.8
  19.1 0.9 %collective-permute-start.3 = (f32[64,128]{1,0:T(8,128)S(1)}, f32[64,128]{1,0:T(8,128)S(1)}, u32[]{:S(2)}, u32[]{:S(2)}) collective-permute-start(f32[64,128]{1,0:T(8,128)S(1)} %get-tuple-element.46), channel_id=1, source_target_pairs={{0,2},{2,0},{1,3},{3,1},{4,6},{6,4},{5,7},{7,5},{8,10},{10,8},{9,1... | collective-permute-start | bytes 98312 | tf_op jit(solution)/shard_map/ppermute | solution.py:39
  20.0 0.0 collective-permute-done.5.refs_4_
  20.0 3.0 %collective-permute-done.3.refs_1_ = f32[64,128]{1,0:T(8,128)S(1)} collective-permute-done((f32[64,128]{1,0:T(8,128)S(1)}, f32[64,128]{1,0:T(8,128)S(1)}, u32[]{:S(2)}, u32[]{:S(2)}) %collective-permute-start.3) | collective-permute-done | bytes 32800 | tf_op jit(solution)/shard_map/ppermute | solution.py:39
  23.0 0.3 merge.2.refs_8_
  23.3 1.5 %collective-permute-start.11 = (f32[136,128]{1,0:T(8,128)S(1)}, f32[136,128]{1,0:T(8,128)S(1)}, u32[]{:S(2)}, u32[]{:S(2)}) collective-permute-start(f32[136,128]{1,0:T(8,128)S(1)} %merge.2.refs_8_), channel_id=1, source_target_pairs={{0,16},{4,20},{8,24},{12,28},{16,0},{20,4},{24,8},{28,12},{1,17},{... | collective-permute-start | bytes 208904 | tf_op jit(solution)/shard_map/ppermute | solution.py:39
  24.8 2.4 %collective-permute-start.10 = (f32[136,128]{1,0:T(8,128)S(1)}, f32[136,128]{1,0:T(8,128)S(1)}, u32[]{:S(2)}, u32[]{:S(2)}) collective-permute-start(f32[136,128]{1,0:T(8,128)S(1)} %merge.2.refs_8_), channel_id=1, source_target_pairs={{0,24},{4,28},{8,16},{12,20},{16,8},{20,12},{24,0},{28,4},{1,25},{... | collective-permute-start | bytes 208904 | tf_op jit(solution)/shard_map/ppermute | solution.py:39
  27.2 1.3 %collective-permute-done.11.refs_11_ = f32[136,128]{1,0:T(8,128)S(1)} collective-permute-done((f32[136,128]{1,0:T(8,128)S(1)}, f32[136,128]{1,0:T(8,128)S(1)}, u32[]{:S(2)}, u32[]{:S(2)}) %collective-permute-start.11) | collective-permute-done | bytes 69664 | tf_op jit(solution)/shard_map/ppermute | solution.py:39
  28.5 2.5 %collective-permute-done.10.refs_10_ = f32[136,128]{1,0:T(8,128)S(1)} collective-permute-done((f32[136,128]{1,0:T(8,128)S(1)}, f32[136,128]{1,0:T(8,128)S(1)}, u32[]{:S(2)}, u32[]{:S(2)}) %collective-permute-start.10) | collective-permute-done | bytes 69664 | tf_op jit(solution)/shard_map/ppermute | solution.py:39
  31.0 0.7 collective-permute-done.9.refs_9_
  31.8 1.4 %backward.2 = (f32[520,128]{1,0:T(8,128)S(1)}, f32[520,128]{1,0:T(8,128)S(1)}, f32[32,1,128]{2,1,0:T(1,128)S(1)}) custom-call(f32[512,256]{1,0:T(8,128)S(1)} %get-tuple-element.39.refs_0_, f32[512,256]{1,0:T(8,128)S(1)} %get-tuple-element.43.refs_1_, f32[8,256]{1,0:T(8,128)S(1)} %get-tuple-element.41.refs_4_.refs_2_, ...), custom_call_target="tpu_custom_call" | custom-call | flops 603979776 | bytes 1048576 | tf_op jit(solution)/shard_map/backward/pallas_call | solution.py:85
  33.1 10.5 %all_to_all.10.refs_6_ = f32[32,1,128]{2,1,0:T(1,128)S(1)} all-to-all(f32[32,1,128]{2,1,0:T(1,128)S(1)} %get-tuple-element.56), channel_id=1, replica_groups=mesh['page'=8,'query'=2,'head'=2] {'page','query','head'}, dimensions={0} | all-to-all | bytes 32768 | tf_op jit(solution)/shard_map/all_to_all | solution.py:646
  43.7 1.1 %update_forward.1 = (f32[1304,128]{1,0:T(8,128)S(1)}, f32[136,128]{1,0:T(8,128)S(1)}, f32[136,128]{1,0:T(8,128)S(1)}, f32[136,128]{1,0:T(8,128)S(1)}, f32[136,12...) custom-call(f32[520,128]{1,0:T(8,128)S(1)} %get-tuple-element.35.refs_0_.refs_4_, ...), custom_call_target="tpu_custom_call" | custom-call | flops 402653184 | bytes 1048576 | tf_op jit(solution)/shard_map/update_forward/pallas_call | solution.py:85
  44.8 0.6 collective-permute-start.18
  45.4 0.6 collective-permute-start.12
  46.0 2.3 %collective-permute-start.13 = (f32[136,128]{1,0:T(8,128)S(1)}, f32[136,128]{1,0:T(8,128)S(1)}, u32[]{:S(2)}, u32[]{:S(2)}) collective-permute-start(f32[136,128]{1,0:T(8,128)S(1)} %get-tuple-element.62), channel_id=1, source_target_pairs={{0,24},{4,28},{8,16},{12,20},{16,8},{20,12},{24,0},{28,4},{1,25},{... | collective-permute-start | bytes 208904 | tf_op jit(solution)/shard_map/ppermute | solution.py:39
  48.3 0.6 collective-permute-start.14
  48.9 4.5 %collective-permute-done.12.refs_3_ = f32[136,128]{1,0:T(8,128)S(1)} collective-permute-done((f32[136,128]{1,0:T(8,128)S(1)}, f32[136,128]{1,0:T(8,128)S(1)}, u32[]{:S(2)}, u32[]{:S(2)}) %collective-permute-start.12) | collective-permute-done | bytes 69664 | tf_op jit(solution)/shard_map/ppermute | solution.py:39
  53.4 0.3 collective-permute-done.14.refs_5_
  53.7 0.1 merge.3.refs_0_
  53.8 0.6 collective-permute-start.17
  54.4 3.1 %collective-permute-start.16 = (f32[136,128]{1,0:T(8,128)S(1)}, f32[136,128]{1,0:T(8,128)S(1)}, u32[]{:S(2)}, u32[]{:S(2)}) collective-permute-start(f32[136,128]{1,0:T(8,128)S(1)} %merge.3.refs_0_), channel_id=1, source_target_pairs={{0,24},{4,28},{8,16},{12,20},{16,8},{20,12},{24,0},{28,4},{1,25},{... | collective-permute-start | bytes 208904 | tf_op jit(solution)/shard_map/ppermute | solution.py:39
  57.5 3.4 %collective-permute-done.17.refs_3_ = f32[136,128]{1,0:T(8,128)S(1)} collective-permute-done((f32[136,128]{1,0:T(8,128)S(1)}, f32[136,128]{1,0:T(8,128)S(1)}, u32[]{:S(2)}, u32[]{:S(2)}) %collective-permute-start.17) | collective-permute-done | bytes 69664 | tf_op jit(solution)/shard_map/ppermute | solution.py:39
  60.9 0.7 collective-permute-done.16.refs_2_
  61.5 0.7 collective-permute-done.15.refs_1_
  62.2 0.1 join.1.refs_5_
  62.3 1.4 %collective-permute-start.19 = (f32[136,512]{1,0:T(8,128)S(1)}, f32[136,512]{1,0:T(8,128)S(1)}, u32[]{:S(2)}, u32[]{:S(2)}) collective-permute-start(f32[136,512]{1,0:T(8,128)S(1)} %join.1.refs_5_), channel_id=1, source_target_pairs={{0,2},{2,0},{1,3},{3,1},{4,6},{6,4},{5,7},{7,5},{8,10},{10,8},{9,1... | collective-permute-start | bytes 835592 | tf_op jit(solution)/shard_map/ppermute | solution.py:39
  63.7 1.3 %backward.3 = (f32[520,128]{1,0:T(8,128)S(1)}, f32[520,128]{1,0:T(8,128)S(1)}, f32[32,1,128]{2,1,0:T(1,128)S(1)}) custom-call(f32[512,512]{1,0:T(8,128)S(1)} %get-tuple-element.57.refs_0_, f32[8,512]{1,0:T(8,128)S(1)} %get-tuple-element.58.refs_1_, f32[1304,128]{1,0:T(8,128)S(1)} %get-tuple-element.59.refs_2_, ...), custom_call_target="tpu_custom_call" | custom-call | flops 603979776 | bytes 1048576 | tf_op jit(solution)/shard_map/backward/pallas_call | solution.py:85
  65.0 9.0 %all_to_all.11.refs_0_ = f32[32,1,128]{2,1,0:T(1,128)S(1)} all-to-all(f32[32,1,128]{2,1,0:T(1,128)S(1)} %get-tuple-element.64), channel_id=1, replica_groups=mesh['page'=8,'query'=2,'head'=2] {'page','query','head'}, dimensions={0} | all-to-all | bytes 32768 | tf_op jit(solution)/shard_map/all_to_all | solution.py:646
  74.1 1.0 %page_update.2.refs_6_ = f32[1040,128]{1,0:T(8,128)S(1)} custom-call(f32[32,1,128]{2,1,0:T(1,128)S(1)} %all_to_all.11.refs_0_, f32[520,128]{1,0:T(8,128)S(1)} %get-tuple-element.66.refs_1_, f32[1304,128]{1,0:T(8,128)S(1)} %get-tuple-element.59.refs_2_, f32[1304,128]{1,0:T(8,128)S(1)} %collective-permute-done.18.refs_3_, ...), custom_call_target="tpu_custom_call" | custom-call | flops 301989888 | bytes 1048576 | tf_op jit(solution)/shard_map/page_update/pallas_call | solution.py:85
  75.1 0.1 collective-permute-start.20
  75.2 1.0 %page_update.3.refs_0_ = f32[1040,128]{1,0:T(8,128)S(1)} custom-call(f32[32,1,128]{2,1,0:T(1,128)S(1)} %all_to_all.11.refs_0_, f32[520,128]{1,0:T(8,128)S(1)} %get-tuple-element.65.refs_1_, f32[1304,128]{1,0:T(8,128)S(1)} %get-tuple-element.59.refs_2_, f32[1304,128]{1,0:T(8,128)S(1)} %collective-permute-done.18.refs_3_, ...), custom_call_target="tpu_custom_call" | custom-call | flops 301989888 | bytes 1048576 | tf_op jit(solution)/shard_map/page_update/pallas_call | solution.py:85
  76.2 0.9 %collective-permute-done.20.refs_1_ = f32[1040,128]{1,0:T(8,128)S(1)} collective-permute-done((f32[1040,128]{1,0:T(8,128)S(1)}, f32[1040,128]{1,0:T(8,128)S(1)}, u32[]{:S(2)}, u32[]{:S(2)}) %collective-permute-start.20) | collective-permute-done | bytes 532512 | tf_op jit(solution)/shard_map/ppermute | solution.py:39
  77.1 1.0 %unpack.1 = (f32[4,256,128]{2,1,0:T(8,128)}, f32[4,256,128]{2,1,0:T(8,128)}, f32[4,256]{1,0:T(4,128)}) custom-call(f32[1040,128]{1,0:T(8,128)S(1)} %page_update.3.refs_0_, f32[1040,128]{1,0:T(8,128)S(1)} %collective-permute-done.20.refs_1_), custom_call_target="tpu_custom_call" | custom-call | flops 1048576 | bytes 1048576 | tf_op jit(solution)/shard_map/unpack/pallas_call | solution.py:85
  (25 shorter events, 0.1 us)
Async XLA Ops:
  0.6 5.2 %copy-start.3 = (f32[4,256,128]{2,1,0:T(8,128)S(1)}, f32[4,256,128]{2,1,0:T(8,128)}, u32[]{:S(2)}) copy-start(f32[4,256,128]{2,1,0:T(8,128)} %refs_4_.3) | copy-start | bytes 1572868
  0.6 5.2 %copy-start.2 = (f32[4,256,128]{2,1,0:T(8,128)S(1)}, f32[4,256,128]{2,1,0:T(8,128)}, u32[]{:S(2)}) copy-start(f32[4,256,128]{2,1,0:T(8,128)} %refs_2_.3) | copy-start | bytes 1572868
  0.7 5.2 %copy-start.1 = (f32[4,256,128]{2,1,0:T(8,128)S(1)}, f32[4,256,128]{2,1,0:T(8,128)}, u32[]{:S(2)}) copy-start(f32[4,256,128]{2,1,0:T(8,128)} %refs_1_.3) | copy-start | bytes 1572868
  0.7 5.2 %copy-start = (f32[4,256,128]{2,1,0:T(8,128)S(1)}, f32[4,256,128]{2,1,0:T(8,128)}, u32[]{:S(2)}) copy-start(f32[4,256,128]{2,1,0:T(8,128)} %refs_0_.3) | copy-start | bytes 1572868
  0.7 5.2 %copy-start.5 = (f32[4,256]{1,0:T(4,128)S(1)}, f32[4,256]{1,0:T(4,128)}, u32[]{:S(2)}) copy-start(f32[4,256]{1,0:T(4,128)} %refs_3_.3) | copy-start | bytes 12292
  0.7 5.2 %copy-start.6 = (s32[4,256]{1,0:T(4,128)S(1)}, s32[4,256]{1,0:T(4,128)}, u32[]{:S(2)}) copy-start(s32[4,256]{1,0:T(4,128)} %refs_5_.3) | copy-start | bytes 12292
  2.7 3.2 %copy-start.7 = (s32[8]{0:T(128)S(1)}, s32[8]{0:T(128)}, u32[]{:S(2)}) copy-start(s32[8]{0:T(128)} %refs_6_.3) | copy-start | bytes 100
  2.7 3.9 %collective-permute-start = (f32[520,128]{1,0:T(8,128)}, f32[520,128]{1,0:T(8,128)S(1)}, u32[]{:S(2)}, u32[]{:S(2)}) collective-permute-start(f32[520,128]{1,0:T(8,128)} %get-tuple-element.36), channel_id=1, source_target_pairs={{0,4},{4,0},{8,12},{12,8},{16,20},{20,16},{24,28},{28,24},{1,5},{5... | collective-permute-start | bytes 798728 | tf_op jit(solution)/shard_map/ppermute | solution.py:39
  3.2 8.5 %collective-permute-start.1 = (f32[264,128]{1,0:T(8,128)}, f32[264,128]{1,0:T(8,128)S(1)}, u32[]{:S(2)}, u32[]{:S(2)}) collective-permute-start(f32[264,128]{1,0:T(8,128)} %get-tuple-element.38.refs_5_), channel_id=1, source_target_pairs={{0,2},{2,0},{1,3},{3,1},{4,6},{6,4},{5,7},{7,5},{8,10},{10,8},{9,1... | collective-permute-start | bytes 405512 | tf_op jit(solution)/shard_map/ppermute | solution.py:39
  7.5 5.3 %collective-permute-start.2 = (f32[72,128]{1,0:T(8,128)S(1)}, f32[72,128]{1,0:T(8,128)S(1)}, u32[]{:S(2)}, u32[]{:S(2)}) collective-permute-start(f32[72,128]{1,0:T(8,128)S(1)} %get-tuple-element.42), channel_id=1, source_target_pairs={{0,16},{4,20},{8,24},{12,28},{16,0},{20,4},{24,8},{28,12},{1,17},{... | collective-permute-start | bytes 110600 | tf_op jit(solution)/shard_map/ppermute | solution.py:39
  10.2 8.9 %collective-permute-start.4 = (f32[72,128]{1,0:T(8,128)S(1)}, f32[72,128]{1,0:T(8,128)S(1)}, u32[]{:S(2)}, u32[]{:S(2)}) collective-permute-start(f32[72,128]{1,0:T(8,128)S(1)} %get-tuple-element.47), channel_id=1, source_target_pairs={{0,24},{4,28},{8,16},{12,20},{16,8},{20,12},{24,0},{28,4},{1,25},{... | collective-permute-start | bytes 110600 | tf_op jit(solution)/shard_map/ppermute | solution.py:39
  11.5 8.4 %collective-permute-start.5 = (f32[72,128]{1,0:T(8,128)S(1)}, f32[72,128]{1,0:T(8,128)S(1)}, u32[]{:S(2)}, u32[]{:S(2)}) collective-permute-start(f32[72,128]{1,0:T(8,128)S(1)} %get-tuple-element.48), channel_id=1, source_target_pairs={{0,8},{4,12},{8,0},{12,4},{16,24},{20,28},{24,16},{28,20},{1,9},{5... | collective-permute-start | bytes 110600 | tf_op jit(solution)/shard_map/ppermute | solution.py:39
  13.8 9.2 %collective-permute-start.6 = (f32[72,128]{1,0:T(8,128)S(1)}, f32[72,128]{1,0:T(8,128)S(1)}, u32[]{:S(2)}, u32[]{:S(2)}) collective-permute-start(f32[72,128]{1,0:T(8,128)S(1)} %get-tuple-element.50), channel_id=1, source_target_pairs={{0,16},{4,20},{8,24},{12,28},{16,0},{20,4},{24,8},{28,12},{1,17},{... | collective-permute-start | bytes 110600 | tf_op jit(solution)/shard_map/ppermute | solution.py:39
  16.2 6.8 %collective-permute-start.7 = (f32[72,128]{1,0:T(8,128)S(1)}, f32[72,128]{1,0:T(8,128)S(1)}, u32[]{:S(2)}, u32[]{:S(2)}) collective-permute-start(f32[72,128]{1,0:T(8,128)S(1)} %get-tuple-element.51), channel_id=1, source_target_pairs={{0,24},{4,28},{8,16},{12,20},{16,8},{20,12},{24,0},{28,4},{1,25},{... | collective-permute-start | bytes 110600 | tf_op jit(solution)/shard_map/ppermute | solution.py:39
  18.6 4.4 %collective-permute-start.8 = (f32[72,128]{1,0:T(8,128)S(1)}, f32[72,128]{1,0:T(8,128)S(1)}, u32[]{:S(2)}, u32[]{:S(2)}) collective-permute-start(f32[72,128]{1,0:T(8,128)S(1)} %get-tuple-element.52), channel_id=1, source_target_pairs={{0,8},{4,12},{8,0},{12,4},{16,24},{20,28},{24,16},{28,20},{1,9},{5... | collective-permute-start | bytes 110600 | tf_op jit(solution)/shard_map/ppermute | solution.py:39
  19.1 3.9 %collective-permute-start.3 = (f32[64,128]{1,0:T(8,128)S(1)}, f32[64,128]{1,0:T(8,128)S(1)}, u32[]{:S(2)}, u32[]{:S(2)}) collective-permute-start(f32[64,128]{1,0:T(8,128)S(1)} %get-tuple-element.46), channel_id=1, source_target_pairs={{0,2},{2,0},{1,3},{3,1},{4,6},{6,4},{5,7},{7,5},{8,10},{10,8},{9,1... | collective-permute-start | bytes 98312 | tf_op jit(solution)/shard_map/ppermute | solution.py:39
  23.3 5.3 %collective-permute-start.11 = (f32[136,128]{1,0:T(8,128)S(1)}, f32[136,128]{1,0:T(8,128)S(1)}, u32[]{:S(2)}, u32[]{:S(2)}) collective-permute-start(f32[136,128]{1,0:T(8,128)S(1)} %merge.2.refs_8_), channel_id=1, source_target_pairs={{0,16},{4,20},{8,24},{12,28},{16,0},{20,4},{24,8},{28,12},{1,17},{... | collective-permute-start | bytes 208904 | tf_op jit(solution)/shard_map/ppermute | solution.py:39
  24.8 6.2 %collective-permute-start.10 = (f32[136,128]{1,0:T(8,128)S(1)}, f32[136,128]{1,0:T(8,128)S(1)}, u32[]{:S(2)}, u32[]{:S(2)}) collective-permute-start(f32[136,128]{1,0:T(8,128)S(1)} %merge.2.refs_8_), channel_id=1, source_target_pairs={{0,24},{4,28},{8,16},{12,20},{16,8},{20,12},{24,0},{28,4},{1,25},{... | collective-permute-start | bytes 208904 | tf_op jit(solution)/shard_map/ppermute | solution.py:39
  27.2 4.5 %collective-permute-start.9 = (f32[136,128]{1,0:T(8,128)S(1)}, f32[136,128]{1,0:T(8,128)S(1)}, u32[]{:S(2)}, u32[]{:S(2)}) collective-permute-start(f32[136,128]{1,0:T(8,128)S(1)} %merge.2.refs_8_), channel_id=1, source_target_pairs={{0,8},{4,12},{8,0},{12,4},{16,24},{20,28},{24,16},{28,20},{1,9},{5... | collective-permute-start | bytes 208904 | tf_op jit(solution)/shard_map/ppermute | solution.py:39
  44.8 29.3 %collective-permute-start.18 = (f32[1304,128]{1,0:T(8,128)S(1)}, f32[1304,128]{1,0:T(8,128)S(1)}, u32[]{:S(2)}, u32[]{:S(2)}) collective-permute-start(f32[1304,128]{1,0:T(8,128)S(1)} %get-tuple-element.59.refs_2_), channel_id=1, source_target_pairs={{0,2},{2,0},{1,3},{3,1},{4,6},{6,4},{5,7},{7,5},{8,10},{10,8},{9,1... | collective-permute-start | bytes 2002952 | tf_op jit(solution)/shard_map/ppermute | solution.py:39
  45.4 8.0 %collective-permute-start.12 = (f32[136,128]{1,0:T(8,128)S(1)}, f32[136,128]{1,0:T(8,128)S(1)}, u32[]{:S(2)}, u32[]{:S(2)}) collective-permute-start(f32[136,128]{1,0:T(8,128)S(1)} %get-tuple-element.61), channel_id=1, source_target_pairs={{0,16},{4,20},{8,24},{12,28},{16,0},{20,4},{24,8},{28,12},{1,17},{... | collective-permute-start | bytes 208904 | tf_op jit(solution)/shard_map/ppermute | solution.py:39
  46.0 7.4 %collective-permute-start.13 = (f32[136,128]{1,0:T(8,128)S(1)}, f32[136,128]{1,0:T(8,128)S(1)}, u32[]{:S(2)}, u32[]{:S(2)}) collective-permute-start(f32[136,128]{1,0:T(8,128)S(1)} %get-tuple-element.62), channel_id=1, source_target_pairs={{0,24},{4,28},{8,16},{12,20},{16,8},{20,12},{24,0},{28,4},{1,25},{... | collective-permute-start | bytes 208904 | tf_op jit(solution)/shard_map/ppermute | solution.py:39
  48.3 5.4 %collective-permute-start.14 = (f32[136,128]{1,0:T(8,128)S(1)}, f32[136,128]{1,0:T(8,128)S(1)}, u32[]{:S(2)}, u32[]{:S(2)}) collective-permute-start(f32[136,128]{1,0:T(8,128)S(1)} %get-tuple-element.63), channel_id=1, source_target_pairs={{0,8},{4,12},{8,0},{12,4},{16,24},{20,28},{24,16},{28,20},{1,9},{5... | collective-permute-start | bytes 208904 | tf_op jit(solution)/shard_map/ppermute | solution.py:39
  53.8 7.1 %collective-permute-start.17 = (f32[136,128]{1,0:T(8,128)S(1)}, f32[136,128]{1,0:T(8,128)S(1)}, u32[]{:S(2)}, u32[]{:S(2)}) collective-permute-start(f32[136,128]{1,0:T(8,128)S(1)} %merge.3.refs_0_), channel_id=1, source_target_pairs={{0,16},{4,20},{8,24},{12,28},{16,0},{20,4},{24,8},{28,12},{1,17},{... | collective-permute-start | bytes 208904 | tf_op jit(solution)/shard_map/ppermute | solution.py:39
  54.4 7.2 %collective-permute-start.16 = (f32[136,128]{1,0:T(8,128)S(1)}, f32[136,128]{1,0:T(8,128)S(1)}, u32[]{:S(2)}, u32[]{:S(2)}) collective-permute-start(f32[136,128]{1,0:T(8,128)S(1)} %merge.3.refs_0_), channel_id=1, source_target_pairs={{0,24},{4,28},{8,16},{12,20},{16,8},{20,12},{24,0},{28,4},{1,25},{... | collective-permute-start | bytes 208904 | tf_op jit(solution)/shard_map/ppermute | solution.py:39
  57.5 4.7 %collective-permute-start.15 = (f32[136,128]{1,0:T(8,128)S(1)}, f32[136,128]{1,0:T(8,128)S(1)}, u32[]{:S(2)}, u32[]{:S(2)}) collective-permute-start(f32[136,128]{1,0:T(8,128)S(1)} %merge.3.refs_0_), channel_id=1, source_target_pairs={{0,8},{4,12},{8,0},{12,4},{16,24},{20,28},{24,16},{28,20},{1,9},{5... | collective-permute-start | bytes 208904 | tf_op jit(solution)/shard_map/ppermute | solution.py:39
  62.3 11.8 %collective-permute-start.19 = (f32[136,512]{1,0:T(8,128)S(1)}, f32[136,512]{1,0:T(8,128)S(1)}, u32[]{:S(2)}, u32[]{:S(2)}) collective-permute-start(f32[136,512]{1,0:T(8,128)S(1)} %join.1.refs_5_), channel_id=1, source_target_pairs={{0,2},{2,0},{1,3},{3,1},{4,6},{6,4},{5,7},{7,5},{8,10},{10,8},{9,1... | collective-permute-start | bytes 835592 | tf_op jit(solution)/shard_map/ppermute | solution.py:39
  63.7 10.3 %copy-start.4 = (f32[264,128]{1,0:T(8,128)S(1)}, f32[264,128]{1,0:T(8,128)}, u32[]{:S(2)}) copy-start(f32[264,128]{1,0:T(8,128)} %get-tuple-element.38.refs_5_) | copy-start | bytes 405508
  75.1 2.0 %collective-permute-start.20 = (f32[1040,128]{1,0:T(8,128)S(1)}, f32[1040,128]{1,0:T(8,128)S(1)}, u32[]{:S(2)}, u32[]{:S(2)}) collective-permute-start(f32[1040,128]{1,0:T(8,128)S(1)} %page_update.2.refs_6_), channel_id=1, source_target_pairs={{0,4},{4,0},{8,12},{12,8},{16,20},{20,16},{24,28},{28,24},{1,5},{5... | collective-permute-start | bytes 1597448 | tf_op jit(solution)/shard_map/ppermute | solution.py:39

commit v26 on v21

--- a/solution.py
+++ b/solution.py
@@ -640,7 +640,7 @@
         grads = [own_grad, mate_grad]
         tiles = [
             lax.all_to_all(
-                squares, ("page", "query", "head"), split_axis=0, concat_axis=0, tiled=True
+                squares, ("head", "query", "page"), split_axis=0, concat_axis=0, tiled=True
             )
         ]
 

time: 75.9 us -> 75.8 us (level)
  no operation moved by 1% of the time
where the time goes in v26:
time: 75.8 us; the launch traced here: 75.7 us
  starting transfers between devices  24.7 us (33%)
  blocking collectives  19.8 us (26%)
  waiting for transfers between devices  18.5 us (24%)
  Pallas kernels  11.8 us (16%)
  between operations  0.83 us (1%)
    ppermute x20, starting transfers between devices, exchange(): return lax.ppermute(value, axes, pairs)  24.7 us
    all_to_all x2, blocking collectives, direct_per_device(): lax.all_to_all(squares, ('head', 'query', 'page'), split_axis=0, concat_a...  19.8 us
    ppermute x20, waiting for transfers between devices, exchange(): return lax.ppermute(value, axes, pairs)  18.5 us
    pallas_call x13, Pallas kernels, call(): pl.pallas_call(without_after, out_shape=[jax.ShapeDtypeStruct(shape, jnp....  11.8 us
  transfers between devices with their start and end apart: 20, of which 11 were waited for; matrix products, arithmetic and copies ran while one was open for 0% of the time, Pallas kernels for 7%

profile of v26, /device:TPU:0, one launch (start us, length us, event | category | flops | bytes accessed | tf_op | source)
XLA Modules:
  0.0 75.7 jit_solution(8942405751180451923)
XLA Ops:
  0.7 2.0 %pack.1 = (f32[520,128]{1,0:T(8,128)}, f32[328,128]{1,0:T(8,128)}) custom-call(f32[4,256,128]{2,1,0:T(8,128)} %refs_0_.3, f32[4,256,128]{2,1,0:T(8,128)} %refs_1_.3, f32[4,256,128]{2,1,0:T(8,128)} %refs_2_.3, f32[4,256]{1,0:T(4,128)} %refs_3_.3, f32[4,256,128]{2,1,0:T(8,128)} %refs_4_.3, s32[4,256]{1,0:T(4,128)} %refs_5_.3, s32[8]{0:T(128)} %refs_6_.3), custom_call_target="tpu_custom_call" | custom-call | flops 1048576 | bytes 1048576 | tf_op jit(solution)/shard_map/pack/pallas_call | solution.py:85
  2.7 0.0 copy-start.7
  2.7 0.5 collective-permute-start
  3.3 2.6 %collective-permute-start.1 = (f32[328,128]{1,0:T(8,128)}, f32[328,128]{1,0:T(8,128)S(1)}, u32[]{:S(2)}, u32[]{:S(2)}) collective-permute-start(f32[328,128]{1,0:T(8,128)} %get-tuple-element.35.refs_5_), channel_id=1, source_target_pairs={{0,2},{2,0},{1,3},{3,1},{4,6},{6,4},{5,7},{7,5},{8,10},{10,8},{9,1... | collective-permute-start | bytes 503816 | tf_op jit(solution)/shard_map/ppermute | solution.py:39
  5.9 0.7 own.1
  6.6 0.9 %forward.2 = (f32[72,128]{1,0:T(8,128)S(1)}, f32[72,128]{1,0:T(8,128)S(1)}, f32[72,128]{1,0:T(8,128)S(1)}, f32[72,128]{1,0:T(8,128)S(1)}, f32[512,256]{1,0:T(8,128)S(1)}, /*index=5*/f32[8,256]{1,0:T(8,128)S(1)}) custom-call(f32[520,128]{1,0:T(8,128)S(1)} %get-tuple-element.32.refs_0_.refs_4_, f32[520,128]{1,0:T(8,128)S(1)} %collective-permute-done.refs_1_.refs_5_, ...), custom_call_target="tpu_custom_call" | custom-call | flops 201326592 | bytes 1048576 | tf_op jit(solution)/shard_map/forward/pallas_call | solution.py:85
  7.5 2.7 %collective-permute-start.2 = (f32[72,128]{1,0:T(8,128)S(1)}, f32[72,128]{1,0:T(8,128)S(1)}, u32[]{:S(2)}, u32[]{:S(2)}) collective-permute-start(f32[72,128]{1,0:T(8,128)S(1)} %get-tuple-element.40), channel_id=1, source_target_pairs={{0,16},{4,20},{8,24},{12,28},{16,0},{20,4},{24,8},{28,12},{1,17},{... | collective-permute-start | bytes 110600 | tf_op jit(solution)/shard_map/ppermute | solution.py:39
  10.2 1.3 %collective-permute-start.3 = (f32[72,128]{1,0:T(8,128)S(1)}, f32[72,128]{1,0:T(8,128)S(1)}, u32[]{:S(2)}, u32[]{:S(2)}) collective-permute-start(f32[72,128]{1,0:T(8,128)S(1)} %get-tuple-element.41), channel_id=1, source_target_pairs={{0,24},{4,28},{8,16},{12,20},{16,8},{20,12},{24,0},{28,4},{1,25},{... | collective-permute-start | bytes 110600 | tf_op jit(solution)/shard_map/ppermute | solution.py:39
  11.5 0.2 collective-permute-start.4
  11.7 0.9 %forward.3 = (f32[72,128]{1,0:T(8,128)S(1)}, f32[72,128]{1,0:T(8,128)S(1)}, f32[72,128]{1,0:T(8,128)S(1)}, f32[72,128]{1,0:T(8,128)S(1)}, f32[512,256]{1,0:T(8,128)S(1)}, /*index=5*/f32[8,256]{1,0:T(8,128)S(1)}) custom-call(f32[520,128]{1,0:T(8,128)S(1)} %get-tuple-element.32.refs_0_.refs_4_, f32[520,128]{1,0:T(8,128)S(1)} %collective-permute-done.refs_1_.refs_5_, ...), custom_call_target="tpu_custom_call" | custom-call | flops 201326592 | bytes 1048576 | tf_op jit(solution)/shard_map/forward/pallas_call | solution.py:85
  12.7 2.9 %collective-permute-start.5 = (f32[72,128]{1,0:T(8,128)S(1)}, f32[72,128]{1,0:T(8,128)S(1)}, u32[]{:S(2)}, u32[]{:S(2)}) collective-permute-start(f32[72,128]{1,0:T(8,128)S(1)} %get-tuple-element.44), channel_id=1, source_target_pairs={{0,16},{4,20},{8,24},{12,28},{16,0},{20,4},{24,8},{28,12},{1,17},{... | collective-permute-start | bytes 110600 | tf_op jit(solution)/shard_map/ppermute | solution.py:39
  15.5 1.3 %collective-permute-start.6 = (f32[72,128]{1,0:T(8,128)S(1)}, f32[72,128]{1,0:T(8,128)S(1)}, u32[]{:S(2)}, u32[]{:S(2)}) collective-permute-start(f32[72,128]{1,0:T(8,128)S(1)} %get-tuple-element.45), channel_id=1, source_target_pairs={{0,24},{4,28},{8,16},{12,20},{16,8},{20,12},{24,0},{28,4},{1,25},{... | collective-permute-start | bytes 110600 | tf_op jit(solution)/shard_map/ppermute | solution.py:39
  16.9 0.0 collective-permute-done.2.refs_2_
  16.9 0.0 collective-permute-start.7
  16.9 0.0 collective-permute-done.3.refs_3_
  16.9 0.7 collective-permute-done.5.refs_6_
  17.6 3.7 %collective-permute-done.6.refs_7_ = f32[72,128]{1,0:T(8,128)S(1)} collective-permute-done((f32[72,128]{1,0:T(8,128)S(1)}, f32[72,128]{1,0:T(8,128)S(1)}, u32[]{:S(2)}, u32[]{:S(2)}) %collective-permute-start.6) | collective-permute-done | bytes 36896 | tf_op jit(solution)/shard_map/ppermute | solution.py:39
  21.3 0.3 merge.2.refs_8_
  21.6 1.0 %collective-permute-start.10 = (f32[136,128]{1,0:T(8,128)S(1)}, f32[136,128]{1,0:T(8,128)S(1)}, u32[]{:S(2)}, u32[]{:S(2)}) collective-permute-start(f32[136,128]{1,0:T(8,128)S(1)} %merge.2.refs_8_), channel_id=1, source_target_pairs={{0,16},{4,20},{8,24},{12,28},{16,0},{20,4},{24,8},{28,12},{1,17},{... | collective-permute-start | bytes 208904 | tf_op jit(solution)/shard_map/ppermute | solution.py:39
  22.6 1.3 %collective-permute-start.9 = (f32[136,128]{1,0:T(8,128)S(1)}, f32[136,128]{1,0:T(8,128)S(1)}, u32[]{:S(2)}, u32[]{:S(2)}) collective-permute-start(f32[136,128]{1,0:T(8,128)S(1)} %merge.2.refs_8_), channel_id=1, source_target_pairs={{0,24},{4,28},{8,16},{12,20},{16,8},{20,12},{24,0},{28,4},{1,25},{... | collective-permute-start | bytes 208904 | tf_op jit(solution)/shard_map/ppermute | solution.py:39
  23.9 1.2 %collective-permute-start.8 = (f32[136,128]{1,0:T(8,128)S(1)}, f32[136,128]{1,0:T(8,128)S(1)}, u32[]{:S(2)}, u32[]{:S(2)}) collective-permute-start(f32[136,128]{1,0:T(8,128)S(1)} %merge.2.refs_8_), channel_id=1, source_target_pairs={{0,8},{4,12},{8,0},{12,4},{16,24},{20,28},{24,16},{28,20},{1,9},{5... | collective-permute-start | bytes 208904 | tf_op jit(solution)/shard_map/ppermute | solution.py:39
  25.1 2.1 %collective-permute-done.10.refs_11_ = f32[136,128]{1,0:T(8,128)S(1)} collective-permute-done((f32[136,128]{1,0:T(8,128)S(1)}, f32[136,128]{1,0:T(8,128)S(1)}, u32[]{:S(2)}, u32[]{:S(2)}) %collective-permute-start.10) | collective-permute-done | bytes 69664 | tf_op jit(solution)/shard_map/ppermute | solution.py:39
  27.3 1.5 %collective-permute-done.9.refs_10_ = f32[136,128]{1,0:T(8,128)S(1)} collective-permute-done((f32[136,128]{1,0:T(8,128)S(1)}, f32[136,128]{1,0:T(8,128)S(1)}, u32[]{:S(2)}, u32[]{:S(2)}) %collective-permute-start.9) | collective-permute-done | bytes 69664 | tf_op jit(solution)/shard_map/ppermute | solution.py:39
  28.8 0.2 collective-permute-done.8.refs_9_
  29.0 1.4 %backward.2 = (f32[520,128]{1,0:T(8,128)S(1)}, f32[520,128]{1,0:T(8,128)S(1)}, f32[32,1,128]{2,1,0:T(1,128)S(1)}) custom-call(f32[512,256]{1,0:T(8,128)S(1)} %get-tuple-element.36.refs_0_, f32[512,256]{1,0:T(8,128)S(1)} %get-tuple-element.38.refs_1_, f32[8,256]{1,0:T(8,128)S(1)} %get-tuple-element.37.refs_3_.refs_2_, ...), custom_call_target="tpu_custom_call" | custom-call | flops 603979776 | bytes 1048576 | tf_op jit(solution)/shard_map/backward/pallas_call | solution.py:85
  30.4 10.9 %all_to_all.10.refs_6_ = f32[32,1,128]{2,1,0:T(1,128)S(1)} all-to-all(f32[32,1,128]{2,1,0:T(1,128)S(1)} %get-tuple-element.50), channel_id=1, replica_groups=mesh['page'=8,'query'=2,'head'=2] {'head','query','page'}, dimensions={0} | all-to-all | bytes 32768 | tf_op jit(solution)/shard_map/all_to_all | solution.py:642
  41.3 1.1 %update_forward.1 = (f32[1368,128]{1,0:T(8,128)S(1)}, f32[136,128]{1,0:T(8,128)S(1)}, f32[136,128]{1,0:T(8,128)S(1)}, f32[136,128]{1,0:T(8,128)S(1)}, f32[136,12...) custom-call(f32[520,128]{1,0:T(8,128)S(1)} %get-tuple-element.32.refs_0_.refs_4_, ...), custom_call_target="tpu_custom_call" | custom-call | flops 402653184 | bytes 1048576 | tf_op jit(solution)/shard_map/update_forward/pallas_call | solution.py:85
  42.4 0.6 collective-permute-start.17
  43.0 0.5 collective-permute-start.11
  43.5 2.4 %collective-permute-start.12 = (f32[136,128]{1,0:T(8,128)S(1)}, f32[136,128]{1,0:T(8,128)S(1)}, u32[]{:S(2)}, u32[]{:S(2)}) collective-permute-start(f32[136,128]{1,0:T(8,128)S(1)} %get-tuple-element.56), channel_id=1, source_target_pairs={{0,24},{4,28},{8,16},{12,20},{16,8},{20,12},{24,0},{28,4},{1,25},{... | collective-permute-start | bytes 208904 | tf_op jit(solution)/shard_map/ppermute | solution.py:39
  45.9 0.6 collective-permute-start.13
  46.5 4.5 %collective-permute-done.11.refs_3_ = f32[136,128]{1,0:T(8,128)S(1)} collective-permute-done((f32[136,128]{1,0:T(8,128)S(1)}, f32[136,128]{1,0:T(8,128)S(1)}, u32[]{:S(2)}, u32[]{:S(2)}) %collective-permute-start.11) | collective-permute-done | bytes 69664 | tf_op jit(solution)/shard_map/ppermute | solution.py:39
  51.0 0.2 collective-permute-done.13.refs_5_
  51.2 0.1 merge.3.refs_0_
  51.4 0.7 collective-permute-start.16
  52.0 3.0 %collective-permute-start.15 = (f32[136,128]{1,0:T(8,128)S(1)}, f32[136,128]{1,0:T(8,128)S(1)}, u32[]{:S(2)}, u32[]{:S(2)}) collective-permute-start(f32[136,128]{1,0:T(8,128)S(1)} %merge.3.refs_0_), channel_id=1, source_target_pairs={{0,24},{4,28},{8,16},{12,20},{16,8},{20,12},{24,0},{28,4},{1,25},{... | collective-permute-start | bytes 208904 | tf_op jit(solution)/shard_map/ppermute | solution.py:39
  55.1 3.1 %collective-permute-done.16.refs_3_ = f32[136,128]{1,0:T(8,128)S(1)} collective-permute-done((f32[136,128]{1,0:T(8,128)S(1)}, f32[136,128]{1,0:T(8,128)S(1)}, u32[]{:S(2)}, u32[]{:S(2)}) %collective-permute-start.16) | collective-permute-done | bytes 69664 | tf_op jit(solution)/shard_map/ppermute | solution.py:39
  58.2 0.8 %collective-permute-done.15.refs_2_ = f32[136,128]{1,0:T(8,128)S(1)} collective-permute-done((f32[136,128]{1,0:T(8,128)S(1)}, f32[136,128]{1,0:T(8,128)S(1)}, u32[]{:S(2)}, u32[]{:S(2)}) %collective-permute-start.15) | collective-permute-done | bytes 69664 | tf_op jit(solution)/shard_map/ppermute | solution.py:39
  59.0 0.7 collective-permute-done.14.refs_1_
  59.7 0.1 join.1.refs_5_
  59.7 1.7 %collective-permute-start.18 = (f32[136,512]{1,0:T(8,128)S(1)}, f32[136,512]{1,0:T(8,128)S(1)}, u32[]{:S(2)}, u32[]{:S(2)}) collective-permute-start(f32[136,512]{1,0:T(8,128)S(1)} %join.1.refs_5_), channel_id=1, source_target_pairs={{0,2},{2,0},{1,3},{3,1},{4,6},{6,4},{5,7},{7,5},{8,10},{10,8},{9,1... | collective-permute-start | bytes 835592 | tf_op jit(solution)/shard_map/ppermute | solution.py:39
  61.5 1.3 %backward.3 = (f32[520,128]{1,0:T(8,128)S(1)}, f32[520,128]{1,0:T(8,128)S(1)}, f32[32,1,128]{2,1,0:T(1,128)S(1)}) custom-call(f32[512,512]{1,0:T(8,128)S(1)} %get-tuple-element.51.refs_0_, f32[8,512]{1,0:T(8,128)S(1)} %get-tuple-element.52.refs_1_, f32[1368,128]{1,0:T(8,128)S(1)} %get-tuple-element.53.refs_2_, ...), custom_call_target="tpu_custom_call" | custom-call | flops 603979776 | bytes 1048576 | tf_op jit(solution)/shard_map/backward/pallas_call | solution.py:85
  62.7 8.9 %all_to_all.11.refs_0_ = f32[32,1,128]{2,1,0:T(1,128)S(1)} all-to-all(f32[32,1,128]{2,1,0:T(1,128)S(1)} %get-tuple-element.58), channel_id=1, replica_groups=mesh['page'=8,'query'=2,'head'=2] {'head','query','page'}, dimensions={0} | all-to-all | bytes 32768 | tf_op jit(solution)/shard_map/all_to_all | solution.py:642
  71.6 1.0 %page_update.2.refs_6_ = f32[1040,128]{1,0:T(8,128)S(1)} custom-call(f32[32,1,128]{2,1,0:T(1,128)S(1)} %all_to_all.11.refs_0_, f32[520,128]{1,0:T(8,128)S(1)} %get-tuple-element.60.refs_1_, f32[1368,128]{1,0:T(8,128)S(1)} %get-tuple-element.53.refs_2_, f32[1368,128]{1,0:T(8,128)S(1)} %collective-permute-done.17.refs_3_, ...), custom_call_target="tpu_custom_call" | custom-call | flops 301989888 | bytes 1048576 | tf_op jit(solution)/shard_map/page_update/pallas_call | solution.py:85
  72.6 0.1 collective-permute-start.19
  72.7 1.0 %page_update.3.refs_0_ = f32[1040,128]{1,0:T(8,128)S(1)} custom-call(f32[32,1,128]{2,1,0:T(1,128)S(1)} %all_to_all.11.refs_0_, f32[520,128]{1,0:T(8,128)S(1)} %get-tuple-element.59.refs_1_, f32[1368,128]{1,0:T(8,128)S(1)} %get-tuple-element.53.refs_2_, f32[1368,128]{1,0:T(8,128)S(1)} %collective-permute-done.17.refs_3_, ...), custom_call_target="tpu_custom_call" | custom-call | flops 301989888 | bytes 1048576 | tf_op jit(solution)/shard_map/page_update/pallas_call | solution.py:85
  73.7 0.9 %collective-permute-done.19.refs_1_ = f32[1040,128]{1,0:T(8,128)S(1)} collective-permute-done((f32[1040,128]{1,0:T(8,128)S(1)}, f32[1040,128]{1,0:T(8,128)S(1)}, u32[]{:S(2)}, u32[]{:S(2)}) %collective-permute-start.19) | collective-permute-done | bytes 532512 | tf_op jit(solution)/shard_map/ppermute | solution.py:39
  74.6 1.0 %unpack.1 = (f32[4,256,128]{2,1,0:T(8,128)}, f32[4,256,128]{2,1,0:T(8,128)}, f32[4,256]{1,0:T(4,128)}) custom-call(f32[1040,128]{1,0:T(8,128)S(1)} %page_update.3.refs_0_, f32[1040,128]{1,0:T(8,128)S(1)} %collective-permute-done.19.refs_1_), custom_call_target="tpu_custom_call" | custom-call | flops 1048576 | bytes 1048576 | tf_op jit(solution)/shard_map/unpack/pallas_call | solution.py:85
  (23 shorter events, 0.1 us)
Async XLA Ops:
  0.6 5.2 %copy-start.3 = (f32[4,256,128]{2,1,0:T(8,128)S(1)}, f32[4,256,128]{2,1,0:T(8,128)}, u32[]{:S(2)}) copy-start(f32[4,256,128]{2,1,0:T(8,128)} %refs_4_.3) | copy-start | bytes 1572868
  0.6 5.2 %copy-start.2 = (f32[4,256,128]{2,1,0:T(8,128)S(1)}, f32[4,256,128]{2,1,0:T(8,128)}, u32[]{:S(2)}) copy-start(f32[4,256,128]{2,1,0:T(8,128)} %refs_2_.3) | copy-start | bytes 1572868
  0.7 5.2 %copy-start.1 = (f32[4,256,128]{2,1,0:T(8,128)S(1)}, f32[4,256,128]{2,1,0:T(8,128)}, u32[]{:S(2)}) copy-start(f32[4,256,128]{2,1,0:T(8,128)} %refs_1_.3) | copy-start | bytes 1572868
  0.7 5.2 %copy-start = (f32[4,256,128]{2,1,0:T(8,128)S(1)}, f32[4,256,128]{2,1,0:T(8,128)}, u32[]{:S(2)}) copy-start(f32[4,256,128]{2,1,0:T(8,128)} %refs_0_.3) | copy-start | bytes 1572868
  0.7 5.2 %copy-start.5 = (f32[4,256]{1,0:T(4,128)S(1)}, f32[4,256]{1,0:T(4,128)}, u32[]{:S(2)}) copy-start(f32[4,256]{1,0:T(4,128)} %refs_3_.3) | copy-start | bytes 12292
  0.7 5.2 %copy-start.6 = (s32[4,256]{1,0:T(4,128)S(1)}, s32[4,256]{1,0:T(4,128)}, u32[]{:S(2)}) copy-start(s32[4,256]{1,0:T(4,128)} %refs_5_.3) | copy-start | bytes 12292
  2.7 3.2 %copy-start.7 = (s32[8]{0:T(128)S(1)}, s32[8]{0:T(128)}, u32[]{:S(2)}) copy-start(s32[8]{0:T(128)} %refs_6_.3) | copy-start | bytes 100
  2.7 3.8 %collective-permute-start = (f32[520,128]{1,0:T(8,128)}, f32[520,128]{1,0:T(8,128)S(1)}, u32[]{:S(2)}, u32[]{:S(2)}) collective-permute-start(f32[520,128]{1,0:T(8,128)} %get-tuple-element.33), channel_id=1, source_target_pairs={{0,4},{4,0},{8,12},{12,8},{16,20},{20,16},{24,28},{28,24},{1,5},{5... | collective-permute-start | bytes 798728 | tf_op jit(solution)/shard_map/ppermute | solution.py:39
  3.3 8.5 %collective-permute-start.1 = (f32[328,128]{1,0:T(8,128)}, f32[328,128]{1,0:T(8,128)S(1)}, u32[]{:S(2)}, u32[]{:S(2)}) collective-permute-start(f32[328,128]{1,0:T(8,128)} %get-tuple-element.35.refs_5_), channel_id=1, source_target_pairs={{0,2},{2,0},{1,3},{3,1},{4,6},{6,4},{5,7},{7,5},{8,10},{10,8},{9,1... | collective-permute-start | bytes 503816 | tf_op jit(solution)/shard_map/ppermute | solution.py:39
  7.5 9.4 %collective-permute-start.2 = (f32[72,128]{1,0:T(8,128)S(1)}, f32[72,128]{1,0:T(8,128)S(1)}, u32[]{:S(2)}, u32[]{:S(2)}) collective-permute-start(f32[72,128]{1,0:T(8,128)S(1)} %get-tuple-element.40), channel_id=1, source_target_pairs={{0,16},{4,20},{8,24},{12,28},{16,0},{20,4},{24,8},{28,12},{1,17},{... | collective-permute-start | bytes 110600 | tf_op jit(solution)/shard_map/ppermute | solution.py:39
  10.2 6.7 %collective-permute-start.3 = (f32[72,128]{1,0:T(8,128)S(1)}, f32[72,128]{1,0:T(8,128)S(1)}, u32[]{:S(2)}, u32[]{:S(2)}) collective-permute-start(f32[72,128]{1,0:T(8,128)S(1)} %get-tuple-element.41), channel_id=1, source_target_pairs={{0,24},{4,28},{8,16},{12,20},{16,8},{20,12},{24,0},{28,4},{1,25},{... | collective-permute-start | bytes 110600 | tf_op jit(solution)/shard_map/ppermute | solution.py:39
  11.5 5.4 %collective-permute-start.4 = (f32[72,128]{1,0:T(8,128)S(1)}, f32[72,128]{1,0:T(8,128)S(1)}, u32[]{:S(2)}, u32[]{:S(2)}) collective-permute-start(f32[72,128]{1,0:T(8,128)S(1)} %get-tuple-element.42), channel_id=1, source_target_pairs={{0,8},{4,12},{8,0},{12,4},{16,24},{20,28},{24,16},{28,20},{1,9},{5... | collective-permute-start | bytes 110600 | tf_op jit(solution)/shard_map/ppermute | solution.py:39
  12.7 4.9 %collective-permute-start.5 = (f32[72,128]{1,0:T(8,128)S(1)}, f32[72,128]{1,0:T(8,128)S(1)}, u32[]{:S(2)}, u32[]{:S(2)}) collective-permute-start(f32[72,128]{1,0:T(8,128)S(1)} %get-tuple-element.44), channel_id=1, source_target_pairs={{0,16},{4,20},{8,24},{12,28},{16,0},{20,4},{24,8},{28,12},{1,17},{... | collective-permute-start | bytes 110600 | tf_op jit(solution)/shard_map/ppermute | solution.py:39
  15.5 5.8 %collective-permute-start.6 = (f32[72,128]{1,0:T(8,128)S(1)}, f32[72,128]{1,0:T(8,128)S(1)}, u32[]{:S(2)}, u32[]{:S(2)}) collective-permute-start(f32[72,128]{1,0:T(8,128)S(1)} %get-tuple-element.45), channel_id=1, source_target_pairs={{0,24},{4,28},{8,16},{12,20},{16,8},{20,12},{24,0},{28,4},{1,25},{... | collective-permute-start | bytes 110600 | tf_op jit(solution)/shard_map/ppermute | solution.py:39
  16.9 4.4 %collective-permute-start.7 = (f32[72,128]{1,0:T(8,128)S(1)}, f32[72,128]{1,0:T(8,128)S(1)}, u32[]{:S(2)}, u32[]{:S(2)}) collective-permute-start(f32[72,128]{1,0:T(8,128)S(1)} %get-tuple-element.46), channel_id=1, source_target_pairs={{0,8},{4,12},{8,0},{12,4},{16,24},{20,28},{24,16},{28,20},{1,9},{5... | collective-permute-start | bytes 110600 | tf_op jit(solution)/shard_map/ppermute | solution.py:39
  21.6 5.7 %collective-permute-start.10 = (f32[136,128]{1,0:T(8,128)S(1)}, f32[136,128]{1,0:T(8,128)S(1)}, u32[]{:S(2)}, u32[]{:S(2)}) collective-permute-start(f32[136,128]{1,0:T(8,128)S(1)} %merge.2.refs_8_), channel_id=1, source_target_pairs={{0,16},{4,20},{8,24},{12,28},{16,0},{20,4},{24,8},{28,12},{1,17},{... | collective-permute-start | bytes 208904 | tf_op jit(solution)/shard_map/ppermute | solution.py:39
  22.6 6.2 %collective-permute-start.9 = (f32[136,128]{1,0:T(8,128)S(1)}, f32[136,128]{1,0:T(8,128)S(1)}, u32[]{:S(2)}, u32[]{:S(2)}) collective-permute-start(f32[136,128]{1,0:T(8,128)S(1)} %merge.2.refs_8_), channel_id=1, source_target_pairs={{0,24},{4,28},{8,16},{12,20},{16,8},{20,12},{24,0},{28,4},{1,25},{... | collective-permute-start | bytes 208904 | tf_op jit(solution)/shard_map/ppermute | solution.py:39
  23.9 5.1 %collective-permute-start.8 = (f32[136,128]{1,0:T(8,128)S(1)}, f32[136,128]{1,0:T(8,128)S(1)}, u32[]{:S(2)}, u32[]{:S(2)}) collective-permute-start(f32[136,128]{1,0:T(8,128)S(1)} %merge.2.refs_8_), channel_id=1, source_target_pairs={{0,8},{4,12},{8,0},{12,4},{16,24},{20,28},{24,16},{28,20},{1,9},{5... | collective-permute-start | bytes 208904 | tf_op jit(solution)/shard_map/ppermute | solution.py:39
  42.4 29.2 %collective-permute-start.17 = (f32[1368,128]{1,0:T(8,128)S(1)}, f32[1368,128]{1,0:T(8,128)S(1)}, u32[]{:S(2)}, u32[]{:S(2)}) collective-permute-start(f32[1368,128]{1,0:T(8,128)S(1)} %get-tuple-element.53.refs_2_), channel_id=1, source_target_pairs={{0,2},{2,0},{1,3},{3,1},{4,6},{6,4},{5,7},{7,5},{8,10},{10,8},{9,1... | collective-permute-start | bytes 2101256 | tf_op jit(solution)/shard_map/ppermute | solution.py:39
  43.0 8.0 %collective-permute-start.11 = (f32[136,128]{1,0:T(8,128)S(1)}, f32[136,128]{1,0:T(8,128)S(1)}, u32[]{:S(2)}, u32[]{:S(2)}) collective-permute-start(f32[136,128]{1,0:T(8,128)S(1)} %get-tuple-element.55), channel_id=1, source_target_pairs={{0,16},{4,20},{8,24},{12,28},{16,0},{20,4},{24,8},{28,12},{1,17},{... | collective-permute-start | bytes 208904 | tf_op jit(solution)/shard_map/ppermute | solution.py:39
  43.5 7.5 %collective-permute-start.12 = (f32[136,128]{1,0:T(8,128)S(1)}, f32[136,128]{1,0:T(8,128)S(1)}, u32[]{:S(2)}, u32[]{:S(2)}) collective-permute-start(f32[136,128]{1,0:T(8,128)S(1)} %get-tuple-element.56), channel_id=1, source_target_pairs={{0,24},{4,28},{8,16},{12,20},{16,8},{20,12},{24,0},{28,4},{1,25},{... | collective-permute-start | bytes 208904 | tf_op jit(solution)/shard_map/ppermute | solution.py:39
  45.9 5.3 %collective-permute-start.13 = (f32[136,128]{1,0:T(8,128)S(1)}, f32[136,128]{1,0:T(8,128)S(1)}, u32[]{:S(2)}, u32[]{:S(2)}) collective-permute-start(f32[136,128]{1,0:T(8,128)S(1)} %get-tuple-element.57), channel_id=1, source_target_pairs={{0,8},{4,12},{8,0},{12,4},{16,24},{20,28},{24,16},{28,20},{1,9},{5... | collective-permute-start | bytes 208904 | tf_op jit(solution)/shard_map/ppermute | solution.py:39
  51.4 6.8 %collective-permute-start.16 = (f32[136,128]{1,0:T(8,128)S(1)}, f32[136,128]{1,0:T(8,128)S(1)}, u32[]{:S(2)}, u32[]{:S(2)}) collective-permute-start(f32[136,128]{1,0:T(8,128)S(1)} %merge.3.refs_0_), channel_id=1, source_target_pairs={{0,16},{4,20},{8,24},{12,28},{16,0},{20,4},{24,8},{28,12},{1,17},{... | collective-permute-start | bytes 208904 | tf_op jit(solution)/shard_map/ppermute | solution.py:39
  52.0 7.0 %collective-permute-start.15 = (f32[136,128]{1,0:T(8,128)S(1)}, f32[136,128]{1,0:T(8,128)S(1)}, u32[]{:S(2)}, u32[]{:S(2)}) collective-permute-start(f32[136,128]{1,0:T(8,128)S(1)} %merge.3.refs_0_), channel_id=1, source_target_pairs={{0,24},{4,28},{8,16},{12,20},{16,8},{20,12},{24,0},{28,4},{1,25},{... | collective-permute-start | bytes 208904 | tf_op jit(solution)/shard_map/ppermute | solution.py:39
  55.1 4.6 %collective-permute-start.14 = (f32[136,128]{1,0:T(8,128)S(1)}, f32[136,128]{1,0:T(8,128)S(1)}, u32[]{:S(2)}, u32[]{:S(2)}) collective-permute-start(f32[136,128]{1,0:T(8,128)S(1)} %merge.3.refs_0_), channel_id=1, source_target_pairs={{0,8},{4,12},{8,0},{12,4},{16,24},{20,28},{24,16},{28,20},{1,9},{5... | collective-permute-start | bytes 208904 | tf_op jit(solution)/shard_map/ppermute | solution.py:39
  59.7 11.9 %collective-permute-start.18 = (f32[136,512]{1,0:T(8,128)S(1)}, f32[136,512]{1,0:T(8,128)S(1)}, u32[]{:S(2)}, u32[]{:S(2)}) collective-permute-start(f32[136,512]{1,0:T(8,128)S(1)} %join.1.refs_5_), channel_id=1, source_target_pairs={{0,2},{2,0},{1,3},{3,1},{4,6},{6,4},{5,7},{7,5},{8,10},{10,8},{9,1... | collective-permute-start | bytes 835592 | tf_op jit(solution)/shard_map/ppermute | solution.py:39
  61.5 10.2 %copy-start.4 = (f32[328,128]{1,0:T(8,128)S(1)}, f32[328,128]{1,0:T(8,128)}, u32[]{:S(2)}) copy-start(f32[328,128]{1,0:T(8,128)} %get-tuple-element.35.refs_5_) | copy-start | bytes 503812
  72.6 2.0 %collective-permute-start.19 = (f32[1040,128]{1,0:T(8,128)S(1)}, f32[1040,128]{1,0:T(8,128)S(1)}, u32[]{:S(2)}, u32[]{:S(2)}) collective-permute-start(f32[1040,128]{1,0:T(8,128)S(1)} %page_update.2.refs_6_), channel_id=1, source_target_pairs={{0,4},{4,0},{8,12},{12,8},{16,20},{20,16},{24,28},{28,24},{1,5},{5... | collective-permute-start | bytes 1597448 | tf_op jit(solution)/shard_map/ppermute | solution.py:39

commit v27 on v26

--- a/solution.py
+++ b/solution.py
@@ -84,7 +84,10 @@
 
     return pl.pallas_call(
         without_after,
-        out_shape=[jax.ShapeDtypeStruct(shape, jnp.float32) for shape in out_shapes],
+        out_shape=[
+            shape if hasattr(shape, "dtype") else jax.ShapeDtypeStruct(shape, jnp.float32)
+            for shape in out_shapes
+        ],
         in_specs=[pl.BlockSpec(memory_space=space) for space in spaces],
         out_specs=[pl.BlockSpec(memory_space=pltpu.VMEM) for _ in out_shapes],
         scratch_shapes=scratch,
@@ -340,9 +343,17 @@
             [tail_as_row(ref, part_rows + piece, pos_rows) for ref in query_refs], 1
         )
 
-    def forward(state_refs, query_refs, chunk_outs, weights_out, max_out, chunks):
+    def split_body(*refs):
+        query_refs, (halves_out, positions_out) = refs[:query_devices], refs[query_devices:]
+        halves_out[...] = jnp.concatenate(read_queries(query_refs), axis=1)
+        positions_out[...] = jnp.broadcast_to(read_positions(query_refs), (TAIL, query_rows))
+
+    def read_halves(ref):
+        return ref[:, :width], ref[:, width:]
+
+    def forward(state_refs, split_refs, chunk_outs, weights_out, max_out, chunks):
         rank, _, _ = places()
-        all_queries, positions = read_queries(query_refs), read_positions(query_refs)
+        all_queries, positions = read_halves(split_refs[0]), split_refs[1][0:1, :]
         all_scores, all_visible = [], []
         for at, ref in enumerate(state_refs):
             scores, visible = page_scores(ref, all_queries, positions)
@@ -427,17 +438,17 @@
 
     def next_body(*refs):
         state_refs, refs = refs[:2], refs[2:]
-        query_refs, refs = refs[:query_devices], refs[query_devices:]
+        split_refs, (pack_ref, *refs) = refs[:2], refs[2:]
         grad_refs, refs = refs[:2], refs[2:]
         tile_refs, refs = refs[: len(tiles)], refs[len(tiles) :]
-        refs[0][CORES * packed_rows :, :] = query_refs[0][...]
+        refs[0][CORES * packed_rows :, :] = pack_ref[...]
         state_outs, refs = parts_of(refs[:1]), refs[1:]
         chunk_outs, refs = refs[:ranks], refs[ranks:]
         sizes = step_sizes(tile_refs)
         for at in range(2):
             state = read_pack(state_refs[at])
             store_pack(state_outs[at], updated(state, read_pack(grad_refs[at]), sizes))
-        forward(state_outs, query_refs, chunk_outs, *refs)
+        forward(state_outs, split_refs, chunk_outs, *refs)
 
     def merged_chunk(query_refs, sums, maxima, totals, out):
         targets = jnp.concatenate(
@@ -516,12 +527,12 @@
         weights_refs, refs = refs[: len(weights)], refs[len(weights) :]
         max_refs, refs = refs[: len(weights)], refs[len(weights) :]
         state_refs, refs = parts_of(refs[: len(states)]), refs[len(states) :]
-        query_refs, refs = refs[:query_devices], refs[query_devices:]
+        query_refs, refs = refs[: len(head_queries)], refs[len(head_queries) :]
         merged_refs, refs = refs[: len(all_merged)], refs[len(all_merged) :]
         grad_outs, (squares_out, *scratch) = refs[:2], refs[2:]
         if len(states) < CORES:
             joined = merged_refs[0][...]
-            all_queries = read_queries(query_refs)
+            all_queries = read_halves(query_refs[0])
         else:
             chunks = read_chunks(merged_refs, *scratch)
             joined = jnp.concatenate(
@@ -602,7 +613,7 @@
                 [(CORES * packed_rows + query_shape[0], width)] + forward_shapes,
                 "update_forward",
                 2 * matmul_cost,
-                states + query_parts + grads + tiles,
+                states + split_queries + [own_queries] + grads + tiles,
                 chunk_scratch,
             )
             states, weights, maxima = [new_state], [part_weights], [part_max]
@@ -629,13 +640,27 @@
             all_joined = [
                 to_device(all_merged[0], query=turn) for turn in range(query_devices)
             ]
+        before_backward = []
+        if repeat == 0:
+            half_shape = jax.ShapeDtypeStruct((query_rows, 2 * width), jnp.bfloat16)
+            split_queries = call(
+                split_body,
+                [half_shape, (TAIL, query_rows)],
+                "split_queries",
+                2**20,
+                query_parts,
+            )
+            split_queries = list(split_queries)
+            before_backward = split_queries[1:]
+        head_queries = split_queries[:1] if repeat else query_parts
         own_grad, mate_grad, squares = call(
             backward_body,
             packed_shapes + [(devices, 1, width)],
             "backward",
             3 * matmul_cost,
-            weights + maxima + states + query_parts + list(all_merged),
+            weights + maxima + states + head_queries + list(all_merged),
             scratch=() if last else chunk_scratch,
+            after=before_backward,
         )
         grads = [own_grad, mate_grad]
         tiles = [

time: 75.8 us -> 75.9 us (level)
    pallas_call x13 -> x14, Pallas kernels: 11.8 us -> 11.9 us  [call(): pl.pallas_call(without_after, out_shape=[shape if hasattr(shape, 'dtype')...]
where the time goes in v27:
time: 75.9 us; the launch traced here: 75.7 us
  starting transfers between devices  24.7 us (33%)
  blocking collectives  19.8 us (26%)
  waiting for transfers between devices  18.4 us (24%)
  Pallas kernels  11.9 us (16%)
  between operations  0.83 us (1%)
    ppermute x20, starting transfers between devices, exchange(): return lax.ppermute(value, axes, pairs)  24.7 us
    all_to_all x2, blocking collectives, direct_per_device(): lax.all_to_all(squares, ('head', 'query', 'page'), split_axis=0, concat_a...  19.8 us
    ppermute x20, waiting for transfers between devices, exchange(): return lax.ppermute(value, axes, pairs)  18.4 us
    pallas_call x14, Pallas kernels, call(): pl.pallas_call(without_after, out_shape=[shape if hasattr(shape, 'dtype')...  11.9 us
  transfers between devices with their start and end apart: 20, of which 11 were waited for; matrix products, arithmetic and copies ran while one was open for 0% of the time, Pallas kernels for 7%

profile of v27, /device:TPU:0, one launch (start us, length us, event | category | flops | bytes accessed | tf_op | source)
XLA Modules:
  0.0 75.7 jit_solution(6476141055574044179)
XLA Ops:
  0.7 2.0 %pack.1 = (f32[520,128]{1,0:T(8,128)}, f32[328,128]{1,0:T(8,128)}) custom-call(f32[4,256,128]{2,1,0:T(8,128)} %refs_0_.3, f32[4,256,128]{2,1,0:T(8,128)} %refs_1_.3, f32[4,256,128]{2,1,0:T(8,128)} %refs_2_.3, f32[4,256]{1,0:T(4,128)} %refs_3_.3, f32[4,256,128]{2,1,0:T(8,128)} %refs_4_.3, s32[4,256]{1,0:T(4,128)} %refs_5_.3, s32[8]{0:T(128)} %refs_6_.3), custom_call_target="tpu_custom_call" | custom-call | flops 1048576 | bytes 1048576 | tf_op jit(solution)/shard_map/pack/pallas_call | solution.py:85
  2.7 0.0 copy-start.7
  2.7 0.5 collective-permute-start
  3.3 2.6 %collective-permute-start.1 = (f32[328,128]{1,0:T(8,128)}, f32[328,128]{1,0:T(8,128)S(1)}, u32[]{:S(2)}, u32[]{:S(2)}) collective-permute-start(f32[328,128]{1,0:T(8,128)} %get-tuple-element.37.refs_5_), channel_id=1, source_target_pairs={{0,2},{2,0},{1,3},{3,1},{4,6},{6,4},{5,7},{7,5},{8,10},{10,8},{9,1... | collective-permute-start | bytes 503816 | tf_op jit(solution)/shard_map/ppermute | solution.py:39
  5.9 0.7 own.1
  6.6 0.9 %forward.2 = (f32[72,128]{1,0:T(8,128)S(1)}, f32[72,128]{1,0:T(8,128)S(1)}, f32[72,128]{1,0:T(8,128)S(1)}, f32[72,128]{1,0:T(8,128)S(1)}, f32[512,256]{1,0:T(8,128)S(1)}, /*index=5*/f32[8,256]{1,0:T(8,128)S(1)}) custom-call(f32[520,128]{1,0:T(8,128)S(1)} %get-tuple-element.34.refs_0_.refs_4_, f32[520,128]{1,0:T(8,128)S(1)} %collective-permute-done.refs_1_.refs_5_, ...), custom_call_target="tpu_custom_call" | custom-call | flops 201326592 | bytes 1048576 | tf_op jit(solution)/shard_map/forward/pallas_call | solution.py:85
  7.5 2.7 %collective-permute-start.2 = (f32[72,128]{1,0:T(8,128)S(1)}, f32[72,128]{1,0:T(8,128)S(1)}, u32[]{:S(2)}, u32[]{:S(2)}) collective-permute-start(f32[72,128]{1,0:T(8,128)S(1)} %get-tuple-element.44), channel_id=1, source_target_pairs={{0,16},{4,20},{8,24},{12,28},{16,0},{20,4},{24,8},{28,12},{1,17},{... | collective-permute-start | bytes 110600 | tf_op jit(solution)/shard_map/ppermute | solution.py:39
  10.2 1.3 %collective-permute-start.3 = (f32[72,128]{1,0:T(8,128)S(1)}, f32[72,128]{1,0:T(8,128)S(1)}, u32[]{:S(2)}, u32[]{:S(2)}) collective-permute-start(f32[72,128]{1,0:T(8,128)S(1)} %get-tuple-element.45), channel_id=1, source_target_pairs={{0,24},{4,28},{8,16},{12,20},{16,8},{20,12},{24,0},{28,4},{1,25},{... | collective-permute-start | bytes 110600 | tf_op jit(solution)/shard_map/ppermute | solution.py:39
  11.5 0.2 collective-permute-start.4
  11.7 0.0 collective-permute-done.1.refs_1_.refs_2_.refs_7_
  11.7 0.9 %forward.3 = (f32[72,128]{1,0:T(8,128)S(1)}, f32[72,128]{1,0:T(8,128)S(1)}, f32[72,128]{1,0:T(8,128)S(1)}, f32[72,128]{1,0:T(8,128)S(1)}, f32[512,256]{1,0:T(8,128)S(1)}, /*index=5*/f32[8,256]{1,0:T(8,128)S(1)}) custom-call(f32[520,128]{1,0:T(8,128)S(1)} %get-tuple-element.34.refs_0_.refs_4_, f32[520,128]{1,0:T(8,128)S(1)} %collective-permute-done.refs_1_.refs_5_, ...), custom_call_target="tpu_custom_call" | custom-call | flops 201326592 | bytes 1048576 | tf_op jit(solution)/shard_map/forward/pallas_call | solution.py:85
  12.7 2.9 %collective-permute-start.5 = (f32[72,128]{1,0:T(8,128)S(1)}, f32[72,128]{1,0:T(8,128)S(1)}, u32[]{:S(2)}, u32[]{:S(2)}) collective-permute-start(f32[72,128]{1,0:T(8,128)S(1)} %get-tuple-element.48), channel_id=1, source_target_pairs={{0,16},{4,20},{8,24},{12,28},{16,0},{20,4},{24,8},{28,12},{1,17},{... | collective-permute-start | bytes 110600 | tf_op jit(solution)/shard_map/ppermute | solution.py:39
  15.5 1.3 %collective-permute-start.6 = (f32[72,128]{1,0:T(8,128)S(1)}, f32[72,128]{1,0:T(8,128)S(1)}, u32[]{:S(2)}, u32[]{:S(2)}) collective-permute-start(f32[72,128]{1,0:T(8,128)S(1)} %get-tuple-element.49), channel_id=1, source_target_pairs={{0,24},{4,28},{8,16},{12,20},{16,8},{20,12},{24,0},{28,4},{1,25},{... | collective-permute-start | bytes 110600 | tf_op jit(solution)/shard_map/ppermute | solution.py:39
  16.9 0.0 collective-permute-done.2.refs_2_
  16.9 0.7 collective-permute-done.5.refs_6_
  17.6 3.7 %collective-permute-done.6.refs_7_ = f32[72,128]{1,0:T(8,128)S(1)} collective-permute-done((f32[72,128]{1,0:T(8,128)S(1)}, f32[72,128]{1,0:T(8,128)S(1)}, u32[]{:S(2)}, u32[]{:S(2)}) %collective-permute-start.6) | collective-permute-done | bytes 36896 | tf_op jit(solution)/shard_map/ppermute | solution.py:39
  21.3 0.3 merge.2.refs_8_
  21.6 1.0 %collective-permute-start.10 = (f32[136,128]{1,0:T(8,128)S(1)}, f32[136,128]{1,0:T(8,128)S(1)}, u32[]{:S(2)}, u32[]{:S(2)}) collective-permute-start(f32[136,128]{1,0:T(8,128)S(1)} %merge.2.refs_8_), channel_id=1, source_target_pairs={{0,16},{4,20},{8,24},{12,28},{16,0},{20,4},{24,8},{28,12},{1,17},{... | collective-permute-start | bytes 208904 | tf_op jit(solution)/shard_map/ppermute | solution.py:39
  22.6 1.3 %collective-permute-start.9 = (f32[136,128]{1,0:T(8,128)S(1)}, f32[136,128]{1,0:T(8,128)S(1)}, u32[]{:S(2)}, u32[]{:S(2)}) collective-permute-start(f32[136,128]{1,0:T(8,128)S(1)} %merge.2.refs_8_), channel_id=1, source_target_pairs={{0,24},{4,28},{8,16},{12,20},{16,8},{20,12},{24,0},{28,4},{1,25},{... | collective-permute-start | bytes 208904 | tf_op jit(solution)/shard_map/ppermute | solution.py:39
  23.9 1.2 %collective-permute-start.8 = (f32[136,128]{1,0:T(8,128)S(1)}, f32[136,128]{1,0:T(8,128)S(1)}, u32[]{:S(2)}, u32[]{:S(2)}) collective-permute-start(f32[136,128]{1,0:T(8,128)S(1)} %merge.2.refs_8_), channel_id=1, source_target_pairs={{0,8},{4,12},{8,0},{12,4},{16,24},{20,28},{24,16},{28,20},{1,9},{5... | collective-permute-start | bytes 208904 | tf_op jit(solution)/shard_map/ppermute | solution.py:39
  25.1 0.1 split_queries.1
  25.2 2.1 %collective-permute-done.10.refs_11_ = f32[136,128]{1,0:T(8,128)S(1)} collective-permute-done((f32[136,128]{1,0:T(8,128)S(1)}, f32[136,128]{1,0:T(8,128)S(1)}, u32[]{:S(2)}, u32[]{:S(2)}) %collective-permute-start.10) | collective-permute-done | bytes 69664 | tf_op jit(solution)/shard_map/ppermute | solution.py:39
  27.3 1.5 %collective-permute-done.9.refs_10_ = f32[136,128]{1,0:T(8,128)S(1)} collective-permute-done((f32[136,128]{1,0:T(8,128)S(1)}, f32[136,128]{1,0:T(8,128)S(1)}, u32[]{:S(2)}, u32[]{:S(2)}) %collective-permute-start.9) | collective-permute-done | bytes 69664 | tf_op jit(solution)/shard_map/ppermute | solution.py:39
  28.8 0.2 collective-permute-done.8.refs_9_
  29.0 1.4 %backward.2 = (f32[520,128]{1,0:T(8,128)S(1)}, f32[520,128]{1,0:T(8,128)S(1)}, f32[32,1,128]{2,1,0:T(1,128)S(1)}) custom-call(f32[512,256]{1,0:T(8,128)S(1)} %get-tuple-element.40.refs_0_, f32[512,256]{1,0:T(8,128)S(1)} %get-tuple-element.42.refs_1_, f32[8,256]{1,0:T(8,128)S(1)} %get-tuple-element.41.refs_3_.refs_2_, ...), custom_call_target="tpu_custom_call" | custom-call | flops 603979776 | bytes 1048576 | tf_op jit(solution)/shard_map/backward/pallas_call | solution.py:85
  30.4 10.9 %all_to_all.10.refs_7_ = f32[32,1,128]{2,1,0:T(1,128)S(1)} all-to-all(f32[32,1,128]{2,1,0:T(1,128)S(1)} %get-tuple-element.54), channel_id=1, replica_groups=mesh['page'=8,'query'=2,'head'=2] {'head','query','page'}, dimensions={0} | all-to-all | bytes 32768 | tf_op jit(solution)/shard_map/all_to_all | solution.py:667
  41.3 1.1 %update_forward.1 = (f32[1368,128]{1,0:T(8,128)S(1)}, f32[136,128]{1,0:T(8,128)S(1)}, f32[136,128]{1,0:T(8,128)S(1)}, f32[136,128]{1,0:T(8,128)S(1)}, f32[136,12...) custom-call(f32[520,128]{1,0:T(8,128)S(1)} %get-tuple-element.34.refs_0_.refs_4_, ...), custom_call_target="tpu_custom_call" | custom-call | flops 402653184 | bytes 1048576 | tf_op jit(solution)/shard_map/update_forward/pallas_call | solution.py:85
  42.4 0.6 collective-permute-start.17
  43.0 0.5 collective-permute-start.11
  43.5 2.4 %collective-permute-start.12 = (f32[136,128]{1,0:T(8,128)S(1)}, f32[136,128]{1,0:T(8,128)S(1)}, u32[]{:S(2)}, u32[]{:S(2)}) collective-permute-start(f32[136,128]{1,0:T(8,128)S(1)} %get-tuple-element.60), channel_id=1, source_target_pairs={{0,24},{4,28},{8,16},{12,20},{16,8},{20,12},{24,0},{28,4},{1,25},{... | collective-permute-start | bytes 208904 | tf_op jit(solution)/shard_map/ppermute | solution.py:39
  45.9 0.6 collective-permute-start.13
  46.5 4.5 %collective-permute-done.11.refs_3_ = f32[136,128]{1,0:T(8,128)S(1)} collective-permute-done((f32[136,128]{1,0:T(8,128)S(1)}, f32[136,128]{1,0:T(8,128)S(1)}, u32[]{:S(2)}, u32[]{:S(2)}) %collective-permute-start.11) | collective-permute-done | bytes 69664 | tf_op jit(solution)/shard_map/ppermute | solution.py:39
  51.0 0.2 collective-permute-done.13.refs_5_
  51.3 0.1 merge.3.refs_0_
  51.4 0.7 collective-permute-start.16
  52.0 3.0 %collective-permute-start.15 = (f32[136,128]{1,0:T(8,128)S(1)}, f32[136,128]{1,0:T(8,128)S(1)}, u32[]{:S(2)}, u32[]{:S(2)}) collective-permute-start(f32[136,128]{1,0:T(8,128)S(1)} %merge.3.refs_0_), channel_id=1, source_target_pairs={{0,24},{4,28},{8,16},{12,20},{16,8},{20,12},{24,0},{28,4},{1,25},{... | collective-permute-start | bytes 208904 | tf_op jit(solution)/shard_map/ppermute | solution.py:39
  55.1 3.1 %collective-permute-done.16.refs_3_ = f32[136,128]{1,0:T(8,128)S(1)} collective-permute-done((f32[136,128]{1,0:T(8,128)S(1)}, f32[136,128]{1,0:T(8,128)S(1)}, u32[]{:S(2)}, u32[]{:S(2)}) %collective-permute-start.16) | collective-permute-done | bytes 69664 | tf_op jit(solution)/shard_map/ppermute | solution.py:39
  58.2 0.8 %collective-permute-done.15.refs_2_ = f32[136,128]{1,0:T(8,128)S(1)} collective-permute-done((f32[136,128]{1,0:T(8,128)S(1)}, f32[136,128]{1,0:T(8,128)S(1)}, u32[]{:S(2)}, u32[]{:S(2)}) %collective-permute-start.15) | collective-permute-done | bytes 69664 | tf_op jit(solution)/shard_map/ppermute | solution.py:39
  59.0 0.7 collective-permute-done.14.refs_1_
  59.7 0.1 join.1.refs_4_
  59.8 1.7 %collective-permute-start.18 = (f32[136,512]{1,0:T(8,128)S(1)}, f32[136,512]{1,0:T(8,128)S(1)}, u32[]{:S(2)}, u32[]{:S(2)}) collective-permute-start(f32[136,512]{1,0:T(8,128)S(1)} %join.1.refs_4_), channel_id=1, source_target_pairs={{0,2},{2,0},{1,3},{3,1},{4,6},{6,4},{5,7},{7,5},{8,10},{10,8},{9,1... | collective-permute-start | bytes 835592 | tf_op jit(solution)/shard_map/ppermute | solution.py:39
  61.5 1.3 %backward.3 = (f32[520,128]{1,0:T(8,128)S(1)}, f32[520,128]{1,0:T(8,128)S(1)}, f32[32,1,128]{2,1,0:T(1,128)S(1)}) custom-call(f32[512,512]{1,0:T(8,128)S(1)} %get-tuple-element.55.refs_0_, f32[8,512]{1,0:T(8,128)S(1)} %get-tuple-element.56.refs_1_, f32[1368,128]{1,0:T(8,128)S(1)} %get-tuple-element.57.refs_2_, ...), custom_call_target="tpu_custom_call" | custom-call | flops 603979776 | bytes 1048576 | tf_op jit(solution)/shard_map/backward/pallas_call | solution.py:85
  62.7 8.9 %all_to_all.11.refs_0_ = f32[32,1,128]{2,1,0:T(1,128)S(1)} all-to-all(f32[32,1,128]{2,1,0:T(1,128)S(1)} %get-tuple-element.62), channel_id=1, replica_groups=mesh['page'=8,'query'=2,'head'=2] {'head','query','page'}, dimensions={0} | all-to-all | bytes 32768 | tf_op jit(solution)/shard_map/all_to_all | solution.py:667
  71.6 1.0 %page_update.2.refs_6_ = f32[1040,128]{1,0:T(8,128)S(1)} custom-call(f32[32,1,128]{2,1,0:T(1,128)S(1)} %all_to_all.11.refs_0_, f32[520,128]{1,0:T(8,128)S(1)} %get-tuple-element.64.refs_1_, f32[1368,128]{1,0:T(8,128)S(1)} %get-tuple-element.57.refs_2_, f32[1368,128]{1,0:T(8,128)S(1)} %collective-permute-done.17.refs_3_, ...), custom_call_target="tpu_custom_call" | custom-call | flops 301989888 | bytes 1048576 | tf_op jit(solution)/shard_map/page_update/pallas_call | solution.py:85
  72.7 0.1 collective-permute-start.19
  72.7 1.0 %page_update.3.refs_0_ = f32[1040,128]{1,0:T(8,128)S(1)} custom-call(f32[32,1,128]{2,1,0:T(1,128)S(1)} %all_to_all.11.refs_0_, f32[520,128]{1,0:T(8,128)S(1)} %get-tuple-element.63.refs_1_, f32[1368,128]{1,0:T(8,128)S(1)} %get-tuple-element.57.refs_2_, f32[1368,128]{1,0:T(8,128)S(1)} %collective-permute-done.17.refs_3_, ...), custom_call_target="tpu_custom_call" | custom-call | flops 301989888 | bytes 1048576 | tf_op jit(solution)/shard_map/page_update/pallas_call | solution.py:85
  73.8 0.9 %collective-permute-done.19.refs_1_ = f32[1040,128]{1,0:T(8,128)S(1)} collective-permute-done((f32[1040,128]{1,0:T(8,128)S(1)}, f32[1040,128]{1,0:T(8,128)S(1)}, u32[]{:S(2)}, u32[]{:S(2)}) %collective-permute-start.19) | collective-permute-done | bytes 532512 | tf_op jit(solution)/shard_map/ppermute | solution.py:39
  74.6 1.0 %unpack.1 = (f32[4,256,128]{2,1,0:T(8,128)}, f32[4,256,128]{2,1,0:T(8,128)}, f32[4,256]{1,0:T(4,128)}) custom-call(f32[1040,128]{1,0:T(8,128)S(1)} %page_update.3.refs_0_, f32[1040,128]{1,0:T(8,128)S(1)} %collective-permute-done.19.refs_1_), custom_call_target="tpu_custom_call" | custom-call | flops 1048576 | bytes 1048576 | tf_op jit(solution)/shard_map/unpack/pallas_call | solution.py:85
  (24 shorter events, 0.1 us)
Async XLA Ops:
  0.6 5.2 %copy-start.3 = (f32[4,256,128]{2,1,0:T(8,128)S(1)}, f32[4,256,128]{2,1,0:T(8,128)}, u32[]{:S(2)}) copy-start(f32[4,256,128]{2,1,0:T(8,128)} %refs_4_.3) | copy-start | bytes 1572868
  0.6 5.2 %copy-start.2 = (f32[4,256,128]{2,1,0:T(8,128)S(1)}, f32[4,256,128]{2,1,0:T(8,128)}, u32[]{:S(2)}) copy-start(f32[4,256,128]{2,1,0:T(8,128)} %refs_2_.3) | copy-start | bytes 1572868
  0.7 5.2 %copy-start.1 = (f32[4,256,128]{2,1,0:T(8,128)S(1)}, f32[4,256,128]{2,1,0:T(8,128)}, u32[]{:S(2)}) copy-start(f32[4,256,128]{2,1,0:T(8,128)} %refs_1_.3) | copy-start | bytes 1572868
  0.7 5.2 %copy-start = (f32[4,256,128]{2,1,0:T(8,128)S(1)}, f32[4,256,128]{2,1,0:T(8,128)}, u32[]{:S(2)}) copy-start(f32[4,256,128]{2,1,0:T(8,128)} %refs_0_.3) | copy-start | bytes 1572868
  0.7 5.2 %copy-start.5 = (f32[4,256]{1,0:T(4,128)S(1)}, f32[4,256]{1,0:T(4,128)}, u32[]{:S(2)}) copy-start(f32[4,256]{1,0:T(4,128)} %refs_3_.3) | copy-start | bytes 12292
  0.7 5.2 %copy-start.6 = (s32[4,256]{1,0:T(4,128)S(1)}, s32[4,256]{1,0:T(4,128)}, u32[]{:S(2)}) copy-start(s32[4,256]{1,0:T(4,128)} %refs_5_.3) | copy-start | bytes 12292
  2.7 3.2 %copy-start.7 = (s32[8]{0:T(128)S(1)}, s32[8]{0:T(128)}, u32[]{:S(2)}) copy-start(s32[8]{0:T(128)} %refs_6_.3) | copy-start | bytes 100
  2.7 3.8 %collective-permute-start = (f32[520,128]{1,0:T(8,128)}, f32[520,128]{1,0:T(8,128)S(1)}, u32[]{:S(2)}, u32[]{:S(2)}) collective-permute-start(f32[520,128]{1,0:T(8,128)} %get-tuple-element.35), channel_id=1, source_target_pairs={{0,4},{4,0},{8,12},{12,8},{16,20},{20,16},{24,28},{28,24},{1,5},{5... | collective-permute-start | bytes 798728 | tf_op jit(solution)/shard_map/ppermute | solution.py:39
  3.3 8.5 %collective-permute-start.1 = (f32[328,128]{1,0:T(8,128)}, f32[328,128]{1,0:T(8,128)S(1)}, u32[]{:S(2)}, u32[]{:S(2)}) collective-permute-start(f32[328,128]{1,0:T(8,128)} %get-tuple-element.37.refs_5_), channel_id=1, source_target_pairs={{0,2},{2,0},{1,3},{3,1},{4,6},{6,4},{5,7},{7,5},{8,10},{10,8},{9,1... | collective-permute-start | bytes 503816 | tf_op jit(solution)/shard_map/ppermute | solution.py:39
  7.5 9.4 %collective-permute-start.2 = (f32[72,128]{1,0:T(8,128)S(1)}, f32[72,128]{1,0:T(8,128)S(1)}, u32[]{:S(2)}, u32[]{:S(2)}) collective-permute-start(f32[72,128]{1,0:T(8,128)S(1)} %get-tuple-element.44), channel_id=1, source_target_pairs={{0,16},{4,20},{8,24},{12,28},{16,0},{20,4},{24,8},{28,12},{1,17},{... | collective-permute-start | bytes 110600 | tf_op jit(solution)/shard_map/ppermute | solution.py:39
  10.2 6.7 %collective-permute-start.3 = (f32[72,128]{1,0:T(8,128)S(1)}, f32[72,128]{1,0:T(8,128)S(1)}, u32[]{:S(2)}, u32[]{:S(2)}) collective-permute-start(f32[72,128]{1,0:T(8,128)S(1)} %get-tuple-element.45), channel_id=1, source_target_pairs={{0,24},{4,28},{8,16},{12,20},{16,8},{20,12},{24,0},{28,4},{1,25},{... | collective-permute-start | bytes 110600 | tf_op jit(solution)/shard_map/ppermute | solution.py:39
  11.5 5.4 %collective-permute-start.4 = (f32[72,128]{1,0:T(8,128)S(1)}, f32[72,128]{1,0:T(8,128)S(1)}, u32[]{:S(2)}, u32[]{:S(2)}) collective-permute-start(f32[72,128]{1,0:T(8,128)S(1)} %get-tuple-element.46), channel_id=1, source_target_pairs={{0,8},{4,12},{8,0},{12,4},{16,24},{20,28},{24,16},{28,20},{1,9},{5... | collective-permute-start | bytes 110600 | tf_op jit(solution)/shard_map/ppermute | solution.py:39
  12.7 4.9 %collective-permute-start.5 = (f32[72,128]{1,0:T(8,128)S(1)}, f32[72,128]{1,0:T(8,128)S(1)}, u32[]{:S(2)}, u32[]{:S(2)}) collective-permute-start(f32[72,128]{1,0:T(8,128)S(1)} %get-tuple-element.48), channel_id=1, source_target_pairs={{0,16},{4,20},{8,24},{12,28},{16,0},{20,4},{24,8},{28,12},{1,17},{... | collective-permute-start | bytes 110600 | tf_op jit(solution)/shard_map/ppermute | solution.py:39
  15.5 5.8 %collective-permute-start.6 = (f32[72,128]{1,0:T(8,128)S(1)}, f32[72,128]{1,0:T(8,128)S(1)}, u32[]{:S(2)}, u32[]{:S(2)}) collective-permute-start(f32[72,128]{1,0:T(8,128)S(1)} %get-tuple-element.49), channel_id=1, source_target_pairs={{0,24},{4,28},{8,16},{12,20},{16,8},{20,12},{24,0},{28,4},{1,25},{... | collective-permute-start | bytes 110600 | tf_op jit(solution)/shard_map/ppermute | solution.py:39
  16.9 4.4 %collective-permute-start.7 = (f32[72,128]{1,0:T(8,128)S(1)}, f32[72,128]{1,0:T(8,128)S(1)}, u32[]{:S(2)}, u32[]{:S(2)}) collective-permute-start(f32[72,128]{1,0:T(8,128)S(1)} %get-tuple-element.50), channel_id=1, source_target_pairs={{0,8},{4,12},{8,0},{12,4},{16,24},{20,28},{24,16},{28,20},{1,9},{5... | collective-permute-start | bytes 110600 | tf_op jit(solution)/shard_map/ppermute | solution.py:39
  21.6 5.7 %collective-permute-start.10 = (f32[136,128]{1,0:T(8,128)S(1)}, f32[136,128]{1,0:T(8,128)S(1)}, u32[]{:S(2)}, u32[]{:S(2)}) collective-permute-start(f32[136,128]{1,0:T(8,128)S(1)} %merge.2.refs_8_), channel_id=1, source_target_pairs={{0,16},{4,20},{8,24},{12,28},{16,0},{20,4},{24,8},{28,12},{1,17},{... | collective-permute-start | bytes 208904 | tf_op jit(solution)/shard_map/ppermute | solution.py:39
  22.6 6.2 %collective-permute-start.9 = (f32[136,128]{1,0:T(8,128)S(1)}, f32[136,128]{1,0:T(8,128)S(1)}, u32[]{:S(2)}, u32[]{:S(2)}) collective-permute-start(f32[136,128]{1,0:T(8,128)S(1)} %merge.2.refs_8_), channel_id=1, source_target_pairs={{0,24},{4,28},{8,16},{12,20},{16,8},{20,12},{24,0},{28,4},{1,25},{... | collective-permute-start | bytes 208904 | tf_op jit(solution)/shard_map/ppermute | solution.py:39
  23.9 5.1 %collective-permute-start.8 = (f32[136,128]{1,0:T(8,128)S(1)}, f32[136,128]{1,0:T(8,128)S(1)}, u32[]{:S(2)}, u32[]{:S(2)}) collective-permute-start(f32[136,128]{1,0:T(8,128)S(1)} %merge.2.refs_8_), channel_id=1, source_target_pairs={{0,8},{4,12},{8,0},{12,4},{16,24},{20,28},{24,16},{28,20},{1,9},{5... | collective-permute-start | bytes 208904 | tf_op jit(solution)/shard_map/ppermute | solution.py:39
  42.4 29.3 %collective-permute-start.17 = (f32[1368,128]{1,0:T(8,128)S(1)}, f32[1368,128]{1,0:T(8,128)S(1)}, u32[]{:S(2)}, u32[]{:S(2)}) collective-permute-start(f32[1368,128]{1,0:T(8,128)S(1)} %get-tuple-element.57.refs_2_), channel_id=1, source_target_pairs={{0,2},{2,0},{1,3},{3,1},{4,6},{6,4},{5,7},{7,5},{8,10},{10,8},{9,1... | collective-permute-start | bytes 2101256 | tf_op jit(solution)/shard_map/ppermute | solution.py:39
  43.0 8.0 %collective-permute-start.11 = (f32[136,128]{1,0:T(8,128)S(1)}, f32[136,128]{1,0:T(8,128)S(1)}, u32[]{:S(2)}, u32[]{:S(2)}) collective-permute-start(f32[136,128]{1,0:T(8,128)S(1)} %get-tuple-element.59), channel_id=1, source_target_pairs={{0,16},{4,20},{8,24},{12,28},{16,0},{20,4},{24,8},{28,12},{1,17},{... | collective-permute-start | bytes 208904 | tf_op jit(solution)/shard_map/ppermute | solution.py:39
  43.5 7.5 %collective-permute-start.12 = (f32[136,128]{1,0:T(8,128)S(1)}, f32[136,128]{1,0:T(8,128)S(1)}, u32[]{:S(2)}, u32[]{:S(2)}) collective-permute-start(f32[136,128]{1,0:T(8,128)S(1)} %get-tuple-element.60), channel_id=1, source_target_pairs={{0,24},{4,28},{8,16},{12,20},{16,8},{20,12},{24,0},{28,4},{1,25},{... | collective-permute-start | bytes 208904 | tf_op jit(solution)/shard_map/ppermute | solution.py:39
  45.9 5.3 %collective-permute-start.13 = (f32[136,128]{1,0:T(8,128)S(1)}, f32[136,128]{1,0:T(8,128)S(1)}, u32[]{:S(2)}, u32[]{:S(2)}) collective-permute-start(f32[136,128]{1,0:T(8,128)S(1)} %get-tuple-element.61), channel_id=1, source_target_pairs={{0,8},{4,12},{8,0},{12,4},{16,24},{20,28},{24,16},{28,20},{1,9},{5... | collective-permute-start | bytes 208904 | tf_op jit(solution)/shard_map/ppermute | solution.py:39
  51.4 6.8 %collective-permute-start.16 = (f32[136,128]{1,0:T(8,128)S(1)}, f32[136,128]{1,0:T(8,128)S(1)}, u32[]{:S(2)}, u32[]{:S(2)}) collective-permute-start(f32[136,128]{1,0:T(8,128)S(1)} %merge.3.refs_0_), channel_id=1, source_target_pairs={{0,16},{4,20},{8,24},{12,28},{16,0},{20,4},{24,8},{28,12},{1,17},{... | collective-permute-start | bytes 208904 | tf_op jit(solution)/shard_map/ppermute | solution.py:39
  52.0 7.0 %collective-permute-start.15 = (f32[136,128]{1,0:T(8,128)S(1)}, f32[136,128]{1,0:T(8,128)S(1)}, u32[]{:S(2)}, u32[]{:S(2)}) collective-permute-start(f32[136,128]{1,0:T(8,128)S(1)} %merge.3.refs_0_), channel_id=1, source_target_pairs={{0,24},{4,28},{8,16},{12,20},{16,8},{20,12},{24,0},{28,4},{1,25},{... | collective-permute-start | bytes 208904 | tf_op jit(solution)/shard_map/ppermute | solution.py:39
  55.1 4.6 %collective-permute-start.14 = (f32[136,128]{1,0:T(8,128)S(1)}, f32[136,128]{1,0:T(8,128)S(1)}, u32[]{:S(2)}, u32[]{:S(2)}) collective-permute-start(f32[136,128]{1,0:T(8,128)S(1)} %merge.3.refs_0_), channel_id=1, source_target_pairs={{0,8},{4,12},{8,0},{12,4},{16,24},{20,28},{24,16},{28,20},{1,9},{5... | collective-permute-start | bytes 208904 | tf_op jit(solution)/shard_map/ppermute | solution.py:39
  59.8 11.9 %collective-permute-start.18 = (f32[136,512]{1,0:T(8,128)S(1)}, f32[136,512]{1,0:T(8,128)S(1)}, u32[]{:S(2)}, u32[]{:S(2)}) collective-permute-start(f32[136,512]{1,0:T(8,128)S(1)} %join.1.refs_4_), channel_id=1, source_target_pairs={{0,2},{2,0},{1,3},{3,1},{4,6},{6,4},{5,7},{7,5},{8,10},{10,8},{9,1... | collective-permute-start | bytes 835592 | tf_op jit(solution)/shard_map/ppermute | solution.py:39
  61.5 10.2 %copy-start.4 = (f32[328,128]{1,0:T(8,128)S(1)}, f32[328,128]{1,0:T(8,128)}, u32[]{:S(2)}) copy-start(f32[328,128]{1,0:T(8,128)} %get-tuple-element.37.refs_5_) | copy-start | bytes 503812
  72.7 2.0 %collective-permute-start.19 = (f32[1040,128]{1,0:T(8,128)S(1)}, f32[1040,128]{1,0:T(8,128)S(1)}, u32[]{:S(2)}, u32[]{:S(2)}) collective-permute-start(f32[1040,128]{1,0:T(8,128)S(1)} %page_update.2.refs_6_), channel_id=1, source_target_pairs={{0,4},{4,0},{8,12},{12,8},{16,20},{20,16},{24,28},{28,24},{1,5},{5... | collective-permute-start | bytes 1597448 | tf_op jit(solution)/shard_map/ppermute | solution.py:39

commit v28 on v26

--- a/solution.py
+++ b/solution.py
@@ -84,7 +84,10 @@
 
     return pl.pallas_call(
         without_after,
-        out_shape=[jax.ShapeDtypeStruct(shape, jnp.float32) for shape in out_shapes],
+        out_shape=[
+            shape if hasattr(shape, "dtype") else jax.ShapeDtypeStruct(shape, jnp.float32)
+            for shape in out_shapes
+        ],
         in_specs=[pl.BlockSpec(memory_space=space) for space in spaces],
         out_specs=[pl.BlockSpec(memory_space=pltpu.VMEM) for _ in out_shapes],
         scratch_shapes=scratch,
@@ -327,9 +330,13 @@
     def updated(state, grads, sizes):
         return [value - size * grad for value, grad, size in zip(state, grads, sizes)]
 
-    def page_scores(ref, queries, positions):
-        scores = dot_deep(halves(ref[:slot_rows, :]), queries, 1, 1) * score_scale
-        bias = row_as_column(tail_as_row(ref, 2 * slot_rows, bias_rows), width)
+    def page_bias(ref):
+        return row_as_column(tail_as_row(ref, 2 * slot_rows, bias_rows), width)
+
+    def page_scores(ref, queries, positions, keys=None, bias=None):
+        keys = halves(ref[:slot_rows, :]) if keys is None else keys
+        bias = page_bias(ref) if bias is None else bias
+        scores = dot_deep(keys, queries, 1, 1) * score_scale
         scores = scores + jnp.concatenate([bias] * (positions.shape[1] // width), axis=1)
         page_start = ref[packed_rows - 1 : packed_rows, 0:1]
         visible = jnp.broadcast_to(positions >= page_start, scores.shape)
@@ -393,13 +400,33 @@
 
     def part_body(*refs):
         state_refs, (query_ref, *refs) = refs[:CORES], refs[CORES:]
-        piece_outs, (weights_out, max_out, pieces) = refs[:ranks], refs[ranks:]
+        if ready:
+            (split_ref, bias_ref), refs = refs[:2], refs[2:]
+            piece_outs, (weights_out, max_out, pieces) = refs[:ranks], refs[ranks:]
+        else:
+            piece_outs, refs = refs[:ranks], refs[ranks:]
+            weights_out, max_out, split_ref, bias_ref, pieces = refs
+            for at, ref in enumerate(state_refs):
+                rows = slice(at * slot_rows, (at + 1) * slot_rows)
+                both = halves(ref[:slot_rows, :]) + halves(ref[slot_rows : 2 * slot_rows, :])
+                for which, half in enumerate(both):
+                    split_ref[rows, which * width : (which + 1) * width] = half
+                bias_ref[rows, :] = page_bias(ref)
+
+        def read_split(at, first):
+            rows = slice(at * slot_rows, (at + 1) * slot_rows)
+            return tuple(
+                split_ref[rows, which * width : (which + 1) * width]
+                for which in (first, first + 1)
+            )
+
         rank, _, _ = places()
         queries = halves(query_ref[:part_rows, :])
         position_row = tail_as_row(query_ref, part_rows + piece, pos_rows)
         all_scores, all_visible = [], []
-        for ref in state_refs:
-            scores, visible = page_scores(ref, queries, position_row)
+        for at, ref in enumerate(state_refs):
+            bias = bias_ref[at * slot_rows : (at + 1) * slot_rows, :]
+            scores, visible = page_scores(ref, queries, position_row, read_split(at, 0), bias)
             all_scores.append(scores)
             all_visible.append(visible)
         row_max = jnp.max(all_scores[0], axis=0, keepdims=True)
@@ -411,8 +438,7 @@
             weights = jnp.where(all_visible[at], jnp.exp(all_scores[at] - row_max), 0.0)
             weights_out[at * slot_rows : (at + 1) * slot_rows, :] = weights
             row_total = row_total + jnp.sum(weights, axis=0, keepdims=True)
-            values = halves(ref[slot_rows : 2 * slot_rows, :])
-            row_sum = row_sum + dot_low(values, halves(weights), 0, 0)
+            row_sum = row_sum + dot_low(read_split(at, 2), halves(weights), 0, 0)
         max_out[...] = jnp.broadcast_to(row_max, (TAIL, part_rows))
         for at in range(ranks):
             own = slice(at * piece, (at + 1) * piece)
@@ -579,16 +605,20 @@
         last = repeat == STEPS - 1
         if repeat == 0:
             sums, weights, maxima = [], [], []
+            split_shape = jax.ShapeDtypeStruct((slots, 4 * width), jnp.bfloat16)
+            ready = []
             for query_pack in query_parts:
-                *pieces, part_weights, part_max = call(
+                outs = call(
                     part_body,
-                    part_shapes,
+                    part_shapes + ([] if ready else [split_shape, (slots, width)]),
                     "forward",
                     2 * matmul_cost // query_devices,
-                    states + [query_pack],
+                    states + [query_pack] + ready,
                     piece_scratch,
                     after=maxima[-1:],
                 )
+                pieces, (part_weights, part_max, *handed) = list(outs[:ranks]), outs[ranks:]
+                ready = ready or handed
                 arrived = {
                     turn: exchange(pieces[turn], page=CORES * turn)
                     for turn in turns

time: 75.8 us -> 75.9 us (level)
  no operation moved by 1% of the time
where the time goes in v28:
time: 75.9 us; the launch traced here: 75.7 us
  starting transfers between devices  24.7 us (33%)
  blocking collectives  19.7 us (26%)
  waiting for transfers between devices  18.5 us (24%)
  Pallas kernels  11.8 us (16%)
  between operations  0.83 us (1%)
    ppermute x20, starting transfers between devices, exchange(): return lax.ppermute(value, axes, pairs)  24.7 us
    all_to_all x2, blocking collectives, direct_per_device(): lax.all_to_all(squares, ('head', 'query', 'page'), split_axis=0, concat_a...  19.7 us
    ppermute x20, waiting for transfers between devices, exchange(): return lax.ppermute(value, axes, pairs)  18.5 us
    pallas_call x13, Pallas kernels, call(): pl.pallas_call(without_after, out_shape=[shape if hasattr(shape, 'dtype')...  11.8 us
  transfers between devices with their start and end apart: 20, of which 11 were waited for; matrix products, arithmetic and copies ran while one was open for 0% of the time, Pallas kernels for 7%

profile of v28, /device:TPU:0, one launch (start us, length us, event | category | flops | bytes accessed | tf_op | source)
XLA Modules:
  0.0 75.7 jit_solution(3895646478613792577)
XLA Ops:
  0.7 2.0 %pack.1 = (f32[520,128]{1,0:T(8,128)}, f32[328,128]{1,0:T(8,128)}) custom-call(f32[4,256,128]{2,1,0:T(8,128)} %refs_0_.3, f32[4,256,128]{2,1,0:T(8,128)} %refs_1_.3, f32[4,256,128]{2,1,0:T(8,128)} %refs_2_.3, f32[4,256]{1,0:T(4,128)} %refs_3_.3, f32[4,256,128]{2,1,0:T(8,128)} %refs_4_.3, s32[4,256]{1,0:T(4,128)} %refs_5_.3, s32[8]{0:T(128)} %refs_6_.3), custom_call_target="tpu_custom_call" | custom-call | flops 1048576 | bytes 1048576 | tf_op jit(solution)/shard_map/pack/pallas_call | solution.py:85
  2.7 0.0 copy-start.7
  2.7 0.5 collective-permute-start
  3.3 2.6 %collective-permute-start.1 = (f32[328,128]{1,0:T(8,128)}, f32[328,128]{1,0:T(8,128)S(1)}, u32[]{:S(2)}, u32[]{:S(2)}) collective-permute-start(f32[328,128]{1,0:T(8,128)} %get-tuple-element.37.refs_5_), channel_id=1, source_target_pairs={{0,2},{2,0},{1,3},{3,1},{4,6},{6,4},{5,7},{7,5},{8,10},{10,8},{9,1... | collective-permute-start | bytes 503816 | tf_op jit(solution)/shard_map/ppermute | solution.py:39
  5.9 0.7 own.1
  6.6 1.0 %forward.2 = (f32[72,128]{1,0:T(8,128)S(1)}, f32[72,128]{1,0:T(8,128)S(1)}, f32[72,128]{1,0:T(8,128)S(1)}, f32[72,128]{1,0:T(8,128)S(1)}, f32[512,256]{1,0:T(8,1...) custom-call(f32[520,128]{1,0:T(8,128)S(1)} %get-tuple-element.34.refs_0_.refs_4_, ...), custom_call_target="tpu_custom_call" | custom-call | flops 201326592 | bytes 1048576 | tf_op jit(solution)/shard_map/forward/pallas_call | solution.py:85
  7.5 2.7 %collective-permute-start.2 = (f32[72,128]{1,0:T(8,128)S(1)}, f32[72,128]{1,0:T(8,128)S(1)}, u32[]{:S(2)}, u32[]{:S(2)}) collective-permute-start(f32[72,128]{1,0:T(8,128)S(1)} %get-tuple-element.44), channel_id=1, source_target_pairs={{0,16},{4,20},{8,24},{12,28},{16,0},{20,4},{24,8},{28,12},{1,17},{... | collective-permute-start | bytes 110600 | tf_op jit(solution)/shard_map/ppermute | solution.py:39
  10.2 1.3 %collective-permute-start.3 = (f32[72,128]{1,0:T(8,128)S(1)}, f32[72,128]{1,0:T(8,128)S(1)}, u32[]{:S(2)}, u32[]{:S(2)}) collective-permute-start(f32[72,128]{1,0:T(8,128)S(1)} %get-tuple-element.45), channel_id=1, source_target_pairs={{0,24},{4,28},{8,16},{12,20},{16,8},{20,12},{24,0},{28,4},{1,25},{... | collective-permute-start | bytes 110600 | tf_op jit(solution)/shard_map/ppermute | solution.py:39
  11.5 0.2 collective-permute-start.4
  11.8 0.0 collective-permute-done.1.refs_2_.refs_1_.refs_7_.refs_3_.refs_4_
  11.8 0.9 %forward.3 = (f32[72,128]{1,0:T(8,128)S(1)}, f32[72,128]{1,0:T(8,128)S(1)}, f32[72,128]{1,0:T(8,128)S(1)}, f32[72,128]{1,0:T(8,128)S(1)}, f32[512,256]{1,0:T(8,128)S(1)}, /*index=5*/f32[8,256]{1,0:T(8,128)S(1)}) custom-call(f32[520,128]{1,0:T(8,128)S(1)} %get-tuple-element.34.refs_0_.refs_4_, f32[520,128]{1,0:T(8,128)S(1)} %collective-permute-done.refs_1_.refs_5_, ...), custom_call_target="tpu_custom_call" | custom-call | flops 201326592 | bytes 1048576 | tf_op jit(solution)/shard_map/forward/pallas_call | solution.py:85
  12.7 2.9 %collective-permute-start.5 = (f32[72,128]{1,0:T(8,128)S(1)}, f32[72,128]{1,0:T(8,128)S(1)}, u32[]{:S(2)}, u32[]{:S(2)}) collective-permute-start(f32[72,128]{1,0:T(8,128)S(1)} %get-tuple-element.48), channel_id=1, source_target_pairs={{0,16},{4,20},{8,24},{12,28},{16,0},{20,4},{24,8},{28,12},{1,17},{... | collective-permute-start | bytes 110600 | tf_op jit(solution)/shard_map/ppermute | solution.py:39
  15.6 1.3 %collective-permute-start.6 = (f32[72,128]{1,0:T(8,128)S(1)}, f32[72,128]{1,0:T(8,128)S(1)}, u32[]{:S(2)}, u32[]{:S(2)}) collective-permute-start(f32[72,128]{1,0:T(8,128)S(1)} %get-tuple-element.49), channel_id=1, source_target_pairs={{0,24},{4,28},{8,16},{12,20},{16,8},{20,12},{24,0},{28,4},{1,25},{... | collective-permute-start | bytes 110600 | tf_op jit(solution)/shard_map/ppermute | solution.py:39
  16.9 0.0 collective-permute-done.2.refs_2_
  16.9 0.0 collective-permute-start.7
  17.0 0.7 collective-permute-done.5.refs_6_
  17.6 3.7 %collective-permute-done.6.refs_7_ = f32[72,128]{1,0:T(8,128)S(1)} collective-permute-done((f32[72,128]{1,0:T(8,128)S(1)}, f32[72,128]{1,0:T(8,128)S(1)}, u32[]{:S(2)}, u32[]{:S(2)}) %collective-permute-start.6) | collective-permute-done | bytes 36896 | tf_op jit(solution)/shard_map/ppermute | solution.py:39
  21.4 0.3 merge.2.refs_8_
  21.6 1.0 %collective-permute-start.10 = (f32[136,128]{1,0:T(8,128)S(1)}, f32[136,128]{1,0:T(8,128)S(1)}, u32[]{:S(2)}, u32[]{:S(2)}) collective-permute-start(f32[136,128]{1,0:T(8,128)S(1)} %merge.2.refs_8_), channel_id=1, source_target_pairs={{0,16},{4,20},{8,24},{12,28},{16,0},{20,4},{24,8},{28,12},{1,17},{... | collective-permute-start | bytes 208904 | tf_op jit(solution)/shard_map/ppermute | solution.py:39
  22.6 1.3 %collective-permute-start.9 = (f32[136,128]{1,0:T(8,128)S(1)}, f32[136,128]{1,0:T(8,128)S(1)}, u32[]{:S(2)}, u32[]{:S(2)}) collective-permute-start(f32[136,128]{1,0:T(8,128)S(1)} %merge.2.refs_8_), channel_id=1, source_target_pairs={{0,24},{4,28},{8,16},{12,20},{16,8},{20,12},{24,0},{28,4},{1,25},{... | collective-permute-start | bytes 208904 | tf_op jit(solution)/shard_map/ppermute | solution.py:39
  24.0 1.2 %collective-permute-start.8 = (f32[136,128]{1,0:T(8,128)S(1)}, f32[136,128]{1,0:T(8,128)S(1)}, u32[]{:S(2)}, u32[]{:S(2)}) collective-permute-start(f32[136,128]{1,0:T(8,128)S(1)} %merge.2.refs_8_), channel_id=1, source_target_pairs={{0,8},{4,12},{8,0},{12,4},{16,24},{20,28},{24,16},{28,20},{1,9},{5... | collective-permute-start | bytes 208904 | tf_op jit(solution)/shard_map/ppermute | solution.py:39
  25.2 2.1 %collective-permute-done.10.refs_11_ = f32[136,128]{1,0:T(8,128)S(1)} collective-permute-done((f32[136,128]{1,0:T(8,128)S(1)}, f32[136,128]{1,0:T(8,128)S(1)}, u32[]{:S(2)}, u32[]{:S(2)}) %collective-permute-start.10) | collective-permute-done | bytes 69664 | tf_op jit(solution)/shard_map/ppermute | solution.py:39
  27.3 1.5 %collective-permute-done.9.refs_10_ = f32[136,128]{1,0:T(8,128)S(1)} collective-permute-done((f32[136,128]{1,0:T(8,128)S(1)}, f32[136,128]{1,0:T(8,128)S(1)}, u32[]{:S(2)}, u32[]{:S(2)}) %collective-permute-start.9) | collective-permute-done | bytes 69664 | tf_op jit(solution)/shard_map/ppermute | solution.py:39
  28.9 0.2 collective-permute-done.8.refs_9_
  29.0 1.4 %backward.2 = (f32[520,128]{1,0:T(8,128)S(1)}, f32[520,128]{1,0:T(8,128)S(1)}, f32[32,1,128]{2,1,0:T(1,128)S(1)}) custom-call(f32[512,256]{1,0:T(8,128)S(1)} %get-tuple-element.38.refs_0_, f32[512,256]{1,0:T(8,128)S(1)} %get-tuple-element.42.refs_1_, f32[8,256]{1,0:T(8,128)S(1)} %get-tuple-element.41.refs_5_.refs_2_, ...), custom_call_target="tpu_custom_call" | custom-call | flops 603979776 | bytes 1048576 | tf_op jit(solution)/shard_map/backward/pallas_call | solution.py:85
  30.4 10.9 %all_to_all.10.refs_6_ = f32[32,1,128]{2,1,0:T(1,128)S(1)} all-to-all(f32[32,1,128]{2,1,0:T(1,128)S(1)} %get-tuple-element.54), channel_id=1, replica_groups=mesh['page'=8,'query'=2,'head'=2] {'head','query','page'}, dimensions={0} | all-to-all | bytes 32768 | tf_op jit(solution)/shard_map/all_to_all | solution.py:672
  41.3 1.1 %update_forward.1 = (f32[1368,128]{1,0:T(8,128)S(1)}, f32[136,128]{1,0:T(8,128)S(1)}, f32[136,128]{1,0:T(8,128)S(1)}, f32[136,128]{1,0:T(8,128)S(1)}, f32[136,12...) custom-call(f32[520,128]{1,0:T(8,128)S(1)} %get-tuple-element.34.refs_0_.refs_4_, ...), custom_call_target="tpu_custom_call" | custom-call | flops 402653184 | bytes 1048576 | tf_op jit(solution)/shard_map/update_forward/pallas_call | solution.py:85
  42.4 0.6 collective-permute-start.17
  43.0 0.5 collective-permute-start.11
  43.5 2.4 %collective-permute-start.12 = (f32[136,128]{1,0:T(8,128)S(1)}, f32[136,128]{1,0:T(8,128)S(1)}, u32[]{:S(2)}, u32[]{:S(2)}) collective-permute-start(f32[136,128]{1,0:T(8,128)S(1)} %get-tuple-element.60), channel_id=1, source_target_pairs={{0,24},{4,28},{8,16},{12,20},{16,8},{20,12},{24,0},{28,4},{1,25},{... | collective-permute-start | bytes 208904 | tf_op jit(solution)/shard_map/ppermute | solution.py:39
  45.9 0.6 collective-permute-start.13
  46.5 4.5 %collective-permute-done.11.refs_3_ = f32[136,128]{1,0:T(8,128)S(1)} collective-permute-done((f32[136,128]{1,0:T(8,128)S(1)}, f32[136,128]{1,0:T(8,128)S(1)}, u32[]{:S(2)}, u32[]{:S(2)}) %collective-permute-start.11) | collective-permute-done | bytes 69664 | tf_op jit(solution)/shard_map/ppermute | solution.py:39
  51.0 0.2 collective-permute-done.13.refs_5_
  51.3 0.1 merge.3.refs_0_
  51.4 0.7 collective-permute-start.16
  52.0 3.0 %collective-permute-start.15 = (f32[136,128]{1,0:T(8,128)S(1)}, f32[136,128]{1,0:T(8,128)S(1)}, u32[]{:S(2)}, u32[]{:S(2)}) collective-permute-start(f32[136,128]{1,0:T(8,128)S(1)} %merge.3.refs_0_), channel_id=1, source_target_pairs={{0,24},{4,28},{8,16},{12,20},{16,8},{20,12},{24,0},{28,4},{1,25},{... | collective-permute-start | bytes 208904 | tf_op jit(solution)/shard_map/ppermute | solution.py:39
  55.1 3.1 %collective-permute-done.16.refs_3_ = f32[136,128]{1,0:T(8,128)S(1)} collective-permute-done((f32[136,128]{1,0:T(8,128)S(1)}, f32[136,128]{1,0:T(8,128)S(1)}, u32[]{:S(2)}, u32[]{:S(2)}) %collective-permute-start.16) | collective-permute-done | bytes 69664 | tf_op jit(solution)/shard_map/ppermute | solution.py:39
  58.2 0.8 %collective-permute-done.15.refs_2_ = f32[136,128]{1,0:T(8,128)S(1)} collective-permute-done((f32[136,128]{1,0:T(8,128)S(1)}, f32[136,128]{1,0:T(8,128)S(1)}, u32[]{:S(2)}, u32[]{:S(2)}) %collective-permute-start.15) | collective-permute-done | bytes 69664 | tf_op jit(solution)/shard_map/ppermute | solution.py:39
  59.0 0.7 collective-permute-done.14.refs_1_
  59.7 0.1 join.1.refs_5_
  59.8 1.7 %collective-permute-start.18 = (f32[136,512]{1,0:T(8,128)S(1)}, f32[136,512]{1,0:T(8,128)S(1)}, u32[]{:S(2)}, u32[]{:S(2)}) collective-permute-start(f32[136,512]{1,0:T(8,128)S(1)} %join.1.refs_5_), channel_id=1, source_target_pairs={{0,2},{2,0},{1,3},{3,1},{4,6},{6,4},{5,7},{7,5},{8,10},{10,8},{9,1... | collective-permute-start | bytes 835592 | tf_op jit(solution)/shard_map/ppermute | solution.py:39
  61.5 1.3 %backward.3 = (f32[520,128]{1,0:T(8,128)S(1)}, f32[520,128]{1,0:T(8,128)S(1)}, f32[32,1,128]{2,1,0:T(1,128)S(1)}) custom-call(f32[512,512]{1,0:T(8,128)S(1)} %get-tuple-element.55.refs_0_, f32[8,512]{1,0:T(8,128)S(1)} %get-tuple-element.56.refs_1_, f32[1368,128]{1,0:T(8,128)S(1)} %get-tuple-element.57.refs_2_, ...), custom_call_target="tpu_custom_call" | custom-call | flops 603979776 | bytes 1048576 | tf_op jit(solution)/shard_map/backward/pallas_call | solution.py:85
  62.8 8.9 %all_to_all.11.refs_0_ = f32[32,1,128]{2,1,0:T(1,128)S(1)} all-to-all(f32[32,1,128]{2,1,0:T(1,128)S(1)} %get-tuple-element.62), channel_id=1, replica_groups=mesh['page'=8,'query'=2,'head'=2] {'head','query','page'}, dimensions={0} | all-to-all | bytes 32768 | tf_op jit(solution)/shard_map/all_to_all | solution.py:672
  71.6 1.0 %page_update.2.refs_6_ = f32[1040,128]{1,0:T(8,128)S(1)} custom-call(f32[32,1,128]{2,1,0:T(1,128)S(1)} %all_to_all.11.refs_0_, f32[520,128]{1,0:T(8,128)S(1)} %get-tuple-element.64.refs_1_, f32[1368,128]{1,0:T(8,128)S(1)} %get-tuple-element.57.refs_2_, f32[1368,128]{1,0:T(8,128)S(1)} %collective-permute-done.17.refs_3_, ...), custom_call_target="tpu_custom_call" | custom-call | flops 301989888 | bytes 1048576 | tf_op jit(solution)/shard_map/page_update/pallas_call | solution.py:85
  72.7 0.1 collective-permute-start.19
  72.7 1.0 %page_update.3.refs_0_ = f32[1040,128]{1,0:T(8,128)S(1)} custom-call(f32[32,1,128]{2,1,0:T(1,128)S(1)} %all_to_all.11.refs_0_, f32[520,128]{1,0:T(8,128)S(1)} %get-tuple-element.63.refs_1_, f32[1368,128]{1,0:T(8,128)S(1)} %get-tuple-element.57.refs_2_, f32[1368,128]{1,0:T(8,128)S(1)} %collective-permute-done.17.refs_3_, ...), custom_call_target="tpu_custom_call" | custom-call | flops 301989888 | bytes 1048576 | tf_op jit(solution)/shard_map/page_update/pallas_call | solution.py:85
  73.7 0.9 %collective-permute-done.19.refs_1_ = f32[1040,128]{1,0:T(8,128)S(1)} collective-permute-done((f32[1040,128]{1,0:T(8,128)S(1)}, f32[1040,128]{1,0:T(8,128)S(1)}, u32[]{:S(2)}, u32[]{:S(2)}) %collective-permute-start.19) | collective-permute-done | bytes 532512 | tf_op jit(solution)/shard_map/ppermute | solution.py:39
  74.6 1.0 %unpack.1 = (f32[4,256,128]{2,1,0:T(8,128)}, f32[4,256,128]{2,1,0:T(8,128)}, f32[4,256]{1,0:T(4,128)}) custom-call(f32[1040,128]{1,0:T(8,128)S(1)} %page_update.3.refs_0_, f32[1040,128]{1,0:T(8,128)S(1)} %collective-permute-done.19.refs_1_), custom_call_target="tpu_custom_call" | custom-call | flops 1048576 | bytes 1048576 | tf_op jit(solution)/shard_map/unpack/pallas_call | solution.py:85
  (23 shorter events, 0.1 us)
Async XLA Ops:
  0.6 5.2 %copy-start.3 = (f32[4,256,128]{2,1,0:T(8,128)S(1)}, f32[4,256,128]{2,1,0:T(8,128)}, u32[]{:S(2)}) copy-start(f32[4,256,128]{2,1,0:T(8,128)} %refs_4_.3) | copy-start | bytes 1572868
  0.6 5.2 %copy-start.2 = (f32[4,256,128]{2,1,0:T(8,128)S(1)}, f32[4,256,128]{2,1,0:T(8,128)}, u32[]{:S(2)}) copy-start(f32[4,256,128]{2,1,0:T(8,128)} %refs_2_.3) | copy-start | bytes 1572868
  0.7 5.2 %copy-start.1 = (f32[4,256,128]{2,1,0:T(8,128)S(1)}, f32[4,256,128]{2,1,0:T(8,128)}, u32[]{:S(2)}) copy-start(f32[4,256,128]{2,1,0:T(8,128)} %refs_1_.3) | copy-start | bytes 1572868
  0.7 5.2 %copy-start = (f32[4,256,128]{2,1,0:T(8,128)S(1)}, f32[4,256,128]{2,1,0:T(8,128)}, u32[]{:S(2)}) copy-start(f32[4,256,128]{2,1,0:T(8,128)} %refs_0_.3) | copy-start | bytes 1572868
  0.7 5.2 %copy-start.5 = (f32[4,256]{1,0:T(4,128)S(1)}, f32[4,256]{1,0:T(4,128)}, u32[]{:S(2)}) copy-start(f32[4,256]{1,0:T(4,128)} %refs_3_.3) | copy-start | bytes 12292
  0.7 5.2 %copy-start.6 = (s32[4,256]{1,0:T(4,128)S(1)}, s32[4,256]{1,0:T(4,128)}, u32[]{:S(2)}) copy-start(s32[4,256]{1,0:T(4,128)} %refs_5_.3) | copy-start | bytes 12292
  2.7 3.2 %copy-start.7 = (s32[8]{0:T(128)S(1)}, s32[8]{0:T(128)}, u32[]{:S(2)}) copy-start(s32[8]{0:T(128)} %refs_6_.3) | copy-start | bytes 100
  2.7 3.8 %collective-permute-start = (f32[520,128]{1,0:T(8,128)}, f32[520,128]{1,0:T(8,128)S(1)}, u32[]{:S(2)}, u32[]{:S(2)}) collective-permute-start(f32[520,128]{1,0:T(8,128)} %get-tuple-element.35), channel_id=1, source_target_pairs={{0,4},{4,0},{8,12},{12,8},{16,20},{20,16},{24,28},{28,24},{1,5},{5... | collective-permute-start | bytes 798728 | tf_op jit(solution)/shard_map/ppermute | solution.py:39
  3.3 8.5 %collective-permute-start.1 = (f32[328,128]{1,0:T(8,128)}, f32[328,128]{1,0:T(8,128)S(1)}, u32[]{:S(2)}, u32[]{:S(2)}) collective-permute-start(f32[328,128]{1,0:T(8,128)} %get-tuple-element.37.refs_5_), channel_id=1, source_target_pairs={{0,2},{2,0},{1,3},{3,1},{4,6},{6,4},{5,7},{7,5},{8,10},{10,8},{9,1... | collective-permute-start | bytes 503816 | tf_op jit(solution)/shard_map/ppermute | solution.py:39
  7.5 9.4 %collective-permute-start.2 = (f32[72,128]{1,0:T(8,128)S(1)}, f32[72,128]{1,0:T(8,128)S(1)}, u32[]{:S(2)}, u32[]{:S(2)}) collective-permute-start(f32[72,128]{1,0:T(8,128)S(1)} %get-tuple-element.44), channel_id=1, source_target_pairs={{0,16},{4,20},{8,24},{12,28},{16,0},{20,4},{24,8},{28,12},{1,17},{... | collective-permute-start | bytes 110600 | tf_op jit(solution)/shard_map/ppermute | solution.py:39
  10.2 6.7 %collective-permute-start.3 = (f32[72,128]{1,0:T(8,128)S(1)}, f32[72,128]{1,0:T(8,128)S(1)}, u32[]{:S(2)}, u32[]{:S(2)}) collective-permute-start(f32[72,128]{1,0:T(8,128)S(1)} %get-tuple-element.45), channel_id=1, source_target_pairs={{0,24},{4,28},{8,16},{12,20},{16,8},{20,12},{24,0},{28,4},{1,25},{... | collective-permute-start | bytes 110600 | tf_op jit(solution)/shard_map/ppermute | solution.py:39
  11.5 5.4 %collective-permute-start.4 = (f32[72,128]{1,0:T(8,128)S(1)}, f32[72,128]{1,0:T(8,128)S(1)}, u32[]{:S(2)}, u32[]{:S(2)}) collective-permute-start(f32[72,128]{1,0:T(8,128)S(1)} %get-tuple-element.46), channel_id=1, source_target_pairs={{0,8},{4,12},{8,0},{12,4},{16,24},{20,28},{24,16},{28,20},{1,9},{5... | collective-permute-start | bytes 110600 | tf_op jit(solution)/shard_map/ppermute | solution.py:39
  12.7 4.9 %collective-permute-start.5 = (f32[72,128]{1,0:T(8,128)S(1)}, f32[72,128]{1,0:T(8,128)S(1)}, u32[]{:S(2)}, u32[]{:S(2)}) collective-permute-start(f32[72,128]{1,0:T(8,128)S(1)} %get-tuple-element.48), channel_id=1, source_target_pairs={{0,16},{4,20},{8,24},{12,28},{16,0},{20,4},{24,8},{28,12},{1,17},{... | collective-permute-start | bytes 110600 | tf_op jit(solution)/shard_map/ppermute | solution.py:39
  15.6 5.8 %collective-permute-start.6 = (f32[72,128]{1,0:T(8,128)S(1)}, f32[72,128]{1,0:T(8,128)S(1)}, u32[]{:S(2)}, u32[]{:S(2)}) collective-permute-start(f32[72,128]{1,0:T(8,128)S(1)} %get-tuple-element.49), channel_id=1, source_target_pairs={{0,24},{4,28},{8,16},{12,20},{16,8},{20,12},{24,0},{28,4},{1,25},{... | collective-permute-start | bytes 110600 | tf_op jit(solution)/shard_map/ppermute | solution.py:39
  16.9 4.4 %collective-permute-start.7 = (f32[72,128]{1,0:T(8,128)S(1)}, f32[72,128]{1,0:T(8,128)S(1)}, u32[]{:S(2)}, u32[]{:S(2)}) collective-permute-start(f32[72,128]{1,0:T(8,128)S(1)} %get-tuple-element.50), channel_id=1, source_target_pairs={{0,8},{4,12},{8,0},{12,4},{16,24},{20,28},{24,16},{28,20},{1,9},{5... | collective-permute-start | bytes 110600 | tf_op jit(solution)/shard_map/ppermute | solution.py:39
  21.6 5.7 %collective-permute-start.10 = (f32[136,128]{1,0:T(8,128)S(1)}, f32[136,128]{1,0:T(8,128)S(1)}, u32[]{:S(2)}, u32[]{:S(2)}) collective-permute-start(f32[136,128]{1,0:T(8,128)S(1)} %merge.2.refs_8_), channel_id=1, source_target_pairs={{0,16},{4,20},{8,24},{12,28},{16,0},{20,4},{24,8},{28,12},{1,17},{... | collective-permute-start | bytes 208904 | tf_op jit(solution)/shard_map/ppermute | solution.py:39
  22.6 6.2 %collective-permute-start.9 = (f32[136,128]{1,0:T(8,128)S(1)}, f32[136,128]{1,0:T(8,128)S(1)}, u32[]{:S(2)}, u32[]{:S(2)}) collective-permute-start(f32[136,128]{1,0:T(8,128)S(1)} %merge.2.refs_8_), channel_id=1, source_target_pairs={{0,24},{4,28},{8,16},{12,20},{16,8},{20,12},{24,0},{28,4},{1,25},{... | collective-permute-start | bytes 208904 | tf_op jit(solution)/shard_map/ppermute | solution.py:39
  24.0 5.1 %collective-permute-start.8 = (f32[136,128]{1,0:T(8,128)S(1)}, f32[136,128]{1,0:T(8,128)S(1)}, u32[]{:S(2)}, u32[]{:S(2)}) collective-permute-start(f32[136,128]{1,0:T(8,128)S(1)} %merge.2.refs_8_), channel_id=1, source_target_pairs={{0,8},{4,12},{8,0},{12,4},{16,24},{20,28},{24,16},{28,20},{1,9},{5... | collective-permute-start | bytes 208904 | tf_op jit(solution)/shard_map/ppermute | solution.py:39
  42.4 29.2 %collective-permute-start.17 = (f32[1368,128]{1,0:T(8,128)S(1)}, f32[1368,128]{1,0:T(8,128)S(1)}, u32[]{:S(2)}, u32[]{:S(2)}) collective-permute-start(f32[1368,128]{1,0:T(8,128)S(1)} %get-tuple-element.57.refs_2_), channel_id=1, source_target_pairs={{0,2},{2,0},{1,3},{3,1},{4,6},{6,4},{5,7},{7,5},{8,10},{10,8},{9,1... | collective-permute-start | bytes 2101256 | tf_op jit(solution)/shard_map/ppermute | solution.py:39
  43.0 8.0 %collective-permute-start.11 = (f32[136,128]{1,0:T(8,128)S(1)}, f32[136,128]{1,0:T(8,128)S(1)}, u32[]{:S(2)}, u32[]{:S(2)}) collective-permute-start(f32[136,128]{1,0:T(8,128)S(1)} %get-tuple-element.59), channel_id=1, source_target_pairs={{0,16},{4,20},{8,24},{12,28},{16,0},{20,4},{24,8},{28,12},{1,17},{... | collective-permute-start | bytes 208904 | tf_op jit(solution)/shard_map/ppermute | solution.py:39
  43.5 7.5 %collective-permute-start.12 = (f32[136,128]{1,0:T(8,128)S(1)}, f32[136,128]{1,0:T(8,128)S(1)}, u32[]{:S(2)}, u32[]{:S(2)}) collective-permute-start(f32[136,128]{1,0:T(8,128)S(1)} %get-tuple-element.60), channel_id=1, source_target_pairs={{0,24},{4,28},{8,16},{12,20},{16,8},{20,12},{24,0},{28,4},{1,25},{... | collective-permute-start | bytes 208904 | tf_op jit(solution)/shard_map/ppermute | solution.py:39
  45.9 5.3 %collective-permute-start.13 = (f32[136,128]{1,0:T(8,128)S(1)}, f32[136,128]{1,0:T(8,128)S(1)}, u32[]{:S(2)}, u32[]{:S(2)}) collective-permute-start(f32[136,128]{1,0:T(8,128)S(1)} %get-tuple-element.61), channel_id=1, source_target_pairs={{0,8},{4,12},{8,0},{12,4},{16,24},{20,28},{24,16},{28,20},{1,9},{5... | collective-permute-start | bytes 208904 | tf_op jit(solution)/shard_map/ppermute | solution.py:39
  51.4 6.8 %collective-permute-start.16 = (f32[136,128]{1,0:T(8,128)S(1)}, f32[136,128]{1,0:T(8,128)S(1)}, u32[]{:S(2)}, u32[]{:S(2)}) collective-permute-start(f32[136,128]{1,0:T(8,128)S(1)} %merge.3.refs_0_), channel_id=1, source_target_pairs={{0,16},{4,20},{8,24},{12,28},{16,0},{20,4},{24,8},{28,12},{1,17},{... | collective-permute-start | bytes 208904 | tf_op jit(solution)/shard_map/ppermute | solution.py:39
  52.0 7.0 %collective-permute-start.15 = (f32[136,128]{1,0:T(8,128)S(1)}, f32[136,128]{1,0:T(8,128)S(1)}, u32[]{:S(2)}, u32[]{:S(2)}) collective-permute-start(f32[136,128]{1,0:T(8,128)S(1)} %merge.3.refs_0_), channel_id=1, source_target_pairs={{0,24},{4,28},{8,16},{12,20},{16,8},{20,12},{24,0},{28,4},{1,25},{... | collective-permute-start | bytes 208904 | tf_op jit(solution)/shard_map/ppermute | solution.py:39
  55.1 4.6 %collective-permute-start.14 = (f32[136,128]{1,0:T(8,128)S(1)}, f32[136,128]{1,0:T(8,128)S(1)}, u32[]{:S(2)}, u32[]{:S(2)}) collective-permute-start(f32[136,128]{1,0:T(8,128)S(1)} %merge.3.refs_0_), channel_id=1, source_target_pairs={{0,8},{4,12},{8,0},{12,4},{16,24},{20,28},{24,16},{28,20},{1,9},{5... | collective-permute-start | bytes 208904 | tf_op jit(solution)/shard_map/ppermute | solution.py:39
  59.8 11.9 %collective-permute-start.18 = (f32[136,512]{1,0:T(8,128)S(1)}, f32[136,512]{1,0:T(8,128)S(1)}, u32[]{:S(2)}, u32[]{:S(2)}) collective-permute-start(f32[136,512]{1,0:T(8,128)S(1)} %join.1.refs_5_), channel_id=1, source_target_pairs={{0,2},{2,0},{1,3},{3,1},{4,6},{6,4},{5,7},{7,5},{8,10},{10,8},{9,1... | collective-permute-start | bytes 835592 | tf_op jit(solution)/shard_map/ppermute | solution.py:39
  61.5 10.2 %copy-start.4 = (f32[328,128]{1,0:T(8,128)S(1)}, f32[328,128]{1,0:T(8,128)}, u32[]{:S(2)}) copy-start(f32[328,128]{1,0:T(8,128)} %get-tuple-element.37.refs_5_) | copy-start | bytes 503812
  72.7 2.0 %collective-permute-start.19 = (f32[1040,128]{1,0:T(8,128)S(1)}, f32[1040,128]{1,0:T(8,128)S(1)}, u32[]{:S(2)}, u32[]{:S(2)}) collective-permute-start(f32[1040,128]{1,0:T(8,128)S(1)} %page_update.2.refs_6_), channel_id=1, source_target_pairs={{0,4},{4,0},{8,12},{12,8},{16,20},{20,16},{24,28},{28,24},{1,5},{5... | collective-permute-start | bytes 1597448 | tf_op jit(solution)/shard_map/ppermute | solution.py:39

commit v29 on v26

--- a/solution.py
+++ b/solution.py
@@ -439,20 +439,21 @@
             store_pack(state_outs[at], updated(state, read_pack(grad_refs[at]), sizes))
         forward(state_outs, query_refs, chunk_outs, *refs)
 
-    def merged_chunk(query_refs, sums, maxima, totals, out):
-        targets = jnp.concatenate(
-            [ref[part_rows : part_rows + piece, :] for ref in query_refs], axis=0
-        )
+    def merged_sums(sums, maxima, totals):
         row_max = maxima[0]
         for other in maxima[1:]:
             row_max = jnp.maximum(row_max, other)
-        row_total = jnp.zeros_like(row_max)
-        row_sum = jnp.zeros((width, chunk), jnp.float32)
+        row_total, row_sum = jnp.zeros_like(row_max), jnp.zeros_like(sums[0])
         for part_sum, part_max, part_total in zip(sums, maxima, totals):
             factor = jnp.exp(part_max - row_max)
             row_total = row_total + part_total * factor
             row_sum = row_sum + part_sum * factor
-        output = row_sum / row_total
+        return row_sum / row_total, row_max, row_total
+
+    def store_chunk(query_refs, output, row_max, row_total, out):
+        targets = jnp.concatenate(
+            [ref[part_rows : part_rows + piece, :] for ref in query_refs], axis=0
+        )
         residual = output - targets.T
         row_delta = jnp.sum(residual * output, axis=0, keepdims=True)
         out[:width, :] = residual
@@ -460,32 +461,26 @@
             [row_max, row_total, row_delta, jnp.zeros((TAIL - 3, chunk), jnp.float32)], axis=0
         )
 
+    def read_sums(refs, rows):
+        return [
+            [ref[:rows, :] for ref in refs],
+            [ref[rows : rows + 1, :] for ref in refs],
+            [ref[rows + 1 : rows + 2, :] for ref in refs],
+        ]
+
     def first_merge_body(*refs):
         query_refs, (*piece_refs, merged_out) = refs[:query_devices], refs[query_devices:]
-
-        def joined(read):
-            return [
-                jnp.concatenate([read(ref) for ref in piece_refs[turn::ranks]], axis=1)
-                for turn in range(ranks)
-            ]
-
-        merged_chunk(
-            query_refs,
-            joined(lambda ref: unfold_rows(ref[:folded, :])),
-            joined(lambda ref: ref[folded : folded + 1, :piece]),
-            joined(lambda ref: ref[folded + 1 : folded + 2, :piece]),
-            merged_out,
-        )
+        parts = []
+        for part in range(query_devices):
+            group = piece_refs[part * ranks : (part + 1) * ranks]
+            output, row_max, row_total = merged_sums(*read_sums(group, folded))
+            parts.append((unfold_rows(output), row_max[:, :piece], row_total[:, :piece]))
+        joined = [jnp.concatenate(values, axis=1) for values in zip(*parts)]
+        store_chunk(query_refs, *joined, merged_out)
 
     def merge_body(*refs):
         query_refs, (*chunk_refs, merged_out) = refs[:query_devices], refs[query_devices:]
-        merged_chunk(
-            query_refs,
-            [ref[:width, :] for ref in chunk_refs],
-            [ref[width : width + 1, :] for ref in chunk_refs],
-            [ref[width + 1 : width + 2, :] for ref in chunk_refs],
-            merged_out,
-        )
+        store_chunk(query_refs, *merged_sums(*read_sums(chunk_refs, width)), merged_out)
 
     def page_gradients(weights, factor, state_ref, all_queries, residual, row_delta):
         attention = weights * factor

time: 75.8 us -> 75.8 us (level)
  no operation moved by 1% of the time
where the time goes in v29:
time: 75.8 us; the launch traced here: 75.6 us
  starting transfers between devices  24.7 us (33%)
  blocking collectives  19.8 us (26%)
  waiting for transfers between devices  18.5 us (24%)
  Pallas kernels  11.7 us (15%)
  between operations  0.83 us (1%)
    ppermute x20, starting transfers between devices, exchange(): return lax.ppermute(value, axes, pairs)  24.7 us
    all_to_all x2, blocking collectives, direct_per_device(): lax.all_to_all(squares, ('head', 'query', 'page'), split_axis=0, concat_a...  19.8 us
    ppermute x20, waiting for transfers between devices, exchange(): return lax.ppermute(value, axes, pairs)  18.5 us
    pallas_call x13, Pallas kernels, call(): pl.pallas_call(without_after, out_shape=[jax.ShapeDtypeStruct(shape, jnp....  11.7 us
  transfers between devices with their start and end apart: 20, of which 11 were waited for; matrix products, arithmetic and copies ran while one was open for 0% of the time, Pallas kernels for 7%

profile of v29, /device:TPU:0, one launch (start us, length us, event | category | flops | bytes accessed | tf_op | source)
XLA Modules:
  0.0 75.6 jit_solution(17824935817289968740)
XLA Ops:
  0.7 2.0 %pack.1 = (f32[520,128]{1,0:T(8,128)}, f32[328,128]{1,0:T(8,128)}) custom-call(f32[4,256,128]{2,1,0:T(8,128)} %refs_0_.3, f32[4,256,128]{2,1,0:T(8,128)} %refs_1_.3, f32[4,256,128]{2,1,0:T(8,128)} %refs_2_.3, f32[4,256]{1,0:T(4,128)} %refs_3_.3, f32[4,256,128]{2,1,0:T(8,128)} %refs_4_.3, s32[4,256]{1,0:T(4,128)} %refs_5_.3, s32[8]{0:T(128)} %refs_6_.3), custom_call_target="tpu_custom_call" | custom-call | flops 1048576 | bytes 1048576 | tf_op jit(solution)/shard_map/pack/pallas_call | solution.py:85
  2.7 0.0 copy-start.7
  2.7 0.5 collective-permute-start
  3.3 2.6 %collective-permute-start.1 = (f32[328,128]{1,0:T(8,128)}, f32[328,128]{1,0:T(8,128)S(1)}, u32[]{:S(2)}, u32[]{:S(2)}) collective-permute-start(f32[328,128]{1,0:T(8,128)} %get-tuple-element.35.refs_5_), channel_id=1, source_target_pairs={{0,2},{2,0},{1,3},{3,1},{4,6},{6,4},{5,7},{7,5},{8,10},{10,8},{9,1... | collective-permute-start | bytes 503816 | tf_op jit(solution)/shard_map/ppermute | solution.py:39
  5.9 0.7 own.1
  6.6 0.9 %forward.2 = (f32[72,128]{1,0:T(8,128)S(1)}, f32[72,128]{1,0:T(8,128)S(1)}, f32[72,128]{1,0:T(8,128)S(1)}, f32[72,128]{1,0:T(8,128)S(1)}, f32[512,256]{1,0:T(8,128)S(1)}, /*index=5*/f32[8,256]{1,0:T(8,128)S(1)}) custom-call(f32[520,128]{1,0:T(8,128)S(1)} %get-tuple-element.32.refs_0_.refs_4_, f32[520,128]{1,0:T(8,128)S(1)} %collective-permute-done.refs_1_.refs_5_, ...), custom_call_target="tpu_custom_call" | custom-call | flops 201326592 | bytes 1048576 | tf_op jit(solution)/shard_map/forward/pallas_call | solution.py:85
  7.5 2.7 %collective-permute-start.2 = (f32[72,128]{1,0:T(8,128)S(1)}, f32[72,128]{1,0:T(8,128)S(1)}, u32[]{:S(2)}, u32[]{:S(2)}) collective-permute-start(f32[72,128]{1,0:T(8,128)S(1)} %get-tuple-element.40), channel_id=1, source_target_pairs={{0,16},{4,20},{8,24},{12,28},{16,0},{20,4},{24,8},{28,12},{1,17},{... | collective-permute-start | bytes 110600 | tf_op jit(solution)/shard_map/ppermute | solution.py:39
  10.2 1.3 %collective-permute-start.3 = (f32[72,128]{1,0:T(8,128)S(1)}, f32[72,128]{1,0:T(8,128)S(1)}, u32[]{:S(2)}, u32[]{:S(2)}) collective-permute-start(f32[72,128]{1,0:T(8,128)S(1)} %get-tuple-element.41), channel_id=1, source_target_pairs={{0,24},{4,28},{8,16},{12,20},{16,8},{20,12},{24,0},{28,4},{1,25},{... | collective-permute-start | bytes 110600 | tf_op jit(solution)/shard_map/ppermute | solution.py:39
  11.5 0.2 collective-permute-start.4
  11.7 0.9 %forward.3 = (f32[72,128]{1,0:T(8,128)S(1)}, f32[72,128]{1,0:T(8,128)S(1)}, f32[72,128]{1,0:T(8,128)S(1)}, f32[72,128]{1,0:T(8,128)S(1)}, f32[512,256]{1,0:T(8,128)S(1)}, /*index=5*/f32[8,256]{1,0:T(8,128)S(1)}) custom-call(f32[520,128]{1,0:T(8,128)S(1)} %get-tuple-element.32.refs_0_.refs_4_, f32[520,128]{1,0:T(8,128)S(1)} %collective-permute-done.refs_1_.refs_5_, ...), custom_call_target="tpu_custom_call" | custom-call | flops 201326592 | bytes 1048576 | tf_op jit(solution)/shard_map/forward/pallas_call | solution.py:85
  12.7 2.9 %collective-permute-start.5 = (f32[72,128]{1,0:T(8,128)S(1)}, f32[72,128]{1,0:T(8,128)S(1)}, u32[]{:S(2)}, u32[]{:S(2)}) collective-permute-start(f32[72,128]{1,0:T(8,128)S(1)} %get-tuple-element.44), channel_id=1, source_target_pairs={{0,16},{4,20},{8,24},{12,28},{16,0},{20,4},{24,8},{28,12},{1,17},{... | collective-permute-start | bytes 110600 | tf_op jit(solution)/shard_map/ppermute | solution.py:39
  15.5 1.3 %collective-permute-start.6 = (f32[72,128]{1,0:T(8,128)S(1)}, f32[72,128]{1,0:T(8,128)S(1)}, u32[]{:S(2)}, u32[]{:S(2)}) collective-permute-start(f32[72,128]{1,0:T(8,128)S(1)} %get-tuple-element.45), channel_id=1, source_target_pairs={{0,24},{4,28},{8,16},{12,20},{16,8},{20,12},{24,0},{28,4},{1,25},{... | collective-permute-start | bytes 110600 | tf_op jit(solution)/shard_map/ppermute | solution.py:39
  16.9 0.0 collective-permute-done.2.refs_2_
  16.9 0.0 collective-permute-start.7
  16.9 0.0 collective-permute-done.3.refs_3_
  16.9 0.7 collective-permute-done.5.refs_6_
  17.6 3.7 %collective-permute-done.6.refs_7_ = f32[72,128]{1,0:T(8,128)S(1)} collective-permute-done((f32[72,128]{1,0:T(8,128)S(1)}, f32[72,128]{1,0:T(8,128)S(1)}, u32[]{:S(2)}, u32[]{:S(2)}) %collective-permute-start.6) | collective-permute-done | bytes 36896 | tf_op jit(solution)/shard_map/ppermute | solution.py:39
  21.3 0.2 merge.2.refs_8_
  21.5 1.0 %collective-permute-start.10 = (f32[136,128]{1,0:T(8,128)S(1)}, f32[136,128]{1,0:T(8,128)S(1)}, u32[]{:S(2)}, u32[]{:S(2)}) collective-permute-start(f32[136,128]{1,0:T(8,128)S(1)} %merge.2.refs_8_), channel_id=1, source_target_pairs={{0,16},{4,20},{8,24},{12,28},{16,0},{20,4},{24,8},{28,12},{1,17},{... | collective-permute-start | bytes 208904 | tf_op jit(solution)/shard_map/ppermute | solution.py:39
  22.5 1.3 %collective-permute-start.9 = (f32[136,128]{1,0:T(8,128)S(1)}, f32[136,128]{1,0:T(8,128)S(1)}, u32[]{:S(2)}, u32[]{:S(2)}) collective-permute-start(f32[136,128]{1,0:T(8,128)S(1)} %merge.2.refs_8_), channel_id=1, source_target_pairs={{0,24},{4,28},{8,16},{12,20},{16,8},{20,12},{24,0},{28,4},{1,25},{... | collective-permute-start | bytes 208904 | tf_op jit(solution)/shard_map/ppermute | solution.py:39
  23.9 1.2 %collective-permute-start.8 = (f32[136,128]{1,0:T(8,128)S(1)}, f32[136,128]{1,0:T(8,128)S(1)}, u32[]{:S(2)}, u32[]{:S(2)}) collective-permute-start(f32[136,128]{1,0:T(8,128)S(1)} %merge.2.refs_8_), channel_id=1, source_target_pairs={{0,8},{4,12},{8,0},{12,4},{16,24},{20,28},{24,16},{28,20},{1,9},{5... | collective-permute-start | bytes 208904 | tf_op jit(solution)/shard_map/ppermute | solution.py:39
  25.0 2.1 %collective-permute-done.10.refs_11_ = f32[136,128]{1,0:T(8,128)S(1)} collective-permute-done((f32[136,128]{1,0:T(8,128)S(1)}, f32[136,128]{1,0:T(8,128)S(1)}, u32[]{:S(2)}, u32[]{:S(2)}) %collective-permute-start.10) | collective-permute-done | bytes 69664 | tf_op jit(solution)/shard_map/ppermute | solution.py:39
  27.2 1.5 %collective-permute-done.9.refs_10_ = f32[136,128]{1,0:T(8,128)S(1)} collective-permute-done((f32[136,128]{1,0:T(8,128)S(1)}, f32[136,128]{1,0:T(8,128)S(1)}, u32[]{:S(2)}, u32[]{:S(2)}) %collective-permute-start.9) | collective-permute-done | bytes 69664 | tf_op jit(solution)/shard_map/ppermute | solution.py:39
  28.7 0.2 collective-permute-done.8.refs_9_
  28.9 1.4 %backward.2 = (f32[520,128]{1,0:T(8,128)S(1)}, f32[520,128]{1,0:T(8,128)S(1)}, f32[32,1,128]{2,1,0:T(1,128)S(1)}) custom-call(f32[512,256]{1,0:T(8,128)S(1)} %get-tuple-element.36.refs_0_, f32[512,256]{1,0:T(8,128)S(1)} %get-tuple-element.38.refs_1_, f32[8,256]{1,0:T(8,128)S(1)} %get-tuple-element.37.refs_3_.refs_2_, ...), custom_call_target="tpu_custom_call" | custom-call | flops 603979776 | bytes 1048576 | tf_op jit(solution)/shard_map/backward/pallas_call | solution.py:85
  30.3 10.9 %all_to_all.10.refs_6_ = f32[32,1,128]{2,1,0:T(1,128)S(1)} all-to-all(f32[32,1,128]{2,1,0:T(1,128)S(1)} %get-tuple-element.50), channel_id=1, replica_groups=mesh['page'=8,'query'=2,'head'=2] {'head','query','page'}, dimensions={0} | all-to-all | bytes 32768 | tf_op jit(solution)/shard_map/all_to_all | solution.py:637
  41.2 1.1 %update_forward.1 = (f32[1368,128]{1,0:T(8,128)S(1)}, f32[136,128]{1,0:T(8,128)S(1)}, f32[136,128]{1,0:T(8,128)S(1)}, f32[136,128]{1,0:T(8,128)S(1)}, f32[136,12...) custom-call(f32[520,128]{1,0:T(8,128)S(1)} %get-tuple-element.32.refs_0_.refs_4_, ...), custom_call_target="tpu_custom_call" | custom-call | flops 402653184 | bytes 1048576 | tf_op jit(solution)/shard_map/update_forward/pallas_call | solution.py:85
  42.3 0.6 collective-permute-start.17
  42.9 0.5 collective-permute-start.11
  43.5 2.4 %collective-permute-start.12 = (f32[136,128]{1,0:T(8,128)S(1)}, f32[136,128]{1,0:T(8,128)S(1)}, u32[]{:S(2)}, u32[]{:S(2)}) collective-permute-start(f32[136,128]{1,0:T(8,128)S(1)} %get-tuple-element.56), channel_id=1, source_target_pairs={{0,24},{4,28},{8,16},{12,20},{16,8},{20,12},{24,0},{28,4},{1,25},{... | collective-permute-start | bytes 208904 | tf_op jit(solution)/shard_map/ppermute | solution.py:39
  45.8 0.6 collective-permute-start.13
  46.4 4.5 %collective-permute-done.11.refs_3_ = f32[136,128]{1,0:T(8,128)S(1)} collective-permute-done((f32[136,128]{1,0:T(8,128)S(1)}, f32[136,128]{1,0:T(8,128)S(1)}, u32[]{:S(2)}, u32[]{:S(2)}) %collective-permute-start.11) | collective-permute-done | bytes 69664 | tf_op jit(solution)/shard_map/ppermute | solution.py:39
  51.0 0.2 collective-permute-done.13.refs_5_
  51.2 0.1 merge.3.refs_0_
  51.3 0.7 collective-permute-start.16
  51.9 3.0 %collective-permute-start.15 = (f32[136,128]{1,0:T(8,128)S(1)}, f32[136,128]{1,0:T(8,128)S(1)}, u32[]{:S(2)}, u32[]{:S(2)}) collective-permute-start(f32[136,128]{1,0:T(8,128)S(1)} %merge.3.refs_0_), channel_id=1, source_target_pairs={{0,24},{4,28},{8,16},{12,20},{16,8},{20,12},{24,0},{28,4},{1,25},{... | collective-permute-start | bytes 208904 | tf_op jit(solution)/shard_map/ppermute | solution.py:39
  55.0 3.1 %collective-permute-done.16.refs_3_ = f32[136,128]{1,0:T(8,128)S(1)} collective-permute-done((f32[136,128]{1,0:T(8,128)S(1)}, f32[136,128]{1,0:T(8,128)S(1)}, u32[]{:S(2)}, u32[]{:S(2)}) %collective-permute-start.16) | collective-permute-done | bytes 69664 | tf_op jit(solution)/shard_map/ppermute | solution.py:39
  58.1 0.8 %collective-permute-done.15.refs_2_ = f32[136,128]{1,0:T(8,128)S(1)} collective-permute-done((f32[136,128]{1,0:T(8,128)S(1)}, f32[136,128]{1,0:T(8,128)S(1)}, u32[]{:S(2)}, u32[]{:S(2)}) %collective-permute-start.15) | collective-permute-done | bytes 69664 | tf_op jit(solution)/shard_map/ppermute | solution.py:39
  58.9 0.7 collective-permute-done.14.refs_1_
  59.6 0.1 join.1.refs_5_
  59.7 1.7 %collective-permute-start.18 = (f32[136,512]{1,0:T(8,128)S(1)}, f32[136,512]{1,0:T(8,128)S(1)}, u32[]{:S(2)}, u32[]{:S(2)}) collective-permute-start(f32[136,512]{1,0:T(8,128)S(1)} %join.1.refs_5_), channel_id=1, source_target_pairs={{0,2},{2,0},{1,3},{3,1},{4,6},{6,4},{5,7},{7,5},{8,10},{10,8},{9,1... | collective-permute-start | bytes 835592 | tf_op jit(solution)/shard_map/ppermute | solution.py:39
  61.4 1.3 %backward.3 = (f32[520,128]{1,0:T(8,128)S(1)}, f32[520,128]{1,0:T(8,128)S(1)}, f32[32,1,128]{2,1,0:T(1,128)S(1)}) custom-call(f32[512,512]{1,0:T(8,128)S(1)} %get-tuple-element.51.refs_0_, f32[8,512]{1,0:T(8,128)S(1)} %get-tuple-element.52.refs_1_, f32[1368,128]{1,0:T(8,128)S(1)} %get-tuple-element.53.refs_2_, ...), custom_call_target="tpu_custom_call" | custom-call | flops 603979776 | bytes 1048576 | tf_op jit(solution)/shard_map/backward/pallas_call | solution.py:85
  62.7 8.9 %all_to_all.11.refs_0_ = f32[32,1,128]{2,1,0:T(1,128)S(1)} all-to-all(f32[32,1,128]{2,1,0:T(1,128)S(1)} %get-tuple-element.58), channel_id=1, replica_groups=mesh['page'=8,'query'=2,'head'=2] {'head','query','page'}, dimensions={0} | all-to-all | bytes 32768 | tf_op jit(solution)/shard_map/all_to_all | solution.py:637
  71.6 1.0 %page_update.2.refs_6_ = f32[1040,128]{1,0:T(8,128)S(1)} custom-call(f32[32,1,128]{2,1,0:T(1,128)S(1)} %all_to_all.11.refs_0_, f32[520,128]{1,0:T(8,128)S(1)} %get-tuple-element.60.refs_1_, f32[1368,128]{1,0:T(8,128)S(1)} %get-tuple-element.53.refs_2_, f32[1368,128]{1,0:T(8,128)S(1)} %collective-permute-done.17.refs_3_, ...), custom_call_target="tpu_custom_call" | custom-call | flops 301989888 | bytes 1048576 | tf_op jit(solution)/shard_map/page_update/pallas_call | solution.py:85
  72.6 0.1 collective-permute-start.19
  72.6 1.0 %page_update.3.refs_0_ = f32[1040,128]{1,0:T(8,128)S(1)} custom-call(f32[32,1,128]{2,1,0:T(1,128)S(1)} %all_to_all.11.refs_0_, f32[520,128]{1,0:T(8,128)S(1)} %get-tuple-element.59.refs_1_, f32[1368,128]{1,0:T(8,128)S(1)} %get-tuple-element.53.refs_2_, f32[1368,128]{1,0:T(8,128)S(1)} %collective-permute-done.17.refs_3_, ...), custom_call_target="tpu_custom_call" | custom-call | flops 301989888 | bytes 1048576 | tf_op jit(solution)/shard_map/page_update/pallas_call | solution.py:85
  73.7 0.9 %collective-permute-done.19.refs_1_ = f32[1040,128]{1,0:T(8,128)S(1)} collective-permute-done((f32[1040,128]{1,0:T(8,128)S(1)}, f32[1040,128]{1,0:T(8,128)S(1)}, u32[]{:S(2)}, u32[]{:S(2)}) %collective-permute-start.19) | collective-permute-done | bytes 532512 | tf_op jit(solution)/shard_map/ppermute | solution.py:39
  74.6 1.0 %unpack.1 = (f32[4,256,128]{2,1,0:T(8,128)}, f32[4,256,128]{2,1,0:T(8,128)}, f32[4,256]{1,0:T(4,128)}) custom-call(f32[1040,128]{1,0:T(8,128)S(1)} %page_update.3.refs_0_, f32[1040,128]{1,0:T(8,128)S(1)} %collective-permute-done.19.refs_1_), custom_call_target="tpu_custom_call" | custom-call | flops 1048576 | bytes 1048576 | tf_op jit(solution)/shard_map/unpack/pallas_call | solution.py:85
  (23 shorter events, 0.1 us)
Async XLA Ops:
  0.6 5.2 %copy-start.3 = (f32[4,256,128]{2,1,0:T(8,128)S(1)}, f32[4,256,128]{2,1,0:T(8,128)}, u32[]{:S(2)}) copy-start(f32[4,256,128]{2,1,0:T(8,128)} %refs_4_.3) | copy-start | bytes 1572868
  0.6 5.2 %copy-start.2 = (f32[4,256,128]{2,1,0:T(8,128)S(1)}, f32[4,256,128]{2,1,0:T(8,128)}, u32[]{:S(2)}) copy-start(f32[4,256,128]{2,1,0:T(8,128)} %refs_2_.3) | copy-start | bytes 1572868
  0.7 5.2 %copy-start.1 = (f32[4,256,128]{2,1,0:T(8,128)S(1)}, f32[4,256,128]{2,1,0:T(8,128)}, u32[]{:S(2)}) copy-start(f32[4,256,128]{2,1,0:T(8,128)} %refs_1_.3) | copy-start | bytes 1572868
  0.7 5.2 %copy-start = (f32[4,256,128]{2,1,0:T(8,128)S(1)}, f32[4,256,128]{2,1,0:T(8,128)}, u32[]{:S(2)}) copy-start(f32[4,256,128]{2,1,0:T(8,128)} %refs_0_.3) | copy-start | bytes 1572868
  0.7 5.2 %copy-start.5 = (f32[4,256]{1,0:T(4,128)S(1)}, f32[4,256]{1,0:T(4,128)}, u32[]{:S(2)}) copy-start(f32[4,256]{1,0:T(4,128)} %refs_3_.3) | copy-start | bytes 12292
  0.7 5.2 %copy-start.6 = (s32[4,256]{1,0:T(4,128)S(1)}, s32[4,256]{1,0:T(4,128)}, u32[]{:S(2)}) copy-start(s32[4,256]{1,0:T(4,128)} %refs_5_.3) | copy-start | bytes 12292
  2.7 3.2 %copy-start.7 = (s32[8]{0:T(128)S(1)}, s32[8]{0:T(128)}, u32[]{:S(2)}) copy-start(s32[8]{0:T(128)} %refs_6_.3) | copy-start | bytes 100
  2.7 3.8 %collective-permute-start = (f32[520,128]{1,0:T(8,128)}, f32[520,128]{1,0:T(8,128)S(1)}, u32[]{:S(2)}, u32[]{:S(2)}) collective-permute-start(f32[520,128]{1,0:T(8,128)} %get-tuple-element.33), channel_id=1, source_target_pairs={{0,4},{4,0},{8,12},{12,8},{16,20},{20,16},{24,28},{28,24},{1,5},{5... | collective-permute-start | bytes 798728 | tf_op jit(solution)/shard_map/ppermute | solution.py:39
  3.3 8.5 %collective-permute-start.1 = (f32[328,128]{1,0:T(8,128)}, f32[328,128]{1,0:T(8,128)S(1)}, u32[]{:S(2)}, u32[]{:S(2)}) collective-permute-start(f32[328,128]{1,0:T(8,128)} %get-tuple-element.35.refs_5_), channel_id=1, source_target_pairs={{0,2},{2,0},{1,3},{3,1},{4,6},{6,4},{5,7},{7,5},{8,10},{10,8},{9,1... | collective-permute-start | bytes 503816 | tf_op jit(solution)/shard_map/ppermute | solution.py:39
  7.5 9.4 %collective-permute-start.2 = (f32[72,128]{1,0:T(8,128)S(1)}, f32[72,128]{1,0:T(8,128)S(1)}, u32[]{:S(2)}, u32[]{:S(2)}) collective-permute-start(f32[72,128]{1,0:T(8,128)S(1)} %get-tuple-element.40), channel_id=1, source_target_pairs={{0,16},{4,20},{8,24},{12,28},{16,0},{20,4},{24,8},{28,12},{1,17},{... | collective-permute-start | bytes 110600 | tf_op jit(solution)/shard_map/ppermute | solution.py:39
  10.2 6.7 %collective-permute-start.3 = (f32[72,128]{1,0:T(8,128)S(1)}, f32[72,128]{1,0:T(8,128)S(1)}, u32[]{:S(2)}, u32[]{:S(2)}) collective-permute-start(f32[72,128]{1,0:T(8,128)S(1)} %get-tuple-element.41), channel_id=1, source_target_pairs={{0,24},{4,28},{8,16},{12,20},{16,8},{20,12},{24,0},{28,4},{1,25},{... | collective-permute-start | bytes 110600 | tf_op jit(solution)/shard_map/ppermute | solution.py:39
  11.5 5.4 %collective-permute-start.4 = (f32[72,128]{1,0:T(8,128)S(1)}, f32[72,128]{1,0:T(8,128)S(1)}, u32[]{:S(2)}, u32[]{:S(2)}) collective-permute-start(f32[72,128]{1,0:T(8,128)S(1)} %get-tuple-element.42), channel_id=1, source_target_pairs={{0,8},{4,12},{8,0},{12,4},{16,24},{20,28},{24,16},{28,20},{1,9},{5... | collective-permute-start | bytes 110600 | tf_op jit(solution)/shard_map/ppermute | solution.py:39
  12.7 4.9 %collective-permute-start.5 = (f32[72,128]{1,0:T(8,128)S(1)}, f32[72,128]{1,0:T(8,128)S(1)}, u32[]{:S(2)}, u32[]{:S(2)}) collective-permute-start(f32[72,128]{1,0:T(8,128)S(1)} %get-tuple-element.44), channel_id=1, source_target_pairs={{0,16},{4,20},{8,24},{12,28},{16,0},{20,4},{24,8},{28,12},{1,17},{... | collective-permute-start | bytes 110600 | tf_op jit(solution)/shard_map/ppermute | solution.py:39
  15.5 5.8 %collective-permute-start.6 = (f32[72,128]{1,0:T(8,128)S(1)}, f32[72,128]{1,0:T(8,128)S(1)}, u32[]{:S(2)}, u32[]{:S(2)}) collective-permute-start(f32[72,128]{1,0:T(8,128)S(1)} %get-tuple-element.45), channel_id=1, source_target_pairs={{0,24},{4,28},{8,16},{12,20},{16,8},{20,12},{24,0},{28,4},{1,25},{... | collective-permute-start | bytes 110600 | tf_op jit(solution)/shard_map/ppermute | solution.py:39
  16.9 4.4 %collective-permute-start.7 = (f32[72,128]{1,0:T(8,128)S(1)}, f32[72,128]{1,0:T(8,128)S(1)}, u32[]{:S(2)}, u32[]{:S(2)}) collective-permute-start(f32[72,128]{1,0:T(8,128)S(1)} %get-tuple-element.46), channel_id=1, source_target_pairs={{0,8},{4,12},{8,0},{12,4},{16,24},{20,28},{24,16},{28,20},{1,9},{5... | collective-permute-start | bytes 110600 | tf_op jit(solution)/shard_map/ppermute | solution.py:39
  21.5 5.7 %collective-permute-start.10 = (f32[136,128]{1,0:T(8,128)S(1)}, f32[136,128]{1,0:T(8,128)S(1)}, u32[]{:S(2)}, u32[]{:S(2)}) collective-permute-start(f32[136,128]{1,0:T(8,128)S(1)} %merge.2.refs_8_), channel_id=1, source_target_pairs={{0,16},{4,20},{8,24},{12,28},{16,0},{20,4},{24,8},{28,12},{1,17},{... | collective-permute-start | bytes 208904 | tf_op jit(solution)/shard_map/ppermute | solution.py:39
  22.5 6.2 %collective-permute-start.9 = (f32[136,128]{1,0:T(8,128)S(1)}, f32[136,128]{1,0:T(8,128)S(1)}, u32[]{:S(2)}, u32[]{:S(2)}) collective-permute-start(f32[136,128]{1,0:T(8,128)S(1)} %merge.2.refs_8_), channel_id=1, source_target_pairs={{0,24},{4,28},{8,16},{12,20},{16,8},{20,12},{24,0},{28,4},{1,25},{... | collective-permute-start | bytes 208904 | tf_op jit(solution)/shard_map/ppermute | solution.py:39
  23.9 5.1 %collective-permute-start.8 = (f32[136,128]{1,0:T(8,128)S(1)}, f32[136,128]{1,0:T(8,128)S(1)}, u32[]{:S(2)}, u32[]{:S(2)}) collective-permute-start(f32[136,128]{1,0:T(8,128)S(1)} %merge.2.refs_8_), channel_id=1, source_target_pairs={{0,8},{4,12},{8,0},{12,4},{16,24},{20,28},{24,16},{28,20},{1,9},{5... | collective-permute-start | bytes 208904 | tf_op jit(solution)/shard_map/ppermute | solution.py:39
  42.3 29.2 %collective-permute-start.17 = (f32[1368,128]{1,0:T(8,128)S(1)}, f32[1368,128]{1,0:T(8,128)S(1)}, u32[]{:S(2)}, u32[]{:S(2)}) collective-permute-start(f32[1368,128]{1,0:T(8,128)S(1)} %get-tuple-element.53.refs_2_), channel_id=1, source_target_pairs={{0,2},{2,0},{1,3},{3,1},{4,6},{6,4},{5,7},{7,5},{8,10},{10,8},{9,1... | collective-permute-start | bytes 2101256 | tf_op jit(solution)/shard_map/ppermute | solution.py:39
  42.9 8.0 %collective-permute-start.11 = (f32[136,128]{1,0:T(8,128)S(1)}, f32[136,128]{1,0:T(8,128)S(1)}, u32[]{:S(2)}, u32[]{:S(2)}) collective-permute-start(f32[136,128]{1,0:T(8,128)S(1)} %get-tuple-element.55), channel_id=1, source_target_pairs={{0,16},{4,20},{8,24},{12,28},{16,0},{20,4},{24,8},{28,12},{1,17},{... | collective-permute-start | bytes 208904 | tf_op jit(solution)/shard_map/ppermute | solution.py:39
  43.5 7.5 %collective-permute-start.12 = (f32[136,128]{1,0:T(8,128)S(1)}, f32[136,128]{1,0:T(8,128)S(1)}, u32[]{:S(2)}, u32[]{:S(2)}) collective-permute-start(f32[136,128]{1,0:T(8,128)S(1)} %get-tuple-element.56), channel_id=1, source_target_pairs={{0,24},{4,28},{8,16},{12,20},{16,8},{20,12},{24,0},{28,4},{1,25},{... | collective-permute-start | bytes 208904 | tf_op jit(solution)/shard_map/ppermute | solution.py:39
  45.8 5.3 %collective-permute-start.13 = (f32[136,128]{1,0:T(8,128)S(1)}, f32[136,128]{1,0:T(8,128)S(1)}, u32[]{:S(2)}, u32[]{:S(2)}) collective-permute-start(f32[136,128]{1,0:T(8,128)S(1)} %get-tuple-element.57), channel_id=1, source_target_pairs={{0,8},{4,12},{8,0},{12,4},{16,24},{20,28},{24,16},{28,20},{1,9},{5... | collective-permute-start | bytes 208904 | tf_op jit(solution)/shard_map/ppermute | solution.py:39
  51.3 6.8 %collective-permute-start.16 = (f32[136,128]{1,0:T(8,128)S(1)}, f32[136,128]{1,0:T(8,128)S(1)}, u32[]{:S(2)}, u32[]{:S(2)}) collective-permute-start(f32[136,128]{1,0:T(8,128)S(1)} %merge.3.refs_0_), channel_id=1, source_target_pairs={{0,16},{4,20},{8,24},{12,28},{16,0},{20,4},{24,8},{28,12},{1,17},{... | collective-permute-start | bytes 208904 | tf_op jit(solution)/shard_map/ppermute | solution.py:39
  51.9 7.0 %collective-permute-start.15 = (f32[136,128]{1,0:T(8,128)S(1)}, f32[136,128]{1,0:T(8,128)S(1)}, u32[]{:S(2)}, u32[]{:S(2)}) collective-permute-start(f32[136,128]{1,0:T(8,128)S(1)} %merge.3.refs_0_), channel_id=1, source_target_pairs={{0,24},{4,28},{8,16},{12,20},{16,8},{20,12},{24,0},{28,4},{1,25},{... | collective-permute-start | bytes 208904 | tf_op jit(solution)/shard_map/ppermute | solution.py:39
  55.0 4.6 %collective-permute-start.14 = (f32[136,128]{1,0:T(8,128)S(1)}, f32[136,128]{1,0:T(8,128)S(1)}, u32[]{:S(2)}, u32[]{:S(2)}) collective-permute-start(f32[136,128]{1,0:T(8,128)S(1)} %merge.3.refs_0_), channel_id=1, source_target_pairs={{0,8},{4,12},{8,0},{12,4},{16,24},{20,28},{24,16},{28,20},{1,9},{5... | collective-permute-start | bytes 208904 | tf_op jit(solution)/shard_map/ppermute | solution.py:39
  59.7 11.9 %collective-permute-start.18 = (f32[136,512]{1,0:T(8,128)S(1)}, f32[136,512]{1,0:T(8,128)S(1)}, u32[]{:S(2)}, u32[]{:S(2)}) collective-permute-start(f32[136,512]{1,0:T(8,128)S(1)} %join.1.refs_5_), channel_id=1, source_target_pairs={{0,2},{2,0},{1,3},{3,1},{4,6},{6,4},{5,7},{7,5},{8,10},{10,8},{9,1... | collective-permute-start | bytes 835592 | tf_op jit(solution)/shard_map/ppermute | solution.py:39
  61.4 10.2 %copy-start.4 = (f32[328,128]{1,0:T(8,128)S(1)}, f32[328,128]{1,0:T(8,128)}, u32[]{:S(2)}) copy-start(f32[328,128]{1,0:T(8,128)} %get-tuple-element.35.refs_5_) | copy-start | bytes 503812
  72.6 2.0 %collective-permute-start.19 = (f32[1040,128]{1,0:T(8,128)S(1)}, f32[1040,128]{1,0:T(8,128)S(1)}, u32[]{:S(2)}, u32[]{:S(2)}) collective-permute-start(f32[1040,128]{1,0:T(8,128)S(1)} %page_update.2.refs_6_), channel_id=1, source_target_pairs={{0,4},{4,0},{8,12},{12,8},{16,20},{20,16},{24,28},{28,24},{1,5},{5... | collective-permute-start | bytes 1597448 | tf_op jit(solution)/shard_map/ppermute | solution.py:39
